TPU v7x, 32 devices: a whole 2x2x4 slice. The times are simulated.
32 devices in a mesh: dp: 4 (over x, core), expert: 8 (over z, y).
Axes of the slice: x: 2, y: 2, z: 4, core: 2. Of those that a mesh axis runs over, the one named last changes fastest.
Arguments:
- hidden_in: bfloat16 [8, 256, 2048], P('expert', 'dp'), may hold values from -6 to 6
- queries: bfloat16 [8, 256, 2048], P('expert', None, 'dp'), may hold values from -150 to 150
- key_pool: bfloat16 [16, 128, 2048], P('expert', None, 'dp'), may hold values from -8 to 8
- value_pool: bfloat16 [16, 128, 2048], P('expert', None, 'dp'), may hold values from -6 to 6
- page_table: int32 [8, 2], P('expert'), may hold values from 0 to 1, as said below
- prompt_lengths: int32 [8, 4], P('expert'), may hold values from 1 to 128, 256 in all within a row
- expert_ids: int32 [8, 256, 8], P('expert', 'dp'), may hold values from 0 to 7, all different within a row; in each aligned block of 64 rows (0 to 63, 64 to 127, ..., all dimensions but the last counted through in order) at most 64 rows name the same one
- gate_weights: float32 [8, 256, 8], P('expert', 'dp'), may hold values from 0.05 to 0.3
- norm_gain: float32 [2048], replicated, may hold values from 0.5 to 1.5
- trainer_gate_up: float32 [8, 2048, 2048], P('expert', 'dp'), may hold values from -0.125 to 0.125
- trainer_down: float32 [8, 1024, 2048], P('expert', 'dp'), may hold values from -0.1875 to 0.1875
Outputs:
- mixed: bfloat16 [8, 256, 2048], P('expert', 'dp')
Inputs may be any that keep to these rules, and one draw needn't show every extreme that they name: `page_table`: each group's row is a permutation of the group's page numbers. `expert_ids`: among the 64 rows of one device (aligned blocks of rows), no expert is named by more than 64 rows, a bound that some block reaches.
All inputs are finite; a program needn't handle non-finite values.
Results may differ from a plain program's by a relative error of at most 0.0075.
Values may be sent and summed in bfloat16 or wider, within the bound.
No kernel may reach another device: no remote copies, remote signals or barrier semaphores. Data moves between devices by JAX's collectives and lax.ppermute only.
A program may use at most 64 MiB of HBM per device.

v0:
```python
import math

import jax
import jax.numpy as jnp
from jax import lax
from jax.sharding import PartitionSpec as P

HDIM = 128
TOPK = 8


epsilon = 1e-05


def fetch_weights(trainer_gate_up, trainer_down):
    return (
        lax.all_gather(trainer_gate_up.astype(jnp.bfloat16), "dp", axis=1, tiled=True),
        lax.all_gather(trainer_down.astype(jnp.bfloat16), "dp", axis=1, tiled=True),
    )


def local(
    hidden_in,
    queries,
    key_pool,
    value_pool,
    page_table,
    prompt_lengths,
    expert_ids,
    gate_weights,
    norm_gain,
    trainer_gate_up,
    trainer_down,
):
    col_tok = queries.shape[1]
    width_dev = queries.shape[2]
    heads_dev = width_dev // HDIM
    keys_all = jnp.take(key_pool, page_table[0], axis=0).reshape(col_tok, heads_dev, HDIM)
    values_all = jnp.take(value_pool, page_table[0], axis=0).reshape(col_tok, heads_dev, HDIM)
    request_ends = jnp.cumsum(prompt_lengths[0])
    positions = lax.iota(jnp.int32, col_tok)
    request = jnp.sum((positions[:, None] >= request_ends[None, :]).astype(jnp.int32), axis=1)
    block_rows = math.gcd(col_tok, 512)
    query_blocks = queries[0].reshape(col_tok // block_rows, block_rows, heads_dev, HDIM)
    request_blocks = request.reshape(col_tok // block_rows, block_rows)
    score_scale = 1.0 / math.sqrt(HDIM)

    def attend(pieces):
        query_block, request_block = pieces
        scores = (
            jnp.einsum("qhd,khd->hqk", query_block, keys_all, preferred_element_type=jnp.float32)
            * score_scale
        )
        same_request = (request_block[:, None] == request[None, :])[None]
        scores = jnp.where(same_request, scores, -1e30)
        highest = jnp.max(scores, axis=-1, keepdims=True)
        weights = jnp.where(same_request, jnp.exp(scores - highest), 0.0)
        totals = jnp.sum(weights, axis=-1, keepdims=True)
        probs = (weights / totals).astype(jnp.bfloat16)
        output = jnp.einsum("hqk,khd->qhd", probs, values_all, preferred_element_type=jnp.float32)
        return output.astype(jnp.bfloat16).reshape(block_rows, width_dev)

    attn_heads = lax.map(attend, (query_blocks, request_blocks)).reshape(1, col_tok, width_dev)
    attn_tokens = lax.all_to_all(attn_heads, "dp", split_axis=1, concat_axis=2, tiled=True)
    resid32 = (
        (hidden_in.astype(jnp.float32) + attn_tokens.astype(jnp.float32))
        .astype(jnp.bfloat16)
        .astype(jnp.float32)
    )
    mean_square = jnp.mean(resid32 * resid32, axis=-1, keepdims=True)
    normed = (resid32 * lax.rsqrt(mean_square + epsilon) * norm_gain).astype(jnp.bfloat16)
    server_gate_up, server_down = fetch_weights(trainer_gate_up, trainer_down)
    token_rows = normed.shape[1]
    width = normed.shape[2]
    expert_count = lax.axis_size("expert")
    capacity = min(token_rows, token_rows * TOPK * 5 // (4 * expert_count))
    hidden_size = server_gate_up.shape[2] // 2
    ids_flat = expert_ids[0].reshape(token_rows * TOPK)
    onehot = (ids_flat[:, None] == lax.iota(jnp.int32, expert_count)[None, :]).astype(jnp.int32)
    earlier = jnp.cumsum(onehot, axis=0) - onehot
    slot_index = jnp.sum(earlier * onehot, axis=1)
    flat_slot = ids_flat * capacity + slot_index
    placement = (
        flat_slot[:, None] == lax.iota(jnp.int32, expert_count * capacity)[None, :]
    ).astype(jnp.bfloat16)
    dispatch_matrix = jnp.sum(placement.reshape(token_rows, TOPK, expert_count * capacity), axis=1)
    outgoing = jnp.einsum(
        "ts,td->sd", dispatch_matrix, normed[0], preferred_element_type=jnp.float32
    )
    outgoing = outgoing.astype(jnp.bfloat16).reshape(expert_count, capacity, width)
    received = lax.all_to_all(outgoing, "expert", split_axis=0, concat_axis=0, tiled=True)
    sources, items, features = received.shape
    slot_rows = received.reshape(sources * items, features)
    gate_up = jnp.dot(slot_rows, server_gate_up[0], preferred_element_type=jnp.float32)
    hidden_units = (jax.nn.silu(gate_up[:, :hidden_size]) * gate_up[:, hidden_size:]).astype(
        jnp.bfloat16
    )
    outputs = jnp.dot(hidden_units, server_down[0], preferred_element_type=jnp.float32).astype(
        jnp.bfloat16
    )
    returned = lax.all_to_all(
        outputs.reshape(sources, items, features), "expert", split_axis=0, concat_axis=0, tiled=True
    )
    copies = jnp.take(returned.reshape(expert_count * capacity, width), flat_slot, axis=0)
    copies = copies.reshape(token_rows, TOPK, width).astype(jnp.float32)
    mixture = jnp.einsum("tk,tkd->td", gate_weights[0], copies)
    mixed = resid32[0] + mixture
    return mixed.astype(jnp.bfloat16)[None]


def solution(mesh):
    placed = (
        P("expert", "dp", None),
        P("expert", None, "dp"),
        P("expert", None, "dp"),
        P("expert", None, "dp"),
        P("expert", None),
        P("expert", None),
        P("expert", "dp", None),
        P("expert", "dp", None),
        P(),
        P("expert", "dp", None),
        P("expert", "dp", None),
    )
    return jax.shard_map(
        local, mesh=mesh, in_specs=placed, out_specs=P("expert", "dp", None), check_vma=False
    )
```

profile of v0, /device:TPU:0, one launch (start us, length us, event | category | flops | bytes accessed | tf_op | source)
XLA Modules:
  0.0 185.4 jit_solution(7760105602044942379)
XLA Ops:
  6.5 3.9 %convert_element_type.94 = bf16[1,512,2048]{2,1,0:T(8,128)(2,1)} convert(f32[1,512,2048]{2,1,0:T(8,128)} %param.22) | non-fusion elementwise | flops 1048576 | bytes 6291456 | tf_op jit(solution)/shard_map/convert_element_type | solution.py:17
  10.5 0.6 copy-done.8
  11.1 0.6 gather_fusion.1
  11.7 0.6 gather_fusion.2
  12.3 0.1 broadcast_select_fusion.1
  12.6 0.2 reduce-window.18
  12.9 0.1 broadcast_compare_fusion
  13.0 0.6 fusion.50
  13.6 0.3 convolution_convert_fusion.1
  13.9 0.5 copy.60
  14.4 0.5 broadcast.163
  14.9 2.3 %reduce.4 = bf16[256,512]{1,0:T(8,128)(2,1)S(1)} reduce(bf16[256,1,512]{2,1,0:T(2,128)(2,1)S(1)} %bitcast.82, bf16[]{:T(256)} %broadcast.163), dimensions={1}, to_apply=%bitcast.69.reduce_sub_computation | reduce | bytes 524290
  17.2 0.9 reshape.237
  18.1 4.2 %all-to-all-start = ((bf16[4,2,16384]{2,1,0:T(2,128)(2,1)}), bf16[4,2,16384]{2,1,0:T(2,128)(2,1)S(1)}, u32[]{:S(2)}, u32[]{:S(2)}) async-start(bf16[4,2,16384]{2,1,0:T(2,128)(2,1)} %reshape.237), calls=%async_computation | async-start | bytes 524288 | tf_op jit(solution)/shard_map/all_to_all | solution.py:64
  22.3 1.1 convert_element_type.96
  23.6 1.1 reduce-window.19
  24.8 0.2 slice_reduce_fusion
  25.5 0.4 fusion.25
  25.9 5.3 %all-to-all-done = bf16[4,2,16384]{2,1,0:T(2,128)(2,1)S(1)} async-done(((bf16[4,2,16384]{2,1,0:T(2,128)(2,1)}), bf16[4,2,16384]{2,1,0:T(2,128)(2,1)S(1)}, u32[]{:S(2)}, u32[]{:S(2)}) %all-to-all-start) | async-done | bytes 262176 | tf_op jit(solution)/shard_map/all_to_all | solution.py:64
  31.2 0.3 reshape.238
  31.6 0.2 fusion.22
  31.8 0.8 convolution_convert_fusion
  32.6 54.5 %all_to_all.19 = bf16[8,64,2048]{2,1,0:T(8,128)(2,1)S(1)} all-to-all(bf16[8,64,2048]{2,1,0:T(8,128)(2,1)S(1)} %bitcast.78), channel_id=1, replica_groups=mesh['dp'=4,'expert'=8] {'expert'}, dimensions={0} | all-to-all | bytes 4194304 | tf_op jit(solution)/shard_map/all_to_all | solution.py:91
  87.1 9.5 %fusion.1 = f32[512,2048]{1,0:T(8,128)} fusion(bf16[512,2048]{1,0:T(8,128)(2,1)S(1)} %bitcast.81, bf16[1,2048,2048]{2,1,0:T(8,128)(2,1)} %all-gather.3.cloned.1.call-done), kind=kOutput, calls=%fused_computation.4 | convolution fusion | flops 4294967296 | bytes 14680064 | tf_op jit(solution)/shard_map/dot_general | solution.py:94
  96.6 13.9 %all-gather.5.cloned.1.call-done = bf16[1,1024,2048]{2,1,0:T(8,128)(2,1)} async-done(((bf16[1,256,2048]{2,1,0:T(8,128)(2,1)}), bf16[1,1024,2048]{2,1,0:T(8,128)(2,1)}) %all-gather.5.cloned.1.call-update) | async-done | bytes 4194320 | tf_op jit(solution)/shard_map/all_gather | solution.py:18
  110.5 7.2 %fusion.5 = bf16[512,2048]{1,0:T(8,128)(2,1)} fusion(bf16[1,1024,2048]{2,1,0:T(8,128)(2,1)} %all-gather.5.cloned.1.call-done, f32[512,2048]{1,0:T(8,128)} %fusion.1), kind=kOutput, calls=%fused_computation.8 | convolution fusion | flops 2151677952 | bytes 10485760 | tf_op jit(solution)/shard_map/dot_general | solution.py:98
  117.7 5.6 %all-to-all-start.2 = ((bf16[8,64,2048]{2,1,0:T(8,128)(2,1)}), bf16[8,64,2048]{2,1,0:T(8,128)(2,1)S(1)}, u32[]{:S(2)}, u32[]{:S(2)}) async-start(bf16[8,64,2048]{2,1,0:T(8,128)(2,1)} %bitcast.80), calls=%async_computation.2 | async-start | bytes 4194304 | tf_op jit(solution)/shard_map/all_to_all | solution.py:101
  123.5 0.1 copy.66
  123.8 48.2 %all-to-all-done.2 = bf16[8,64,2048]{2,1,0:T(8,128)(2,1)S(1)} async-done(((bf16[8,64,2048]{2,1,0:T(8,128)(2,1)}), bf16[8,64,2048]{2,1,0:T(8,128)(2,1)S(1)}, u32[]{:S(2)}, u32[]{:S(2)}) %all-to-all-start.2) | async-done | bytes 2097184 | tf_op jit(solution)/shard_map/all_to_all | solution.py:101
  172.0 3.3 %gather_fusion = bf16[512,2048]{1,0:T(8,128)(2,1)} fusion(bf16[512,2048]{1,0:T(8,128)(2,1)S(1)} %bitcast.77, s32[1024]{0:T(1024)S(1)} %pad_clamp_fusion), kind=kCustom, calls=%fused_computation.2 | custom fusion | bytes 4196352 | tf_op jit(solution)/shard_map/jit(_take)/gather | solution.py:104
  175.3 2.4 %fusion.9 = f32[64,1,2048]{2,1,0:T(1,128)S(1)} fusion(bf16[64,8,1]{1,2,0:T(2,128)(2,1)S(1)} %copy.70, bf16[512,2048]{1,0:T(8,128)(2,1)} %gather_fusion, pred[64,8]{1,0:T(8,128)(4,1)S(1)} %copy.66), kind=kOutput, calls=%fused_computation.13 | convolution fusion | flops 3145728 | bytes 2622976 | tf_op jit(solution)/shard_map/tk,tkd->td/dot_general | solution.py:106
  177.7 0.9 fusion.28
  (52 shorter events, 1.5 us)
Async XLA Ops:
  6.5 4.6 %copy-start = (bf16[2,128,512]{2,1,0:T(8,128)(2,1)S(1)}, bf16[2,128,512]{2,1,0:T(8,128)(2,1)}, u32[]{:S(2)}) copy-start(bf16[2,128,512]{2,1,0:T(8,128)(2,1)} %param.16) | copy-start | bytes 786436
  6.5 80.6 %all-gather.3.cloned.1.call-start = ((), (), s32[]{:S(2)}) async-start(), calls=%async_computation.3 | async-start | bytes 10485760 | tf_op jit(solution)/shard_map/all_gather | solution.py:17
  10.5 0.7 copy-start.8
  10.5 1.3 copy-start.2
  10.5 2.0 %copy-start.3 = (bf16[1,256,512]{2,1,0:T(8,128)(2,1)S(1)}, bf16[1,256,512]{2,1,0:T(8,128)(2,1)}, u32[]{:S(2)}) copy-start(bf16[1,256,512]{2,1,0:T(8,128)(2,1)} %param.14) | copy-start | bytes 786436
  11.1 1.5 copy-start.9
  13.9 8.4 %copy-start.1 = (f32[1,256,2048]{2,1,0:T(8,128)S(1)}, f32[1,256,2048]{2,1,0:T(8,128)}, u32[]{:S(2)}) copy-start(f32[1,256,2048]{2,1,0:T(8,128)} %param.23) | copy-start | bytes 6291460
  18.1 13.1 %all-to-all-start = ((bf16[4,2,16384]{2,1,0:T(2,128)(2,1)}), bf16[4,2,16384]{2,1,0:T(2,128)(2,1)S(1)}, u32[]{:S(2)}, u32[]{:S(2)}) async-start(bf16[4,2,16384]{2,1,0:T(2,128)(2,1)} %reshape.237), calls=%async_computation | async-start | bytes 524288 | tf_op jit(solution)/shard_map/all_to_all | solution.py:64
  22.3 1.2 copy-start.5
  22.3 88.2 %all-gather.5.cloned.1.call-start = ((), (), s32[]{:S(2)}) async-start(), calls=%async_computation.4 | async-start | bytes 5242880 | tf_op jit(solution)/shard_map/all_gather | solution.py:18
  23.4 8.2 %copy-start.4 = (bf16[1,64,2048]{2,1,0:T(8,128)(2,1)S(1)}, bf16[1,64,2048]{2,1,0:T(8,128)(2,1)}, u32[]{:S(2)}) copy-start(bf16[1,64,2048]{2,1,0:T(8,128)(2,1)} %param.13) | copy-start | bytes 786436
  25.9 5.9 %copy-start.6 = (f32[2048]{0:T(1024)S(1)}, f32[2048]{0:T(1024)}, u32[]{:S(2)}) copy-start(f32[2048]{0:T(1024)} %param.21) | copy-start | bytes 24580
  117.7 5.9 %copy-start.7 = (f32[1,64,8]{1,2,0:T(8,128)S(1)}, f32[1,64,8]{1,2,0:T(8,128)}, u32[]{:S(2)}) copy-start(f32[1,64,8]{1,2,0:T(8,128)} %param.20) | copy-start | bytes 6148
  117.7 54.3 %all-to-all-start.2 = ((bf16[8,64,2048]{2,1,0:T(8,128)(2,1)}), bf16[8,64,2048]{2,1,0:T(8,128)(2,1)S(1)}, u32[]{:S(2)}, u32[]{:S(2)}) async-start(bf16[8,64,2048]{2,1,0:T(8,128)(2,1)} %bitcast.80), calls=%async_computation.2 | async-start | bytes 4194304 | tf_op jit(solution)/shard_map/all_to_all | solution.py:101
Sparse Core Ops, SparseCore 0:
  10.6 63.7 all-gather.2
  76.0 34.4 all-gather.4
where the time goes:
time: 186 us; the launch traced here: 185 us
  waiting for transfers between devices  67.4 us (36%)
  blocking collectives  54.5 us (29%)
  matrix products  20.7 us (11%)
  between operations  13.6 us (7%)
  other arithmetic  10.6 us (6%)
  starting transfers between devices  9.86 us (5%)
  local copies, waits for them, and re-layouts  8.64 us (5%)
    all_to_all x1, blocking collectives, local(): lax.all_to_all(outgoing, 'expert', split_axis=0, concat_axis=0, tiled=True)  54.5 us
    all_to_all x1, waiting for transfers between devices, local(): lax.all_to_all(outputs.reshape(sources, items, features), 'expert', split...  48.2 us
    all_gather x1, waiting for transfers between devices, fetch_weights(): lax.all_gather(trainer_down.astype(jnp.bfloat16), 'dp', axis=1, tiled=True)  13.9 us
    dot_general x1, matrix products, local(): jnp.dot(slot_rows, server_gate_up[0], preferred_element_type=jnp.float32)  9.47 us
    dot_general x1, matrix products, local(): jnp.dot(hidden_units, server_down[0], preferred_element_type=jnp.float32)  7.18 us
    all_to_all x1, starting transfers between devices, local(): lax.all_to_all(outputs.reshape(sources, items, features), 'expert', split...  5.65 us
    all_to_all x1, waiting for transfers between devices, local(): lax.all_to_all(attn_heads, 'dp', split_axis=1, concat_axis=2, tiled=True)  5.28 us
    all_to_all x1, starting transfers between devices, local(): lax.all_to_all(attn_heads, 'dp', split_axis=1, concat_axis=2, tiled=True)  4.21 us
  transfers between devices with their start and end apart: 4, of which 3 were waited for; matrix products, arithmetic and copies ran while one was open for 12% of the time, Pallas kernels for 0%

commit v1 on v0

--- a/solution.py
+++ b/solution.py
@@ -17,6 +17,25 @@
         lax.all_gather(trainer_gate_up.astype(jnp.bfloat16), "dp", axis=1, tiled=True),
         lax.all_gather(trainer_down.astype(jnp.bfloat16), "dp", axis=1, tiled=True),
     )
+
+
+def every_expert(normed, expert_ids, gate_weights, gate_up_weights, down_weights):
+    expert_count = lax.axis_size("expert")
+    experts = lax.iota(jnp.int32, expert_count)
+    chosen = expert_ids[:, :, None] == experts[None, None, :]
+    gates = jnp.sum(jnp.where(chosen, gate_weights[:, :, None], 0.0), axis=1)
+    gates_all = lax.all_gather(gates, "expert", axis=0, tiled=True)
+    own = experts == lax.axis_index("expert")
+    own_gates = jnp.sum(jnp.where(own[None, :], gates_all, 0.0), axis=1, keepdims=True)
+    rows = lax.all_gather(normed, "expert", axis=0, tiled=True)
+    gate_up = jnp.dot(rows, gate_up_weights, preferred_element_type=jnp.float32)
+    hidden_size = gate_up.shape[1] // 2
+    hidden_units = (jax.nn.silu(gate_up[:, :hidden_size]) * gate_up[:, hidden_size:]).astype(
+        jnp.bfloat16
+    )
+    outputs = jnp.dot(hidden_units, down_weights, preferred_element_type=jnp.float32)
+    weighted = (outputs * own_gates).astype(jnp.bfloat16)
+    return lax.psum_scatter(weighted, "expert", scatter_dimension=0, tiled=True).astype(jnp.float32)
 
 
 def local(
@@ -73,6 +92,11 @@
     token_rows = normed.shape[1]
     width = normed.shape[2]
     expert_count = lax.axis_size("expert")
+    if expert_count == TOPK:
+        mixture = every_expert(
+            normed[0], expert_ids[0], gate_weights[0], server_gate_up[0], server_down[0]
+        )
+        return (resid32[0] + mixture).astype(jnp.bfloat16)[None]
     capacity = min(token_rows, token_rows * TOPK * 5 // (4 * expert_count))
     hidden_size = server_gate_up.shape[2] // 2
     ids_flat = expert_ids[0].reshape(token_rows * TOPK)

time: 186 us -> 255 us (1.37)
  waiting for transfers between devices: 67.4 us -> 164 us
  blocking collectives: 54.5 us -> 41.3 us
  starting transfers between devices: 9.86 us -> 0.13 us
  local copies, waits for them, and re-layouts: 8.64 us -> 5.44 us
    reduce_scatter x0 -> x1, waiting for transfers between devices: none -> 68.4 us  [every_expert(): lax.psum_scatter(weighted, 'expert', scatter_dimension=0, tiled=True)]
    all_gather x1, waiting for transfers between devices: 0.01 us -> 58.4 us  [fetch_weights(): lax.all_gather(trainer_gate_up.astype(jnp.bfloat16), 'dp', axis=1, tiled=...]
    all_to_all x2 -> x0, waiting for transfers between devices: 53.5 us -> none  [the longest x1 48.2 us: local(): lax.all_to_all(outputs.reshape(sources, items, features), 'expert', split...]
    all_to_all x1, blocking collectives: 54.5 us -> 10.2 us  [local(): lax.all_to_all(attn_heads, 'dp', split_axis=1, concat_axis=2, tiled=True)]
    all_gather x0 -> x1, blocking collectives: none -> 31.1 us  [every_expert(): gates_all = lax.all_gather(gates, 'expert', axis=0, tiled=True)]
    all_gather x0 -> x1, waiting for transfers between devices: none -> 11.9 us  [every_expert(): rows = lax.all_gather(normed, 'expert', axis=0, tiled=True)]
    all_gather x1, waiting for transfers between devices: 13.9 us -> 25.5 us  [fetch_weights(): lax.all_gather(trainer_down.astype(jnp.bfloat16), 'dp', axis=1, tiled=True)]
    all_to_all x2 -> x0, starting transfers between devices: 9.85 us -> none  [the longest x1 5.65 us: local(): lax.all_to_all(outputs.reshape(sources, items, features), 'expert', split...]
  transfers between devices with their start and end apart: 4 -> 4, of which waited for: 3 -> 4; matrix products, arithmetic and copies ran while one was open for 12% -> 6% of each run, Pallas kernels for 0% -> 0%
where the time goes in v1:
time: 255 us
  waiting for transfers between devices  164 us (64%)
  blocking collectives  41.3 us (16%)
  matrix products  18.7 us (7%)
  between operations  13.3 us (5%)
  other arithmetic  12 us (5%)
  local copies, waits for them, and re-layouts  5.44 us (2%)
    reduce_scatter x1, waiting for transfers between devices, every_expert(): lax.psum_scatter(weighted, 'expert', scatter_dimension=0, tiled=True)  68.4 us
    all_gather x1, waiting for transfers between devices, fetch_weights(): lax.all_gather(trainer_gate_up.astype(jnp.bfloat16), 'dp', axis=1, tiled=...  58.4 us
    all_gather x1, blocking collectives, every_expert(): gates_all = lax.all_gather(gates, 'expert', axis=0, tiled=True)  31.1 us
    all_gather x1, waiting for transfers between devices, fetch_weights(): lax.all_gather(trainer_down.astype(jnp.bfloat16), 'dp', axis=1, tiled=True)  25.5 us
    all_gather x1, waiting for transfers between devices, every_expert(): rows = lax.all_gather(normed, 'expert', axis=0, tiled=True)  11.9 us
    dot_general x1, matrix products, every_expert(): gate_up = jnp.dot(rows, gate_up_weights, preferred_element_type=jnp.float32)  10.6 us
    all_to_all x1, blocking collectives, local(): lax.all_to_all(attn_heads, 'dp', split_axis=1, concat_axis=2, tiled=True)  10.2 us
    dot_general x1, matrix products, every_expert(): jnp.dot(hidden_units, down_weights, preferred_element_type=jnp.float32)  7.2 us
  transfers between devices with their start and end apart: 4, of which 4 were waited for; matrix products, arithmetic and copies ran while one was open for 6% of the time, Pallas kernels for 0%

profile of v1, /device:TPU:0, one launch (start us, length us, event | category | flops | bytes accessed | tf_op | source)
XLA Modules:
  0.0 255.1 jit_solution(54704341990255140)
XLA Ops:
  6.5 0.7 compare_select_fusion
  7.3 0.7 compare_and_fusion
  7.9 0.6 gather_fusion
  8.5 1.5 gather_fusion.1
  10.0 0.1 broadcast_select_fusion.1
  10.2 0.1 reshape.114
  10.3 0.2 reduce-window.8
  10.5 0.1 convert_reduce_fusion
  10.6 0.1 broadcast_compare_fusion
  10.8 0.6 fusion.37
  11.4 0.3 convolution_convert_fusion
  11.6 0.5 copy.50
  12.1 0.5 broadcast.92
  12.6 2.2 reduce.1
  14.8 0.2 reshape.142
  15.0 10.2 %all_to_all.4 = bf16[4,2,16384]{2,1,0:T(2,128)(2,1)S(1)} all-to-all(bf16[4,2,16384]{2,1,0:T(2,128)(2,1)S(1)} %reshape.142), channel_id=1, replica_groups=mesh['dp'=4,'expert'=8] {'dp'}, dimensions={0} | all-to-all | bytes 524288 | tf_op jit(solution)/shard_map/all_to_all | solution.py:83
  25.2 0.3 reshape.143
  25.7 0.2 fusion.18
  25.9 0.8 fusion.20
  26.8 3.9 %convert_element_type.76 = bf16[1,512,2048]{2,1,0:T(8,128)(2,1)} convert(f32[1,512,2048]{2,1,0:T(8,128)} %param.22) | non-fusion elementwise | flops 1048576 | bytes 6291456 | tf_op jit(solution)/shard_map/convert_element_type | solution.py:17
  30.8 1.5 copy-done.1
  32.3 1.1 convert_element_type.78
  33.5 31.1 %all-gather.1 = f32[8,64,8]{1,2,0:T(8,128)S(1)} all-gather(f32[1,64,8]{1,2,0:T(8,128)S(1)} %bitcast.58), channel_id=1, replica_groups=mesh['dp'=4,'expert'=8] {'expert'}, dimensions={0}, use_global_device_ids=true | all-gather | bytes 18432 | tf_op jit(solution)/shard_map/all_gather | solution.py:27
  64.6 0.1 reshape.137
  64.7 0.1 select_reduce_fusion.1
  64.8 11.9 %all-gather.10.cloned.1.call-done = bf16[1,512,2048]{2,1,0:T(8,128)(2,1)} async-done(((bf16[1,64,2048]{2,1,0:T(8,128)(2,1)}), bf16[1,512,2048]{2,1,0:T(8,128)(2,1)}) %all-gather.10.cloned.1.call-update) | async-done | bytes 2097168 | tf_op jit(solution)/shard_map/all_gather | solution.py:30
  76.7 58.4 %all-gather.6.cloned.1.call-done = bf16[1,2048,2048]{2,1,0:T(8,128)(2,1)} async-done(((bf16[1,512,2048]{2,1,0:T(8,128)(2,1)}), bf16[1,2048,2048]{2,1,0:T(8,128)(2,1)}) %all-gather.6.cloned.1.call-update) | async-done | bytes 8388624 | tf_op jit(solution)/shard_map/all_gather | solution.py:17
  135.1 10.6 %fusion.1 = f32[512,2048]{1,0:T(8,128)} fusion(bf16[1,2048,2048]{2,1,0:T(8,128)(2,1)} %all-gather.6.cloned.1.call-done, bf16[1,512,2048]{2,1,0:T(8,128)(2,1)} %all-gather.10.cloned.1.call-done), kind=kOutput, calls=%fused_computation.3 | convolution fusion | flops 4294967296 | bytes 14680064 | tf_op jit(solution)/shard_map/dot_general | solution.py:31
  145.7 25.5 %all-gather.8.cloned.1.call-done = bf16[1,1024,2048]{2,1,0:T(8,128)(2,1)} async-done(((bf16[1,256,2048]{2,1,0:T(8,128)(2,1)}), bf16[1,1024,2048]{2,1,0:T(8,128)(2,1)}) %all-gather.8.cloned.1.call-update) | async-done | bytes 4194320 | tf_op jit(solution)/shard_map/all_gather | solution.py:18
  171.2 7.2 %multiply_convert_fusion = bf16[512,2048]{1,0:T(8,128)(2,1)} fusion(bf16[1,1024,2048]{2,1,0:T(8,128)(2,1)} %all-gather.8.cloned.1.call-done, f32[512]{0:T(512)S(1)} %select_reduce_fusion.1, f32[512,2048]{1,0:T(8,128)} %fusion.1), kind=kOutput, calls=%fused_computation.7 | convolution fusion | flops 2152726528 | bytes 10487808 | tf_op jit(solution)/shard_map/dot_general | solution.py:36
  178.4 68.4 %reduce-scatter.2.cloned.1.call-done = bf16[64,2048]{1,0:T(8,128)(2,1)} async-done(((bf16[512,2048]{1,0:T(8,128)(2,1)}), bf16[64,2048]{1,0:T(8,128)(2,1)}) %reduce-scatter.2.cloned.1.call-update) | async-done | bytes 262160 | tf_op jit(solution)/shard_map/reduce_scatter | solution.py:38
  246.8 1.7 fusion.21
  (33 shorter events, 0.6 us)
Async XLA Ops:
  6.5 1.4 copy-start
  6.5 3.7 %copy-start.2 = (bf16[1,256,512]{2,1,0:T(8,128)(2,1)S(1)}, bf16[1,256,512]{2,1,0:T(8,128)(2,1)}, u32[]{:S(2)}) copy-start(bf16[1,256,512]{2,1,0:T(8,128)(2,1)} %param.14) | copy-start | bytes 786436
  6.5 3.8 %copy-start.7 = (s32[1,4]{1,0:T(1,128)S(1)}, s32[1,4]{1,0:T(1,128)}, u32[]{:S(2)}) copy-start(s32[1,4]{1,0:T(1,128)} %param.18) | copy-start | bytes 52
  6.5 70.1 %all-gather.10.cloned.1.call-start = ((), (), s32[]{:S(2)}) async-start(), calls=%async_computation.5 | async-start | bytes 2359296 | tf_op jit(solution)/shard_map/all_gather | solution.py:30
  15.0 10.6 %copy-start.3 = (bf16[1,64,2048]{2,1,0:T(8,128)(2,1)S(1)}, bf16[1,64,2048]{2,1,0:T(8,128)(2,1)}, u32[]{:S(2)}) copy-start(bf16[1,64,2048]{2,1,0:T(8,128)(2,1)} %param.13) | copy-start | bytes 786436
  25.2 0.7 copy-start.4
  26.8 108.3 %all-gather.6.cloned.1.call-start = ((), (), s32[]{:S(2)}) async-start(), calls=%async_computation.2 | async-start | bytes 10485760 | tf_op jit(solution)/shard_map/all_gather | solution.py:17
  30.7 1.6 copy-start.1
  30.7 2.8 %copy-start.5 = (f32[1,64,8]{1,2,0:T(8,128)S(1)}, f32[1,64,8]{1,2,0:T(8,128)}, u32[]{:S(2)}) copy-start(f32[1,64,8]{1,2,0:T(8,128)} %param.20) | copy-start | bytes 6148
  30.7 2.8 %copy-start.6 = (s32[1,64,8]{1,2,0:T(8,128)S(1)}, s32[1,64,8]{1,2,0:T(8,128)}, u32[]{:S(2)}) copy-start(s32[1,64,8]{1,2,0:T(8,128)} %param.19) | copy-start | bytes 6148
  30.7 140.4 %all-gather.8.cloned.1.call-start = ((), (), s32[]{:S(2)}) async-start(), calls=%async_computation.3 | async-start | bytes 5242880 | tf_op jit(solution)/shard_map/all_gather | solution.py:18
  33.4 213.4 %reduce-scatter.2.cloned.1.call-start = ((), (), s32[]{:S(2)}) async-start(), calls=%async_computation.4 | async-start | bytes 2359296 | tf_op jit(solution)/shard_map/reduce_scatter | solution.py:38
Sparse Core Ops, SparseCore 0:
  26.9 49.7 all-gather.9
  78.2 56.7 all-gather.5
  136.6 34.4 all-gather.7
  178.5 68.2 reduce-scatter.1

commit v2 on v0

--- a/solution.py
+++ b/solution.py
@@ -3,6 +3,8 @@
 import jax
 import jax.numpy as jnp
 from jax import lax
+from jax.experimental import pallas as pl
+from jax.experimental.pallas import tpu as pltpu
 from jax.sharding import PartitionSpec as P
 
 HDIM = 128
@@ -107,6 +109,343 @@
     mixed = resid32[0] + mixture
     return mixed.astype(jnp.bfloat16)[None]
 
+LANES = 128
+VMEM_LIMIT = 48 * 2**20
+ROW_PIECES = 4
+COLUMN_PIECES = 4
+
+
+def params():
+    return pltpu.CompilerParams(vmem_limit_bytes=VMEM_LIMIT)
+
+
+def vmem(count):
+    return [pl.BlockSpec(memory_space=pltpu.VMEM)] * count
+
+
+def attention_kernel(table, lengths, q_ref, k_ref, v_ref, *refs):
+    outs, attn = refs[:4], refs[4]
+    tokens, width = q_ref.shape
+    pages, page = k_ref.shape[0], k_ref.shape[1]
+    row = lax.broadcasted_iota(jnp.int32, (tokens, tokens), 0)
+    column = lax.broadcasted_iota(jnp.int32, (tokens, tokens), 1)
+    row_request = jnp.zeros((tokens, tokens), jnp.int32)
+    column_request = jnp.zeros((tokens, tokens), jnp.int32)
+    end = jnp.int32(0)
+    for r in range(lengths.shape[1]):
+        end = end + lengths[0, r]
+        row_request += (row >= end).astype(jnp.int32)
+        column_request += (column >= end).astype(jnp.int32)
+    same = row_request == column_request
+    for h in range(width // HDIM):
+        lanes = slice(h * HDIM, (h + 1) * HDIM)
+        keys = jnp.concatenate([k_ref[table[0, p], :, lanes] for p in range(pages)], axis=0)
+        values = jnp.concatenate([v_ref[table[0, p], :, lanes] for p in range(pages)], axis=0)
+        scores = lax.dot_general(
+            q_ref[:, lanes], keys, (((1,), (1,)), ((), ())), preferred_element_type=jnp.float32
+        ) * (1.0 / math.sqrt(HDIM))
+        scores = jnp.where(same, scores, -1e30)
+        highest = jnp.max(scores, axis=-1, keepdims=True)
+        weights = jnp.where(same, jnp.exp(scores - highest), 0.0)
+        probs = (weights / jnp.sum(weights, axis=-1, keepdims=True)).astype(jnp.bfloat16)
+        attn[:, lanes] = jnp.dot(probs, values, preferred_element_type=jnp.float32).astype(
+            jnp.bfloat16
+        )
+    own = lax.axis_index("dp")
+    rows = tokens // 4
+    for d in range(4):
+        first = pl.multiple_of((own ^ d) * rows, rows)
+        outs[d][...] = attn[pl.ds(first, rows), :]
+
+
+def attention(queries, key_pool, value_pool, page_table, prompt_lengths):
+    tokens, width = queries.shape
+    smem = [pl.BlockSpec(memory_space=pltpu.SMEM)] * 2
+    return pl.pallas_call(
+        attention_kernel,
+        out_shape=[jax.ShapeDtypeStruct((tokens // 4, width), jnp.bfloat16)] * 4,
+        in_specs=smem + vmem(3),
+        out_specs=vmem(4),
+        scratch_shapes=[pltpu.VMEM((tokens, width), jnp.bfloat16)],
+        compiler_params=params(),
+        name="attention",
+    )(page_table, prompt_lengths, queries, key_pool, value_pool)
+
+
+def norm_kernel(hidden_ref, a0, a1, a2, a3, gain_ref, ids_ref, gates_ref, resid_ref, rows_ref):
+    own = lax.axis_index("dp")
+    tokens, width = hidden_ref.shape
+    block = width // 4
+    total = jnp.zeros((tokens, 1), jnp.float32)
+    for d, attn in enumerate((a0, a1, a2, a3)):
+        columns = pl.ds(pl.multiple_of((own ^ d) * block, block), block)
+        resid = (
+            hidden_ref[:, columns].astype(jnp.float32) + attn[...].astype(jnp.float32)
+        ).astype(jnp.bfloat16)
+        resid_ref[:, columns] = resid
+        resid32 = resid.astype(jnp.float32)
+        total += jnp.sum(resid32 * resid32, axis=-1, keepdims=True)
+    inverse = lax.rsqrt(total / width + epsilon)
+    for d in range(4):
+        columns = pl.ds(pl.multiple_of((own ^ d) * block, block), block)
+        rows_ref[:, d * block : (d + 1) * block] = (
+            resid_ref[:, columns].astype(jnp.float32) * inverse * gain_ref[:, columns]
+        ).astype(jnp.bfloat16)
+    lane = lax.broadcasted_iota(jnp.int32, (tokens, LANES), 1)
+    gates = jnp.zeros((tokens, LANES), jnp.float32)
+    for k in range(TOPK):
+        gates += jnp.where(ids_ref[:, k : k + 1] == lane % TOPK, gates_ref[:, k : k + 1], 0.0)
+    high = gates.astype(jnp.bfloat16).astype(jnp.float32)
+    middle = (gates - high).astype(jnp.bfloat16).astype(jnp.float32)
+    low = gates - high - middle
+    part = lane // TOPK
+    terms = jnp.where(part == 0, high, jnp.where(part == 1, middle, jnp.where(part == 2, low, 0.0)))
+    rows_ref[:, width:] = terms.astype(jnp.bfloat16)
+
+
+def norm(hidden_in, attn, norm_gain, expert_ids, gate_weights):
+    tokens, width = hidden_in.shape
+    return pl.pallas_call(
+        norm_kernel,
+        out_shape=[
+            jax.ShapeDtypeStruct((tokens, width), jnp.bfloat16),
+            jax.ShapeDtypeStruct((tokens, width + LANES), jnp.bfloat16),
+        ],
+        in_specs=vmem(8),
+        out_specs=vmem(2),
+        compiler_params=params(),
+        name="norm",
+    )(hidden_in, *attn, norm_gain[None, :], expert_ids, gate_weights)
+
+
+def up_kernel(sources, pieces, *refs):
+    row_refs = refs[:sources]
+    gate_refs = refs[sources : sources + 4 * pieces]
+    up_refs = refs[sources + 4 * pieces : sources + 8 * pieces]
+    hidden_ref, own_gate_ref, rows, units = refs[sources + 8 * pieces :]
+    step = pl.program_id(0)
+    width = rows.shape[1]
+    depth = width // (4 * pieces)
+
+    @pl.when(step == 0)
+    def _():
+        expert = lax.axis_index("expert")
+        first = 0
+        for ref in row_refs:
+            count = ref.shape[0]
+            rows[first : first + count, :] = ref[:, :width]
+            terms = ref[:, width:].astype(jnp.float32)
+            lane = lax.broadcasted_iota(jnp.int32, terms.shape, 1)
+            own_gate_ref[first : first + count, :] = jnp.sum(
+                jnp.where(lane % TOPK == expert, terms, 0.0), axis=-1, keepdims=True
+            )
+            first += count
+
+    def product(weights):
+        total = None
+        for i, ref in enumerate(weights):
+            term = jnp.dot(
+                rows[:, i * depth : (i + 1) * depth], ref[...], preferred_element_type=jnp.float32
+            )
+            total = term if total is None else total + term
+        return total
+
+    gate = product(gate_refs)
+    up = product(up_refs)
+    units[step] = (gate / (1.0 + jnp.exp(-gate)) * up).astype(jnp.bfloat16)
+
+    @pl.when(step == pl.num_programs(0) - 1)
+    def _():
+        own = lax.axis_index("dp")
+        block = units.shape[2]
+        for d in range(4):
+            hidden_ref[:, d * block : (d + 1) * block] = units[own ^ d]
+
+
+def expert_up(rows, weights, hidden_size):
+    tokens = sum(piece.shape[0] for piece in rows)
+    width = weights[0].shape[1]
+    depth = weights[0].shape[0]
+    features = depth * len(weights)
+    block = hidden_size // 4
+    pieces = len(weights) // 4
+    whole = [
+        pl.BlockSpec(piece.shape, lambda i: (0, 0), pipeline_mode=pl.Buffered(1)) for piece in rows
+    ]
+    gate = [pl.BlockSpec((depth, block), lambda i: (0, i))] * len(weights)
+    up = [pl.BlockSpec((depth, block), lambda i: (0, i + 4))] * len(weights)
+    return pl.pallas_call(
+        lambda *refs: up_kernel(len(rows), pieces, *refs),
+        grid=(4,),
+        out_shape=[
+            jax.ShapeDtypeStruct((tokens, hidden_size), jnp.bfloat16),
+            jax.ShapeDtypeStruct((tokens, 1), jnp.float32),
+        ],
+        in_specs=whole + gate + up,
+        out_specs=[
+            pl.BlockSpec((tokens, hidden_size), lambda i: (0, 0)),
+            pl.BlockSpec((tokens, 1), lambda i: (0, 0)),
+        ],
+        scratch_shapes=[
+            pltpu.VMEM((tokens, features), jnp.bfloat16),
+            pltpu.VMEM((4, tokens, block), jnp.bfloat16),
+        ],
+        compiler_params=params(),
+        cost_estimate=pl.CostEstimate(
+            flops=2 * tokens * features * width,
+            bytes_accessed=2 * features * width,
+            transcendentals=0,
+        ),
+        name="expert_up",
+    )(*rows, *weights, *weights)
+
+
+def down_kernel(hidden_ref, gate_ref, w0, w1, w2, w3, out_ref, left_ref, right_ref):
+    block = w0.shape[0]
+    total = None
+    for d, ref in enumerate((w0, w1, w2, w3)):
+        term = jnp.dot(
+            hidden_ref[:, d * block : (d + 1) * block],
+            ref[...],
+            preferred_element_type=jnp.float32,
+        )
+        total = term if total is None else total + term
+    weighted = (total * gate_ref[...]).astype(jnp.bfloat16)
+    sources, rows, width = out_ref.shape
+    out_ref[...] = weighted.reshape(sources, rows, width)
+    middle, half = sources // 2 * rows, rows // 2
+    left_ref[...] = weighted[middle : middle + half]
+    right_ref[...] = weighted[middle + half : middle + rows]
+
+
+def expert_down(hidden_units, gates, weights, sources):
+    tokens, hidden_size = hidden_units.shape
+    width = weights[0].shape[1]
+    rows = tokens // sources
+    return pl.pallas_call(
+        down_kernel,
+        out_shape=[
+            jax.ShapeDtypeStruct((sources, rows, width), jnp.bfloat16),
+            jax.ShapeDtypeStruct((rows // 2, width), jnp.bfloat16),
+            jax.ShapeDtypeStruct((rows // 2, width), jnp.bfloat16),
+        ],
+        in_specs=vmem(6),
+        out_specs=vmem(3),
+        compiler_params=params(),
+        cost_estimate=pl.CostEstimate(
+            flops=2 * tokens * hidden_size * width,
+            bytes_accessed=2 * (hidden_size * width + tokens * hidden_size + tokens * width),
+            transcendentals=0,
+        ),
+        name="expert_down",
+    )(hidden_units, gates, *weights)
+
+
+def partner(x, distance):
+    return lax.ppermute(x, "dp", [(i, i ^ distance) for i in range(4)])
+
+
+def ring_order(count):
+    return list(range(0, count, 2)) + list(range(count - 1, 0, -2))
+
+
+def around(x, step):
+    ring = ring_order(lax.axis_size("expert"))
+    count = len(ring)
+    return lax.ppermute(x, "expert", [(ring[i], ring[(i + step) % count]) for i in range(count)])
+
+
+def after(x, *others):
+    return lax.optimization_barrier((x, *others))[0]
+
+
+def add(a, b):
+    return (a.astype(jnp.float32) + b.astype(jnp.float32)).astype(jnp.bfloat16)
+
+
+def gather_rows(rows):
+    half = rows.shape[0] // 2
+    reach = lax.axis_size("expert") // 2
+    above, below = [rows], [rows]
+    for _ in range(reach - 1):
+        above.append(around(above[-1], -1))
+        below.append(around(below[-1], 1))
+    far = [around(above[-1][:half], -1), around(below[-1][half:], 1)]
+    return above + far + below[:0:-1]
+
+
+def scatter_sum(weighted, left, right):
+    sources, rows, _ = weighted.shape
+    half = rows // 2
+    reach = sources // 2
+    up, down = around(left, 1), around(right, -1)
+    up = jnp.concatenate([add(weighted[reach - 1, :half], up), weighted[reach - 1, half:]])
+    down = jnp.concatenate([weighted[reach + 1, :half], add(weighted[reach + 1, half:], down)])
+    for away in range(reach - 2, 0, -1):
+        up = add(weighted[away], around(up, 1))
+        down = add(weighted[sources - away], around(down, -1))
+    return weighted[0], around(up, 1), around(down, -1)
+
+
+def every_expert(
+    hidden_in,
+    queries,
+    key_pool,
+    value_pool,
+    page_table,
+    prompt_lengths,
+    expert_ids,
+    gate_weights,
+    norm_gain,
+    trainer_gate_up,
+    trainer_down,
+):
+    depth = trainer_gate_up.shape[1] // ROW_PIECES
+    slab = trainer_down.shape[2] // COLUMN_PIECES
+    up_own = [
+        trainer_gate_up[0, i * depth : (i + 1) * depth].astype(jnp.bfloat16)
+        for i in range(ROW_PIECES)
+    ]
+    down_own = [
+        trainer_down[0, :, i * slab : (i + 1) * slab].astype(jnp.bfloat16)
+        for i in range(COLUMN_PIECES)
+    ]
+    across = []
+    for i, piece in enumerate(up_own + down_own):
+        if i >= 2:
+            piece = after(piece, across[i - 2])
+        across.append(partner(piece, 2))
+    beside = [partner(piece, 1) for piece in up_own + down_own]
+    opposite = [partner(piece, 1) for piece in across]
+
+    attn = attention(queries[0], key_pool, value_pool, page_table, prompt_lengths)
+    attn = [attn[0]] + [partner(attn[d], d) for d in (1, 2, 3)]
+    resid, rows = norm(hidden_in[0], attn, norm_gain, expert_ids[0], gate_weights[0])
+    gathered = gather_rows(rows)
+    up_weights = (
+        up_own + beside[:ROW_PIECES] + across[:ROW_PIECES] + opposite[:ROW_PIECES]
+    )
+    hidden_units, gates = expert_up(gathered, up_weights, trainer_gate_up.shape[2] // 2)
+    slabs = []
+    for i in range(COLUMN_PIECES):
+        at = ROW_PIECES + i
+        weighted = expert_down(
+            hidden_units,
+            gates,
+            (down_own[i], beside[at], across[at], opposite[at]),
+            lax.axis_size("expert"),
+        )
+        own, up, down = scatter_sum(*weighted)
+        slabs.append(
+            (
+                resid[:, i * slab : (i + 1) * slab].astype(jnp.float32)
+                + own.astype(jnp.float32)
+                + up.astype(jnp.float32)
+                + down.astype(jnp.float32)
+            ).astype(jnp.bfloat16)
+        )
+    return jnp.concatenate(slabs, axis=1)[None]
+
 
 def solution(mesh):
     placed = (
@@ -122,6 +461,7 @@
         P("expert", "dp", None),
         P("expert", "dp", None),
     )
+    dense = mesh.shape["expert"] == TOPK and mesh.shape["dp"] == 4
     return jax.shard_map(
-        local, mesh=mesh, in_specs=placed, out_specs=P("expert", "dp", None), check_vma=False
-    )
+        every_expert if dense else local, mesh=mesh, in_specs=placed, out_specs=P("expert", "dp", None), check_vma=False
+    )

time: 186 us -> 178 us (0.957)
  blocking collectives: 54.5 us -> 0 us
  starting transfers between devices: 9.86 us -> 62.7 us
  waiting for transfers between devices: 67.4 us -> 89.1 us
  matrix products: 20.7 us -> 0 us
  Pallas kernels: 0 us -> 17.5 us
  between operations: 13.6 us -> 0.54 us
  local copies, waits for them, and re-layouts: 8.64 us -> 2.39 us
  other arithmetic: 10.6 us -> 5.49 us
    ppermute x0 -> x67, waiting for transfers between devices: none -> 89.1 us  [the longest x40 63.8 us: around(): lax.ppermute(x, 'expert', [(ring[i], ring[(i + step) % count]) for i in r...]
    ppermute x0 -> x67, starting transfers between devices: none -> 62.7 us  [the longest x40 47.2 us: around(): lax.ppermute(x, 'expert', [(ring[i], ring[(i + step) % count]) for i in r...]
    all_to_all x1 -> x0, blocking collectives: 54.5 us -> none  [local(): lax.all_to_all(outgoing, 'expert', split_axis=0, concat_axis=0, tiled=True)]
    all_to_all x2 -> x0, waiting for transfers between devices: 53.5 us -> none  [the longest x1 48.2 us: local(): lax.all_to_all(outputs.reshape(sources, items, features), 'expert', split...]
    dot_general x5 -> x0, matrix products: 20.1 us -> none  [the longest x1 9.47 us: local(): jnp.dot(slot_rows, server_gate_up[0], preferred_element_type=jnp.float32)]
    pallas_call x0 -> x7, Pallas kernels: none -> 17.5 us  [the longest x1 12.6 us: expert_up(): pl.pallas_call(lambda *refs: up_kernel(len(rows), pieces, *refs), grid=(4...]
    all_gather x2 -> x0, waiting for transfers between devices: 13.9 us -> none  [the longest x1 13.9 us: fetch_weights(): lax.all_gather(trainer_down.astype(jnp.bfloat16), 'dp', axis=1, tiled=True)]
    all_to_all x2 -> x0, starting transfers between devices: 9.85 us -> none  [the longest x1 5.65 us: local(): lax.all_to_all(outputs.reshape(sources, items, features), 'expert', split...]
  transfers between devices with their start and end apart: 4 -> 67, of which waited for: 3 -> 35; matrix products, arithmetic and copies ran while one was open for 12% -> 1% of each run, Pallas kernels for 0% -> 10%
where the time goes in v2:
time: 178 us
  waiting for transfers between devices  89.1 us (50%)
  starting transfers between devices  62.7 us (35%)
  Pallas kernels  17.5 us (10%)
  other arithmetic  5.49 us (3%)
  local copies, waits for them, and re-layouts  2.39 us (1%)
    ppermute x40, waiting for transfers between devices, around(): lax.ppermute(x, 'expert', [(ring[i], ring[(i + step) % count]) for i in r...  63.8 us
    ppermute x40, starting transfers between devices, around(): lax.ppermute(x, 'expert', [(ring[i], ring[(i + step) % count]) for i in r...  47.2 us
    ppermute x27, waiting for transfers between devices, partner(): return lax.ppermute(x, 'dp', [(i, i ^ distance) for i in range(4)])  25.3 us
    ppermute x27, starting transfers between devices, partner(): return lax.ppermute(x, 'dp', [(i, i ^ distance) for i in range(4)])  15.5 us
    pallas_call x1, Pallas kernels, expert_up(): pl.pallas_call(lambda *refs: up_kernel(len(rows), pieces, *refs), grid=(4...  12.6 us
    another operation x2, other arithmetic  4.23 us
  transfers between devices with their start and end apart: 67, of which 35 were waited for; matrix products, arithmetic and copies ran while one was open for 1% of the time, Pallas kernels for 10%

profile of v2, /device:TPU:0, one launch (start us, length us, event | category | flops | bytes accessed | tf_op | source)
XLA Modules:
  0.0 177.7 jit_solution(6865129871003975920)
XLA Ops:
  0.0 2.5 %convert.40 = bf16[1,512,2048]{2,1,0:T(8,128)(2,1)S(1)} convert(f32[1,512,2048]{2,1,0:T(8,128)} %param.20) | non-fusion elementwise | flops 1048576 | bytes 6291456 | tf_op jit(solution)/shard_map/convert.35
  2.8 3.0 %collective-permute-start.16 = (bf16[128,2048]{1,0:T(8,128)(2,1)S(1)}, bf16[128,2048]{1,0:T(8,128)(2,1)S(1)}, u32[]{:S(2)}, u32[]{:S(2)}) collective-permute-start(bf16[128,2048]{1,0:T(8,128)(2,1)S(1)} %get-tuple-element.59.refs_10_.refs_26_), channel_id=1, source_target_pairs={{0,16},{8,24},{16,0},{24,8},{1,17},{9,25},{17,1},{25,9},{2,18},{10... | collective-permute-start | bytes 1572872 | tf_op jit(solution)/shard_map/ppermute | solution.py:345
  10.4 9.6 %collective-permute-done.1.a2 = bf16[64,512]{1,0:T(8,128)(2,1)S(1)} collective-permute-done((bf16[64,512]{1,0:T(8,128)(2,1)S(1)}, bf16[64,512]{1,0:T(8,128)(2,1)S(1)}, u32[]{:S(2)}, u32[]{:S(2)}) %collective-permute-start.1) | collective-permute-done | bytes 65568 | tf_op jit(solution)/shard_map/ppermute | solution.py:345
  23.8 6.7 %collective-permute-done.7.refs_8_ = bf16[64,2176]{1,0:T(8,128)(2,1)S(1)} collective-permute-done((bf16[64,2176]{1,0:T(8,128)(2,1)S(1)}, bf16[64,2176]{1,0:T(8,128)(2,1)S(1)}, u32[]{:S(2)}, u32[]{:S(2)}) %collective-permute-start.7) | collective-permute-done | bytes 278560 | tf_op jit(solution)/shard_map/ppermute | solution.py:355
  34.6 5.9 %collective-permute-done.8.refs_7_ = bf16[64,2176]{1,0:T(8,128)(2,1)S(1)} collective-permute-done((bf16[64,2176]{1,0:T(8,128)(2,1)S(1)}, bf16[64,2176]{1,0:T(8,128)(2,1)S(1)}, u32[]{:S(2)}, u32[]{:S(2)}) %collective-permute-start.8) | collective-permute-done | bytes 278560 | tf_op jit(solution)/shard_map/ppermute | solution.py:355
  52.3 4.3 %collective-permute-done.17.refs_19_.refs_35_ = bf16[128,2048]{1,0:T(8,128)(2,1)S(1)} collective-permute-done((bf16[128,2048]{1,0:T(8,128)(2,1)S(1)}, bf16[128,2048]{1,0:T(8,128)(2,1)S(1)}, u32[]{:S(2)}, u32[]{:S(2)}) %collective-permute-start.17) | collective-permute-done | bytes 524320 | tf_op jit(solution)/shard_map/ppermute | solution.py:345
  57.1 4.1 %collective-permute-done.35.w2 = bf16[256,512]{1,0:T(8,128)(2,1)S(1)} collective-permute-done((bf16[256,512]{1,0:T(8,128)(2,1)S(1)}, bf16[256,512]{1,0:T(8,128)(2,1)S(1)}, u32[]{:S(2)}, u32[]{:S(2)}) %collective-permute-start.35) | collective-permute-done | bytes 262176 | tf_op jit(solution)/shard_map/ppermute | solution.py:345
  62.9 6.1 %collective-permute-done.24.w2 = bf16[256,512]{1,0:T(8,128)(2,1)S(1)} collective-permute-done((bf16[256,512]{1,0:T(8,128)(2,1)S(1)}, bf16[256,512]{1,0:T(8,128)(2,1)S(1)}, u32[]{:S(2)}, u32[]{:S(2)}) %collective-permute-start.24) | collective-permute-done | bytes 262176 | tf_op jit(solution)/shard_map/ppermute | solution.py:345
  70.6 3.5 %collective-permute-done.6.refs_4_ = bf16[32,2176]{1,0:T(8,128)(2,1)S(1)} collective-permute-done((bf16[32,2176]{1,0:T(8,128)(2,1)S(1)}, bf16[32,2176]{1,0:T(8,128)(2,1)S(1)}, u32[]{:S(2)}, u32[]{:S(2)}) %collective-permute-start.6) | collective-permute-done | bytes 139296 | tf_op jit(solution)/shard_map/ppermute | solution.py:355
  77.3 12.6 %expert_up.1 = (bf16[512,1024]{1,0:T(8,128)(2,1)}, f32[512,1]{1,0:T(8,128)S(1)}) custom-call(bf16[64,2176]{1,0:T(8,128)(2,1)S(1)} %get-tuple-element.36.refs_0_, bf16[64,2176]{1,0:T(8,128)(2,1)S(1)} %collective-permute-done.3.refs_1_, bf16[64,2176]{1,0:T(8,128)(2,1)S(1)} %collective-permute-done.4.refs_2_, ...), custom_call_target="tpu_custom_call" | custom-call | flops 4294967296 | bytes 8388608 | tf_op jit(solution)/shard_map/expert_up/pallas_call | solution.py:277
  103.7 3.1 %collective-permute-done.38 = bf16[64,512]{1,0:T(8,128)(2,1)S(1)} collective-permute-done((bf16[64,512]{1,0:T(8,128)(2,1)S(1)}, bf16[64,512]{1,0:T(8,128)(2,1)S(1)}, u32[]{:S(2)}, u32[]{:S(2)}) %collective-permute-start.38) | collective-permute-done | bytes 65568 | tf_op jit(solution)/shard_map/ppermute | solution.py:355
  108.4 2.7 %collective-permute-done.27 = bf16[64,512]{1,0:T(8,128)(2,1)S(1)} collective-permute-done((bf16[64,512]{1,0:T(8,128)(2,1)S(1)}, bf16[64,512]{1,0:T(8,128)(2,1)S(1)}, u32[]{:S(2)}, u32[]{:S(2)}) %collective-permute-start.27) | collective-permute-done | bytes 65568 | tf_op jit(solution)/shard_map/ppermute | solution.py:355
  113.2 2.2 %collective-permute-done.39 = bf16[64,512]{1,0:T(8,128)(2,1)S(1)} collective-permute-done((bf16[64,512]{1,0:T(8,128)(2,1)S(1)}, bf16[64,512]{1,0:T(8,128)(2,1)S(1)}, u32[]{:S(2)}, u32[]{:S(2)}) %collective-permute-start.39) | collective-permute-done | bytes 65568 | tf_op jit(solution)/shard_map/ppermute | solution.py:355
  117.6 2.0 %collective-permute-done.28 = bf16[64,512]{1,0:T(8,128)(2,1)S(1)} collective-permute-done((bf16[64,512]{1,0:T(8,128)(2,1)S(1)}, bf16[64,512]{1,0:T(8,128)(2,1)S(1)}, u32[]{:S(2)}, u32[]{:S(2)}) %collective-permute-start.28) | collective-permute-done | bytes 65568 | tf_op jit(solution)/shard_map/ppermute | solution.py:355
  120.8 3.3 %collective-permute-done.43 = bf16[64,512]{1,0:T(8,128)(2,1)S(1)} collective-permute-done((bf16[64,512]{1,0:T(8,128)(2,1)S(1)}, bf16[64,512]{1,0:T(8,128)(2,1)S(1)}, u32[]{:S(2)}, u32[]{:S(2)}) %collective-permute-start.43) | collective-permute-done | bytes 65568 | tf_op jit(solution)/shard_map/ppermute | solution.py:355
  125.6 2.6 %collective-permute-done.32 = bf16[64,512]{1,0:T(8,128)(2,1)S(1)} collective-permute-done((bf16[64,512]{1,0:T(8,128)(2,1)S(1)}, bf16[64,512]{1,0:T(8,128)(2,1)S(1)}, u32[]{:S(2)}, u32[]{:S(2)}) %collective-permute-start.32) | collective-permute-done | bytes 65568 | tf_op jit(solution)/shard_map/ppermute | solution.py:355
  129.9 2.0 %collective-permute-start.29 = (bf16[64,512]{1,0:T(8,128)(2,1)S(1)}, bf16[64,512]{1,0:T(8,128)(2,1)S(1)}, u32[]{:S(2)}, u32[]{:S(2)}) collective-permute-start(bf16[64,512]{1,0:T(8,128)(2,1)S(1)} %get-tuple-element.65), channel_id=1, source_target_pairs={{0,2},{2,4},{4,6},{6,7},{7,5},{5,3},{3,1},{1,0},{8,10},{10,12},{12... | collective-permute-start | bytes 196616 | tf_op jit(solution)/shard_map/ppermute | solution.py:355
  132.7 2.0 %collective-permute-start.48 = (bf16[32,512]{1,0:T(8,128)(2,1)S(1)}, bf16[32,512]{1,0:T(8,128)(2,1)S(1)}, u32[]{:S(2)}, u32[]{:S(2)}) collective-permute-start(bf16[32,512]{1,0:T(8,128)(2,1)S(1)} %get-tuple-element.51), channel_id=1, source_target_pairs={{0,2},{2,4},{4,6},{6,7},{7,5},{5,3},{3,1},{1,0},{8,10},{10,12},{12... | collective-permute-start | bytes 98312 | tf_op jit(solution)/shard_map/ppermute | solution.py:355
  136.7 2.1 %collective-permute-start.59 = (bf16[32,512]{1,0:T(8,128)(2,1)S(1)}, bf16[32,512]{1,0:T(8,128)(2,1)S(1)}, u32[]{:S(2)}, u32[]{:S(2)}) collective-permute-start(bf16[32,512]{1,0:T(8,128)(2,1)S(1)} %get-tuple-element.55), channel_id=1, source_target_pairs={{0,2},{2,4},{4,6},{6,7},{7,5},{5,3},{3,1},{1,0},{8,10},{10,12},{12... | collective-permute-start | bytes 98312 | tf_op jit(solution)/shard_map/ppermute | solution.py:355
  144.5 2.4 %collective-permute-done.49 = bf16[64,512]{1,0:T(8,128)(2,1)S(1)} collective-permute-done((bf16[64,512]{1,0:T(8,128)(2,1)S(1)}, bf16[64,512]{1,0:T(8,128)(2,1)S(1)}, u32[]{:S(2)}, u32[]{:S(2)}) %collective-permute-start.49) | collective-permute-done | bytes 65568 | tf_op jit(solution)/shard_map/ppermute | solution.py:355
  147.0 2.2 %collective-permute-start.60 = (bf16[64,512]{1,0:T(8,128)(2,1)S(1)}, bf16[64,512]{1,0:T(8,128)(2,1)S(1)}, u32[]{:S(2)}, u32[]{:S(2)}) collective-permute-start(bf16[64,512]{1,0:T(8,128)(2,1)S(1)} %pad_maximum_fusion.6), channel_id=1, source_target_pairs={{0,2},{2,4},{4,6},{6,7},{7,5},{5,3},{3,1},{1,0},{8,10},{10,12},{12... | collective-permute-start | bytes 196616 | tf_op jit(solution)/shard_map/ppermute | solution.py:355
  149.2 2.0 %collective-permute-done.60 = bf16[64,512]{1,0:T(8,128)(2,1)S(1)} collective-permute-done((bf16[64,512]{1,0:T(8,128)(2,1)S(1)}, bf16[64,512]{1,0:T(8,128)(2,1)S(1)}, u32[]{:S(2)}, u32[]{:S(2)}) %collective-permute-start.60) | collective-permute-done | bytes 65568 | tf_op jit(solution)/shard_map/ppermute | solution.py:355
  151.2 2.2 %collective-permute-start.50 = (bf16[64,512]{1,0:T(8,128)(2,1)S(1)}, bf16[64,512]{1,0:T(8,128)(2,1)S(1)}, u32[]{:S(2)}, u32[]{:S(2)}) collective-permute-start(bf16[64,512]{1,0:T(8,128)(2,1)S(1)} %fusion.9), channel_id=1, source_target_pairs={{0,2},{2,4},{4,6},{6,7},{7,5},{5,3},{3,1},{1,0},{8,10},{10,12},{12... | collective-permute-start | bytes 196616 | tf_op jit(solution)/shard_map/ppermute | solution.py:355
  153.5 2.0 %collective-permute-done.50 = bf16[64,512]{1,0:T(8,128)(2,1)S(1)} collective-permute-done((bf16[64,512]{1,0:T(8,128)(2,1)S(1)}, bf16[64,512]{1,0:T(8,128)(2,1)S(1)}, u32[]{:S(2)}, u32[]{:S(2)}) %collective-permute-start.50) | collective-permute-done | bytes 65568 | tf_op jit(solution)/shard_map/ppermute | solution.py:355
  155.5 2.2 %collective-permute-start.61 = (bf16[64,512]{1,0:T(8,128)(2,1)S(1)}, bf16[64,512]{1,0:T(8,128)(2,1)S(1)}, u32[]{:S(2)}, u32[]{:S(2)}) collective-permute-start(bf16[64,512]{1,0:T(8,128)(2,1)S(1)} %fusion.2), channel_id=1, source_target_pairs={{0,2},{2,4},{4,6},{6,7},{7,5},{5,3},{3,1},{1,0},{8,10},{10,12},{12... | collective-permute-start | bytes 196616 | tf_op jit(solution)/shard_map/ppermute | solution.py:355
  157.8 1.9 %collective-permute-done.61 = bf16[64,512]{1,0:T(8,128)(2,1)S(1)} collective-permute-done((bf16[64,512]{1,0:T(8,128)(2,1)S(1)}, bf16[64,512]{1,0:T(8,128)(2,1)S(1)}, u32[]{:S(2)}, u32[]{:S(2)}) %collective-permute-start.61) | collective-permute-done | bytes 65568 | tf_op jit(solution)/shard_map/ppermute | solution.py:355
  160.3 3.9 %collective-permute-done.54 = bf16[64,512]{1,0:T(8,128)(2,1)S(1)} collective-permute-done((bf16[64,512]{1,0:T(8,128)(2,1)S(1)}, bf16[64,512]{1,0:T(8,128)(2,1)S(1)}, u32[]{:S(2)}, u32[]{:S(2)}) %collective-permute-start.54) | collective-permute-done | bytes 65568 | tf_op jit(solution)/shard_map/ppermute | solution.py:355
  164.6 3.9 %collective-permute-done.65 = bf16[64,512]{1,0:T(8,128)(2,1)S(1)} collective-permute-done((bf16[64,512]{1,0:T(8,128)(2,1)S(1)}, bf16[64,512]{1,0:T(8,128)(2,1)S(1)}, u32[]{:S(2)}, u32[]{:S(2)}) %collective-permute-start.65) | collective-permute-done | bytes 65568 | tf_op jit(solution)/shard_map/ppermute | solution.py:355
  168.5 2.0 %collective-permute-start.51 = (bf16[64,512]{1,0:T(8,128)(2,1)S(1)}, bf16[64,512]{1,0:T(8,128)(2,1)S(1)}, u32[]{:S(2)}, u32[]{:S(2)}) collective-permute-start(bf16[64,512]{1,0:T(8,128)(2,1)S(1)} %get-tuple-element.77), channel_id=1, source_target_pairs={{0,2},{2,4},{4,6},{6,7},{7,5},{5,3},{3,1},{1,0},{8,10},{10,12},{12... | collective-permute-start | bytes 196616 | tf_op jit(solution)/shard_map/ppermute | solution.py:355
  170.6 2.0 %collective-permute-start.55 = (bf16[64,512]{1,0:T(8,128)(2,1)S(1)}, bf16[64,512]{1,0:T(8,128)(2,1)S(1)}, u32[]{:S(2)}, u32[]{:S(2)}) collective-permute-start(bf16[64,512]{1,0:T(8,128)(2,1)S(1)} %fusion.8), channel_id=1, source_target_pairs={{0,1},{2,0},{4,2},{6,4},{7,6},{5,7},{3,5},{1,3},{8,9},{10,8},{12,1... | collective-permute-start | bytes 196616 | tf_op jit(solution)/shard_map/ppermute | solution.py:355
  172.7 2.1 %collective-permute-done.62 = bf16[64,512]{1,0:T(8,128)(2,1)S(1)} collective-permute-done((bf16[64,512]{1,0:T(8,128)(2,1)S(1)}, bf16[64,512]{1,0:T(8,128)(2,1)S(1)}, u32[]{:S(2)}, u32[]{:S(2)}) %collective-permute-start.62) | collective-permute-done | bytes 65568 | tf_op jit(solution)/shard_map/ppermute | solution.py:355
  174.9 2.0 %collective-permute-done.66 = bf16[64,512]{1,0:T(8,128)(2,1)S(1)} collective-permute-done((bf16[64,512]{1,0:T(8,128)(2,1)S(1)}, bf16[64,512]{1,0:T(8,128)(2,1)S(1)}, u32[]{:S(2)}, u32[]{:S(2)}) %collective-permute-start.66) | collective-permute-done | bytes 65568 | tf_op jit(solution)/shard_map/ppermute | solution.py:355
  (183 shorter events, 66.2 us)
Async XLA Ops:
  2.8 21.0 %collective-permute-start.16 = (bf16[128,2048]{1,0:T(8,128)(2,1)S(1)}, bf16[128,2048]{1,0:T(8,128)(2,1)S(1)}, u32[]{:S(2)}, u32[]{:S(2)}) collective-permute-start(bf16[128,2048]{1,0:T(8,128)(2,1)S(1)} %get-tuple-element.59.refs_10_.refs_26_), channel_id=1, source_target_pairs={{0,16},{8,24},{16,0},{24,8},{1,17},{9,25},{17,1},{25,9},{2,18},{10... | collective-permute-start | bytes 1572872 | tf_op jit(solution)/shard_map/ppermute | solution.py:345
  7.6 12.3 %collective-permute-start.1 = (bf16[64,512]{1,0:T(8,128)(2,1)S(1)}, bf16[64,512]{1,0:T(8,128)(2,1)S(1)}, u32[]{:S(2)}, u32[]{:S(2)}) collective-permute-start(bf16[64,512]{1,0:T(8,128)(2,1)S(1)} %get-tuple-element.33), channel_id=1, source_target_pairs={{0,16},{8,24},{16,0},{24,8},{1,17},{9,25},{17,1},{25,9},{2,18},{10... | collective-permute-start | bytes 196616 | tf_op jit(solution)/shard_map/ppermute | solution.py:345
  8.4 12.5 %collective-permute-start.2 = (bf16[64,512]{1,0:T(8,128)(2,1)S(1)}, bf16[64,512]{1,0:T(8,128)(2,1)S(1)}, u32[]{:S(2)}, u32[]{:S(2)}) collective-permute-start(bf16[64,512]{1,0:T(8,128)(2,1)S(1)} %get-tuple-element.34), channel_id=1, source_target_pairs={{0,24},{8,16},{16,8},{24,0},{1,25},{9,17},{17,9},{25,1},{2,26},{10... | collective-permute-start | bytes 196616 | tf_op jit(solution)/shard_map/ppermute | solution.py:345
  9.5 24.2 %collective-permute-start.15 = (bf16[128,2048]{1,0:T(8,128)(2,1)S(1)}, bf16[128,2048]{1,0:T(8,128)(2,1)}, u32[]{:S(2)}, u32[]{:S(2)}) collective-permute-start(bf16[128,2048]{1,0:T(8,128)(2,1)S(1)} %get-tuple-element.60.refs_9_.refs_25_), channel_id=1, source_target_pairs={{0,16},{8,24},{16,0},{24,8},{1,17},{9,25},{17,1},{25,9},{2,18},{10... | collective-permute-start | bytes 1572872 | tf_op jit(solution)/shard_map/ppermute | solution.py:345
  21.3 9.2 %collective-permute-start.7 = (bf16[64,2176]{1,0:T(8,128)(2,1)S(1)}, bf16[64,2176]{1,0:T(8,128)(2,1)S(1)}, u32[]{:S(2)}, u32[]{:S(2)}) collective-permute-start(bf16[64,2176]{1,0:T(8,128)(2,1)S(1)} %get-tuple-element.36.refs_0_), channel_id=1, source_target_pairs={{0,2},{2,4},{4,6},{6,7},{7,5},{5,3},{3,1},{1,0},{8,10},{10,12},{12... | collective-permute-start | bytes 835592 | tf_op jit(solution)/shard_map/ppermute | solution.py:355
  23.0 11.1 %collective-permute-start.11 = (bf16[128,2048]{1,0:T(8,128)(2,1)S(1)}, bf16[128,2048]{1,0:T(8,128)(2,1)S(1)}, u32[]{:S(2)}, u32[]{:S(2)}) collective-permute-start(bf16[128,2048]{1,0:T(8,128)(2,1)S(1)} %get-tuple-element.60.refs_9_.refs_25_), channel_id=1, source_target_pairs={{0,8},{8,0},{16,24},{24,16},{1,9},{9,1},{17,25},{25,17},{2,10},{10... | collective-permute-start | bytes 1572872 | tf_op jit(solution)/shard_map/ppermute | solution.py:345
  23.5 8.6 %collective-permute-start.3 = (bf16[64,2176]{1,0:T(8,128)(2,1)S(1)}, bf16[64,2176]{1,0:T(8,128)(2,1)S(1)}, u32[]{:S(2)}, u32[]{:S(2)}) collective-permute-start(bf16[64,2176]{1,0:T(8,128)(2,1)S(1)} %get-tuple-element.36.refs_0_), channel_id=1, source_target_pairs={{0,1},{2,0},{4,2},{6,4},{7,6},{5,7},{3,5},{1,3},{8,9},{10,8},{12,1... | collective-permute-start | bytes 835592 | tf_op jit(solution)/shard_map/ppermute | solution.py:355
  23.8 10.3 %collective-permute-start.12 = (bf16[128,2048]{1,0:T(8,128)(2,1)S(1)}, bf16[128,2048]{1,0:T(8,128)(2,1)S(1)}, u32[]{:S(2)}, u32[]{:S(2)}) collective-permute-start(bf16[128,2048]{1,0:T(8,128)(2,1)S(1)} %get-tuple-element.59.refs_10_.refs_26_), channel_id=1, source_target_pairs={{0,8},{8,0},{16,24},{24,16},{1,9},{9,1},{17,25},{25,17},{2,10},{10... | collective-permute-start | bytes 1572872 | tf_op jit(solution)/shard_map/ppermute | solution.py:345
  30.6 14.8 %collective-permute-start.18 = (bf16[128,2048]{1,0:T(8,128)(2,1)S(1)}, bf16[128,2048]{1,0:T(8,128)(2,1)S(1)}, u32[]{:S(2)}, u32[]{:S(2)}) collective-permute-start(bf16[128,2048]{1,0:T(8,128)(2,1)S(1)} %get-tuple-element.38.refs_12_.refs_28_), channel_id=1, source_target_pairs={{0,16},{8,24},{16,0},{24,8},{1,17},{9,25},{17,1},{25,9},{2,18},{10... | collective-permute-start | bytes 1572872 | tf_op jit(solution)/shard_map/ppermute | solution.py:345
  34.1 15.9 %collective-permute-start.13 = (bf16[128,2048]{1,0:T(8,128)(2,1)S(1)}, bf16[128,2048]{1,0:T(8,128)(2,1)S(1)}, u32[]{:S(2)}, u32[]{:S(2)}) collective-permute-start(bf16[128,2048]{1,0:T(8,128)(2,1)S(1)} %get-tuple-element.37.refs_11_.refs_27_), channel_id=1, source_target_pairs={{0,8},{8,0},{16,24},{24,16},{1,9},{9,1},{17,25},{25,17},{2,10},{10... | collective-permute-start | bytes 1572872 | tf_op jit(solution)/shard_map/ppermute | solution.py:345
  34.1 17.4 %collective-permute-start.14 = (bf16[128,2048]{1,0:T(8,128)(2,1)S(1)}, bf16[128,2048]{1,0:T(8,128)(2,1)S(1)}, u32[]{:S(2)}, u32[]{:S(2)}) collective-permute-start(bf16[128,2048]{1,0:T(8,128)(2,1)S(1)} %get-tuple-element.38.refs_12_.refs_28_), channel_id=1, source_target_pairs={{0,8},{8,0},{16,24},{24,16},{1,9},{9,1},{17,25},{25,17},{2,10},{10... | collective-permute-start | bytes 1572872 | tf_op jit(solution)/shard_map/ppermute | solution.py:345
  40.5 16.1 %collective-permute-start.17 = (bf16[128,2048]{1,0:T(8,128)(2,1)S(1)}, bf16[128,2048]{1,0:T(8,128)(2,1)S(1)}, u32[]{:S(2)}, u32[]{:S(2)}) collective-permute-start(bf16[128,2048]{1,0:T(8,128)(2,1)S(1)} %get-tuple-element.37.refs_11_.refs_27_), channel_id=1, source_target_pairs={{0,16},{8,24},{16,0},{24,8},{1,17},{9,25},{17,1},{25,9},{2,18},{10... | collective-permute-start | bytes 1572872 | tf_op jit(solution)/shard_map/ppermute | solution.py:345
  49.1 12.1 %collective-permute-start.35 = (bf16[256,512]{1,0:T(8,128)(2,1)S(1)}, bf16[256,512]{1,0:T(8,128)(2,1)S(1)}, u32[]{:S(2)}, u32[]{:S(2)}) collective-permute-start(bf16[256,512]{1,0:T(8,128)(2,1)S(1)} %get-tuple-element.45.w0), channel_id=1, source_target_pairs={{0,16},{8,24},{16,0},{24,8},{1,17},{9,25},{17,1},{25,9},{2,18},{10... | collective-permute-start | bytes 786440 | tf_op jit(solution)/shard_map/ppermute | solution.py:345
  51.5 22.6 %collective-permute-start.19 = (bf16[128,2048]{1,0:T(8,128)(2,1)}, bf16[128,2048]{1,0:T(8,128)(2,1)S(1)}, u32[]{:S(2)}, u32[]{:S(2)}) collective-permute-start(bf16[128,2048]{1,0:T(8,128)(2,1)} %collective-permute-done.15.refs_17_.refs_33_), channel_id=1, source_target_pairs={{0,8},{8,0},{16,24},{24,16},{1,9},{9,1},{17,25},{25,17},{2,10},{10... | collective-permute-start | bytes 1572872 | tf_op jit(solution)/shard_map/ppermute | solution.py:345
  52.3 22.4 %collective-permute-start.20 = (bf16[128,2048]{1,0:T(8,128)(2,1)S(1)}, bf16[128,2048]{1,0:T(8,128)(2,1)S(1)}, u32[]{:S(2)}, u32[]{:S(2)}) collective-permute-start(bf16[128,2048]{1,0:T(8,128)(2,1)S(1)} %collective-permute-done.16.refs_18_.refs_34_), channel_id=1, source_target_pairs={{0,8},{8,0},{16,24},{24,16},{1,9},{9,1},{17,25},{25,17},{2,10},{10... | collective-permute-start | bytes 1572872 | tf_op jit(solution)/shard_map/ppermute | solution.py:345
  56.6 18.2 %collective-permute-start.21 = (bf16[128,2048]{1,0:T(8,128)(2,1)S(1)}, bf16[128,2048]{1,0:T(8,128)(2,1)S(1)}, u32[]{:S(2)}, u32[]{:S(2)}) collective-permute-start(bf16[128,2048]{1,0:T(8,128)(2,1)S(1)} %collective-permute-done.17.refs_19_.refs_35_), channel_id=1, source_target_pairs={{0,8},{8,0},{16,24},{24,16},{1,9},{9,1},{17,25},{25,17},{2,10},{10... | collective-permute-start | bytes 1572872 | tf_op jit(solution)/shard_map/ppermute | solution.py:345
  56.6 19.9 %collective-permute-start.22 = (bf16[128,2048]{1,0:T(8,128)(2,1)S(1)}, bf16[128,2048]{1,0:T(8,128)(2,1)S(1)}, u32[]{:S(2)}, u32[]{:S(2)}) collective-permute-start(bf16[128,2048]{1,0:T(8,128)(2,1)S(1)} %collective-permute-done.18.refs_20_.refs_36_), channel_id=1, source_target_pairs={{0,8},{8,0},{16,24},{24,16},{1,9},{9,1},{17,25},{25,17},{2,10},{10... | collective-permute-start | bytes 1572872 | tf_op jit(solution)/shard_map/ppermute | solution.py:345
  74.1 15.8 %collective-permute-start.34 = (bf16[256,512]{1,0:T(8,128)(2,1)S(1)}, bf16[256,512]{1,0:T(8,128)(2,1)S(1)}, u32[]{:S(2)}, u32[]{:S(2)}) collective-permute-start(bf16[256,512]{1,0:T(8,128)(2,1)S(1)} %get-tuple-element.45.w0), channel_id=1, source_target_pairs={{0,8},{8,0},{16,24},{24,16},{1,9},{9,1},{17,25},{25,17},{2,10},{10... | collective-permute-start | bytes 786440 | tf_op jit(solution)/shard_map/ppermute | solution.py:345
  74.1 55.8 %collective-permute-start.45 = (bf16[256,512]{1,0:T(8,128)(2,1)S(1)}, bf16[256,512]{1,0:T(8,128)(2,1)S(1)}, u32[]{:S(2)}, u32[]{:S(2)}) collective-permute-start(bf16[256,512]{1,0:T(8,128)(2,1)S(1)} %get-tuple-element.49.w0), channel_id=1, source_target_pairs={{0,8},{8,0},{16,24},{24,16},{1,9},{9,1},{17,25},{25,17},{2,10},{10... | collective-permute-start | bytes 786440 | tf_op jit(solution)/shard_map/ppermute | solution.py:345
  74.6 17.6 %collective-permute-start.23 = (bf16[256,512]{1,0:T(8,128)(2,1)S(1)}, bf16[256,512]{1,0:T(8,128)(2,1)S(1)}, u32[]{:S(2)}, u32[]{:S(2)}) collective-permute-start(bf16[256,512]{1,0:T(8,128)(2,1)S(1)} %get-tuple-element.41.w0), channel_id=1, source_target_pairs={{0,8},{8,0},{16,24},{24,16},{1,9},{9,1},{17,25},{25,17},{2,10},{10... | collective-permute-start | bytes 786440 | tf_op jit(solution)/shard_map/ppermute | solution.py:345
  74.7 42.2 %collective-permute-start.46 = (bf16[256,512]{1,0:T(8,128)(2,1)S(1)}, bf16[256,512]{1,0:T(8,128)(2,1)S(1)}, u32[]{:S(2)}, u32[]{:S(2)}) collective-permute-start(bf16[256,512]{1,0:T(8,128)(2,1)S(1)} %get-tuple-element.49.w0), channel_id=1, source_target_pairs={{0,16},{8,24},{16,0},{24,8},{1,17},{9,25},{17,1},{25,9},{2,18},{10... | collective-permute-start | bytes 786440 | tf_op jit(solution)/shard_map/ppermute | solution.py:345
  76.5 13.8 %collective-permute-start.36 = (bf16[256,512]{1,0:T(8,128)(2,1)S(1)}, bf16[256,512]{1,0:T(8,128)(2,1)S(1)}, u32[]{:S(2)}, u32[]{:S(2)}) collective-permute-start(bf16[256,512]{1,0:T(8,128)(2,1)S(1)} %collective-permute-done.35.w2), channel_id=1, source_target_pairs={{0,8},{8,0},{16,24},{24,16},{1,9},{9,1},{17,25},{25,17},{2,10},{10... | collective-permute-start | bytes 786440 | tf_op jit(solution)/shard_map/ppermute | solution.py:345
  89.9 27.1 %collective-permute-start.57 = (bf16[256,512]{1,0:T(8,128)(2,1)S(1)}, bf16[256,512]{1,0:T(8,128)(2,1)S(1)}, u32[]{:S(2)}, u32[]{:S(2)}) collective-permute-start(bf16[256,512]{1,0:T(8,128)(2,1)S(1)} %get-tuple-element.53.w0), channel_id=1, source_target_pairs={{0,16},{8,24},{16,0},{24,8},{1,17},{9,25},{17,1},{25,9},{2,18},{10... | collective-permute-start | bytes 786440 | tf_op jit(solution)/shard_map/ppermute | solution.py:345
  100.2 12.5 %collective-permute-start.42 = (bf16[64,512]{1,0:T(8,128)(2,1)S(1)}, bf16[64,512]{1,0:T(8,128)(2,1)S(1)}, u32[]{:S(2)}, u32[]{:S(2)}) collective-permute-start(bf16[64,512]{1,0:T(8,128)(2,1)S(1)} %pad_maximum_fusion.3), channel_id=1, source_target_pairs={{0,1},{2,0},{4,2},{6,4},{7,6},{5,7},{3,5},{1,3},{8,9},{10,8},{12,1... | collective-permute-start | bytes 196616 | tf_op jit(solution)/shard_map/ppermute | solution.py:355
  117.0 15.8 %collective-permute-start.56 = (bf16[256,512]{1,0:T(8,128)(2,1)S(1)}, bf16[256,512]{1,0:T(8,128)(2,1)S(1)}, u32[]{:S(2)}, u32[]{:S(2)}) collective-permute-start(bf16[256,512]{1,0:T(8,128)(2,1)S(1)} %get-tuple-element.53.w0), channel_id=1, source_target_pairs={{0,8},{8,0},{16,24},{24,16},{1,9},{9,1},{17,25},{25,17},{2,10},{10... | collective-permute-start | bytes 786440 | tf_op jit(solution)/shard_map/ppermute | solution.py:345
  117.1 14.8 %collective-permute-start.47 = (bf16[256,512]{1,0:T(8,128)(2,1)S(1)}, bf16[256,512]{1,0:T(8,128)(2,1)S(1)}, u32[]{:S(2)}, u32[]{:S(2)}) collective-permute-start(bf16[256,512]{1,0:T(8,128)(2,1)S(1)} %collective-permute-done.46.w2), channel_id=1, source_target_pairs={{0,8},{8,0},{16,24},{24,16},{1,9},{9,1},{17,25},{25,17},{2,10},{10... | collective-permute-start | bytes 786440 | tf_op jit(solution)/shard_map/ppermute | solution.py:345
  117.5 17.1 %collective-permute-start.58 = (bf16[256,512]{1,0:T(8,128)(2,1)S(1)}, bf16[256,512]{1,0:T(8,128)(2,1)S(1)}, u32[]{:S(2)}, u32[]{:S(2)}) collective-permute-start(bf16[256,512]{1,0:T(8,128)(2,1)S(1)} %collective-permute-done.57.w2), channel_id=1, source_target_pairs={{0,8},{8,0},{16,24},{24,16},{1,9},{9,1},{17,25},{25,17},{2,10},{10... | collective-permute-start | bytes 786440 | tf_op jit(solution)/shard_map/ppermute | solution.py:345
  128.3 42.2 %collective-permute-start.40 = (bf16[64,512]{1,0:T(8,128)(2,1)S(1)}, bf16[64,512]{1,0:T(8,128)(2,1)S(1)}, u32[]{:S(2)}, u32[]{:S(2)}) collective-permute-start(bf16[64,512]{1,0:T(8,128)(2,1)S(1)} %get-tuple-element.71), channel_id=1, source_target_pairs={{0,2},{2,4},{4,6},{6,7},{7,5},{5,3},{3,1},{1,0},{8,10},{10,12},{12... | collective-permute-start | bytes 196616 | tf_op jit(solution)/shard_map/ppermute | solution.py:355
  129.9 40.7 %collective-permute-start.29 = (bf16[64,512]{1,0:T(8,128)(2,1)S(1)}, bf16[64,512]{1,0:T(8,128)(2,1)S(1)}, u32[]{:S(2)}, u32[]{:S(2)}) collective-permute-start(bf16[64,512]{1,0:T(8,128)(2,1)S(1)} %get-tuple-element.65), channel_id=1, source_target_pairs={{0,2},{2,4},{4,6},{6,7},{7,5},{5,3},{3,1},{1,0},{8,10},{10,12},{12... | collective-permute-start | bytes 196616 | tf_op jit(solution)/shard_map/ppermute | solution.py:355
  131.9 40.7 %collective-permute-start.44 = (bf16[64,512]{1,0:T(8,128)(2,1)S(1)}, bf16[64,512]{1,0:T(8,128)(2,1)S(1)}, u32[]{:S(2)}, u32[]{:S(2)}) collective-permute-start(bf16[64,512]{1,0:T(8,128)(2,1)S(1)} %fusion.15), channel_id=1, source_target_pairs={{0,1},{2,0},{4,2},{6,4},{7,6},{5,7},{3,5},{1,3},{8,9},{10,8},{12,1... | collective-permute-start | bytes 196616 | tf_op jit(solution)/shard_map/ppermute | solution.py:355
  140.6 12.8 %collective-permute-start.53 = (bf16[64,512]{1,0:T(8,128)(2,1)S(1)}, bf16[64,512]{1,0:T(8,128)(2,1)S(1)}, u32[]{:S(2)}, u32[]{:S(2)}) collective-permute-start(bf16[64,512]{1,0:T(8,128)(2,1)S(1)} %pad_maximum_fusion.5), channel_id=1, source_target_pairs={{0,1},{2,0},{4,2},{6,4},{7,6},{5,7},{3,5},{1,3},{8,9},{10,8},{12,1... | collective-permute-start | bytes 196616 | tf_op jit(solution)/shard_map/ppermute | solution.py:355
  157.8 14.9 %collective-permute-start.33 = (bf16[64,512]{1,0:T(8,128)(2,1)S(1)}, bf16[64,512]{1,0:T(8,128)(2,1)S(1)}, u32[]{:S(2)}, u32[]{:S(2)}) collective-permute-start(bf16[64,512]{1,0:T(8,128)(2,1)S(1)} %fusion.22), channel_id=1, source_target_pairs={{0,1},{2,0},{4,2},{6,4},{7,6},{5,7},{3,5},{1,3},{8,9},{10,8},{12,1... | collective-permute-start | bytes 196616 | tf_op jit(solution)/shard_map/ppermute | solution.py:355
  (53 other events, 349.1 us)

commit v3 on v2

--- a/solution.py
+++ b/solution.py
@@ -110,9 +110,8 @@
     return mixed.astype(jnp.bfloat16)[None]
 
 LANES = 128
-VMEM_LIMIT = 48 * 2**20
-ROW_PIECES = 4
-COLUMN_PIECES = 4
+VMEM_LIMIT = 32 * 2**20
+ROW_PIECES = 2
 
 
 def params():
@@ -220,75 +219,70 @@
 
 def up_kernel(sources, pieces, *refs):
     row_refs = refs[:sources]
-    gate_refs = refs[sources : sources + 4 * pieces]
-    up_refs = refs[sources + 4 * pieces : sources + 8 * pieces]
-    hidden_ref, own_gate_ref, rows, units = refs[sources + 8 * pieces :]
-    step = pl.program_id(0)
-    width = rows.shape[1]
-    depth = width // (4 * pieces)
-
-    @pl.when(step == 0)
-    def _():
-        expert = lax.axis_index("expert")
-        first = 0
-        for ref in row_refs:
-            count = ref.shape[0]
-            rows[first : first + count, :] = ref[:, :width]
-            terms = ref[:, width:].astype(jnp.float32)
-            lane = lax.broadcasted_iota(jnp.int32, terms.shape, 1)
-            own_gate_ref[first : first + count, :] = jnp.sum(
-                jnp.where(lane % TOPK == expert, terms, 0.0), axis=-1, keepdims=True
+    weight_refs = refs[sources : sources + pieces]
+    hidden_ref, own_gate_ref, rows, weights, units, arrived = refs[sources + pieces :]
+    tokens, width = rows.shape
+    tiles, _, block = units.shape
+    depth = width // pieces
+
+    def copy(tile, piece, part):
+        columns = pl.ds((part * tiles + tile) * block, block)
+        return pltpu.make_async_copy(
+            weight_refs[piece].at[:, columns],
+            weights.at[pl.ds(piece * depth, depth), columns],
+            arrived.at[tile, piece, part],
+        )
+
+    for tile in range(tiles):
+        for piece in range(pieces):
+            for part in range(2):
+                copy(tile, piece, part).start()
+    expert = lax.axis_index("expert")
+    first = 0
+    for ref in row_refs:
+        count = ref.shape[0]
+        rows[first : first + count, :] = ref[:, :width]
+        terms = ref[:, width:].astype(jnp.float32)
+        lane = lax.broadcasted_iota(jnp.int32, terms.shape, 1)
+        own_gate_ref[first : first + count, :] = jnp.sum(
+            jnp.where(lane % TOPK == expert, terms, 0.0), axis=-1, keepdims=True
+        )
+        first += count
+    for tile in range(tiles):
+        for piece in range(pieces):
+            for part in range(2):
+                copy(tile, piece, part).wait()
+        gate, up = (
+            jnp.dot(
+                rows[...],
+                weights[:, (part * tiles + tile) * block : (part * tiles + tile + 1) * block],
+                preferred_element_type=jnp.float32,
             )
-            first += count
-
-    def product(weights):
-        total = None
-        for i, ref in enumerate(weights):
-            term = jnp.dot(
-                rows[:, i * depth : (i + 1) * depth], ref[...], preferred_element_type=jnp.float32
-            )
-            total = term if total is None else total + term
-        return total
-
-    gate = product(gate_refs)
-    up = product(up_refs)
-    units[step] = (gate / (1.0 + jnp.exp(-gate)) * up).astype(jnp.bfloat16)
-
-    @pl.when(step == pl.num_programs(0) - 1)
-    def _():
-        own = lax.axis_index("dp")
-        block = units.shape[2]
-        for d in range(4):
-            hidden_ref[:, d * block : (d + 1) * block] = units[own ^ d]
+            for part in range(2)
+        )
+        units[tile] = (gate / (1.0 + jnp.exp(-gate)) * up).astype(jnp.bfloat16)
+    own = lax.axis_index("dp")
+    for d in range(4):
+        hidden_ref[:, d * block : (d + 1) * block] = units[own ^ d]
 
 
 def expert_up(rows, weights, hidden_size):
     tokens = sum(piece.shape[0] for piece in rows)
-    width = weights[0].shape[1]
-    depth = weights[0].shape[0]
+    depth, width = weights[0].shape
     features = depth * len(weights)
-    block = hidden_size // 4
-    pieces = len(weights) // 4
-    whole = [
-        pl.BlockSpec(piece.shape, lambda i: (0, 0), pipeline_mode=pl.Buffered(1)) for piece in rows
-    ]
-    gate = [pl.BlockSpec((depth, block), lambda i: (0, i))] * len(weights)
-    up = [pl.BlockSpec((depth, block), lambda i: (0, i + 4))] * len(weights)
     return pl.pallas_call(
-        lambda *refs: up_kernel(len(rows), pieces, *refs),
-        grid=(4,),
+        lambda *refs: up_kernel(len(rows), len(weights), *refs),
         out_shape=[
             jax.ShapeDtypeStruct((tokens, hidden_size), jnp.bfloat16),
             jax.ShapeDtypeStruct((tokens, 1), jnp.float32),
         ],
-        in_specs=whole + gate + up,
-        out_specs=[
-            pl.BlockSpec((tokens, hidden_size), lambda i: (0, 0)),
-            pl.BlockSpec((tokens, 1), lambda i: (0, 0)),
-        ],
+        in_specs=vmem(len(rows)) + [pl.BlockSpec(memory_space=pl.ANY)] * len(weights),
+        out_specs=vmem(2),
         scratch_shapes=[
             pltpu.VMEM((tokens, features), jnp.bfloat16),
-            pltpu.VMEM((4, tokens, block), jnp.bfloat16),
+            pltpu.VMEM((features, width), jnp.bfloat16),
+            pltpu.VMEM((4, tokens, hidden_size // 4), jnp.bfloat16),
+            pltpu.SemaphoreType.DMA((4, len(weights), 2)),
         ],
         compiler_params=params(),
         cost_estimate=pl.CostEstimate(
@@ -297,7 +291,7 @@
             transcendentals=0,
         ),
         name="expert_up",
-    )(*rows, *weights, *weights)
+    )(*rows, *weights)
 
 
 def down_kernel(hidden_ref, gate_ref, w0, w1, w2, w3, out_ref, left_ref, right_ref):
@@ -371,7 +365,7 @@
         above.append(around(above[-1], -1))
         below.append(around(below[-1], 1))
     far = [around(above[-1][:half], -1), around(below[-1][half:], 1)]
-    return above + far + below[:0:-1]
+    return above + far + below[:0:-1], list(zip(above[1:], below[1:])) + [tuple(far)]
 
 
 def scatter_sum(weighted, left, right):
@@ -379,12 +373,15 @@
     half = rows // 2
     reach = sources // 2
     up, down = around(left, 1), around(right, -1)
+    yield up, down
     up = jnp.concatenate([add(weighted[reach - 1, :half], up), weighted[reach - 1, half:]])
     down = jnp.concatenate([weighted[reach + 1, :half], add(weighted[reach + 1, half:], down)])
-    for away in range(reach - 2, 0, -1):
-        up = add(weighted[away], around(up, 1))
-        down = add(weighted[sources - away], around(down, -1))
-    return weighted[0], around(up, 1), around(down, -1)
+    for away in range(reach - 2, -1, -1):
+        up, down = around(up, 1), around(down, -1)
+        yield up, down
+        if away:
+            up = add(weighted[away], up)
+            down = add(weighted[sources - away], down)
 
 
 def every_expert(
@@ -400,51 +397,55 @@
     trainer_gate_up,
     trainer_down,
 ):
+    attn = attention(queries[0], key_pool, value_pool, page_table, prompt_lengths)
     depth = trainer_gate_up.shape[1] // ROW_PIECES
-    slab = trainer_down.shape[2] // COLUMN_PIECES
-    up_own = [
-        trainer_gate_up[0, i * depth : (i + 1) * depth].astype(jnp.bfloat16)
-        for i in range(ROW_PIECES)
+    width = trainer_down.shape[2]
+    first = width * 5 // 8
+    bounds = [(0, first), (first, width)]
+    gate_up = after(trainer_gate_up[0], attn[0]).astype(jnp.bfloat16)
+    up_own = [gate_up[i * depth : (i + 1) * depth] for i in range(ROW_PIECES)]
+    down = trainer_down[0].astype(jnp.bfloat16)
+    down_own = [down[:, low:high] for low, high in bounds]
+    attn = [attn[0]] + [partner(attn[d], d) for d in (1, 2, 3)]
+    up_across = [partner(after(piece, *attn), 2) for piece in up_own]
+    resid, rows = norm(
+        after(hidden_in[0], *up_own), attn, norm_gain, expert_ids[0], gate_weights[0]
+    )
+    gathered, arrived = gather_rows(rows)
+    up_beside = [partner(after(piece, *arrived[0]), 1) for piece in up_own]
+    down_beside = [partner(after(piece, *arrived[1]), 1) for piece in down_own]
+    down_across = [
+        partner(after(down_own[0], *arrived[2]), 2),
+        partner(after(down_own[1], up_across[0], *arrived[3]), 2),
     ]
-    down_own = [
-        trainer_down[0, :, i * slab : (i + 1) * slab].astype(jnp.bfloat16)
-        for i in range(COLUMN_PIECES)
+    up_opposite = [
+        partner(after(up_across[0], *arrived[1]), 1),
+        partner(after(up_across[1], *arrived[3]), 1),
     ]
-    across = []
-    for i, piece in enumerate(up_own + down_own):
-        if i >= 2:
-            piece = after(piece, across[i - 2])
-        across.append(partner(piece, 2))
-    beside = [partner(piece, 1) for piece in up_own + down_own]
-    opposite = [partner(piece, 1) for piece in across]
-
-    attn = attention(queries[0], key_pool, value_pool, page_table, prompt_lengths)
-    attn = [attn[0]] + [partner(attn[d], d) for d in (1, 2, 3)]
-    resid, rows = norm(hidden_in[0], attn, norm_gain, expert_ids[0], gate_weights[0])
-    gathered = gather_rows(rows)
-    up_weights = (
-        up_own + beside[:ROW_PIECES] + across[:ROW_PIECES] + opposite[:ROW_PIECES]
-    )
-    hidden_units, gates = expert_up(gathered, up_weights, trainer_gate_up.shape[2] // 2)
-    slabs = []
-    for i in range(COLUMN_PIECES):
-        at = ROW_PIECES + i
+    hidden_units, gates = expert_up(
+        gathered, up_own + up_beside + up_across + up_opposite, trainer_gate_up.shape[2] // 2
+    )
+
+    def down_slab(i, *before):
+        opposite = partner(after(down_across[i], *before), 1)
         weighted = expert_down(
             hidden_units,
             gates,
-            (down_own[i], beside[at], across[at], opposite[at]),
+            (down_own[i], down_beside[i], down_across[i], opposite),
             lax.axis_size("expert"),
         )
-        own, up, down = scatter_sum(*weighted)
-        slabs.append(
-            (
-                resid[:, i * slab : (i + 1) * slab].astype(jnp.float32)
-                + own.astype(jnp.float32)
-                + up.astype(jnp.float32)
-                + down.astype(jnp.float32)
-            ).astype(jnp.bfloat16)
-        )
-    return jnp.concatenate(slabs, axis=1)[None]
+        return weighted[0][0], scatter_sum(*weighted)
+
+    own0, sums0 = down_slab(0, hidden_units)
+    own1, sums1 = down_slab(1, *next(sums0))
+    ends = [(own, *list(sums)[-1]) for own, sums in ((own0, sums0), (own1, sums1))]
+    mixed = []
+    for (low, high), terms in zip(bounds, ends):
+        total = resid[:, low:high].astype(jnp.float32)
+        for term in terms:
+            total = total + term.astype(jnp.float32)
+        mixed.append(total.astype(jnp.bfloat16))
+    return jnp.concatenate(mixed, axis=1)[None]
 
 
 def solution(mesh):

time: 178 us -> 125 us (0.70)
  starting transfers between devices: 62.7 us -> 34.4 us
  waiting for transfers between devices: 89.1 us -> 68.5 us
  Pallas kernels: 17.5 us -> 11.9 us
  local copies, waits for them, and re-layouts: 2.39 us -> 4.72 us
    ppermute x40 -> x24, starting transfers between devices: 47.2 us -> 25.5 us  [around(): lax.ppermute(x, 'expert', [(ring[i], ring[(i + step) % count]) for i in r...]
    ppermute x40 -> x24, waiting for transfers between devices: 63.8 us -> 43 us  [around(): lax.ppermute(x, 'expert', [(ring[i], ring[(i + step) % count]) for i in r...]
    ppermute x27 -> x15, starting transfers between devices: 15.5 us -> 8.97 us  [partner(): return lax.ppermute(x, 'dp', [(i, i ^ distance) for i in range(4)])]
    pallas_call x1, Pallas kernels: 12.6 us -> 7.29 us  [expert_up(): pl.pallas_call(lambda *refs: up_kernel(len(rows), len(weights), *refs), o...]
    convert_element_type x1 -> x4, other arithmetic: 0.14 us -> 4.36 us  [the longest x1 2.5 us: every_expert(): gate_up = after(trainer_gate_up[0], attn[0]).astype(jnp.bfloat16)]
    another operation x2 -> x0, other arithmetic: 4.23 us -> none
    unnamed x38 -> x20, local copies, waits for them, and re-layouts: 2.08 us -> 4.35 us
    ppermute x27 -> x15, waiting for transfers between devices: 25.3 us -> 25.5 us  [partner(): return lax.ppermute(x, 'dp', [(i, i ^ distance) for i in range(4)])]
  transfers between devices with their start and end apart: 67 -> 39, of which waited for: 35 -> 19; matrix products, arithmetic and copies ran while one was open for 1% -> 4% of each run, Pallas kernels for 10% -> 8%
where the time goes in v3:
time: 125 us
  waiting for transfers between devices  68.5 us (55%)
  starting transfers between devices  34.4 us (28%)
  Pallas kernels  11.9 us (10%)
  other arithmetic  5.45 us (4%)
  local copies, waits for them, and re-layouts  4.72 us (4%)
    ppermute x24, waiting for transfers between devices, around(): lax.ppermute(x, 'expert', [(ring[i], ring[(i + step) % count]) for i in r...  43 us
    ppermute x15, waiting for transfers between devices, partner(): return lax.ppermute(x, 'dp', [(i, i ^ distance) for i in range(4)])  25.5 us
    ppermute x24, starting transfers between devices, around(): lax.ppermute(x, 'expert', [(ring[i], ring[(i + step) % count]) for i in r...  25.5 us
    ppermute x15, starting transfers between devices, partner(): return lax.ppermute(x, 'dp', [(i, i ^ distance) for i in range(4)])  8.97 us
    pallas_call x1, Pallas kernels, expert_up(): pl.pallas_call(lambda *refs: up_kernel(len(rows), len(weights), *refs), o...  7.29 us
    unnamed x20, local copies, waits for them, and re-layouts  4.35 us
    pallas_call x2, Pallas kernels, expert_down(): pl.pallas_call(down_kernel, out_shape=[jax.ShapeDtypeStruct((sources, row...  2.52 us
  transfers between devices with their start and end apart: 39, of which 19 were waited for; matrix products, arithmetic and copies ran while one was open for 4% of the time, Pallas kernels for 8%

profile of v3, /device:TPU:0, one launch (start us, length us, event | category | flops | bytes accessed | tf_op | source)
XLA Modules:
  0.0 125.2 jit_solution(445268915683408764)
XLA Ops:
  4.2 1.7 %attention.1 = (bf16[64,512]{1,0:T(8,128)(2,1)S(1)}, bf16[64,512]{1,0:T(8,128)(2,1)S(1)}, bf16[64,512]{1,0:T(8,128)(2,1)S(1)}, bf16[64,512]{1,0:T(8,128)(2,1)S(1)}) custom-call(s32[1,2]{1,0:T(1,128)S(1)} %copy-done.5, s32[1,4]{1,0:T(1,128)S(1)} %copy-done.6, bf16[256,512]{1,0:T(8,128)(2,1)S(1)} %bitcast.61, bf16[2,128,512]{2,1,0:T(8,128)(2,1)S(1)} %copy-done.2, ...), custom_call_target="tpu_custom_call" | custom-call | tf_op jit(solution)/shard_map/attention/pallas_call | solution.py:163
  6.4 2.6 %collective-permute-start.1 = (bf16[64,512]{1,0:T(8,128)(2,1)S(1)}, bf16[64,512]{1,0:T(8,128)(2,1)S(1)}, u32[]{:S(2)}, u32[]{:S(2)}) collective-permute-start(bf16[64,512]{1,0:T(8,128)(2,1)S(1)} %get-tuple-element.37), channel_id=1, source_target_pairs={{0,16},{8,24},{16,0},{24,8},{1,17},{9,25},{17,1},{25,9},{2,18},{10... | collective-permute-start | bytes 196616 | tf_op jit(solution)/shard_map/ppermute | solution.py:339
  9.0 2.5 %convert_element_type.189 = bf16[512,2048]{1,0:T(8,128)(2,1)S(1)} convert(f32[512,2048]{1,0:T(8,128)} %bitcast.65) | non-fusion elementwise | flops 1048576 | bytes 6291456 | tf_op jit(solution)/shard_map/convert_element_type | solution.py:405
  15.6 1.6 %collective-permute-start.7 = (bf16[64,2176]{1,0:T(8,128)(2,1)S(1)}, bf16[64,2176]{1,0:T(8,128)(2,1)S(1)}, u32[]{:S(2)}, u32[]{:S(2)}) collective-permute-start(bf16[64,2176]{1,0:T(8,128)(2,1)S(1)} %get-tuple-element.40.refs_0_), channel_id=1, source_target_pairs={{0,2},{2,4},{4,6},{6,7},{7,5},{5,3},{3,1},{1,0},{8,10},{10,12},{12... | collective-permute-start | bytes 835592 | tf_op jit(solution)/shard_map/ppermute | solution.py:349
  17.7 6.1 %collective-permute-done.7.refs_8_ = bf16[64,2176]{1,0:T(8,128)(2,1)S(1)} collective-permute-done((bf16[64,2176]{1,0:T(8,128)(2,1)S(1)}, bf16[64,2176]{1,0:T(8,128)(2,1)S(1)}, u32[]{:S(2)}, u32[]{:S(2)}) %collective-permute-start.7) | collective-permute-done | bytes 278560 | tf_op jit(solution)/shard_map/ppermute | solution.py:349
  23.8 1.6 %collective-permute-start.8 = (bf16[64,2176]{1,0:T(8,128)(2,1)S(1)}, bf16[64,2176]{1,0:T(8,128)(2,1)S(1)}, u32[]{:S(2)}, u32[]{:S(2)}) collective-permute-start(bf16[64,2176]{1,0:T(8,128)(2,1)S(1)} %collective-permute-done.7.refs_8_), channel_id=1, source_target_pairs={{0,2},{2,4},{4,6},{6,7},{7,5},{5,3},{3,1},{1,0},{8,10},{10,12},{12... | collective-permute-start | bytes 835592 | tf_op jit(solution)/shard_map/ppermute | solution.py:349
  25.9 5.3 %collective-permute-done.8.refs_7_ = bf16[64,2176]{1,0:T(8,128)(2,1)S(1)} collective-permute-done((bf16[64,2176]{1,0:T(8,128)(2,1)S(1)}, bf16[64,2176]{1,0:T(8,128)(2,1)S(1)}, u32[]{:S(2)}, u32[]{:S(2)}) %collective-permute-start.8) | collective-permute-done | bytes 278560 | tf_op jit(solution)/shard_map/ppermute | solution.py:349
  31.2 1.6 %collective-permute-start.9 = (bf16[64,2176]{1,0:T(8,128)(2,1)S(1)}, bf16[64,2176]{1,0:T(8,128)(2,1)S(1)}, u32[]{:S(2)}, u32[]{:S(2)}) collective-permute-start(bf16[64,2176]{1,0:T(8,128)(2,1)S(1)} %collective-permute-done.8.refs_7_), channel_id=1, source_target_pairs={{0,2},{2,4},{4,6},{6,7},{7,5},{5,3},{3,1},{1,0},{8,10},{10,12},{12... | collective-permute-start | bytes 835592 | tf_op jit(solution)/shard_map/ppermute | solution.py:349
  33.2 4.6 %collective-permute-done.9.refs_6_ = bf16[64,2176]{1,0:T(8,128)(2,1)S(1)} collective-permute-done((bf16[64,2176]{1,0:T(8,128)(2,1)S(1)}, bf16[64,2176]{1,0:T(8,128)(2,1)S(1)}, u32[]{:S(2)}, u32[]{:S(2)}) %collective-permute-start.9) | collective-permute-done | bytes 278560 | tf_op jit(solution)/shard_map/ppermute | solution.py:349
  37.8 1.6 %collective-permute-start.10 = (bf16[32,2176]{1,0:T(8,128)(2,1)S(1)}, bf16[32,2176]{1,0:T(8,128)(2,1)S(1)}, u32[]{:S(2)}, u32[]{:S(2)}) collective-permute-start(bf16[32,2176]{1,0:T(8,128)(2,1)S(1)} %slice.107), channel_id=1, source_target_pairs={{0,2},{2,4},{4,6},{6,7},{7,5},{5,3},{3,1},{1,0},{8,10},{10,12},{12... | collective-permute-start | bytes 417800 | tf_op jit(solution)/shard_map/ppermute | solution.py:349
  40.1 2.8 %collective-permute-done.10.refs_5_ = bf16[32,2176]{1,0:T(8,128)(2,1)S(1)} collective-permute-done((bf16[32,2176]{1,0:T(8,128)(2,1)S(1)}, bf16[32,2176]{1,0:T(8,128)(2,1)S(1)}, u32[]{:S(2)}, u32[]{:S(2)}) %collective-permute-start.10) | collective-permute-done | bytes 139296 | tf_op jit(solution)/shard_map/ppermute | solution.py:349
  42.9 1.8 %collective-permute-done.6.refs_4_ = bf16[32,2176]{1,0:T(8,128)(2,1)S(1)} collective-permute-done((bf16[32,2176]{1,0:T(8,128)(2,1)S(1)}, bf16[32,2176]{1,0:T(8,128)(2,1)S(1)}, u32[]{:S(2)}, u32[]{:S(2)}) %collective-permute-start.6) | collective-permute-done | bytes 139296 | tf_op jit(solution)/shard_map/ppermute | solution.py:349
  44.7 16.1 %collective-permute-done.13.refs_13_ = bf16[256,2048]{1,0:T(8,128)(2,1)} collective-permute-done((bf16[256,2048]{1,0:T(8,128)(2,1)S(1)}, bf16[256,2048]{1,0:T(8,128)(2,1)}, u32[]{:S(2)}, u32[]{:S(2)}) %collective-permute-start.13) | collective-permute-done | bytes 1048608 | tf_op jit(solution)/shard_map/ppermute | solution.py:339
  60.8 1.7 %convert_bitcast_fusion = bf16[256,2048]{1,0:T(8,128)(2,1)S(1)} fusion(f32[1,256,2048]{2,1,0:T(8,128)} %param.21), kind=kLoop, calls=%fused_computation | loop fusion | flops 524288 | bytes 3145728 | tf_op jit(solution)/shard_map/convert_element_type | solution.py:407
  64.4 7.3 %expert_up.1 = (bf16[512,1024]{1,0:T(8,128)(2,1)S(1)}, f32[512,1]{1,0:T(8,128)S(1)}) custom-call(bf16[64,2176]{1,0:T(8,128)(2,1)S(1)} %get-tuple-element.40.refs_0_, bf16[64,2176]{1,0:T(8,128)(2,1)S(1)} %collective-permute-done.3.refs_1_, bf16[64,2176]{1,0:T(8,128)(2,1)S(1)} %collective-permute-done.4.refs_2_, ...), custom_call_target="tpu_custom_call" | custom-call | flops 4294967296 | bytes 8388608 | tf_op jit(solution)/shard_map/expert_up/pallas_call | solution.py:273
  71.7 8.1 %collective-permute-done.18.w2 = bf16[256,1280]{1,0:T(8,128)(2,1)S(1)} collective-permute-done((bf16[256,1280]{1,0:T(8,128)(2,1)S(1)}, bf16[256,1280]{1,0:T(8,128)(2,1)S(1)}, u32[]{:S(2)}, u32[]{:S(2)}) %collective-permute-start.18) | collective-permute-done | bytes 655392 | tf_op jit(solution)/shard_map/ppermute | solution.py:339
  83.5 1.6 %collective-permute-start.20 = (bf16[32,1280]{1,0:T(8,128)(2,1)S(1)}, bf16[32,1280]{1,0:T(8,128)(2,1)S(1)}, u32[]{:S(2)}, u32[]{:S(2)}) collective-permute-start(bf16[32,1280]{1,0:T(8,128)(2,1)S(1)} %get-tuple-element.53), channel_id=1, source_target_pairs={{0,2},{2,4},{4,6},{6,7},{7,5},{5,3},{3,1},{1,0},{8,10},{10,12},{12... | collective-permute-start | bytes 245768 | tf_op jit(solution)/shard_map/ppermute | solution.py:349
  85.6 2.4 %collective-permute-done.20 = bf16[32,1280]{1,0:T(8,128)(2,1)S(1)} collective-permute-done((bf16[32,1280]{1,0:T(8,128)(2,1)S(1)}, bf16[32,1280]{1,0:T(8,128)(2,1)S(1)}, u32[]{:S(2)}, u32[]{:S(2)}) %collective-permute-start.20) | collective-permute-done | bytes 81952 | tf_op jit(solution)/shard_map/ppermute | solution.py:349
  88.0 1.5 %collective-permute-done.24 = bf16[32,1280]{1,0:T(8,128)(2,1)S(1)} collective-permute-done((bf16[32,1280]{1,0:T(8,128)(2,1)S(1)}, bf16[32,1280]{1,0:T(8,128)(2,1)S(1)}, u32[]{:S(2)}, u32[]{:S(2)}) %collective-permute-start.24) | collective-permute-done | bytes 81952 | tf_op jit(solution)/shard_map/ppermute | solution.py:349
  89.6 1.6 %collective-permute-start.21 = (bf16[64,1280]{1,0:T(8,128)(2,1)S(1)}, bf16[64,1280]{1,0:T(8,128)(2,1)S(1)}, u32[]{:S(2)}, u32[]{:S(2)}) collective-permute-start(bf16[64,1280]{1,0:T(8,128)(2,1)S(1)} %pad_maximum_fusion), channel_id=1, source_target_pairs={{0,2},{2,4},{4,6},{6,7},{7,5},{5,3},{3,1},{1,0},{8,10},{10,12},{12... | collective-permute-start | bytes 491528 | tf_op jit(solution)/shard_map/ppermute | solution.py:349
  91.7 3.2 %collective-permute-done.21 = bf16[64,1280]{1,0:T(8,128)(2,1)S(1)} collective-permute-done((bf16[64,1280]{1,0:T(8,128)(2,1)S(1)}, bf16[64,1280]{1,0:T(8,128)(2,1)S(1)}, u32[]{:S(2)}, u32[]{:S(2)}) %collective-permute-start.21) | collective-permute-done | bytes 163872 | tf_op jit(solution)/shard_map/ppermute | solution.py:349
  95.0 1.8 %collective-permute-start.22 = (bf16[64,1280]{1,0:T(8,128)(2,1)S(1)}, bf16[64,1280]{1,0:T(8,128)(2,1)S(1)}, u32[]{:S(2)}, u32[]{:S(2)}) collective-permute-start(bf16[64,1280]{1,0:T(8,128)(2,1)S(1)} %fusion.2), channel_id=1, source_target_pairs={{0,2},{2,4},{4,6},{6,7},{7,5},{5,3},{3,1},{1,0},{8,10},{10,12},{12... | collective-permute-start | bytes 491528 | tf_op jit(solution)/shard_map/ppermute | solution.py:349
  97.8 1.6 %collective-permute-start.31 = (bf16[32,768]{1,0:T(8,128)(2,1)S(1)}, bf16[32,768]{1,0:T(8,128)(2,1)S(1)}, u32[]{:S(2)}, u32[]{:S(2)}) collective-permute-start(bf16[32,768]{1,0:T(8,128)(2,1)S(1)} %get-tuple-element.59), channel_id=1, source_target_pairs={{0,2},{2,4},{4,6},{6,7},{7,5},{5,3},{3,1},{1,0},{8,10},{10,12},{12... | collective-permute-start | bytes 147464 | tf_op jit(solution)/shard_map/ppermute | solution.py:349
  99.9 2.1 %collective-permute-done.31 = bf16[32,768]{1,0:T(8,128)(2,1)S(1)} collective-permute-done((bf16[32,768]{1,0:T(8,128)(2,1)S(1)}, bf16[32,768]{1,0:T(8,128)(2,1)S(1)}, u32[]{:S(2)}, u32[]{:S(2)}) %collective-permute-start.31) | collective-permute-done | bytes 49184 | tf_op jit(solution)/shard_map/ppermute | solution.py:349
  102.0 1.6 %collective-permute-done.35 = bf16[32,768]{1,0:T(8,128)(2,1)S(1)} collective-permute-done((bf16[32,768]{1,0:T(8,128)(2,1)S(1)}, bf16[32,768]{1,0:T(8,128)(2,1)S(1)}, u32[]{:S(2)}, u32[]{:S(2)}) %collective-permute-start.35) | collective-permute-done | bytes 49184 | tf_op jit(solution)/shard_map/ppermute | solution.py:349
  103.6 1.9 %collective-permute-start.32 = (bf16[64,768]{1,0:T(8,128)(2,1)S(1)}, bf16[64,768]{1,0:T(8,128)(2,1)S(1)}, u32[]{:S(2)}, u32[]{:S(2)}) collective-permute-start(bf16[64,768]{1,0:T(8,128)(2,1)S(1)} %pad_maximum_fusion.2), channel_id=1, source_target_pairs={{0,2},{2,4},{4,6},{6,7},{7,5},{5,3},{3,1},{1,0},{8,10},{10,12},{12... | collective-permute-start | bytes 294920 | tf_op jit(solution)/shard_map/ppermute | solution.py:349
  105.7 3.2 %collective-permute-done.32 = bf16[64,768]{1,0:T(8,128)(2,1)S(1)} collective-permute-done((bf16[64,768]{1,0:T(8,128)(2,1)S(1)}, bf16[64,768]{1,0:T(8,128)(2,1)S(1)}, u32[]{:S(2)}, u32[]{:S(2)}) %collective-permute-start.32) | collective-permute-done | bytes 98336 | tf_op jit(solution)/shard_map/ppermute | solution.py:349
  109.0 1.8 %collective-permute-start.33 = (bf16[64,768]{1,0:T(8,128)(2,1)S(1)}, bf16[64,768]{1,0:T(8,128)(2,1)S(1)}, u32[]{:S(2)}, u32[]{:S(2)}) collective-permute-start(bf16[64,768]{1,0:T(8,128)(2,1)S(1)} %fusion.9), channel_id=1, source_target_pairs={{0,2},{2,4},{4,6},{6,7},{7,5},{5,3},{3,1},{1,0},{8,10},{10,12},{12... | collective-permute-start | bytes 294920 | tf_op jit(solution)/shard_map/ppermute | solution.py:349
  111.2 1.7 %collective-permute-start.23 = (bf16[64,1280]{1,0:T(8,128)(2,1)S(1)}, bf16[64,1280]{1,0:T(8,128)(2,1)S(1)}, u32[]{:S(2)}, u32[]{:S(2)}) collective-permute-start(bf16[64,1280]{1,0:T(8,128)(2,1)S(1)} %get-tuple-element.63), channel_id=1, source_target_pairs={{0,2},{2,4},{4,6},{6,7},{7,5},{5,3},{3,1},{1,0},{8,10},{10,12},{12... | collective-permute-start | bytes 491528 | tf_op jit(solution)/shard_map/ppermute | solution.py:349
  114.8 2.8 %collective-permute-done.26 = bf16[64,1280]{1,0:T(8,128)(2,1)S(1)} collective-permute-done((bf16[64,1280]{1,0:T(8,128)(2,1)S(1)}, bf16[64,1280]{1,0:T(8,128)(2,1)S(1)}, u32[]{:S(2)}, u32[]{:S(2)}) %collective-permute-start.26) | collective-permute-done | bytes 163872 | tf_op jit(solution)/shard_map/ppermute | solution.py:349
  118.1 1.6 %collective-permute-start.34 = (bf16[64,768]{1,0:T(8,128)(2,1)S(1)}, bf16[64,768]{1,0:T(8,128)(2,1)S(1)}, u32[]{:S(2)}, u32[]{:S(2)}) collective-permute-start(bf16[64,768]{1,0:T(8,128)(2,1)S(1)} %get-tuple-element.69), channel_id=1, source_target_pairs={{0,2},{2,4},{4,6},{6,7},{7,5},{5,3},{3,1},{1,0},{8,10},{10,12},{12... | collective-permute-start | bytes 294920 | tf_op jit(solution)/shard_map/ppermute | solution.py:349
  120.2 2.8 %collective-permute-done.27 = bf16[64,1280]{1,0:T(8,128)(2,1)S(1)} collective-permute-done((bf16[64,1280]{1,0:T(8,128)(2,1)S(1)}, bf16[64,1280]{1,0:T(8,128)(2,1)S(1)}, u32[]{:S(2)}, u32[]{:S(2)}) %collective-permute-start.27) | collective-permute-done | bytes 163872 | tf_op jit(solution)/shard_map/ppermute | solution.py:349
  (95 shorter events, 24.6 us)
Async XLA Ops:
  5.9 6.0 %collective-permute-start = (bf16[64,512]{1,0:T(8,128)(2,1)S(1)}, bf16[64,512]{1,0:T(8,128)(2,1)S(1)}, u32[]{:S(2)}, u32[]{:S(2)}) collective-permute-start(bf16[64,512]{1,0:T(8,128)(2,1)S(1)} %get-tuple-element.36), channel_id=1, source_target_pairs={{0,8},{8,0},{16,24},{24,16},{1,9},{9,1},{17,25},{25,17},{2,10},{10... | collective-permute-start | bytes 196616 | tf_op jit(solution)/shard_map/ppermute | solution.py:339
  6.4 5.4 %collective-permute-start.1 = (bf16[64,512]{1,0:T(8,128)(2,1)S(1)}, bf16[64,512]{1,0:T(8,128)(2,1)S(1)}, u32[]{:S(2)}, u32[]{:S(2)}) collective-permute-start(bf16[64,512]{1,0:T(8,128)(2,1)S(1)} %get-tuple-element.37), channel_id=1, source_target_pairs={{0,16},{8,24},{16,0},{24,8},{1,17},{9,25},{17,1},{25,9},{2,18},{10... | collective-permute-start | bytes 196616 | tf_op jit(solution)/shard_map/ppermute | solution.py:339
  13.0 31.7 %collective-permute-start.14 = (bf16[256,2048]{1,0:T(8,128)(2,1)S(1)}, bf16[256,2048]{1,0:T(8,128)(2,1)}, u32[]{:S(2)}, u32[]{:S(2)}) collective-permute-start(bf16[256,2048]{1,0:T(8,128)(2,1)S(1)} %get-tuple-element.44.refs_10_), channel_id=1, source_target_pairs={{0,16},{8,24},{16,0},{24,8},{1,17},{9,25},{17,1},{25,9},{2,18},{10... | collective-permute-start | bytes 3145736 | tf_op jit(solution)/shard_map/ppermute | solution.py:339
  14.3 46.5 %collective-permute-start.13 = (bf16[256,2048]{1,0:T(8,128)(2,1)S(1)}, bf16[256,2048]{1,0:T(8,128)(2,1)}, u32[]{:S(2)}, u32[]{:S(2)}) collective-permute-start(bf16[256,2048]{1,0:T(8,128)(2,1)S(1)} %get-tuple-element.43.refs_9_), channel_id=1, source_target_pairs={{0,16},{8,24},{16,0},{24,8},{1,17},{9,25},{17,1},{25,9},{2,18},{10... | collective-permute-start | bytes 3145736 | tf_op jit(solution)/shard_map/ppermute | solution.py:339
  15.6 8.2 %collective-permute-start.7 = (bf16[64,2176]{1,0:T(8,128)(2,1)S(1)}, bf16[64,2176]{1,0:T(8,128)(2,1)S(1)}, u32[]{:S(2)}, u32[]{:S(2)}) collective-permute-start(bf16[64,2176]{1,0:T(8,128)(2,1)S(1)} %get-tuple-element.40.refs_0_), channel_id=1, source_target_pairs={{0,2},{2,4},{4,6},{6,7},{7,5},{5,3},{3,1},{1,0},{8,10},{10,12},{12... | collective-permute-start | bytes 835592 | tf_op jit(solution)/shard_map/ppermute | solution.py:349
  17.2 8.2 %collective-permute-start.3 = (bf16[64,2176]{1,0:T(8,128)(2,1)S(1)}, bf16[64,2176]{1,0:T(8,128)(2,1)S(1)}, u32[]{:S(2)}, u32[]{:S(2)}) collective-permute-start(bf16[64,2176]{1,0:T(8,128)(2,1)S(1)} %get-tuple-element.40.refs_0_), channel_id=1, source_target_pairs={{0,1},{2,0},{4,2},{6,4},{7,6},{5,7},{3,5},{1,3},{8,9},{10,8},{12,1... | collective-permute-start | bytes 835592 | tf_op jit(solution)/shard_map/ppermute | solution.py:349
  23.8 7.4 %collective-permute-start.8 = (bf16[64,2176]{1,0:T(8,128)(2,1)S(1)}, bf16[64,2176]{1,0:T(8,128)(2,1)S(1)}, u32[]{:S(2)}, u32[]{:S(2)}) collective-permute-start(bf16[64,2176]{1,0:T(8,128)(2,1)S(1)} %collective-permute-done.7.refs_8_), channel_id=1, source_target_pairs={{0,2},{2,4},{4,6},{6,7},{7,5},{5,3},{3,1},{1,0},{8,10},{10,12},{12... | collective-permute-start | bytes 835592 | tf_op jit(solution)/shard_map/ppermute | solution.py:349
  25.4 7.4 %collective-permute-start.4 = (bf16[64,2176]{1,0:T(8,128)(2,1)S(1)}, bf16[64,2176]{1,0:T(8,128)(2,1)S(1)}, u32[]{:S(2)}, u32[]{:S(2)}) collective-permute-start(bf16[64,2176]{1,0:T(8,128)(2,1)S(1)} %collective-permute-done.3.refs_1_), channel_id=1, source_target_pairs={{0,1},{2,0},{4,2},{6,4},{7,6},{5,7},{3,5},{1,3},{8,9},{10,8},{12,1... | collective-permute-start | bytes 835592 | tf_op jit(solution)/shard_map/ppermute | solution.py:349
  31.2 6.6 %collective-permute-start.9 = (bf16[64,2176]{1,0:T(8,128)(2,1)S(1)}, bf16[64,2176]{1,0:T(8,128)(2,1)S(1)}, u32[]{:S(2)}, u32[]{:S(2)}) collective-permute-start(bf16[64,2176]{1,0:T(8,128)(2,1)S(1)} %collective-permute-done.8.refs_7_), channel_id=1, source_target_pairs={{0,2},{2,4},{4,6},{6,7},{7,5},{5,3},{3,1},{1,0},{8,10},{10,12},{12... | collective-permute-start | bytes 835592 | tf_op jit(solution)/shard_map/ppermute | solution.py:349
  32.8 6.8 %collective-permute-start.5 = (bf16[64,2176]{1,0:T(8,128)(2,1)S(1)}, bf16[64,2176]{1,0:T(8,128)(2,1)S(1)}, u32[]{:S(2)}, u32[]{:S(2)}) collective-permute-start(bf16[64,2176]{1,0:T(8,128)(2,1)S(1)} %collective-permute-done.4.refs_2_), channel_id=1, source_target_pairs={{0,1},{2,0},{4,2},{6,4},{7,6},{5,7},{3,5},{1,3},{8,9},{10,8},{12,1... | collective-permute-start | bytes 835592 | tf_op jit(solution)/shard_map/ppermute | solution.py:349
  37.8 5.1 %collective-permute-start.10 = (bf16[32,2176]{1,0:T(8,128)(2,1)S(1)}, bf16[32,2176]{1,0:T(8,128)(2,1)S(1)}, u32[]{:S(2)}, u32[]{:S(2)}) collective-permute-start(bf16[32,2176]{1,0:T(8,128)(2,1)S(1)} %slice.107), channel_id=1, source_target_pairs={{0,2},{2,4},{4,6},{6,7},{7,5},{5,3},{3,1},{1,0},{8,10},{10,12},{12... | collective-permute-start | bytes 417800 | tf_op jit(solution)/shard_map/ppermute | solution.py:349
  39.6 5.1 %collective-permute-start.6 = (bf16[32,2176]{1,0:T(8,128)(2,1)S(1)}, bf16[32,2176]{1,0:T(8,128)(2,1)S(1)}, u32[]{:S(2)}, u32[]{:S(2)}) collective-permute-start(bf16[32,2176]{1,0:T(8,128)(2,1)S(1)} %slice.106), channel_id=1, source_target_pairs={{0,1},{2,0},{4,2},{6,4},{7,6},{5,7},{3,5},{1,3},{8,9},{10,8},{12,1... | collective-permute-start | bytes 417800 | tf_op jit(solution)/shard_map/ppermute | solution.py:349
  40.1 24.1 %collective-permute-start.12 = (bf16[256,2048]{1,0:T(8,128)(2,1)S(1)}, bf16[256,2048]{1,0:T(8,128)(2,1)S(1)}, u32[]{:S(2)}, u32[]{:S(2)}) collective-permute-start(bf16[256,2048]{1,0:T(8,128)(2,1)S(1)} %get-tuple-element.44.refs_10_), channel_id=1, source_target_pairs={{0,8},{8,0},{16,24},{24,16},{1,9},{9,1},{17,25},{25,17},{2,10},{10... | collective-permute-start | bytes 3145736 | tf_op jit(solution)/shard_map/ppermute | solution.py:339
  42.9 21.5 %collective-permute-start.11 = (bf16[256,2048]{1,0:T(8,128)(2,1)S(1)}, bf16[256,2048]{1,0:T(8,128)(2,1)S(1)}, u32[]{:S(2)}, u32[]{:S(2)}) collective-permute-start(bf16[256,2048]{1,0:T(8,128)(2,1)S(1)} %get-tuple-element.43.refs_9_), channel_id=1, source_target_pairs={{0,8},{8,0},{16,24},{24,16},{1,9},{9,1},{17,25},{25,17},{2,10},{10... | collective-permute-start | bytes 3145736 | tf_op jit(solution)/shard_map/ppermute | solution.py:339
  44.7 19.7 %collective-permute-start.16 = (bf16[256,2048]{1,0:T(8,128)(2,1)}, bf16[256,2048]{1,0:T(8,128)(2,1)S(1)}, u32[]{:S(2)}, u32[]{:S(2)}) collective-permute-start(bf16[256,2048]{1,0:T(8,128)(2,1)} %collective-permute-done.14.refs_14_), channel_id=1, source_target_pairs={{0,8},{8,0},{16,24},{24,16},{1,9},{9,1},{17,25},{25,17},{2,10},{10... | collective-permute-start | bytes 3145736 | tf_op jit(solution)/shard_map/ppermute | solution.py:339
  62.6 17.2 %collective-permute-start.18 = (bf16[256,1280]{1,0:T(8,128)(2,1)S(1)}, bf16[256,1280]{1,0:T(8,128)(2,1)S(1)}, u32[]{:S(2)}, u32[]{:S(2)}) collective-permute-start(bf16[256,1280]{1,0:T(8,128)(2,1)S(1)} %slice.108.w0), channel_id=1, source_target_pairs={{0,16},{8,24},{16,0},{24,8},{1,17},{9,25},{17,1},{25,9},{2,18},{10... | collective-permute-start | bytes 1966088 | tf_op jit(solution)/shard_map/ppermute | solution.py:339
  64.1 17.8 %collective-permute-start.17 = (bf16[256,1280]{1,0:T(8,128)(2,1)S(1)}, bf16[256,1280]{1,0:T(8,128)(2,1)S(1)}, u32[]{:S(2)}, u32[]{:S(2)}) collective-permute-start(bf16[256,1280]{1,0:T(8,128)(2,1)S(1)} %slice.108.w0), channel_id=1, source_target_pairs={{0,8},{8,0},{16,24},{24,16},{1,9},{9,1},{17,25},{25,17},{2,10},{10... | collective-permute-start | bytes 1966088 | tf_op jit(solution)/shard_map/ppermute | solution.py:339
  79.9 17.0 %collective-permute-start.28 = (bf16[256,768]{1,0:T(8,128)(2,1)S(1)}, bf16[256,768]{1,0:T(8,128)(2,1)S(1)}, u32[]{:S(2)}, u32[]{:S(2)}) collective-permute-start(bf16[256,768]{1,0:T(8,128)(2,1)S(1)} %slice.109.w0), channel_id=1, source_target_pairs={{0,8},{8,0},{16,24},{24,16},{1,9},{9,1},{17,25},{25,17},{2,10},{10... | collective-permute-start | bytes 1179656 | tf_op jit(solution)/shard_map/ppermute | solution.py:339
  80.4 11.3 %collective-permute-start.29 = (bf16[256,768]{1,0:T(8,128)(2,1)S(1)}, bf16[256,768]{1,0:T(8,128)(2,1)S(1)}, u32[]{:S(2)}, u32[]{:S(2)}) collective-permute-start(bf16[256,768]{1,0:T(8,128)(2,1)S(1)} %slice.109.w0), channel_id=1, source_target_pairs={{0,16},{8,24},{16,0},{24,8},{1,17},{9,25},{17,1},{25,9},{2,18},{10... | collective-permute-start | bytes 1179656 | tf_op jit(solution)/shard_map/ppermute | solution.py:339
  89.6 5.4 %collective-permute-start.21 = (bf16[64,1280]{1,0:T(8,128)(2,1)S(1)}, bf16[64,1280]{1,0:T(8,128)(2,1)S(1)}, u32[]{:S(2)}, u32[]{:S(2)}) collective-permute-start(bf16[64,1280]{1,0:T(8,128)(2,1)S(1)} %pad_maximum_fusion), channel_id=1, source_target_pairs={{0,2},{2,4},{4,6},{6,7},{7,5},{5,3},{3,1},{1,0},{8,10},{10,12},{12... | collective-permute-start | bytes 491528 | tf_op jit(solution)/shard_map/ppermute | solution.py:349
  91.2 19.5 %collective-permute-start.25 = (bf16[64,1280]{1,0:T(8,128)(2,1)S(1)}, bf16[64,1280]{1,0:T(8,128)(2,1)S(1)}, u32[]{:S(2)}, u32[]{:S(2)}) collective-permute-start(bf16[64,1280]{1,0:T(8,128)(2,1)S(1)} %pad_maximum_fusion.1), channel_id=1, source_target_pairs={{0,1},{2,0},{4,2},{6,4},{7,6},{5,7},{3,5},{1,3},{8,9},{10,8},{12,1... | collective-permute-start | bytes 491528 | tf_op jit(solution)/shard_map/ppermute | solution.py:349
  91.7 5.1 %collective-permute-start.30 = (bf16[256,768]{1,0:T(8,128)(2,1)S(1)}, bf16[256,768]{1,0:T(8,128)(2,1)S(1)}, u32[]{:S(2)}, u32[]{:S(2)}) collective-permute-start(bf16[256,768]{1,0:T(8,128)(2,1)S(1)} %collective-permute-done.29.w2), channel_id=1, source_target_pairs={{0,8},{8,0},{16,24},{24,16},{1,9},{9,1},{17,25},{25,17},{2,10},{10... | collective-permute-start | bytes 1179656 | tf_op jit(solution)/shard_map/ppermute | solution.py:339
  95.0 15.8 %collective-permute-start.22 = (bf16[64,1280]{1,0:T(8,128)(2,1)S(1)}, bf16[64,1280]{1,0:T(8,128)(2,1)S(1)}, u32[]{:S(2)}, u32[]{:S(2)}) collective-permute-start(bf16[64,1280]{1,0:T(8,128)(2,1)S(1)} %fusion.2), channel_id=1, source_target_pairs={{0,2},{2,4},{4,6},{6,7},{7,5},{5,3},{3,1},{1,0},{8,10},{10,12},{12... | collective-permute-start | bytes 491528 | tf_op jit(solution)/shard_map/ppermute | solution.py:349
  103.6 5.4 %collective-permute-start.32 = (bf16[64,768]{1,0:T(8,128)(2,1)S(1)}, bf16[64,768]{1,0:T(8,128)(2,1)S(1)}, u32[]{:S(2)}, u32[]{:S(2)}) collective-permute-start(bf16[64,768]{1,0:T(8,128)(2,1)S(1)} %pad_maximum_fusion.2), channel_id=1, source_target_pairs={{0,2},{2,4},{4,6},{6,7},{7,5},{5,3},{3,1},{1,0},{8,10},{10,12},{12... | collective-permute-start | bytes 294920 | tf_op jit(solution)/shard_map/ppermute | solution.py:349
  105.4 7.5 %collective-permute-start.36 = (bf16[64,768]{1,0:T(8,128)(2,1)S(1)}, bf16[64,768]{1,0:T(8,128)(2,1)S(1)}, u32[]{:S(2)}, u32[]{:S(2)}) collective-permute-start(bf16[64,768]{1,0:T(8,128)(2,1)S(1)} %pad_maximum_fusion.3), channel_id=1, source_target_pairs={{0,1},{2,0},{4,2},{6,4},{7,6},{5,7},{3,5},{1,3},{8,9},{10,8},{12,1... | collective-permute-start | bytes 294920 | tf_op jit(solution)/shard_map/ppermute | solution.py:349
  109.0 5.2 %collective-permute-start.33 = (bf16[64,768]{1,0:T(8,128)(2,1)S(1)}, bf16[64,768]{1,0:T(8,128)(2,1)S(1)}, u32[]{:S(2)}, u32[]{:S(2)}) collective-permute-start(bf16[64,768]{1,0:T(8,128)(2,1)S(1)} %fusion.9), channel_id=1, source_target_pairs={{0,2},{2,4},{4,6},{6,7},{7,5},{5,3},{3,1},{1,0},{8,10},{10,12},{12... | collective-permute-start | bytes 294920 | tf_op jit(solution)/shard_map/ppermute | solution.py:349
  110.9 6.7 %collective-permute-start.26 = (bf16[64,1280]{1,0:T(8,128)(2,1)S(1)}, bf16[64,1280]{1,0:T(8,128)(2,1)S(1)}, u32[]{:S(2)}, u32[]{:S(2)}) collective-permute-start(bf16[64,1280]{1,0:T(8,128)(2,1)S(1)} %get-tuple-element.64), channel_id=1, source_target_pairs={{0,1},{2,0},{4,2},{6,4},{7,6},{5,7},{3,5},{1,3},{8,9},{10,8},{12,1... | collective-permute-start | bytes 491528 | tf_op jit(solution)/shard_map/ppermute | solution.py:349
  111.2 9.0 %collective-permute-start.23 = (bf16[64,1280]{1,0:T(8,128)(2,1)S(1)}, bf16[64,1280]{1,0:T(8,128)(2,1)S(1)}, u32[]{:S(2)}, u32[]{:S(2)}) collective-permute-start(bf16[64,1280]{1,0:T(8,128)(2,1)S(1)} %get-tuple-element.63), channel_id=1, source_target_pairs={{0,2},{2,4},{4,6},{6,7},{7,5},{5,3},{3,1},{1,0},{8,10},{10,12},{12... | collective-permute-start | bytes 491528 | tf_op jit(solution)/shard_map/ppermute | solution.py:349
  114.2 5.5 %collective-permute-start.37 = (bf16[64,768]{1,0:T(8,128)(2,1)S(1)}, bf16[64,768]{1,0:T(8,128)(2,1)S(1)}, u32[]{:S(2)}, u32[]{:S(2)}) collective-permute-start(bf16[64,768]{1,0:T(8,128)(2,1)S(1)} %get-tuple-element.70), channel_id=1, source_target_pairs={{0,1},{2,0},{4,2},{6,4},{7,6},{5,7},{3,5},{1,3},{8,9},{10,8},{12,1... | collective-permute-start | bytes 294920 | tf_op jit(solution)/shard_map/ppermute | solution.py:349
  117.6 5.4 %collective-permute-start.27 = (bf16[64,1280]{1,0:T(8,128)(2,1)S(1)}, bf16[64,1280]{1,0:T(8,128)(2,1)S(1)}, u32[]{:S(2)}, u32[]{:S(2)}) collective-permute-start(bf16[64,1280]{1,0:T(8,128)(2,1)S(1)} %fusion.1), channel_id=1, source_target_pairs={{0,1},{2,0},{4,2},{6,4},{7,6},{5,7},{3,5},{1,3},{8,9},{10,8},{12,1... | collective-permute-start | bytes 491528 | tf_op jit(solution)/shard_map/ppermute | solution.py:349
  118.1 5.0 %collective-permute-start.34 = (bf16[64,768]{1,0:T(8,128)(2,1)S(1)}, bf16[64,768]{1,0:T(8,128)(2,1)S(1)}, u32[]{:S(2)}, u32[]{:S(2)}) collective-permute-start(bf16[64,768]{1,0:T(8,128)(2,1)S(1)} %get-tuple-element.69), channel_id=1, source_target_pairs={{0,2},{2,4},{4,6},{6,7},{7,5},{5,3},{3,1},{1,0},{8,10},{10,12},{12... | collective-permute-start | bytes 294920 | tf_op jit(solution)/shard_map/ppermute | solution.py:349
  119.7 4.7 %collective-permute-start.38 = (bf16[64,768]{1,0:T(8,128)(2,1)S(1)}, bf16[64,768]{1,0:T(8,128)(2,1)S(1)}, u32[]{:S(2)}, u32[]{:S(2)}) collective-permute-start(bf16[64,768]{1,0:T(8,128)(2,1)S(1)} %fusion.8), channel_id=1, source_target_pairs={{0,1},{2,0},{4,2},{6,4},{7,6},{5,7},{3,5},{1,3},{8,9},{10,8},{12,1... | collective-permute-start | bytes 294920 | tf_op jit(solution)/shard_map/ppermute | solution.py:349
  (16 other events, 45.5 us)

commit v4 on v3

--- a/solution.py
+++ b/solution.py
@@ -111,7 +111,9 @@
 
 LANES = 128
 VMEM_LIMIT = 32 * 2**20
-ROW_PIECES = 2
+SLABS = (768, 768, 512)
+CAST_STEPS = 4
+SMALL = pl.CostEstimate(flops=1, bytes_accessed=1, transcendentals=0)
 
 
 def params():
@@ -122,10 +124,28 @@
     return [pl.BlockSpec(memory_space=pltpu.VMEM)] * count
 
 
-def attention_kernel(table, lengths, q_ref, k_ref, v_ref, *refs):
-    outs, attn = refs[:4], refs[4]
+def attention_kernel(*refs):
+    sources, outs, piece_ref, scratch = refs[:6], refs[6:10], refs[10], refs[11:]
+    table, lengths, q_ref, k_ref, v_ref, weights, attn, arrived = scratch
+    copies = [
+        pltpu.make_async_copy(source, target, arrived.at[i])
+        for i, (source, target) in enumerate(
+            zip(
+                (*sources[:2], sources[2].at[0], *sources[3:5]),
+                (table, lengths, q_ref, k_ref, v_ref),
+            )
+        )
+    ]
+    rows = weights.shape[0]
+    copies.append(
+        pltpu.make_async_copy(sources[5].at[0, pl.ds(0, rows)], weights, arrived.at[5])
+    )
+    for copy in copies:
+        copy.start()
+    for copy in copies[:5]:
+        copy.wait()
     tokens, width = q_ref.shape
-    pages, page = k_ref.shape[0], k_ref.shape[1]
+    pages = k_ref.shape[0]
     row = lax.broadcasted_iota(jnp.int32, (tokens, tokens), 0)
     column = lax.broadcasted_iota(jnp.int32, (tokens, tokens), 1)
     row_request = jnp.zeros((tokens, tokens), jnp.int32)
@@ -145,8 +165,8 @@
         ) * (1.0 / math.sqrt(HDIM))
         scores = jnp.where(same, scores, -1e30)
         highest = jnp.max(scores, axis=-1, keepdims=True)
-        weights = jnp.where(same, jnp.exp(scores - highest), 0.0)
-        probs = (weights / jnp.sum(weights, axis=-1, keepdims=True)).astype(jnp.bfloat16)
+        weight = jnp.where(same, jnp.exp(scores - highest), 0.0)
+        probs = (weight / jnp.sum(weight, axis=-1, keepdims=True)).astype(jnp.bfloat16)
         attn[:, lanes] = jnp.dot(probs, values, preferred_element_type=jnp.float32).astype(
             jnp.bfloat16
         )
@@ -155,20 +175,33 @@
     for d in range(4):
         first = pl.multiple_of((own ^ d) * rows, rows)
         outs[d][...] = attn[pl.ds(first, rows), :]
-
-
-def attention(queries, key_pool, value_pool, page_table, prompt_lengths):
-    tokens, width = queries.shape
-    smem = [pl.BlockSpec(memory_space=pltpu.SMEM)] * 2
+    copies[5].wait()
+    piece_ref[...] = weights[...].astype(jnp.bfloat16)
+
+
+def attention(queries, key_pool, value_pool, page_table, prompt_lengths, gate_up):
+    tokens, width = queries.shape[1:]
+    rows = gate_up.shape[1] // 2
     return pl.pallas_call(
         attention_kernel,
-        out_shape=[jax.ShapeDtypeStruct((tokens // 4, width), jnp.bfloat16)] * 4,
-        in_specs=smem + vmem(3),
-        out_specs=vmem(4),
-        scratch_shapes=[pltpu.VMEM((tokens, width), jnp.bfloat16)],
+        out_shape=[jax.ShapeDtypeStruct((tokens // 4, width), jnp.bfloat16)] * 4
+        + [jax.ShapeDtypeStruct((rows, gate_up.shape[2]), jnp.bfloat16)],
+        in_specs=[pl.BlockSpec(memory_space=pltpu.HBM)] * 6,
+        out_specs=vmem(5),
+        scratch_shapes=[
+            pltpu.SMEM(page_table.shape, jnp.int32),
+            pltpu.SMEM(prompt_lengths.shape, jnp.int32),
+            pltpu.VMEM((tokens, width), jnp.bfloat16),
+            pltpu.VMEM(key_pool.shape, jnp.bfloat16),
+            pltpu.VMEM(value_pool.shape, jnp.bfloat16),
+            pltpu.VMEM((rows, gate_up.shape[2]), jnp.float32),
+            pltpu.VMEM((tokens, width), jnp.bfloat16),
+            pltpu.SemaphoreType.DMA((6,)),
+        ],
         compiler_params=params(),
+        cost_estimate=SMALL,
         name="attention",
-    )(page_table, prompt_lengths, queries, key_pool, value_pool)
+    )(page_table, prompt_lengths, queries, key_pool, value_pool, gate_up)
 
 
 def norm_kernel(hidden_ref, a0, a1, a2, a3, gain_ref, ids_ref, gates_ref, resid_ref, rows_ref):
@@ -213,48 +246,153 @@
         in_specs=vmem(8),
         out_specs=vmem(2),
         compiler_params=params(),
+        cost_estimate=SMALL,
         name="norm",
     )(hidden_in, *attn, norm_gain[None, :], expert_ids, gate_weights)
 
 
-def up_kernel(sources, pieces, *refs):
+def cast_kernel(up_source, down_source, whole_ref, *refs):
+    piece_refs, (up_ref, down_ref, arrived) = refs[:-3], refs[-3:]
+    total, width = up_ref.shape
+    rows = total // CAST_STEPS
+
+    def copies(step):
+        here = pl.ds(step * rows, rows)
+        late = pl.ds(total + step * rows, rows)
+        return (
+            pltpu.make_async_copy(up_source.at[0, late], up_ref.at[here], arrived.at[step, 0]),
+            pltpu.make_async_copy(down_source.at[0, here], down_ref.at[here], arrived.at[step, 1]),
+        )
+
+    for step in range(CAST_STEPS):
+        for copy in copies(step):
+            copy.start()
+    for step in range(CAST_STEPS):
+        for copy in copies(step):
+            copy.wait()
+        here = slice(step * rows, (step + 1) * rows)
+        whole_ref[here, :width] = up_ref[here].astype(jnp.bfloat16)
+        whole_ref[here, width:] = down_ref[here].astype(jnp.bfloat16)
+        first = 0
+        for ref in piece_refs:
+            ref[here, :] = whole_ref[here, first : first + ref.shape[1]]
+            first += ref.shape[1]
+
+
+def cast_late(gate_up, down, slabs):
+    rows, width = down.shape[1:]
+    depth = gate_up.shape[2]
+    widths = (depth + width, depth + slabs[0], *slabs[1:])
+    return pl.pallas_call(
+        cast_kernel,
+        out_shape=[jax.ShapeDtypeStruct((rows, wide), jnp.bfloat16) for wide in widths],
+        in_specs=[pl.BlockSpec(memory_space=pltpu.HBM)] * 2,
+        out_specs=vmem(len(widths)),
+        scratch_shapes=[
+            pltpu.VMEM((rows, depth), jnp.float32),
+            pltpu.VMEM((rows, width), jnp.float32),
+            pltpu.SemaphoreType.DMA((CAST_STEPS, 2)),
+        ],
+        compiler_params=params(),
+        cost_estimate=SMALL,
+        name="cast_late",
+    )(gate_up, down)
+
+
+def load_tiles(pieces, weights, arrived, tiles, block):
+    def copies(tile):
+        first = 0
+        for index, piece in enumerate(pieces):
+            depth = piece.shape[0]
+            for part in range(2):
+                columns = pl.ds((part * tiles + tile) * block, block)
+                yield pltpu.make_async_copy(
+                    piece.at[:, columns],
+                    weights.at[pl.ds(first, depth), columns],
+                    arrived.at[tile, index, part],
+                )
+            first += depth
+
+    for tile in range(tiles):
+        for copy in copies(tile):
+            copy.start()
+
+    def wait(tile):
+        for copy in copies(tile):
+            copy.wait()
+
+    return wait
+
+
+def early_kernel(sources, pieces, *refs):
     row_refs = refs[:sources]
     weight_refs = refs[sources : sources + pieces]
-    hidden_ref, own_gate_ref, rows, weights, units, arrived = refs[sources + pieces :]
-    tokens, width = rows.shape
-    tiles, _, block = units.shape
-    depth = width // pieces
-
-    def copy(tile, piece, part):
-        columns = pl.ds((part * tiles + tile) * block, block)
-        return pltpu.make_async_copy(
-            weight_refs[piece].at[:, columns],
-            weights.at[pl.ds(piece * depth, depth), columns],
-            arrived.at[tile, piece, part],
-        )
-
-    for tile in range(tiles):
-        for piece in range(pieces):
-            for part in range(2):
-                copy(tile, piece, part).start()
+    total_ref, late_ref, own_gate_ref, rows, weights, arrived = refs[sources + pieces :]
+    width = row_refs[0].shape[1] - LANES
+    depth = width // 4
+    half = depth // 2
+    tiles = 4
+    block = weights.shape[1] // (2 * tiles)
+    wait = load_tiles(weight_refs, weights, arrived, tiles, block)
     expert = lax.axis_index("expert")
     first = 0
     for ref in row_refs:
         count = ref.shape[0]
-        rows[first : first + count, :] = ref[:, :width]
+        here = slice(first, first + count)
+        rows[here, : 2 * depth + half] = ref[:, : 2 * depth + half]
+        rows[here, 2 * depth + half :] = ref[:, 3 * depth : 3 * depth + half]
+        late_ref[here, :half] = ref[:, 2 * depth + half : 3 * depth]
+        late_ref[here, half:] = ref[:, 3 * depth + half : width]
         terms = ref[:, width:].astype(jnp.float32)
         lane = lax.broadcasted_iota(jnp.int32, terms.shape, 1)
-        own_gate_ref[first : first + count, :] = jnp.sum(
+        own_gate_ref[here, :] = jnp.sum(
             jnp.where(lane % TOPK == expert, terms, 0.0), axis=-1, keepdims=True
         )
         first += count
     for tile in range(tiles):
-        for piece in range(pieces):
-            for part in range(2):
-                copy(tile, piece, part).wait()
+        wait(tile)
+        for part in range(2):
+            columns = slice((part * tiles + tile) * block, (part * tiles + tile + 1) * block)
+            total_ref[:, columns] = jnp.dot(
+                rows[...], weights[:, columns], preferred_element_type=jnp.float32
+            )
+
+
+def up_early(rows, weights, width):
+    tokens = sum(piece.shape[0] for piece in rows)
+    features = sum(piece.shape[0] for piece in weights)
+    late = rows[0].shape[1] - LANES - features
+    return pl.pallas_call(
+        lambda *refs: early_kernel(len(rows), len(weights), *refs),
+        out_shape=[
+            jax.ShapeDtypeStruct((tokens, width), jnp.float32),
+            jax.ShapeDtypeStruct((tokens, late), jnp.bfloat16),
+            jax.ShapeDtypeStruct((tokens, 1), jnp.float32),
+        ],
+        in_specs=vmem(len(rows)) + [pl.BlockSpec(memory_space=pl.ANY)] * len(weights),
+        out_specs=vmem(3),
+        scratch_shapes=[
+            pltpu.VMEM((tokens, features), jnp.bfloat16),
+            pltpu.VMEM((features, width), jnp.bfloat16),
+            pltpu.SemaphoreType.DMA((4, len(weights), 2)),
+        ],
+        compiler_params=params(),
+        cost_estimate=SMALL,
+        name="up_early",
+    )(*rows, *weights)
+
+
+def late_kernel(pieces, total_ref, late_ref, *refs):
+    weight_refs = refs[:pieces]
+    hidden_ref, weights, units, arrived = refs[pieces:]
+    tiles, _, block = units.shape
+    wait = load_tiles(weight_refs, weights, arrived, tiles, block)
+    for tile in range(tiles):
+        wait(tile)
         gate, up = (
-            jnp.dot(
-                rows[...],
+            total_ref[:, (part * tiles + tile) * block : (part * tiles + tile + 1) * block]
+            + jnp.dot(
+                late_ref[...],
                 weights[:, (part * tiles + tile) * block : (part * tiles + tile + 1) * block],
                 preferred_element_type=jnp.float32,
             )
@@ -266,71 +404,65 @@
         hidden_ref[:, d * block : (d + 1) * block] = units[own ^ d]
 
 
-def expert_up(rows, weights, hidden_size):
-    tokens = sum(piece.shape[0] for piece in rows)
-    depth, width = weights[0].shape
-    features = depth * len(weights)
+def up_late(total, late, weights):
+    tokens, width = total.shape
+    hidden_size = width // 2
     return pl.pallas_call(
-        lambda *refs: up_kernel(len(rows), len(weights), *refs),
-        out_shape=[
-            jax.ShapeDtypeStruct((tokens, hidden_size), jnp.bfloat16),
-            jax.ShapeDtypeStruct((tokens, 1), jnp.float32),
-        ],
-        in_specs=vmem(len(rows)) + [pl.BlockSpec(memory_space=pl.ANY)] * len(weights),
-        out_specs=vmem(2),
+        lambda *refs: late_kernel(len(weights), *refs),
+        out_shape=jax.ShapeDtypeStruct((tokens, hidden_size), jnp.bfloat16),
+        in_specs=vmem(2) + [pl.BlockSpec(memory_space=pl.ANY)] * len(weights),
+        out_specs=pl.BlockSpec(memory_space=pltpu.VMEM),
         scratch_shapes=[
-            pltpu.VMEM((tokens, features), jnp.bfloat16),
-            pltpu.VMEM((features, width), jnp.bfloat16),
+            pltpu.VMEM((late.shape[1], width), jnp.bfloat16),
             pltpu.VMEM((4, tokens, hidden_size // 4), jnp.bfloat16),
             pltpu.SemaphoreType.DMA((4, len(weights), 2)),
         ],
         compiler_params=params(),
-        cost_estimate=pl.CostEstimate(
-            flops=2 * tokens * features * width,
-            bytes_accessed=2 * features * width,
-            transcendentals=0,
-        ),
-        name="expert_up",
-    )(*rows, *weights)
-
-
-def down_kernel(hidden_ref, gate_ref, w0, w1, w2, w3, out_ref, left_ref, right_ref):
-    block = w0.shape[0]
-    total = None
-    for d, ref in enumerate((w0, w1, w2, w3)):
-        term = jnp.dot(
-            hidden_ref[:, d * block : (d + 1) * block],
-            ref[...],
-            preferred_element_type=jnp.float32,
-        )
-        total = term if total is None else total + term
+        cost_estimate=SMALL,
+        name="up_late",
+    )(total, late, *weights)
+
+
+def down_kernel(firsts, hidden_ref, gate_ref, w0, w1, w2, w3, *refs):
+    out_ref, left_ref, right_ref, weights, arrived = refs
+    depth, width = w0.shape[0], weights.shape[1]
+    copies = [
+        pltpu.make_async_copy(
+            ref.at[:, pl.ds(first, width)], weights.at[pl.ds(d * depth, depth)], arrived.at[d]
+        )
+        for d, (ref, first) in enumerate(zip((w0, w1, w2, w3), firsts))
+    ]
+    for copy in copies:
+        copy.start()
+    for copy in copies:
+        copy.wait()
+    total = jnp.dot(hidden_ref[...], weights[...], preferred_element_type=jnp.float32)
     weighted = (total * gate_ref[...]).astype(jnp.bfloat16)
-    sources, rows, width = out_ref.shape
+    sources, rows, _ = out_ref.shape
     out_ref[...] = weighted.reshape(sources, rows, width)
     middle, half = sources // 2 * rows, rows // 2
     left_ref[...] = weighted[middle : middle + half]
     right_ref[...] = weighted[middle + half : middle + rows]
 
 
-def expert_down(hidden_units, gates, weights, sources):
+def expert_down(hidden_units, gates, weights, firsts, width, sources):
     tokens, hidden_size = hidden_units.shape
-    width = weights[0].shape[1]
     rows = tokens // sources
     return pl.pallas_call(
-        down_kernel,
+        lambda *refs: down_kernel(firsts, *refs),
         out_shape=[
             jax.ShapeDtypeStruct((sources, rows, width), jnp.bfloat16),
             jax.ShapeDtypeStruct((rows // 2, width), jnp.bfloat16),
             jax.ShapeDtypeStruct((rows // 2, width), jnp.bfloat16),
         ],
-        in_specs=vmem(6),
+        in_specs=vmem(2) + [pl.BlockSpec(memory_space=pl.ANY)] * 4,
         out_specs=vmem(3),
+        scratch_shapes=[
+            pltpu.VMEM((hidden_size, width), jnp.bfloat16),
+            pltpu.SemaphoreType.DMA((4,)),
+        ],
         compiler_params=params(),
-        cost_estimate=pl.CostEstimate(
-            flops=2 * tokens * hidden_size * width,
-            bytes_accessed=2 * (hidden_size * width + tokens * hidden_size + tokens * width),
-            transcendentals=0,
-        ),
+        cost_estimate=SMALL,
         name="expert_down",
     )(hidden_units, gates, *weights)
 
@@ -373,12 +505,14 @@
     half = rows // 2
     reach = sources // 2
     up, down = around(left, 1), around(right, -1)
-    yield up, down
+    before = yield up, down
     up = jnp.concatenate([add(weighted[reach - 1, :half], up), weighted[reach - 1, half:]])
     down = jnp.concatenate([weighted[reach + 1, :half], add(weighted[reach + 1, half:], down)])
     for away in range(reach - 2, -1, -1):
+        if before:
+            up, down = after(up, *before), after(down, *before)
         up, down = around(up, 1), around(down, -1)
-        yield up, down
+        before = yield up, down
         if away:
             up = add(weighted[away], up)
             down = add(weighted[sources - away], down)
@@ -397,54 +531,65 @@
     trainer_gate_up,
     trainer_down,
 ):
-    attn = attention(queries[0], key_pool, value_pool, page_table, prompt_lengths)
-    depth = trainer_gate_up.shape[1] // ROW_PIECES
-    width = trainer_down.shape[2]
-    first = width * 5 // 8
-    bounds = [(0, first), (first, width)]
-    gate_up = after(trainer_gate_up[0], attn[0]).astype(jnp.bfloat16)
-    up_own = [gate_up[i * depth : (i + 1) * depth] for i in range(ROW_PIECES)]
-    down = trainer_down[0].astype(jnp.bfloat16)
-    down_own = [down[:, low:high] for low, high in bounds]
+    expert_count = lax.axis_size("expert")
+    width = trainer_gate_up.shape[2]
+    *attn, first_own = attention(
+        queries, key_pool, value_pool, page_table, prompt_lengths, trainer_gate_up
+    )
+    whole_own, joined_own, *slabs_own = cast_late(
+        after(trainer_gate_up, attn[0]), trainer_down, SLABS
+    )
     attn = [attn[0]] + [partner(attn[d], d) for d in (1, 2, 3)]
-    up_across = [partner(after(piece, *attn), 2) for piece in up_own]
+    first_across = partner(after(first_own, *attn), 2)
+    joined_across = partner(after(joined_own, *attn), 2)
     resid, rows = norm(
-        after(hidden_in[0], *up_own), attn, norm_gain, expert_ids[0], gate_weights[0]
+        after(hidden_in[0], joined_own), attn, norm_gain, expert_ids[0], gate_weights[0]
     )
     gathered, arrived = gather_rows(rows)
-    up_beside = [partner(after(piece, *arrived[0]), 1) for piece in up_own]
-    down_beside = [partner(after(piece, *arrived[1]), 1) for piece in down_own]
-    down_across = [
-        partner(after(down_own[0], *arrived[2]), 2),
-        partner(after(down_own[1], up_across[0], *arrived[3]), 2),
+    first_beside = partner(after(first_own, *arrived[0]), 1)
+    whole_beside = partner(after(whole_own, *arrived[1]), 1)
+    first_opposite = partner(after(first_across, *arrived[2]), 1)
+    total, late, gates = up_early(
+        gathered,
+        [first_own, whole_own, first_beside, whole_beside, first_across, first_opposite],
+        width,
+    )
+    joined_opposite = partner(after(joined_across, total), 1)
+    hidden_units = up_late(total, late, [joined_across, joined_opposite])
+    slabs_across = [
+        partner(after(slab, hidden_units if i else arrived[2][0]), 2)
+        for i, slab in enumerate(slabs_own)
     ]
-    up_opposite = [
-        partner(after(up_across[0], *arrived[1]), 1),
-        partner(after(up_across[1], *arrived[3]), 1),
-    ]
-    hidden_units, gates = expert_up(
-        gathered, up_own + up_beside + up_across + up_opposite, trainer_gate_up.shape[2] // 2
-    )
-
-    def down_slab(i, *before):
-        opposite = partner(after(down_across[i], *before), 1)
-        weighted = expert_down(
+
+    def down_slab(i, across, opposite):
+        whole_first = width + sum(SLABS[:i])
+        first = 0 if i else width
+        return expert_down(
             hidden_units,
             gates,
-            (down_own[i], down_beside[i], down_across[i], opposite),
-            lax.axis_size("expert"),
-        )
-        return weighted[0][0], scatter_sum(*weighted)
-
-    own0, sums0 = down_slab(0, hidden_units)
-    own1, sums1 = down_slab(1, *next(sums0))
-    ends = [(own, *list(sums)[-1]) for own, sums in ((own0, sums0), (own1, sums1))]
-    mixed = []
-    for (low, high), terms in zip(bounds, ends):
-        total = resid[:, low:high].astype(jnp.float32)
-        for term in terms:
-            total = total + term.astype(jnp.float32)
-        mixed.append(total.astype(jnp.bfloat16))
+            (whole_own, whole_beside, across, opposite),
+            (whole_first, whole_first, first, first),
+            SLABS[i],
+            expert_count,
+        )
+
+    weighted = [down_slab(0, joined_across, joined_opposite)]
+    sums = [scatter_sum(*weighted[0])]
+    ends = [next(sums[0])]
+    for i, across in enumerate(slabs_across):
+        opposite = partner(after(across, *ends[0], *weighted[i][0:i]), 1)
+        ends[0] = sums[0].send((across, *weighted[i][0:i]))
+        weighted.append(down_slab(i + 1, across, opposite))
+        sums.append(scatter_sum(*weighted[-1]))
+    ends[0] = sums[0].send(weighted[-1][:1])
+    ends += [list(part)[-1] for part in sums[1:]]
+    mixed, first = [], 0
+    for slab, partial, end in zip(SLABS, weighted, ends):
+        sum_here = resid[:, first : first + slab].astype(jnp.float32)
+        for term in (partial[0][0], *end):
+            sum_here = sum_here + term.astype(jnp.float32)
+        mixed.append(sum_here.astype(jnp.bfloat16))
+        first += slab
     return jnp.concatenate(mixed, axis=1)[None]
 
 

time: 125 us -> 145 us (1.16)
  starting transfers between devices: 34.4 us -> 45.5 us
  local copies, waits for them, and re-layouts: 4.72 us -> 10.8 us
  Pallas kernels: 11.9 us -> 16.2 us
  other arithmetic: 5.45 us -> 1.24 us
  waiting for transfers between devices: 68.5 us -> 70.2 us
    ppermute x24 -> x32, starting transfers between devices: 25.5 us -> 36 us  [around(): lax.ppermute(x, 'expert', [(ring[i], ring[(i + step) % count]) for i in r...]
    unnamed x20 -> x36, local copies, waits for them, and re-layouts: 4.35 us -> 10.7 us
    convert_element_type x4 -> x2, other arithmetic: 4.36 us -> 0.14 us  [every_expert(): mixed.append(sum_here.astype(jnp.bfloat16))]
    ppermute x24 -> x32, waiting for transfers between devices: 43 us -> 46.4 us  [around(): lax.ppermute(x, 'expert', [(ring[i], ring[(i + step) % count]) for i in r...]
    pallas_call x3 -> x6, Pallas kernels: 9.81 us -> 12.4 us  [the longest x1 5.74 us: up_early(): pl.pallas_call(lambda *refs: early_kernel(len(rows), len(weights), *refs)...]
    ppermute x15 -> x13, waiting for transfers between devices: 25.5 us -> 23.8 us  [partner(): return lax.ppermute(x, 'dp', [(i, i ^ distance) for i in range(4)])]
    ppermute x15 -> x13, starting transfers between devices: 8.97 us -> 9.53 us  [partner(): return lax.ppermute(x, 'dp', [(i, i ^ distance) for i in range(4)])]
  transfers between devices with their start and end apart: 39 -> 45, of which waited for: 19 -> 23; matrix products, arithmetic and copies ran while one was open for 4% -> 0% of each run, Pallas kernels for 8% -> 9%
where the time goes in v4:
time: 145 us; the launch traced here: 144 us
  waiting for transfers between devices  70.2 us (48%)
  starting transfers between devices  45.5 us (31%)
  Pallas kernels  16.2 us (11%)
  local copies, waits for them, and re-layouts  10.8 us (7%)
    ppermute x32, waiting for transfers between devices, around(): lax.ppermute(x, 'expert', [(ring[i], ring[(i + step) % count]) for i in r...  46.4 us
    ppermute x32, starting transfers between devices, around(): lax.ppermute(x, 'expert', [(ring[i], ring[(i + step) % count]) for i in r...  36 us
    ppermute x13, waiting for transfers between devices, partner(): return lax.ppermute(x, 'dp', [(i, i ^ distance) for i in range(4)])  23.8 us
    unnamed x36, local copies, waits for them, and re-layouts  10.7 us
    ppermute x13, starting transfers between devices, partner(): return lax.ppermute(x, 'dp', [(i, i ^ distance) for i in range(4)])  9.53 us
    pallas_call x1, Pallas kernels, up_early(): pl.pallas_call(lambda *refs: early_kernel(len(rows), len(weights), *refs)...  5.74 us
    pallas_call x3, Pallas kernels, expert_down(): pl.pallas_call(lambda *refs: down_kernel(firsts, *refs), out_shape=[jax.S...  3.46 us
  transfers between devices with their start and end apart: 45, of which 23 were waited for; matrix products, arithmetic and copies ran while one was open for 0% of the time, Pallas kernels for 9%

profile of v4, /device:TPU:0, one launch (start us, length us, event | category | flops | bytes accessed | tf_op | source)
XLA Modules:
  0.0 144.2 jit_solution(9886841776672451666)
XLA Ops:
  0.0 2.2 %copy-done = f32[1,512,2048]{2,1,0:T(8,128)S(1)} copy-done((f32[1,512,2048]{2,1,0:T(8,128)S(1)}, f32[1,512,2048]{2,1,0:T(8,128)}, u32[]{:S(2)}) %copy-start) | copy-done | bytes 4194328
  6.4 2.4 %attention.1 = (bf16[64,512]{1,0:T(8,128)(2,1)S(1)}, bf16[64,512]{1,0:T(8,128)(2,1)}, bf16[64,512]{1,0:T(8,128)(2,1)}, bf16[64,512]{1,0:T(8,128)(2,1)}, bf16[256,2048]{1,0:T(8,128)(2,1)S(1)}) custom-call(s32[1,2]{1,0:T(1,128)S(1)} %copy-done.8, s32[1,4]{1,0:T(1,128)S(1)} %copy-done.9, bf16[1,256,512]{2,1,0:T(8,128)(2,1)S(1)} %copy-done.4, ...), custom_call_target="tpu_custom_call" | custom-call | flops 1 | bytes 1 | tf_op jit(solution)/shard_map/attention/pallas_call | solution.py:185
  9.3 2.6 %collective-permute-start.1 = (bf16[64,512]{1,0:T(8,128)(2,1)}, bf16[64,512]{1,0:T(8,128)(2,1)}, u32[]{:S(2)}, u32[]{:S(2)}) collective-permute-start(bf16[64,512]{1,0:T(8,128)(2,1)} %get-tuple-element.51), channel_id=1, source_target_pairs={{0,16},{8,24},{16,0},{24,8},{1,17},{9,25},{17,1},{25,9},{2,18},{10... | collective-permute-start | bytes 196616 | tf_op jit(solution)/shard_map/ppermute | solution.py:471
  18.3 1.9 %collective-permute-start.7 = (bf16[64,2176]{1,0:T(8,128)(2,1)S(1)}, bf16[64,2176]{1,0:T(8,128)(2,1)S(1)}, u32[]{:S(2)}, u32[]{:S(2)}) collective-permute-start(bf16[64,2176]{1,0:T(8,128)(2,1)S(1)} %get-tuple-element.54.refs_0_), channel_id=1, source_target_pairs={{0,2},{2,4},{4,6},{6,7},{7,5},{5,3},{3,1},{1,0},{8,10},{10,12},{12... | collective-permute-start | bytes 835592 | tf_op jit(solution)/shard_map/ppermute | solution.py:481
  20.4 6.9 %collective-permute-done.7.refs_8_ = bf16[64,2176]{1,0:T(8,128)(2,1)S(1)} collective-permute-done((bf16[64,2176]{1,0:T(8,128)(2,1)S(1)}, bf16[64,2176]{1,0:T(8,128)(2,1)S(1)}, u32[]{:S(2)}, u32[]{:S(2)}) %collective-permute-start.7) | collective-permute-done | bytes 278560 | tf_op jit(solution)/shard_map/ppermute | solution.py:481
  27.3 1.8 %collective-permute-start.8 = (bf16[64,2176]{1,0:T(8,128)(2,1)S(1)}, bf16[64,2176]{1,0:T(8,128)(2,1)S(1)}, u32[]{:S(2)}, u32[]{:S(2)}) collective-permute-start(bf16[64,2176]{1,0:T(8,128)(2,1)S(1)} %collective-permute-done.7.refs_8_), channel_id=1, source_target_pairs={{0,2},{2,4},{4,6},{6,7},{7,5},{5,3},{3,1},{1,0},{8,10},{10,12},{12... | collective-permute-start | bytes 835592 | tf_op jit(solution)/shard_map/ppermute | solution.py:481
  29.3 1.7 %collective-permute-start.13 = (bf16[256,2048]{1,0:T(8,128)(2,1)S(1)}, bf16[256,2048]{1,0:T(8,128)(2,1)S(1)}, u32[]{:S(2)}, u32[]{:S(2)}) collective-permute-start(bf16[256,2048]{1,0:T(8,128)(2,1)S(1)} %get-tuple-element.59.refs_9_), channel_id=1, source_target_pairs={{0,16},{8,24},{16,0},{24,8},{1,17},{9,25},{17,1},{25,9},{2,18},{10... | collective-permute-start | bytes 3145736 | tf_op jit(solution)/shard_map/ppermute | solution.py:471
  31.1 4.4 %collective-permute-done.8.refs_7_ = bf16[64,2176]{1,0:T(8,128)(2,1)S(1)} collective-permute-done((bf16[64,2176]{1,0:T(8,128)(2,1)S(1)}, bf16[64,2176]{1,0:T(8,128)(2,1)S(1)}, u32[]{:S(2)}, u32[]{:S(2)}) %collective-permute-start.8) | collective-permute-done | bytes 278560 | tf_op jit(solution)/shard_map/ppermute | solution.py:481
  40.5 6.8 %collective-permute-done.9.refs_6_ = bf16[64,2176]{1,0:T(8,128)(2,1)S(1)} collective-permute-done((bf16[64,2176]{1,0:T(8,128)(2,1)S(1)}, bf16[64,2176]{1,0:T(8,128)(2,1)S(1)}, u32[]{:S(2)}, u32[]{:S(2)}) %collective-permute-start.9) | collective-permute-done | bytes 278560 | tf_op jit(solution)/shard_map/ppermute | solution.py:481
  48.5 6.9 %collective-permute-done.13.refs_13_ = bf16[256,2048]{1,0:T(8,128)(2,1)S(1)} collective-permute-done((bf16[256,2048]{1,0:T(8,128)(2,1)S(1)}, bf16[256,2048]{1,0:T(8,128)(2,1)S(1)}, u32[]{:S(2)}, u32[]{:S(2)}) %collective-permute-start.13) | collective-permute-done | bytes 1048608 | tf_op jit(solution)/shard_map/ppermute | solution.py:471
  55.5 1.8 %collective-permute-start.10 = (bf16[32,2176]{1,0:T(8,128)(2,1)S(1)}, bf16[32,2176]{1,0:T(8,128)(2,1)S(1)}, u32[]{:S(2)}, u32[]{:S(2)}) collective-permute-start(bf16[32,2176]{1,0:T(8,128)(2,1)S(1)} %slice.129), channel_id=1, source_target_pairs={{0,2},{2,4},{4,6},{6,7},{7,5},{5,3},{3,1},{1,0},{8,10},{10,12},{12... | collective-permute-start | bytes 417800 | tf_op jit(solution)/shard_map/ppermute | solution.py:481
  57.3 4.3 %collective-permute-done.10.refs_5_ = bf16[32,2176]{1,0:T(8,128)(2,1)S(1)} collective-permute-done((bf16[32,2176]{1,0:T(8,128)(2,1)S(1)}, bf16[32,2176]{1,0:T(8,128)(2,1)S(1)}, u32[]{:S(2)}, u32[]{:S(2)}) %collective-permute-start.10) | collective-permute-done | bytes 139296 | tf_op jit(solution)/shard_map/ppermute | solution.py:481
  61.6 1.7 %collective-permute-start.6 = (bf16[32,2176]{1,0:T(8,128)(2,1)S(1)}, bf16[32,2176]{1,0:T(8,128)(2,1)S(1)}, u32[]{:S(2)}, u32[]{:S(2)}) collective-permute-start(bf16[32,2176]{1,0:T(8,128)(2,1)S(1)} %slice.128), channel_id=1, source_target_pairs={{0,1},{2,0},{4,2},{6,4},{7,6},{5,7},{3,5},{1,3},{8,9},{10,8},{12,1... | collective-permute-start | bytes 417800 | tf_op jit(solution)/shard_map/ppermute | solution.py:481
  63.3 3.6 %collective-permute-done.6.refs_4_ = bf16[32,2176]{1,0:T(8,128)(2,1)S(1)} collective-permute-done((bf16[32,2176]{1,0:T(8,128)(2,1)S(1)}, bf16[32,2176]{1,0:T(8,128)(2,1)S(1)}, u32[]{:S(2)}, u32[]{:S(2)}) %collective-permute-start.6) | collective-permute-done | bytes 139296 | tf_op jit(solution)/shard_map/ppermute | solution.py:481
  67.0 5.7 %up_early.1 = (f32[512,2048]{1,0:T(8,128)S(1)}, bf16[512,512]{1,0:T(8,128)(2,1)S(1)}, f32[512,1]{1,0:T(8,128)S(1)}) custom-call(bf16[64,2176]{1,0:T(8,128)(2,1)S(1)} %get-tuple-element.54.refs_0_, bf16[64,2176]{1,0:T(8,128)(2,1)S(1)} %collective-permute-done.3.refs_1_, bf16[64,2176]{1,0:T(8,128)(2,1)S(1)} %collective-permute-done.4.refs_2_, ...), custom_call_target="tpu_custom_call" | custom-call | flops 1 | bytes 1 | tf_op jit(solution)/shard_map/up_early/pallas_call | solution.py:365
  72.7 11.6 %collective-permute-done.15.refs_2_.refs_4_ = bf16[256,2816]{1,0:T(8,128)(2,1)S(1)} collective-permute-done((bf16[256,2816]{1,0:T(8,128)(2,1)}, bf16[256,2816]{1,0:T(8,128)(2,1)S(1)}, u32[]{:S(2)}, u32[]{:S(2)}) %collective-permute-start.15) | collective-permute-done | bytes 1441824 | tf_op jit(solution)/shard_map/ppermute | solution.py:471
  84.3 1.7 %collective-permute-start.18 = (bf16[256,768]{1,0:T(8,128)(2,1)S(1)}, bf16[256,768]{1,0:T(8,128)(2,1)S(1)}, u32[]{:S(2)}, u32[]{:S(2)}) collective-permute-start(bf16[256,768]{1,0:T(8,128)(2,1)S(1)} %copy-done.12), channel_id=1, source_target_pairs={{0,16},{8,24},{16,0},{24,8},{1,17},{9,25},{17,1},{25,9},{2,18},{10... | collective-permute-start | bytes 1179656 | tf_op jit(solution)/shard_map/ppermute | solution.py:471
  87.6 2.6 %up_late.1.refs_0_ = bf16[512,1024]{1,0:T(8,128)(2,1)S(1)} custom-call(f32[512,2048]{1,0:T(8,128)S(1)} %get-tuple-element.61.refs_0_, bf16[512,512]{1,0:T(8,128)(2,1)S(1)} %get-tuple-element.62.refs_1_, bf16[256,2816]{1,0:T(8,128)(2,1)S(1)} %collective-permute-done.15.refs_2_.refs_4_, bf16[256,2816]{1,0:T(8,128)(2,1)S(1)} %collective-permute-done.16.refs_3_.refs_5_), custom_call_target="tpu_custom_call" | custom-call | flops 1 | bytes 1 | tf_op jit(solution)/shard_map/up_late/pallas_call | solution.py:410
  91.3 1.8 %collective-permute-start.17 = (bf16[32,768]{1,0:T(8,128)(2,1)S(1)}, bf16[32,768]{1,0:T(8,128)(2,1)S(1)}, u32[]{:S(2)}, u32[]{:S(2)}) collective-permute-start(bf16[32,768]{1,0:T(8,128)(2,1)S(1)} %get-tuple-element.67), channel_id=1, source_target_pairs={{0,2},{2,4},{4,6},{6,7},{7,5},{5,3},{3,1},{1,0},{8,10},{10,12},{12... | collective-permute-start | bytes 147464 | tf_op jit(solution)/shard_map/ppermute | solution.py:481
  93.4 2.5 %collective-permute-done.18.refs_4_ = bf16[256,768]{1,0:T(8,128)(2,1)S(1)} collective-permute-done((bf16[256,768]{1,0:T(8,128)(2,1)S(1)}, bf16[256,768]{1,0:T(8,128)(2,1)S(1)}, u32[]{:S(2)}, u32[]{:S(2)}) %collective-permute-start.18) | collective-permute-done | bytes 393248 | tf_op jit(solution)/shard_map/ppermute | solution.py:471
  97.3 1.6 %collective-permute-start.19 = (bf16[64,768]{1,0:T(8,128)(2,1)S(1)}, bf16[64,768]{1,0:T(8,128)(2,1)S(1)}, u32[]{:S(2)}, u32[]{:S(2)}) collective-permute-start(bf16[64,768]{1,0:T(8,128)(2,1)S(1)} %get-tuple-element.70), channel_id=1, source_target_pairs={{0,2},{2,4},{4,6},{6,7},{7,5},{5,3},{3,1},{1,0},{8,10},{10,12},{12... | collective-permute-start | bytes 294920 | tf_op jit(solution)/shard_map/ppermute | solution.py:481
  100.8 1.7 %collective-permute-done.19 = bf16[64,768]{1,0:T(8,128)(2,1)S(1)} collective-permute-done((bf16[64,768]{1,0:T(8,128)(2,1)S(1)}, bf16[64,768]{1,0:T(8,128)(2,1)S(1)}, u32[]{:S(2)}, u32[]{:S(2)}) %collective-permute-start.19) | collective-permute-done | bytes 98336 | tf_op jit(solution)/shard_map/ppermute | solution.py:481
  104.0 1.6 %collective-permute-start.29 = (bf16[32,768]{1,0:T(8,128)(2,1)S(1)}, bf16[32,768]{1,0:T(8,128)(2,1)S(1)}, u32[]{:S(2)}, u32[]{:S(2)}) collective-permute-start(bf16[32,768]{1,0:T(8,128)(2,1)S(1)} %get-tuple-element.83), channel_id=1, source_target_pairs={{0,2},{2,4},{4,6},{6,7},{7,5},{5,3},{3,1},{1,0},{8,10},{10,12},{12... | collective-permute-start | bytes 147464 | tf_op jit(solution)/shard_map/ppermute | solution.py:481
  112.5 2.5 %collective-permute-done.30 = bf16[64,768]{1,0:T(8,128)(2,1)S(1)} collective-permute-done((bf16[64,768]{1,0:T(8,128)(2,1)S(1)}, bf16[64,768]{1,0:T(8,128)(2,1)S(1)}, u32[]{:S(2)}, u32[]{:S(2)}) %collective-permute-start.30) | collective-permute-done | bytes 98336 | tf_op jit(solution)/shard_map/ppermute | solution.py:481
  115.0 1.6 %collective-permute-start.31 = (bf16[64,768]{1,0:T(8,128)(2,1)S(1)}, bf16[64,768]{1,0:T(8,128)(2,1)S(1)}, u32[]{:S(2)}, u32[]{:S(2)}) collective-permute-start(bf16[64,768]{1,0:T(8,128)(2,1)S(1)} %fusion.2), channel_id=1, source_target_pairs={{0,2},{2,4},{4,6},{6,7},{7,5},{5,3},{3,1},{1,0},{8,10},{10,12},{12... | collective-permute-start | bytes 294920 | tf_op jit(solution)/shard_map/ppermute | solution.py:481
  117.6 1.6 %collective-permute-start.37 = (bf16[32,512]{1,0:T(8,128)(2,1)S(1)}, bf16[32,512]{1,0:T(8,128)(2,1)S(1)}, u32[]{:S(2)}, u32[]{:S(2)}) collective-permute-start(bf16[32,512]{1,0:T(8,128)(2,1)S(1)} %get-tuple-element.85), channel_id=1, source_target_pairs={{0,2},{2,4},{4,6},{6,7},{7,5},{5,3},{3,1},{1,0},{8,10},{10,12},{12... | collective-permute-start | bytes 98312 | tf_op jit(solution)/shard_map/ppermute | solution.py:481
  119.6 1.9 %collective-permute-done.37 = bf16[32,512]{1,0:T(8,128)(2,1)S(1)} collective-permute-done((bf16[32,512]{1,0:T(8,128)(2,1)S(1)}, bf16[32,512]{1,0:T(8,128)(2,1)S(1)}, u32[]{:S(2)}, u32[]{:S(2)}) %collective-permute-start.37) | collective-permute-done | bytes 32800 | tf_op jit(solution)/shard_map/ppermute | solution.py:481
  123.1 1.9 %collective-permute-start.38 = (bf16[64,512]{1,0:T(8,128)(2,1)S(1)}, bf16[64,512]{1,0:T(8,128)(2,1)S(1)}, u32[]{:S(2)}, u32[]{:S(2)}) collective-permute-start(bf16[64,512]{1,0:T(8,128)(2,1)S(1)} %pad_maximum_fusion.4), channel_id=1, source_target_pairs={{0,2},{2,4},{4,6},{6,7},{7,5},{5,3},{3,1},{1,0},{8,10},{10,12},{12... | collective-permute-start | bytes 196616 | tf_op jit(solution)/shard_map/ppermute | solution.py:481
  125.2 2.6 %collective-permute-done.38 = bf16[64,512]{1,0:T(8,128)(2,1)S(1)} collective-permute-done((bf16[64,512]{1,0:T(8,128)(2,1)S(1)}, bf16[64,512]{1,0:T(8,128)(2,1)S(1)}, u32[]{:S(2)}, u32[]{:S(2)}) %collective-permute-start.38) | collective-permute-done | bytes 65568 | tf_op jit(solution)/shard_map/ppermute | solution.py:481
  127.9 2.1 %collective-permute-start.39 = (bf16[64,512]{1,0:T(8,128)(2,1)S(1)}, bf16[64,512]{1,0:T(8,128)(2,1)S(1)}, u32[]{:S(2)}, u32[]{:S(2)}) collective-permute-start(bf16[64,512]{1,0:T(8,128)(2,1)S(1)} %fusion.16), channel_id=1, source_target_pairs={{0,2},{2,4},{4,6},{6,7},{7,5},{5,3},{3,1},{1,0},{8,10},{10,12},{12... | collective-permute-start | bytes 196616 | tf_op jit(solution)/shard_map/ppermute | solution.py:481
  135.7 1.6 %collective-permute-start.36 = (bf16[64,768]{1,0:T(8,128)(2,1)S(1)}, bf16[64,768]{1,0:T(8,128)(2,1)S(1)}, u32[]{:S(2)}, u32[]{:S(2)}) collective-permute-start(bf16[64,768]{1,0:T(8,128)(2,1)S(1)} %fusion.1), channel_id=1, source_target_pairs={{0,1},{2,0},{4,2},{6,4},{7,6},{5,7},{3,5},{1,3},{8,9},{10,8},{12,1... | collective-permute-start | bytes 294920 | tf_op jit(solution)/shard_map/ppermute | solution.py:481
  140.8 2.0 %collective-permute-done.40 = bf16[64,512]{1,0:T(8,128)(2,1)S(1)} collective-permute-done((bf16[64,512]{1,0:T(8,128)(2,1)S(1)}, bf16[64,512]{1,0:T(8,128)(2,1)S(1)}, u32[]{:S(2)}, u32[]{:S(2)}) %collective-permute-start.40) | collective-permute-done | bytes 65568 | tf_op jit(solution)/shard_map/ppermute | solution.py:481
  (127 shorter events, 46.2 us)
Async XLA Ops:
  8.8 8.2 %collective-permute-start = (bf16[64,512]{1,0:T(8,128)(2,1)}, bf16[64,512]{1,0:T(8,128)(2,1)}, u32[]{:S(2)}, u32[]{:S(2)}) collective-permute-start(bf16[64,512]{1,0:T(8,128)(2,1)} %get-tuple-element.50), channel_id=1, source_target_pairs={{0,8},{8,0},{16,24},{24,16},{1,9},{9,1},{17,25},{25,17},{2,10},{10... | collective-permute-start | bytes 196616 | tf_op jit(solution)/shard_map/ppermute | solution.py:471
  9.3 7.7 %collective-permute-start.1 = (bf16[64,512]{1,0:T(8,128)(2,1)}, bf16[64,512]{1,0:T(8,128)(2,1)}, u32[]{:S(2)}, u32[]{:S(2)}) collective-permute-start(bf16[64,512]{1,0:T(8,128)(2,1)} %get-tuple-element.51), channel_id=1, source_target_pairs={{0,16},{8,24},{16,0},{24,8},{1,17},{9,25},{17,1},{25,9},{2,18},{10... | collective-permute-start | bytes 196616 | tf_op jit(solution)/shard_map/ppermute | solution.py:471
  11.9 5.1 %collective-permute-start.2 = (bf16[64,512]{1,0:T(8,128)(2,1)}, bf16[64,512]{1,0:T(8,128)(2,1)}, u32[]{:S(2)}, u32[]{:S(2)}) collective-permute-start(bf16[64,512]{1,0:T(8,128)(2,1)} %get-tuple-element.52), channel_id=1, source_target_pairs={{0,24},{8,16},{16,8},{24,0},{1,25},{9,17},{17,9},{25,1},{2,26},{10... | collective-permute-start | bytes 196616 | tf_op jit(solution)/shard_map/ppermute | solution.py:471
  18.3 9.0 %collective-permute-start.7 = (bf16[64,2176]{1,0:T(8,128)(2,1)S(1)}, bf16[64,2176]{1,0:T(8,128)(2,1)S(1)}, u32[]{:S(2)}, u32[]{:S(2)}) collective-permute-start(bf16[64,2176]{1,0:T(8,128)(2,1)S(1)} %get-tuple-element.54.refs_0_), channel_id=1, source_target_pairs={{0,2},{2,4},{4,6},{6,7},{7,5},{5,3},{3,1},{1,0},{8,10},{10,12},{12... | collective-permute-start | bytes 835592 | tf_op jit(solution)/shard_map/ppermute | solution.py:481
  20.2 8.9 %collective-permute-start.3 = (bf16[64,2176]{1,0:T(8,128)(2,1)S(1)}, bf16[64,2176]{1,0:T(8,128)(2,1)S(1)}, u32[]{:S(2)}, u32[]{:S(2)}) collective-permute-start(bf16[64,2176]{1,0:T(8,128)(2,1)S(1)} %get-tuple-element.54.refs_0_), channel_id=1, source_target_pairs={{0,1},{2,0},{4,2},{6,4},{7,6},{5,7},{3,5},{1,3},{8,9},{10,8},{12,1... | collective-permute-start | bytes 835592 | tf_op jit(solution)/shard_map/ppermute | solution.py:481
  27.3 8.1 %collective-permute-start.8 = (bf16[64,2176]{1,0:T(8,128)(2,1)S(1)}, bf16[64,2176]{1,0:T(8,128)(2,1)S(1)}, u32[]{:S(2)}, u32[]{:S(2)}) collective-permute-start(bf16[64,2176]{1,0:T(8,128)(2,1)S(1)} %collective-permute-done.7.refs_8_), channel_id=1, source_target_pairs={{0,2},{2,4},{4,6},{6,7},{7,5},{5,3},{3,1},{1,0},{8,10},{10,12},{12... | collective-permute-start | bytes 835592 | tf_op jit(solution)/shard_map/ppermute | solution.py:481
  29.1 7.8 %collective-permute-start.4 = (bf16[64,2176]{1,0:T(8,128)(2,1)S(1)}, bf16[64,2176]{1,0:T(8,128)(2,1)S(1)}, u32[]{:S(2)}, u32[]{:S(2)}) collective-permute-start(bf16[64,2176]{1,0:T(8,128)(2,1)S(1)} %collective-permute-done.3.refs_1_), channel_id=1, source_target_pairs={{0,1},{2,0},{4,2},{6,4},{7,6},{5,7},{3,5},{1,3},{8,9},{10,8},{12,1... | collective-permute-start | bytes 835592 | tf_op jit(solution)/shard_map/ppermute | solution.py:481
  29.3 26.1 %collective-permute-start.13 = (bf16[256,2048]{1,0:T(8,128)(2,1)S(1)}, bf16[256,2048]{1,0:T(8,128)(2,1)S(1)}, u32[]{:S(2)}, u32[]{:S(2)}) collective-permute-start(bf16[256,2048]{1,0:T(8,128)(2,1)S(1)} %get-tuple-element.59.refs_9_), channel_id=1, source_target_pairs={{0,16},{8,24},{16,0},{24,8},{1,17},{9,25},{17,1},{25,9},{2,18},{10... | collective-permute-start | bytes 3145736 | tf_op jit(solution)/shard_map/ppermute | solution.py:471
  36.9 30.0 %collective-permute-start.12 = (bf16[256,4096]{1,0:T(8,128)(2,1)S(1)}, bf16[256,4096]{1,0:T(8,128)(2,1)S(1)}, u32[]{:S(2)}, u32[]{:S(2)}) collective-permute-start(bf16[256,4096]{1,0:T(8,128)(2,1)S(1)} %get-tuple-element.58.refs_10_.refs_2_), channel_id=1, source_target_pairs={{0,8},{8,0},{16,24},{24,16},{1,9},{9,1},{17,25},{25,17},{2,10},{10... | collective-permute-start | bytes 6291464 | tf_op jit(solution)/shard_map/ppermute | solution.py:471
  36.9 47.4 %collective-permute-start.15 = (bf16[256,2816]{1,0:T(8,128)(2,1)}, bf16[256,2816]{1,0:T(8,128)(2,1)S(1)}, u32[]{:S(2)}, u32[]{:S(2)}) collective-permute-start(bf16[256,2816]{1,0:T(8,128)(2,1)} %copy-done.10), channel_id=1, source_target_pairs={{0,16},{8,24},{16,0},{24,8},{1,17},{9,25},{17,1},{25,9},{2,18},{10... | collective-permute-start | bytes 4325384 | tf_op jit(solution)/shard_map/ppermute | solution.py:471
  38.4 8.8 %collective-permute-start.9 = (bf16[64,2176]{1,0:T(8,128)(2,1)S(1)}, bf16[64,2176]{1,0:T(8,128)(2,1)S(1)}, u32[]{:S(2)}, u32[]{:S(2)}) collective-permute-start(bf16[64,2176]{1,0:T(8,128)(2,1)S(1)} %collective-permute-done.8.refs_7_), channel_id=1, source_target_pairs={{0,2},{2,4},{4,6},{6,7},{7,5},{5,3},{3,1},{1,0},{8,10},{10,12},{12... | collective-permute-start | bytes 835592 | tf_op jit(solution)/shard_map/ppermute | solution.py:481
  40.0 8.5 %collective-permute-start.5 = (bf16[64,2176]{1,0:T(8,128)(2,1)S(1)}, bf16[64,2176]{1,0:T(8,128)(2,1)S(1)}, u32[]{:S(2)}, u32[]{:S(2)}) collective-permute-start(bf16[64,2176]{1,0:T(8,128)(2,1)S(1)} %collective-permute-done.4.refs_2_), channel_id=1, source_target_pairs={{0,1},{2,0},{4,2},{6,4},{7,6},{5,7},{3,5},{1,3},{8,9},{10,8},{12,1... | collective-permute-start | bytes 835592 | tf_op jit(solution)/shard_map/ppermute | solution.py:481
  47.2 19.7 %collective-permute-start.11 = (bf16[256,2048]{1,0:T(8,128)(2,1)S(1)}, bf16[256,2048]{1,0:T(8,128)(2,1)S(1)}, u32[]{:S(2)}, u32[]{:S(2)}) collective-permute-start(bf16[256,2048]{1,0:T(8,128)(2,1)S(1)} %get-tuple-element.59.refs_9_), channel_id=1, source_target_pairs={{0,8},{8,0},{16,24},{24,16},{1,9},{9,1},{17,25},{25,17},{2,10},{10... | collective-permute-start | bytes 3145736 | tf_op jit(solution)/shard_map/ppermute | solution.py:471
  55.4 11.5 %collective-permute-start.14 = (bf16[256,2048]{1,0:T(8,128)(2,1)S(1)}, bf16[256,2048]{1,0:T(8,128)(2,1)S(1)}, u32[]{:S(2)}, u32[]{:S(2)}) collective-permute-start(bf16[256,2048]{1,0:T(8,128)(2,1)S(1)} %collective-permute-done.13.refs_13_), channel_id=1, source_target_pairs={{0,8},{8,0},{16,24},{24,16},{1,9},{9,1},{17,25},{25,17},{2,10},{10... | collective-permute-start | bytes 3145736 | tf_op jit(solution)/shard_map/ppermute | solution.py:471
  55.5 6.1 %collective-permute-start.10 = (bf16[32,2176]{1,0:T(8,128)(2,1)S(1)}, bf16[32,2176]{1,0:T(8,128)(2,1)S(1)}, u32[]{:S(2)}, u32[]{:S(2)}) collective-permute-start(bf16[32,2176]{1,0:T(8,128)(2,1)S(1)} %slice.129), channel_id=1, source_target_pairs={{0,2},{2,4},{4,6},{6,7},{7,5},{5,3},{3,1},{1,0},{8,10},{10,12},{12... | collective-permute-start | bytes 417800 | tf_op jit(solution)/shard_map/ppermute | solution.py:481
  61.6 5.4 %collective-permute-start.6 = (bf16[32,2176]{1,0:T(8,128)(2,1)S(1)}, bf16[32,2176]{1,0:T(8,128)(2,1)S(1)}, u32[]{:S(2)}, u32[]{:S(2)}) collective-permute-start(bf16[32,2176]{1,0:T(8,128)(2,1)S(1)} %slice.128), channel_id=1, source_target_pairs={{0,1},{2,0},{4,2},{6,4},{7,6},{5,7},{3,5},{1,3},{8,9},{10,8},{12,1... | collective-permute-start | bytes 417800 | tf_op jit(solution)/shard_map/ppermute | solution.py:481
  84.3 11.5 %collective-permute-start.18 = (bf16[256,768]{1,0:T(8,128)(2,1)S(1)}, bf16[256,768]{1,0:T(8,128)(2,1)S(1)}, u32[]{:S(2)}, u32[]{:S(2)}) collective-permute-start(bf16[256,768]{1,0:T(8,128)(2,1)S(1)} %copy-done.12), channel_id=1, source_target_pairs={{0,16},{8,24},{16,0},{24,8},{1,17},{9,25},{17,1},{25,9},{2,18},{10... | collective-permute-start | bytes 1179656 | tf_op jit(solution)/shard_map/ppermute | solution.py:471
  97.2 5.3 %collective-permute-start.22 = (bf16[256,768]{1,0:T(8,128)(2,1)S(1)}, bf16[256,768]{1,0:T(8,128)(2,1)S(1)}, u32[]{:S(2)}, u32[]{:S(2)}) collective-permute-start(bf16[256,768]{1,0:T(8,128)(2,1)S(1)} %collective-permute-done.18.refs_4_), channel_id=1, source_target_pairs={{0,8},{8,0},{16,24},{24,16},{1,9},{9,1},{17,25},{25,17},{2,10},{10... | collective-permute-start | bytes 1179656 | tf_op jit(solution)/shard_map/ppermute | solution.py:471
  97.3 5.3 %collective-permute-start.19 = (bf16[64,768]{1,0:T(8,128)(2,1)S(1)}, bf16[64,768]{1,0:T(8,128)(2,1)S(1)}, u32[]{:S(2)}, u32[]{:S(2)}) collective-permute-start(bf16[64,768]{1,0:T(8,128)(2,1)S(1)} %get-tuple-element.70), channel_id=1, source_target_pairs={{0,2},{2,4},{4,6},{6,7},{7,5},{5,3},{3,1},{1,0},{8,10},{10,12},{12... | collective-permute-start | bytes 294920 | tf_op jit(solution)/shard_map/ppermute | solution.py:481
  98.9 8.4 %collective-permute-start.20 = (bf16[256,512]{1,0:T(8,128)(2,1)S(1)}, bf16[256,512]{1,0:T(8,128)(2,1)S(1)}, u32[]{:S(2)}, u32[]{:S(2)}) collective-permute-start(bf16[256,512]{1,0:T(8,128)(2,1)S(1)} %copy-done.14), channel_id=1, source_target_pairs={{0,16},{8,24},{16,0},{24,8},{1,17},{9,25},{17,1},{25,9},{2,18},{10... | collective-permute-start | bytes 786440 | tf_op jit(solution)/shard_map/ppermute | solution.py:471
  100.4 5.7 %collective-permute-start.24 = (bf16[64,768]{1,0:T(8,128)(2,1)S(1)}, bf16[64,768]{1,0:T(8,128)(2,1)S(1)}, u32[]{:S(2)}, u32[]{:S(2)}) collective-permute-start(bf16[64,768]{1,0:T(8,128)(2,1)S(1)} %get-tuple-element.77), channel_id=1, source_target_pairs={{0,1},{2,0},{4,2},{6,4},{7,6},{5,7},{3,5},{1,3},{8,9},{10,8},{12,1... | collective-permute-start | bytes 294920 | tf_op jit(solution)/shard_map/ppermute | solution.py:481
  104.0 4.9 %collective-permute-start.29 = (bf16[32,768]{1,0:T(8,128)(2,1)S(1)}, bf16[32,768]{1,0:T(8,128)(2,1)S(1)}, u32[]{:S(2)}, u32[]{:S(2)}) collective-permute-start(bf16[32,768]{1,0:T(8,128)(2,1)S(1)} %get-tuple-element.83), channel_id=1, source_target_pairs={{0,2},{2,4},{4,6},{6,7},{7,5},{5,3},{3,1},{1,0},{8,10},{10,12},{12... | collective-permute-start | bytes 147464 | tf_op jit(solution)/shard_map/ppermute | solution.py:481
  108.9 7.8 %collective-permute-start.25 = (bf16[256,512]{1,0:T(8,128)(2,1)S(1)}, bf16[256,512]{1,0:T(8,128)(2,1)S(1)}, u32[]{:S(2)}, u32[]{:S(2)}) collective-permute-start(bf16[256,512]{1,0:T(8,128)(2,1)S(1)} %collective-permute-done.20.refs_4_), channel_id=1, source_target_pairs={{0,8},{8,0},{16,24},{24,16},{1,9},{9,1},{17,25},{25,17},{2,10},{10... | collective-permute-start | bytes 786440 | tf_op jit(solution)/shard_map/ppermute | solution.py:471
  109.8 20.2 %collective-permute-start.34 = (bf16[64,768]{1,0:T(8,128)(2,1)S(1)}, bf16[64,768]{1,0:T(8,128)(2,1)S(1)}, u32[]{:S(2)}, u32[]{:S(2)}) collective-permute-start(bf16[64,768]{1,0:T(8,128)(2,1)S(1)} %pad_maximum_fusion.3), channel_id=1, source_target_pairs={{0,1},{2,0},{4,2},{6,4},{7,6},{5,7},{3,5},{1,3},{8,9},{10,8},{12,1... | collective-permute-start | bytes 294920 | tf_op jit(solution)/shard_map/ppermute | solution.py:481
  115.0 15.0 %collective-permute-start.31 = (bf16[64,768]{1,0:T(8,128)(2,1)S(1)}, bf16[64,768]{1,0:T(8,128)(2,1)S(1)}, u32[]{:S(2)}, u32[]{:S(2)}) collective-permute-start(bf16[64,768]{1,0:T(8,128)(2,1)S(1)} %fusion.2), channel_id=1, source_target_pairs={{0,2},{2,4},{4,6},{6,7},{7,5},{5,3},{3,1},{1,0},{8,10},{10,12},{12... | collective-permute-start | bytes 294920 | tf_op jit(solution)/shard_map/ppermute | solution.py:481
  125.0 7.7 %collective-permute-start.42 = (bf16[64,512]{1,0:T(8,128)(2,1)S(1)}, bf16[64,512]{1,0:T(8,128)(2,1)S(1)}, u32[]{:S(2)}, u32[]{:S(2)}) collective-permute-start(bf16[64,512]{1,0:T(8,128)(2,1)S(1)} %pad_maximum_fusion.5), channel_id=1, source_target_pairs={{0,1},{2,0},{4,2},{6,4},{7,6},{5,7},{3,5},{1,3},{8,9},{10,8},{12,1... | collective-permute-start | bytes 196616 | tf_op jit(solution)/shard_map/ppermute | solution.py:481
  127.9 6.3 %collective-permute-start.39 = (bf16[64,512]{1,0:T(8,128)(2,1)S(1)}, bf16[64,512]{1,0:T(8,128)(2,1)S(1)}, u32[]{:S(2)}, u32[]{:S(2)}) collective-permute-start(bf16[64,512]{1,0:T(8,128)(2,1)S(1)} %fusion.16), channel_id=1, source_target_pairs={{0,2},{2,4},{4,6},{6,7},{7,5},{5,3},{3,1},{1,0},{8,10},{10,12},{12... | collective-permute-start | bytes 196616 | tf_op jit(solution)/shard_map/ppermute | solution.py:481
  130.1 9.0 %collective-permute-start.32 = (bf16[64,768]{1,0:T(8,128)(2,1)S(1)}, bf16[64,768]{1,0:T(8,128)(2,1)S(1)}, u32[]{:S(2)}, u32[]{:S(2)}) collective-permute-start(bf16[64,768]{1,0:T(8,128)(2,1)S(1)} %get-tuple-element.89), channel_id=1, source_target_pairs={{0,2},{2,4},{4,6},{6,7},{7,5},{5,3},{3,1},{1,0},{8,10},{10,12},{12... | collective-permute-start | bytes 294920 | tf_op jit(solution)/shard_map/ppermute | solution.py:481
  130.7 5.0 %collective-permute-start.35 = (bf16[64,768]{1,0:T(8,128)(2,1)S(1)}, bf16[64,768]{1,0:T(8,128)(2,1)S(1)}, u32[]{:S(2)}, u32[]{:S(2)}) collective-permute-start(bf16[64,768]{1,0:T(8,128)(2,1)S(1)} %get-tuple-element.90), channel_id=1, source_target_pairs={{0,1},{2,0},{4,2},{6,4},{7,6},{5,7},{3,5},{1,3},{8,9},{10,8},{12,1... | collective-permute-start | bytes 294920 | tf_op jit(solution)/shard_map/ppermute | solution.py:481
  132.2 8.5 %collective-permute-start.26 = (bf16[64,768]{1,0:T(8,128)(2,1)S(1)}, bf16[64,768]{1,0:T(8,128)(2,1)S(1)}, u32[]{:S(2)}, u32[]{:S(2)}) collective-permute-start(bf16[64,768]{1,0:T(8,128)(2,1)S(1)} %get-tuple-element.80), channel_id=1, source_target_pairs={{0,2},{2,4},{4,6},{6,7},{7,5},{5,3},{3,1},{1,0},{8,10},{10,12},{12... | collective-permute-start | bytes 294920 | tf_op jit(solution)/shard_map/ppermute | solution.py:481
  132.7 8.0 %collective-permute-start.28 = (bf16[64,768]{1,0:T(8,128)(2,1)S(1)}, bf16[64,768]{1,0:T(8,128)(2,1)S(1)}, u32[]{:S(2)}, u32[]{:S(2)}) collective-permute-start(bf16[64,768]{1,0:T(8,128)(2,1)S(1)} %fusion.8), channel_id=1, source_target_pairs={{0,1},{2,0},{4,2},{6,4},{7,6},{5,7},{3,5},{1,3},{8,9},{10,8},{12,1... | collective-permute-start | bytes 294920 | tf_op jit(solution)/shard_map/ppermute | solution.py:481
  135.7 5.0 %collective-permute-start.36 = (bf16[64,768]{1,0:T(8,128)(2,1)S(1)}, bf16[64,768]{1,0:T(8,128)(2,1)S(1)}, u32[]{:S(2)}, u32[]{:S(2)}) collective-permute-start(bf16[64,768]{1,0:T(8,128)(2,1)S(1)} %fusion.1), channel_id=1, source_target_pairs={{0,1},{2,0},{4,2},{6,4},{7,6},{5,7},{3,5},{1,3},{8,9},{10,8},{12,1... | collective-permute-start | bytes 294920 | tf_op jit(solution)/shard_map/ppermute | solution.py:481
  (30 other events, 120.8 us)

commit v5 on v3

--- a/solution.py
+++ b/solution.py
@@ -111,21 +111,38 @@
 
 LANES = 128
 VMEM_LIMIT = 32 * 2**20
-ROW_PIECES = 2
-
-
-def params():
-    return pltpu.CompilerParams(vmem_limit_bytes=VMEM_LIMIT)
+VMEM_MOST = 60 * 2**20
+SLABS = 2
+CAST_STEPS = 4
+SMALL = pl.CostEstimate(flops=1, bytes_accessed=1, transcendentals=0)
+
+
+def params(limit=VMEM_LIMIT):
+    return pltpu.CompilerParams(vmem_limit_bytes=limit)
 
 
 def vmem(count):
     return [pl.BlockSpec(memory_space=pltpu.VMEM)] * count
 
 
-def attention_kernel(table, lengths, q_ref, k_ref, v_ref, *refs):
-    outs, attn = refs[:4], refs[4]
+def attention_kernel(*refs):
+    sources, outs, scratch = refs[:5], refs[5:9], refs[9:]
+    table, lengths, q_ref, k_ref, v_ref, attn, arrived = scratch
+    copies = [
+        pltpu.make_async_copy(source, target, arrived.at[i])
+        for i, (source, target) in enumerate(
+            zip(
+                (*sources[:2], sources[2].at[0], *sources[3:5]),
+                (table, lengths, q_ref, k_ref, v_ref),
+            )
+        )
+    ]
+    for copy in copies:
+        copy.start()
+    for copy in copies:
+        copy.wait()
     tokens, width = q_ref.shape
-    pages, page = k_ref.shape[0], k_ref.shape[1]
+    pages = k_ref.shape[0]
     row = lax.broadcasted_iota(jnp.int32, (tokens, tokens), 0)
     column = lax.broadcasted_iota(jnp.int32, (tokens, tokens), 1)
     row_request = jnp.zeros((tokens, tokens), jnp.int32)
@@ -145,8 +162,8 @@
         ) * (1.0 / math.sqrt(HDIM))
         scores = jnp.where(same, scores, -1e30)
         highest = jnp.max(scores, axis=-1, keepdims=True)
-        weights = jnp.where(same, jnp.exp(scores - highest), 0.0)
-        probs = (weights / jnp.sum(weights, axis=-1, keepdims=True)).astype(jnp.bfloat16)
+        weight = jnp.where(same, jnp.exp(scores - highest), 0.0)
+        probs = (weight / jnp.sum(weight, axis=-1, keepdims=True)).astype(jnp.bfloat16)
         attn[:, lanes] = jnp.dot(probs, values, preferred_element_type=jnp.float32).astype(
             jnp.bfloat16
         )
@@ -158,15 +175,22 @@
 
 
 def attention(queries, key_pool, value_pool, page_table, prompt_lengths):
-    tokens, width = queries.shape
-    smem = [pl.BlockSpec(memory_space=pltpu.SMEM)] * 2
+    tokens, width = queries.shape[1:]
     return pl.pallas_call(
         attention_kernel,
         out_shape=[jax.ShapeDtypeStruct((tokens // 4, width), jnp.bfloat16)] * 4,
-        in_specs=smem + vmem(3),
+        in_specs=[pl.BlockSpec(memory_space=pltpu.HBM)] * 5,
         out_specs=vmem(4),
-        scratch_shapes=[pltpu.VMEM((tokens, width), jnp.bfloat16)],
-        compiler_params=params(),
+        scratch_shapes=[
+            pltpu.SMEM(page_table.shape, jnp.int32),
+            pltpu.SMEM(prompt_lengths.shape, jnp.int32),
+            pltpu.VMEM((tokens, width), jnp.bfloat16),
+            pltpu.VMEM(key_pool.shape, jnp.bfloat16),
+            pltpu.VMEM(value_pool.shape, jnp.bfloat16),
+            pltpu.VMEM((tokens, width), jnp.bfloat16),
+            pltpu.SemaphoreType.DMA((5,)),
+        ],
+        compiler_params=params(VMEM_MOST),
         name="attention",
     )(page_table, prompt_lengths, queries, key_pool, value_pool)
 
@@ -213,45 +237,90 @@
         in_specs=vmem(8),
         out_specs=vmem(2),
         compiler_params=params(),
+        cost_estimate=SMALL,
         name="norm",
     )(hidden_in, *attn, norm_gain[None, :], expert_ids, gate_weights)
+
+
+def cast_kernel(up_source, down_source, up_out, down_out, up_ref, down_ref, arrived):
+    def copies(step):
+        for i, (source, target) in enumerate(((up_source, up_ref), (down_source, down_ref))):
+            rows = target.shape[0] // CAST_STEPS
+            here = pl.ds(step * rows, rows)
+            yield pltpu.make_async_copy(source.at[0, here], target.at[here], arrived.at[step, i])
+
+    for step in range(CAST_STEPS):
+        for copy in copies(step):
+            copy.start()
+    for step in range(CAST_STEPS):
+        for copy in copies(step):
+            copy.wait()
+        for source, target in ((up_ref, up_out), (down_ref, down_out)):
+            rows = target.shape[0] // CAST_STEPS
+            here = slice(step * rows, (step + 1) * rows)
+            target[here] = source[here].astype(jnp.bfloat16)
+
+
+def cast_weights(gate_up, down):
+    shapes = gate_up.shape[1:], down.shape[1:]
+    return pl.pallas_call(
+        cast_kernel,
+        out_shape=[jax.ShapeDtypeStruct(shape, jnp.bfloat16) for shape in shapes],
+        in_specs=[pl.BlockSpec(memory_space=pltpu.HBM)] * 2,
+        out_specs=vmem(2),
+        scratch_shapes=[pltpu.VMEM(shape, jnp.float32) for shape in shapes]
+        + [pltpu.SemaphoreType.DMA((CAST_STEPS, 2))],
+        compiler_params=params(VMEM_MOST),
+        name="cast_weights",
+    )(gate_up, down)
+
+
+def load_tiles(pieces, weights, arrived, tiles, block):
+    def copies(tile):
+        first = 0
+        for index, piece in enumerate(pieces):
+            depth = piece.shape[0]
+            for part in range(2):
+                columns = pl.ds((part * tiles + tile) * block, block)
+                yield pltpu.make_async_copy(
+                    piece.at[:, columns],
+                    weights.at[pl.ds(first, depth), columns],
+                    arrived.at[tile, index, part],
+                )
+            first += depth
+
+    for tile in range(tiles):
+        for copy in copies(tile):
+            copy.start()
+
+    def wait(tile):
+        for copy in copies(tile):
+            copy.wait()
+
+    return wait
 
 
 def up_kernel(sources, pieces, *refs):
     row_refs = refs[:sources]
     weight_refs = refs[sources : sources + pieces]
     hidden_ref, own_gate_ref, rows, weights, units, arrived = refs[sources + pieces :]
-    tokens, width = rows.shape
+    width = rows.shape[1]
     tiles, _, block = units.shape
-    depth = width // pieces
-
-    def copy(tile, piece, part):
-        columns = pl.ds((part * tiles + tile) * block, block)
-        return pltpu.make_async_copy(
-            weight_refs[piece].at[:, columns],
-            weights.at[pl.ds(piece * depth, depth), columns],
-            arrived.at[tile, piece, part],
-        )
-
-    for tile in range(tiles):
-        for piece in range(pieces):
-            for part in range(2):
-                copy(tile, piece, part).start()
+    wait = load_tiles(weight_refs, weights, arrived, tiles, block)
     expert = lax.axis_index("expert")
     first = 0
     for ref in row_refs:
         count = ref.shape[0]
-        rows[first : first + count, :] = ref[:, :width]
+        here = slice(first, first + count)
+        rows[here, :] = ref[:, :width]
         terms = ref[:, width:].astype(jnp.float32)
         lane = lax.broadcasted_iota(jnp.int32, terms.shape, 1)
-        own_gate_ref[first : first + count, :] = jnp.sum(
+        own_gate_ref[here, :] = jnp.sum(
             jnp.where(lane % TOPK == expert, terms, 0.0), axis=-1, keepdims=True
         )
         first += count
     for tile in range(tiles):
-        for piece in range(pieces):
-            for part in range(2):
-                copy(tile, piece, part).wait()
+        wait(tile)
         gate, up = (
             jnp.dot(
                 rows[...],
@@ -266,10 +335,11 @@
         hidden_ref[:, d * block : (d + 1) * block] = units[own ^ d]
 
 
-def expert_up(rows, weights, hidden_size):
+def expert_up(rows, weights):
     tokens = sum(piece.shape[0] for piece in rows)
-    depth, width = weights[0].shape
-    features = depth * len(weights)
+    features = sum(piece.shape[0] for piece in weights)
+    width = weights[0].shape[1]
+    hidden_size = width // 2
     return pl.pallas_call(
         lambda *refs: up_kernel(len(rows), len(weights), *refs),
         out_shape=[
@@ -285,52 +355,51 @@
             pltpu.SemaphoreType.DMA((4, len(weights), 2)),
         ],
         compiler_params=params(),
-        cost_estimate=pl.CostEstimate(
-            flops=2 * tokens * features * width,
-            bytes_accessed=2 * features * width,
-            transcendentals=0,
-        ),
+        cost_estimate=SMALL,
         name="expert_up",
     )(*rows, *weights)
 
 
-def down_kernel(hidden_ref, gate_ref, w0, w1, w2, w3, out_ref, left_ref, right_ref):
-    block = w0.shape[0]
-    total = None
-    for d, ref in enumerate((w0, w1, w2, w3)):
-        term = jnp.dot(
-            hidden_ref[:, d * block : (d + 1) * block],
-            ref[...],
-            preferred_element_type=jnp.float32,
+def down_kernel(firsts, hidden_ref, gate_ref, w0, w1, w2, w3, *refs):
+    out_ref, left_ref, right_ref, weights, arrived = refs
+    depth, width = w0.shape[0], weights.shape[1]
+    copies = [
+        pltpu.make_async_copy(
+            ref.at[:, pl.ds(first, width)], weights.at[pl.ds(d * depth, depth)], arrived.at[d]
         )
-        total = term if total is None else total + term
+        for d, (ref, first) in enumerate(zip((w0, w1, w2, w3), firsts))
+    ]
+    for copy in copies:
+        copy.start()
+    for copy in copies:
+        copy.wait()
+    total = jnp.dot(hidden_ref[...], weights[...], preferred_element_type=jnp.float32)
     weighted = (total * gate_ref[...]).astype(jnp.bfloat16)
-    sources, rows, width = out_ref.shape
+    sources, rows, _ = out_ref.shape
     out_ref[...] = weighted.reshape(sources, rows, width)
     middle, half = sources // 2 * rows, rows // 2
     left_ref[...] = weighted[middle : middle + half]
     right_ref[...] = weighted[middle + half : middle + rows]
 
 
-def expert_down(hidden_units, gates, weights, sources):
+def expert_down(hidden_units, gates, weights, firsts, width, sources):
     tokens, hidden_size = hidden_units.shape
-    width = weights[0].shape[1]
     rows = tokens // sources
     return pl.pallas_call(
-        down_kernel,
+        lambda *refs: down_kernel(firsts, *refs),
         out_shape=[
             jax.ShapeDtypeStruct((sources, rows, width), jnp.bfloat16),
             jax.ShapeDtypeStruct((rows // 2, width), jnp.bfloat16),
             jax.ShapeDtypeStruct((rows // 2, width), jnp.bfloat16),
         ],
-        in_specs=vmem(6),
+        in_specs=vmem(2) + [pl.BlockSpec(memory_space=pl.ANY)] * 4,
         out_specs=vmem(3),
+        scratch_shapes=[
+            pltpu.VMEM((hidden_size, width), jnp.bfloat16),
+            pltpu.SemaphoreType.DMA((4,)),
+        ],
         compiler_params=params(),
-        cost_estimate=pl.CostEstimate(
-            flops=2 * tokens * hidden_size * width,
-            bytes_accessed=2 * (hidden_size * width + tokens * hidden_size + tokens * width),
-            transcendentals=0,
-        ),
+        cost_estimate=SMALL,
         name="expert_down",
     )(hidden_units, gates, *weights)
 
@@ -397,52 +466,33 @@
     trainer_gate_up,
     trainer_down,
 ):
-    attn = attention(queries[0], key_pool, value_pool, page_table, prompt_lengths)
-    depth = trainer_gate_up.shape[1] // ROW_PIECES
+    expert_count = lax.axis_size("expert")
     width = trainer_down.shape[2]
-    first = width * 5 // 8
-    bounds = [(0, first), (first, width)]
-    gate_up = after(trainer_gate_up[0], attn[0]).astype(jnp.bfloat16)
-    up_own = [gate_up[i * depth : (i + 1) * depth] for i in range(ROW_PIECES)]
-    down = trainer_down[0].astype(jnp.bfloat16)
-    down_own = [down[:, low:high] for low, high in bounds]
+    attn = attention(queries, key_pool, value_pool, page_table, prompt_lengths)
+    up_own, down_own = cast_weights(after(trainer_gate_up, attn[0]), trainer_down)
     attn = [attn[0]] + [partner(attn[d], d) for d in (1, 2, 3)]
-    up_across = [partner(after(piece, *attn), 2) for piece in up_own]
+    up_across = partner(after(up_own, *attn), 2)
     resid, rows = norm(
-        after(hidden_in[0], *up_own), attn, norm_gain, expert_ids[0], gate_weights[0]
+        after(hidden_in[0], up_own), attn, norm_gain, expert_ids[0], gate_weights[0]
     )
     gathered, arrived = gather_rows(rows)
-    up_beside = [partner(after(piece, *arrived[0]), 1) for piece in up_own]
-    down_beside = [partner(after(piece, *arrived[1]), 1) for piece in down_own]
-    down_across = [
-        partner(after(down_own[0], *arrived[2]), 2),
-        partner(after(down_own[1], up_across[0], *arrived[3]), 2),
+    up_beside = partner(after(up_own, *arrived[0]), 1)
+    down_beside = partner(after(down_own, *arrived[1]), 1)
+    down_across = partner(after(down_own, *arrived[2]), 2)
+    up_opposite = partner(after(up_across, *arrived[3]), 1)
+    hidden_units, gates = expert_up(gathered, [up_own, up_beside, up_across, up_opposite])
+    down_opposite = partner(after(down_across, hidden_units), 1)
+    weights = (down_own, down_beside, down_across, down_opposite)
+    slab = width // SLABS
+    starts = range(0, width, slab)
+    weighted = [
+        expert_down(hidden_units, gates, weights, (first,) * 4, slab, expert_count)
+        for first in starts
     ]
-    up_opposite = [
-        partner(after(up_across[0], *arrived[1]), 1),
-        partner(after(up_across[1], *arrived[3]), 1),
-    ]
-    hidden_units, gates = expert_up(
-        gathered, up_own + up_beside + up_across + up_opposite, trainer_gate_up.shape[2] // 2
-    )
-
-    def down_slab(i, *before):
-        opposite = partner(after(down_across[i], *before), 1)
-        weighted = expert_down(
-            hidden_units,
-            gates,
-            (down_own[i], down_beside[i], down_across[i], opposite),
-            lax.axis_size("expert"),
-        )
-        return weighted[0][0], scatter_sum(*weighted)
-
-    own0, sums0 = down_slab(0, hidden_units)
-    own1, sums1 = down_slab(1, *next(sums0))
-    ends = [(own, *list(sums)[-1]) for own, sums in ((own0, sums0), (own1, sums1))]
     mixed = []
-    for (low, high), terms in zip(bounds, ends):
-        total = resid[:, low:high].astype(jnp.float32)
-        for term in terms:
+    for first, partial in zip(starts, weighted):
+        total = resid[:, first : first + slab].astype(jnp.float32)
+        for term in (partial[0][0], *list(scatter_sum(*partial))[-1]):
             total = total + term.astype(jnp.float32)
         mixed.append(total.astype(jnp.bfloat16))
     return jnp.concatenate(mixed, axis=1)[None]

time: 125 us -> 123 us (0.984)
  Pallas kernels: 11.9 us -> 18.3 us
  other arithmetic: 5.45 us -> 1.27 us
  starting transfers between devices: 34.4 us -> 31.3 us
  local copies, waits for them, and re-layouts: 4.72 us -> 1.82 us
  waiting for transfers between devices: 68.5 us -> 70.4 us
    ppermute x15 -> x9, waiting for transfers between devices: 25.5 us -> 33.2 us  [partner(): return lax.ppermute(x, 'dp', [(i, i ^ distance) for i in range(4)])]
    ppermute x24, waiting for transfers between devices: 43 us -> 37.1 us  [around(): lax.ppermute(x, 'expert', [(ring[i], ring[(i + step) % count]) for i in r...]
    pallas_call x2 -> x3, Pallas kernels: 2.52 us -> 7.53 us  [the longest x1 4.56 us: cast_weights(): pl.pallas_call(cast_kernel, out_shape=[jax.ShapeDtypeStruct(shape, jnp.bf...]
    convert_element_type x2 -> x0, other arithmetic: 4.23 us -> none  [the longest x1 2.5 us: every_expert(): gate_up = after(trainer_gate_up[0], attn[0]).astype(jnp.bfloat16)]
    unnamed x20 -> x16, local copies, waits for them, and re-layouts: 4.35 us -> 1.78 us
    ppermute x15 -> x9, starting transfers between devices: 8.97 us -> 6.92 us  [partner(): return lax.ppermute(x, 'dp', [(i, i ^ distance) for i in range(4)])]
    pallas_call x1, Pallas kernels: 1.7 us -> 2.98 us  [attention(): pl.pallas_call(attention_kernel, out_shape=[jax.ShapeDtypeStruct((tokens...]
  transfers between devices with their start and end apart: 39 -> 33, of which waited for: 19 -> 19; matrix products, arithmetic and copies ran while one was open for 4% -> 0% of each run, Pallas kernels for 8% -> 11%
where the time goes in v5:
time: 123 us
  waiting for transfers between devices  70.4 us (57%)
  starting transfers between devices  31.3 us (25%)
  Pallas kernels  18.3 us (15%)
  local copies, waits for them, and re-layouts  1.82 us (1%)
  other arithmetic  1.27 us (1%)
    ppermute x24, waiting for transfers between devices, around(): lax.ppermute(x, 'expert', [(ring[i], ring[(i + step) % count]) for i in r...  37.1 us
    ppermute x9, waiting for transfers between devices, partner(): return lax.ppermute(x, 'dp', [(i, i ^ distance) for i in range(4)])  33.2 us
    ppermute x24, starting transfers between devices, around(): lax.ppermute(x, 'expert', [(ring[i], ring[(i + step) % count]) for i in r...  24.3 us
    pallas_call x1, Pallas kernels, expert_up(): pl.pallas_call(lambda *refs: up_kernel(len(rows), len(weights), *refs), o...  7.38 us
    ppermute x9, starting transfers between devices, partner(): return lax.ppermute(x, 'dp', [(i, i ^ distance) for i in range(4)])  6.92 us
    pallas_call x1, Pallas kernels, cast_weights(): pl.pallas_call(cast_kernel, out_shape=[jax.ShapeDtypeStruct(shape, jnp.bf...  4.56 us
    pallas_call x1, Pallas kernels, attention(): pl.pallas_call(attention_kernel, out_shape=[jax.ShapeDtypeStruct((tokens...  2.98 us
    pallas_call x2, Pallas kernels, expert_down(): pl.pallas_call(lambda *refs: down_kernel(firsts, *refs), out_shape=[jax.S...  2.97 us
  transfers between devices with their start and end apart: 33, of which 19 were waited for; matrix products, arithmetic and copies ran while one was open for 0% of the time, Pallas kernels for 11%

profile of v5, /device:TPU:0, one launch (start us, length us, event | category | flops | bytes accessed | tf_op | source)
XLA Modules:
  0.0 123.2 jit_solution(5776286458315486063)
XLA Ops:
  0.0 3.0 %attention.1 = (bf16[64,512]{1,0:T(8,128)(2,1)}, bf16[64,512]{1,0:T(8,128)(2,1)}, bf16[64,512]{1,0:T(8,128)(2,1)}, bf16[64,512]{1,0:T(8,128)(2,1)}) custom-call(s32[1,2]{1,0:T(1,128)} %refs_0_.1, s32[1,4]{1,0:T(1,128)} %refs_1_.1, bf16[1,256,512]{2,1,0:T(8,128)(2,1)} %refs_2_.1, bf16[2,128,512]{2,1,0:T(8,128)(2,1)} %refs_3_.1, bf16[2,128,512]{2,1,0:T(8,128)(2,1)} %refs_4_.1), custom_call_target="tpu_custom_call" | custom-call | tf_op jit(solution)/shard_map/attention/pallas_call | solution.py:179
  3.5 2.6 %collective-permute-start.1 = (bf16[64,512]{1,0:T(8,128)(2,1)}, bf16[64,512]{1,0:T(8,128)(2,1)S(1)}, u32[]{:S(2)}, u32[]{:S(2)}) collective-permute-start(bf16[64,512]{1,0:T(8,128)(2,1)} %get-tuple-element.34), channel_id=1, source_target_pairs={{0,16},{8,24},{16,0},{24,8},{1,17},{9,25},{17,1},{25,9},{2,18},{10... | collective-permute-start | bytes 196616 | tf_op jit(solution)/shard_map/ppermute | solution.py:408
  6.2 4.6 %cast_weights.1 = (bf16[512,2048]{1,0:T(8,128)(2,1)}, bf16[256,2048]{1,0:T(8,128)(2,1)}) custom-call(f32[1,512,2048]{2,1,0:T(8,128)} %up_source, f32[1,256,2048]{2,1,0:T(8,128)} %down_source.1), custom_call_target="tpu_custom_call" | custom-call | tf_op jit(solution)/shard_map/cast_weights/pallas_call | solution.py:266
  10.8 1.8 %collective-permute-start.12 = (bf16[512,2048]{1,0:T(8,128)(2,1)}, bf16[512,2048]{1,0:T(8,128)(2,1)S(1)}, u32[]{:S(2)}, u32[]{:S(2)}) collective-permute-start(bf16[512,2048]{1,0:T(8,128)(2,1)} %get-tuple-element.39.refs_9_), channel_id=1, source_target_pairs={{0,16},{8,24},{16,0},{24,8},{1,17},{9,25},{17,1},{25,9},{2,18},{10... | collective-permute-start | bytes 6291464 | tf_op jit(solution)/shard_map/ppermute | solution.py:408
  13.1 1.6 %collective-permute-start.7 = (bf16[64,2176]{1,0:T(8,128)(2,1)S(1)}, bf16[64,2176]{1,0:T(8,128)(2,1)S(1)}, u32[]{:S(2)}, u32[]{:S(2)}) collective-permute-start(bf16[64,2176]{1,0:T(8,128)(2,1)S(1)} %get-tuple-element.37.refs_0_), channel_id=1, source_target_pairs={{0,2},{2,4},{4,6},{6,7},{7,5},{5,3},{3,1},{1,0},{8,10},{10,12},{12... | collective-permute-start | bytes 835592 | tf_op jit(solution)/shard_map/ppermute | solution.py:418
  15.2 6.6 %collective-permute-done.7.refs_8_ = bf16[64,2176]{1,0:T(8,128)(2,1)S(1)} collective-permute-done((bf16[64,2176]{1,0:T(8,128)(2,1)S(1)}, bf16[64,2176]{1,0:T(8,128)(2,1)S(1)}, u32[]{:S(2)}, u32[]{:S(2)}) %collective-permute-start.7) | collective-permute-done | bytes 278560 | tf_op jit(solution)/shard_map/ppermute | solution.py:418
  21.8 1.6 %collective-permute-start.8 = (bf16[64,2176]{1,0:T(8,128)(2,1)S(1)}, bf16[64,2176]{1,0:T(8,128)(2,1)S(1)}, u32[]{:S(2)}, u32[]{:S(2)}) collective-permute-start(bf16[64,2176]{1,0:T(8,128)(2,1)S(1)} %collective-permute-done.7.refs_8_), channel_id=1, source_target_pairs={{0,2},{2,4},{4,6},{6,7},{7,5},{5,3},{3,1},{1,0},{8,10},{10,12},{12... | collective-permute-start | bytes 835592 | tf_op jit(solution)/shard_map/ppermute | solution.py:418
  23.9 5.8 %collective-permute-done.8.refs_7_ = bf16[64,2176]{1,0:T(8,128)(2,1)S(1)} collective-permute-done((bf16[64,2176]{1,0:T(8,128)(2,1)S(1)}, bf16[64,2176]{1,0:T(8,128)(2,1)S(1)}, u32[]{:S(2)}, u32[]{:S(2)}) %collective-permute-start.8) | collective-permute-done | bytes 278560 | tf_op jit(solution)/shard_map/ppermute | solution.py:418
  29.6 1.6 %collective-permute-start.9 = (bf16[64,2176]{1,0:T(8,128)(2,1)S(1)}, bf16[64,2176]{1,0:T(8,128)(2,1)S(1)}, u32[]{:S(2)}, u32[]{:S(2)}) collective-permute-start(bf16[64,2176]{1,0:T(8,128)(2,1)S(1)} %collective-permute-done.8.refs_7_), channel_id=1, source_target_pairs={{0,2},{2,4},{4,6},{6,7},{7,5},{5,3},{3,1},{1,0},{8,10},{10,12},{12... | collective-permute-start | bytes 835592 | tf_op jit(solution)/shard_map/ppermute | solution.py:418
  31.6 4.8 %collective-permute-done.9.refs_6_ = bf16[64,2176]{1,0:T(8,128)(2,1)S(1)} collective-permute-done((bf16[64,2176]{1,0:T(8,128)(2,1)S(1)}, bf16[64,2176]{1,0:T(8,128)(2,1)S(1)}, u32[]{:S(2)}, u32[]{:S(2)}) %collective-permute-start.9) | collective-permute-done | bytes 278560 | tf_op jit(solution)/shard_map/ppermute | solution.py:418
  36.5 1.6 %collective-permute-start.10 = (bf16[32,2176]{1,0:T(8,128)(2,1)S(1)}, bf16[32,2176]{1,0:T(8,128)(2,1)S(1)}, u32[]{:S(2)}, u32[]{:S(2)}) collective-permute-start(bf16[32,2176]{1,0:T(8,128)(2,1)S(1)} %slice.89), channel_id=1, source_target_pairs={{0,2},{2,4},{4,6},{6,7},{7,5},{5,3},{3,1},{1,0},{8,10},{10,12},{12... | collective-permute-start | bytes 417800 | tf_op jit(solution)/shard_map/ppermute | solution.py:418
  38.6 3.0 %collective-permute-done.10.refs_5_ = bf16[32,2176]{1,0:T(8,128)(2,1)S(1)} collective-permute-done((bf16[32,2176]{1,0:T(8,128)(2,1)S(1)}, bf16[32,2176]{1,0:T(8,128)(2,1)S(1)}, u32[]{:S(2)}, u32[]{:S(2)}) %collective-permute-start.10) | collective-permute-done | bytes 139296 | tf_op jit(solution)/shard_map/ppermute | solution.py:418
  41.6 1.6 %collective-permute-done.6.refs_4_ = bf16[32,2176]{1,0:T(8,128)(2,1)S(1)} collective-permute-done((bf16[32,2176]{1,0:T(8,128)(2,1)S(1)}, bf16[32,2176]{1,0:T(8,128)(2,1)S(1)}, u32[]{:S(2)}, u32[]{:S(2)}) %collective-permute-start.6) | collective-permute-done | bytes 139296 | tf_op jit(solution)/shard_map/ppermute | solution.py:418
  43.2 15.7 %collective-permute-done.12.refs_11_ = bf16[512,2048]{1,0:T(8,128)(2,1)S(1)} collective-permute-done((bf16[512,2048]{1,0:T(8,128)(2,1)}, bf16[512,2048]{1,0:T(8,128)(2,1)S(1)}, u32[]{:S(2)}, u32[]{:S(2)}) %collective-permute-start.12) | collective-permute-done | bytes 2097184 | tf_op jit(solution)/shard_map/ppermute | solution.py:408
  58.9 1.7 %collective-permute-start.15 = (bf16[256,2048]{1,0:T(8,128)(2,1)}, bf16[256,2048]{1,0:T(8,128)(2,1)S(1)}, u32[]{:S(2)}, u32[]{:S(2)}) collective-permute-start(bf16[256,2048]{1,0:T(8,128)(2,1)} %get-tuple-element.45.refs_2_), channel_id=1, source_target_pairs={{0,16},{8,24},{16,0},{24,8},{1,17},{9,25},{17,1},{25,9},{2,18},{10... | collective-permute-start | bytes 3145736 | tf_op jit(solution)/shard_map/ppermute | solution.py:408
  60.9 2.2 %collective-permute-done.13.refs_12_ = bf16[512,2048]{1,0:T(8,128)(2,1)S(1)} collective-permute-done((bf16[512,2048]{1,0:T(8,128)(2,1)S(1)}, bf16[512,2048]{1,0:T(8,128)(2,1)S(1)}, u32[]{:S(2)}, u32[]{:S(2)}) %collective-permute-start.13) | collective-permute-done | bytes 2097184 | tf_op jit(solution)/shard_map/ppermute | solution.py:408
  63.1 1.6 %copy-done.1 = bf16[512,2048]{1,0:T(8,128)(2,1)S(1)} copy-done((bf16[512,2048]{1,0:T(8,128)(2,1)S(1)}, bf16[512,2048]{1,0:T(8,128)(2,1)}, u32[]{:S(2)}) %copy-start.1) | copy-done | bytes 2097176
  64.7 7.4 %expert_up.1 = (bf16[512,1024]{1,0:T(8,128)(2,1)S(1)}, f32[512,1]{1,0:T(8,128)S(1)}) custom-call(bf16[64,2176]{1,0:T(8,128)(2,1)S(1)} %get-tuple-element.37.refs_0_, bf16[64,2176]{1,0:T(8,128)(2,1)S(1)} %collective-permute-done.3.refs_1_, bf16[64,2176]{1,0:T(8,128)(2,1)S(1)} %collective-permute-done.4.refs_2_, ...), custom_call_target="tpu_custom_call" | custom-call | flops 1 | bytes 1 | tf_op jit(solution)/shard_map/expert_up/pallas_call | solution.py:343
  72.0 12.7 %collective-permute-done.15.refs_4_ = bf16[256,2048]{1,0:T(8,128)(2,1)S(1)} collective-permute-done((bf16[256,2048]{1,0:T(8,128)(2,1)}, bf16[256,2048]{1,0:T(8,128)(2,1)S(1)}, u32[]{:S(2)}, u32[]{:S(2)}) %collective-permute-start.15) | collective-permute-done | bytes 1048608 | tf_op jit(solution)/shard_map/ppermute | solution.py:408
  84.8 2.7 %collective-permute-done.16.refs_5_ = bf16[256,2048]{1,0:T(8,128)(2,1)S(1)} collective-permute-done((bf16[256,2048]{1,0:T(8,128)(2,1)S(1)}, bf16[256,2048]{1,0:T(8,128)(2,1)S(1)}, u32[]{:S(2)}, u32[]{:S(2)}) %collective-permute-start.16) | collective-permute-done | bytes 1048608 | tf_op jit(solution)/shard_map/ppermute | solution.py:408
  87.4 1.5 %expert_down.3 = (bf16[8,64,1024]{2,1,0:T(8,128)(2,1)S(1)}, bf16[32,1024]{1,0:T(8,128)(2,1)S(1)}, bf16[32,1024]{1,0:T(8,128)(2,1)S(1)}) custom-call(bf16[512,1024]{1,0:T(8,128)(2,1)S(1)} %get-tuple-element.41.refs_0_, f32[512,1]{1,0:T(8,128)S(1)} %get-tuple-element.42.refs_1_, bf16[256,2048]{1,0:T(8,128)(2,1)S(1)} %copy-done, ...), custom_call_target="tpu_custom_call" | custom-call | flops 1 | bytes 1 | tf_op jit(solution)/shard_map/expert_down/pallas_call | solution.py:388
  88.9 1.8 %collective-permute-start.25 = (bf16[32,1024]{1,0:T(8,128)(2,1)S(1)}, bf16[32,1024]{1,0:T(8,128)(2,1)S(1)}, u32[]{:S(2)}, u32[]{:S(2)}) collective-permute-start(bf16[32,1024]{1,0:T(8,128)(2,1)S(1)} %get-tuple-element.51), channel_id=1, source_target_pairs={{0,2},{2,4},{4,6},{6,7},{7,5},{5,3},{3,1},{1,0},{8,10},{10,12},{12... | collective-permute-start | bytes 196616 | tf_op jit(solution)/shard_map/ppermute | solution.py:418
  91.0 1.5 %expert_down.2 = (bf16[8,64,1024]{2,1,0:T(8,128)(2,1)S(1)}, bf16[32,1024]{1,0:T(8,128)(2,1)S(1)}, bf16[32,1024]{1,0:T(8,128)(2,1)S(1)}) custom-call(bf16[512,1024]{1,0:T(8,128)(2,1)S(1)} %get-tuple-element.41.refs_0_, f32[512,1]{1,0:T(8,128)S(1)} %get-tuple-element.42.refs_1_, bf16[256,2048]{1,0:T(8,128)(2,1)S(1)} %copy-done, ...), custom_call_target="tpu_custom_call" | custom-call | flops 1 | bytes 1 | tf_op jit(solution)/shard_map/expert_down/pallas_call | solution.py:388
  92.5 1.8 %collective-permute-start.17 = (bf16[32,1024]{1,0:T(8,128)(2,1)S(1)}, bf16[32,1024]{1,0:T(8,128)(2,1)S(1)}, u32[]{:S(2)}, u32[]{:S(2)}) collective-permute-start(bf16[32,1024]{1,0:T(8,128)(2,1)S(1)} %get-tuple-element.48), channel_id=1, source_target_pairs={{0,2},{2,4},{4,6},{6,7},{7,5},{5,3},{3,1},{1,0},{8,10},{10,12},{12... | collective-permute-start | bytes 196616 | tf_op jit(solution)/shard_map/ppermute | solution.py:418
  97.2 1.8 %collective-permute-done.21 = bf16[32,1024]{1,0:T(8,128)(2,1)S(1)} collective-permute-done((bf16[32,1024]{1,0:T(8,128)(2,1)S(1)}, bf16[32,1024]{1,0:T(8,128)(2,1)S(1)}, u32[]{:S(2)}, u32[]{:S(2)}) %collective-permute-start.21) | collective-permute-done | bytes 65568 | tf_op jit(solution)/shard_map/ppermute | solution.py:418
  99.7 1.5 %collective-permute-start.18 = (bf16[64,1024]{1,0:T(8,128)(2,1)S(1)}, bf16[64,1024]{1,0:T(8,128)(2,1)S(1)}, u32[]{:S(2)}, u32[]{:S(2)}) collective-permute-start(bf16[64,1024]{1,0:T(8,128)(2,1)S(1)} %pad_maximum_fusion), channel_id=1, source_target_pairs={{0,2},{2,4},{4,6},{6,7},{7,5},{5,3},{3,1},{1,0},{8,10},{10,12},{12... | collective-permute-start | bytes 393224 | tf_op jit(solution)/shard_map/ppermute | solution.py:418
  101.2 1.7 %collective-permute-done.26 = bf16[64,1024]{1,0:T(8,128)(2,1)S(1)} collective-permute-done((bf16[64,1024]{1,0:T(8,128)(2,1)S(1)}, bf16[64,1024]{1,0:T(8,128)(2,1)S(1)}, u32[]{:S(2)}, u32[]{:S(2)}) %collective-permute-start.26) | collective-permute-done | bytes 131104 | tf_op jit(solution)/shard_map/ppermute | solution.py:418
  103.0 2.6 %collective-permute-done.18 = bf16[64,1024]{1,0:T(8,128)(2,1)S(1)} collective-permute-done((bf16[64,1024]{1,0:T(8,128)(2,1)S(1)}, bf16[64,1024]{1,0:T(8,128)(2,1)S(1)}, u32[]{:S(2)}, u32[]{:S(2)}) %collective-permute-start.18) | collective-permute-done | bytes 131104 | tf_op jit(solution)/shard_map/ppermute | solution.py:418
  108.2 1.5 %collective-permute-start.31 = (bf16[64,1024]{1,0:T(8,128)(2,1)S(1)}, bf16[64,1024]{1,0:T(8,128)(2,1)S(1)}, u32[]{:S(2)}, u32[]{:S(2)}) collective-permute-start(bf16[64,1024]{1,0:T(8,128)(2,1)S(1)} %get-tuple-element.60), channel_id=1, source_target_pairs={{0,1},{2,0},{4,2},{6,4},{7,6},{5,7},{3,5},{1,3},{8,9},{10,8},{12,1... | collective-permute-start | bytes 393224 | tf_op jit(solution)/shard_map/ppermute | solution.py:418
  111.3 1.8 %collective-permute-start.23 = (bf16[64,1024]{1,0:T(8,128)(2,1)S(1)}, bf16[64,1024]{1,0:T(8,128)(2,1)S(1)}, u32[]{:S(2)}, u32[]{:S(2)}) collective-permute-start(bf16[64,1024]{1,0:T(8,128)(2,1)S(1)} %get-tuple-element.54), channel_id=1, source_target_pairs={{0,1},{2,0},{4,2},{6,4},{7,6},{5,7},{3,5},{1,3},{8,9},{10,8},{12,1... | collective-permute-start | bytes 393224 | tf_op jit(solution)/shard_map/ppermute | solution.py:418
  115.7 1.6 %collective-permute-done.23 = bf16[64,1024]{1,0:T(8,128)(2,1)S(1)} collective-permute-done((bf16[64,1024]{1,0:T(8,128)(2,1)S(1)}, bf16[64,1024]{1,0:T(8,128)(2,1)S(1)}, u32[]{:S(2)}, u32[]{:S(2)}) %collective-permute-start.23) | collective-permute-done | bytes 131104 | tf_op jit(solution)/shard_map/ppermute | solution.py:418
  119.5 2.8 %collective-permute-done.24 = bf16[64,1024]{1,0:T(8,128)(2,1)S(1)} collective-permute-done((bf16[64,1024]{1,0:T(8,128)(2,1)S(1)}, bf16[64,1024]{1,0:T(8,128)(2,1)S(1)}, u32[]{:S(2)}, u32[]{:S(2)}) %collective-permute-start.24) | collective-permute-done | bytes 131104 | tf_op jit(solution)/shard_map/ppermute | solution.py:418
  (74 shorter events, 17.1 us)
Async XLA Ops:
  3.0 7.7 %collective-permute-start = (bf16[64,512]{1,0:T(8,128)(2,1)}, bf16[64,512]{1,0:T(8,128)(2,1)S(1)}, u32[]{:S(2)}, u32[]{:S(2)}) collective-permute-start(bf16[64,512]{1,0:T(8,128)(2,1)} %get-tuple-element.33), channel_id=1, source_target_pairs={{0,8},{8,0},{16,24},{24,16},{1,9},{9,1},{17,25},{25,17},{2,10},{10... | collective-permute-start | bytes 196616 | tf_op jit(solution)/shard_map/ppermute | solution.py:408
  3.5 7.2 %collective-permute-start.1 = (bf16[64,512]{1,0:T(8,128)(2,1)}, bf16[64,512]{1,0:T(8,128)(2,1)S(1)}, u32[]{:S(2)}, u32[]{:S(2)}) collective-permute-start(bf16[64,512]{1,0:T(8,128)(2,1)} %get-tuple-element.34), channel_id=1, source_target_pairs={{0,16},{8,24},{16,0},{24,8},{1,17},{9,25},{17,1},{25,9},{2,18},{10... | collective-permute-start | bytes 196616 | tf_op jit(solution)/shard_map/ppermute | solution.py:408
  6.1 4.7 %collective-permute-start.2 = (bf16[64,512]{1,0:T(8,128)(2,1)}, bf16[64,512]{1,0:T(8,128)(2,1)S(1)}, u32[]{:S(2)}, u32[]{:S(2)}) collective-permute-start(bf16[64,512]{1,0:T(8,128)(2,1)} %get-tuple-element.35), channel_id=1, source_target_pairs={{0,24},{8,16},{16,8},{24,0},{1,25},{9,17},{17,9},{25,1},{2,26},{10... | collective-permute-start | bytes 196616 | tf_op jit(solution)/shard_map/ppermute | solution.py:408
  10.8 48.1 %collective-permute-start.12 = (bf16[512,2048]{1,0:T(8,128)(2,1)}, bf16[512,2048]{1,0:T(8,128)(2,1)S(1)}, u32[]{:S(2)}, u32[]{:S(2)}) collective-permute-start(bf16[512,2048]{1,0:T(8,128)(2,1)} %get-tuple-element.39.refs_9_), channel_id=1, source_target_pairs={{0,16},{8,24},{16,0},{24,8},{1,17},{9,25},{17,1},{25,9},{2,18},{10... | collective-permute-start | bytes 6291464 | tf_op jit(solution)/shard_map/ppermute | solution.py:408
  13.1 8.7 %collective-permute-start.7 = (bf16[64,2176]{1,0:T(8,128)(2,1)S(1)}, bf16[64,2176]{1,0:T(8,128)(2,1)S(1)}, u32[]{:S(2)}, u32[]{:S(2)}) collective-permute-start(bf16[64,2176]{1,0:T(8,128)(2,1)S(1)} %get-tuple-element.37.refs_0_), channel_id=1, source_target_pairs={{0,2},{2,4},{4,6},{6,7},{7,5},{5,3},{3,1},{1,0},{8,10},{10,12},{12... | collective-permute-start | bytes 835592 | tf_op jit(solution)/shard_map/ppermute | solution.py:418
  14.8 8.6 %collective-permute-start.3 = (bf16[64,2176]{1,0:T(8,128)(2,1)S(1)}, bf16[64,2176]{1,0:T(8,128)(2,1)S(1)}, u32[]{:S(2)}, u32[]{:S(2)}) collective-permute-start(bf16[64,2176]{1,0:T(8,128)(2,1)S(1)} %get-tuple-element.37.refs_0_), channel_id=1, source_target_pairs={{0,1},{2,0},{4,2},{6,4},{7,6},{5,7},{3,5},{1,3},{8,9},{10,8},{12,1... | collective-permute-start | bytes 835592 | tf_op jit(solution)/shard_map/ppermute | solution.py:418
  21.8 7.8 %collective-permute-start.8 = (bf16[64,2176]{1,0:T(8,128)(2,1)S(1)}, bf16[64,2176]{1,0:T(8,128)(2,1)S(1)}, u32[]{:S(2)}, u32[]{:S(2)}) collective-permute-start(bf16[64,2176]{1,0:T(8,128)(2,1)S(1)} %collective-permute-done.7.refs_8_), channel_id=1, source_target_pairs={{0,2},{2,4},{4,6},{6,7},{7,5},{5,3},{3,1},{1,0},{8,10},{10,12},{12... | collective-permute-start | bytes 835592 | tf_op jit(solution)/shard_map/ppermute | solution.py:418
  23.4 7.8 %collective-permute-start.4 = (bf16[64,2176]{1,0:T(8,128)(2,1)S(1)}, bf16[64,2176]{1,0:T(8,128)(2,1)S(1)}, u32[]{:S(2)}, u32[]{:S(2)}) collective-permute-start(bf16[64,2176]{1,0:T(8,128)(2,1)S(1)} %collective-permute-done.3.refs_1_), channel_id=1, source_target_pairs={{0,1},{2,0},{4,2},{6,4},{7,6},{5,7},{3,5},{1,3},{8,9},{10,8},{12,1... | collective-permute-start | bytes 835592 | tf_op jit(solution)/shard_map/ppermute | solution.py:418
  29.6 6.9 %collective-permute-start.9 = (bf16[64,2176]{1,0:T(8,128)(2,1)S(1)}, bf16[64,2176]{1,0:T(8,128)(2,1)S(1)}, u32[]{:S(2)}, u32[]{:S(2)}) collective-permute-start(bf16[64,2176]{1,0:T(8,128)(2,1)S(1)} %collective-permute-done.8.refs_7_), channel_id=1, source_target_pairs={{0,2},{2,4},{4,6},{6,7},{7,5},{5,3},{3,1},{1,0},{8,10},{10,12},{12... | collective-permute-start | bytes 835592 | tf_op jit(solution)/shard_map/ppermute | solution.py:418
  31.2 6.9 %collective-permute-start.5 = (bf16[64,2176]{1,0:T(8,128)(2,1)S(1)}, bf16[64,2176]{1,0:T(8,128)(2,1)S(1)}, u32[]{:S(2)}, u32[]{:S(2)}) collective-permute-start(bf16[64,2176]{1,0:T(8,128)(2,1)S(1)} %collective-permute-done.4.refs_2_), channel_id=1, source_target_pairs={{0,1},{2,0},{4,2},{6,4},{7,6},{5,7},{3,5},{1,3},{8,9},{10,8},{12,1... | collective-permute-start | bytes 835592 | tf_op jit(solution)/shard_map/ppermute | solution.py:418
  36.5 5.1 %collective-permute-start.10 = (bf16[32,2176]{1,0:T(8,128)(2,1)S(1)}, bf16[32,2176]{1,0:T(8,128)(2,1)S(1)}, u32[]{:S(2)}, u32[]{:S(2)}) collective-permute-start(bf16[32,2176]{1,0:T(8,128)(2,1)S(1)} %slice.89), channel_id=1, source_target_pairs={{0,2},{2,4},{4,6},{6,7},{7,5},{5,3},{3,1},{1,0},{8,10},{10,12},{12... | collective-permute-start | bytes 417800 | tf_op jit(solution)/shard_map/ppermute | solution.py:418
  38.1 5.1 %collective-permute-start.6 = (bf16[32,2176]{1,0:T(8,128)(2,1)S(1)}, bf16[32,2176]{1,0:T(8,128)(2,1)S(1)}, u32[]{:S(2)}, u32[]{:S(2)}) collective-permute-start(bf16[32,2176]{1,0:T(8,128)(2,1)S(1)} %slice.88), channel_id=1, source_target_pairs={{0,1},{2,0},{4,2},{6,4},{7,6},{5,7},{3,5},{1,3},{8,9},{10,8},{12,1... | collective-permute-start | bytes 417800 | tf_op jit(solution)/shard_map/ppermute | solution.py:418
  38.6 22.2 %collective-permute-start.11 = (bf16[512,2048]{1,0:T(8,128)(2,1)}, bf16[512,2048]{1,0:T(8,128)(2,1)S(1)}, u32[]{:S(2)}, u32[]{:S(2)}) collective-permute-start(bf16[512,2048]{1,0:T(8,128)(2,1)} %get-tuple-element.39.refs_9_), channel_id=1, source_target_pairs={{0,8},{8,0},{16,24},{24,16},{1,9},{9,1},{17,25},{25,17},{2,10},{10... | collective-permute-start | bytes 6291464 | tf_op jit(solution)/shard_map/ppermute | solution.py:408
  58.9 4.2 %collective-permute-start.13 = (bf16[512,2048]{1,0:T(8,128)(2,1)S(1)}, bf16[512,2048]{1,0:T(8,128)(2,1)S(1)}, u32[]{:S(2)}, u32[]{:S(2)}) collective-permute-start(bf16[512,2048]{1,0:T(8,128)(2,1)S(1)} %collective-permute-done.12.refs_11_), channel_id=1, source_target_pairs={{0,8},{8,0},{16,24},{24,16},{1,9},{9,1},{17,25},{25,17},{2,10},{10... | collective-permute-start | bytes 6291464 | tf_op jit(solution)/shard_map/ppermute | solution.py:408
  58.9 25.9 %collective-permute-start.15 = (bf16[256,2048]{1,0:T(8,128)(2,1)}, bf16[256,2048]{1,0:T(8,128)(2,1)S(1)}, u32[]{:S(2)}, u32[]{:S(2)}) collective-permute-start(bf16[256,2048]{1,0:T(8,128)(2,1)} %get-tuple-element.45.refs_2_), channel_id=1, source_target_pairs={{0,16},{8,24},{16,0},{24,8},{1,17},{9,25},{17,1},{25,9},{2,18},{10... | collective-permute-start | bytes 3145736 | tf_op jit(solution)/shard_map/ppermute | solution.py:408
  60.7 24.1 %collective-permute-start.14 = (bf16[256,2048]{1,0:T(8,128)(2,1)}, bf16[256,2048]{1,0:T(8,128)(2,1)S(1)}, u32[]{:S(2)}, u32[]{:S(2)}) collective-permute-start(bf16[256,2048]{1,0:T(8,128)(2,1)} %get-tuple-element.45.refs_2_), channel_id=1, source_target_pairs={{0,8},{8,0},{16,24},{24,16},{1,9},{9,1},{17,25},{25,17},{2,10},{10... | collective-permute-start | bytes 3145736 | tf_op jit(solution)/shard_map/ppermute | solution.py:408
  88.9 5.7 %collective-permute-start.25 = (bf16[32,1024]{1,0:T(8,128)(2,1)S(1)}, bf16[32,1024]{1,0:T(8,128)(2,1)S(1)}, u32[]{:S(2)}, u32[]{:S(2)}) collective-permute-start(bf16[32,1024]{1,0:T(8,128)(2,1)S(1)} %get-tuple-element.51), channel_id=1, source_target_pairs={{0,2},{2,4},{4,6},{6,7},{7,5},{5,3},{3,1},{1,0},{8,10},{10,12},{12... | collective-permute-start | bytes 196616 | tf_op jit(solution)/shard_map/ppermute | solution.py:418
  90.7 4.3 %collective-permute-start.29 = (bf16[32,1024]{1,0:T(8,128)(2,1)S(1)}, bf16[32,1024]{1,0:T(8,128)(2,1)S(1)}, u32[]{:S(2)}, u32[]{:S(2)}) collective-permute-start(bf16[32,1024]{1,0:T(8,128)(2,1)S(1)} %get-tuple-element.52), channel_id=1, source_target_pairs={{0,1},{2,0},{4,2},{6,4},{7,6},{5,7},{3,5},{1,3},{8,9},{10,8},{12,1... | collective-permute-start | bytes 196616 | tf_op jit(solution)/shard_map/ppermute | solution.py:418
  92.5 4.7 %collective-permute-start.17 = (bf16[32,1024]{1,0:T(8,128)(2,1)S(1)}, bf16[32,1024]{1,0:T(8,128)(2,1)S(1)}, u32[]{:S(2)}, u32[]{:S(2)}) collective-permute-start(bf16[32,1024]{1,0:T(8,128)(2,1)S(1)} %get-tuple-element.48), channel_id=1, source_target_pairs={{0,2},{2,4},{4,6},{6,7},{7,5},{5,3},{3,1},{1,0},{8,10},{10,12},{12... | collective-permute-start | bytes 196616 | tf_op jit(solution)/shard_map/ppermute | solution.py:418
  94.3 4.7 %collective-permute-start.21 = (bf16[32,1024]{1,0:T(8,128)(2,1)S(1)}, bf16[32,1024]{1,0:T(8,128)(2,1)S(1)}, u32[]{:S(2)}, u32[]{:S(2)}) collective-permute-start(bf16[32,1024]{1,0:T(8,128)(2,1)S(1)} %get-tuple-element.49), channel_id=1, source_target_pairs={{0,1},{2,0},{4,2},{6,4},{7,6},{5,7},{3,5},{1,3},{8,9},{10,8},{12,1... | collective-permute-start | bytes 196616 | tf_op jit(solution)/shard_map/ppermute | solution.py:418
  95.0 11.7 %collective-permute-start.30 = (bf16[64,1024]{1,0:T(8,128)(2,1)S(1)}, bf16[64,1024]{1,0:T(8,128)(2,1)S(1)}, u32[]{:S(2)}, u32[]{:S(2)}) collective-permute-start(bf16[64,1024]{1,0:T(8,128)(2,1)S(1)} %pad_maximum_fusion.3), channel_id=1, source_target_pairs={{0,1},{2,0},{4,2},{6,4},{7,6},{5,7},{3,5},{1,3},{8,9},{10,8},{12,1... | collective-permute-start | bytes 393224 | tf_op jit(solution)/shard_map/ppermute | solution.py:418
  96.4 6.4 %collective-permute-start.26 = (bf16[64,1024]{1,0:T(8,128)(2,1)S(1)}, bf16[64,1024]{1,0:T(8,128)(2,1)S(1)}, u32[]{:S(2)}, u32[]{:S(2)}) collective-permute-start(bf16[64,1024]{1,0:T(8,128)(2,1)S(1)} %pad_maximum_fusion.2), channel_id=1, source_target_pairs={{0,2},{2,4},{4,6},{6,7},{7,5},{5,3},{3,1},{1,0},{8,10},{10,12},{12... | collective-permute-start | bytes 393224 | tf_op jit(solution)/shard_map/ppermute | solution.py:418
  99.1 11.2 %collective-permute-start.22 = (bf16[64,1024]{1,0:T(8,128)(2,1)S(1)}, bf16[64,1024]{1,0:T(8,128)(2,1)S(1)}, u32[]{:S(2)}, u32[]{:S(2)}) collective-permute-start(bf16[64,1024]{1,0:T(8,128)(2,1)S(1)} %pad_maximum_fusion.1), channel_id=1, source_target_pairs={{0,1},{2,0},{4,2},{6,4},{7,6},{5,7},{3,5},{1,3},{8,9},{10,8},{12,1... | collective-permute-start | bytes 393224 | tf_op jit(solution)/shard_map/ppermute | solution.py:418
  99.7 6.0 %collective-permute-start.18 = (bf16[64,1024]{1,0:T(8,128)(2,1)S(1)}, bf16[64,1024]{1,0:T(8,128)(2,1)S(1)}, u32[]{:S(2)}, u32[]{:S(2)}) collective-permute-start(bf16[64,1024]{1,0:T(8,128)(2,1)S(1)} %pad_maximum_fusion), channel_id=1, source_target_pairs={{0,2},{2,4},{4,6},{6,7},{7,5},{5,3},{3,1},{1,0},{8,10},{10,12},{12... | collective-permute-start | bytes 393224 | tf_op jit(solution)/shard_map/ppermute | solution.py:418
  102.9 5.2 %collective-permute-start.27 = (bf16[64,1024]{1,0:T(8,128)(2,1)S(1)}, bf16[64,1024]{1,0:T(8,128)(2,1)S(1)}, u32[]{:S(2)}, u32[]{:S(2)}) collective-permute-start(bf16[64,1024]{1,0:T(8,128)(2,1)S(1)} %fusion.2), channel_id=1, source_target_pairs={{0,2},{2,4},{4,6},{6,7},{7,5},{5,3},{3,1},{1,0},{8,10},{10,12},{12... | collective-permute-start | bytes 393224 | tf_op jit(solution)/shard_map/ppermute | solution.py:418
  105.7 5.6 %collective-permute-start.19 = (bf16[64,1024]{1,0:T(8,128)(2,1)S(1)}, bf16[64,1024]{1,0:T(8,128)(2,1)S(1)}, u32[]{:S(2)}, u32[]{:S(2)}) collective-permute-start(bf16[64,1024]{1,0:T(8,128)(2,1)S(1)} %fusion.9), channel_id=1, source_target_pairs={{0,2},{2,4},{4,6},{6,7},{7,5},{5,3},{3,1},{1,0},{8,10},{10,12},{12... | collective-permute-start | bytes 393224 | tf_op jit(solution)/shard_map/ppermute | solution.py:418
  108.2 6.2 %collective-permute-start.31 = (bf16[64,1024]{1,0:T(8,128)(2,1)S(1)}, bf16[64,1024]{1,0:T(8,128)(2,1)S(1)}, u32[]{:S(2)}, u32[]{:S(2)}) collective-permute-start(bf16[64,1024]{1,0:T(8,128)(2,1)S(1)} %get-tuple-element.60), channel_id=1, source_target_pairs={{0,1},{2,0},{4,2},{6,4},{7,6},{5,7},{3,5},{1,3},{8,9},{10,8},{12,1... | collective-permute-start | bytes 393224 | tf_op jit(solution)/shard_map/ppermute | solution.py:418
  109.8 8.7 %collective-permute-start.28 = (bf16[64,1024]{1,0:T(8,128)(2,1)S(1)}, bf16[64,1024]{1,0:T(8,128)(2,1)S(1)}, u32[]{:S(2)}, u32[]{:S(2)}) collective-permute-start(bf16[64,1024]{1,0:T(8,128)(2,1)S(1)} %get-tuple-element.59), channel_id=1, source_target_pairs={{0,2},{2,4},{4,6},{6,7},{7,5},{5,3},{3,1},{1,0},{8,10},{10,12},{12... | collective-permute-start | bytes 393224 | tf_op jit(solution)/shard_map/ppermute | solution.py:418
  111.3 5.9 %collective-permute-start.23 = (bf16[64,1024]{1,0:T(8,128)(2,1)S(1)}, bf16[64,1024]{1,0:T(8,128)(2,1)S(1)}, u32[]{:S(2)}, u32[]{:S(2)}) collective-permute-start(bf16[64,1024]{1,0:T(8,128)(2,1)S(1)} %get-tuple-element.54), channel_id=1, source_target_pairs={{0,1},{2,0},{4,2},{6,4},{7,6},{5,7},{3,5},{1,3},{8,9},{10,8},{12,1... | collective-permute-start | bytes 393224 | tf_op jit(solution)/shard_map/ppermute | solution.py:418
  113.1 5.3 %collective-permute-start.20 = (bf16[64,1024]{1,0:T(8,128)(2,1)S(1)}, bf16[64,1024]{1,0:T(8,128)(2,1)S(1)}, u32[]{:S(2)}, u32[]{:S(2)}) collective-permute-start(bf16[64,1024]{1,0:T(8,128)(2,1)S(1)} %get-tuple-element.53), channel_id=1, source_target_pairs={{0,2},{2,4},{4,6},{6,7},{7,5},{5,3},{3,1},{1,0},{8,10},{10,12},{12... | collective-permute-start | bytes 393224 | tf_op jit(solution)/shard_map/ppermute | solution.py:418
  114.5 5.0 %collective-permute-start.32 = (bf16[64,1024]{1,0:T(8,128)(2,1)S(1)}, bf16[64,1024]{1,0:T(8,128)(2,1)S(1)}, u32[]{:S(2)}, u32[]{:S(2)}) collective-permute-start(bf16[64,1024]{1,0:T(8,128)(2,1)S(1)} %fusion.1), channel_id=1, source_target_pairs={{0,1},{2,0},{4,2},{6,4},{7,6},{5,7},{3,5},{1,3},{8,9},{10,8},{12,1... | collective-permute-start | bytes 393224 | tf_op jit(solution)/shard_map/ppermute | solution.py:418
  117.3 5.0 %collective-permute-start.24 = (bf16[64,1024]{1,0:T(8,128)(2,1)S(1)}, bf16[64,1024]{1,0:T(8,128)(2,1)S(1)}, u32[]{:S(2)}, u32[]{:S(2)}) collective-permute-start(bf16[64,1024]{1,0:T(8,128)(2,1)S(1)} %fusion.8), channel_id=1, source_target_pairs={{0,1},{2,0},{4,2},{6,4},{7,6},{5,7},{3,5},{1,3},{8,9},{10,8},{12,1... | collective-permute-start | bytes 393224 | tf_op jit(solution)/shard_map/ppermute | solution.py:418
  (8 other events, 65.4 us)

commit v6 on v5

--- a/solution.py
+++ b/solution.py
@@ -242,37 +242,57 @@
     )(hidden_in, *attn, norm_gain[None, :], expert_ids, gate_weights)
 
 
-def cast_kernel(up_source, down_source, up_out, down_out, up_ref, down_ref, arrived):
-    def copies(step):
-        for i, (source, target) in enumerate(((up_source, up_ref), (down_source, down_ref))):
-            rows = target.shape[0] // CAST_STEPS
-            here = pl.ds(step * rows, rows)
-            yield pltpu.make_async_copy(source.at[0, here], target.at[here], arrived.at[step, i])
+def cast_kernel(spans, *refs):
+    count = len(spans)
+    sources, targets, scratch = refs[:count], refs[count : 2 * count], refs[2 * count :]
+    wide, narrow, arrived, left = scratch[:count], scratch[count : 2 * count], *scratch[-2:]
+
+    def rows_of(i, step, first=0):
+        rows = wide[i].shape[0] // CAST_STEPS
+        return pl.ds(first + step * rows, rows)
+
+    def copies_in(step):
+        for i, (first, _) in enumerate(spans):
+            yield pltpu.make_async_copy(
+                sources[i].at[0, rows_of(i, step, first)],
+                wide[i].at[rows_of(i, step)],
+                arrived.at[step, i],
+            )
+
+    def copies_out(step):
+        for i in range(count):
+            here = rows_of(i, step)
+            yield pltpu.make_async_copy(narrow[i].at[here], targets[i].at[here], left.at[step, i])
 
     for step in range(CAST_STEPS):
-        for copy in copies(step):
+        for copy in copies_in(step):
             copy.start()
     for step in range(CAST_STEPS):
-        for copy in copies(step):
+        for copy in copies_in(step):
             copy.wait()
-        for source, target in ((up_ref, up_out), (down_ref, down_out)):
-            rows = target.shape[0] // CAST_STEPS
-            here = slice(step * rows, (step + 1) * rows)
-            target[here] = source[here].astype(jnp.bfloat16)
-
-
-def cast_weights(gate_up, down):
-    shapes = gate_up.shape[1:], down.shape[1:]
+        for i in range(count):
+            here = rows_of(i, step)
+            narrow[i][here] = wide[i][here].astype(jnp.bfloat16)
+        for copy in copies_out(step):
+            copy.start()
+    for step in range(CAST_STEPS):
+        for copy in copies_out(step):
+            copy.wait()
+
+
+def cast_rows(arrays, spans):
+    shapes = [(count, x.shape[2]) for x, (_, count) in zip(arrays, spans)]
     return pl.pallas_call(
-        cast_kernel,
+        lambda *refs: cast_kernel(spans, *refs),
         out_shape=[jax.ShapeDtypeStruct(shape, jnp.bfloat16) for shape in shapes],
-        in_specs=[pl.BlockSpec(memory_space=pltpu.HBM)] * 2,
-        out_specs=vmem(2),
+        in_specs=[pl.BlockSpec(memory_space=pltpu.HBM)] * len(arrays),
+        out_specs=[pl.BlockSpec(memory_space=pltpu.HBM)] * len(arrays),
         scratch_shapes=[pltpu.VMEM(shape, jnp.float32) for shape in shapes]
-        + [pltpu.SemaphoreType.DMA((CAST_STEPS, 2))],
+        + [pltpu.VMEM(shape, jnp.bfloat16) for shape in shapes]
+        + [pltpu.SemaphoreType.DMA((CAST_STEPS, len(arrays)))] * 2,
         compiler_params=params(VMEM_MOST),
-        name="cast_weights",
-    )(gate_up, down)
+        name="cast_rows",
+    )(*arrays)
 
 
 def load_tiles(pieces, weights, arrived, tiles, block):
@@ -437,20 +457,30 @@
     return above + far + below[:0:-1], list(zip(above[1:], below[1:])) + [tuple(far)]
 
 
-def scatter_sum(weighted, left, right):
-    sources, rows, _ = weighted.shape
+def scatter_sums(parts):
+    sources, rows, _ = parts[0][0].shape
     half = rows // 2
     reach = sources // 2
-    up, down = around(left, 1), around(right, -1)
-    yield up, down
-    up = jnp.concatenate([add(weighted[reach - 1, :half], up), weighted[reach - 1, half:]])
-    down = jnp.concatenate([weighted[reach + 1, :half], add(weighted[reach + 1, half:], down)])
-    for away in range(reach - 2, -1, -1):
-        up, down = around(up, 1), around(down, -1)
-        yield up, down
-        if away:
-            up = add(weighted[away], up)
-            down = add(weighted[sources - away], down)
+    moving = [(left, right) for _, left, right in parts]
+    for step in range(reach):
+        previous = None
+        for i, (weighted, _, _) in enumerate(parts):
+            up, down = moving[i]
+            if step:
+                up, down = lax.optimization_barrier((up, down))
+                away = reach - step
+                if step == 1:
+                    up = jnp.concatenate([add(weighted[away, :half], up), weighted[away, half:]])
+                    down = jnp.concatenate(
+                        [weighted[-away, :half], add(weighted[-away, half:], down)]
+                    )
+                else:
+                    up, down = add(weighted[away], up), add(weighted[-away], down)
+            if previous is not None:
+                up, down = after(up, *previous), after(down, *previous)
+            previous = moving[i] if step else None
+            moving[i] = around(up, 1), around(down, -1)
+    return [(weighted[0], *ends) for (weighted, _, _), ends in zip(parts, moving)]
 
 
 def every_expert(
@@ -468,19 +498,40 @@
 ):
     expert_count = lax.axis_size("expert")
     width = trainer_down.shape[2]
-    attn = attention(queries, key_pool, value_pool, page_table, prompt_lengths)
-    up_own, down_own = cast_weights(after(trainer_gate_up, attn[0]), trainer_down)
+    depth = trainer_gate_up.shape[1]
+    early = depth // 4
+    late = depth - early
+    (first_own,) = cast_rows([trainer_gate_up], [(0, early)])
+    first_across = partner(first_own, 2)
+    attn = attention(
+        after(queries, first_own), key_pool, value_pool, page_table, prompt_lengths
+    )
+    rest_own, down_own = cast_rows(
+        [after(trainer_gate_up, attn[0]), trainer_down],
+        [(early, late), (0, trainer_down.shape[1])],
+    )
     attn = [attn[0]] + [partner(attn[d], d) for d in (1, 2, 3)]
-    up_across = partner(after(up_own, *attn), 2)
+    rest_across = partner(after(rest_own, *attn), 2)
     resid, rows = norm(
-        after(hidden_in[0], up_own), attn, norm_gain, expert_ids[0], gate_weights[0]
+        after(hidden_in[0], rest_own, first_across),
+        attn,
+        norm_gain,
+        expert_ids[0],
+        gate_weights[0],
     )
     gathered, arrived = gather_rows(rows)
-    up_beside = partner(after(up_own, *arrived[0]), 1)
+    first_beside = partner(after(first_own, *arrived[0]), 1)
+    first_opposite = partner(after(first_across, *arrived[0]), 1)
+    rest_beside = partner(after(rest_own, *arrived[0]), 1)
     down_beside = partner(after(down_own, *arrived[1]), 1)
     down_across = partner(after(down_own, *arrived[2]), 2)
-    up_opposite = partner(after(up_across, *arrived[3]), 1)
-    hidden_units, gates = expert_up(gathered, [up_own, up_beside, up_across, up_opposite])
+    ready = after(rest_across, *arrived[3])
+    rest_opposite = [partner(ready[i : i + early], 1) for i in range(0, late, early)]
+    hidden_units, gates = expert_up(
+        gathered,
+        [first_own, rest_own, first_beside, rest_beside]
+        + [first_across, rest_across, first_opposite, *rest_opposite],
+    )
     down_opposite = partner(after(down_across, hidden_units), 1)
     weights = (down_own, down_beside, down_across, down_opposite)
     slab = width // SLABS
@@ -490,9 +541,9 @@
         for first in starts
     ]
     mixed = []
-    for first, partial in zip(starts, weighted):
+    for first, terms in zip(starts, scatter_sums(weighted)):
         total = resid[:, first : first + slab].astype(jnp.float32)
-        for term in (partial[0][0], *list(scatter_sum(*partial))[-1]):
+        for term in terms:
             total = total + term.astype(jnp.float32)
         mixed.append(total.astype(jnp.bfloat16))
     return jnp.concatenate(mixed, axis=1)[None]

time: 123 us -> 156 us (1.27)
  waiting for transfers between devices: 70.4 us -> 101 us
  Pallas kernels: 18.3 us -> 20.3 us
    ppermute x9 -> x14, waiting for transfers between devices: 33.2 us -> 62.2 us  [partner(): return lax.ppermute(x, 'dp', [(i, i ^ distance) for i in range(4)])]
    ppermute x24, waiting for transfers between devices: 37.1 us -> 39 us  [around(): lax.ppermute(x, 'expert', [(ring[i], ring[(i + step) % count]) for i in r...]
    unnamed x16 -> x18, local copies, waits for them, and re-layouts: 1.78 us -> 0.2 us
    pallas_call x1 -> x2, Pallas kernels: 4.56 us -> 5.94 us  [cast_rows(): pl.pallas_call(lambda *refs: cast_kernel(spans, *refs), out_shape=[jax.Sh...]
    ppermute x9 -> x14, starting transfers between devices: 6.92 us -> 7.47 us  [partner(): return lax.ppermute(x, 'dp', [(i, i ^ distance) for i in range(4)])]
  transfers between devices with their start and end apart: 33 -> 38, of which waited for: 19 -> 27; matrix products, arithmetic and copies ran while one was open for 0% -> 0% of each run, Pallas kernels for 11% -> 9%
where the time goes in v6:
time: 156 us
  waiting for transfers between devices  101 us (65%)
  starting transfers between devices  32.4 us (21%)
  Pallas kernels  20.3 us (13%)
    ppermute x14, waiting for transfers between devices, partner(): return lax.ppermute(x, 'dp', [(i, i ^ distance) for i in range(4)])  62.2 us
    ppermute x24, waiting for transfers between devices, around(): lax.ppermute(x, 'expert', [(ring[i], ring[(i + step) % count]) for i in r...  39 us
    ppermute x24, starting transfers between devices, around(): lax.ppermute(x, 'expert', [(ring[i], ring[(i + step) % count]) for i in r...  24.9 us
    pallas_call x1, Pallas kernels, expert_up(): pl.pallas_call(lambda *refs: up_kernel(len(rows), len(weights), *refs), o...  7.95 us
    ppermute x14, starting transfers between devices, partner(): return lax.ppermute(x, 'dp', [(i, i ^ distance) for i in range(4)])  7.47 us
    pallas_call x2, Pallas kernels, cast_rows(): pl.pallas_call(lambda *refs: cast_kernel(spans, *refs), out_shape=[jax.Sh...  5.94 us
  transfers between devices with their start and end apart: 38, of which 27 were waited for; matrix products, arithmetic and copies ran while one was open for 0% of the time, Pallas kernels for 9%

profile of v6, /device:TPU:0, one launch (start us, length us, event | category | flops | bytes accessed | tf_op | source)
XLA Modules:
  0.0 155.7 jit_solution(341796244362768497)
XLA Ops:
  0.0 1.9 %cast_rows.2.refs_9_ = bf16[128,2048]{1,0:T(8,128)(2,1)} custom-call(f32[1,512,2048]{2,1,0:T(8,128)} %refs_0_.4), custom_call_target="tpu_custom_call" | custom-call | tf_op jit(solution)/shard_map/cast_rows/pallas_call | solution.py:285
  1.9 3.0 %attention.1 = (bf16[64,512]{1,0:T(8,128)(2,1)}, bf16[64,512]{1,0:T(8,128)(2,1)}, bf16[64,512]{1,0:T(8,128)(2,1)}, bf16[64,512]{1,0:T(8,128)(2,1)}) custom-call(s32[1,2]{1,0:T(1,128)} %refs_0_.3, s32[1,4]{1,0:T(1,128)} %refs_1_.2, bf16[1,256,512]{2,1,0:T(8,128)(2,1)} %refs_2_, bf16[2,128,512]{2,1,0:T(8,128)(2,1)} %refs_3_.1, bf16[2,128,512]{2,1,0:T(8,128)(2,1)} %refs_4_.1), custom_call_target="tpu_custom_call" | custom-call | tf_op jit(solution)/shard_map/attention/pallas_call | solution.py:179
  5.5 2.6 %collective-permute-start.2 = (bf16[64,512]{1,0:T(8,128)(2,1)}, bf16[64,512]{1,0:T(8,128)(2,1)S(1)}, u32[]{:S(2)}, u32[]{:S(2)}) collective-permute-start(bf16[64,512]{1,0:T(8,128)(2,1)} %get-tuple-element.56), channel_id=1, source_target_pairs={{0,16},{8,24},{16,0},{24,8},{1,17},{9,25},{17,1},{25,9},{2,18},{10... | collective-permute-start | bytes 196616 | tf_op jit(solution)/shard_map/ppermute | solution.py:428
  8.1 4.0 %cast_rows.3 = (bf16[384,2048]{1,0:T(8,128)(2,1)}, bf16[256,2048]{1,0:T(8,128)(2,1)}) custom-call(f32[1,512,2048]{2,1,0:T(8,128)} %refs_0_.4, f32[1,256,2048]{2,1,0:T(8,128)} %refs_1_.3), custom_call_target="tpu_custom_call" | custom-call | tf_op jit(solution)/shard_map/cast_rows/pallas_call | solution.py:285
  12.4 1.6 %collective-permute-start.14 = (bf16[384,2048]{1,0:T(8,128)(2,1)}, bf16[384,2048]{1,0:T(8,128)(2,1)S(1)}, u32[]{:S(2)}, u32[]{:S(2)}) collective-permute-start(bf16[384,2048]{1,0:T(8,128)(2,1)} %get-tuple-element.62.refs_10_), channel_id=1, source_target_pairs={{0,16},{8,24},{16,0},{24,8},{1,17},{9,25},{17,1},{25,9},{2,18},{10... | collective-permute-start | bytes 4718600 | tf_op jit(solution)/shard_map/ppermute | solution.py:428
  14.6 45.7 %collective-permute-done.refs_13_ = bf16[128,2048]{1,0:T(8,128)(2,1)S(1)} collective-permute-done((bf16[128,2048]{1,0:T(8,128)(2,1)S(1)}, bf16[128,2048]{1,0:T(8,128)(2,1)S(1)}, u32[]{:S(2)}, u32[]{:S(2)}) %collective-permute-start) | collective-permute-done | bytes 524320 | tf_op jit(solution)/shard_map/ppermute | solution.py:428
  60.7 1.9 %collective-permute-start.8 = (bf16[64,2176]{1,0:T(8,128)(2,1)S(1)}, bf16[64,2176]{1,0:T(8,128)(2,1)S(1)}, u32[]{:S(2)}, u32[]{:S(2)}) collective-permute-start(bf16[64,2176]{1,0:T(8,128)(2,1)S(1)} %get-tuple-element.59.refs_0_), channel_id=1, source_target_pairs={{0,2},{2,4},{4,6},{6,7},{7,5},{5,3},{3,1},{1,0},{8,10},{10,12},{12... | collective-permute-start | bytes 835592 | tf_op jit(solution)/shard_map/ppermute | solution.py:438
  62.8 6.1 %collective-permute-done.8.refs_8_ = bf16[64,2176]{1,0:T(8,128)(2,1)S(1)} collective-permute-done((bf16[64,2176]{1,0:T(8,128)(2,1)S(1)}, bf16[64,2176]{1,0:T(8,128)(2,1)S(1)}, u32[]{:S(2)}, u32[]{:S(2)}) %collective-permute-start.8) | collective-permute-done | bytes 278560 | tf_op jit(solution)/shard_map/ppermute | solution.py:438
  68.9 1.8 %collective-permute-start.9 = (bf16[64,2176]{1,0:T(8,128)(2,1)S(1)}, bf16[64,2176]{1,0:T(8,128)(2,1)S(1)}, u32[]{:S(2)}, u32[]{:S(2)}) collective-permute-start(bf16[64,2176]{1,0:T(8,128)(2,1)S(1)} %collective-permute-done.8.refs_8_), channel_id=1, source_target_pairs={{0,2},{2,4},{4,6},{6,7},{7,5},{5,3},{3,1},{1,0},{8,10},{10,12},{12... | collective-permute-start | bytes 835592 | tf_op jit(solution)/shard_map/ppermute | solution.py:438
  70.9 5.2 %collective-permute-done.9.refs_7_ = bf16[64,2176]{1,0:T(8,128)(2,1)S(1)} collective-permute-done((bf16[64,2176]{1,0:T(8,128)(2,1)S(1)}, bf16[64,2176]{1,0:T(8,128)(2,1)S(1)}, u32[]{:S(2)}, u32[]{:S(2)}) %collective-permute-start.9) | collective-permute-done | bytes 278560 | tf_op jit(solution)/shard_map/ppermute | solution.py:438
  76.1 1.8 %collective-permute-start.10 = (bf16[64,2176]{1,0:T(8,128)(2,1)S(1)}, bf16[64,2176]{1,0:T(8,128)(2,1)S(1)}, u32[]{:S(2)}, u32[]{:S(2)}) collective-permute-start(bf16[64,2176]{1,0:T(8,128)(2,1)S(1)} %collective-permute-done.9.refs_7_), channel_id=1, source_target_pairs={{0,2},{2,4},{4,6},{6,7},{7,5},{5,3},{3,1},{1,0},{8,10},{10,12},{12... | collective-permute-start | bytes 835592 | tf_op jit(solution)/shard_map/ppermute | solution.py:438
  78.2 5.2 %collective-permute-done.10.refs_6_ = bf16[64,2176]{1,0:T(8,128)(2,1)S(1)} collective-permute-done((bf16[64,2176]{1,0:T(8,128)(2,1)S(1)}, bf16[64,2176]{1,0:T(8,128)(2,1)S(1)}, u32[]{:S(2)}, u32[]{:S(2)}) %collective-permute-start.10) | collective-permute-done | bytes 278560 | tf_op jit(solution)/shard_map/ppermute | solution.py:438
  83.4 1.8 %collective-permute-start.11 = (bf16[32,2176]{1,0:T(8,128)(2,1)S(1)}, bf16[32,2176]{1,0:T(8,128)(2,1)S(1)}, u32[]{:S(2)}, u32[]{:S(2)}) collective-permute-start(bf16[32,2176]{1,0:T(8,128)(2,1)S(1)} %slice.101), channel_id=1, source_target_pairs={{0,2},{2,4},{4,6},{6,7},{7,5},{5,3},{3,1},{1,0},{8,10},{10,12},{12... | collective-permute-start | bytes 417800 | tf_op jit(solution)/shard_map/ppermute | solution.py:438
  85.5 3.0 %collective-permute-done.11.refs_5_ = bf16[32,2176]{1,0:T(8,128)(2,1)S(1)} collective-permute-done((bf16[32,2176]{1,0:T(8,128)(2,1)S(1)}, bf16[32,2176]{1,0:T(8,128)(2,1)S(1)}, u32[]{:S(2)}, u32[]{:S(2)}) %collective-permute-start.11) | collective-permute-done | bytes 139296 | tf_op jit(solution)/shard_map/ppermute | solution.py:438
  88.5 1.9 %collective-permute-done.7.refs_4_ = bf16[32,2176]{1,0:T(8,128)(2,1)S(1)} collective-permute-done((bf16[32,2176]{1,0:T(8,128)(2,1)S(1)}, bf16[32,2176]{1,0:T(8,128)(2,1)S(1)}, u32[]{:S(2)}, u32[]{:S(2)}) %collective-permute-start.7) | collective-permute-done | bytes 139296 | tf_op jit(solution)/shard_map/ppermute | solution.py:438
  90.4 1.5 collective-permute-start.20
  95.4 8.0 %expert_up.1 = (bf16[512,1024]{1,0:T(8,128)(2,1)S(1)}, f32[512,1]{1,0:T(8,128)S(1)}) custom-call(bf16[64,2176]{1,0:T(8,128)(2,1)S(1)} %get-tuple-element.59.refs_0_, bf16[64,2176]{1,0:T(8,128)(2,1)S(1)} %collective-permute-done.4.refs_1_, bf16[64,2176]{1,0:T(8,128)(2,1)S(1)} %collective-permute-done.5.refs_2_, ...), custom_call_target="tpu_custom_call" | custom-call | flops 1 | bytes 1 | tf_op jit(solution)/shard_map/expert_up/pallas_call | solution.py:363
  103.4 10.9 %collective-permute-done.20.refs_4_ = bf16[256,2048]{1,0:T(8,128)(2,1)S(1)} collective-permute-done((bf16[256,2048]{1,0:T(8,128)(2,1)}, bf16[256,2048]{1,0:T(8,128)(2,1)S(1)}, u32[]{:S(2)}, u32[]{:S(2)}) %collective-permute-start.20) | collective-permute-done | bytes 1048608 | tf_op jit(solution)/shard_map/ppermute | solution.py:428
  114.3 2.7 %collective-permute-done.21.refs_5_ = bf16[256,2048]{1,0:T(8,128)(2,1)S(1)} collective-permute-done((bf16[256,2048]{1,0:T(8,128)(2,1)S(1)}, bf16[256,2048]{1,0:T(8,128)(2,1)S(1)}, u32[]{:S(2)}, u32[]{:S(2)}) %collective-permute-start.21) | collective-permute-done | bytes 1048608 | tf_op jit(solution)/shard_map/ppermute | solution.py:428
  117.0 1.5 expert_down.3
  118.5 1.8 %collective-permute-start.30 = (bf16[32,1024]{1,0:T(8,128)(2,1)S(1)}, bf16[32,1024]{1,0:T(8,128)(2,1)S(1)}, u32[]{:S(2)}, u32[]{:S(2)}) collective-permute-start(bf16[32,1024]{1,0:T(8,128)(2,1)S(1)} %get-tuple-element.81), channel_id=1, source_target_pairs={{0,2},{2,4},{4,6},{6,7},{7,5},{5,3},{3,1},{1,0},{8,10},{10,12},{12... | collective-permute-start | bytes 196616 | tf_op jit(solution)/shard_map/ppermute | solution.py:438
  120.6 1.5 expert_down.2
  122.1 1.8 %collective-permute-start.22 = (bf16[32,1024]{1,0:T(8,128)(2,1)S(1)}, bf16[32,1024]{1,0:T(8,128)(2,1)S(1)}, u32[]{:S(2)}, u32[]{:S(2)}) collective-permute-start(bf16[32,1024]{1,0:T(8,128)(2,1)S(1)} %get-tuple-element.72), channel_id=1, source_target_pairs={{0,2},{2,4},{4,6},{6,7},{7,5},{5,3},{3,1},{1,0},{8,10},{10,12},{12... | collective-permute-start | bytes 196616 | tf_op jit(solution)/shard_map/ppermute | solution.py:438
  124.6 1.8 %collective-permute-done.22 = bf16[32,1024]{1,0:T(8,128)(2,1)S(1)} collective-permute-done((bf16[32,1024]{1,0:T(8,128)(2,1)S(1)}, bf16[32,1024]{1,0:T(8,128)(2,1)S(1)}, u32[]{:S(2)}, u32[]{:S(2)}) %collective-permute-start.22) | collective-permute-done | bytes 65568 | tf_op jit(solution)/shard_map/ppermute | solution.py:438
  126.4 1.8 %collective-permute-done.23 = bf16[32,1024]{1,0:T(8,128)(2,1)S(1)} collective-permute-done((bf16[32,1024]{1,0:T(8,128)(2,1)S(1)}, bf16[32,1024]{1,0:T(8,128)(2,1)S(1)}, u32[]{:S(2)}, u32[]{:S(2)}) %collective-permute-start.23) | collective-permute-done | bytes 65568 | tf_op jit(solution)/shard_map/ppermute | solution.py:438
  128.4 1.8 %collective-permute-start.32 = (bf16[64,1024]{1,0:T(8,128)(2,1)S(1)}, bf16[64,1024]{1,0:T(8,128)(2,1)S(1)}, u32[]{:S(2)}, u32[]{:S(2)}) collective-permute-start(bf16[64,1024]{1,0:T(8,128)(2,1)S(1)} %get-tuple-element.84), channel_id=1, source_target_pairs={{0,2},{2,4},{4,6},{6,7},{7,5},{5,3},{3,1},{1,0},{8,10},{10,12},{12... | collective-permute-start | bytes 393224 | tf_op jit(solution)/shard_map/ppermute | solution.py:438
  130.6 1.8 %collective-permute-start.24 = (bf16[64,1024]{1,0:T(8,128)(2,1)S(1)}, bf16[64,1024]{1,0:T(8,128)(2,1)S(1)}, u32[]{:S(2)}, u32[]{:S(2)}) collective-permute-start(bf16[64,1024]{1,0:T(8,128)(2,1)S(1)} %pad_maximum_fusion), channel_id=1, source_target_pairs={{0,2},{2,4},{4,6},{6,7},{7,5},{5,3},{3,1},{1,0},{8,10},{10,12},{12... | collective-permute-start | bytes 393224 | tf_op jit(solution)/shard_map/ppermute | solution.py:438
  133.6 1.6 %collective-permute-done.25 = bf16[64,1024]{1,0:T(8,128)(2,1)S(1)} collective-permute-done((bf16[64,1024]{1,0:T(8,128)(2,1)S(1)}, bf16[64,1024]{1,0:T(8,128)(2,1)S(1)}, u32[]{:S(2)}, u32[]{:S(2)}) %collective-permute-start.25) | collective-permute-done | bytes 131104 | tf_op jit(solution)/shard_map/ppermute | solution.py:438
  135.6 1.7 %collective-permute-start.35 = (bf16[64,1024]{1,0:T(8,128)(2,1)S(1)}, bf16[64,1024]{1,0:T(8,128)(2,1)S(1)}, u32[]{:S(2)}, u32[]{:S(2)}) collective-permute-start(bf16[64,1024]{1,0:T(8,128)(2,1)S(1)} %get-tuple-element.90), channel_id=1, source_target_pairs={{0,1},{2,0},{4,2},{6,4},{7,6},{5,7},{3,5},{1,3},{8,9},{10,8},{12,1... | collective-permute-start | bytes 393224 | tf_op jit(solution)/shard_map/ppermute | solution.py:438
  137.8 2.1 %collective-permute-start.26 = (bf16[64,1024]{1,0:T(8,128)(2,1)S(1)}, bf16[64,1024]{1,0:T(8,128)(2,1)S(1)}, u32[]{:S(2)}, u32[]{:S(2)}) collective-permute-start(bf16[64,1024]{1,0:T(8,128)(2,1)S(1)} %get-tuple-element.103), channel_id=1, source_target_pairs={{0,2},{2,4},{4,6},{6,7},{7,5},{5,3},{3,1},{1,0},{8,10},{10,12},{12... | collective-permute-start | bytes 393224 | tf_op jit(solution)/shard_map/ppermute | solution.py:438
  142.3 2.3 %collective-permute-done.26 = bf16[64,1024]{1,0:T(8,128)(2,1)S(1)} collective-permute-done((bf16[64,1024]{1,0:T(8,128)(2,1)S(1)}, bf16[64,1024]{1,0:T(8,128)(2,1)S(1)}, u32[]{:S(2)}, u32[]{:S(2)}) %collective-permute-start.26) | collective-permute-done | bytes 131104 | tf_op jit(solution)/shard_map/ppermute | solution.py:438
  144.6 1.7 %collective-permute-done.27 = bf16[64,1024]{1,0:T(8,128)(2,1)S(1)} collective-permute-done((bf16[64,1024]{1,0:T(8,128)(2,1)S(1)}, bf16[64,1024]{1,0:T(8,128)(2,1)S(1)}, u32[]{:S(2)}, u32[]{:S(2)}) %collective-permute-start.27) | collective-permute-done | bytes 131104 | tf_op jit(solution)/shard_map/ppermute | solution.py:438
  (85 shorter events, 21.9 us)
Async XLA Ops:
  4.9 7.2 %collective-permute-start.1 = (bf16[64,512]{1,0:T(8,128)(2,1)}, bf16[64,512]{1,0:T(8,128)(2,1)S(1)}, u32[]{:S(2)}, u32[]{:S(2)}) collective-permute-start(bf16[64,512]{1,0:T(8,128)(2,1)} %get-tuple-element.55), channel_id=1, source_target_pairs={{0,8},{8,0},{16,24},{24,16},{1,9},{9,1},{17,25},{25,17},{2,10},{10... | collective-permute-start | bytes 196616 | tf_op jit(solution)/shard_map/ppermute | solution.py:428
  5.5 6.7 %collective-permute-start.2 = (bf16[64,512]{1,0:T(8,128)(2,1)}, bf16[64,512]{1,0:T(8,128)(2,1)S(1)}, u32[]{:S(2)}, u32[]{:S(2)}) collective-permute-start(bf16[64,512]{1,0:T(8,128)(2,1)} %get-tuple-element.56), channel_id=1, source_target_pairs={{0,16},{8,24},{16,0},{24,8},{1,17},{9,25},{17,1},{25,9},{2,18},{10... | collective-permute-start | bytes 196616 | tf_op jit(solution)/shard_map/ppermute | solution.py:428
  8.0 4.3 %collective-permute-start.3 = (bf16[64,512]{1,0:T(8,128)(2,1)}, bf16[64,512]{1,0:T(8,128)(2,1)S(1)}, u32[]{:S(2)}, u32[]{:S(2)}) collective-permute-start(bf16[64,512]{1,0:T(8,128)(2,1)} %get-tuple-element.57), channel_id=1, source_target_pairs={{0,24},{8,16},{16,8},{24,0},{1,25},{9,17},{17,9},{25,1},{2,26},{10... | collective-permute-start | bytes 196616 | tf_op jit(solution)/shard_map/ppermute | solution.py:428
  12.4 79.5 %collective-permute-start.14 = (bf16[384,2048]{1,0:T(8,128)(2,1)}, bf16[384,2048]{1,0:T(8,128)(2,1)S(1)}, u32[]{:S(2)}, u32[]{:S(2)}) collective-permute-start(bf16[384,2048]{1,0:T(8,128)(2,1)} %get-tuple-element.62.refs_10_), channel_id=1, source_target_pairs={{0,16},{8,24},{16,0},{24,8},{1,17},{9,25},{17,1},{25,9},{2,18},{10... | collective-permute-start | bytes 4718600 | tf_op jit(solution)/shard_map/ppermute | solution.py:428
  14.0 46.3 %collective-permute-start = (bf16[128,2048]{1,0:T(8,128)(2,1)S(1)}, bf16[128,2048]{1,0:T(8,128)(2,1)S(1)}, u32[]{:S(2)}, u32[]{:S(2)}) collective-permute-start(bf16[128,2048]{1,0:T(8,128)(2,1)S(1)} %copy-done.1), channel_id=1, source_target_pairs={{0,16},{8,24},{16,0},{24,8},{1,17},{9,25},{17,1},{25,9},{2,18},{10... | collective-permute-start | bytes 1572872 | tf_op jit(solution)/shard_map/ppermute | solution.py:428
  60.7 8.2 %collective-permute-start.8 = (bf16[64,2176]{1,0:T(8,128)(2,1)S(1)}, bf16[64,2176]{1,0:T(8,128)(2,1)S(1)}, u32[]{:S(2)}, u32[]{:S(2)}) collective-permute-start(bf16[64,2176]{1,0:T(8,128)(2,1)S(1)} %get-tuple-element.59.refs_0_), channel_id=1, source_target_pairs={{0,2},{2,4},{4,6},{6,7},{7,5},{5,3},{3,1},{1,0},{8,10},{10,12},{12... | collective-permute-start | bytes 835592 | tf_op jit(solution)/shard_map/ppermute | solution.py:438
  62.6 8.1 %collective-permute-start.4 = (bf16[64,2176]{1,0:T(8,128)(2,1)S(1)}, bf16[64,2176]{1,0:T(8,128)(2,1)S(1)}, u32[]{:S(2)}, u32[]{:S(2)}) collective-permute-start(bf16[64,2176]{1,0:T(8,128)(2,1)S(1)} %get-tuple-element.59.refs_0_), channel_id=1, source_target_pairs={{0,1},{2,0},{4,2},{6,4},{7,6},{5,7},{3,5},{1,3},{8,9},{10,8},{12,1... | collective-permute-start | bytes 835592 | tf_op jit(solution)/shard_map/ppermute | solution.py:438
  68.9 7.2 %collective-permute-start.9 = (bf16[64,2176]{1,0:T(8,128)(2,1)S(1)}, bf16[64,2176]{1,0:T(8,128)(2,1)S(1)}, u32[]{:S(2)}, u32[]{:S(2)}) collective-permute-start(bf16[64,2176]{1,0:T(8,128)(2,1)S(1)} %collective-permute-done.8.refs_8_), channel_id=1, source_target_pairs={{0,2},{2,4},{4,6},{6,7},{7,5},{5,3},{3,1},{1,0},{8,10},{10,12},{12... | collective-permute-start | bytes 835592 | tf_op jit(solution)/shard_map/ppermute | solution.py:438
  70.7 7.2 %collective-permute-start.5 = (bf16[64,2176]{1,0:T(8,128)(2,1)S(1)}, bf16[64,2176]{1,0:T(8,128)(2,1)S(1)}, u32[]{:S(2)}, u32[]{:S(2)}) collective-permute-start(bf16[64,2176]{1,0:T(8,128)(2,1)S(1)} %collective-permute-done.4.refs_1_), channel_id=1, source_target_pairs={{0,1},{2,0},{4,2},{6,4},{7,6},{5,7},{3,5},{1,3},{8,9},{10,8},{12,1... | collective-permute-start | bytes 835592 | tf_op jit(solution)/shard_map/ppermute | solution.py:438
  70.9 24.5 %collective-permute-start.13 = (bf16[384,2048]{1,0:T(8,128)(2,1)}, bf16[384,2048]{1,0:T(8,128)(2,1)S(1)}, u32[]{:S(2)}, u32[]{:S(2)}) collective-permute-start(bf16[384,2048]{1,0:T(8,128)(2,1)} %get-tuple-element.62.refs_10_), channel_id=1, source_target_pairs={{0,8},{8,0},{16,24},{24,16},{1,9},{9,1},{17,25},{25,17},{2,10},{10... | collective-permute-start | bytes 4718600 | tf_op jit(solution)/shard_map/ppermute | solution.py:428
  76.1 7.2 %collective-permute-start.10 = (bf16[64,2176]{1,0:T(8,128)(2,1)S(1)}, bf16[64,2176]{1,0:T(8,128)(2,1)S(1)}, u32[]{:S(2)}, u32[]{:S(2)}) collective-permute-start(bf16[64,2176]{1,0:T(8,128)(2,1)S(1)} %collective-permute-done.9.refs_7_), channel_id=1, source_target_pairs={{0,2},{2,4},{4,6},{6,7},{7,5},{5,3},{3,1},{1,0},{8,10},{10,12},{12... | collective-permute-start | bytes 835592 | tf_op jit(solution)/shard_map/ppermute | solution.py:438
  77.9 7.3 %collective-permute-start.6 = (bf16[64,2176]{1,0:T(8,128)(2,1)S(1)}, bf16[64,2176]{1,0:T(8,128)(2,1)S(1)}, u32[]{:S(2)}, u32[]{:S(2)}) collective-permute-start(bf16[64,2176]{1,0:T(8,128)(2,1)S(1)} %collective-permute-done.5.refs_2_), channel_id=1, source_target_pairs={{0,1},{2,0},{4,2},{6,4},{7,6},{5,7},{3,5},{1,3},{8,9},{10,8},{12,1... | collective-permute-start | bytes 835592 | tf_op jit(solution)/shard_map/ppermute | solution.py:438
  83.4 5.1 %collective-permute-start.11 = (bf16[32,2176]{1,0:T(8,128)(2,1)S(1)}, bf16[32,2176]{1,0:T(8,128)(2,1)S(1)}, u32[]{:S(2)}, u32[]{:S(2)}) collective-permute-start(bf16[32,2176]{1,0:T(8,128)(2,1)S(1)} %slice.101), channel_id=1, source_target_pairs={{0,2},{2,4},{4,6},{6,7},{7,5},{5,3},{3,1},{1,0},{8,10},{10,12},{12... | collective-permute-start | bytes 417800 | tf_op jit(solution)/shard_map/ppermute | solution.py:438
  85.2 5.1 %collective-permute-start.7 = (bf16[32,2176]{1,0:T(8,128)(2,1)S(1)}, bf16[32,2176]{1,0:T(8,128)(2,1)S(1)}, u32[]{:S(2)}, u32[]{:S(2)}) collective-permute-start(bf16[32,2176]{1,0:T(8,128)(2,1)S(1)} %slice.100), channel_id=1, source_target_pairs={{0,1},{2,0},{4,2},{6,4},{7,6},{5,7},{3,5},{1,3},{8,9},{10,8},{12,1... | collective-permute-start | bytes 417800 | tf_op jit(solution)/shard_map/ppermute | solution.py:438
  85.5 6.5 %collective-permute-start.15 = (bf16[128,2048]{1,0:T(8,128)(2,1)S(1)}, bf16[128,2048]{1,0:T(8,128)(2,1)S(1)}, u32[]{:S(2)}, u32[]{:S(2)}) collective-permute-start(bf16[128,2048]{1,0:T(8,128)(2,1)S(1)} %collective-permute-done.refs_13_), channel_id=1, source_target_pairs={{0,8},{8,0},{16,24},{24,16},{1,9},{9,1},{17,25},{25,17},{2,10},{10... | collective-permute-start | bytes 1572872 | tf_op jit(solution)/shard_map/ppermute | solution.py:428
  90.4 24.0 %collective-permute-start.20 = (bf16[256,2048]{1,0:T(8,128)(2,1)}, bf16[256,2048]{1,0:T(8,128)(2,1)S(1)}, u32[]{:S(2)}, u32[]{:S(2)}) collective-permute-start(bf16[256,2048]{1,0:T(8,128)(2,1)} %get-tuple-element.69.refs_2_), channel_id=1, source_target_pairs={{0,16},{8,24},{16,0},{24,8},{1,17},{9,25},{17,1},{25,9},{2,18},{10... | collective-permute-start | bytes 3145736 | tf_op jit(solution)/shard_map/ppermute | solution.py:428
  93.9 20.4 %collective-permute-start.19 = (bf16[256,2048]{1,0:T(8,128)(2,1)S(1)}, bf16[256,2048]{1,0:T(8,128)(2,1)S(1)}, u32[]{:S(2)}, u32[]{:S(2)}) collective-permute-start(bf16[256,2048]{1,0:T(8,128)(2,1)S(1)} %copy-done), channel_id=1, source_target_pairs={{0,8},{8,0},{16,24},{24,16},{1,9},{9,1},{17,25},{25,17},{2,10},{10... | collective-permute-start | bytes 3145736 | tf_op jit(solution)/shard_map/ppermute | solution.py:428
  118.5 5.7 %collective-permute-start.30 = (bf16[32,1024]{1,0:T(8,128)(2,1)S(1)}, bf16[32,1024]{1,0:T(8,128)(2,1)S(1)}, u32[]{:S(2)}, u32[]{:S(2)}) collective-permute-start(bf16[32,1024]{1,0:T(8,128)(2,1)S(1)} %get-tuple-element.81), channel_id=1, source_target_pairs={{0,2},{2,4},{4,6},{6,7},{7,5},{5,3},{3,1},{1,0},{8,10},{10,12},{12... | collective-permute-start | bytes 196616 | tf_op jit(solution)/shard_map/ppermute | solution.py:438
  120.3 4.3 %collective-permute-start.31 = (bf16[32,1024]{1,0:T(8,128)(2,1)S(1)}, bf16[32,1024]{1,0:T(8,128)(2,1)S(1)}, u32[]{:S(2)}, u32[]{:S(2)}) collective-permute-start(bf16[32,1024]{1,0:T(8,128)(2,1)S(1)} %get-tuple-element.82), channel_id=1, source_target_pairs={{0,1},{2,0},{4,2},{6,4},{7,6},{5,7},{3,5},{1,3},{8,9},{10,8},{12,1... | collective-permute-start | bytes 196616 | tf_op jit(solution)/shard_map/ppermute | solution.py:438
  122.1 4.3 %collective-permute-start.22 = (bf16[32,1024]{1,0:T(8,128)(2,1)S(1)}, bf16[32,1024]{1,0:T(8,128)(2,1)S(1)}, u32[]{:S(2)}, u32[]{:S(2)}) collective-permute-start(bf16[32,1024]{1,0:T(8,128)(2,1)S(1)} %get-tuple-element.72), channel_id=1, source_target_pairs={{0,2},{2,4},{4,6},{6,7},{7,5},{5,3},{3,1},{1,0},{8,10},{10,12},{12... | collective-permute-start | bytes 196616 | tf_op jit(solution)/shard_map/ppermute | solution.py:438
  128.1 5.3 %collective-permute-start.33 = (bf16[64,1024]{1,0:T(8,128)(2,1)S(1)}, bf16[64,1024]{1,0:T(8,128)(2,1)S(1)}, u32[]{:S(2)}, u32[]{:S(2)}) collective-permute-start(bf16[64,1024]{1,0:T(8,128)(2,1)S(1)} %get-tuple-element.86), channel_id=1, source_target_pairs={{0,1},{2,0},{4,2},{6,4},{7,6},{5,7},{3,5},{1,3},{8,9},{10,8},{12,1... | collective-permute-start | bytes 393224 | tf_op jit(solution)/shard_map/ppermute | solution.py:438
  128.4 5.2 %collective-permute-start.32 = (bf16[64,1024]{1,0:T(8,128)(2,1)S(1)}, bf16[64,1024]{1,0:T(8,128)(2,1)S(1)}, u32[]{:S(2)}, u32[]{:S(2)}) collective-permute-start(bf16[64,1024]{1,0:T(8,128)(2,1)S(1)} %get-tuple-element.84), channel_id=1, source_target_pairs={{0,2},{2,4},{4,6},{6,7},{7,5},{5,3},{3,1},{1,0},{8,10},{10,12},{12... | collective-permute-start | bytes 393224 | tf_op jit(solution)/shard_map/ppermute | solution.py:438
  130.2 5.1 %collective-permute-start.25 = (bf16[64,1024]{1,0:T(8,128)(2,1)S(1)}, bf16[64,1024]{1,0:T(8,128)(2,1)S(1)}, u32[]{:S(2)}, u32[]{:S(2)}) collective-permute-start(bf16[64,1024]{1,0:T(8,128)(2,1)S(1)} %pad_maximum_fusion.1), channel_id=1, source_target_pairs={{0,1},{2,0},{4,2},{6,4},{7,6},{5,7},{3,5},{1,3},{8,9},{10,8},{12,1... | collective-permute-start | bytes 393224 | tf_op jit(solution)/shard_map/ppermute | solution.py:438
  130.6 5.0 %collective-permute-start.24 = (bf16[64,1024]{1,0:T(8,128)(2,1)S(1)}, bf16[64,1024]{1,0:T(8,128)(2,1)S(1)}, u32[]{:S(2)}, u32[]{:S(2)}) collective-permute-start(bf16[64,1024]{1,0:T(8,128)(2,1)S(1)} %pad_maximum_fusion), channel_id=1, source_target_pairs={{0,2},{2,4},{4,6},{6,7},{7,5},{5,3},{3,1},{1,0},{8,10},{10,12},{12... | collective-permute-start | bytes 393224 | tf_op jit(solution)/shard_map/ppermute | solution.py:438
  135.6 5.5 %collective-permute-start.35 = (bf16[64,1024]{1,0:T(8,128)(2,1)S(1)}, bf16[64,1024]{1,0:T(8,128)(2,1)S(1)}, u32[]{:S(2)}, u32[]{:S(2)}) collective-permute-start(bf16[64,1024]{1,0:T(8,128)(2,1)S(1)} %get-tuple-element.90), channel_id=1, source_target_pairs={{0,1},{2,0},{4,2},{6,4},{7,6},{5,7},{3,5},{1,3},{8,9},{10,8},{12,1... | collective-permute-start | bytes 393224 | tf_op jit(solution)/shard_map/ppermute | solution.py:438
  137.3 5.0 %collective-permute-start.34 = (bf16[64,1024]{1,0:T(8,128)(2,1)S(1)}, bf16[64,1024]{1,0:T(8,128)(2,1)S(1)}, u32[]{:S(2)}, u32[]{:S(2)}) collective-permute-start(bf16[64,1024]{1,0:T(8,128)(2,1)S(1)} %get-tuple-element.88), channel_id=1, source_target_pairs={{0,2},{2,4},{4,6},{6,7},{7,5},{5,3},{3,1},{1,0},{8,10},{10,12},{12... | collective-permute-start | bytes 393224 | tf_op jit(solution)/shard_map/ppermute | solution.py:438
  137.8 6.8 %collective-permute-start.26 = (bf16[64,1024]{1,0:T(8,128)(2,1)S(1)}, bf16[64,1024]{1,0:T(8,128)(2,1)S(1)}, u32[]{:S(2)}, u32[]{:S(2)}) collective-permute-start(bf16[64,1024]{1,0:T(8,128)(2,1)S(1)} %get-tuple-element.103), channel_id=1, source_target_pairs={{0,2},{2,4},{4,6},{6,7},{7,5},{5,3},{3,1},{1,0},{8,10},{10,12},{12... | collective-permute-start | bytes 393224 | tf_op jit(solution)/shard_map/ppermute | solution.py:438
  139.9 6.4 %collective-permute-start.27 = (bf16[64,1024]{1,0:T(8,128)(2,1)S(1)}, bf16[64,1024]{1,0:T(8,128)(2,1)S(1)}, u32[]{:S(2)}, u32[]{:S(2)}) collective-permute-start(bf16[64,1024]{1,0:T(8,128)(2,1)S(1)} %get-tuple-element.102), channel_id=1, source_target_pairs={{0,1},{2,0},{4,2},{6,4},{7,6},{5,7},{3,5},{1,3},{8,9},{10,8},{12,1... | collective-permute-start | bytes 393224 | tf_op jit(solution)/shard_map/ppermute | solution.py:438
  146.3 5.0 %collective-permute-start.36 = (bf16[64,1024]{1,0:T(8,128)(2,1)S(1)}, bf16[64,1024]{1,0:T(8,128)(2,1)S(1)}, u32[]{:S(2)}, u32[]{:S(2)}) collective-permute-start(bf16[64,1024]{1,0:T(8,128)(2,1)S(1)} %get-tuple-element.92), channel_id=1, source_target_pairs={{0,2},{2,4},{4,6},{6,7},{7,5},{5,3},{3,1},{1,0},{8,10},{10,12},{12... | collective-permute-start | bytes 393224 | tf_op jit(solution)/shard_map/ppermute | solution.py:438
  147.6 5.0 %collective-permute-start.37 = (bf16[64,1024]{1,0:T(8,128)(2,1)S(1)}, bf16[64,1024]{1,0:T(8,128)(2,1)S(1)}, u32[]{:S(2)}, u32[]{:S(2)}) collective-permute-start(bf16[64,1024]{1,0:T(8,128)(2,1)S(1)} %get-tuple-element.94), channel_id=1, source_target_pairs={{0,1},{2,0},{4,2},{6,4},{7,6},{5,7},{3,5},{1,3},{8,9},{10,8},{12,1... | collective-permute-start | bytes 393224 | tf_op jit(solution)/shard_map/ppermute | solution.py:438
  148.4 5.0 %collective-permute-start.28 = (bf16[64,1024]{1,0:T(8,128)(2,1)S(1)}, bf16[64,1024]{1,0:T(8,128)(2,1)S(1)}, u32[]{:S(2)}, u32[]{:S(2)}) collective-permute-start(bf16[64,1024]{1,0:T(8,128)(2,1)S(1)} %get-tuple-element.98), channel_id=1, source_target_pairs={{0,2},{2,4},{4,6},{6,7},{7,5},{5,3},{3,1},{1,0},{8,10},{10,12},{12... | collective-permute-start | bytes 393224 | tf_op jit(solution)/shard_map/ppermute | solution.py:438
  149.8 5.0 %collective-permute-start.29 = (bf16[64,1024]{1,0:T(8,128)(2,1)S(1)}, bf16[64,1024]{1,0:T(8,128)(2,1)S(1)}, u32[]{:S(2)}, u32[]{:S(2)}) collective-permute-start(bf16[64,1024]{1,0:T(8,128)(2,1)S(1)} %get-tuple-element.99), channel_id=1, source_target_pairs={{0,1},{2,0},{4,2},{6,4},{7,6},{5,7},{3,5},{1,3},{8,9},{10,8},{12,1... | collective-permute-start | bytes 393224 | tf_op jit(solution)/shard_map/ppermute | solution.py:438
  (14 other events, 206.1 us)

commit v7 on v6

--- a/solution.py
+++ b/solution.py
@@ -112,8 +112,8 @@
 LANES = 128
 VMEM_LIMIT = 32 * 2**20
 VMEM_MOST = 60 * 2**20
+CAST_STEPS = 4
 SLABS = 2
-CAST_STEPS = 4
 SMALL = pl.CostEstimate(flops=1, bytes_accessed=1, transcendentals=0)
 
 
@@ -126,8 +126,8 @@
 
 
 def attention_kernel(*refs):
-    sources, outs, scratch = refs[:5], refs[5:9], refs[9:]
-    table, lengths, q_ref, k_ref, v_ref, attn, arrived = scratch
+    sources, outs, piece_ref, scratch = refs[:6], refs[6:10], refs[10], refs[11:]
+    table, lengths, q_ref, k_ref, v_ref, weights, attn, arrived = scratch
     copies = [
         pltpu.make_async_copy(source, target, arrived.at[i])
         for i, (source, target) in enumerate(
@@ -137,9 +137,13 @@
             )
         )
     ]
+    rows = weights.shape[0]
+    copies.append(
+        pltpu.make_async_copy(sources[5].at[0, pl.ds(0, rows)], weights, arrived.at[5])
+    )
     for copy in copies:
         copy.start()
-    for copy in copies:
+    for copy in copies[:5]:
         copy.wait()
     tokens, width = q_ref.shape
     pages = k_ref.shape[0]
@@ -172,27 +176,31 @@
     for d in range(4):
         first = pl.multiple_of((own ^ d) * rows, rows)
         outs[d][...] = attn[pl.ds(first, rows), :]
-
-
-def attention(queries, key_pool, value_pool, page_table, prompt_lengths):
+    copies[5].wait()
+    piece_ref[...] = weights[...].astype(jnp.bfloat16)
+
+
+def attention(queries, key_pool, value_pool, page_table, prompt_lengths, gate_up, early):
     tokens, width = queries.shape[1:]
     return pl.pallas_call(
         attention_kernel,
-        out_shape=[jax.ShapeDtypeStruct((tokens // 4, width), jnp.bfloat16)] * 4,
-        in_specs=[pl.BlockSpec(memory_space=pltpu.HBM)] * 5,
-        out_specs=vmem(4),
+        out_shape=[jax.ShapeDtypeStruct((tokens // 4, width), jnp.bfloat16)] * 4
+        + [jax.ShapeDtypeStruct((early, gate_up.shape[2]), jnp.bfloat16)],
+        in_specs=[pl.BlockSpec(memory_space=pltpu.HBM)] * 6,
+        out_specs=vmem(5),
         scratch_shapes=[
             pltpu.SMEM(page_table.shape, jnp.int32),
             pltpu.SMEM(prompt_lengths.shape, jnp.int32),
             pltpu.VMEM((tokens, width), jnp.bfloat16),
             pltpu.VMEM(key_pool.shape, jnp.bfloat16),
             pltpu.VMEM(value_pool.shape, jnp.bfloat16),
+            pltpu.VMEM((early, gate_up.shape[2]), jnp.float32),
             pltpu.VMEM((tokens, width), jnp.bfloat16),
-            pltpu.SemaphoreType.DMA((5,)),
+            pltpu.SemaphoreType.DMA((6,)),
         ],
         compiler_params=params(VMEM_MOST),
         name="attention",
-    )(page_table, prompt_lengths, queries, key_pool, value_pool)
+    )(page_table, prompt_lengths, queries, key_pool, value_pool, gate_up)
 
 
 def norm_kernel(hidden_ref, a0, a1, a2, a3, gain_ref, ids_ref, gates_ref, resid_ref, rows_ref):
@@ -252,9 +260,9 @@
         return pl.ds(first + step * rows, rows)
 
     def copies_in(step):
-        for i, (first, _) in enumerate(spans):
+        for i, (first, _, column, columns) in enumerate(spans):
             yield pltpu.make_async_copy(
-                sources[i].at[0, rows_of(i, step, first)],
+                sources[i].at[0, rows_of(i, step, first), pl.ds(column, columns)],
                 wide[i].at[rows_of(i, step)],
                 arrived.at[step, i],
             )
@@ -281,7 +289,7 @@
 
 
 def cast_rows(arrays, spans):
-    shapes = [(count, x.shape[2]) for x, (_, count) in zip(arrays, spans)]
+    shapes = [(rows, columns) for _, rows, _, columns in spans]
     return pl.pallas_call(
         lambda *refs: cast_kernel(spans, *refs),
         out_shape=[jax.ShapeDtypeStruct(shape, jnp.bfloat16) for shape in shapes],
@@ -380,43 +388,47 @@
     )(*rows, *weights)
 
 
-def down_kernel(firsts, hidden_ref, gate_ref, w0, w1, w2, w3, *refs):
-    out_ref, left_ref, right_ref, weights, arrived = refs
-    depth, width = w0.shape[0], weights.shape[1]
-    copies = [
-        pltpu.make_async_copy(
-            ref.at[:, pl.ds(first, width)], weights.at[pl.ds(d * depth, depth)], arrived.at[d]
+def down_kernel(column, hidden_ref, gate_ref, *refs):
+    pieces, (out_ref, left_ref, right_ref, weights, arrived) = refs[:-5], refs[-5:]
+    copies, first = [], 0
+    for i, ref in enumerate(pieces):
+        depth = ref.shape[0]
+        copies.append(
+            pltpu.make_async_copy(
+                ref.at[:, pl.ds(column, weights.shape[1])],
+                weights.at[pl.ds(first, depth)],
+                arrived.at[i],
+            )
         )
-        for d, (ref, first) in enumerate(zip((w0, w1, w2, w3), firsts))
-    ]
+        first += depth
     for copy in copies:
         copy.start()
     for copy in copies:
         copy.wait()
     total = jnp.dot(hidden_ref[...], weights[...], preferred_element_type=jnp.float32)
     weighted = (total * gate_ref[...]).astype(jnp.bfloat16)
-    sources, rows, _ = out_ref.shape
+    sources, rows, width = out_ref.shape
     out_ref[...] = weighted.reshape(sources, rows, width)
     middle, half = sources // 2 * rows, rows // 2
     left_ref[...] = weighted[middle : middle + half]
     right_ref[...] = weighted[middle + half : middle + rows]
 
 
-def expert_down(hidden_units, gates, weights, firsts, width, sources):
+def expert_down(hidden_units, gates, weights, column, width, sources):
     tokens, hidden_size = hidden_units.shape
     rows = tokens // sources
     return pl.pallas_call(
-        lambda *refs: down_kernel(firsts, *refs),
+        lambda *refs: down_kernel(column, *refs),
         out_shape=[
             jax.ShapeDtypeStruct((sources, rows, width), jnp.bfloat16),
             jax.ShapeDtypeStruct((rows // 2, width), jnp.bfloat16),
             jax.ShapeDtypeStruct((rows // 2, width), jnp.bfloat16),
         ],
-        in_specs=vmem(2) + [pl.BlockSpec(memory_space=pl.ANY)] * 4,
+        in_specs=vmem(2) + [pl.BlockSpec(memory_space=pl.ANY)] * len(weights),
         out_specs=vmem(3),
         scratch_shapes=[
             pltpu.VMEM((hidden_size, width), jnp.bfloat16),
-            pltpu.SemaphoreType.DMA((4,)),
+            pltpu.SemaphoreType.DMA((len(weights),)),
         ],
         compiler_params=params(),
         cost_estimate=SMALL,
@@ -457,30 +469,21 @@
     return above + far + below[:0:-1], list(zip(above[1:], below[1:])) + [tuple(far)]
 
 
-def scatter_sums(parts):
-    sources, rows, _ = parts[0][0].shape
+def scatter_sum(weighted, left, right):
+    sources, rows, _ = weighted.shape
     half = rows // 2
     reach = sources // 2
-    moving = [(left, right) for _, left, right in parts]
-    for step in range(reach):
-        previous = None
-        for i, (weighted, _, _) in enumerate(parts):
-            up, down = moving[i]
-            if step:
-                up, down = lax.optimization_barrier((up, down))
-                away = reach - step
-                if step == 1:
-                    up = jnp.concatenate([add(weighted[away, :half], up), weighted[away, half:]])
-                    down = jnp.concatenate(
-                        [weighted[-away, :half], add(weighted[-away, half:], down)]
-                    )
-                else:
-                    up, down = add(weighted[away], up), add(weighted[-away], down)
-            if previous is not None:
-                up, down = after(up, *previous), after(down, *previous)
-            previous = moving[i] if step else None
-            moving[i] = around(up, 1), around(down, -1)
-    return [(weighted[0], *ends) for (weighted, _, _), ends in zip(parts, moving)]
+    up, down = around(left, 1), around(right, -1)
+    up = jnp.concatenate([add(weighted[reach - 1, :half], up), weighted[reach - 1, half:]])
+    down = jnp.concatenate([weighted[reach + 1, :half], add(weighted[reach + 1, half:], down)])
+    for away in range(reach - 2, 0, -1):
+        up = add(weighted[away], around(up, 1))
+        down = add(weighted[sources - away], around(down, -1))
+    return weighted[0], around(up, 1), around(down, -1)
+
+
+def relayed(x, rows):
+    return [partner(x[i : i + rows], 1) for i in range(0, x.shape[0], rows)]
 
 
 def every_expert(
@@ -498,26 +501,22 @@
 ):
     expert_count = lax.axis_size("expert")
     width = trainer_down.shape[2]
-    depth = trainer_gate_up.shape[1]
-    early = depth // 4
-    late = depth - early
-    (first_own,) = cast_rows([trainer_gate_up], [(0, early)])
+    depth, columns = trainer_gate_up.shape[1:]
+    down_depth = trainer_down.shape[1]
+    early = depth // 8
+    slab = width // SLABS
+    *attn, first_own = attention(
+        queries, key_pool, value_pool, page_table, prompt_lengths, trainer_gate_up, early
+    )
     first_across = partner(first_own, 2)
-    attn = attention(
-        after(queries, first_own), key_pool, value_pool, page_table, prompt_lengths
-    )
     rest_own, down_own = cast_rows(
         [after(trainer_gate_up, attn[0]), trainer_down],
-        [(early, late), (0, trainer_down.shape[1])],
+        [(early, depth - early, 0, columns), (0, down_depth, 0, width)],
     )
     attn = [attn[0]] + [partner(attn[d], d) for d in (1, 2, 3)]
-    rest_across = partner(after(rest_own, *attn), 2)
+    rest_across = partner(after(rest_own, first_across, *attn), 2)
     resid, rows = norm(
-        after(hidden_in[0], rest_own, first_across),
-        attn,
-        norm_gain,
-        expert_ids[0],
-        gate_weights[0],
+        after(hidden_in[0], rest_own), attn, norm_gain, expert_ids[0], gate_weights[0]
     )
     gathered, arrived = gather_rows(rows)
     first_beside = partner(after(first_own, *arrived[0]), 1)
@@ -525,25 +524,19 @@
     rest_beside = partner(after(rest_own, *arrived[0]), 1)
     down_beside = partner(after(down_own, *arrived[1]), 1)
     down_across = partner(after(down_own, *arrived[2]), 2)
-    ready = after(rest_across, *arrived[3])
-    rest_opposite = [partner(ready[i : i + early], 1) for i in range(0, late, early)]
+    rest_opposite = relayed(after(rest_across, *arrived[3]), early)
     hidden_units, gates = expert_up(
         gathered,
         [first_own, rest_own, first_beside, rest_beside]
         + [first_across, rest_across, first_opposite, *rest_opposite],
     )
-    down_opposite = partner(after(down_across, hidden_units), 1)
-    weights = (down_own, down_beside, down_across, down_opposite)
-    slab = width // SLABS
-    starts = range(0, width, slab)
-    weighted = [
-        expert_down(hidden_units, gates, weights, (first,) * 4, slab, expert_count)
-        for first in starts
-    ]
+    down_opposite = relayed(after(down_across, hidden_units), down_depth // 2)
+    weights = [down_own, down_beside, down_across, *down_opposite]
     mixed = []
-    for first, terms in zip(starts, scatter_sums(weighted)):
+    for first in range(0, width, slab):
+        weighted = expert_down(hidden_units, gates, weights, first, slab, expert_count)
         total = resid[:, first : first + slab].astype(jnp.float32)
-        for term in terms:
+        for term in scatter_sum(*weighted):
             total = total + term.astype(jnp.float32)
         mixed.append(total.astype(jnp.bfloat16))
     return jnp.concatenate(mixed, axis=1)[None]

time: 156 us -> 119 us (0.76)
  waiting for transfers between devices: 101 us -> 63.2 us
  starting transfers between devices: 32.4 us -> 34.2 us
    ppermute x14 -> x19, waiting for transfers between devices: 62.2 us -> 22.9 us  [partner(): return lax.ppermute(x, 'dp', [(i, i ^ distance) for i in range(4)])]
    ppermute x14 -> x19, starting transfers between devices: 7.47 us -> 9.27 us  [partner(): return lax.ppermute(x, 'dp', [(i, i ^ distance) for i in range(4)])]
    pallas_call x2 -> x1, Pallas kernels: 5.94 us -> 4.25 us  [cast_rows(): pl.pallas_call(lambda *refs: cast_kernel(spans, *refs), out_shape=[jax.Sh...]
  transfers between devices with their start and end apart: 38 -> 43, of which waited for: 27 -> 29; matrix products, arithmetic and copies ran while one was open for 0% -> 1% of each run, Pallas kernels for 9% -> 12%
where the time goes in v7:
time: 119 us
  waiting for transfers between devices  63.2 us (53%)
  starting transfers between devices  34.2 us (29%)
  Pallas kernels  19.2 us (16%)
  other arithmetic  1.27 us (1%)
    ppermute x24, waiting for transfers between devices, around(): lax.ppermute(x, 'expert', [(ring[i], ring[(i + step) % count]) for i in r...  40.3 us
    ppermute x24, starting transfers between devices, around(): lax.ppermute(x, 'expert', [(ring[i], ring[(i + step) % count]) for i in r...  24.9 us
    ppermute x19, waiting for transfers between devices, partner(): return lax.ppermute(x, 'dp', [(i, i ^ distance) for i in range(4)])  22.9 us
    ppermute x19, starting transfers between devices, partner(): return lax.ppermute(x, 'dp', [(i, i ^ distance) for i in range(4)])  9.27 us
    pallas_call x1, Pallas kernels, expert_up(): pl.pallas_call(lambda *refs: up_kernel(len(rows), len(weights), *refs), o...  8.49 us
    pallas_call x1, Pallas kernels, cast_rows(): pl.pallas_call(lambda *refs: cast_kernel(spans, *refs), out_shape=[jax.Sh...  4.25 us
    pallas_call x1, Pallas kernels, attention(): pl.pallas_call(attention_kernel, out_shape=[jax.ShapeDtypeStruct((tokens...  3.11 us
    pallas_call x2, Pallas kernels, expert_down(): pl.pallas_call(lambda *refs: down_kernel(column, *refs), out_shape=[jax.S...  2.97 us
  transfers between devices with their start and end apart: 43, of which 29 were waited for; matrix products, arithmetic and copies ran while one was open for 1% of the time, Pallas kernels for 12%

profile of v7, /device:TPU:0, one launch (start us, length us, event | category | flops | bytes accessed | tf_op | source)
XLA Modules:
  0.0 118.6 jit_solution(9781173389751985945)
XLA Ops:
  0.0 3.1 %attention.1 = (bf16[64,512]{1,0:T(8,128)(2,1)}, bf16[64,512]{1,0:T(8,128)(2,1)}, bf16[64,512]{1,0:T(8,128)(2,1)}, bf16[64,512]{1,0:T(8,128)(2,1)}, bf16[64,2048]{1,0:T(8,128)(2,1)}) custom-call(s32[1,2]{1,0:T(1,128)} %refs_0_.1, s32[1,4]{1,0:T(1,128)} %refs_1_.2, bf16[1,256,512]{2,1,0:T(8,128)(2,1)} %refs_2_.1, bf16[2,128,512]{2,1,0:T(8,128)(2,1)} %refs_3_.1, ...), custom_call_target="tpu_custom_call" | custom-call | tf_op jit(solution)/shard_map/attention/pallas_call | solution.py:185
  3.1 3.0 %collective-permute-start.13 = (bf16[64,2048]{1,0:T(8,128)(2,1)}, bf16[64,2048]{1,0:T(8,128)(2,1)S(1)}, u32[]{:S(2)}, u32[]{:S(2)}) collective-permute-start(bf16[64,2048]{1,0:T(8,128)(2,1)} %get-tuple-element.42.refs_9_), channel_id=1, source_target_pairs={{0,16},{8,24},{16,0},{24,8},{1,17},{9,25},{17,1},{25,9},{2,18},{10... | collective-permute-start | bytes 786440 | tf_op jit(solution)/shard_map/ppermute | solution.py:440
  6.3 1.7 %collective-permute-start.2 = (bf16[64,512]{1,0:T(8,128)(2,1)}, bf16[64,512]{1,0:T(8,128)(2,1)S(1)}, u32[]{:S(2)}, u32[]{:S(2)}) collective-permute-start(bf16[64,512]{1,0:T(8,128)(2,1)} %get-tuple-element.38), channel_id=1, source_target_pairs={{0,24},{8,16},{16,8},{24,0},{1,25},{9,17},{17,9},{25,1},{2,26},{10... | collective-permute-start | bytes 196616 | tf_op jit(solution)/shard_map/ppermute | solution.py:440
  8.0 4.2 %cast_rows.1 = (bf16[448,2048]{1,0:T(8,128)(2,1)}, bf16[256,2048]{1,0:T(8,128)(2,1)}) custom-call(f32[1,512,2048]{2,1,0:T(8,128)} %refs_0_.2, f32[1,256,2048]{2,1,0:T(8,128)} %refs_1_.3), custom_call_target="tpu_custom_call" | custom-call | tf_op jit(solution)/shard_map/cast_rows/pallas_call | solution.py:293
  12.3 2.5 %collective-permute-done.1.a2 = bf16[64,512]{1,0:T(8,128)(2,1)S(1)} collective-permute-done((bf16[64,512]{1,0:T(8,128)(2,1)}, bf16[64,512]{1,0:T(8,128)(2,1)S(1)}, u32[]{:S(2)}, u32[]{:S(2)}) %collective-permute-start.1) | collective-permute-done | bytes 65568 | tf_op jit(solution)/shard_map/ppermute | solution.py:440
  14.8 1.7 %collective-permute-start.14 = (bf16[448,2048]{1,0:T(8,128)(2,1)}, bf16[448,2048]{1,0:T(8,128)(2,1)S(1)}, u32[]{:S(2)}, u32[]{:S(2)}) collective-permute-start(bf16[448,2048]{1,0:T(8,128)(2,1)} %get-tuple-element.44.refs_10_), channel_id=1, source_target_pairs={{0,16},{8,24},{16,0},{24,8},{1,17},{9,25},{17,1},{25,9},{2,18},{10... | collective-permute-start | bytes 5505032 | tf_op jit(solution)/shard_map/ppermute | solution.py:440
  17.1 1.6 %collective-permute-start.7 = (bf16[64,2176]{1,0:T(8,128)(2,1)S(1)}, bf16[64,2176]{1,0:T(8,128)(2,1)S(1)}, u32[]{:S(2)}, u32[]{:S(2)}) collective-permute-start(bf16[64,2176]{1,0:T(8,128)(2,1)S(1)} %get-tuple-element.40.refs_0_), channel_id=1, source_target_pairs={{0,2},{2,4},{4,6},{6,7},{7,5},{5,3},{3,1},{1,0},{8,10},{10,12},{12... | collective-permute-start | bytes 835592 | tf_op jit(solution)/shard_map/ppermute | solution.py:450
  19.2 6.8 %collective-permute-done.7.refs_8_ = bf16[64,2176]{1,0:T(8,128)(2,1)S(1)} collective-permute-done((bf16[64,2176]{1,0:T(8,128)(2,1)S(1)}, bf16[64,2176]{1,0:T(8,128)(2,1)S(1)}, u32[]{:S(2)}, u32[]{:S(2)}) %collective-permute-start.7) | collective-permute-done | bytes 278560 | tf_op jit(solution)/shard_map/ppermute | solution.py:450
  27.2 1.6 %collective-permute-start.8 = (bf16[64,2176]{1,0:T(8,128)(2,1)S(1)}, bf16[64,2176]{1,0:T(8,128)(2,1)S(1)}, u32[]{:S(2)}, u32[]{:S(2)}) collective-permute-start(bf16[64,2176]{1,0:T(8,128)(2,1)S(1)} %collective-permute-done.7.refs_8_), channel_id=1, source_target_pairs={{0,2},{2,4},{4,6},{6,7},{7,5},{5,3},{3,1},{1,0},{8,10},{10,12},{12... | collective-permute-start | bytes 835592 | tf_op jit(solution)/shard_map/ppermute | solution.py:450
  29.3 7.0 %collective-permute-done.8.refs_7_ = bf16[64,2176]{1,0:T(8,128)(2,1)S(1)} collective-permute-done((bf16[64,2176]{1,0:T(8,128)(2,1)S(1)}, bf16[64,2176]{1,0:T(8,128)(2,1)S(1)}, u32[]{:S(2)}, u32[]{:S(2)}) %collective-permute-start.8) | collective-permute-done | bytes 278560 | tf_op jit(solution)/shard_map/ppermute | solution.py:450
  36.3 1.6 %collective-permute-start.9 = (bf16[64,2176]{1,0:T(8,128)(2,1)S(1)}, bf16[64,2176]{1,0:T(8,128)(2,1)S(1)}, u32[]{:S(2)}, u32[]{:S(2)}) collective-permute-start(bf16[64,2176]{1,0:T(8,128)(2,1)S(1)} %collective-permute-done.8.refs_7_), channel_id=1, source_target_pairs={{0,2},{2,4},{4,6},{6,7},{7,5},{5,3},{3,1},{1,0},{8,10},{10,12},{12... | collective-permute-start | bytes 835592 | tf_op jit(solution)/shard_map/ppermute | solution.py:450
  38.3 6.3 %collective-permute-done.9.refs_6_ = bf16[64,2176]{1,0:T(8,128)(2,1)S(1)} collective-permute-done((bf16[64,2176]{1,0:T(8,128)(2,1)S(1)}, bf16[64,2176]{1,0:T(8,128)(2,1)S(1)}, u32[]{:S(2)}, u32[]{:S(2)}) %collective-permute-start.9) | collective-permute-done | bytes 278560 | tf_op jit(solution)/shard_map/ppermute | solution.py:450
  44.6 1.6 %collective-permute-start.10 = (bf16[32,2176]{1,0:T(8,128)(2,1)S(1)}, bf16[32,2176]{1,0:T(8,128)(2,1)S(1)}, u32[]{:S(2)}, u32[]{:S(2)}) collective-permute-start(bf16[32,2176]{1,0:T(8,128)(2,1)S(1)} %slice.125), channel_id=1, source_target_pairs={{0,2},{2,4},{4,6},{6,7},{7,5},{5,3},{3,1},{1,0},{8,10},{10,12},{12... | collective-permute-start | bytes 417800 | tf_op jit(solution)/shard_map/ppermute | solution.py:450
  47.3 2.4 %collective-permute-done.10.refs_5_ = bf16[32,2176]{1,0:T(8,128)(2,1)S(1)} collective-permute-done((bf16[32,2176]{1,0:T(8,128)(2,1)S(1)}, bf16[32,2176]{1,0:T(8,128)(2,1)S(1)}, u32[]{:S(2)}, u32[]{:S(2)}) %collective-permute-start.10) | collective-permute-done | bytes 139296 | tf_op jit(solution)/shard_map/ppermute | solution.py:450
  49.7 1.6 %collective-permute-done.6.refs_4_ = bf16[32,2176]{1,0:T(8,128)(2,1)S(1)} collective-permute-done((bf16[32,2176]{1,0:T(8,128)(2,1)S(1)}, bf16[32,2176]{1,0:T(8,128)(2,1)S(1)}, u32[]{:S(2)}, u32[]{:S(2)}) %collective-permute-start.6) | collective-permute-done | bytes 139296 | tf_op jit(solution)/shard_map/ppermute | solution.py:450
  51.4 6.5 %collective-permute-done.14.refs_14_ = bf16[448,2048]{1,0:T(8,128)(2,1)S(1)} collective-permute-done((bf16[448,2048]{1,0:T(8,128)(2,1)}, bf16[448,2048]{1,0:T(8,128)(2,1)S(1)}, u32[]{:S(2)}, u32[]{:S(2)}) %collective-permute-start.14) | collective-permute-done | bytes 1835040 | tf_op jit(solution)/shard_map/ppermute | solution.py:440
  61.9 8.5 %expert_up.1 = (bf16[512,1024]{1,0:T(8,128)(2,1)S(1)}, f32[512,1]{1,0:T(8,128)S(1)}) custom-call(bf16[64,2176]{1,0:T(8,128)(2,1)S(1)} %get-tuple-element.40.refs_0_, bf16[64,2176]{1,0:T(8,128)(2,1)S(1)} %collective-permute-done.3.refs_1_, bf16[64,2176]{1,0:T(8,128)(2,1)S(1)} %collective-permute-done.4.refs_2_, ...), custom_call_target="tpu_custom_call" | custom-call | flops 1 | bytes 1 | tf_op jit(solution)/shard_map/expert_up/pallas_call | solution.py:371
  70.4 9.5 %collective-permute-done.24.refs_4_ = bf16[256,2048]{1,0:T(8,128)(2,1)S(1)} collective-permute-done((bf16[256,2048]{1,0:T(8,128)(2,1)}, bf16[256,2048]{1,0:T(8,128)(2,1)S(1)}, u32[]{:S(2)}, u32[]{:S(2)}) %collective-permute-start.24) | collective-permute-done | bytes 1048608 | tf_op jit(solution)/shard_map/ppermute | solution.py:440
  80.6 1.4 %collective-permute-done.25.refs_5_ = bf16[128,2048]{1,0:T(8,128)(2,1)S(1)} collective-permute-done((bf16[128,2048]{1,0:T(8,128)(2,1)S(1)}, bf16[128,2048]{1,0:T(8,128)(2,1)S(1)}, u32[]{:S(2)}, u32[]{:S(2)}) %collective-permute-start.25) | collective-permute-done | bytes 524320 | tf_op jit(solution)/shard_map/ppermute | solution.py:440
  82.7 1.5 %expert_down.3 = (bf16[8,64,1024]{2,1,0:T(8,128)(2,1)S(1)}, bf16[32,1024]{1,0:T(8,128)(2,1)S(1)}, bf16[32,1024]{1,0:T(8,128)(2,1)S(1)}) custom-call(bf16[512,1024]{1,0:T(8,128)(2,1)S(1)} %get-tuple-element.47.refs_0_, f32[512,1]{1,0:T(8,128)S(1)} %get-tuple-element.48.refs_1_, bf16[256,2048]{1,0:T(8,128)(2,1)S(1)} %copy-done, ...), custom_call_target="tpu_custom_call" | custom-call | flops 1 | bytes 1 | tf_op jit(solution)/shard_map/expert_down/pallas_call | solution.py:420
  84.2 1.9 %collective-permute-start.35 = (bf16[32,1024]{1,0:T(8,128)(2,1)S(1)}, bf16[32,1024]{1,0:T(8,128)(2,1)S(1)}, u32[]{:S(2)}, u32[]{:S(2)}) collective-permute-start(bf16[32,1024]{1,0:T(8,128)(2,1)S(1)} %get-tuple-element.57), channel_id=1, source_target_pairs={{0,2},{2,4},{4,6},{6,7},{7,5},{5,3},{3,1},{1,0},{8,10},{10,12},{12... | collective-permute-start | bytes 196616 | tf_op jit(solution)/shard_map/ppermute | solution.py:450
  86.3 1.5 %expert_down.2 = (bf16[8,64,1024]{2,1,0:T(8,128)(2,1)S(1)}, bf16[32,1024]{1,0:T(8,128)(2,1)S(1)}, bf16[32,1024]{1,0:T(8,128)(2,1)S(1)}) custom-call(bf16[512,1024]{1,0:T(8,128)(2,1)S(1)} %get-tuple-element.47.refs_0_, f32[512,1]{1,0:T(8,128)S(1)} %get-tuple-element.48.refs_1_, bf16[256,2048]{1,0:T(8,128)(2,1)S(1)} %copy-done, ...), custom_call_target="tpu_custom_call" | custom-call | flops 1 | bytes 1 | tf_op jit(solution)/shard_map/expert_down/pallas_call | solution.py:420
  87.8 1.9 %collective-permute-start.27 = (bf16[32,1024]{1,0:T(8,128)(2,1)S(1)}, bf16[32,1024]{1,0:T(8,128)(2,1)S(1)}, u32[]{:S(2)}, u32[]{:S(2)}) collective-permute-start(bf16[32,1024]{1,0:T(8,128)(2,1)S(1)} %get-tuple-element.54), channel_id=1, source_target_pairs={{0,2},{2,4},{4,6},{6,7},{7,5},{5,3},{3,1},{1,0},{8,10},{10,12},{12... | collective-permute-start | bytes 196616 | tf_op jit(solution)/shard_map/ppermute | solution.py:450
  92.5 1.8 %collective-permute-done.31 = bf16[32,1024]{1,0:T(8,128)(2,1)S(1)} collective-permute-done((bf16[32,1024]{1,0:T(8,128)(2,1)S(1)}, bf16[32,1024]{1,0:T(8,128)(2,1)S(1)}, u32[]{:S(2)}, u32[]{:S(2)}) %collective-permute-start.31) | collective-permute-done | bytes 65568 | tf_op jit(solution)/shard_map/ppermute | solution.py:450
  94.9 1.6 %collective-permute-start.28 = (bf16[64,1024]{1,0:T(8,128)(2,1)S(1)}, bf16[64,1024]{1,0:T(8,128)(2,1)S(1)}, u32[]{:S(2)}, u32[]{:S(2)}) collective-permute-start(bf16[64,1024]{1,0:T(8,128)(2,1)S(1)} %pad_maximum_fusion), channel_id=1, source_target_pairs={{0,2},{2,4},{4,6},{6,7},{7,5},{5,3},{3,1},{1,0},{8,10},{10,12},{12... | collective-permute-start | bytes 393224 | tf_op jit(solution)/shard_map/ppermute | solution.py:450
  96.6 1.6 %collective-permute-done.36 = bf16[64,1024]{1,0:T(8,128)(2,1)S(1)} collective-permute-done((bf16[64,1024]{1,0:T(8,128)(2,1)S(1)}, bf16[64,1024]{1,0:T(8,128)(2,1)S(1)}, u32[]{:S(2)}, u32[]{:S(2)}) %collective-permute-start.36) | collective-permute-done | bytes 131104 | tf_op jit(solution)/shard_map/ppermute | solution.py:450
  98.4 2.5 %collective-permute-done.28 = bf16[64,1024]{1,0:T(8,128)(2,1)S(1)} collective-permute-done((bf16[64,1024]{1,0:T(8,128)(2,1)S(1)}, bf16[64,1024]{1,0:T(8,128)(2,1)S(1)}, u32[]{:S(2)}, u32[]{:S(2)}) %collective-permute-start.28) | collective-permute-done | bytes 131104 | tf_op jit(solution)/shard_map/ppermute | solution.py:450
  102.0 1.4 %collective-permute-done.37 = bf16[64,1024]{1,0:T(8,128)(2,1)S(1)} collective-permute-done((bf16[64,1024]{1,0:T(8,128)(2,1)S(1)}, bf16[64,1024]{1,0:T(8,128)(2,1)S(1)}, u32[]{:S(2)}, u32[]{:S(2)}) %collective-permute-start.37) | collective-permute-done | bytes 131104 | tf_op jit(solution)/shard_map/ppermute | solution.py:450
  103.5 1.6 %collective-permute-start.41 = (bf16[64,1024]{1,0:T(8,128)(2,1)S(1)}, bf16[64,1024]{1,0:T(8,128)(2,1)S(1)}, u32[]{:S(2)}, u32[]{:S(2)}) collective-permute-start(bf16[64,1024]{1,0:T(8,128)(2,1)S(1)} %get-tuple-element.73), channel_id=1, source_target_pairs={{0,1},{2,0},{4,2},{6,4},{7,6},{5,7},{3,5},{1,3},{8,9},{10,8},{12,1... | collective-permute-start | bytes 393224 | tf_op jit(solution)/shard_map/ppermute | solution.py:450
  106.8 1.6 %collective-permute-start.33 = (bf16[64,1024]{1,0:T(8,128)(2,1)S(1)}, bf16[64,1024]{1,0:T(8,128)(2,1)S(1)}, u32[]{:S(2)}, u32[]{:S(2)}) collective-permute-start(bf16[64,1024]{1,0:T(8,128)(2,1)S(1)} %get-tuple-element.67), channel_id=1, source_target_pairs={{0,1},{2,0},{4,2},{6,4},{7,6},{5,7},{3,5},{1,3},{8,9},{10,8},{12,1... | collective-permute-start | bytes 393224 | tf_op jit(solution)/shard_map/ppermute | solution.py:450
  109.8 1.4 %collective-permute-start.42 = (bf16[64,1024]{1,0:T(8,128)(2,1)S(1)}, bf16[64,1024]{1,0:T(8,128)(2,1)S(1)}, u32[]{:S(2)}, u32[]{:S(2)}) collective-permute-start(bf16[64,1024]{1,0:T(8,128)(2,1)S(1)} %fusion.1), channel_id=1, source_target_pairs={{0,1},{2,0},{4,2},{6,4},{7,6},{5,7},{3,5},{1,3},{8,9},{10,8},{12,1... | collective-permute-start | bytes 393224 | tf_op jit(solution)/shard_map/ppermute | solution.py:450
  114.8 2.8 %collective-permute-done.34 = bf16[64,1024]{1,0:T(8,128)(2,1)S(1)} collective-permute-done((bf16[64,1024]{1,0:T(8,128)(2,1)S(1)}, bf16[64,1024]{1,0:T(8,128)(2,1)S(1)}, u32[]{:S(2)}, u32[]{:S(2)}) %collective-permute-start.34) | collective-permute-done | bytes 131104 | tf_op jit(solution)/shard_map/ppermute | solution.py:450
  (98 shorter events, 22.6 us)
Async XLA Ops:
  3.1 11.7 %collective-permute-start.13 = (bf16[64,2048]{1,0:T(8,128)(2,1)}, bf16[64,2048]{1,0:T(8,128)(2,1)S(1)}, u32[]{:S(2)}, u32[]{:S(2)}) collective-permute-start(bf16[64,2048]{1,0:T(8,128)(2,1)} %get-tuple-element.42.refs_9_), channel_id=1, source_target_pairs={{0,16},{8,24},{16,0},{24,8},{1,17},{9,25},{17,1},{25,9},{2,18},{10... | collective-permute-start | bytes 786440 | tf_op jit(solution)/shard_map/ppermute | solution.py:440
  6.1 6.2 %collective-permute-start = (bf16[64,512]{1,0:T(8,128)(2,1)}, bf16[64,512]{1,0:T(8,128)(2,1)S(1)}, u32[]{:S(2)}, u32[]{:S(2)}) collective-permute-start(bf16[64,512]{1,0:T(8,128)(2,1)} %get-tuple-element.36), channel_id=1, source_target_pairs={{0,8},{8,0},{16,24},{24,16},{1,9},{9,1},{17,25},{25,17},{2,10},{10... | collective-permute-start | bytes 196616 | tf_op jit(solution)/shard_map/ppermute | solution.py:440
  6.1 8.6 %collective-permute-start.1 = (bf16[64,512]{1,0:T(8,128)(2,1)}, bf16[64,512]{1,0:T(8,128)(2,1)S(1)}, u32[]{:S(2)}, u32[]{:S(2)}) collective-permute-start(bf16[64,512]{1,0:T(8,128)(2,1)} %get-tuple-element.37), channel_id=1, source_target_pairs={{0,16},{8,24},{16,0},{24,8},{1,17},{9,25},{17,1},{25,9},{2,18},{10... | collective-permute-start | bytes 196616 | tf_op jit(solution)/shard_map/ppermute | solution.py:440
  6.3 8.5 %collective-permute-start.2 = (bf16[64,512]{1,0:T(8,128)(2,1)}, bf16[64,512]{1,0:T(8,128)(2,1)S(1)}, u32[]{:S(2)}, u32[]{:S(2)}) collective-permute-start(bf16[64,512]{1,0:T(8,128)(2,1)} %get-tuple-element.38), channel_id=1, source_target_pairs={{0,24},{8,16},{16,8},{24,0},{1,25},{9,17},{17,9},{25,1},{2,26},{10... | collective-permute-start | bytes 196616 | tf_op jit(solution)/shard_map/ppermute | solution.py:440
  14.8 43.0 %collective-permute-start.14 = (bf16[448,2048]{1,0:T(8,128)(2,1)}, bf16[448,2048]{1,0:T(8,128)(2,1)S(1)}, u32[]{:S(2)}, u32[]{:S(2)}) collective-permute-start(bf16[448,2048]{1,0:T(8,128)(2,1)} %get-tuple-element.44.refs_10_), channel_id=1, source_target_pairs={{0,16},{8,24},{16,0},{24,8},{1,17},{9,25},{17,1},{25,9},{2,18},{10... | collective-permute-start | bytes 5505032 | tf_op jit(solution)/shard_map/ppermute | solution.py:440
  17.1 8.9 %collective-permute-start.7 = (bf16[64,2176]{1,0:T(8,128)(2,1)S(1)}, bf16[64,2176]{1,0:T(8,128)(2,1)S(1)}, u32[]{:S(2)}, u32[]{:S(2)}) collective-permute-start(bf16[64,2176]{1,0:T(8,128)(2,1)S(1)} %get-tuple-element.40.refs_0_), channel_id=1, source_target_pairs={{0,2},{2,4},{4,6},{6,7},{7,5},{5,3},{3,1},{1,0},{8,10},{10,12},{12... | collective-permute-start | bytes 835592 | tf_op jit(solution)/shard_map/ppermute | solution.py:450
  18.7 8.5 %collective-permute-start.3 = (bf16[64,2176]{1,0:T(8,128)(2,1)S(1)}, bf16[64,2176]{1,0:T(8,128)(2,1)S(1)}, u32[]{:S(2)}, u32[]{:S(2)}) collective-permute-start(bf16[64,2176]{1,0:T(8,128)(2,1)S(1)} %get-tuple-element.40.refs_0_), channel_id=1, source_target_pairs={{0,1},{2,0},{4,2},{6,4},{7,6},{5,7},{3,5},{1,3},{8,9},{10,8},{12,1... | collective-permute-start | bytes 835592 | tf_op jit(solution)/shard_map/ppermute | solution.py:450
  27.2 31.4 %collective-permute-start.12 = (bf16[448,2048]{1,0:T(8,128)(2,1)}, bf16[448,2048]{1,0:T(8,128)(2,1)S(1)}, u32[]{:S(2)}, u32[]{:S(2)}) collective-permute-start(bf16[448,2048]{1,0:T(8,128)(2,1)} %get-tuple-element.44.refs_10_), channel_id=1, source_target_pairs={{0,8},{8,0},{16,24},{24,16},{1,9},{9,1},{17,25},{25,17},{2,10},{10... | collective-permute-start | bytes 5505032 | tf_op jit(solution)/shard_map/ppermute | solution.py:440
  27.2 9.1 %collective-permute-start.8 = (bf16[64,2176]{1,0:T(8,128)(2,1)S(1)}, bf16[64,2176]{1,0:T(8,128)(2,1)S(1)}, u32[]{:S(2)}, u32[]{:S(2)}) collective-permute-start(bf16[64,2176]{1,0:T(8,128)(2,1)S(1)} %collective-permute-done.7.refs_8_), channel_id=1, source_target_pairs={{0,2},{2,4},{4,6},{6,7},{7,5},{5,3},{3,1},{1,0},{8,10},{10,12},{12... | collective-permute-start | bytes 835592 | tf_op jit(solution)/shard_map/ppermute | solution.py:450
  28.8 9.1 %collective-permute-start.4 = (bf16[64,2176]{1,0:T(8,128)(2,1)S(1)}, bf16[64,2176]{1,0:T(8,128)(2,1)S(1)}, u32[]{:S(2)}, u32[]{:S(2)}) collective-permute-start(bf16[64,2176]{1,0:T(8,128)(2,1)S(1)} %collective-permute-done.3.refs_1_), channel_id=1, source_target_pairs={{0,1},{2,0},{4,2},{6,4},{7,6},{5,7},{3,5},{1,3},{8,9},{10,8},{12,1... | collective-permute-start | bytes 835592 | tf_op jit(solution)/shard_map/ppermute | solution.py:450
  36.3 8.3 %collective-permute-start.9 = (bf16[64,2176]{1,0:T(8,128)(2,1)S(1)}, bf16[64,2176]{1,0:T(8,128)(2,1)S(1)}, u32[]{:S(2)}, u32[]{:S(2)}) collective-permute-start(bf16[64,2176]{1,0:T(8,128)(2,1)S(1)} %collective-permute-done.8.refs_7_), channel_id=1, source_target_pairs={{0,2},{2,4},{4,6},{6,7},{7,5},{5,3},{3,1},{1,0},{8,10},{10,12},{12... | collective-permute-start | bytes 835592 | tf_op jit(solution)/shard_map/ppermute | solution.py:450
  37.9 8.4 %collective-permute-start.5 = (bf16[64,2176]{1,0:T(8,128)(2,1)S(1)}, bf16[64,2176]{1,0:T(8,128)(2,1)S(1)}, u32[]{:S(2)}, u32[]{:S(2)}) collective-permute-start(bf16[64,2176]{1,0:T(8,128)(2,1)S(1)} %collective-permute-done.4.refs_2_), channel_id=1, source_target_pairs={{0,1},{2,0},{4,2},{6,4},{7,6},{5,7},{3,5},{1,3},{8,9},{10,8},{12,1... | collective-permute-start | bytes 835592 | tf_op jit(solution)/shard_map/ppermute | solution.py:450
  44.6 5.1 %collective-permute-start.10 = (bf16[32,2176]{1,0:T(8,128)(2,1)S(1)}, bf16[32,2176]{1,0:T(8,128)(2,1)S(1)}, u32[]{:S(2)}, u32[]{:S(2)}) collective-permute-start(bf16[32,2176]{1,0:T(8,128)(2,1)S(1)} %slice.125), channel_id=1, source_target_pairs={{0,2},{2,4},{4,6},{6,7},{7,5},{5,3},{3,1},{1,0},{8,10},{10,12},{12... | collective-permute-start | bytes 417800 | tf_op jit(solution)/shard_map/ppermute | solution.py:450
  46.3 5.1 %collective-permute-start.6 = (bf16[32,2176]{1,0:T(8,128)(2,1)S(1)}, bf16[32,2176]{1,0:T(8,128)(2,1)S(1)}, u32[]{:S(2)}, u32[]{:S(2)}) collective-permute-start(bf16[32,2176]{1,0:T(8,128)(2,1)S(1)} %slice.124), channel_id=1, source_target_pairs={{0,1},{2,0},{4,2},{6,4},{7,6},{5,7},{3,5},{1,3},{8,9},{10,8},{12,1... | collective-permute-start | bytes 417800 | tf_op jit(solution)/shard_map/ppermute | solution.py:450
  46.8 33.1 %collective-permute-start.24 = (bf16[256,2048]{1,0:T(8,128)(2,1)}, bf16[256,2048]{1,0:T(8,128)(2,1)S(1)}, u32[]{:S(2)}, u32[]{:S(2)}) collective-permute-start(bf16[256,2048]{1,0:T(8,128)(2,1)} %get-tuple-element.51.refs_2_), channel_id=1, source_target_pairs={{0,16},{8,24},{16,0},{24,8},{1,17},{9,25},{17,1},{25,9},{2,18},{10... | collective-permute-start | bytes 3145736 | tf_op jit(solution)/shard_map/ppermute | solution.py:440
  49.7 8.4 %collective-permute-start.15 = (bf16[64,2048]{1,0:T(8,128)(2,1)S(1)}, bf16[64,2048]{1,0:T(8,128)(2,1)S(1)}, u32[]{:S(2)}, u32[]{:S(2)}) collective-permute-start(bf16[64,2048]{1,0:T(8,128)(2,1)S(1)} %collective-permute-done.13.refs_13_), channel_id=1, source_target_pairs={{0,8},{8,0},{16,24},{24,16},{1,9},{9,1},{17,25},{25,17},{2,10},{10... | collective-permute-start | bytes 786440 | tf_op jit(solution)/shard_map/ppermute | solution.py:440
  51.4 7.2 %collective-permute-start.11 = (bf16[64,2048]{1,0:T(8,128)(2,1)S(1)}, bf16[64,2048]{1,0:T(8,128)(2,1)S(1)}, u32[]{:S(2)}, u32[]{:S(2)}) collective-permute-start(bf16[64,2048]{1,0:T(8,128)(2,1)S(1)} %copy-done.3), channel_id=1, source_target_pairs={{0,8},{8,0},{16,24},{24,16},{1,9},{9,1},{17,25},{25,17},{2,10},{10... | collective-permute-start | bytes 786440 | tf_op jit(solution)/shard_map/ppermute | solution.py:440
  60.7 19.8 %collective-permute-start.23 = (bf16[256,2048]{1,0:T(8,128)(2,1)S(1)}, bf16[256,2048]{1,0:T(8,128)(2,1)S(1)}, u32[]{:S(2)}, u32[]{:S(2)}) collective-permute-start(bf16[256,2048]{1,0:T(8,128)(2,1)S(1)} %copy-done), channel_id=1, source_target_pairs={{0,8},{8,0},{16,24},{24,16},{1,9},{9,1},{17,25},{25,17},{2,10},{10... | collective-permute-start | bytes 3145736 | tf_op jit(solution)/shard_map/ppermute | solution.py:440
  84.2 5.7 %collective-permute-start.35 = (bf16[32,1024]{1,0:T(8,128)(2,1)S(1)}, bf16[32,1024]{1,0:T(8,128)(2,1)S(1)}, u32[]{:S(2)}, u32[]{:S(2)}) collective-permute-start(bf16[32,1024]{1,0:T(8,128)(2,1)S(1)} %get-tuple-element.57), channel_id=1, source_target_pairs={{0,2},{2,4},{4,6},{6,7},{7,5},{5,3},{3,1},{1,0},{8,10},{10,12},{12... | collective-permute-start | bytes 196616 | tf_op jit(solution)/shard_map/ppermute | solution.py:450
  87.8 4.7 %collective-permute-start.27 = (bf16[32,1024]{1,0:T(8,128)(2,1)S(1)}, bf16[32,1024]{1,0:T(8,128)(2,1)S(1)}, u32[]{:S(2)}, u32[]{:S(2)}) collective-permute-start(bf16[32,1024]{1,0:T(8,128)(2,1)S(1)} %get-tuple-element.54), channel_id=1, source_target_pairs={{0,2},{2,4},{4,6},{6,7},{7,5},{5,3},{3,1},{1,0},{8,10},{10,12},{12... | collective-permute-start | bytes 196616 | tf_op jit(solution)/shard_map/ppermute | solution.py:450
  90.4 11.7 %collective-permute-start.40 = (bf16[64,1024]{1,0:T(8,128)(2,1)S(1)}, bf16[64,1024]{1,0:T(8,128)(2,1)S(1)}, u32[]{:S(2)}, u32[]{:S(2)}) collective-permute-start(bf16[64,1024]{1,0:T(8,128)(2,1)S(1)} %pad_maximum_fusion.3), channel_id=1, source_target_pairs={{0,1},{2,0},{4,2},{6,4},{7,6},{5,7},{3,5},{1,3},{8,9},{10,8},{12,1... | collective-permute-start | bytes 393224 | tf_op jit(solution)/shard_map/ppermute | solution.py:450
  91.8 6.3 %collective-permute-start.36 = (bf16[64,1024]{1,0:T(8,128)(2,1)S(1)}, bf16[64,1024]{1,0:T(8,128)(2,1)S(1)}, u32[]{:S(2)}, u32[]{:S(2)}) collective-permute-start(bf16[64,1024]{1,0:T(8,128)(2,1)S(1)} %pad_maximum_fusion.2), channel_id=1, source_target_pairs={{0,2},{2,4},{4,6},{6,7},{7,5},{5,3},{3,1},{1,0},{8,10},{10,12},{12... | collective-permute-start | bytes 393224 | tf_op jit(solution)/shard_map/ppermute | solution.py:450
  94.4 11.2 %collective-permute-start.32 = (bf16[64,1024]{1,0:T(8,128)(2,1)S(1)}, bf16[64,1024]{1,0:T(8,128)(2,1)S(1)}, u32[]{:S(2)}, u32[]{:S(2)}) collective-permute-start(bf16[64,1024]{1,0:T(8,128)(2,1)S(1)} %pad_maximum_fusion.1), channel_id=1, source_target_pairs={{0,1},{2,0},{4,2},{6,4},{7,6},{5,7},{3,5},{1,3},{8,9},{10,8},{12,1... | collective-permute-start | bytes 393224 | tf_op jit(solution)/shard_map/ppermute | solution.py:450
  94.9 5.9 %collective-permute-start.28 = (bf16[64,1024]{1,0:T(8,128)(2,1)S(1)}, bf16[64,1024]{1,0:T(8,128)(2,1)S(1)}, u32[]{:S(2)}, u32[]{:S(2)}) collective-permute-start(bf16[64,1024]{1,0:T(8,128)(2,1)S(1)} %pad_maximum_fusion), channel_id=1, source_target_pairs={{0,2},{2,4},{4,6},{6,7},{7,5},{5,3},{3,1},{1,0},{8,10},{10,12},{12... | collective-permute-start | bytes 393224 | tf_op jit(solution)/shard_map/ppermute | solution.py:450
  98.2 5.3 %collective-permute-start.37 = (bf16[64,1024]{1,0:T(8,128)(2,1)S(1)}, bf16[64,1024]{1,0:T(8,128)(2,1)S(1)}, u32[]{:S(2)}, u32[]{:S(2)}) collective-permute-start(bf16[64,1024]{1,0:T(8,128)(2,1)S(1)} %fusion.2), channel_id=1, source_target_pairs={{0,2},{2,4},{4,6},{6,7},{7,5},{5,3},{3,1},{1,0},{8,10},{10,12},{12... | collective-permute-start | bytes 393224 | tf_op jit(solution)/shard_map/ppermute | solution.py:450
  100.9 5.8 %collective-permute-start.29 = (bf16[64,1024]{1,0:T(8,128)(2,1)S(1)}, bf16[64,1024]{1,0:T(8,128)(2,1)S(1)}, u32[]{:S(2)}, u32[]{:S(2)}) collective-permute-start(bf16[64,1024]{1,0:T(8,128)(2,1)S(1)} %fusion.9), channel_id=1, source_target_pairs={{0,2},{2,4},{4,6},{6,7},{7,5},{5,3},{3,1},{1,0},{8,10},{10,12},{12... | collective-permute-start | bytes 393224 | tf_op jit(solution)/shard_map/ppermute | solution.py:450
  103.5 6.3 %collective-permute-start.41 = (bf16[64,1024]{1,0:T(8,128)(2,1)S(1)}, bf16[64,1024]{1,0:T(8,128)(2,1)S(1)}, u32[]{:S(2)}, u32[]{:S(2)}) collective-permute-start(bf16[64,1024]{1,0:T(8,128)(2,1)S(1)} %get-tuple-element.73), channel_id=1, source_target_pairs={{0,1},{2,0},{4,2},{6,4},{7,6},{5,7},{3,5},{1,3},{8,9},{10,8},{12,1... | collective-permute-start | bytes 393224 | tf_op jit(solution)/shard_map/ppermute | solution.py:450
  105.2 8.8 %collective-permute-start.38 = (bf16[64,1024]{1,0:T(8,128)(2,1)S(1)}, bf16[64,1024]{1,0:T(8,128)(2,1)S(1)}, u32[]{:S(2)}, u32[]{:S(2)}) collective-permute-start(bf16[64,1024]{1,0:T(8,128)(2,1)S(1)} %get-tuple-element.72), channel_id=1, source_target_pairs={{0,2},{2,4},{4,6},{6,7},{7,5},{5,3},{3,1},{1,0},{8,10},{10,12},{12... | collective-permute-start | bytes 393224 | tf_op jit(solution)/shard_map/ppermute | solution.py:450
  106.8 5.8 %collective-permute-start.33 = (bf16[64,1024]{1,0:T(8,128)(2,1)S(1)}, bf16[64,1024]{1,0:T(8,128)(2,1)S(1)}, u32[]{:S(2)}, u32[]{:S(2)}) collective-permute-start(bf16[64,1024]{1,0:T(8,128)(2,1)S(1)} %get-tuple-element.67), channel_id=1, source_target_pairs={{0,1},{2,0},{4,2},{6,4},{7,6},{5,7},{3,5},{1,3},{8,9},{10,8},{12,1... | collective-permute-start | bytes 393224 | tf_op jit(solution)/shard_map/ppermute | solution.py:450
  108.4 5.5 %collective-permute-start.30 = (bf16[64,1024]{1,0:T(8,128)(2,1)S(1)}, bf16[64,1024]{1,0:T(8,128)(2,1)S(1)}, u32[]{:S(2)}, u32[]{:S(2)}) collective-permute-start(bf16[64,1024]{1,0:T(8,128)(2,1)S(1)} %get-tuple-element.66), channel_id=1, source_target_pairs={{0,2},{2,4},{4,6},{6,7},{7,5},{5,3},{3,1},{1,0},{8,10},{10,12},{12... | collective-permute-start | bytes 393224 | tf_op jit(solution)/shard_map/ppermute | solution.py:450
  109.8 5.0 %collective-permute-start.42 = (bf16[64,1024]{1,0:T(8,128)(2,1)S(1)}, bf16[64,1024]{1,0:T(8,128)(2,1)S(1)}, u32[]{:S(2)}, u32[]{:S(2)}) collective-permute-start(bf16[64,1024]{1,0:T(8,128)(2,1)S(1)} %fusion.1), channel_id=1, source_target_pairs={{0,1},{2,0},{4,2},{6,4},{7,6},{5,7},{3,5},{1,3},{8,9},{10,8},{12,1... | collective-permute-start | bytes 393224 | tf_op jit(solution)/shard_map/ppermute | solution.py:450
  112.7 5.0 %collective-permute-start.34 = (bf16[64,1024]{1,0:T(8,128)(2,1)S(1)}, bf16[64,1024]{1,0:T(8,128)(2,1)S(1)}, u32[]{:S(2)}, u32[]{:S(2)}) collective-permute-start(bf16[64,1024]{1,0:T(8,128)(2,1)S(1)} %fusion.8), channel_id=1, source_target_pairs={{0,1},{2,0},{4,2},{6,4},{7,6},{5,7},{3,5},{1,3},{8,9},{10,8},{12,1... | collective-permute-start | bytes 393224 | tf_op jit(solution)/shard_map/ppermute | solution.py:450
  (19 other events, 141.2 us)

commit v8 on v7

--- a/solution.py
+++ b/solution.py
@@ -113,7 +113,7 @@
 VMEM_LIMIT = 32 * 2**20
 VMEM_MOST = 60 * 2**20
 CAST_STEPS = 4
-SLABS = 2
+FIRST_SLAB = 10
 SMALL = pl.CostEstimate(flops=1, bytes_accessed=1, transcendentals=0)
 
 
@@ -388,10 +388,10 @@
     )(*rows, *weights)
 
 
-def down_kernel(column, hidden_ref, gate_ref, *refs):
+def down_kernel(columns, hidden_ref, gate_ref, *refs):
     pieces, (out_ref, left_ref, right_ref, weights, arrived) = refs[:-5], refs[-5:]
     copies, first = [], 0
-    for i, ref in enumerate(pieces):
+    for i, (ref, column) in enumerate(zip(pieces, columns)):
         depth = ref.shape[0]
         copies.append(
             pltpu.make_async_copy(
@@ -414,11 +414,12 @@
     right_ref[...] = weighted[middle + half : middle + rows]
 
 
-def expert_down(hidden_units, gates, weights, column, width, sources):
+def expert_down(hidden_units, gates, weights, width, sources):
+    weights, columns = zip(*weights)
     tokens, hidden_size = hidden_units.shape
     rows = tokens // sources
     return pl.pallas_call(
-        lambda *refs: down_kernel(column, *refs),
+        lambda *refs: down_kernel(columns, *refs),
         out_shape=[
             jax.ShapeDtypeStruct((sources, rows, width), jnp.bfloat16),
             jax.ShapeDtypeStruct((rows // 2, width), jnp.bfloat16),
@@ -503,15 +504,18 @@
     width = trainer_down.shape[2]
     depth, columns = trainer_gate_up.shape[1:]
     down_depth = trainer_down.shape[1]
-    early = depth // 8
-    slab = width // SLABS
+    early = depth // 4
+    piece = depth // 8
+    first_slab = width * FIRST_SLAB // 16
+    slabs = [(0, first_slab), (first_slab, width - first_slab)]
     *attn, first_own = attention(
         queries, key_pool, value_pool, page_table, prompt_lengths, trainer_gate_up, early
     )
     first_across = partner(first_own, 2)
-    rest_own, down_own = cast_rows(
-        [after(trainer_gate_up, attn[0]), trainer_down],
-        [(early, depth - early, 0, columns), (0, down_depth, 0, width)],
+    rest_own, down_own, *down_sent = cast_rows(
+        [after(trainer_gate_up, attn[0])] + [trainer_down] * 3,
+        [(early, depth - early, 0, columns)]
+        + [(0, down_depth, *slab) for slab in ((0, width), *slabs)],
     )
     attn = [attn[0]] + [partner(attn[d], d) for d in (1, 2, 3)]
     rest_across = partner(after(rest_own, first_across, *attn), 2)
@@ -523,19 +527,21 @@
     first_opposite = partner(after(first_across, *arrived[0]), 1)
     rest_beside = partner(after(rest_own, *arrived[0]), 1)
     down_beside = partner(after(down_own, *arrived[1]), 1)
-    down_across = partner(after(down_own, *arrived[2]), 2)
-    rest_opposite = relayed(after(rest_across, *arrived[3]), early)
+    down_across = [partner(after(slab, *arrived[2]), 2) for slab in down_sent]
+    rest_opposite = relayed(after(rest_across, *arrived[3]), piece)
     hidden_units, gates = expert_up(
         gathered,
         [first_own, rest_own, first_beside, rest_beside]
         + [first_across, rest_across, first_opposite, *rest_opposite],
     )
-    down_opposite = relayed(after(down_across, hidden_units), down_depth // 2)
-    weights = [down_own, down_beside, down_across, *down_opposite]
+    before = hidden_units
     mixed = []
-    for first in range(0, width, slab):
-        weighted = expert_down(hidden_units, gates, weights, first, slab, expert_count)
-        total = resid[:, first : first + slab].astype(jnp.float32)
+    for (first, wide), across in zip(slabs, down_across):
+        weights = [(down_own, first), (down_beside, first), (across, 0)]
+        weights += [(ref, 0) for ref in relayed(after(across, before), piece)]
+        weighted = expert_down(hidden_units, gates, weights, wide, expert_count)
+        before = weighted[1]
+        total = resid[:, first : first + wide].astype(jnp.float32)
         for term in scatter_sum(*weighted):
             total = total + term.astype(jnp.float32)
         mixed.append(total.astype(jnp.bfloat16))

time: 119 us -> 122 us (1.025)
  Pallas kernels: 19.2 us -> 21.3 us
  starting transfers between devices: 34.2 us -> 35.9 us
    ppermute x19 -> x25, waiting for transfers between devices: 22.9 us -> 18.6 us  [partner(): return lax.ppermute(x, 'dp', [(i, i ^ distance) for i in range(4)])]
    ppermute x24, waiting for transfers between devices: 40.3 us -> 43.7 us  [around(): lax.ppermute(x, 'expert', [(ring[i], ring[(i + step) % count]) for i in r...]
    ppermute x19 -> x25, starting transfers between devices: 9.27 us -> 11.2 us  [partner(): return lax.ppermute(x, 'dp', [(i, i ^ distance) for i in range(4)])]
    pallas_call x2, Pallas kernels: 2.97 us -> 4.58 us  [expert_down(): pl.pallas_call(lambda *refs: down_kernel(columns, *refs), out_shape=[jax....]
  transfers between devices with their start and end apart: 43 -> 49, of which waited for: 29 -> 27; matrix products, arithmetic and copies ran while one was open for 1% -> 1% of each run, Pallas kernels for 12% -> 15%
where the time goes in v8:
time: 122 us; the launch traced here: 121 us
  waiting for transfers between devices  62.3 us (51%)
  starting transfers between devices  35.9 us (29%)
  Pallas kernels  21.3 us (17%)
  other arithmetic  1.22 us (1%)
    ppermute x24, waiting for transfers between devices, around(): lax.ppermute(x, 'expert', [(ring[i], ring[(i + step) % count]) for i in r...  43.7 us
    ppermute x24, starting transfers between devices, around(): lax.ppermute(x, 'expert', [(ring[i], ring[(i + step) % count]) for i in r...  24.7 us
    ppermute x25, waiting for transfers between devices, partner(): return lax.ppermute(x, 'dp', [(i, i ^ distance) for i in range(4)])  18.6 us
    ppermute x25, starting transfers between devices, partner(): return lax.ppermute(x, 'dp', [(i, i ^ distance) for i in range(4)])  11.2 us
    pallas_call x1, Pallas kernels, expert_up(): pl.pallas_call(lambda *refs: up_kernel(len(rows), len(weights), *refs), o...  8 us
    pallas_call x1, Pallas kernels, cast_rows(): pl.pallas_call(lambda *refs: cast_kernel(spans, *refs), out_shape=[jax.Sh...  5.08 us
    pallas_call x2, Pallas kernels, expert_down(): pl.pallas_call(lambda *refs: down_kernel(columns, *refs), out_shape=[jax....  4.58 us
    pallas_call x1, Pallas kernels, attention(): pl.pallas_call(attention_kernel, out_shape=[jax.ShapeDtypeStruct((tokens...  3.21 us
  transfers between devices with their start and end apart: 49, of which 27 were waited for; matrix products, arithmetic and copies ran while one was open for 1% of the time, Pallas kernels for 15%

profile of v8, /device:TPU:0, one launch (start us, length us, event | category | flops | bytes accessed | tf_op | source)
XLA Modules:
  0.0 121.4 jit_solution(14977811277011223222)
XLA Ops:
  0.0 3.2 %attention.1 = (bf16[64,512]{1,0:T(8,128)(2,1)}, bf16[64,512]{1,0:T(8,128)(2,1)}, bf16[64,512]{1,0:T(8,128)(2,1)}, bf16[64,512]{1,0:T(8,128)(2,1)}, bf16[128,2048]{1,0:T(8,128)(2,1)}) custom-call(s32[1,2]{1,0:T(1,128)} %refs_0_.1, s32[1,4]{1,0:T(1,128)} %refs_1_.2, bf16[1,256,512]{2,1,0:T(8,128)(2,1)} %refs_2_.2, bf16[2,128,512]{2,1,0:T(8,128)(2,1)} %refs_3_.2, ...), custom_call_target="tpu_custom_call" | custom-call | tf_op jit(solution)/shard_map/attention/pallas_call | solution.py:185
  3.2 3.0 %collective-permute-start.13 = (bf16[128,2048]{1,0:T(8,128)(2,1)}, bf16[128,2048]{1,0:T(8,128)(2,1)S(1)}, u32[]{:S(2)}, u32[]{:S(2)}) collective-permute-start(bf16[128,2048]{1,0:T(8,128)(2,1)} %get-tuple-element.46.refs_9_), channel_id=1, source_target_pairs={{0,16},{8,24},{16,0},{24,8},{1,17},{9,25},{17,1},{25,9},{2,18},{10... | collective-permute-start | bytes 1572872 | tf_op jit(solution)/shard_map/ppermute | solution.py:441
  6.4 1.7 %collective-permute-start.2 = (bf16[64,512]{1,0:T(8,128)(2,1)}, bf16[64,512]{1,0:T(8,128)(2,1)S(1)}, u32[]{:S(2)}, u32[]{:S(2)}) collective-permute-start(bf16[64,512]{1,0:T(8,128)(2,1)} %get-tuple-element.42), channel_id=1, source_target_pairs={{0,24},{8,16},{16,8},{24,0},{1,25},{9,17},{17,9},{25,1},{2,26},{10... | collective-permute-start | bytes 196616 | tf_op jit(solution)/shard_map/ppermute | solution.py:441
  8.1 5.1 %cast_rows.1 = (bf16[384,2048]{1,0:T(8,128)(2,1)}, bf16[256,2048]{1,0:T(8,128)(2,1)}, bf16[256,1280]{1,0:T(8,128)(2,1)}, bf16[256,768]{1,0:T(8,128)(2,1)}) custom-call(f32[1,512,2048]{2,1,0:T(8,128)} %refs_0_.2, f32[1,256,2048]{2,1,0:T(8,128)} %refs_3_.3, f32[1,256,2048]{2,1,0:T(8,128)} %refs_3_.3, f32[1,256,2048]{2,1,0:T(8,128)} %refs_3_.3), custom_call_target="tpu_custom_call" | custom-call | tf_op jit(solution)/shard_map/cast_rows/pallas_call | solution.py:293
  13.2 7.3 %collective-permute-done.1.a2 = bf16[64,512]{1,0:T(8,128)(2,1)S(1)} collective-permute-done((bf16[64,512]{1,0:T(8,128)(2,1)}, bf16[64,512]{1,0:T(8,128)(2,1)S(1)}, u32[]{:S(2)}, u32[]{:S(2)}) %collective-permute-start.1) | collective-permute-done | bytes 65568 | tf_op jit(solution)/shard_map/ppermute | solution.py:441
  20.5 1.7 %collective-permute-start.14 = (bf16[384,2048]{1,0:T(8,128)(2,1)}, bf16[384,2048]{1,0:T(8,128)(2,1)S(1)}, u32[]{:S(2)}, u32[]{:S(2)}) collective-permute-start(bf16[384,2048]{1,0:T(8,128)(2,1)} %get-tuple-element.48.refs_10_), channel_id=1, source_target_pairs={{0,16},{8,24},{16,0},{24,8},{1,17},{9,25},{17,1},{25,9},{2,18},{10... | collective-permute-start | bytes 4718600 | tf_op jit(solution)/shard_map/ppermute | solution.py:441
  22.8 1.6 %collective-permute-start.7 = (bf16[64,2176]{1,0:T(8,128)(2,1)S(1)}, bf16[64,2176]{1,0:T(8,128)(2,1)S(1)}, u32[]{:S(2)}, u32[]{:S(2)}) collective-permute-start(bf16[64,2176]{1,0:T(8,128)(2,1)S(1)} %get-tuple-element.44.refs_0_), channel_id=1, source_target_pairs={{0,2},{2,4},{4,6},{6,7},{7,5},{5,3},{3,1},{1,0},{8,10},{10,12},{12... | collective-permute-start | bytes 835592 | tf_op jit(solution)/shard_map/ppermute | solution.py:451
  24.9 6.8 %collective-permute-done.7.refs_8_ = bf16[64,2176]{1,0:T(8,128)(2,1)S(1)} collective-permute-done((bf16[64,2176]{1,0:T(8,128)(2,1)S(1)}, bf16[64,2176]{1,0:T(8,128)(2,1)S(1)}, u32[]{:S(2)}, u32[]{:S(2)}) %collective-permute-start.7) | collective-permute-done | bytes 278560 | tf_op jit(solution)/shard_map/ppermute | solution.py:451
  33.0 1.6 %collective-permute-start.8 = (bf16[64,2176]{1,0:T(8,128)(2,1)S(1)}, bf16[64,2176]{1,0:T(8,128)(2,1)S(1)}, u32[]{:S(2)}, u32[]{:S(2)}) collective-permute-start(bf16[64,2176]{1,0:T(8,128)(2,1)S(1)} %collective-permute-done.7.refs_8_), channel_id=1, source_target_pairs={{0,2},{2,4},{4,6},{6,7},{7,5},{5,3},{3,1},{1,0},{8,10},{10,12},{12... | collective-permute-start | bytes 835592 | tf_op jit(solution)/shard_map/ppermute | solution.py:451
  35.0 7.0 %collective-permute-done.8.refs_7_ = bf16[64,2176]{1,0:T(8,128)(2,1)S(1)} collective-permute-done((bf16[64,2176]{1,0:T(8,128)(2,1)S(1)}, bf16[64,2176]{1,0:T(8,128)(2,1)S(1)}, u32[]{:S(2)}, u32[]{:S(2)}) %collective-permute-start.8) | collective-permute-done | bytes 278560 | tf_op jit(solution)/shard_map/ppermute | solution.py:451
  44.1 6.3 %collective-permute-done.9.refs_6_ = bf16[64,2176]{1,0:T(8,128)(2,1)S(1)} collective-permute-done((bf16[64,2176]{1,0:T(8,128)(2,1)S(1)}, bf16[64,2176]{1,0:T(8,128)(2,1)S(1)}, u32[]{:S(2)}, u32[]{:S(2)}) %collective-permute-start.9) | collective-permute-done | bytes 278560 | tf_op jit(solution)/shard_map/ppermute | solution.py:451
  50.3 1.6 %collective-permute-start.10 = (bf16[32,2176]{1,0:T(8,128)(2,1)S(1)}, bf16[32,2176]{1,0:T(8,128)(2,1)S(1)}, u32[]{:S(2)}, u32[]{:S(2)}) collective-permute-start(bf16[32,2176]{1,0:T(8,128)(2,1)S(1)} %slice.145), channel_id=1, source_target_pairs={{0,2},{2,4},{4,6},{6,7},{7,5},{5,3},{3,1},{1,0},{8,10},{10,12},{12... | collective-permute-start | bytes 417800 | tf_op jit(solution)/shard_map/ppermute | solution.py:451
  52.5 3.0 %collective-permute-done.10.refs_5_ = bf16[32,2176]{1,0:T(8,128)(2,1)S(1)} collective-permute-done((bf16[32,2176]{1,0:T(8,128)(2,1)S(1)}, bf16[32,2176]{1,0:T(8,128)(2,1)S(1)}, u32[]{:S(2)}, u32[]{:S(2)}) %collective-permute-start.10) | collective-permute-done | bytes 139296 | tf_op jit(solution)/shard_map/ppermute | solution.py:451
  55.5 1.6 %collective-permute-done.6.refs_4_ = bf16[32,2176]{1,0:T(8,128)(2,1)S(1)} collective-permute-done((bf16[32,2176]{1,0:T(8,128)(2,1)S(1)}, bf16[32,2176]{1,0:T(8,128)(2,1)S(1)}, u32[]{:S(2)}, u32[]{:S(2)}) %collective-permute-start.6) | collective-permute-done | bytes 139296 | tf_op jit(solution)/shard_map/ppermute | solution.py:451
  60.2 1.7 %collective-permute-done.19.refs_19_ = bf16[64,2048]{1,0:T(8,128)(2,1)S(1)} collective-permute-done((bf16[64,2048]{1,0:T(8,128)(2,1)S(1)}, bf16[64,2048]{1,0:T(8,128)(2,1)S(1)}, u32[]{:S(2)}, u32[]{:S(2)}) %collective-permute-start.19) | collective-permute-done | bytes 262176 | tf_op jit(solution)/shard_map/ppermute | solution.py:441
  62.7 8.0 %expert_up.1 = (bf16[512,1024]{1,0:T(8,128)(2,1)S(1)}, f32[512,1]{1,0:T(8,128)S(1)}) custom-call(bf16[64,2176]{1,0:T(8,128)(2,1)S(1)} %get-tuple-element.44.refs_0_, bf16[64,2176]{1,0:T(8,128)(2,1)S(1)} %collective-permute-done.3.refs_1_, bf16[64,2176]{1,0:T(8,128)(2,1)S(1)} %collective-permute-done.4.refs_2_, ...), custom_call_target="tpu_custom_call" | custom-call | flops 1 | bytes 1 | tf_op jit(solution)/shard_map/expert_up/pallas_call | solution.py:371
  70.7 2.1 %collective-permute-done.23.refs_4_ = bf16[256,1280]{1,0:T(8,128)(2,1)S(1)} collective-permute-done((bf16[256,1280]{1,0:T(8,128)(2,1)}, bf16[256,1280]{1,0:T(8,128)(2,1)S(1)}, u32[]{:S(2)}, u32[]{:S(2)}) %collective-permute-start.23) | collective-permute-done | bytes 655392 | tf_op jit(solution)/shard_map/ppermute | solution.py:441
  75.1 2.8 %expert_down.2 = (bf16[8,64,1280]{2,1,0:T(8,128)(2,1)S(1)}, bf16[32,1280]{1,0:T(8,128)(2,1)S(1)}, bf16[32,1280]{1,0:T(8,128)(2,1)S(1)}) custom-call(bf16[512,1024]{1,0:T(8,128)(2,1)S(1)} %get-tuple-element.51.refs_0_, f32[512,1]{1,0:T(8,128)S(1)} %get-tuple-element.52.refs_1_, bf16[256,2048]{1,0:T(8,128)(2,1)S(1)} %copy-done, ...), custom_call_target="tpu_custom_call" | custom-call | flops 1 | bytes 1 | tf_op jit(solution)/shard_map/expert_down/pallas_call | solution.py:421
  77.8 1.6 %collective-permute-start.28 = (bf16[32,1280]{1,0:T(8,128)(2,1)S(1)}, bf16[32,1280]{1,0:T(8,128)(2,1)S(1)}, u32[]{:S(2)}, u32[]{:S(2)}) collective-permute-start(bf16[32,1280]{1,0:T(8,128)(2,1)S(1)} %get-tuple-element.59), channel_id=1, source_target_pairs={{0,2},{2,4},{4,6},{6,7},{7,5},{5,3},{3,1},{1,0},{8,10},{10,12},{12... | collective-permute-start | bytes 245768 | tf_op jit(solution)/shard_map/ppermute | solution.py:451
  79.9 5.1 %collective-permute-done.36.refs_4_ = bf16[256,768]{1,0:T(8,128)(2,1)S(1)} collective-permute-done((bf16[256,768]{1,0:T(8,128)(2,1)S(1)}, bf16[256,768]{1,0:T(8,128)(2,1)S(1)}, u32[]{:S(2)}, u32[]{:S(2)}) %collective-permute-start.36) | collective-permute-done | bytes 393248 | tf_op jit(solution)/shard_map/ppermute | solution.py:441
  86.8 1.6 %collective-permute-start.29 = (bf16[64,1280]{1,0:T(8,128)(2,1)S(1)}, bf16[64,1280]{1,0:T(8,128)(2,1)S(1)}, u32[]{:S(2)}, u32[]{:S(2)}) collective-permute-start(bf16[64,1280]{1,0:T(8,128)(2,1)S(1)} %pad_maximum_fusion), channel_id=1, source_target_pairs={{0,2},{2,4},{4,6},{6,7},{7,5},{5,3},{3,1},{1,0},{8,10},{10,12},{12... | collective-permute-start | bytes 491528 | tf_op jit(solution)/shard_map/ppermute | solution.py:451
  88.4 1.8 %expert_down.3 = (bf16[8,64,768]{2,1,0:T(8,128)(2,1)S(1)}, bf16[32,768]{1,0:T(8,128)(2,1)S(1)}, bf16[32,768]{1,0:T(8,128)(2,1)S(1)}) custom-call(bf16[512,1024]{1,0:T(8,128)(2,1)S(1)} %get-tuple-element.51.refs_0_, f32[512,1]{1,0:T(8,128)S(1)} %get-tuple-element.52.refs_1_, bf16[256,2048]{1,0:T(8,128)(2,1)S(1)} %copy-done, ...), custom_call_target="tpu_custom_call" | custom-call | flops 1 | bytes 1 | tf_op jit(solution)/shard_map/expert_down/pallas_call | solution.py:421
  90.2 1.6 %collective-permute-start.41 = (bf16[32,768]{1,0:T(8,128)(2,1)S(1)}, bf16[32,768]{1,0:T(8,128)(2,1)S(1)}, u32[]{:S(2)}, u32[]{:S(2)}) collective-permute-start(bf16[32,768]{1,0:T(8,128)(2,1)S(1)} %get-tuple-element.65), channel_id=1, source_target_pairs={{0,2},{2,4},{4,6},{6,7},{7,5},{5,3},{3,1},{1,0},{8,10},{10,12},{12... | collective-permute-start | bytes 147464 | tf_op jit(solution)/shard_map/ppermute | solution.py:451
  92.3 2.1 %collective-permute-done.41 = bf16[32,768]{1,0:T(8,128)(2,1)S(1)} collective-permute-done((bf16[32,768]{1,0:T(8,128)(2,1)S(1)}, bf16[32,768]{1,0:T(8,128)(2,1)S(1)}, u32[]{:S(2)}, u32[]{:S(2)}) %collective-permute-start.41) | collective-permute-done | bytes 49184 | tf_op jit(solution)/shard_map/ppermute | solution.py:451
  96.0 1.6 %collective-permute-start.42 = (bf16[64,768]{1,0:T(8,128)(2,1)S(1)}, bf16[64,768]{1,0:T(8,128)(2,1)S(1)}, u32[]{:S(2)}, u32[]{:S(2)}) collective-permute-start(bf16[64,768]{1,0:T(8,128)(2,1)S(1)} %pad_maximum_fusion.2), channel_id=1, source_target_pairs={{0,2},{2,4},{4,6},{6,7},{7,5},{5,3},{3,1},{1,0},{8,10},{10,12},{12... | collective-permute-start | bytes 294920 | tf_op jit(solution)/shard_map/ppermute | solution.py:451
  98.2 2.6 %collective-permute-done.42 = bf16[64,768]{1,0:T(8,128)(2,1)S(1)} collective-permute-done((bf16[64,768]{1,0:T(8,128)(2,1)S(1)}, bf16[64,768]{1,0:T(8,128)(2,1)S(1)}, u32[]{:S(2)}, u32[]{:S(2)}) %collective-permute-start.42) | collective-permute-done | bytes 98336 | tf_op jit(solution)/shard_map/ppermute | solution.py:451
  100.8 1.6 %collective-permute-start.43 = (bf16[64,768]{1,0:T(8,128)(2,1)S(1)}, bf16[64,768]{1,0:T(8,128)(2,1)S(1)}, u32[]{:S(2)}, u32[]{:S(2)}) collective-permute-start(bf16[64,768]{1,0:T(8,128)(2,1)S(1)} %fusion.9), channel_id=1, source_target_pairs={{0,2},{2,4},{4,6},{6,7},{7,5},{5,3},{3,1},{1,0},{8,10},{10,12},{12... | collective-permute-start | bytes 294920 | tf_op jit(solution)/shard_map/ppermute | solution.py:451
  104.1 2.2 %collective-permute-done.43 = bf16[64,768]{1,0:T(8,128)(2,1)S(1)} collective-permute-done((bf16[64,768]{1,0:T(8,128)(2,1)S(1)}, bf16[64,768]{1,0:T(8,128)(2,1)S(1)}, u32[]{:S(2)}, u32[]{:S(2)}) %collective-permute-start.43) | collective-permute-done | bytes 98336 | tf_op jit(solution)/shard_map/ppermute | solution.py:451
  106.3 2.0 %collective-permute-start.44 = (bf16[64,768]{1,0:T(8,128)(2,1)S(1)}, bf16[64,768]{1,0:T(8,128)(2,1)S(1)}, u32[]{:S(2)}, u32[]{:S(2)}) collective-permute-start(bf16[64,768]{1,0:T(8,128)(2,1)S(1)} %get-tuple-element.79), channel_id=1, source_target_pairs={{0,2},{2,4},{4,6},{6,7},{7,5},{5,3},{3,1},{1,0},{8,10},{10,12},{12... | collective-permute-start | bytes 294920 | tf_op jit(solution)/shard_map/ppermute | solution.py:451
  110.2 1.7 %collective-permute-start.31 = (bf16[64,1280]{1,0:T(8,128)(2,1)S(1)}, bf16[64,1280]{1,0:T(8,128)(2,1)S(1)}, u32[]{:S(2)}, u32[]{:S(2)}) collective-permute-start(bf16[64,1280]{1,0:T(8,128)(2,1)S(1)} %get-tuple-element.73), channel_id=1, source_target_pairs={{0,2},{2,4},{4,6},{6,7},{7,5},{5,3},{3,1},{1,0},{8,10},{10,12},{12... | collective-permute-start | bytes 491528 | tf_op jit(solution)/shard_map/ppermute | solution.py:451
  112.3 2.9 %collective-permute-done.34 = bf16[64,1280]{1,0:T(8,128)(2,1)S(1)} collective-permute-done((bf16[64,1280]{1,0:T(8,128)(2,1)S(1)}, bf16[64,1280]{1,0:T(8,128)(2,1)S(1)}, u32[]{:S(2)}, u32[]{:S(2)}) %collective-permute-start.34) | collective-permute-done | bytes 163872 | tf_op jit(solution)/shard_map/ppermute | solution.py:451
  116.7 3.9 %collective-permute-done.35 = bf16[64,1280]{1,0:T(8,128)(2,1)S(1)} collective-permute-done((bf16[64,1280]{1,0:T(8,128)(2,1)S(1)}, bf16[64,1280]{1,0:T(8,128)(2,1)S(1)}, u32[]{:S(2)}, u32[]{:S(2)}) %collective-permute-start.35) | collective-permute-done | bytes 163872 | tf_op jit(solution)/shard_map/ppermute | solution.py:451
  (114 shorter events, 22.6 us)
Async XLA Ops:
  3.2 17.3 %collective-permute-start.13 = (bf16[128,2048]{1,0:T(8,128)(2,1)}, bf16[128,2048]{1,0:T(8,128)(2,1)S(1)}, u32[]{:S(2)}, u32[]{:S(2)}) collective-permute-start(bf16[128,2048]{1,0:T(8,128)(2,1)} %get-tuple-element.46.refs_9_), channel_id=1, source_target_pairs={{0,16},{8,24},{16,0},{24,8},{1,17},{9,25},{17,1},{25,9},{2,18},{10... | collective-permute-start | bytes 1572872 | tf_op jit(solution)/shard_map/ppermute | solution.py:441
  6.2 7.0 %collective-permute-start = (bf16[64,512]{1,0:T(8,128)(2,1)}, bf16[64,512]{1,0:T(8,128)(2,1)S(1)}, u32[]{:S(2)}, u32[]{:S(2)}) collective-permute-start(bf16[64,512]{1,0:T(8,128)(2,1)} %get-tuple-element.40), channel_id=1, source_target_pairs={{0,8},{8,0},{16,24},{24,16},{1,9},{9,1},{17,25},{25,17},{2,10},{10... | collective-permute-start | bytes 196616 | tf_op jit(solution)/shard_map/ppermute | solution.py:441
  6.2 14.3 %collective-permute-start.1 = (bf16[64,512]{1,0:T(8,128)(2,1)}, bf16[64,512]{1,0:T(8,128)(2,1)S(1)}, u32[]{:S(2)}, u32[]{:S(2)}) collective-permute-start(bf16[64,512]{1,0:T(8,128)(2,1)} %get-tuple-element.41), channel_id=1, source_target_pairs={{0,16},{8,24},{16,0},{24,8},{1,17},{9,25},{17,1},{25,9},{2,18},{10... | collective-permute-start | bytes 196616 | tf_op jit(solution)/shard_map/ppermute | solution.py:441
  6.4 14.2 %collective-permute-start.2 = (bf16[64,512]{1,0:T(8,128)(2,1)}, bf16[64,512]{1,0:T(8,128)(2,1)S(1)}, u32[]{:S(2)}, u32[]{:S(2)}) collective-permute-start(bf16[64,512]{1,0:T(8,128)(2,1)} %get-tuple-element.42), channel_id=1, source_target_pairs={{0,24},{8,16},{16,8},{24,0},{1,25},{9,17},{17,9},{25,1},{2,26},{10... | collective-permute-start | bytes 196616 | tf_op jit(solution)/shard_map/ppermute | solution.py:441
  20.5 37.1 %collective-permute-start.14 = (bf16[384,2048]{1,0:T(8,128)(2,1)}, bf16[384,2048]{1,0:T(8,128)(2,1)S(1)}, u32[]{:S(2)}, u32[]{:S(2)}) collective-permute-start(bf16[384,2048]{1,0:T(8,128)(2,1)} %get-tuple-element.48.refs_10_), channel_id=1, source_target_pairs={{0,16},{8,24},{16,0},{24,8},{1,17},{9,25},{17,1},{25,9},{2,18},{10... | collective-permute-start | bytes 4718600 | tf_op jit(solution)/shard_map/ppermute | solution.py:441
  22.8 8.9 %collective-permute-start.7 = (bf16[64,2176]{1,0:T(8,128)(2,1)S(1)}, bf16[64,2176]{1,0:T(8,128)(2,1)S(1)}, u32[]{:S(2)}, u32[]{:S(2)}) collective-permute-start(bf16[64,2176]{1,0:T(8,128)(2,1)S(1)} %get-tuple-element.44.refs_0_), channel_id=1, source_target_pairs={{0,2},{2,4},{4,6},{6,7},{7,5},{5,3},{3,1},{1,0},{8,10},{10,12},{12... | collective-permute-start | bytes 835592 | tf_op jit(solution)/shard_map/ppermute | solution.py:451
  24.4 8.5 %collective-permute-start.3 = (bf16[64,2176]{1,0:T(8,128)(2,1)S(1)}, bf16[64,2176]{1,0:T(8,128)(2,1)S(1)}, u32[]{:S(2)}, u32[]{:S(2)}) collective-permute-start(bf16[64,2176]{1,0:T(8,128)(2,1)S(1)} %get-tuple-element.44.refs_0_), channel_id=1, source_target_pairs={{0,1},{2,0},{4,2},{6,4},{7,6},{5,7},{3,5},{1,3},{8,9},{10,8},{12,1... | collective-permute-start | bytes 835592 | tf_op jit(solution)/shard_map/ppermute | solution.py:451
  33.0 25.4 %collective-permute-start.12 = (bf16[384,2048]{1,0:T(8,128)(2,1)}, bf16[384,2048]{1,0:T(8,128)(2,1)S(1)}, u32[]{:S(2)}, u32[]{:S(2)}) collective-permute-start(bf16[384,2048]{1,0:T(8,128)(2,1)} %get-tuple-element.48.refs_10_), channel_id=1, source_target_pairs={{0,8},{8,0},{16,24},{24,16},{1,9},{9,1},{17,25},{25,17},{2,10},{10... | collective-permute-start | bytes 4718600 | tf_op jit(solution)/shard_map/ppermute | solution.py:441
  33.0 9.1 %collective-permute-start.8 = (bf16[64,2176]{1,0:T(8,128)(2,1)S(1)}, bf16[64,2176]{1,0:T(8,128)(2,1)S(1)}, u32[]{:S(2)}, u32[]{:S(2)}) collective-permute-start(bf16[64,2176]{1,0:T(8,128)(2,1)S(1)} %collective-permute-done.7.refs_8_), channel_id=1, source_target_pairs={{0,2},{2,4},{4,6},{6,7},{7,5},{5,3},{3,1},{1,0},{8,10},{10,12},{12... | collective-permute-start | bytes 835592 | tf_op jit(solution)/shard_map/ppermute | solution.py:451
  34.5 9.1 %collective-permute-start.4 = (bf16[64,2176]{1,0:T(8,128)(2,1)S(1)}, bf16[64,2176]{1,0:T(8,128)(2,1)S(1)}, u32[]{:S(2)}, u32[]{:S(2)}) collective-permute-start(bf16[64,2176]{1,0:T(8,128)(2,1)S(1)} %collective-permute-done.3.refs_1_), channel_id=1, source_target_pairs={{0,1},{2,0},{4,2},{6,4},{7,6},{5,7},{3,5},{1,3},{8,9},{10,8},{12,1... | collective-permute-start | bytes 835592 | tf_op jit(solution)/shard_map/ppermute | solution.py:451
  42.0 8.3 %collective-permute-start.9 = (bf16[64,2176]{1,0:T(8,128)(2,1)S(1)}, bf16[64,2176]{1,0:T(8,128)(2,1)S(1)}, u32[]{:S(2)}, u32[]{:S(2)}) collective-permute-start(bf16[64,2176]{1,0:T(8,128)(2,1)S(1)} %collective-permute-done.8.refs_7_), channel_id=1, source_target_pairs={{0,2},{2,4},{4,6},{6,7},{7,5},{5,3},{3,1},{1,0},{8,10},{10,12},{12... | collective-permute-start | bytes 835592 | tf_op jit(solution)/shard_map/ppermute | solution.py:451
  43.6 8.4 %collective-permute-start.5 = (bf16[64,2176]{1,0:T(8,128)(2,1)S(1)}, bf16[64,2176]{1,0:T(8,128)(2,1)S(1)}, u32[]{:S(2)}, u32[]{:S(2)}) collective-permute-start(bf16[64,2176]{1,0:T(8,128)(2,1)S(1)} %collective-permute-done.4.refs_2_), channel_id=1, source_target_pairs={{0,1},{2,0},{4,2},{6,4},{7,6},{5,7},{3,5},{1,3},{8,9},{10,8},{12,1... | collective-permute-start | bytes 835592 | tf_op jit(solution)/shard_map/ppermute | solution.py:451
  50.3 5.1 %collective-permute-start.10 = (bf16[32,2176]{1,0:T(8,128)(2,1)S(1)}, bf16[32,2176]{1,0:T(8,128)(2,1)S(1)}, u32[]{:S(2)}, u32[]{:S(2)}) collective-permute-start(bf16[32,2176]{1,0:T(8,128)(2,1)S(1)} %slice.145), channel_id=1, source_target_pairs={{0,2},{2,4},{4,6},{6,7},{7,5},{5,3},{3,1},{1,0},{8,10},{10,12},{12... | collective-permute-start | bytes 417800 | tf_op jit(solution)/shard_map/ppermute | solution.py:451
  52.0 5.1 %collective-permute-start.6 = (bf16[32,2176]{1,0:T(8,128)(2,1)S(1)}, bf16[32,2176]{1,0:T(8,128)(2,1)S(1)}, u32[]{:S(2)}, u32[]{:S(2)}) collective-permute-start(bf16[32,2176]{1,0:T(8,128)(2,1)S(1)} %slice.144), channel_id=1, source_target_pairs={{0,1},{2,0},{4,2},{6,4},{7,6},{5,7},{3,5},{1,3},{8,9},{10,8},{12,1... | collective-permute-start | bytes 417800 | tf_op jit(solution)/shard_map/ppermute | solution.py:451
  52.5 5.3 %collective-permute-start.11 = (bf16[128,2048]{1,0:T(8,128)(2,1)S(1)}, bf16[128,2048]{1,0:T(8,128)(2,1)S(1)}, u32[]{:S(2)}, u32[]{:S(2)}) collective-permute-start(bf16[128,2048]{1,0:T(8,128)(2,1)S(1)} %copy-done.2), channel_id=1, source_target_pairs={{0,8},{8,0},{16,24},{24,16},{1,9},{9,1},{17,25},{25,17},{2,10},{10... | collective-permute-start | bytes 1572872 | tf_op jit(solution)/shard_map/ppermute | solution.py:441
  57.1 15.7 %collective-permute-start.23 = (bf16[256,1280]{1,0:T(8,128)(2,1)}, bf16[256,1280]{1,0:T(8,128)(2,1)S(1)}, u32[]{:S(2)}, u32[]{:S(2)}) collective-permute-start(bf16[256,1280]{1,0:T(8,128)(2,1)} %get-tuple-element.56), channel_id=1, source_target_pairs={{0,16},{8,24},{16,0},{24,8},{1,17},{9,25},{17,1},{25,9},{2,18},{10... | collective-permute-start | bytes 1966088 | tf_op jit(solution)/shard_map/ppermute | solution.py:441
  58.4 15.6 %collective-permute-start.22 = (bf16[256,2048]{1,0:T(8,128)(2,1)S(1)}, bf16[256,2048]{1,0:T(8,128)(2,1)S(1)}, u32[]{:S(2)}, u32[]{:S(2)}) collective-permute-start(bf16[256,2048]{1,0:T(8,128)(2,1)S(1)} %copy-done), channel_id=1, source_target_pairs={{0,8},{8,0},{16,24},{24,16},{1,9},{9,1},{17,25},{25,17},{2,10},{10... | collective-permute-start | bytes 3145736 | tf_op jit(solution)/shard_map/ppermute | solution.py:441
  74.0 11.1 %collective-permute-start.36 = (bf16[256,768]{1,0:T(8,128)(2,1)S(1)}, bf16[256,768]{1,0:T(8,128)(2,1)S(1)}, u32[]{:S(2)}, u32[]{:S(2)}) collective-permute-start(bf16[256,768]{1,0:T(8,128)(2,1)S(1)} %copy-done.8), channel_id=1, source_target_pairs={{0,16},{8,24},{16,0},{24,8},{1,17},{9,25},{17,1},{25,9},{2,18},{10... | collective-permute-start | bytes 1179656 | tf_op jit(solution)/shard_map/ppermute | solution.py:441
  77.8 7.9 %collective-permute-start.28 = (bf16[32,1280]{1,0:T(8,128)(2,1)S(1)}, bf16[32,1280]{1,0:T(8,128)(2,1)S(1)}, u32[]{:S(2)}, u32[]{:S(2)}) collective-permute-start(bf16[32,1280]{1,0:T(8,128)(2,1)S(1)} %get-tuple-element.59), channel_id=1, source_target_pairs={{0,2},{2,4},{4,6},{6,7},{7,5},{5,3},{3,1},{1,0},{8,10},{10,12},{12... | collective-permute-start | bytes 245768 | tf_op jit(solution)/shard_map/ppermute | solution.py:451
  79.5 6.7 %collective-permute-start.32 = (bf16[32,1280]{1,0:T(8,128)(2,1)S(1)}, bf16[32,1280]{1,0:T(8,128)(2,1)S(1)}, u32[]{:S(2)}, u32[]{:S(2)}) collective-permute-start(bf16[32,1280]{1,0:T(8,128)(2,1)S(1)} %get-tuple-element.60), channel_id=1, source_target_pairs={{0,1},{2,0},{4,2},{6,4},{7,6},{5,7},{3,5},{1,3},{8,9},{10,8},{12,1... | collective-permute-start | bytes 245768 | tf_op jit(solution)/shard_map/ppermute | solution.py:451
  86.3 22.1 %collective-permute-start.33 = (bf16[64,1280]{1,0:T(8,128)(2,1)S(1)}, bf16[64,1280]{1,0:T(8,128)(2,1)S(1)}, u32[]{:S(2)}, u32[]{:S(2)}) collective-permute-start(bf16[64,1280]{1,0:T(8,128)(2,1)S(1)} %pad_maximum_fusion.1), channel_id=1, source_target_pairs={{0,1},{2,0},{4,2},{6,4},{7,6},{5,7},{3,5},{1,3},{8,9},{10,8},{12,1... | collective-permute-start | bytes 491528 | tf_op jit(solution)/shard_map/ppermute | solution.py:451
  86.8 15.6 %collective-permute-start.29 = (bf16[64,1280]{1,0:T(8,128)(2,1)S(1)}, bf16[64,1280]{1,0:T(8,128)(2,1)S(1)}, u32[]{:S(2)}, u32[]{:S(2)}) collective-permute-start(bf16[64,1280]{1,0:T(8,128)(2,1)S(1)} %pad_maximum_fusion), channel_id=1, source_target_pairs={{0,2},{2,4},{4,6},{6,7},{7,5},{5,3},{3,1},{1,0},{8,10},{10,12},{12... | collective-permute-start | bytes 491528 | tf_op jit(solution)/shard_map/ppermute | solution.py:451
  96.0 4.8 %collective-permute-start.42 = (bf16[64,768]{1,0:T(8,128)(2,1)S(1)}, bf16[64,768]{1,0:T(8,128)(2,1)S(1)}, u32[]{:S(2)}, u32[]{:S(2)}) collective-permute-start(bf16[64,768]{1,0:T(8,128)(2,1)S(1)} %pad_maximum_fusion.2), channel_id=1, source_target_pairs={{0,2},{2,4},{4,6},{6,7},{7,5},{5,3},{3,1},{1,0},{8,10},{10,12},{12... | collective-permute-start | bytes 294920 | tf_op jit(solution)/shard_map/ppermute | solution.py:451
  97.7 6.4 %collective-permute-start.46 = (bf16[64,768]{1,0:T(8,128)(2,1)S(1)}, bf16[64,768]{1,0:T(8,128)(2,1)S(1)}, u32[]{:S(2)}, u32[]{:S(2)}) collective-permute-start(bf16[64,768]{1,0:T(8,128)(2,1)S(1)} %pad_maximum_fusion.3), channel_id=1, source_target_pairs={{0,1},{2,0},{4,2},{6,4},{7,6},{5,7},{3,5},{1,3},{8,9},{10,8},{12,1... | collective-permute-start | bytes 294920 | tf_op jit(solution)/shard_map/ppermute | solution.py:451
  100.8 5.4 %collective-permute-start.43 = (bf16[64,768]{1,0:T(8,128)(2,1)S(1)}, bf16[64,768]{1,0:T(8,128)(2,1)S(1)}, u32[]{:S(2)}, u32[]{:S(2)}) collective-permute-start(bf16[64,768]{1,0:T(8,128)(2,1)S(1)} %fusion.9), channel_id=1, source_target_pairs={{0,2},{2,4},{4,6},{6,7},{7,5},{5,3},{3,1},{1,0},{8,10},{10,12},{12... | collective-permute-start | bytes 294920 | tf_op jit(solution)/shard_map/ppermute | solution.py:451
  102.5 7.3 %collective-permute-start.30 = (bf16[64,1280]{1,0:T(8,128)(2,1)S(1)}, bf16[64,1280]{1,0:T(8,128)(2,1)S(1)}, u32[]{:S(2)}, u32[]{:S(2)}) collective-permute-start(bf16[64,1280]{1,0:T(8,128)(2,1)S(1)} %fusion.2), channel_id=1, source_target_pairs={{0,2},{2,4},{4,6},{6,7},{7,5},{5,3},{3,1},{1,0},{8,10},{10,12},{12... | collective-permute-start | bytes 491528 | tf_op jit(solution)/shard_map/ppermute | solution.py:451
  106.3 5.6 %collective-permute-start.47 = (bf16[64,768]{1,0:T(8,128)(2,1)S(1)}, bf16[64,768]{1,0:T(8,128)(2,1)S(1)}, u32[]{:S(2)}, u32[]{:S(2)}) collective-permute-start(bf16[64,768]{1,0:T(8,128)(2,1)S(1)} %get-tuple-element.80), channel_id=1, source_target_pairs={{0,1},{2,0},{4,2},{6,4},{7,6},{5,7},{3,5},{1,3},{8,9},{10,8},{12,1... | collective-permute-start | bytes 294920 | tf_op jit(solution)/shard_map/ppermute | solution.py:451
  106.3 9.2 %collective-permute-start.44 = (bf16[64,768]{1,0:T(8,128)(2,1)S(1)}, bf16[64,768]{1,0:T(8,128)(2,1)S(1)}, u32[]{:S(2)}, u32[]{:S(2)}) collective-permute-start(bf16[64,768]{1,0:T(8,128)(2,1)S(1)} %get-tuple-element.79), channel_id=1, source_target_pairs={{0,2},{2,4},{4,6},{6,7},{7,5},{5,3},{3,1},{1,0},{8,10},{10,12},{12... | collective-permute-start | bytes 294920 | tf_op jit(solution)/shard_map/ppermute | solution.py:451
  109.8 5.4 %collective-permute-start.34 = (bf16[64,1280]{1,0:T(8,128)(2,1)S(1)}, bf16[64,1280]{1,0:T(8,128)(2,1)S(1)}, u32[]{:S(2)}, u32[]{:S(2)}) collective-permute-start(bf16[64,1280]{1,0:T(8,128)(2,1)S(1)} %get-tuple-element.74), channel_id=1, source_target_pairs={{0,1},{2,0},{4,2},{6,4},{7,6},{5,7},{3,5},{1,3},{8,9},{10,8},{12,1... | collective-permute-start | bytes 491528 | tf_op jit(solution)/shard_map/ppermute | solution.py:451
  110.2 6.5 %collective-permute-start.31 = (bf16[64,1280]{1,0:T(8,128)(2,1)S(1)}, bf16[64,1280]{1,0:T(8,128)(2,1)S(1)}, u32[]{:S(2)}, u32[]{:S(2)}) collective-permute-start(bf16[64,1280]{1,0:T(8,128)(2,1)S(1)} %get-tuple-element.73), channel_id=1, source_target_pairs={{0,2},{2,4},{4,6},{6,7},{7,5},{5,3},{3,1},{1,0},{8,10},{10,12},{12... | collective-permute-start | bytes 491528 | tf_op jit(solution)/shard_map/ppermute | solution.py:451
  111.9 4.7 %collective-permute-start.48 = (bf16[64,768]{1,0:T(8,128)(2,1)S(1)}, bf16[64,768]{1,0:T(8,128)(2,1)S(1)}, u32[]{:S(2)}, u32[]{:S(2)}) collective-permute-start(bf16[64,768]{1,0:T(8,128)(2,1)S(1)} %fusion.8), channel_id=1, source_target_pairs={{0,1},{2,0},{4,2},{6,4},{7,6},{5,7},{3,5},{1,3},{8,9},{10,8},{12,1... | collective-permute-start | bytes 294920 | tf_op jit(solution)/shard_map/ppermute | solution.py:451
  115.2 5.4 %collective-permute-start.35 = (bf16[64,1280]{1,0:T(8,128)(2,1)S(1)}, bf16[64,1280]{1,0:T(8,128)(2,1)S(1)}, u32[]{:S(2)}, u32[]{:S(2)}) collective-permute-start(bf16[64,1280]{1,0:T(8,128)(2,1)S(1)} %fusion.1), channel_id=1, source_target_pairs={{0,1},{2,0},{4,2},{6,4},{7,6},{5,7},{3,5},{1,3},{8,9},{10,8},{12,1... | collective-permute-start | bytes 491528 | tf_op jit(solution)/shard_map/ppermute | solution.py:451
  (26 other events, 169.9 us)

commit v9 on v7

--- a/solution.py
+++ b/solution.py
@@ -388,8 +388,9 @@
     )(*rows, *weights)
 
 
-def down_kernel(column, hidden_ref, gate_ref, *refs):
-    pieces, (out_ref, left_ref, right_ref, weights, arrived) = refs[:-5], refs[-5:]
+def down_kernel(column, sources, hidden_ref, gate_ref, *refs):
+    (weights, arrived), refs = refs[-2:], refs[:-2]
+    pieces, outs = refs[: len(refs) - sources - 3], refs[len(refs) - sources - 3 :]
     copies, first = [], 0
     for i, ref in enumerate(pieces):
         depth = ref.shape[0]
@@ -407,25 +408,33 @@
         copy.wait()
     total = jnp.dot(hidden_ref[...], weights[...], preferred_element_type=jnp.float32)
     weighted = (total * gate_ref[...]).astype(jnp.bfloat16)
-    sources, rows, width = out_ref.shape
-    out_ref[...] = weighted.reshape(sources, rows, width)
-    middle, half = sources // 2 * rows, rows // 2
-    left_ref[...] = weighted[middle : middle + half]
-    right_ref[...] = weighted[middle + half : middle + rows]
+    rows = weighted.shape[0] // sources
+    for (first, count), ref in zip(down_blocks(rows, sources), outs):
+        ref[...] = weighted[first : first + count]
+
+
+def down_blocks(rows, sources):
+    half, reach = rows // 2, sources // 2
+    blocks = [(0, rows)]
+    for step, middle in ((-1, reach * rows), (1, reach * rows + half)):
+        blocks.append((middle, half))
+        second = (reach + step) * rows
+        blocks += [(second, half), (second + half, half)]
+        blocks += [((reach + step * away) * rows, rows) for away in range(2, reach)]
+    return blocks
 
 
 def expert_down(hidden_units, gates, weights, column, width, sources):
     tokens, hidden_size = hidden_units.shape
     rows = tokens // sources
     return pl.pallas_call(
-        lambda *refs: down_kernel(column, *refs),
+        lambda *refs: down_kernel(column, sources, *refs),
         out_shape=[
-            jax.ShapeDtypeStruct((sources, rows, width), jnp.bfloat16),
-            jax.ShapeDtypeStruct((rows // 2, width), jnp.bfloat16),
-            jax.ShapeDtypeStruct((rows // 2, width), jnp.bfloat16),
+            jax.ShapeDtypeStruct((count, width), jnp.bfloat16)
+            for _, count in down_blocks(rows, sources)
         ],
         in_specs=vmem(2) + [pl.BlockSpec(memory_space=pl.ANY)] * len(weights),
-        out_specs=vmem(3),
+        out_specs=vmem(sources + 3),
         scratch_shapes=[
             pltpu.VMEM((hidden_size, width), jnp.bfloat16),
             pltpu.SemaphoreType.DMA((len(weights),)),
@@ -469,17 +478,19 @@
     return above + far + below[:0:-1], list(zip(above[1:], below[1:])) + [tuple(far)]
 
 
-def scatter_sum(weighted, left, right):
-    sources, rows, _ = weighted.shape
-    half = rows // 2
-    reach = sources // 2
-    up, down = around(left, 1), around(right, -1)
-    up = jnp.concatenate([add(weighted[reach - 1, :half], up), weighted[reach - 1, half:]])
-    down = jnp.concatenate([weighted[reach + 1, :half], add(weighted[reach + 1, half:], down)])
-    for away in range(reach - 2, 0, -1):
-        up = add(weighted[away], around(up, 1))
-        down = add(weighted[sources - away], around(down, -1))
-    return weighted[0], around(up, 1), around(down, -1)
+def scatter_sum(own, *blocks):
+    reach = len(blocks) // 2
+    terms = [own]
+    for step, (far, first, second, *near) in ((1, blocks[:reach]), (-1, blocks[reach:])):
+        moving = around(far, step)
+        if step > 0:
+            moving = jnp.concatenate([add(first, moving), second])
+        else:
+            moving = jnp.concatenate([first, add(second, moving)])
+        for block in near:
+            moving = add(block, around(moving, step))
+        terms.append(around(moving, step))
+    return terms
 
 
 def relayed(x, rows):
@@ -503,7 +514,7 @@
     width = trainer_down.shape[2]
     depth, columns = trainer_gate_up.shape[1:]
     down_depth = trainer_down.shape[1]
-    early = depth // 8
+    early = depth // 4
     slab = width // SLABS
     *attn, first_own = attention(
         queries, key_pool, value_pool, page_table, prompt_lengths, trainer_gate_up, early
@@ -524,7 +535,7 @@
     rest_beside = partner(after(rest_own, *arrived[0]), 1)
     down_beside = partner(after(down_own, *arrived[1]), 1)
     down_across = partner(after(down_own, *arrived[2]), 2)
-    rest_opposite = relayed(after(rest_across, *arrived[3]), early)
+    rest_opposite = relayed(after(rest_across, *arrived[3]), depth // 8)
     hidden_units, gates = expert_up(
         gathered,
         [first_own, rest_own, first_beside, rest_beside]

time: 119 us -> 114 us (0.958)
  waiting for transfers between devices: 63.2 us -> 58.8 us
    ppermute x24, waiting for transfers between devices: 40.3 us -> 35.2 us  [around(): lax.ppermute(x, 'expert', [(ring[i], ring[(i + step) % count]) for i in r...]
    ppermute x19 -> x18, waiting for transfers between devices: 22.9 us -> 23.6 us  [partner(): return lax.ppermute(x, 'dp', [(i, i ^ distance) for i in range(4)])]
    ppermute x19 -> x18, starting transfers between devices: 9.27 us -> 9.12 us  [partner(): return lax.ppermute(x, 'dp', [(i, i ^ distance) for i in range(4)])]
  transfers between devices with their start and end apart: 43 -> 42, of which waited for: 29 -> 30; matrix products, arithmetic and copies ran while one was open for 1% -> 1% of each run, Pallas kernels for 12% -> 12%
where the time goes in v9:
time: 114 us
  waiting for transfers between devices  58.8 us (52%)
  starting transfers between devices  34 us (30%)
  Pallas kernels  18.7 us (16%)
  other arithmetic  1.28 us (1%)
    ppermute x24, waiting for transfers between devices, around(): lax.ppermute(x, 'expert', [(ring[i], ring[(i + step) % count]) for i in r...  35.2 us
    ppermute x24, starting transfers between devices, around(): lax.ppermute(x, 'expert', [(ring[i], ring[(i + step) % count]) for i in r...  24.9 us
    ppermute x18, waiting for transfers between devices, partner(): return lax.ppermute(x, 'dp', [(i, i ^ distance) for i in range(4)])  23.6 us
    ppermute x18, starting transfers between devices, partner(): return lax.ppermute(x, 'dp', [(i, i ^ distance) for i in range(4)])  9.12 us
    pallas_call x1, Pallas kernels, expert_up(): pl.pallas_call(lambda *refs: up_kernel(len(rows), len(weights), *refs), o...  8.17 us
    pallas_call x1, Pallas kernels, cast_rows(): pl.pallas_call(lambda *refs: cast_kernel(spans, *refs), out_shape=[jax.Sh...  3.99 us
    pallas_call x1, Pallas kernels, attention(): pl.pallas_call(attention_kernel, out_shape=[jax.ShapeDtypeStruct((tokens...  3.2 us
    pallas_call x2, Pallas kernels, expert_down(): pl.pallas_call(lambda *refs: down_kernel(column, sources, *refs), out_sha...  2.97 us
  transfers between devices with their start and end apart: 42, of which 30 were waited for; matrix products, arithmetic and copies ran while one was open for 1% of the time, Pallas kernels for 12%

profile of v9, /device:TPU:0, one launch (start us, length us, event | category | flops | bytes accessed | tf_op | source)
XLA Modules:
  0.0 113.6 jit_solution(17224326954535469996)
XLA Ops:
  0.0 3.2 %attention.1 = (bf16[64,512]{1,0:T(8,128)(2,1)}, bf16[64,512]{1,0:T(8,128)(2,1)}, bf16[64,512]{1,0:T(8,128)(2,1)}, bf16[64,512]{1,0:T(8,128)(2,1)}, bf16[128,2048]{1,0:T(8,128)(2,1)}) custom-call(s32[1,2]{1,0:T(1,128)} %refs_0_.1, s32[1,4]{1,0:T(1,128)} %refs_1_.2, bf16[1,256,512]{2,1,0:T(8,128)(2,1)} %refs_2_.1, bf16[2,128,512]{2,1,0:T(8,128)(2,1)} %refs_3_.1, ...), custom_call_target="tpu_custom_call" | custom-call | tf_op jit(solution)/shard_map/attention/pallas_call | solution.py:185
  3.2 3.0 %collective-permute-start.13 = (bf16[128,2048]{1,0:T(8,128)(2,1)}, bf16[128,2048]{1,0:T(8,128)(2,1)S(1)}, u32[]{:S(2)}, u32[]{:S(2)}) collective-permute-start(bf16[128,2048]{1,0:T(8,128)(2,1)} %get-tuple-element.58.refs_9_), channel_id=1, source_target_pairs={{0,16},{8,24},{16,0},{24,8},{1,17},{9,25},{17,1},{25,9},{2,18},{10... | collective-permute-start | bytes 1572872 | tf_op jit(solution)/shard_map/ppermute | solution.py:449
  6.4 1.7 %collective-permute-start.2 = (bf16[64,512]{1,0:T(8,128)(2,1)}, bf16[64,512]{1,0:T(8,128)(2,1)S(1)}, u32[]{:S(2)}, u32[]{:S(2)}) collective-permute-start(bf16[64,512]{1,0:T(8,128)(2,1)} %get-tuple-element.54), channel_id=1, source_target_pairs={{0,24},{8,16},{16,8},{24,0},{1,25},{9,17},{17,9},{25,1},{2,26},{10... | collective-permute-start | bytes 196616 | tf_op jit(solution)/shard_map/ppermute | solution.py:449
  8.1 4.0 %cast_rows.1 = (bf16[384,2048]{1,0:T(8,128)(2,1)}, bf16[256,2048]{1,0:T(8,128)(2,1)}) custom-call(f32[1,512,2048]{2,1,0:T(8,128)} %refs_0_.2, f32[1,256,2048]{2,1,0:T(8,128)} %refs_1_.3), custom_call_target="tpu_custom_call" | custom-call | tf_op jit(solution)/shard_map/cast_rows/pallas_call | solution.py:293
  12.1 8.3 %collective-permute-done.1.a2 = bf16[64,512]{1,0:T(8,128)(2,1)S(1)} collective-permute-done((bf16[64,512]{1,0:T(8,128)(2,1)}, bf16[64,512]{1,0:T(8,128)(2,1)S(1)}, u32[]{:S(2)}, u32[]{:S(2)}) %collective-permute-start.1) | collective-permute-done | bytes 65568 | tf_op jit(solution)/shard_map/ppermute | solution.py:449
  20.5 1.7 %collective-permute-start.14 = (bf16[384,2048]{1,0:T(8,128)(2,1)}, bf16[384,2048]{1,0:T(8,128)(2,1)S(1)}, u32[]{:S(2)}, u32[]{:S(2)}) collective-permute-start(bf16[384,2048]{1,0:T(8,128)(2,1)} %get-tuple-element.60.refs_10_), channel_id=1, source_target_pairs={{0,16},{8,24},{16,0},{24,8},{1,17},{9,25},{17,1},{25,9},{2,18},{10... | collective-permute-start | bytes 4718600 | tf_op jit(solution)/shard_map/ppermute | solution.py:449
  22.8 1.6 %collective-permute-start.7 = (bf16[64,2176]{1,0:T(8,128)(2,1)S(1)}, bf16[64,2176]{1,0:T(8,128)(2,1)S(1)}, u32[]{:S(2)}, u32[]{:S(2)}) collective-permute-start(bf16[64,2176]{1,0:T(8,128)(2,1)S(1)} %get-tuple-element.56.refs_0_), channel_id=1, source_target_pairs={{0,2},{2,4},{4,6},{6,7},{7,5},{5,3},{3,1},{1,0},{8,10},{10,12},{12... | collective-permute-start | bytes 835592 | tf_op jit(solution)/shard_map/ppermute | solution.py:459
  24.9 6.8 %collective-permute-done.7.refs_8_ = bf16[64,2176]{1,0:T(8,128)(2,1)S(1)} collective-permute-done((bf16[64,2176]{1,0:T(8,128)(2,1)S(1)}, bf16[64,2176]{1,0:T(8,128)(2,1)S(1)}, u32[]{:S(2)}, u32[]{:S(2)}) %collective-permute-start.7) | collective-permute-done | bytes 278560 | tf_op jit(solution)/shard_map/ppermute | solution.py:459
  31.7 1.3 %collective-permute-done.3.refs_1_ = bf16[64,2176]{1,0:T(8,128)(2,1)S(1)} collective-permute-done((bf16[64,2176]{1,0:T(8,128)(2,1)S(1)}, bf16[64,2176]{1,0:T(8,128)(2,1)S(1)}, u32[]{:S(2)}, u32[]{:S(2)}) %collective-permute-start.3) | collective-permute-done | bytes 278560 | tf_op jit(solution)/shard_map/ppermute | solution.py:459
  33.0 1.6 %collective-permute-start.8 = (bf16[64,2176]{1,0:T(8,128)(2,1)S(1)}, bf16[64,2176]{1,0:T(8,128)(2,1)S(1)}, u32[]{:S(2)}, u32[]{:S(2)}) collective-permute-start(bf16[64,2176]{1,0:T(8,128)(2,1)S(1)} %collective-permute-done.7.refs_8_), channel_id=1, source_target_pairs={{0,2},{2,4},{4,6},{6,7},{7,5},{5,3},{3,1},{1,0},{8,10},{10,12},{12... | collective-permute-start | bytes 835592 | tf_op jit(solution)/shard_map/ppermute | solution.py:459
  35.0 7.0 %collective-permute-done.8.refs_7_ = bf16[64,2176]{1,0:T(8,128)(2,1)S(1)} collective-permute-done((bf16[64,2176]{1,0:T(8,128)(2,1)S(1)}, bf16[64,2176]{1,0:T(8,128)(2,1)S(1)}, u32[]{:S(2)}, u32[]{:S(2)}) %collective-permute-start.8) | collective-permute-done | bytes 278560 | tf_op jit(solution)/shard_map/ppermute | solution.py:459
  42.0 1.6 %collective-permute-start.9 = (bf16[64,2176]{1,0:T(8,128)(2,1)S(1)}, bf16[64,2176]{1,0:T(8,128)(2,1)S(1)}, u32[]{:S(2)}, u32[]{:S(2)}) collective-permute-start(bf16[64,2176]{1,0:T(8,128)(2,1)S(1)} %collective-permute-done.8.refs_7_), channel_id=1, source_target_pairs={{0,2},{2,4},{4,6},{6,7},{7,5},{5,3},{3,1},{1,0},{8,10},{10,12},{12... | collective-permute-start | bytes 835592 | tf_op jit(solution)/shard_map/ppermute | solution.py:459
  44.1 6.3 %collective-permute-done.9.refs_6_ = bf16[64,2176]{1,0:T(8,128)(2,1)S(1)} collective-permute-done((bf16[64,2176]{1,0:T(8,128)(2,1)S(1)}, bf16[64,2176]{1,0:T(8,128)(2,1)S(1)}, u32[]{:S(2)}, u32[]{:S(2)}) %collective-permute-start.9) | collective-permute-done | bytes 278560 | tf_op jit(solution)/shard_map/ppermute | solution.py:459
  50.3 1.6 %collective-permute-start.10 = (bf16[32,2176]{1,0:T(8,128)(2,1)S(1)}, bf16[32,2176]{1,0:T(8,128)(2,1)S(1)}, u32[]{:S(2)}, u32[]{:S(2)}) collective-permute-start(bf16[32,2176]{1,0:T(8,128)(2,1)S(1)} %slice.49), channel_id=1, source_target_pairs={{0,2},{2,4},{4,6},{6,7},{7,5},{5,3},{3,1},{1,0},{8,10},{10,12},{12... | collective-permute-start | bytes 417800 | tf_op jit(solution)/shard_map/ppermute | solution.py:459
  52.5 2.9 %collective-permute-done.10.refs_5_ = bf16[32,2176]{1,0:T(8,128)(2,1)S(1)} collective-permute-done((bf16[32,2176]{1,0:T(8,128)(2,1)S(1)}, bf16[32,2176]{1,0:T(8,128)(2,1)S(1)}, u32[]{:S(2)}, u32[]{:S(2)}) %collective-permute-start.10) | collective-permute-done | bytes 139296 | tf_op jit(solution)/shard_map/ppermute | solution.py:459
  61.7 8.2 %expert_up.1 = (bf16[512,1024]{1,0:T(8,128)(2,1)S(1)}, f32[512,1]{1,0:T(8,128)S(1)}) custom-call(bf16[64,2176]{1,0:T(8,128)(2,1)S(1)} %get-tuple-element.56.refs_0_, bf16[64,2176]{1,0:T(8,128)(2,1)S(1)} %collective-permute-done.3.refs_1_, bf16[64,2176]{1,0:T(8,128)(2,1)S(1)} %collective-permute-done.4.refs_2_, ...), custom_call_target="tpu_custom_call" | custom-call | flops 1 | bytes 1 | tf_op jit(solution)/shard_map/expert_up/pallas_call | solution.py:371
  69.8 10.1 %collective-permute-done.23.refs_4_ = bf16[256,2048]{1,0:T(8,128)(2,1)S(1)} collective-permute-done((bf16[256,2048]{1,0:T(8,128)(2,1)}, bf16[256,2048]{1,0:T(8,128)(2,1)S(1)}, u32[]{:S(2)}, u32[]{:S(2)}) %collective-permute-start.23) | collective-permute-done | bytes 1048608 | tf_op jit(solution)/shard_map/ppermute | solution.py:449
  80.7 1.4 %collective-permute-done.24.refs_5_ = bf16[128,2048]{1,0:T(8,128)(2,1)S(1)} collective-permute-done((bf16[128,2048]{1,0:T(8,128)(2,1)S(1)}, bf16[128,2048]{1,0:T(8,128)(2,1)S(1)}, u32[]{:S(2)}, u32[]{:S(2)}) %collective-permute-start.24) | collective-permute-done | bytes 524320 | tf_op jit(solution)/shard_map/ppermute | solution.py:449
  82.8 1.5 %expert_down.3 = (bf16[64,1024]{1,0:T(8,128)(2,1)S(1)}, bf16[32,1024]{1,0:T(8,128)(2,1)S(1)}, bf16[32,1024]{1,0:T(8,128)(2,1)S(1)}, bf16[32,1024]{1,0:T(8,128)(2...) custom-call(bf16[512,1024]{1,0:T(8,128)(2,1)S(1)} %get-tuple-element, ...), custom_call_target="tpu_custom_call" | custom-call | flops 1 | bytes 1 | tf_op jit(solution)/shard_map/expert_down/pallas_call | solution.py:430
  84.3 1.9 %collective-permute-start.34 = (bf16[32,1024]{1,0:T(8,128)(2,1)S(1)}, bf16[32,1024]{1,0:T(8,128)(2,1)S(1)}, u32[]{:S(2)}, u32[]{:S(2)}) collective-permute-start(bf16[32,1024]{1,0:T(8,128)(2,1)S(1)} %get-tuple-element.84), channel_id=1, source_target_pairs={{0,2},{2,4},{4,6},{6,7},{7,5},{5,3},{3,1},{1,0},{8,10},{10,12},{12... | collective-permute-start | bytes 196616 | tf_op jit(solution)/shard_map/ppermute | solution.py:459
  86.4 1.5 %expert_down.2 = (bf16[64,1024]{1,0:T(8,128)(2,1)S(1)}, bf16[32,1024]{1,0:T(8,128)(2,1)S(1)}, bf16[32,1024]{1,0:T(8,128)(2,1)S(1)}, bf16[32,1024]{1,0:T(8,128)(2...) custom-call(bf16[512,1024]{1,0:T(8,128)(2,1)S(1)} %get-tuple-element, ...), custom_call_target="tpu_custom_call" | custom-call | flops 1 | bytes 1 | tf_op jit(solution)/shard_map/expert_down/pallas_call | solution.py:430
  87.9 1.9 %collective-permute-start.26 = (bf16[32,1024]{1,0:T(8,128)(2,1)S(1)}, bf16[32,1024]{1,0:T(8,128)(2,1)S(1)}, u32[]{:S(2)}, u32[]{:S(2)}) collective-permute-start(bf16[32,1024]{1,0:T(8,128)(2,1)S(1)} %get-tuple-element.73), channel_id=1, source_target_pairs={{0,2},{2,4},{4,6},{6,7},{7,5},{5,3},{3,1},{1,0},{8,10},{10,12},{12... | collective-permute-start | bytes 196616 | tf_op jit(solution)/shard_map/ppermute | solution.py:459
  90.0 1.9 %collective-permute-start.35 = (bf16[64,1024]{1,0:T(8,128)(2,1)S(1)}, bf16[64,1024]{1,0:T(8,128)(2,1)S(1)}, u32[]{:S(2)}, u32[]{:S(2)}) collective-permute-start(bf16[64,1024]{1,0:T(8,128)(2,1)S(1)} %pad_maximum_fusion.2), channel_id=1, source_target_pairs={{0,2},{2,4},{4,6},{6,7},{7,5},{5,3},{3,1},{1,0},{8,10},{10,12},{12... | collective-permute-start | bytes 393224 | tf_op jit(solution)/shard_map/ppermute | solution.py:459
  92.6 2.0 %collective-permute-start.27 = (bf16[64,1024]{1,0:T(8,128)(2,1)S(1)}, bf16[64,1024]{1,0:T(8,128)(2,1)S(1)}, u32[]{:S(2)}, u32[]{:S(2)}) collective-permute-start(bf16[64,1024]{1,0:T(8,128)(2,1)S(1)} %pad_maximum_fusion), channel_id=1, source_target_pairs={{0,2},{2,4},{4,6},{6,7},{7,5},{5,3},{3,1},{1,0},{8,10},{10,12},{12... | collective-permute-start | bytes 393224 | tf_op jit(solution)/shard_map/ppermute | solution.py:459
  94.8 1.6 %collective-permute-done.35 = bf16[64,1024]{1,0:T(8,128)(2,1)S(1)} collective-permute-done((bf16[64,1024]{1,0:T(8,128)(2,1)S(1)}, bf16[64,1024]{1,0:T(8,128)(2,1)S(1)}, u32[]{:S(2)}, u32[]{:S(2)}) %collective-permute-start.35) | collective-permute-done | bytes 131104 | tf_op jit(solution)/shard_map/ppermute | solution.py:459
  96.4 1.9 %collective-permute-start.36 = (bf16[64,1024]{1,0:T(8,128)(2,1)S(1)}, bf16[64,1024]{1,0:T(8,128)(2,1)S(1)}, u32[]{:S(2)}, u32[]{:S(2)}) collective-permute-start(bf16[64,1024]{1,0:T(8,128)(2,1)S(1)} %add_convert_fusion.4), channel_id=1, source_target_pairs={{0,2},{2,4},{4,6},{6,7},{7,5},{5,3},{3,1},{1,0},{8,10},{10,12},{12... | collective-permute-start | bytes 393224 | tf_op jit(solution)/shard_map/ppermute | solution.py:459
  99.2 1.9 %collective-permute-start.28 = (bf16[64,1024]{1,0:T(8,128)(2,1)S(1)}, bf16[64,1024]{1,0:T(8,128)(2,1)S(1)}, u32[]{:S(2)}, u32[]{:S(2)}) collective-permute-start(bf16[64,1024]{1,0:T(8,128)(2,1)S(1)} %add_convert_fusion.9), channel_id=1, source_target_pairs={{0,2},{2,4},{4,6},{6,7},{7,5},{5,3},{3,1},{1,0},{8,10},{10,12},{12... | collective-permute-start | bytes 393224 | tf_op jit(solution)/shard_map/ppermute | solution.py:459
  102.1 1.9 %collective-permute-start.37 = (bf16[64,1024]{1,0:T(8,128)(2,1)S(1)}, bf16[64,1024]{1,0:T(8,128)(2,1)S(1)}, u32[]{:S(2)}, u32[]{:S(2)}) collective-permute-start(bf16[64,1024]{1,0:T(8,128)(2,1)S(1)} %add_convert_fusion.3), channel_id=1, source_target_pairs={{0,2},{2,4},{4,6},{6,7},{7,5},{5,3},{3,1},{1,0},{8,10},{10,12},{12... | collective-permute-start | bytes 393224 | tf_op jit(solution)/shard_map/ppermute | solution.py:459
  104.2 1.3 %collective-permute-done.28 = bf16[64,1024]{1,0:T(8,128)(2,1)S(1)} collective-permute-done((bf16[64,1024]{1,0:T(8,128)(2,1)S(1)}, bf16[64,1024]{1,0:T(8,128)(2,1)S(1)}, u32[]{:S(2)}, u32[]{:S(2)}) %collective-permute-start.28) | collective-permute-done | bytes 131104 | tf_op jit(solution)/shard_map/ppermute | solution.py:459
  105.6 1.9 %collective-permute-start.29 = (bf16[64,1024]{1,0:T(8,128)(2,1)S(1)}, bf16[64,1024]{1,0:T(8,128)(2,1)S(1)}, u32[]{:S(2)}, u32[]{:S(2)}) collective-permute-start(bf16[64,1024]{1,0:T(8,128)(2,1)S(1)} %add_convert_fusion.8), channel_id=1, source_target_pairs={{0,2},{2,4},{4,6},{6,7},{7,5},{5,3},{3,1},{1,0},{8,10},{10,12},{12... | collective-permute-start | bytes 393224 | tf_op jit(solution)/shard_map/ppermute | solution.py:459
  107.8 1.6 %collective-permute-done.41 = bf16[64,1024]{1,0:T(8,128)(2,1)S(1)} collective-permute-done((bf16[64,1024]{1,0:T(8,128)(2,1)S(1)}, bf16[64,1024]{1,0:T(8,128)(2,1)S(1)}, u32[]{:S(2)}, u32[]{:S(2)}) %collective-permute-start.41) | collective-permute-done | bytes 131104 | tf_op jit(solution)/shard_map/ppermute | solution.py:459
  110.6 2.1 %collective-permute-done.33 = bf16[64,1024]{1,0:T(8,128)(2,1)S(1)} collective-permute-done((bf16[64,1024]{1,0:T(8,128)(2,1)S(1)}, bf16[64,1024]{1,0:T(8,128)(2,1)S(1)}, u32[]{:S(2)}, u32[]{:S(2)}) %collective-permute-start.33) | collective-permute-done | bytes 131104 | tf_op jit(solution)/shard_map/ppermute | solution.py:459
  (98 shorter events, 16.3 us)
Async XLA Ops:
  3.2 17.3 %collective-permute-start.13 = (bf16[128,2048]{1,0:T(8,128)(2,1)}, bf16[128,2048]{1,0:T(8,128)(2,1)S(1)}, u32[]{:S(2)}, u32[]{:S(2)}) collective-permute-start(bf16[128,2048]{1,0:T(8,128)(2,1)} %get-tuple-element.58.refs_9_), channel_id=1, source_target_pairs={{0,16},{8,24},{16,0},{24,8},{1,17},{9,25},{17,1},{25,9},{2,18},{10... | collective-permute-start | bytes 1572872 | tf_op jit(solution)/shard_map/ppermute | solution.py:449
  6.2 5.9 %collective-permute-start = (bf16[64,512]{1,0:T(8,128)(2,1)}, bf16[64,512]{1,0:T(8,128)(2,1)S(1)}, u32[]{:S(2)}, u32[]{:S(2)}) collective-permute-start(bf16[64,512]{1,0:T(8,128)(2,1)} %get-tuple-element.52), channel_id=1, source_target_pairs={{0,8},{8,0},{16,24},{24,16},{1,9},{9,1},{17,25},{25,17},{2,10},{10... | collective-permute-start | bytes 196616 | tf_op jit(solution)/shard_map/ppermute | solution.py:449
  6.2 14.3 %collective-permute-start.1 = (bf16[64,512]{1,0:T(8,128)(2,1)}, bf16[64,512]{1,0:T(8,128)(2,1)S(1)}, u32[]{:S(2)}, u32[]{:S(2)}) collective-permute-start(bf16[64,512]{1,0:T(8,128)(2,1)} %get-tuple-element.53), channel_id=1, source_target_pairs={{0,16},{8,24},{16,0},{24,8},{1,17},{9,25},{17,1},{25,9},{2,18},{10... | collective-permute-start | bytes 196616 | tf_op jit(solution)/shard_map/ppermute | solution.py:449
  6.4 14.2 %collective-permute-start.2 = (bf16[64,512]{1,0:T(8,128)(2,1)}, bf16[64,512]{1,0:T(8,128)(2,1)S(1)}, u32[]{:S(2)}, u32[]{:S(2)}) collective-permute-start(bf16[64,512]{1,0:T(8,128)(2,1)} %get-tuple-element.54), channel_id=1, source_target_pairs={{0,24},{8,16},{16,8},{24,0},{1,25},{9,17},{17,9},{25,1},{2,26},{10... | collective-permute-start | bytes 196616 | tf_op jit(solution)/shard_map/ppermute | solution.py:449
  20.5 37.4 %collective-permute-start.14 = (bf16[384,2048]{1,0:T(8,128)(2,1)}, bf16[384,2048]{1,0:T(8,128)(2,1)S(1)}, u32[]{:S(2)}, u32[]{:S(2)}) collective-permute-start(bf16[384,2048]{1,0:T(8,128)(2,1)} %get-tuple-element.60.refs_10_), channel_id=1, source_target_pairs={{0,16},{8,24},{16,0},{24,8},{1,17},{9,25},{17,1},{25,9},{2,18},{10... | collective-permute-start | bytes 4718600 | tf_op jit(solution)/shard_map/ppermute | solution.py:449
  22.8 8.9 %collective-permute-start.7 = (bf16[64,2176]{1,0:T(8,128)(2,1)S(1)}, bf16[64,2176]{1,0:T(8,128)(2,1)S(1)}, u32[]{:S(2)}, u32[]{:S(2)}) collective-permute-start(bf16[64,2176]{1,0:T(8,128)(2,1)S(1)} %get-tuple-element.56.refs_0_), channel_id=1, source_target_pairs={{0,2},{2,4},{4,6},{6,7},{7,5},{5,3},{3,1},{1,0},{8,10},{10,12},{12... | collective-permute-start | bytes 835592 | tf_op jit(solution)/shard_map/ppermute | solution.py:459
  24.4 8.5 %collective-permute-start.3 = (bf16[64,2176]{1,0:T(8,128)(2,1)S(1)}, bf16[64,2176]{1,0:T(8,128)(2,1)S(1)}, u32[]{:S(2)}, u32[]{:S(2)}) collective-permute-start(bf16[64,2176]{1,0:T(8,128)(2,1)S(1)} %get-tuple-element.56.refs_0_), channel_id=1, source_target_pairs={{0,1},{2,0},{4,2},{6,4},{7,6},{5,7},{3,5},{1,3},{8,9},{10,8},{12,1... | collective-permute-start | bytes 835592 | tf_op jit(solution)/shard_map/ppermute | solution.py:459
  33.0 26.2 %collective-permute-start.12 = (bf16[384,2048]{1,0:T(8,128)(2,1)}, bf16[384,2048]{1,0:T(8,128)(2,1)S(1)}, u32[]{:S(2)}, u32[]{:S(2)}) collective-permute-start(bf16[384,2048]{1,0:T(8,128)(2,1)} %get-tuple-element.60.refs_10_), channel_id=1, source_target_pairs={{0,8},{8,0},{16,24},{24,16},{1,9},{9,1},{17,25},{25,17},{2,10},{10... | collective-permute-start | bytes 4718600 | tf_op jit(solution)/shard_map/ppermute | solution.py:449
  33.0 9.1 %collective-permute-start.8 = (bf16[64,2176]{1,0:T(8,128)(2,1)S(1)}, bf16[64,2176]{1,0:T(8,128)(2,1)S(1)}, u32[]{:S(2)}, u32[]{:S(2)}) collective-permute-start(bf16[64,2176]{1,0:T(8,128)(2,1)S(1)} %collective-permute-done.7.refs_8_), channel_id=1, source_target_pairs={{0,2},{2,4},{4,6},{6,7},{7,5},{5,3},{3,1},{1,0},{8,10},{10,12},{12... | collective-permute-start | bytes 835592 | tf_op jit(solution)/shard_map/ppermute | solution.py:459
  34.5 9.1 %collective-permute-start.4 = (bf16[64,2176]{1,0:T(8,128)(2,1)S(1)}, bf16[64,2176]{1,0:T(8,128)(2,1)S(1)}, u32[]{:S(2)}, u32[]{:S(2)}) collective-permute-start(bf16[64,2176]{1,0:T(8,128)(2,1)S(1)} %collective-permute-done.3.refs_1_), channel_id=1, source_target_pairs={{0,1},{2,0},{4,2},{6,4},{7,6},{5,7},{3,5},{1,3},{8,9},{10,8},{12,1... | collective-permute-start | bytes 835592 | tf_op jit(solution)/shard_map/ppermute | solution.py:459
  42.0 8.3 %collective-permute-start.9 = (bf16[64,2176]{1,0:T(8,128)(2,1)S(1)}, bf16[64,2176]{1,0:T(8,128)(2,1)S(1)}, u32[]{:S(2)}, u32[]{:S(2)}) collective-permute-start(bf16[64,2176]{1,0:T(8,128)(2,1)S(1)} %collective-permute-done.8.refs_7_), channel_id=1, source_target_pairs={{0,2},{2,4},{4,6},{6,7},{7,5},{5,3},{3,1},{1,0},{8,10},{10,12},{12... | collective-permute-start | bytes 835592 | tf_op jit(solution)/shard_map/ppermute | solution.py:459
  43.6 8.4 %collective-permute-start.5 = (bf16[64,2176]{1,0:T(8,128)(2,1)S(1)}, bf16[64,2176]{1,0:T(8,128)(2,1)S(1)}, u32[]{:S(2)}, u32[]{:S(2)}) collective-permute-start(bf16[64,2176]{1,0:T(8,128)(2,1)S(1)} %collective-permute-done.4.refs_2_), channel_id=1, source_target_pairs={{0,1},{2,0},{4,2},{6,4},{7,6},{5,7},{3,5},{1,3},{8,9},{10,8},{12,1... | collective-permute-start | bytes 835592 | tf_op jit(solution)/shard_map/ppermute | solution.py:459
  50.3 5.1 %collective-permute-start.10 = (bf16[32,2176]{1,0:T(8,128)(2,1)S(1)}, bf16[32,2176]{1,0:T(8,128)(2,1)S(1)}, u32[]{:S(2)}, u32[]{:S(2)}) collective-permute-start(bf16[32,2176]{1,0:T(8,128)(2,1)S(1)} %slice.49), channel_id=1, source_target_pairs={{0,2},{2,4},{4,6},{6,7},{7,5},{5,3},{3,1},{1,0},{8,10},{10,12},{12... | collective-permute-start | bytes 417800 | tf_op jit(solution)/shard_map/ppermute | solution.py:459
  52.0 5.1 %collective-permute-start.6 = (bf16[32,2176]{1,0:T(8,128)(2,1)S(1)}, bf16[32,2176]{1,0:T(8,128)(2,1)S(1)}, u32[]{:S(2)}, u32[]{:S(2)}) collective-permute-start(bf16[32,2176]{1,0:T(8,128)(2,1)S(1)} %slice.48), channel_id=1, source_target_pairs={{0,1},{2,0},{4,2},{6,4},{7,6},{5,7},{3,5},{1,3},{8,9},{10,8},{12,1... | collective-permute-start | bytes 417800 | tf_op jit(solution)/shard_map/ppermute | solution.py:459
  52.5 5.7 %collective-permute-start.11 = (bf16[128,2048]{1,0:T(8,128)(2,1)S(1)}, bf16[128,2048]{1,0:T(8,128)(2,1)S(1)}, u32[]{:S(2)}, u32[]{:S(2)}) collective-permute-start(bf16[128,2048]{1,0:T(8,128)(2,1)S(1)} %copy-done.2), channel_id=1, source_target_pairs={{0,8},{8,0},{16,24},{24,16},{1,9},{9,1},{17,25},{25,17},{2,10},{10... | collective-permute-start | bytes 1572872 | tf_op jit(solution)/shard_map/ppermute | solution.py:449
  55.4 24.5 %collective-permute-start.23 = (bf16[256,2048]{1,0:T(8,128)(2,1)}, bf16[256,2048]{1,0:T(8,128)(2,1)S(1)}, u32[]{:S(2)}, u32[]{:S(2)}) collective-permute-start(bf16[256,2048]{1,0:T(8,128)(2,1)} %get-tuple-element.67.refs_2_), channel_id=1, source_target_pairs={{0,16},{8,24},{16,0},{24,8},{1,17},{9,25},{17,1},{25,9},{2,18},{10... | collective-permute-start | bytes 3145736 | tf_op jit(solution)/shard_map/ppermute | solution.py:449
  60.5 20.1 %collective-permute-start.22 = (bf16[256,2048]{1,0:T(8,128)(2,1)S(1)}, bf16[256,2048]{1,0:T(8,128)(2,1)S(1)}, u32[]{:S(2)}, u32[]{:S(2)}) collective-permute-start(bf16[256,2048]{1,0:T(8,128)(2,1)S(1)} %copy-done), channel_id=1, source_target_pairs={{0,8},{8,0},{16,24},{24,16},{1,9},{9,1},{17,25},{25,17},{2,10},{10... | collective-permute-start | bytes 3145736 | tf_op jit(solution)/shard_map/ppermute | solution.py:449
  84.3 5.7 %collective-permute-start.34 = (bf16[32,1024]{1,0:T(8,128)(2,1)S(1)}, bf16[32,1024]{1,0:T(8,128)(2,1)S(1)}, u32[]{:S(2)}, u32[]{:S(2)}) collective-permute-start(bf16[32,1024]{1,0:T(8,128)(2,1)S(1)} %get-tuple-element.84), channel_id=1, source_target_pairs={{0,2},{2,4},{4,6},{6,7},{7,5},{5,3},{3,1},{1,0},{8,10},{10,12},{12... | collective-permute-start | bytes 196616 | tf_op jit(solution)/shard_map/ppermute | solution.py:459
  86.2 5.7 %collective-permute-start.38 = (bf16[32,1024]{1,0:T(8,128)(2,1)S(1)}, bf16[32,1024]{1,0:T(8,128)(2,1)S(1)}, u32[]{:S(2)}, u32[]{:S(2)}) collective-permute-start(bf16[32,1024]{1,0:T(8,128)(2,1)S(1)} %get-tuple-element.90), channel_id=1, source_target_pairs={{0,1},{2,0},{4,2},{6,4},{7,6},{5,7},{3,5},{1,3},{8,9},{10,8},{12,1... | collective-permute-start | bytes 196616 | tf_op jit(solution)/shard_map/ppermute | solution.py:459
  89.7 5.0 %collective-permute-start.30 = (bf16[32,1024]{1,0:T(8,128)(2,1)S(1)}, bf16[32,1024]{1,0:T(8,128)(2,1)S(1)}, u32[]{:S(2)}, u32[]{:S(2)}) collective-permute-start(bf16[32,1024]{1,0:T(8,128)(2,1)S(1)} %get-tuple-element.79), channel_id=1, source_target_pairs={{0,1},{2,0},{4,2},{6,4},{7,6},{5,7},{3,5},{1,3},{8,9},{10,8},{12,1... | collective-permute-start | bytes 196616 | tf_op jit(solution)/shard_map/ppermute | solution.py:459
  90.0 6.4 %collective-permute-start.35 = (bf16[64,1024]{1,0:T(8,128)(2,1)S(1)}, bf16[64,1024]{1,0:T(8,128)(2,1)S(1)}, u32[]{:S(2)}, u32[]{:S(2)}) collective-permute-start(bf16[64,1024]{1,0:T(8,128)(2,1)S(1)} %pad_maximum_fusion.2), channel_id=1, source_target_pairs={{0,2},{2,4},{4,6},{6,7},{7,5},{5,3},{3,1},{1,0},{8,10},{10,12},{12... | collective-permute-start | bytes 393224 | tf_op jit(solution)/shard_map/ppermute | solution.py:459
  91.9 6.4 %collective-permute-start.39 = (bf16[64,1024]{1,0:T(8,128)(2,1)S(1)}, bf16[64,1024]{1,0:T(8,128)(2,1)S(1)}, u32[]{:S(2)}, u32[]{:S(2)}) collective-permute-start(bf16[64,1024]{1,0:T(8,128)(2,1)S(1)} %pad_maximum_fusion.3), channel_id=1, source_target_pairs={{0,1},{2,0},{4,2},{6,4},{7,6},{5,7},{3,5},{1,3},{8,9},{10,8},{12,1... | collective-permute-start | bytes 393224 | tf_op jit(solution)/shard_map/ppermute | solution.py:459
  92.6 6.6 %collective-permute-start.27 = (bf16[64,1024]{1,0:T(8,128)(2,1)S(1)}, bf16[64,1024]{1,0:T(8,128)(2,1)S(1)}, u32[]{:S(2)}, u32[]{:S(2)}) collective-permute-start(bf16[64,1024]{1,0:T(8,128)(2,1)S(1)} %pad_maximum_fusion), channel_id=1, source_target_pairs={{0,2},{2,4},{4,6},{6,7},{7,5},{5,3},{3,1},{1,0},{8,10},{10,12},{12... | collective-permute-start | bytes 393224 | tf_op jit(solution)/shard_map/ppermute | solution.py:459
  94.7 6.4 %collective-permute-start.31 = (bf16[64,1024]{1,0:T(8,128)(2,1)S(1)}, bf16[64,1024]{1,0:T(8,128)(2,1)S(1)}, u32[]{:S(2)}, u32[]{:S(2)}) collective-permute-start(bf16[64,1024]{1,0:T(8,128)(2,1)S(1)} %pad_maximum_fusion.1), channel_id=1, source_target_pairs={{0,1},{2,0},{4,2},{6,4},{7,6},{5,7},{3,5},{1,3},{8,9},{10,8},{12,1... | collective-permute-start | bytes 393224 | tf_op jit(solution)/shard_map/ppermute | solution.py:459
  96.4 5.6 %collective-permute-start.36 = (bf16[64,1024]{1,0:T(8,128)(2,1)S(1)}, bf16[64,1024]{1,0:T(8,128)(2,1)S(1)}, u32[]{:S(2)}, u32[]{:S(2)}) collective-permute-start(bf16[64,1024]{1,0:T(8,128)(2,1)S(1)} %add_convert_fusion.4), channel_id=1, source_target_pairs={{0,2},{2,4},{4,6},{6,7},{7,5},{5,3},{3,1},{1,0},{8,10},{10,12},{12... | collective-permute-start | bytes 393224 | tf_op jit(solution)/shard_map/ppermute | solution.py:459
  98.3 5.6 %collective-permute-start.40 = (bf16[64,1024]{1,0:T(8,128)(2,1)S(1)}, bf16[64,1024]{1,0:T(8,128)(2,1)S(1)}, u32[]{:S(2)}, u32[]{:S(2)}) collective-permute-start(bf16[64,1024]{1,0:T(8,128)(2,1)S(1)} %add_convert_fusion.2), channel_id=1, source_target_pairs={{0,1},{2,0},{4,2},{6,4},{7,6},{5,7},{3,5},{1,3},{8,9},{10,8},{12,1... | collective-permute-start | bytes 393224 | tf_op jit(solution)/shard_map/ppermute | solution.py:459
  99.2 6.4 %collective-permute-start.28 = (bf16[64,1024]{1,0:T(8,128)(2,1)S(1)}, bf16[64,1024]{1,0:T(8,128)(2,1)S(1)}, u32[]{:S(2)}, u32[]{:S(2)}) collective-permute-start(bf16[64,1024]{1,0:T(8,128)(2,1)S(1)} %add_convert_fusion.9), channel_id=1, source_target_pairs={{0,2},{2,4},{4,6},{6,7},{7,5},{5,3},{3,1},{1,0},{8,10},{10,12},{12... | collective-permute-start | bytes 393224 | tf_op jit(solution)/shard_map/ppermute | solution.py:459
  101.2 6.4 %collective-permute-start.32 = (bf16[64,1024]{1,0:T(8,128)(2,1)S(1)}, bf16[64,1024]{1,0:T(8,128)(2,1)S(1)}, u32[]{:S(2)}, u32[]{:S(2)}) collective-permute-start(bf16[64,1024]{1,0:T(8,128)(2,1)S(1)} %add_convert_fusion.7), channel_id=1, source_target_pairs={{0,1},{2,0},{4,2},{6,4},{7,6},{5,7},{3,5},{1,3},{8,9},{10,8},{12,1... | collective-permute-start | bytes 393224 | tf_op jit(solution)/shard_map/ppermute | solution.py:459
  102.1 5.8 %collective-permute-start.37 = (bf16[64,1024]{1,0:T(8,128)(2,1)S(1)}, bf16[64,1024]{1,0:T(8,128)(2,1)S(1)}, u32[]{:S(2)}, u32[]{:S(2)}) collective-permute-start(bf16[64,1024]{1,0:T(8,128)(2,1)S(1)} %add_convert_fusion.3), channel_id=1, source_target_pairs={{0,2},{2,4},{4,6},{6,7},{7,5},{5,3},{3,1},{1,0},{8,10},{10,12},{12... | collective-permute-start | bytes 393224 | tf_op jit(solution)/shard_map/ppermute | solution.py:459
  104.0 5.5 %collective-permute-start.41 = (bf16[64,1024]{1,0:T(8,128)(2,1)S(1)}, bf16[64,1024]{1,0:T(8,128)(2,1)S(1)}, u32[]{:S(2)}, u32[]{:S(2)}) collective-permute-start(bf16[64,1024]{1,0:T(8,128)(2,1)S(1)} %add_convert_fusion.1), channel_id=1, source_target_pairs={{0,1},{2,0},{4,2},{6,4},{7,6},{5,7},{3,5},{1,3},{8,9},{10,8},{12,1... | collective-permute-start | bytes 393224 | tf_op jit(solution)/shard_map/ppermute | solution.py:459
  105.6 5.0 %collective-permute-start.29 = (bf16[64,1024]{1,0:T(8,128)(2,1)S(1)}, bf16[64,1024]{1,0:T(8,128)(2,1)S(1)}, u32[]{:S(2)}, u32[]{:S(2)}) collective-permute-start(bf16[64,1024]{1,0:T(8,128)(2,1)S(1)} %add_convert_fusion.8), channel_id=1, source_target_pairs={{0,2},{2,4},{4,6},{6,7},{7,5},{5,3},{3,1},{1,0},{8,10},{10,12},{12... | collective-permute-start | bytes 393224 | tf_op jit(solution)/shard_map/ppermute | solution.py:459
  107.7 5.0 %collective-permute-start.33 = (bf16[64,1024]{1,0:T(8,128)(2,1)S(1)}, bf16[64,1024]{1,0:T(8,128)(2,1)S(1)}, u32[]{:S(2)}, u32[]{:S(2)}) collective-permute-start(bf16[64,1024]{1,0:T(8,128)(2,1)S(1)} %add_convert_fusion.6), channel_id=1, source_target_pairs={{0,1},{2,0},{4,2},{6,4},{7,6},{5,7},{3,5},{1,3},{8,9},{10,8},{12,1... | collective-permute-start | bytes 393224 | tf_op jit(solution)/shard_map/ppermute | solution.py:459
  (18 other events, 154.2 us)

commit v10 on v9

--- a/solution.py
+++ b/solution.py
@@ -126,8 +126,8 @@
 
 
 def attention_kernel(*refs):
-    sources, outs, piece_ref, scratch = refs[:6], refs[6:10], refs[10], refs[11:]
-    table, lengths, q_ref, k_ref, v_ref, weights, attn, arrived = scratch
+    sources, outs, scratch = refs[:5], refs[5:9], refs[9:]
+    table, lengths, q_ref, k_ref, v_ref, attn, arrived = scratch
     copies = [
         pltpu.make_async_copy(source, target, arrived.at[i])
         for i, (source, target) in enumerate(
@@ -137,13 +137,9 @@
             )
         )
     ]
-    rows = weights.shape[0]
-    copies.append(
-        pltpu.make_async_copy(sources[5].at[0, pl.ds(0, rows)], weights, arrived.at[5])
-    )
     for copy in copies:
         copy.start()
-    for copy in copies[:5]:
+    for copy in copies:
         copy.wait()
     tokens, width = q_ref.shape
     pages = k_ref.shape[0]
@@ -176,31 +172,27 @@
     for d in range(4):
         first = pl.multiple_of((own ^ d) * rows, rows)
         outs[d][...] = attn[pl.ds(first, rows), :]
-    copies[5].wait()
-    piece_ref[...] = weights[...].astype(jnp.bfloat16)
-
-
-def attention(queries, key_pool, value_pool, page_table, prompt_lengths, gate_up, early):
+
+
+def attention(queries, key_pool, value_pool, page_table, prompt_lengths):
     tokens, width = queries.shape[1:]
     return pl.pallas_call(
         attention_kernel,
-        out_shape=[jax.ShapeDtypeStruct((tokens // 4, width), jnp.bfloat16)] * 4
-        + [jax.ShapeDtypeStruct((early, gate_up.shape[2]), jnp.bfloat16)],
-        in_specs=[pl.BlockSpec(memory_space=pltpu.HBM)] * 6,
-        out_specs=vmem(5),
+        out_shape=[jax.ShapeDtypeStruct((tokens // 4, width), jnp.bfloat16)] * 4,
+        in_specs=[pl.BlockSpec(memory_space=pltpu.HBM)] * 5,
+        out_specs=vmem(4),
         scratch_shapes=[
             pltpu.SMEM(page_table.shape, jnp.int32),
             pltpu.SMEM(prompt_lengths.shape, jnp.int32),
             pltpu.VMEM((tokens, width), jnp.bfloat16),
             pltpu.VMEM(key_pool.shape, jnp.bfloat16),
             pltpu.VMEM(value_pool.shape, jnp.bfloat16),
-            pltpu.VMEM((early, gate_up.shape[2]), jnp.float32),
             pltpu.VMEM((tokens, width), jnp.bfloat16),
-            pltpu.SemaphoreType.DMA((6,)),
+            pltpu.SemaphoreType.DMA((5,)),
         ],
         compiler_params=params(VMEM_MOST),
         name="attention",
-    )(page_table, prompt_lengths, queries, key_pool, value_pool, gate_up)
+    )(page_table, prompt_lengths, queries, key_pool, value_pool)
 
 
 def norm_kernel(hidden_ref, a0, a1, a2, a3, gain_ref, ids_ref, gates_ref, resid_ref, rows_ref):
@@ -388,11 +380,11 @@
     )(*rows, *weights)
 
 
-def down_kernel(column, sources, hidden_ref, gate_ref, *refs):
+def down_kernel(columns, sources, hidden_ref, gate_ref, *refs):
     (weights, arrived), refs = refs[-2:], refs[:-2]
     pieces, outs = refs[: len(refs) - sources - 3], refs[len(refs) - sources - 3 :]
     copies, first = [], 0
-    for i, ref in enumerate(pieces):
+    for i, (ref, column) in enumerate(zip(pieces, columns)):
         depth = ref.shape[0]
         copies.append(
             pltpu.make_async_copy(
@@ -424,11 +416,12 @@
     return blocks
 
 
-def expert_down(hidden_units, gates, weights, column, width, sources):
+def expert_down(hidden_units, gates, weights, width, sources):
+    weights, columns = zip(*weights)
     tokens, hidden_size = hidden_units.shape
     rows = tokens // sources
     return pl.pallas_call(
-        lambda *refs: down_kernel(column, sources, *refs),
+        lambda *refs: down_kernel(columns, sources, *refs),
         out_shape=[
             jax.ShapeDtypeStruct((count, width), jnp.bfloat16)
             for _, count in down_blocks(rows, sources)
@@ -516,10 +509,11 @@
     down_depth = trainer_down.shape[1]
     early = depth // 4
     slab = width // SLABS
-    *attn, first_own = attention(
-        queries, key_pool, value_pool, page_table, prompt_lengths, trainer_gate_up, early
-    )
+    (first_own,) = cast_rows([trainer_gate_up], [(0, early, 0, columns)])
     first_across = partner(first_own, 2)
+    attn = attention(
+        after(queries, first_own), key_pool, value_pool, page_table, prompt_lengths
+    )
     rest_own, down_own = cast_rows(
         [after(trainer_gate_up, attn[0]), trainer_down],
         [(early, depth - early, 0, columns), (0, down_depth, 0, width)],
@@ -541,11 +535,12 @@
         [first_own, rest_own, first_beside, rest_beside]
         + [first_across, rest_across, first_opposite, *rest_opposite],
     )
-    down_opposite = relayed(after(down_across, hidden_units), down_depth // 2)
-    weights = [down_own, down_beside, down_across, *down_opposite]
+    down_ready = after(down_across, hidden_units)
     mixed = []
     for first in range(0, width, slab):
-        weighted = expert_down(hidden_units, gates, weights, first, slab, expert_count)
+        opposite = partner(down_ready[:, first : first + slab], 1)
+        weights = [(down_own, first), (down_beside, first), (down_across, first), (opposite, 0)]
+        weighted = expert_down(hidden_units, gates, weights, slab, expert_count)
         total = resid[:, first : first + slab].astype(jnp.float32)
         for term in scatter_sum(*weighted):
             total = total + term.astype(jnp.float32)

time: 114 us -> 112 us (0.982)
  waiting for transfers between devices: 58.8 us -> 54.9 us
  Pallas kernels: 18.7 us -> 20.5 us
    ppermute x18, waiting for transfers between devices: 23.6 us -> 19.7 us  [partner(): return lax.ppermute(x, 'dp', [(i, i ^ distance) for i in range(4)])]
    pallas_call x1 -> x2, Pallas kernels: 3.99 us -> 5.92 us  [cast_rows(): pl.pallas_call(lambda *refs: cast_kernel(spans, *refs), out_shape=[jax.Sh...]
  transfers between devices with their start and end apart: 42 -> 42, of which waited for: 30 -> 29; matrix products, arithmetic and copies ran while one was open for 1% -> 1% of each run, Pallas kernels for 12% -> 17%
where the time goes in v10:
time: 112 us
  waiting for transfers between devices  54.9 us (49%)
  starting transfers between devices  34.1 us (30%)
  Pallas kernels  20.5 us (18%)
  other arithmetic  1.28 us (1%)
    ppermute x24, waiting for transfers between devices, around(): lax.ppermute(x, 'expert', [(ring[i], ring[(i + step) % count]) for i in r...  35.2 us
    ppermute x24, starting transfers between devices, around(): lax.ppermute(x, 'expert', [(ring[i], ring[(i + step) % count]) for i in r...  24.9 us
    ppermute x18, waiting for transfers between devices, partner(): return lax.ppermute(x, 'dp', [(i, i ^ distance) for i in range(4)])  19.7 us
    ppermute x18, starting transfers between devices, partner(): return lax.ppermute(x, 'dp', [(i, i ^ distance) for i in range(4)])  9.21 us
    pallas_call x1, Pallas kernels, expert_up(): pl.pallas_call(lambda *refs: up_kernel(len(rows), len(weights), *refs), o...  8.28 us
    pallas_call x2, Pallas kernels, cast_rows(): pl.pallas_call(lambda *refs: cast_kernel(spans, *refs), out_shape=[jax.Sh...  5.92 us
    pallas_call x1, Pallas kernels, attention(): pl.pallas_call(attention_kernel, out_shape=[jax.ShapeDtypeStruct((tokens...  2.98 us
    pallas_call x2, Pallas kernels, expert_down(): pl.pallas_call(lambda *refs: down_kernel(columns, sources, *refs), out_sh...  2.95 us
  transfers between devices with their start and end apart: 42, of which 29 were waited for; matrix products, arithmetic and copies ran while one was open for 1% of the time, Pallas kernels for 17%

profile of v10, /device:TPU:0, one launch (start us, length us, event | category | flops | bytes accessed | tf_op | source)
XLA Modules:
  0.0 111.5 jit_solution(1305108246327461031)
XLA Ops:
  0.0 1.9 %cast_rows.2.refs_9_ = bf16[128,2048]{1,0:T(8,128)(2,1)} custom-call(f32[1,512,2048]{2,1,0:T(8,128)} %refs_0_.4), custom_call_target="tpu_custom_call" | custom-call | tf_op jit(solution)/shard_map/cast_rows/pallas_call | solution.py:285
  1.9 3.0 %collective-permute-start.13 = (bf16[128,2048]{1,0:T(8,128)(2,1)}, bf16[128,2048]{1,0:T(8,128)(2,1)S(1)}, u32[]{:S(2)}, u32[]{:S(2)}) collective-permute-start(bf16[128,2048]{1,0:T(8,128)(2,1)} %cast_rows.2.refs_9_), channel_id=1, source_target_pairs={{0,16},{8,24},{16,0},{24,8},{1,17},{9,25},{17,1},{25,9},{2,18},{10... | collective-permute-start | bytes 1572872 | tf_op jit(solution)/shard_map/ppermute | solution.py:442
  4.9 3.0 %attention.1 = (bf16[64,512]{1,0:T(8,128)(2,1)}, bf16[64,512]{1,0:T(8,128)(2,1)}, bf16[64,512]{1,0:T(8,128)(2,1)}, bf16[64,512]{1,0:T(8,128)(2,1)}) custom-call(s32[1,2]{1,0:T(1,128)} %refs_0_.3, s32[1,4]{1,0:T(1,128)} %refs_1_.2, bf16[1,256,512]{2,1,0:T(8,128)(2,1)} %refs_2_, bf16[2,128,512]{2,1,0:T(8,128)(2,1)} %refs_3_.1, bf16[2,128,512]{2,1,0:T(8,128)(2,1)} %refs_4_.1), custom_call_target="tpu_custom_call" | custom-call | tf_op jit(solution)/shard_map/attention/pallas_call | solution.py:179
  8.1 1.8 %collective-permute-start.2 = (bf16[64,512]{1,0:T(8,128)(2,1)}, bf16[64,512]{1,0:T(8,128)(2,1)S(1)}, u32[]{:S(2)}, u32[]{:S(2)}) collective-permute-start(bf16[64,512]{1,0:T(8,128)(2,1)} %get-tuple-element.55), channel_id=1, source_target_pairs={{0,24},{8,16},{16,8},{24,0},{1,25},{9,17},{17,9},{25,1},{2,26},{10... | collective-permute-start | bytes 196616 | tf_op jit(solution)/shard_map/ppermute | solution.py:442
  9.9 4.0 %cast_rows.3 = (bf16[384,2048]{1,0:T(8,128)(2,1)}, bf16[256,2048]{1,0:T(8,128)(2,1)}) custom-call(f32[1,512,2048]{2,1,0:T(8,128)} %refs_0_.4, f32[1,256,2048]{2,1,0:T(8,128)} %refs_1_.3), custom_call_target="tpu_custom_call" | custom-call | tf_op jit(solution)/shard_map/cast_rows/pallas_call | solution.py:285
  13.9 5.3 %collective-permute-done.1.a2 = bf16[64,512]{1,0:T(8,128)(2,1)S(1)} collective-permute-done((bf16[64,512]{1,0:T(8,128)(2,1)}, bf16[64,512]{1,0:T(8,128)(2,1)S(1)}, u32[]{:S(2)}, u32[]{:S(2)}) %collective-permute-start.1) | collective-permute-done | bytes 65568 | tf_op jit(solution)/shard_map/ppermute | solution.py:442
  19.3 1.7 %collective-permute-start.14 = (bf16[384,2048]{1,0:T(8,128)(2,1)}, bf16[384,2048]{1,0:T(8,128)(2,1)S(1)}, u32[]{:S(2)}, u32[]{:S(2)}) collective-permute-start(bf16[384,2048]{1,0:T(8,128)(2,1)} %get-tuple-element.60.refs_10_), channel_id=1, source_target_pairs={{0,16},{8,24},{16,0},{24,8},{1,17},{9,25},{17,1},{25,9},{2,18},{10... | collective-permute-start | bytes 4718600 | tf_op jit(solution)/shard_map/ppermute | solution.py:442
  21.5 1.6 %collective-permute-start.7 = (bf16[64,2176]{1,0:T(8,128)(2,1)S(1)}, bf16[64,2176]{1,0:T(8,128)(2,1)S(1)}, u32[]{:S(2)}, u32[]{:S(2)}) collective-permute-start(bf16[64,2176]{1,0:T(8,128)(2,1)S(1)} %get-tuple-element.57.refs_0_), channel_id=1, source_target_pairs={{0,2},{2,4},{4,6},{6,7},{7,5},{5,3},{3,1},{1,0},{8,10},{10,12},{12... | collective-permute-start | bytes 835592 | tf_op jit(solution)/shard_map/ppermute | solution.py:452
  23.6 6.8 %collective-permute-done.7.refs_8_ = bf16[64,2176]{1,0:T(8,128)(2,1)S(1)} collective-permute-done((bf16[64,2176]{1,0:T(8,128)(2,1)S(1)}, bf16[64,2176]{1,0:T(8,128)(2,1)S(1)}, u32[]{:S(2)}, u32[]{:S(2)}) %collective-permute-start.7) | collective-permute-done | bytes 278560 | tf_op jit(solution)/shard_map/ppermute | solution.py:452
  31.7 1.6 %collective-permute-start.8 = (bf16[64,2176]{1,0:T(8,128)(2,1)S(1)}, bf16[64,2176]{1,0:T(8,128)(2,1)S(1)}, u32[]{:S(2)}, u32[]{:S(2)}) collective-permute-start(bf16[64,2176]{1,0:T(8,128)(2,1)S(1)} %collective-permute-done.7.refs_8_), channel_id=1, source_target_pairs={{0,2},{2,4},{4,6},{6,7},{7,5},{5,3},{3,1},{1,0},{8,10},{10,12},{12... | collective-permute-start | bytes 835592 | tf_op jit(solution)/shard_map/ppermute | solution.py:452
  33.7 7.0 %collective-permute-done.8.refs_7_ = bf16[64,2176]{1,0:T(8,128)(2,1)S(1)} collective-permute-done((bf16[64,2176]{1,0:T(8,128)(2,1)S(1)}, bf16[64,2176]{1,0:T(8,128)(2,1)S(1)}, u32[]{:S(2)}, u32[]{:S(2)}) %collective-permute-start.8) | collective-permute-done | bytes 278560 | tf_op jit(solution)/shard_map/ppermute | solution.py:452
  40.7 1.6 %collective-permute-start.9 = (bf16[64,2176]{1,0:T(8,128)(2,1)S(1)}, bf16[64,2176]{1,0:T(8,128)(2,1)S(1)}, u32[]{:S(2)}, u32[]{:S(2)}) collective-permute-start(bf16[64,2176]{1,0:T(8,128)(2,1)S(1)} %collective-permute-done.8.refs_7_), channel_id=1, source_target_pairs={{0,2},{2,4},{4,6},{6,7},{7,5},{5,3},{3,1},{1,0},{8,10},{10,12},{12... | collective-permute-start | bytes 835592 | tf_op jit(solution)/shard_map/ppermute | solution.py:452
  42.8 6.3 %collective-permute-done.9.refs_6_ = bf16[64,2176]{1,0:T(8,128)(2,1)S(1)} collective-permute-done((bf16[64,2176]{1,0:T(8,128)(2,1)S(1)}, bf16[64,2176]{1,0:T(8,128)(2,1)S(1)}, u32[]{:S(2)}, u32[]{:S(2)}) %collective-permute-start.9) | collective-permute-done | bytes 278560 | tf_op jit(solution)/shard_map/ppermute | solution.py:452
  49.0 1.6 %collective-permute-start.10 = (bf16[32,2176]{1,0:T(8,128)(2,1)S(1)}, bf16[32,2176]{1,0:T(8,128)(2,1)S(1)}, u32[]{:S(2)}, u32[]{:S(2)}) collective-permute-start(bf16[32,2176]{1,0:T(8,128)(2,1)S(1)} %slice.49), channel_id=1, source_target_pairs={{0,2},{2,4},{4,6},{6,7},{7,5},{5,3},{3,1},{1,0},{8,10},{10,12},{12... | collective-permute-start | bytes 417800 | tf_op jit(solution)/shard_map/ppermute | solution.py:452
  51.2 2.9 %collective-permute-done.10.refs_5_ = bf16[32,2176]{1,0:T(8,128)(2,1)S(1)} collective-permute-done((bf16[32,2176]{1,0:T(8,128)(2,1)S(1)}, bf16[32,2176]{1,0:T(8,128)(2,1)S(1)}, u32[]{:S(2)}, u32[]{:S(2)}) %collective-permute-start.10) | collective-permute-done | bytes 139296 | tf_op jit(solution)/shard_map/ppermute | solution.py:452
  60.4 8.3 %expert_up.1 = (bf16[512,1024]{1,0:T(8,128)(2,1)S(1)}, f32[512,1]{1,0:T(8,128)S(1)}) custom-call(bf16[64,2176]{1,0:T(8,128)(2,1)S(1)} %get-tuple-element.57.refs_0_, bf16[64,2176]{1,0:T(8,128)(2,1)S(1)} %collective-permute-done.3.refs_1_, bf16[64,2176]{1,0:T(8,128)(2,1)S(1)} %collective-permute-done.4.refs_2_, ...), custom_call_target="tpu_custom_call" | custom-call | flops 1 | bytes 1 | tf_op jit(solution)/shard_map/expert_up/pallas_call | solution.py:363
  68.7 10.0 %collective-permute-done.23.refs_4_ = bf16[256,2048]{1,0:T(8,128)(2,1)S(1)} collective-permute-done((bf16[256,2048]{1,0:T(8,128)(2,1)}, bf16[256,2048]{1,0:T(8,128)(2,1)S(1)}, u32[]{:S(2)}, u32[]{:S(2)}) %collective-permute-start.23) | collective-permute-done | bytes 1048608 | tf_op jit(solution)/shard_map/ppermute | solution.py:442
  79.4 1.4 %collective-permute-done.33.refs_5_ = bf16[256,1024]{1,0:T(8,128)(2,1)S(1)} collective-permute-done((bf16[256,1024]{1,0:T(8,128)(2,1)S(1)}, bf16[256,1024]{1,0:T(8,128)(2,1)S(1)}, u32[]{:S(2)}, u32[]{:S(2)}) %collective-permute-start.33) | collective-permute-done | bytes 524320 | tf_op jit(solution)/shard_map/ppermute | solution.py:442
  80.8 1.5 %expert_down.3 = (bf16[64,1024]{1,0:T(8,128)(2,1)S(1)}, bf16[32,1024]{1,0:T(8,128)(2,1)S(1)}, bf16[32,1024]{1,0:T(8,128)(2,1)S(1)}, bf16[32,1024]{1,0:T(8,128)(2...) custom-call(bf16[512,1024]{1,0:T(8,128)(2,1)S(1)} %get-tuple-element, ...), custom_call_target="tpu_custom_call" | custom-call | flops 1 | bytes 1 | tf_op jit(solution)/shard_map/expert_down/pallas_call | solution.py:423
  82.2 1.9 %collective-permute-start.34 = (bf16[32,1024]{1,0:T(8,128)(2,1)S(1)}, bf16[32,1024]{1,0:T(8,128)(2,1)S(1)}, u32[]{:S(2)}, u32[]{:S(2)}) collective-permute-start(bf16[32,1024]{1,0:T(8,128)(2,1)S(1)} %get-tuple-element.84), channel_id=1, source_target_pairs={{0,2},{2,4},{4,6},{6,7},{7,5},{5,3},{3,1},{1,0},{8,10},{10,12},{12... | collective-permute-start | bytes 196616 | tf_op jit(solution)/shard_map/ppermute | solution.py:452
  84.3 1.5 %expert_down.2 = (bf16[64,1024]{1,0:T(8,128)(2,1)S(1)}, bf16[32,1024]{1,0:T(8,128)(2,1)S(1)}, bf16[32,1024]{1,0:T(8,128)(2,1)S(1)}, bf16[32,1024]{1,0:T(8,128)(2...) custom-call(bf16[512,1024]{1,0:T(8,128)(2,1)S(1)} %get-tuple-element, ...), custom_call_target="tpu_custom_call" | custom-call | flops 1 | bytes 1 | tf_op jit(solution)/shard_map/expert_down/pallas_call | solution.py:423
  85.8 1.9 %collective-permute-start.25 = (bf16[32,1024]{1,0:T(8,128)(2,1)S(1)}, bf16[32,1024]{1,0:T(8,128)(2,1)S(1)}, u32[]{:S(2)}, u32[]{:S(2)}) collective-permute-start(bf16[32,1024]{1,0:T(8,128)(2,1)S(1)} %get-tuple-element.73), channel_id=1, source_target_pairs={{0,2},{2,4},{4,6},{6,7},{7,5},{5,3},{3,1},{1,0},{8,10},{10,12},{12... | collective-permute-start | bytes 196616 | tf_op jit(solution)/shard_map/ppermute | solution.py:452
  87.9 1.9 %collective-permute-start.35 = (bf16[64,1024]{1,0:T(8,128)(2,1)S(1)}, bf16[64,1024]{1,0:T(8,128)(2,1)S(1)}, u32[]{:S(2)}, u32[]{:S(2)}) collective-permute-start(bf16[64,1024]{1,0:T(8,128)(2,1)S(1)} %pad_maximum_fusion.2), channel_id=1, source_target_pairs={{0,2},{2,4},{4,6},{6,7},{7,5},{5,3},{3,1},{1,0},{8,10},{10,12},{12... | collective-permute-start | bytes 393224 | tf_op jit(solution)/shard_map/ppermute | solution.py:452
  90.5 2.1 %collective-permute-start.26 = (bf16[64,1024]{1,0:T(8,128)(2,1)S(1)}, bf16[64,1024]{1,0:T(8,128)(2,1)S(1)}, u32[]{:S(2)}, u32[]{:S(2)}) collective-permute-start(bf16[64,1024]{1,0:T(8,128)(2,1)S(1)} %pad_maximum_fusion), channel_id=1, source_target_pairs={{0,2},{2,4},{4,6},{6,7},{7,5},{5,3},{3,1},{1,0},{8,10},{10,12},{12... | collective-permute-start | bytes 393224 | tf_op jit(solution)/shard_map/ppermute | solution.py:452
  92.7 1.6 %collective-permute-done.35 = bf16[64,1024]{1,0:T(8,128)(2,1)S(1)} collective-permute-done((bf16[64,1024]{1,0:T(8,128)(2,1)S(1)}, bf16[64,1024]{1,0:T(8,128)(2,1)S(1)}, u32[]{:S(2)}, u32[]{:S(2)}) %collective-permute-start.35) | collective-permute-done | bytes 131104 | tf_op jit(solution)/shard_map/ppermute | solution.py:452
  94.4 1.9 %collective-permute-start.36 = (bf16[64,1024]{1,0:T(8,128)(2,1)S(1)}, bf16[64,1024]{1,0:T(8,128)(2,1)S(1)}, u32[]{:S(2)}, u32[]{:S(2)}) collective-permute-start(bf16[64,1024]{1,0:T(8,128)(2,1)S(1)} %add_convert_fusion.4), channel_id=1, source_target_pairs={{0,2},{2,4},{4,6},{6,7},{7,5},{5,3},{3,1},{1,0},{8,10},{10,12},{12... | collective-permute-start | bytes 393224 | tf_op jit(solution)/shard_map/ppermute | solution.py:452
  97.1 1.9 %collective-permute-start.27 = (bf16[64,1024]{1,0:T(8,128)(2,1)S(1)}, bf16[64,1024]{1,0:T(8,128)(2,1)S(1)}, u32[]{:S(2)}, u32[]{:S(2)}) collective-permute-start(bf16[64,1024]{1,0:T(8,128)(2,1)S(1)} %add_convert_fusion.9), channel_id=1, source_target_pairs={{0,2},{2,4},{4,6},{6,7},{7,5},{5,3},{3,1},{1,0},{8,10},{10,12},{12... | collective-permute-start | bytes 393224 | tf_op jit(solution)/shard_map/ppermute | solution.py:452
  100.0 1.9 %collective-permute-start.37 = (bf16[64,1024]{1,0:T(8,128)(2,1)S(1)}, bf16[64,1024]{1,0:T(8,128)(2,1)S(1)}, u32[]{:S(2)}, u32[]{:S(2)}) collective-permute-start(bf16[64,1024]{1,0:T(8,128)(2,1)S(1)} %add_convert_fusion.3), channel_id=1, source_target_pairs={{0,2},{2,4},{4,6},{6,7},{7,5},{5,3},{3,1},{1,0},{8,10},{10,12},{12... | collective-permute-start | bytes 393224 | tf_op jit(solution)/shard_map/ppermute | solution.py:452
  102.2 1.3 %collective-permute-done.27 = bf16[64,1024]{1,0:T(8,128)(2,1)S(1)} collective-permute-done((bf16[64,1024]{1,0:T(8,128)(2,1)S(1)}, bf16[64,1024]{1,0:T(8,128)(2,1)S(1)}, u32[]{:S(2)}, u32[]{:S(2)}) %collective-permute-start.27) | collective-permute-done | bytes 131104 | tf_op jit(solution)/shard_map/ppermute | solution.py:452
  103.5 1.9 %collective-permute-start.28 = (bf16[64,1024]{1,0:T(8,128)(2,1)S(1)}, bf16[64,1024]{1,0:T(8,128)(2,1)S(1)}, u32[]{:S(2)}, u32[]{:S(2)}) collective-permute-start(bf16[64,1024]{1,0:T(8,128)(2,1)S(1)} %add_convert_fusion.8), channel_id=1, source_target_pairs={{0,2},{2,4},{4,6},{6,7},{7,5},{5,3},{3,1},{1,0},{8,10},{10,12},{12... | collective-permute-start | bytes 393224 | tf_op jit(solution)/shard_map/ppermute | solution.py:452
  105.7 1.6 %collective-permute-done.41 = bf16[64,1024]{1,0:T(8,128)(2,1)S(1)} collective-permute-done((bf16[64,1024]{1,0:T(8,128)(2,1)S(1)}, bf16[64,1024]{1,0:T(8,128)(2,1)S(1)}, u32[]{:S(2)}, u32[]{:S(2)}) %collective-permute-start.41) | collective-permute-done | bytes 131104 | tf_op jit(solution)/shard_map/ppermute | solution.py:452
  108.6 2.1 %collective-permute-done.32 = bf16[64,1024]{1,0:T(8,128)(2,1)S(1)} collective-permute-done((bf16[64,1024]{1,0:T(8,128)(2,1)S(1)}, bf16[64,1024]{1,0:T(8,128)(2,1)S(1)}, u32[]{:S(2)}, u32[]{:S(2)}) %collective-permute-start.32) | collective-permute-done | bytes 131104 | tf_op jit(solution)/shard_map/ppermute | solution.py:452
  (99 shorter events, 16.7 us)
Async XLA Ops:
  1.9 17.3 %collective-permute-start.13 = (bf16[128,2048]{1,0:T(8,128)(2,1)}, bf16[128,2048]{1,0:T(8,128)(2,1)S(1)}, u32[]{:S(2)}, u32[]{:S(2)}) collective-permute-start(bf16[128,2048]{1,0:T(8,128)(2,1)} %cast_rows.2.refs_9_), channel_id=1, source_target_pairs={{0,16},{8,24},{16,0},{24,8},{1,17},{9,25},{17,1},{25,9},{2,18},{10... | collective-permute-start | bytes 1572872 | tf_op jit(solution)/shard_map/ppermute | solution.py:442
  7.9 6.0 %collective-permute-start = (bf16[64,512]{1,0:T(8,128)(2,1)}, bf16[64,512]{1,0:T(8,128)(2,1)S(1)}, u32[]{:S(2)}, u32[]{:S(2)}) collective-permute-start(bf16[64,512]{1,0:T(8,128)(2,1)} %get-tuple-element.53), channel_id=1, source_target_pairs={{0,8},{8,0},{16,24},{24,16},{1,9},{9,1},{17,25},{25,17},{2,10},{10... | collective-permute-start | bytes 196616 | tf_op jit(solution)/shard_map/ppermute | solution.py:442
  8.0 11.2 %collective-permute-start.1 = (bf16[64,512]{1,0:T(8,128)(2,1)}, bf16[64,512]{1,0:T(8,128)(2,1)S(1)}, u32[]{:S(2)}, u32[]{:S(2)}) collective-permute-start(bf16[64,512]{1,0:T(8,128)(2,1)} %get-tuple-element.54), channel_id=1, source_target_pairs={{0,16},{8,24},{16,0},{24,8},{1,17},{9,25},{17,1},{25,9},{2,18},{10... | collective-permute-start | bytes 196616 | tf_op jit(solution)/shard_map/ppermute | solution.py:442
  8.1 11.2 %collective-permute-start.2 = (bf16[64,512]{1,0:T(8,128)(2,1)}, bf16[64,512]{1,0:T(8,128)(2,1)S(1)}, u32[]{:S(2)}, u32[]{:S(2)}) collective-permute-start(bf16[64,512]{1,0:T(8,128)(2,1)} %get-tuple-element.55), channel_id=1, source_target_pairs={{0,24},{8,16},{16,8},{24,0},{1,25},{9,17},{17,9},{25,1},{2,26},{10... | collective-permute-start | bytes 196616 | tf_op jit(solution)/shard_map/ppermute | solution.py:442
  19.3 37.4 %collective-permute-start.14 = (bf16[384,2048]{1,0:T(8,128)(2,1)}, bf16[384,2048]{1,0:T(8,128)(2,1)S(1)}, u32[]{:S(2)}, u32[]{:S(2)}) collective-permute-start(bf16[384,2048]{1,0:T(8,128)(2,1)} %get-tuple-element.60.refs_10_), channel_id=1, source_target_pairs={{0,16},{8,24},{16,0},{24,8},{1,17},{9,25},{17,1},{25,9},{2,18},{10... | collective-permute-start | bytes 4718600 | tf_op jit(solution)/shard_map/ppermute | solution.py:442
  21.5 8.9 %collective-permute-start.7 = (bf16[64,2176]{1,0:T(8,128)(2,1)S(1)}, bf16[64,2176]{1,0:T(8,128)(2,1)S(1)}, u32[]{:S(2)}, u32[]{:S(2)}) collective-permute-start(bf16[64,2176]{1,0:T(8,128)(2,1)S(1)} %get-tuple-element.57.refs_0_), channel_id=1, source_target_pairs={{0,2},{2,4},{4,6},{6,7},{7,5},{5,3},{3,1},{1,0},{8,10},{10,12},{12... | collective-permute-start | bytes 835592 | tf_op jit(solution)/shard_map/ppermute | solution.py:452
  23.2 8.5 %collective-permute-start.3 = (bf16[64,2176]{1,0:T(8,128)(2,1)S(1)}, bf16[64,2176]{1,0:T(8,128)(2,1)S(1)}, u32[]{:S(2)}, u32[]{:S(2)}) collective-permute-start(bf16[64,2176]{1,0:T(8,128)(2,1)S(1)} %get-tuple-element.57.refs_0_), channel_id=1, source_target_pairs={{0,1},{2,0},{4,2},{6,4},{7,6},{5,7},{3,5},{1,3},{8,9},{10,8},{12,1... | collective-permute-start | bytes 835592 | tf_op jit(solution)/shard_map/ppermute | solution.py:452
  31.7 26.2 %collective-permute-start.12 = (bf16[384,2048]{1,0:T(8,128)(2,1)}, bf16[384,2048]{1,0:T(8,128)(2,1)S(1)}, u32[]{:S(2)}, u32[]{:S(2)}) collective-permute-start(bf16[384,2048]{1,0:T(8,128)(2,1)} %get-tuple-element.60.refs_10_), channel_id=1, source_target_pairs={{0,8},{8,0},{16,24},{24,16},{1,9},{9,1},{17,25},{25,17},{2,10},{10... | collective-permute-start | bytes 4718600 | tf_op jit(solution)/shard_map/ppermute | solution.py:442
  31.7 9.1 %collective-permute-start.8 = (bf16[64,2176]{1,0:T(8,128)(2,1)S(1)}, bf16[64,2176]{1,0:T(8,128)(2,1)S(1)}, u32[]{:S(2)}, u32[]{:S(2)}) collective-permute-start(bf16[64,2176]{1,0:T(8,128)(2,1)S(1)} %collective-permute-done.7.refs_8_), channel_id=1, source_target_pairs={{0,2},{2,4},{4,6},{6,7},{7,5},{5,3},{3,1},{1,0},{8,10},{10,12},{12... | collective-permute-start | bytes 835592 | tf_op jit(solution)/shard_map/ppermute | solution.py:452
  33.3 9.1 %collective-permute-start.4 = (bf16[64,2176]{1,0:T(8,128)(2,1)S(1)}, bf16[64,2176]{1,0:T(8,128)(2,1)S(1)}, u32[]{:S(2)}, u32[]{:S(2)}) collective-permute-start(bf16[64,2176]{1,0:T(8,128)(2,1)S(1)} %collective-permute-done.3.refs_1_), channel_id=1, source_target_pairs={{0,1},{2,0},{4,2},{6,4},{7,6},{5,7},{3,5},{1,3},{8,9},{10,8},{12,1... | collective-permute-start | bytes 835592 | tf_op jit(solution)/shard_map/ppermute | solution.py:452
  40.7 8.3 %collective-permute-start.9 = (bf16[64,2176]{1,0:T(8,128)(2,1)S(1)}, bf16[64,2176]{1,0:T(8,128)(2,1)S(1)}, u32[]{:S(2)}, u32[]{:S(2)}) collective-permute-start(bf16[64,2176]{1,0:T(8,128)(2,1)S(1)} %collective-permute-done.8.refs_7_), channel_id=1, source_target_pairs={{0,2},{2,4},{4,6},{6,7},{7,5},{5,3},{3,1},{1,0},{8,10},{10,12},{12... | collective-permute-start | bytes 835592 | tf_op jit(solution)/shard_map/ppermute | solution.py:452
  42.3 8.4 %collective-permute-start.5 = (bf16[64,2176]{1,0:T(8,128)(2,1)S(1)}, bf16[64,2176]{1,0:T(8,128)(2,1)S(1)}, u32[]{:S(2)}, u32[]{:S(2)}) collective-permute-start(bf16[64,2176]{1,0:T(8,128)(2,1)S(1)} %collective-permute-done.4.refs_2_), channel_id=1, source_target_pairs={{0,1},{2,0},{4,2},{6,4},{7,6},{5,7},{3,5},{1,3},{8,9},{10,8},{12,1... | collective-permute-start | bytes 835592 | tf_op jit(solution)/shard_map/ppermute | solution.py:452
  49.0 5.1 %collective-permute-start.10 = (bf16[32,2176]{1,0:T(8,128)(2,1)S(1)}, bf16[32,2176]{1,0:T(8,128)(2,1)S(1)}, u32[]{:S(2)}, u32[]{:S(2)}) collective-permute-start(bf16[32,2176]{1,0:T(8,128)(2,1)S(1)} %slice.49), channel_id=1, source_target_pairs={{0,2},{2,4},{4,6},{6,7},{7,5},{5,3},{3,1},{1,0},{8,10},{10,12},{12... | collective-permute-start | bytes 417800 | tf_op jit(solution)/shard_map/ppermute | solution.py:452
  50.7 5.1 %collective-permute-start.6 = (bf16[32,2176]{1,0:T(8,128)(2,1)S(1)}, bf16[32,2176]{1,0:T(8,128)(2,1)S(1)}, u32[]{:S(2)}, u32[]{:S(2)}) collective-permute-start(bf16[32,2176]{1,0:T(8,128)(2,1)S(1)} %slice.48), channel_id=1, source_target_pairs={{0,1},{2,0},{4,2},{6,4},{7,6},{5,7},{3,5},{1,3},{8,9},{10,8},{12,1... | collective-permute-start | bytes 417800 | tf_op jit(solution)/shard_map/ppermute | solution.py:452
  51.2 5.7 %collective-permute-start.11 = (bf16[128,2048]{1,0:T(8,128)(2,1)S(1)}, bf16[128,2048]{1,0:T(8,128)(2,1)S(1)}, u32[]{:S(2)}, u32[]{:S(2)}) collective-permute-start(bf16[128,2048]{1,0:T(8,128)(2,1)S(1)} %copy-done.1), channel_id=1, source_target_pairs={{0,8},{8,0},{16,24},{24,16},{1,9},{9,1},{17,25},{25,17},{2,10},{10... | collective-permute-start | bytes 1572872 | tf_op jit(solution)/shard_map/ppermute | solution.py:442
  54.2 24.5 %collective-permute-start.23 = (bf16[256,2048]{1,0:T(8,128)(2,1)}, bf16[256,2048]{1,0:T(8,128)(2,1)S(1)}, u32[]{:S(2)}, u32[]{:S(2)}) collective-permute-start(bf16[256,2048]{1,0:T(8,128)(2,1)} %get-tuple-element.67.refs_2_), channel_id=1, source_target_pairs={{0,16},{8,24},{16,0},{24,8},{1,17},{9,25},{17,1},{25,9},{2,18},{10... | collective-permute-start | bytes 3145736 | tf_op jit(solution)/shard_map/ppermute | solution.py:442
  59.3 20.1 %collective-permute-start.22 = (bf16[256,2048]{1,0:T(8,128)(2,1)S(1)}, bf16[256,2048]{1,0:T(8,128)(2,1)S(1)}, u32[]{:S(2)}, u32[]{:S(2)}) collective-permute-start(bf16[256,2048]{1,0:T(8,128)(2,1)S(1)} %copy-done), channel_id=1, source_target_pairs={{0,8},{8,0},{16,24},{24,16},{1,9},{9,1},{17,25},{25,17},{2,10},{10... | collective-permute-start | bytes 3145736 | tf_op jit(solution)/shard_map/ppermute | solution.py:442
  78.9 5.5 %collective-permute-start.24 = (bf16[256,1024]{1,0:T(8,128)(2,1)S(1)}, bf16[256,1024]{1,0:T(8,128)(2,1)S(1)}, u32[]{:S(2)}, u32[]{:S(2)}) collective-permute-start(bf16[256,1024]{1,0:T(8,128)(2,1)S(1)} %get-tuple-element.97), channel_id=1, source_target_pairs={{0,8},{8,0},{16,24},{24,16},{1,9},{9,1},{17,25},{25,17},{2,10},{10... | collective-permute-start | bytes 1572872 | tf_op jit(solution)/shard_map/ppermute | solution.py:442
  82.2 5.6 %collective-permute-start.34 = (bf16[32,1024]{1,0:T(8,128)(2,1)S(1)}, bf16[32,1024]{1,0:T(8,128)(2,1)S(1)}, u32[]{:S(2)}, u32[]{:S(2)}) collective-permute-start(bf16[32,1024]{1,0:T(8,128)(2,1)S(1)} %get-tuple-element.84), channel_id=1, source_target_pairs={{0,2},{2,4},{4,6},{6,7},{7,5},{5,3},{3,1},{1,0},{8,10},{10,12},{12... | collective-permute-start | bytes 196616 | tf_op jit(solution)/shard_map/ppermute | solution.py:452
  84.1 5.7 %collective-permute-start.38 = (bf16[32,1024]{1,0:T(8,128)(2,1)S(1)}, bf16[32,1024]{1,0:T(8,128)(2,1)S(1)}, u32[]{:S(2)}, u32[]{:S(2)}) collective-permute-start(bf16[32,1024]{1,0:T(8,128)(2,1)S(1)} %get-tuple-element.90), channel_id=1, source_target_pairs={{0,1},{2,0},{4,2},{6,4},{7,6},{5,7},{3,5},{1,3},{8,9},{10,8},{12,1... | collective-permute-start | bytes 196616 | tf_op jit(solution)/shard_map/ppermute | solution.py:452
  87.9 6.4 %collective-permute-start.35 = (bf16[64,1024]{1,0:T(8,128)(2,1)S(1)}, bf16[64,1024]{1,0:T(8,128)(2,1)S(1)}, u32[]{:S(2)}, u32[]{:S(2)}) collective-permute-start(bf16[64,1024]{1,0:T(8,128)(2,1)S(1)} %pad_maximum_fusion.2), channel_id=1, source_target_pairs={{0,2},{2,4},{4,6},{6,7},{7,5},{5,3},{3,1},{1,0},{8,10},{10,12},{12... | collective-permute-start | bytes 393224 | tf_op jit(solution)/shard_map/ppermute | solution.py:452
  89.8 6.4 %collective-permute-start.39 = (bf16[64,1024]{1,0:T(8,128)(2,1)S(1)}, bf16[64,1024]{1,0:T(8,128)(2,1)S(1)}, u32[]{:S(2)}, u32[]{:S(2)}) collective-permute-start(bf16[64,1024]{1,0:T(8,128)(2,1)S(1)} %pad_maximum_fusion.3), channel_id=1, source_target_pairs={{0,1},{2,0},{4,2},{6,4},{7,6},{5,7},{3,5},{1,3},{8,9},{10,8},{12,1... | collective-permute-start | bytes 393224 | tf_op jit(solution)/shard_map/ppermute | solution.py:452
  90.5 6.6 %collective-permute-start.26 = (bf16[64,1024]{1,0:T(8,128)(2,1)S(1)}, bf16[64,1024]{1,0:T(8,128)(2,1)S(1)}, u32[]{:S(2)}, u32[]{:S(2)}) collective-permute-start(bf16[64,1024]{1,0:T(8,128)(2,1)S(1)} %pad_maximum_fusion), channel_id=1, source_target_pairs={{0,2},{2,4},{4,6},{6,7},{7,5},{5,3},{3,1},{1,0},{8,10},{10,12},{12... | collective-permute-start | bytes 393224 | tf_op jit(solution)/shard_map/ppermute | solution.py:452
  92.7 6.4 %collective-permute-start.30 = (bf16[64,1024]{1,0:T(8,128)(2,1)S(1)}, bf16[64,1024]{1,0:T(8,128)(2,1)S(1)}, u32[]{:S(2)}, u32[]{:S(2)}) collective-permute-start(bf16[64,1024]{1,0:T(8,128)(2,1)S(1)} %pad_maximum_fusion.1), channel_id=1, source_target_pairs={{0,1},{2,0},{4,2},{6,4},{7,6},{5,7},{3,5},{1,3},{8,9},{10,8},{12,1... | collective-permute-start | bytes 393224 | tf_op jit(solution)/shard_map/ppermute | solution.py:452
  94.4 5.6 %collective-permute-start.36 = (bf16[64,1024]{1,0:T(8,128)(2,1)S(1)}, bf16[64,1024]{1,0:T(8,128)(2,1)S(1)}, u32[]{:S(2)}, u32[]{:S(2)}) collective-permute-start(bf16[64,1024]{1,0:T(8,128)(2,1)S(1)} %add_convert_fusion.4), channel_id=1, source_target_pairs={{0,2},{2,4},{4,6},{6,7},{7,5},{5,3},{3,1},{1,0},{8,10},{10,12},{12... | collective-permute-start | bytes 393224 | tf_op jit(solution)/shard_map/ppermute | solution.py:452
  96.3 5.6 %collective-permute-start.40 = (bf16[64,1024]{1,0:T(8,128)(2,1)S(1)}, bf16[64,1024]{1,0:T(8,128)(2,1)S(1)}, u32[]{:S(2)}, u32[]{:S(2)}) collective-permute-start(bf16[64,1024]{1,0:T(8,128)(2,1)S(1)} %add_convert_fusion.2), channel_id=1, source_target_pairs={{0,1},{2,0},{4,2},{6,4},{7,6},{5,7},{3,5},{1,3},{8,9},{10,8},{12,1... | collective-permute-start | bytes 393224 | tf_op jit(solution)/shard_map/ppermute | solution.py:452
  97.1 6.4 %collective-permute-start.27 = (bf16[64,1024]{1,0:T(8,128)(2,1)S(1)}, bf16[64,1024]{1,0:T(8,128)(2,1)S(1)}, u32[]{:S(2)}, u32[]{:S(2)}) collective-permute-start(bf16[64,1024]{1,0:T(8,128)(2,1)S(1)} %add_convert_fusion.9), channel_id=1, source_target_pairs={{0,2},{2,4},{4,6},{6,7},{7,5},{5,3},{3,1},{1,0},{8,10},{10,12},{12... | collective-permute-start | bytes 393224 | tf_op jit(solution)/shard_map/ppermute | solution.py:452
  99.1 6.4 %collective-permute-start.31 = (bf16[64,1024]{1,0:T(8,128)(2,1)S(1)}, bf16[64,1024]{1,0:T(8,128)(2,1)S(1)}, u32[]{:S(2)}, u32[]{:S(2)}) collective-permute-start(bf16[64,1024]{1,0:T(8,128)(2,1)S(1)} %add_convert_fusion.7), channel_id=1, source_target_pairs={{0,1},{2,0},{4,2},{6,4},{7,6},{5,7},{3,5},{1,3},{8,9},{10,8},{12,1... | collective-permute-start | bytes 393224 | tf_op jit(solution)/shard_map/ppermute | solution.py:452
  100.0 5.8 %collective-permute-start.37 = (bf16[64,1024]{1,0:T(8,128)(2,1)S(1)}, bf16[64,1024]{1,0:T(8,128)(2,1)S(1)}, u32[]{:S(2)}, u32[]{:S(2)}) collective-permute-start(bf16[64,1024]{1,0:T(8,128)(2,1)S(1)} %add_convert_fusion.3), channel_id=1, source_target_pairs={{0,2},{2,4},{4,6},{6,7},{7,5},{5,3},{3,1},{1,0},{8,10},{10,12},{12... | collective-permute-start | bytes 393224 | tf_op jit(solution)/shard_map/ppermute | solution.py:452
  101.9 5.5 %collective-permute-start.41 = (bf16[64,1024]{1,0:T(8,128)(2,1)S(1)}, bf16[64,1024]{1,0:T(8,128)(2,1)S(1)}, u32[]{:S(2)}, u32[]{:S(2)}) collective-permute-start(bf16[64,1024]{1,0:T(8,128)(2,1)S(1)} %add_convert_fusion.1), channel_id=1, source_target_pairs={{0,1},{2,0},{4,2},{6,4},{7,6},{5,7},{3,5},{1,3},{8,9},{10,8},{12,1... | collective-permute-start | bytes 393224 | tf_op jit(solution)/shard_map/ppermute | solution.py:452
  103.5 5.0 %collective-permute-start.28 = (bf16[64,1024]{1,0:T(8,128)(2,1)S(1)}, bf16[64,1024]{1,0:T(8,128)(2,1)S(1)}, u32[]{:S(2)}, u32[]{:S(2)}) collective-permute-start(bf16[64,1024]{1,0:T(8,128)(2,1)S(1)} %add_convert_fusion.8), channel_id=1, source_target_pairs={{0,2},{2,4},{4,6},{6,7},{7,5},{5,3},{3,1},{1,0},{8,10},{10,12},{12... | collective-permute-start | bytes 393224 | tf_op jit(solution)/shard_map/ppermute | solution.py:452
  105.6 5.0 %collective-permute-start.32 = (bf16[64,1024]{1,0:T(8,128)(2,1)S(1)}, bf16[64,1024]{1,0:T(8,128)(2,1)S(1)}, u32[]{:S(2)}, u32[]{:S(2)}) collective-permute-start(bf16[64,1024]{1,0:T(8,128)(2,1)S(1)} %add_convert_fusion.6), channel_id=1, source_target_pairs={{0,1},{2,0},{4,2},{6,4},{7,6},{5,7},{3,5},{1,3},{8,9},{10,8},{12,1... | collective-permute-start | bytes 393224 | tf_op jit(solution)/shard_map/ppermute | solution.py:452
  (18 other events, 137.9 us)

commit v11 on v10

--- a/solution.py
+++ b/solution.py
@@ -380,25 +380,54 @@
     )(*rows, *weights)
 
 
-def down_kernel(columns, sources, hidden_ref, gate_ref, *refs):
-    (weights, arrived), refs = refs[-2:], refs[:-2]
-    pieces, outs = refs[: len(refs) - sources - 3], refs[len(refs) - sources - 3 :]
+def load_rows(pieces, weights, arrived):
     copies, first = [], 0
-    for i, (ref, column) in enumerate(zip(pieces, columns)):
+    for i, ref in enumerate(pieces):
         depth = ref.shape[0]
         copies.append(
-            pltpu.make_async_copy(
-                ref.at[:, pl.ds(column, weights.shape[1])],
-                weights.at[pl.ds(first, depth)],
-                arrived.at[i],
-            )
+            pltpu.make_async_copy(ref, weights.at[pl.ds(first, depth)], arrived.at[i])
         )
         first += depth
     for copy in copies:
         copy.start()
     for copy in copies:
         copy.wait()
-    total = jnp.dot(hidden_ref[...], weights[...], preferred_element_type=jnp.float32)
+
+
+def part_kernel(hidden_ref, *refs):
+    pieces, (total_ref, weights, arrived) = refs[:-3], refs[-3:]
+    load_rows(pieces, weights, arrived)
+    total_ref[...] = jnp.dot(
+        hidden_ref[:, : weights.shape[0]], weights[...], preferred_element_type=jnp.float32
+    )
+
+
+def down_part(hidden_units, weights):
+    depth = sum(piece.shape[0] for piece in weights)
+    shape = hidden_units.shape[0], weights[0].shape[1]
+    return pl.pallas_call(
+        part_kernel,
+        out_shape=jax.ShapeDtypeStruct(shape, jnp.float32),
+        in_specs=vmem(1) + [pl.BlockSpec(memory_space=pl.ANY)] * len(weights),
+        out_specs=pl.BlockSpec(memory_space=pltpu.VMEM),
+        scratch_shapes=[
+            pltpu.VMEM((depth, shape[1]), jnp.bfloat16),
+            pltpu.SemaphoreType.DMA((len(weights),)),
+        ],
+        compiler_params=params(),
+        cost_estimate=SMALL,
+        name="down_part",
+    )(hidden_units, *weights)
+
+
+def down_kernel(first, column, sources, hidden_ref, total_ref, gate_ref, piece, *refs):
+    outs, (weights, arrived) = refs[:-2], refs[-2:]
+    load_rows([piece], weights, arrived)
+    depth, width = weights.shape
+    units = hidden_ref[:, first : first + depth]
+    total = total_ref[:, column : column + width] + jnp.dot(
+        units, weights[...], preferred_element_type=jnp.float32
+    )
     weighted = (total * gate_ref[...]).astype(jnp.bfloat16)
     rows = weighted.shape[0] // sources
     for (first, count), ref in zip(down_blocks(rows, sources), outs):
@@ -416,26 +445,26 @@
     return blocks
 
 
-def expert_down(hidden_units, gates, weights, width, sources):
-    weights, columns = zip(*weights)
+def expert_down(hidden_units, total, gates, weights, column, sources):
     tokens, hidden_size = hidden_units.shape
+    depth, width = weights.shape
     rows = tokens // sources
     return pl.pallas_call(
-        lambda *refs: down_kernel(columns, sources, *refs),
+        lambda *refs: down_kernel(hidden_size - depth, column, sources, *refs),
         out_shape=[
             jax.ShapeDtypeStruct((count, width), jnp.bfloat16)
             for _, count in down_blocks(rows, sources)
         ],
-        in_specs=vmem(2) + [pl.BlockSpec(memory_space=pl.ANY)] * len(weights),
+        in_specs=vmem(3) + [pl.BlockSpec(memory_space=pl.ANY)],
         out_specs=vmem(sources + 3),
         scratch_shapes=[
-            pltpu.VMEM((hidden_size, width), jnp.bfloat16),
-            pltpu.SemaphoreType.DMA((len(weights),)),
+            pltpu.VMEM((depth, width), jnp.bfloat16),
+            pltpu.SemaphoreType.DMA((1,)),
         ],
         compiler_params=params(),
         cost_estimate=SMALL,
         name="expert_down",
-    )(hidden_units, gates, *weights)
+    )(hidden_units, total, gates, weights)
 
 
 def partner(x, distance):
@@ -536,15 +565,15 @@
         + [first_across, rest_across, first_opposite, *rest_opposite],
     )
     down_ready = after(down_across, hidden_units)
+    total = down_part(hidden_units, [down_own, down_beside, down_ready])
     mixed = []
     for first in range(0, width, slab):
         opposite = partner(down_ready[:, first : first + slab], 1)
-        weights = [(down_own, first), (down_beside, first), (down_across, first), (opposite, 0)]
-        weighted = expert_down(hidden_units, gates, weights, slab, expert_count)
-        total = resid[:, first : first + slab].astype(jnp.float32)
+        weighted = expert_down(hidden_units, total, gates, opposite, first, expert_count)
+        sum_here = resid[:, first : first + slab].astype(jnp.float32)
         for term in scatter_sum(*weighted):
-            total = total + term.astype(jnp.float32)
-        mixed.append(total.astype(jnp.bfloat16))
+            sum_here = sum_here + term.astype(jnp.float32)
+        mixed.append(sum_here.astype(jnp.bfloat16))
     return jnp.concatenate(mixed, axis=1)[None]
 
 

time: 112 us -> 110 us (0.982)
  waiting for transfers between devices: 54.9 us -> 53 us
    ppermute x18, waiting for transfers between devices: 19.7 us -> 18.3 us  [partner(): return lax.ppermute(x, 'dp', [(i, i ^ distance) for i in range(4)])]
    pallas_call x2 -> x3, Pallas kernels: 2.95 us -> 3.04 us  [the longest x1 2.04 us: down_part(): pl.pallas_call(part_kernel, out_shape=jax.ShapeDtypeStruct(shape, jnp.flo...]
  transfers between devices with their start and end apart: 42 -> 42, of which waited for: 29 -> 26; matrix products, arithmetic and copies ran while one was open for 1% -> 1% of each run, Pallas kernels for 17% -> 17%
where the time goes in v11:
time: 110 us
  waiting for transfers between devices  53 us (48%)
  starting transfers between devices  34.6 us (31%)
  Pallas kernels  20.6 us (19%)
  other arithmetic  1.28 us (1%)
    ppermute x24, waiting for transfers between devices, around(): lax.ppermute(x, 'expert', [(ring[i], ring[(i + step) % count]) for i in r...  34.7 us
    ppermute x24, starting transfers between devices, around(): lax.ppermute(x, 'expert', [(ring[i], ring[(i + step) % count]) for i in r...  25.4 us
    ppermute x18, waiting for transfers between devices, partner(): return lax.ppermute(x, 'dp', [(i, i ^ distance) for i in range(4)])  18.3 us
    ppermute x18, starting transfers between devices, partner(): return lax.ppermute(x, 'dp', [(i, i ^ distance) for i in range(4)])  9.21 us
    pallas_call x1, Pallas kernels, expert_up(): pl.pallas_call(lambda *refs: up_kernel(len(rows), len(weights), *refs), o...  8.28 us
    pallas_call x2, Pallas kernels, cast_rows(): pl.pallas_call(lambda *refs: cast_kernel(spans, *refs), out_shape=[jax.Sh...  5.92 us
    pallas_call x1, Pallas kernels, attention(): pl.pallas_call(attention_kernel, out_shape=[jax.ShapeDtypeStruct((tokens...  2.98 us
  transfers between devices with their start and end apart: 42, of which 26 were waited for; matrix products, arithmetic and copies ran while one was open for 1% of the time, Pallas kernels for 17%

profile of v11, /device:TPU:0, one launch (start us, length us, event | category | flops | bytes accessed | tf_op | source)
XLA Modules:
  0.0 110.3 jit_solution(976182193327180014)
XLA Ops:
  0.0 1.9 %cast_rows.2.refs_9_ = bf16[128,2048]{1,0:T(8,128)(2,1)} custom-call(f32[1,512,2048]{2,1,0:T(8,128)} %refs_0_.4), custom_call_target="tpu_custom_call" | custom-call | tf_op jit(solution)/shard_map/cast_rows/pallas_call | solution.py:285
  1.9 3.0 %collective-permute-start.13 = (bf16[128,2048]{1,0:T(8,128)(2,1)}, bf16[128,2048]{1,0:T(8,128)(2,1)S(1)}, u32[]{:S(2)}, u32[]{:S(2)}) collective-permute-start(bf16[128,2048]{1,0:T(8,128)(2,1)} %cast_rows.2.refs_9_), channel_id=1, source_target_pairs={{0,16},{8,24},{16,0},{24,8},{1,17},{9,25},{17,1},{25,9},{2,18},{10... | collective-permute-start | bytes 1572872 | tf_op jit(solution)/shard_map/ppermute | solution.py:471
  4.9 3.0 %attention.1 = (bf16[64,512]{1,0:T(8,128)(2,1)}, bf16[64,512]{1,0:T(8,128)(2,1)}, bf16[64,512]{1,0:T(8,128)(2,1)}, bf16[64,512]{1,0:T(8,128)(2,1)}) custom-call(s32[1,2]{1,0:T(1,128)} %refs_0_.3, s32[1,4]{1,0:T(1,128)} %refs_1_.2, bf16[1,256,512]{2,1,0:T(8,128)(2,1)} %refs_2_, bf16[2,128,512]{2,1,0:T(8,128)(2,1)} %refs_3_.1, bf16[2,128,512]{2,1,0:T(8,128)(2,1)} %refs_4_.1), custom_call_target="tpu_custom_call" | custom-call | tf_op jit(solution)/shard_map/attention/pallas_call | solution.py:179
  8.1 1.8 %collective-permute-start.2 = (bf16[64,512]{1,0:T(8,128)(2,1)}, bf16[64,512]{1,0:T(8,128)(2,1)S(1)}, u32[]{:S(2)}, u32[]{:S(2)}) collective-permute-start(bf16[64,512]{1,0:T(8,128)(2,1)} %get-tuple-element.55), channel_id=1, source_target_pairs={{0,24},{8,16},{16,8},{24,0},{1,25},{9,17},{17,9},{25,1},{2,26},{10... | collective-permute-start | bytes 196616 | tf_op jit(solution)/shard_map/ppermute | solution.py:471
  9.9 4.0 %cast_rows.3 = (bf16[384,2048]{1,0:T(8,128)(2,1)}, bf16[256,2048]{1,0:T(8,128)(2,1)}) custom-call(f32[1,512,2048]{2,1,0:T(8,128)} %refs_0_.4, f32[1,256,2048]{2,1,0:T(8,128)} %refs_1_.3), custom_call_target="tpu_custom_call" | custom-call | tf_op jit(solution)/shard_map/cast_rows/pallas_call | solution.py:285
  13.9 5.3 %collective-permute-done.1.a2 = bf16[64,512]{1,0:T(8,128)(2,1)S(1)} collective-permute-done((bf16[64,512]{1,0:T(8,128)(2,1)}, bf16[64,512]{1,0:T(8,128)(2,1)S(1)}, u32[]{:S(2)}, u32[]{:S(2)}) %collective-permute-start.1) | collective-permute-done | bytes 65568 | tf_op jit(solution)/shard_map/ppermute | solution.py:471
  19.3 1.7 %collective-permute-start.14 = (bf16[384,2048]{1,0:T(8,128)(2,1)}, bf16[384,2048]{1,0:T(8,128)(2,1)S(1)}, u32[]{:S(2)}, u32[]{:S(2)}) collective-permute-start(bf16[384,2048]{1,0:T(8,128)(2,1)} %get-tuple-element.60.refs_10_), channel_id=1, source_target_pairs={{0,16},{8,24},{16,0},{24,8},{1,17},{9,25},{17,1},{25,9},{2,18},{10... | collective-permute-start | bytes 4718600 | tf_op jit(solution)/shard_map/ppermute | solution.py:471
  21.5 1.6 %collective-permute-start.7 = (bf16[64,2176]{1,0:T(8,128)(2,1)S(1)}, bf16[64,2176]{1,0:T(8,128)(2,1)S(1)}, u32[]{:S(2)}, u32[]{:S(2)}) collective-permute-start(bf16[64,2176]{1,0:T(8,128)(2,1)S(1)} %get-tuple-element.57.refs_0_), channel_id=1, source_target_pairs={{0,2},{2,4},{4,6},{6,7},{7,5},{5,3},{3,1},{1,0},{8,10},{10,12},{12... | collective-permute-start | bytes 835592 | tf_op jit(solution)/shard_map/ppermute | solution.py:481
  23.6 6.8 %collective-permute-done.7.refs_8_ = bf16[64,2176]{1,0:T(8,128)(2,1)S(1)} collective-permute-done((bf16[64,2176]{1,0:T(8,128)(2,1)S(1)}, bf16[64,2176]{1,0:T(8,128)(2,1)S(1)}, u32[]{:S(2)}, u32[]{:S(2)}) %collective-permute-start.7) | collective-permute-done | bytes 278560 | tf_op jit(solution)/shard_map/ppermute | solution.py:481
  30.4 1.3 %collective-permute-done.3.refs_1_ = bf16[64,2176]{1,0:T(8,128)(2,1)S(1)} collective-permute-done((bf16[64,2176]{1,0:T(8,128)(2,1)S(1)}, bf16[64,2176]{1,0:T(8,128)(2,1)S(1)}, u32[]{:S(2)}, u32[]{:S(2)}) %collective-permute-start.3) | collective-permute-done | bytes 278560 | tf_op jit(solution)/shard_map/ppermute | solution.py:481
  31.7 1.6 %collective-permute-start.8 = (bf16[64,2176]{1,0:T(8,128)(2,1)S(1)}, bf16[64,2176]{1,0:T(8,128)(2,1)S(1)}, u32[]{:S(2)}, u32[]{:S(2)}) collective-permute-start(bf16[64,2176]{1,0:T(8,128)(2,1)S(1)} %collective-permute-done.7.refs_8_), channel_id=1, source_target_pairs={{0,2},{2,4},{4,6},{6,7},{7,5},{5,3},{3,1},{1,0},{8,10},{10,12},{12... | collective-permute-start | bytes 835592 | tf_op jit(solution)/shard_map/ppermute | solution.py:481
  33.7 7.0 %collective-permute-done.8.refs_7_ = bf16[64,2176]{1,0:T(8,128)(2,1)S(1)} collective-permute-done((bf16[64,2176]{1,0:T(8,128)(2,1)S(1)}, bf16[64,2176]{1,0:T(8,128)(2,1)S(1)}, u32[]{:S(2)}, u32[]{:S(2)}) %collective-permute-start.8) | collective-permute-done | bytes 278560 | tf_op jit(solution)/shard_map/ppermute | solution.py:481
  40.7 1.6 %collective-permute-start.9 = (bf16[64,2176]{1,0:T(8,128)(2,1)S(1)}, bf16[64,2176]{1,0:T(8,128)(2,1)S(1)}, u32[]{:S(2)}, u32[]{:S(2)}) collective-permute-start(bf16[64,2176]{1,0:T(8,128)(2,1)S(1)} %collective-permute-done.8.refs_7_), channel_id=1, source_target_pairs={{0,2},{2,4},{4,6},{6,7},{7,5},{5,3},{3,1},{1,0},{8,10},{10,12},{12... | collective-permute-start | bytes 835592 | tf_op jit(solution)/shard_map/ppermute | solution.py:481
  42.8 6.3 %collective-permute-done.9.refs_6_ = bf16[64,2176]{1,0:T(8,128)(2,1)S(1)} collective-permute-done((bf16[64,2176]{1,0:T(8,128)(2,1)S(1)}, bf16[64,2176]{1,0:T(8,128)(2,1)S(1)}, u32[]{:S(2)}, u32[]{:S(2)}) %collective-permute-start.9) | collective-permute-done | bytes 278560 | tf_op jit(solution)/shard_map/ppermute | solution.py:481
  49.0 1.6 %collective-permute-start.10 = (bf16[32,2176]{1,0:T(8,128)(2,1)S(1)}, bf16[32,2176]{1,0:T(8,128)(2,1)S(1)}, u32[]{:S(2)}, u32[]{:S(2)}) collective-permute-start(bf16[32,2176]{1,0:T(8,128)(2,1)S(1)} %slice.49), channel_id=1, source_target_pairs={{0,2},{2,4},{4,6},{6,7},{7,5},{5,3},{3,1},{1,0},{8,10},{10,12},{12... | collective-permute-start | bytes 417800 | tf_op jit(solution)/shard_map/ppermute | solution.py:481
  51.2 2.9 %collective-permute-done.10.refs_5_ = bf16[32,2176]{1,0:T(8,128)(2,1)S(1)} collective-permute-done((bf16[32,2176]{1,0:T(8,128)(2,1)S(1)}, bf16[32,2176]{1,0:T(8,128)(2,1)S(1)}, u32[]{:S(2)}, u32[]{:S(2)}) %collective-permute-start.10) | collective-permute-done | bytes 139296 | tf_op jit(solution)/shard_map/ppermute | solution.py:481
  54.7 1.1 %collective-permute-done.6.refs_4_ = bf16[32,2176]{1,0:T(8,128)(2,1)S(1)} collective-permute-done((bf16[32,2176]{1,0:T(8,128)(2,1)S(1)}, bf16[32,2176]{1,0:T(8,128)(2,1)S(1)}, u32[]{:S(2)}, u32[]{:S(2)}) %collective-permute-start.6) | collective-permute-done | bytes 139296 | tf_op jit(solution)/shard_map/ppermute | solution.py:481
  60.4 8.3 %expert_up.1 = (bf16[512,1024]{1,0:T(8,128)(2,1)S(1)}, f32[512,1]{1,0:T(8,128)S(1)}) custom-call(bf16[64,2176]{1,0:T(8,128)(2,1)S(1)} %get-tuple-element.57.refs_0_, bf16[64,2176]{1,0:T(8,128)(2,1)S(1)} %collective-permute-done.3.refs_1_, bf16[64,2176]{1,0:T(8,128)(2,1)S(1)} %collective-permute-done.4.refs_2_, ...), custom_call_target="tpu_custom_call" | custom-call | flops 1 | bytes 1 | tf_op jit(solution)/shard_map/expert_up/pallas_call | solution.py:363
  68.7 10.0 %collective-permute-done.23.refs_2_ = bf16[256,2048]{1,0:T(8,128)(2,1)S(1)} collective-permute-done((bf16[256,2048]{1,0:T(8,128)(2,1)}, bf16[256,2048]{1,0:T(8,128)(2,1)S(1)}, u32[]{:S(2)}, u32[]{:S(2)}) %collective-permute-start.23) | collective-permute-done | bytes 1048608 | tf_op jit(solution)/shard_map/ppermute | solution.py:471
  79.4 2.0 %down_part.1.refs_1_ = f32[512,2048]{1,0:T(8,128)S(1)} custom-call(bf16[512,1024]{1,0:T(8,128)(2,1)S(1)} %get-tuple-element.63.hidden_ref.refs_0_, bf16[256,2048]{1,0:T(8,128)(2,1)S(1)} %copy-done.2, bf16[256,2048]{1,0:T(8,128)(2,1)S(1)} %collective-permute-done.22.refs_1_, bf16[256,2048]{1,0:T(8,128)(2,1)S(1)} %collective-permute-done.23.refs_2_), custom_call_target="tpu_custom_call" | custom-call | flops 1 | bytes 1 | tf_op jit(solution)/shard_map/down_part/pallas_call | solution.py:408
  81.9 1.9 %collective-permute-start.34 = (bf16[32,1024]{1,0:T(8,128)(2,1)S(1)}, bf16[32,1024]{1,0:T(8,128)(2,1)S(1)}, u32[]{:S(2)}, u32[]{:S(2)}) collective-permute-start(bf16[32,1024]{1,0:T(8,128)(2,1)S(1)} %get-tuple-element.84), channel_id=1, source_target_pairs={{0,2},{2,4},{4,6},{6,7},{7,5},{5,3},{3,1},{1,0},{8,10},{10,12},{12... | collective-permute-start | bytes 196616 | tf_op jit(solution)/shard_map/ppermute | solution.py:481
  84.5 1.9 %collective-permute-start.25 = (bf16[32,1024]{1,0:T(8,128)(2,1)S(1)}, bf16[32,1024]{1,0:T(8,128)(2,1)S(1)}, u32[]{:S(2)}, u32[]{:S(2)}) collective-permute-start(bf16[32,1024]{1,0:T(8,128)(2,1)S(1)} %get-tuple-element.73), channel_id=1, source_target_pairs={{0,2},{2,4},{4,6},{6,7},{7,5},{5,3},{3,1},{1,0},{8,10},{10,12},{12... | collective-permute-start | bytes 196616 | tf_op jit(solution)/shard_map/ppermute | solution.py:481
  86.6 1.9 %collective-permute-start.35 = (bf16[64,1024]{1,0:T(8,128)(2,1)S(1)}, bf16[64,1024]{1,0:T(8,128)(2,1)S(1)}, u32[]{:S(2)}, u32[]{:S(2)}) collective-permute-start(bf16[64,1024]{1,0:T(8,128)(2,1)S(1)} %pad_maximum_fusion.2), channel_id=1, source_target_pairs={{0,2},{2,4},{4,6},{6,7},{7,5},{5,3},{3,1},{1,0},{8,10},{10,12},{12... | collective-permute-start | bytes 393224 | tf_op jit(solution)/shard_map/ppermute | solution.py:481
  89.3 2.1 %collective-permute-start.26 = (bf16[64,1024]{1,0:T(8,128)(2,1)S(1)}, bf16[64,1024]{1,0:T(8,128)(2,1)S(1)}, u32[]{:S(2)}, u32[]{:S(2)}) collective-permute-start(bf16[64,1024]{1,0:T(8,128)(2,1)S(1)} %pad_maximum_fusion), channel_id=1, source_target_pairs={{0,2},{2,4},{4,6},{6,7},{7,5},{5,3},{3,1},{1,0},{8,10},{10,12},{12... | collective-permute-start | bytes 393224 | tf_op jit(solution)/shard_map/ppermute | solution.py:481
  91.5 1.4 %collective-permute-done.35 = bf16[64,1024]{1,0:T(8,128)(2,1)S(1)} collective-permute-done((bf16[64,1024]{1,0:T(8,128)(2,1)S(1)}, bf16[64,1024]{1,0:T(8,128)(2,1)S(1)}, u32[]{:S(2)}, u32[]{:S(2)}) %collective-permute-start.35) | collective-permute-done | bytes 131104 | tf_op jit(solution)/shard_map/ppermute | solution.py:481
  92.9 2.1 %collective-permute-start.36 = (bf16[64,1024]{1,0:T(8,128)(2,1)S(1)}, bf16[64,1024]{1,0:T(8,128)(2,1)S(1)}, u32[]{:S(2)}, u32[]{:S(2)}) collective-permute-start(bf16[64,1024]{1,0:T(8,128)(2,1)S(1)} %add_convert_fusion.4), channel_id=1, source_target_pairs={{0,2},{2,4},{4,6},{6,7},{7,5},{5,3},{3,1},{1,0},{8,10},{10,12},{12... | collective-permute-start | bytes 393224 | tf_op jit(solution)/shard_map/ppermute | solution.py:481
  95.8 2.0 %collective-permute-start.27 = (bf16[64,1024]{1,0:T(8,128)(2,1)S(1)}, bf16[64,1024]{1,0:T(8,128)(2,1)S(1)}, u32[]{:S(2)}, u32[]{:S(2)}) collective-permute-start(bf16[64,1024]{1,0:T(8,128)(2,1)S(1)} %add_convert_fusion.9), channel_id=1, source_target_pairs={{0,2},{2,4},{4,6},{6,7},{7,5},{5,3},{3,1},{1,0},{8,10},{10,12},{12... | collective-permute-start | bytes 393224 | tf_op jit(solution)/shard_map/ppermute | solution.py:481
  98.9 1.7 %collective-permute-start.37 = (bf16[64,1024]{1,0:T(8,128)(2,1)S(1)}, bf16[64,1024]{1,0:T(8,128)(2,1)S(1)}, u32[]{:S(2)}, u32[]{:S(2)}) collective-permute-start(bf16[64,1024]{1,0:T(8,128)(2,1)S(1)} %add_convert_fusion.3), channel_id=1, source_target_pairs={{0,2},{2,4},{4,6},{6,7},{7,5},{5,3},{3,1},{1,0},{8,10},{10,12},{12... | collective-permute-start | bytes 393224 | tf_op jit(solution)/shard_map/ppermute | solution.py:481
  102.1 2.2 %collective-permute-start.28 = (bf16[64,1024]{1,0:T(8,128)(2,1)S(1)}, bf16[64,1024]{1,0:T(8,128)(2,1)S(1)}, u32[]{:S(2)}, u32[]{:S(2)}) collective-permute-start(bf16[64,1024]{1,0:T(8,128)(2,1)S(1)} %add_convert_fusion.8), channel_id=1, source_target_pairs={{0,2},{2,4},{4,6},{6,7},{7,5},{5,3},{3,1},{1,0},{8,10},{10,12},{12... | collective-permute-start | bytes 393224 | tf_op jit(solution)/shard_map/ppermute | solution.py:481
  104.4 1.6 %collective-permute-done.41 = bf16[64,1024]{1,0:T(8,128)(2,1)S(1)} collective-permute-done((bf16[64,1024]{1,0:T(8,128)(2,1)S(1)}, bf16[64,1024]{1,0:T(8,128)(2,1)S(1)}, u32[]{:S(2)}, u32[]{:S(2)}) %collective-permute-start.41) | collective-permute-done | bytes 131104 | tf_op jit(solution)/shard_map/ppermute | solution.py:481
  106.0 1.2 %collective-permute-done.28 = bf16[64,1024]{1,0:T(8,128)(2,1)S(1)} collective-permute-done((bf16[64,1024]{1,0:T(8,128)(2,1)S(1)}, bf16[64,1024]{1,0:T(8,128)(2,1)S(1)}, u32[]{:S(2)}, u32[]{:S(2)}) %collective-permute-start.28) | collective-permute-done | bytes 131104 | tf_op jit(solution)/shard_map/ppermute | solution.py:481
  107.2 2.2 %collective-permute-done.32 = bf16[64,1024]{1,0:T(8,128)(2,1)S(1)} collective-permute-done((bf16[64,1024]{1,0:T(8,128)(2,1)S(1)}, bf16[64,1024]{1,0:T(8,128)(2,1)S(1)}, u32[]{:S(2)}, u32[]{:S(2)}) %collective-permute-start.32) | collective-permute-done | bytes 131104 | tf_op jit(solution)/shard_map/ppermute | solution.py:481
  (100 shorter events, 15.2 us)
Async XLA Ops:
  1.9 17.3 %collective-permute-start.13 = (bf16[128,2048]{1,0:T(8,128)(2,1)}, bf16[128,2048]{1,0:T(8,128)(2,1)S(1)}, u32[]{:S(2)}, u32[]{:S(2)}) collective-permute-start(bf16[128,2048]{1,0:T(8,128)(2,1)} %cast_rows.2.refs_9_), channel_id=1, source_target_pairs={{0,16},{8,24},{16,0},{24,8},{1,17},{9,25},{17,1},{25,9},{2,18},{10... | collective-permute-start | bytes 1572872 | tf_op jit(solution)/shard_map/ppermute | solution.py:471
  7.9 6.0 %collective-permute-start = (bf16[64,512]{1,0:T(8,128)(2,1)}, bf16[64,512]{1,0:T(8,128)(2,1)S(1)}, u32[]{:S(2)}, u32[]{:S(2)}) collective-permute-start(bf16[64,512]{1,0:T(8,128)(2,1)} %get-tuple-element.53), channel_id=1, source_target_pairs={{0,8},{8,0},{16,24},{24,16},{1,9},{9,1},{17,25},{25,17},{2,10},{10... | collective-permute-start | bytes 196616 | tf_op jit(solution)/shard_map/ppermute | solution.py:471
  8.0 11.2 %collective-permute-start.1 = (bf16[64,512]{1,0:T(8,128)(2,1)}, bf16[64,512]{1,0:T(8,128)(2,1)S(1)}, u32[]{:S(2)}, u32[]{:S(2)}) collective-permute-start(bf16[64,512]{1,0:T(8,128)(2,1)} %get-tuple-element.54), channel_id=1, source_target_pairs={{0,16},{8,24},{16,0},{24,8},{1,17},{9,25},{17,1},{25,9},{2,18},{10... | collective-permute-start | bytes 196616 | tf_op jit(solution)/shard_map/ppermute | solution.py:471
  8.1 11.2 %collective-permute-start.2 = (bf16[64,512]{1,0:T(8,128)(2,1)}, bf16[64,512]{1,0:T(8,128)(2,1)S(1)}, u32[]{:S(2)}, u32[]{:S(2)}) collective-permute-start(bf16[64,512]{1,0:T(8,128)(2,1)} %get-tuple-element.55), channel_id=1, source_target_pairs={{0,24},{8,16},{16,8},{24,0},{1,25},{9,17},{17,9},{25,1},{2,26},{10... | collective-permute-start | bytes 196616 | tf_op jit(solution)/shard_map/ppermute | solution.py:471
  19.3 37.4 %collective-permute-start.14 = (bf16[384,2048]{1,0:T(8,128)(2,1)}, bf16[384,2048]{1,0:T(8,128)(2,1)S(1)}, u32[]{:S(2)}, u32[]{:S(2)}) collective-permute-start(bf16[384,2048]{1,0:T(8,128)(2,1)} %get-tuple-element.60.refs_10_), channel_id=1, source_target_pairs={{0,16},{8,24},{16,0},{24,8},{1,17},{9,25},{17,1},{25,9},{2,18},{10... | collective-permute-start | bytes 4718600 | tf_op jit(solution)/shard_map/ppermute | solution.py:471
  21.5 8.9 %collective-permute-start.7 = (bf16[64,2176]{1,0:T(8,128)(2,1)S(1)}, bf16[64,2176]{1,0:T(8,128)(2,1)S(1)}, u32[]{:S(2)}, u32[]{:S(2)}) collective-permute-start(bf16[64,2176]{1,0:T(8,128)(2,1)S(1)} %get-tuple-element.57.refs_0_), channel_id=1, source_target_pairs={{0,2},{2,4},{4,6},{6,7},{7,5},{5,3},{3,1},{1,0},{8,10},{10,12},{12... | collective-permute-start | bytes 835592 | tf_op jit(solution)/shard_map/ppermute | solution.py:481
  23.2 8.5 %collective-permute-start.3 = (bf16[64,2176]{1,0:T(8,128)(2,1)S(1)}, bf16[64,2176]{1,0:T(8,128)(2,1)S(1)}, u32[]{:S(2)}, u32[]{:S(2)}) collective-permute-start(bf16[64,2176]{1,0:T(8,128)(2,1)S(1)} %get-tuple-element.57.refs_0_), channel_id=1, source_target_pairs={{0,1},{2,0},{4,2},{6,4},{7,6},{5,7},{3,5},{1,3},{8,9},{10,8},{12,1... | collective-permute-start | bytes 835592 | tf_op jit(solution)/shard_map/ppermute | solution.py:481
  31.7 26.2 %collective-permute-start.12 = (bf16[384,2048]{1,0:T(8,128)(2,1)}, bf16[384,2048]{1,0:T(8,128)(2,1)S(1)}, u32[]{:S(2)}, u32[]{:S(2)}) collective-permute-start(bf16[384,2048]{1,0:T(8,128)(2,1)} %get-tuple-element.60.refs_10_), channel_id=1, source_target_pairs={{0,8},{8,0},{16,24},{24,16},{1,9},{9,1},{17,25},{25,17},{2,10},{10... | collective-permute-start | bytes 4718600 | tf_op jit(solution)/shard_map/ppermute | solution.py:471
  31.7 9.1 %collective-permute-start.8 = (bf16[64,2176]{1,0:T(8,128)(2,1)S(1)}, bf16[64,2176]{1,0:T(8,128)(2,1)S(1)}, u32[]{:S(2)}, u32[]{:S(2)}) collective-permute-start(bf16[64,2176]{1,0:T(8,128)(2,1)S(1)} %collective-permute-done.7.refs_8_), channel_id=1, source_target_pairs={{0,2},{2,4},{4,6},{6,7},{7,5},{5,3},{3,1},{1,0},{8,10},{10,12},{12... | collective-permute-start | bytes 835592 | tf_op jit(solution)/shard_map/ppermute | solution.py:481
  33.3 9.1 %collective-permute-start.4 = (bf16[64,2176]{1,0:T(8,128)(2,1)S(1)}, bf16[64,2176]{1,0:T(8,128)(2,1)S(1)}, u32[]{:S(2)}, u32[]{:S(2)}) collective-permute-start(bf16[64,2176]{1,0:T(8,128)(2,1)S(1)} %collective-permute-done.3.refs_1_), channel_id=1, source_target_pairs={{0,1},{2,0},{4,2},{6,4},{7,6},{5,7},{3,5},{1,3},{8,9},{10,8},{12,1... | collective-permute-start | bytes 835592 | tf_op jit(solution)/shard_map/ppermute | solution.py:481
  40.7 8.3 %collective-permute-start.9 = (bf16[64,2176]{1,0:T(8,128)(2,1)S(1)}, bf16[64,2176]{1,0:T(8,128)(2,1)S(1)}, u32[]{:S(2)}, u32[]{:S(2)}) collective-permute-start(bf16[64,2176]{1,0:T(8,128)(2,1)S(1)} %collective-permute-done.8.refs_7_), channel_id=1, source_target_pairs={{0,2},{2,4},{4,6},{6,7},{7,5},{5,3},{3,1},{1,0},{8,10},{10,12},{12... | collective-permute-start | bytes 835592 | tf_op jit(solution)/shard_map/ppermute | solution.py:481
  42.3 8.4 %collective-permute-start.5 = (bf16[64,2176]{1,0:T(8,128)(2,1)S(1)}, bf16[64,2176]{1,0:T(8,128)(2,1)S(1)}, u32[]{:S(2)}, u32[]{:S(2)}) collective-permute-start(bf16[64,2176]{1,0:T(8,128)(2,1)S(1)} %collective-permute-done.4.refs_2_), channel_id=1, source_target_pairs={{0,1},{2,0},{4,2},{6,4},{7,6},{5,7},{3,5},{1,3},{8,9},{10,8},{12,1... | collective-permute-start | bytes 835592 | tf_op jit(solution)/shard_map/ppermute | solution.py:481
  49.0 5.1 %collective-permute-start.10 = (bf16[32,2176]{1,0:T(8,128)(2,1)S(1)}, bf16[32,2176]{1,0:T(8,128)(2,1)S(1)}, u32[]{:S(2)}, u32[]{:S(2)}) collective-permute-start(bf16[32,2176]{1,0:T(8,128)(2,1)S(1)} %slice.49), channel_id=1, source_target_pairs={{0,2},{2,4},{4,6},{6,7},{7,5},{5,3},{3,1},{1,0},{8,10},{10,12},{12... | collective-permute-start | bytes 417800 | tf_op jit(solution)/shard_map/ppermute | solution.py:481
  50.7 5.1 %collective-permute-start.6 = (bf16[32,2176]{1,0:T(8,128)(2,1)S(1)}, bf16[32,2176]{1,0:T(8,128)(2,1)S(1)}, u32[]{:S(2)}, u32[]{:S(2)}) collective-permute-start(bf16[32,2176]{1,0:T(8,128)(2,1)S(1)} %slice.48), channel_id=1, source_target_pairs={{0,1},{2,0},{4,2},{6,4},{7,6},{5,7},{3,5},{1,3},{8,9},{10,8},{12,1... | collective-permute-start | bytes 417800 | tf_op jit(solution)/shard_map/ppermute | solution.py:481
  51.2 5.7 %collective-permute-start.11 = (bf16[128,2048]{1,0:T(8,128)(2,1)S(1)}, bf16[128,2048]{1,0:T(8,128)(2,1)S(1)}, u32[]{:S(2)}, u32[]{:S(2)}) collective-permute-start(bf16[128,2048]{1,0:T(8,128)(2,1)S(1)} %copy-done), channel_id=1, source_target_pairs={{0,8},{8,0},{16,24},{24,16},{1,9},{9,1},{17,25},{25,17},{2,10},{10... | collective-permute-start | bytes 1572872 | tf_op jit(solution)/shard_map/ppermute | solution.py:471
  54.2 24.5 %collective-permute-start.23 = (bf16[256,2048]{1,0:T(8,128)(2,1)}, bf16[256,2048]{1,0:T(8,128)(2,1)S(1)}, u32[]{:S(2)}, u32[]{:S(2)}) collective-permute-start(bf16[256,2048]{1,0:T(8,128)(2,1)} %get-tuple-element.66.refs_0_), channel_id=1, source_target_pairs={{0,16},{8,24},{16,0},{24,8},{1,17},{9,25},{17,1},{25,9},{2,18},{10... | collective-permute-start | bytes 3145736 | tf_op jit(solution)/shard_map/ppermute | solution.py:471
  59.3 20.1 %collective-permute-start.22 = (bf16[256,2048]{1,0:T(8,128)(2,1)S(1)}, bf16[256,2048]{1,0:T(8,128)(2,1)S(1)}, u32[]{:S(2)}, u32[]{:S(2)}) collective-permute-start(bf16[256,2048]{1,0:T(8,128)(2,1)S(1)} %copy-done.2), channel_id=1, source_target_pairs={{0,8},{8,0},{16,24},{24,16},{1,9},{9,1},{17,25},{25,17},{2,10},{10... | collective-permute-start | bytes 3145736 | tf_op jit(solution)/shard_map/ppermute | solution.py:471
  78.9 5.2 %collective-permute-start.24 = (bf16[256,1024]{1,0:T(8,128)(2,1)S(1)}, bf16[256,1024]{1,0:T(8,128)(2,1)S(1)}, u32[]{:S(2)}, u32[]{:S(2)}) collective-permute-start(bf16[256,1024]{1,0:T(8,128)(2,1)S(1)} %get-tuple-element.97), channel_id=1, source_target_pairs={{0,8},{8,0},{16,24},{24,16},{1,9},{9,1},{17,25},{25,17},{2,10},{10... | collective-permute-start | bytes 1572872 | tf_op jit(solution)/shard_map/ppermute | solution.py:471
  84.5 4.7 %collective-permute-start.25 = (bf16[32,1024]{1,0:T(8,128)(2,1)S(1)}, bf16[32,1024]{1,0:T(8,128)(2,1)S(1)}, u32[]{:S(2)}, u32[]{:S(2)}) collective-permute-start(bf16[32,1024]{1,0:T(8,128)(2,1)S(1)} %get-tuple-element.73), channel_id=1, source_target_pairs={{0,2},{2,4},{4,6},{6,7},{7,5},{5,3},{3,1},{1,0},{8,10},{10,12},{12... | collective-permute-start | bytes 196616 | tf_op jit(solution)/shard_map/ppermute | solution.py:481
  86.4 5.0 %collective-permute-start.29 = (bf16[32,1024]{1,0:T(8,128)(2,1)S(1)}, bf16[32,1024]{1,0:T(8,128)(2,1)S(1)}, u32[]{:S(2)}, u32[]{:S(2)}) collective-permute-start(bf16[32,1024]{1,0:T(8,128)(2,1)S(1)} %get-tuple-element.79), channel_id=1, source_target_pairs={{0,1},{2,0},{4,2},{6,4},{7,6},{5,7},{3,5},{1,3},{8,9},{10,8},{12,1... | collective-permute-start | bytes 196616 | tf_op jit(solution)/shard_map/ppermute | solution.py:481
  86.6 6.2 %collective-permute-start.35 = (bf16[64,1024]{1,0:T(8,128)(2,1)S(1)}, bf16[64,1024]{1,0:T(8,128)(2,1)S(1)}, u32[]{:S(2)}, u32[]{:S(2)}) collective-permute-start(bf16[64,1024]{1,0:T(8,128)(2,1)S(1)} %pad_maximum_fusion.2), channel_id=1, source_target_pairs={{0,2},{2,4},{4,6},{6,7},{7,5},{5,3},{3,1},{1,0},{8,10},{10,12},{12... | collective-permute-start | bytes 393224 | tf_op jit(solution)/shard_map/ppermute | solution.py:481
  88.6 6.4 %collective-permute-start.39 = (bf16[64,1024]{1,0:T(8,128)(2,1)S(1)}, bf16[64,1024]{1,0:T(8,128)(2,1)S(1)}, u32[]{:S(2)}, u32[]{:S(2)}) collective-permute-start(bf16[64,1024]{1,0:T(8,128)(2,1)S(1)} %pad_maximum_fusion.3), channel_id=1, source_target_pairs={{0,1},{2,0},{4,2},{6,4},{7,6},{5,7},{3,5},{1,3},{8,9},{10,8},{12,1... | collective-permute-start | bytes 393224 | tf_op jit(solution)/shard_map/ppermute | solution.py:481
  89.3 6.5 %collective-permute-start.26 = (bf16[64,1024]{1,0:T(8,128)(2,1)S(1)}, bf16[64,1024]{1,0:T(8,128)(2,1)S(1)}, u32[]{:S(2)}, u32[]{:S(2)}) collective-permute-start(bf16[64,1024]{1,0:T(8,128)(2,1)S(1)} %pad_maximum_fusion), channel_id=1, source_target_pairs={{0,2},{2,4},{4,6},{6,7},{7,5},{5,3},{3,1},{1,0},{8,10},{10,12},{12... | collective-permute-start | bytes 393224 | tf_op jit(solution)/shard_map/ppermute | solution.py:481
  91.4 6.4 %collective-permute-start.30 = (bf16[64,1024]{1,0:T(8,128)(2,1)S(1)}, bf16[64,1024]{1,0:T(8,128)(2,1)S(1)}, u32[]{:S(2)}, u32[]{:S(2)}) collective-permute-start(bf16[64,1024]{1,0:T(8,128)(2,1)S(1)} %pad_maximum_fusion.1), channel_id=1, source_target_pairs={{0,1},{2,0},{4,2},{6,4},{7,6},{5,7},{3,5},{1,3},{8,9},{10,8},{12,1... | collective-permute-start | bytes 393224 | tf_op jit(solution)/shard_map/ppermute | solution.py:481
  92.9 5.9 %collective-permute-start.36 = (bf16[64,1024]{1,0:T(8,128)(2,1)S(1)}, bf16[64,1024]{1,0:T(8,128)(2,1)S(1)}, u32[]{:S(2)}, u32[]{:S(2)}) collective-permute-start(bf16[64,1024]{1,0:T(8,128)(2,1)S(1)} %add_convert_fusion.4), channel_id=1, source_target_pairs={{0,2},{2,4},{4,6},{6,7},{7,5},{5,3},{3,1},{1,0},{8,10},{10,12},{12... | collective-permute-start | bytes 393224 | tf_op jit(solution)/shard_map/ppermute | solution.py:481
  95.0 5.6 %collective-permute-start.40 = (bf16[64,1024]{1,0:T(8,128)(2,1)S(1)}, bf16[64,1024]{1,0:T(8,128)(2,1)S(1)}, u32[]{:S(2)}, u32[]{:S(2)}) collective-permute-start(bf16[64,1024]{1,0:T(8,128)(2,1)S(1)} %add_convert_fusion.2), channel_id=1, source_target_pairs={{0,1},{2,0},{4,2},{6,4},{7,6},{5,7},{3,5},{1,3},{8,9},{10,8},{12,1... | collective-permute-start | bytes 393224 | tf_op jit(solution)/shard_map/ppermute | solution.py:481
  95.8 6.2 %collective-permute-start.27 = (bf16[64,1024]{1,0:T(8,128)(2,1)S(1)}, bf16[64,1024]{1,0:T(8,128)(2,1)S(1)}, u32[]{:S(2)}, u32[]{:S(2)}) collective-permute-start(bf16[64,1024]{1,0:T(8,128)(2,1)S(1)} %add_convert_fusion.9), channel_id=1, source_target_pairs={{0,2},{2,4},{4,6},{6,7},{7,5},{5,3},{3,1},{1,0},{8,10},{10,12},{12... | collective-permute-start | bytes 393224 | tf_op jit(solution)/shard_map/ppermute | solution.py:481
  97.8 6.5 %collective-permute-start.31 = (bf16[64,1024]{1,0:T(8,128)(2,1)S(1)}, bf16[64,1024]{1,0:T(8,128)(2,1)S(1)}, u32[]{:S(2)}, u32[]{:S(2)}) collective-permute-start(bf16[64,1024]{1,0:T(8,128)(2,1)S(1)} %add_convert_fusion.7), channel_id=1, source_target_pairs={{0,1},{2,0},{4,2},{6,4},{7,6},{5,7},{3,5},{1,3},{8,9},{10,8},{12,1... | collective-permute-start | bytes 393224 | tf_op jit(solution)/shard_map/ppermute | solution.py:481
  98.9 5.5 %collective-permute-start.37 = (bf16[64,1024]{1,0:T(8,128)(2,1)S(1)}, bf16[64,1024]{1,0:T(8,128)(2,1)S(1)}, u32[]{:S(2)}, u32[]{:S(2)}) collective-permute-start(bf16[64,1024]{1,0:T(8,128)(2,1)S(1)} %add_convert_fusion.3), channel_id=1, source_target_pairs={{0,2},{2,4},{4,6},{6,7},{7,5},{5,3},{3,1},{1,0},{8,10},{10,12},{12... | collective-permute-start | bytes 393224 | tf_op jit(solution)/shard_map/ppermute | solution.py:481
  100.6 5.4 %collective-permute-start.41 = (bf16[64,1024]{1,0:T(8,128)(2,1)S(1)}, bf16[64,1024]{1,0:T(8,128)(2,1)S(1)}, u32[]{:S(2)}, u32[]{:S(2)}) collective-permute-start(bf16[64,1024]{1,0:T(8,128)(2,1)S(1)} %add_convert_fusion.1), channel_id=1, source_target_pairs={{0,1},{2,0},{4,2},{6,4},{7,6},{5,7},{3,5},{1,3},{8,9},{10,8},{12,1... | collective-permute-start | bytes 393224 | tf_op jit(solution)/shard_map/ppermute | solution.py:481
  102.1 5.1 %collective-permute-start.28 = (bf16[64,1024]{1,0:T(8,128)(2,1)S(1)}, bf16[64,1024]{1,0:T(8,128)(2,1)S(1)}, u32[]{:S(2)}, u32[]{:S(2)}) collective-permute-start(bf16[64,1024]{1,0:T(8,128)(2,1)S(1)} %add_convert_fusion.8), channel_id=1, source_target_pairs={{0,2},{2,4},{4,6},{6,7},{7,5},{5,3},{3,1},{1,0},{8,10},{10,12},{12... | collective-permute-start | bytes 393224 | tf_op jit(solution)/shard_map/ppermute | solution.py:481
  104.3 5.0 %collective-permute-start.32 = (bf16[64,1024]{1,0:T(8,128)(2,1)S(1)}, bf16[64,1024]{1,0:T(8,128)(2,1)S(1)}, u32[]{:S(2)}, u32[]{:S(2)}) collective-permute-start(bf16[64,1024]{1,0:T(8,128)(2,1)S(1)} %add_convert_fusion.6), channel_id=1, source_target_pairs={{0,1},{2,0},{4,2},{6,4},{7,6},{5,7},{3,5},{1,3},{8,9},{10,8},{12,1... | collective-permute-start | bytes 393224 | tf_op jit(solution)/shard_map/ppermute | solution.py:481
  (18 other events, 138.3 us)

commit v12 on v11

--- a/solution.py
+++ b/solution.py
@@ -113,6 +113,7 @@
 VMEM_LIMIT = 32 * 2**20
 VMEM_MOST = 60 * 2**20
 CAST_STEPS = 4
+FIRST_BLOCKS = 2
 SLABS = 2
 SMALL = pl.CostEstimate(flops=1, bytes_accessed=1, transcendentals=0)
 
@@ -126,8 +127,9 @@
 
 
 def attention_kernel(*refs):
-    sources, outs, scratch = refs[:5], refs[5:9], refs[9:]
-    table, lengths, q_ref, k_ref, v_ref, attn, arrived = scratch
+    sources, outs, scratch = refs[:6], refs[6:10], refs[10:]
+    own_ref, beside_ref, sent_ref, rows_ref = outs
+    table, lengths, q_ref, k_ref, v_ref, weights, attn, arrived = scratch
     copies = [
         pltpu.make_async_copy(source, target, arrived.at[i])
         for i, (source, target) in enumerate(
@@ -137,9 +139,13 @@
             )
         )
     ]
+    rows = weights.shape[0]
+    copies.append(
+        pltpu.make_async_copy(sources[5].at[0, pl.ds(0, rows)], weights, arrived.at[5])
+    )
     for copy in copies:
         copy.start()
-    for copy in copies:
+    for copy in copies[:5]:
         copy.wait()
     tokens, width = q_ref.shape
     pages = k_ref.shape[0]
@@ -168,18 +174,34 @@
             jnp.bfloat16
         )
     own = lax.axis_index("dp")
-    rows = tokens // 4
-    for d in range(4):
-        first = pl.multiple_of((own ^ d) * rows, rows)
-        outs[d][...] = attn[pl.ds(first, rows), :]
-
-
-def attention(queries, key_pool, value_pool, page_table, prompt_lengths):
+    block = tokens // 4
+    split = weights.shape[1]
+    end = sent_ref.shape[1]
+    targets = (
+        own_ref,
+        beside_ref,
+        sent_ref.at[:, end - 2 * width : end - width],
+        sent_ref.at[:, end - width :],
+    )
+    for d, target in enumerate(targets):
+        target[...] = attn[pl.ds(pl.multiple_of((own ^ d) * block, block), block), :]
+    copies[5].wait()
+    rows_ref[...] = weights[...].astype(jnp.bfloat16)
+    for i in range(rows // block):
+        here = slice(i * block, (i + 1) * block)
+        sent_ref[:, i * split : (i + 1) * split] = rows_ref[here]
+
+
+def attention(queries, key_pool, value_pool, page_table, prompt_lengths, gate_up, blocks):
     tokens, width = queries.shape[1:]
+    split = gate_up.shape[2]
+    block = tokens // 4
+    shapes = [(block, width)] * 2
+    shapes += [(block, blocks * split + 2 * width), (blocks * block, split)]
     return pl.pallas_call(
         attention_kernel,
-        out_shape=[jax.ShapeDtypeStruct((tokens // 4, width), jnp.bfloat16)] * 4,
-        in_specs=[pl.BlockSpec(memory_space=pltpu.HBM)] * 5,
+        out_shape=[jax.ShapeDtypeStruct(shape, jnp.bfloat16) for shape in shapes],
+        in_specs=[pl.BlockSpec(memory_space=pltpu.HBM)] * 6,
         out_specs=vmem(4),
         scratch_shapes=[
             pltpu.SMEM(page_table.shape, jnp.int32),
@@ -187,18 +209,21 @@
             pltpu.VMEM((tokens, width), jnp.bfloat16),
             pltpu.VMEM(key_pool.shape, jnp.bfloat16),
             pltpu.VMEM(value_pool.shape, jnp.bfloat16),
+            pltpu.VMEM((blocks * block, split), jnp.float32),
             pltpu.VMEM((tokens, width), jnp.bfloat16),
-            pltpu.SemaphoreType.DMA((5,)),
+            pltpu.SemaphoreType.DMA((6,)),
         ],
         compiler_params=params(VMEM_MOST),
         name="attention",
-    )(page_table, prompt_lengths, queries, key_pool, value_pool)
-
-
-def norm_kernel(hidden_ref, a0, a1, a2, a3, gain_ref, ids_ref, gates_ref, resid_ref, rows_ref):
+    )(page_table, prompt_lengths, queries, key_pool, value_pool, gate_up)
+
+
+def norm_kernel(hidden_ref, a0, a1, first, a3, gain_ref, ids_ref, gates_ref, resid_ref, *row_refs):
     own = lax.axis_index("dp")
     tokens, width = hidden_ref.shape
     block = width // 4
+    end = first.shape[1]
+    a2 = first.at[:, end - 2 * block : end - block]
     total = jnp.zeros((tokens, 1), jnp.float32)
     for d, attn in enumerate((a0, a1, a2, a3)):
         columns = pl.ds(pl.multiple_of((own ^ d) * block, block), block)
@@ -211,9 +236,10 @@
     inverse = lax.rsqrt(total / width + epsilon)
     for d in range(4):
         columns = pl.ds(pl.multiple_of((own ^ d) * block, block), block)
-        rows_ref[:, d * block : (d + 1) * block] = (
-            resid_ref[:, columns].astype(jnp.float32) * inverse * gain_ref[:, columns]
-        ).astype(jnp.bfloat16)
+        normed = resid_ref[:, columns].astype(jnp.float32) * inverse * gain_ref[:, columns]
+        for i, ref in enumerate(row_refs):
+            here = slice(i * tokens // 2, (i + 1) * tokens // 2)
+            ref[:, d * block : (d + 1) * block] = normed[here].astype(jnp.bfloat16)
     lane = lax.broadcasted_iota(jnp.int32, (tokens, LANES), 1)
     gates = jnp.zeros((tokens, LANES), jnp.float32)
     for k in range(TOPK):
@@ -223,7 +249,9 @@
     low = gates - high - middle
     part = lane // TOPK
     terms = jnp.where(part == 0, high, jnp.where(part == 1, middle, jnp.where(part == 2, low, 0.0)))
-    rows_ref[:, width:] = terms.astype(jnp.bfloat16)
+    for i, ref in enumerate(row_refs):
+        here = slice(i * tokens // 2, (i + 1) * tokens // 2)
+        ref[:, width:] = terms[here].astype(jnp.bfloat16)
 
 
 def norm(hidden_in, attn, norm_gain, expert_ids, gate_weights):
@@ -232,10 +260,10 @@
         norm_kernel,
         out_shape=[
             jax.ShapeDtypeStruct((tokens, width), jnp.bfloat16),
-            jax.ShapeDtypeStruct((tokens, width + LANES), jnp.bfloat16),
-        ],
+        ]
+        + [jax.ShapeDtypeStruct((tokens // 2, width + LANES), jnp.bfloat16)] * 2,
         in_specs=vmem(8),
-        out_specs=vmem(2),
+        out_specs=vmem(3),
         compiler_params=params(),
         cost_estimate=SMALL,
         name="norm",
@@ -295,16 +323,16 @@
     )(*arrays)
 
 
-def load_tiles(pieces, weights, arrived, tiles, block):
+def load_tiles(pieces, starts, weights, arrived, tiles, block):
     def copies(tile):
         first = 0
-        for index, piece in enumerate(pieces):
+        for index, (piece, start) in enumerate(zip(pieces, starts)):
             depth = piece.shape[0]
             for part in range(2):
-                columns = pl.ds((part * tiles + tile) * block, block)
+                column = (part * tiles + tile) * block
                 yield pltpu.make_async_copy(
-                    piece.at[:, columns],
-                    weights.at[pl.ds(first, depth), columns],
+                    piece.at[:, pl.ds(start + column, block)],
+                    weights.at[pl.ds(first, depth), pl.ds(column, block)],
                     arrived.at[tile, index, part],
                 )
             first += depth
@@ -320,13 +348,14 @@
     return wait
 
 
-def up_kernel(sources, pieces, *refs):
+def up_kernel(sources, starts, *refs):
+    pieces = len(starts)
     row_refs = refs[:sources]
     weight_refs = refs[sources : sources + pieces]
     hidden_ref, own_gate_ref, rows, weights, units, arrived = refs[sources + pieces :]
     width = rows.shape[1]
     tiles, _, block = units.shape
-    wait = load_tiles(weight_refs, weights, arrived, tiles, block)
+    wait = load_tiles(weight_refs, starts, weights, arrived, tiles, block)
     expert = lax.axis_index("expert")
     first = 0
     for ref in row_refs:
@@ -355,13 +384,13 @@
         hidden_ref[:, d * block : (d + 1) * block] = units[own ^ d]
 
 
-def expert_up(rows, weights):
+def expert_up(rows, weights, width):
+    weights, starts = zip(*weights)
     tokens = sum(piece.shape[0] for piece in rows)
     features = sum(piece.shape[0] for piece in weights)
-    width = weights[0].shape[1]
     hidden_size = width // 2
     return pl.pallas_call(
-        lambda *refs: up_kernel(len(rows), len(weights), *refs),
+        lambda *refs: up_kernel(len(rows), starts, *refs),
         out_shape=[
             jax.ShapeDtypeStruct((tokens, hidden_size), jnp.bfloat16),
             jax.ShapeDtypeStruct((tokens, 1), jnp.float32),
@@ -489,15 +518,15 @@
     return (a.astype(jnp.float32) + b.astype(jnp.float32)).astype(jnp.bfloat16)
 
 
-def gather_rows(rows):
-    half = rows.shape[0] // 2
+def gather_rows(halves):
     reach = lax.axis_size("expert") // 2
-    above, below = [rows], [rows]
+    above, below = [halves], [halves]
     for _ in range(reach - 1):
-        above.append(around(above[-1], -1))
-        below.append(around(below[-1], 1))
-    far = [around(above[-1][:half], -1), around(below[-1][half:], 1)]
-    return above + far + below[:0:-1], list(zip(above[1:], below[1:])) + [tuple(far)]
+        above.append([around(half, -1) for half in above[-1]])
+        below.append([around(half, 1) for half in below[-1]])
+    far = [around(above[-1][0], -1), around(below[-1][1], 1)]
+    rows = [half for pair in (*above, far, *below[:0:-1]) for half in pair]
+    return rows, [(*a, *b) for a, b in zip(above[1:], below[1:])] + [tuple(far)]
 
 
 def scatter_sum(own, *blocks):
@@ -536,33 +565,47 @@
     width = trainer_down.shape[2]
     depth, columns = trainer_gate_up.shape[1:]
     down_depth = trainer_down.shape[1]
-    early = depth // 4
     slab = width // SLABS
-    (first_own,) = cast_rows([trainer_gate_up], [(0, early, 0, columns)])
-    first_across = partner(first_own, 2)
-    attn = attention(
-        after(queries, first_own), key_pool, value_pool, page_table, prompt_lengths
-    )
+    early = queries.shape[1] // 4 * FIRST_BLOCKS
+    side = [i * columns for i in range(FIRST_BLOCKS)]
+    attn_own, attn_beside, first_sent, first_own = attention(
+        queries,
+        key_pool,
+        value_pool,
+        page_table,
+        prompt_lengths,
+        trainer_gate_up,
+        FIRST_BLOCKS,
+    )
+    first_across = partner(first_sent, 2)
     rest_own, down_own = cast_rows(
-        [after(trainer_gate_up, attn[0]), trainer_down],
+        [after(trainer_gate_up, attn_own), trainer_down],
         [(early, depth - early, 0, columns), (0, down_depth, 0, width)],
     )
-    attn = [attn[0]] + [partner(attn[d], d) for d in (1, 2, 3)]
-    rest_across = partner(after(rest_own, first_across, *attn), 2)
-    resid, rows = norm(
-        after(hidden_in[0], rest_own), attn, norm_gain, expert_ids[0], gate_weights[0]
-    )
-    gathered, arrived = gather_rows(rows)
+    attn_beside = partner(attn_beside, 1)
+    attn_opposite = partner(first_across[:, -attn_own.shape[1] :], 1)
+    rest_across = partner(rest_own, 2)
+    resid, *halves = norm(
+        after(hidden_in[0], rest_own),
+        (attn_own, attn_beside, first_across, attn_opposite),
+        norm_gain,
+        expert_ids[0],
+        gate_weights[0],
+    )
+    gathered, arrived = gather_rows(halves)
     first_beside = partner(after(first_own, *arrived[0]), 1)
-    first_opposite = partner(after(first_across, *arrived[0]), 1)
     rest_beside = partner(after(rest_own, *arrived[0]), 1)
+    first_ready = after(first_across, *arrived[0])
+    first_opposite = [partner(first_ready[:, start : start + columns], 1) for start in side]
     down_beside = partner(after(down_own, *arrived[1]), 1)
     down_across = partner(after(down_own, *arrived[2]), 2)
-    rest_opposite = relayed(after(rest_across, *arrived[3]), depth // 8)
+    rest_opposite = relayed(after(rest_across, *arrived[3]), (depth - early) // 2)
     hidden_units, gates = expert_up(
         gathered,
-        [first_own, rest_own, first_beside, rest_beside]
-        + [first_across, rest_across, first_opposite, *rest_opposite],
+        [(ref, 0) for ref in (first_own, rest_own, first_beside, rest_beside)]
+        + [(first_across, start) for start in side]
+        + [(ref, 0) for ref in (rest_across, *first_opposite, *rest_opposite)],
+        columns,
     )
     down_ready = after(down_across, hidden_units)
     total = down_part(hidden_units, [down_own, down_beside, down_ready])

time: 110 us -> 111 us (level)
  waiting for transfers between devices: 53 us -> 45 us
  starting transfers between devices: 34.6 us -> 40 us
  local copies, waits for them, and re-layouts: 0.44 us -> 4.59 us
    ppermute x24 -> x30, waiting for transfers between devices: 34.7 us -> 19 us  [around(): lax.ppermute(x, 'expert', [(ring[i], ring[(i + step) % count]) for i in r...]
    ppermute x24 -> x30, starting transfers between devices: 25.4 us -> 34 us  [around(): lax.ppermute(x, 'expert', [(ring[i], ring[(i + step) % count]) for i in r...]
    ppermute x18 -> x14, waiting for transfers between devices: 18.3 us -> 26 us  [partner(): return lax.ppermute(x, 'dp', [(i, i ^ distance) for i in range(4)])]
    unnamed x18 -> x22, local copies, waits for them, and re-layouts: 0.2 us -> 3.76 us
    ppermute x18 -> x14, starting transfers between devices: 9.21 us -> 6.01 us  [partner(): return lax.ppermute(x, 'dp', [(i, i ^ distance) for i in range(4)])]
    pallas_call x2 -> x1, Pallas kernels: 5.92 us -> 3.99 us  [cast_rows(): pl.pallas_call(lambda *refs: cast_kernel(spans, *refs), out_shape=[jax.Sh...]
  transfers between devices with their start and end apart: 42 -> 44, of which waited for: 26 -> 21; matrix products, arithmetic and copies ran while one was open for 1% -> 2% of each run, Pallas kernels for 17% -> 15%
where the time goes in v12:
time: 111 us
  waiting for transfers between devices  45 us (41%)
  starting transfers between devices  40 us (36%)
  Pallas kernels  19.8 us (18%)
  local copies, waits for them, and re-layouts  4.59 us (4%)
  other arithmetic  1.28 us (1%)
    ppermute x30, starting transfers between devices, around(): lax.ppermute(x, 'expert', [(ring[i], ring[(i + step) % count]) for i in r...  34 us
    ppermute x14, waiting for transfers between devices, partner(): return lax.ppermute(x, 'dp', [(i, i ^ distance) for i in range(4)])  26 us
    ppermute x30, waiting for transfers between devices, around(): lax.ppermute(x, 'expert', [(ring[i], ring[(i + step) % count]) for i in r...  19 us
    pallas_call x1, Pallas kernels, expert_up(): pl.pallas_call(lambda *refs: up_kernel(len(rows), starts, *refs), out_sha...  8.07 us
    ppermute x14, starting transfers between devices, partner(): return lax.ppermute(x, 'dp', [(i, i ^ distance) for i in range(4)])  6.01 us
    pallas_call x1, Pallas kernels, cast_rows(): pl.pallas_call(lambda *refs: cast_kernel(spans, *refs), out_shape=[jax.Sh...  3.99 us
    unnamed x22, local copies, waits for them, and re-layouts  3.76 us
    pallas_call x1, Pallas kernels, attention(): pl.pallas_call(attention_kernel, out_shape=[jax.ShapeDtypeStruct(shape, j...  3.4 us
  transfers between devices with their start and end apart: 44, of which 21 were waited for; matrix products, arithmetic and copies ran while one was open for 2% of the time, Pallas kernels for 15%

profile of v12, /device:TPU:0, one launch (start us, length us, event | category | flops | bytes accessed | tf_op | source)
XLA Modules:
  0.0 110.9 jit_solution(2710317605192520648)
XLA Ops:
  0.0 3.4 %attention.1 = (bf16[64,512]{1,0:T(8,128)(2,1)}, bf16[64,512]{1,0:T(8,128)(2,1)}, bf16[64,5120]{1,0:T(8,128)(2,1)}, bf16[128,2048]{1,0:T(8,128)(2,1)}) custom-call(s32[1,2]{1,0:T(1,128)} %refs_0_.1, s32[1,4]{1,0:T(1,128)} %refs_1_.2, bf16[1,256,512]{2,1,0:T(8,128)(2,1)} %refs_2_.1, bf16[2,128,512]{2,1,0:T(8,128)(2,1)} %refs_3_.1, ...), custom_call_target="tpu_custom_call" | custom-call | tf_op jit(solution)/shard_map/attention/pallas_call | solution.py:201
  3.4 3.0 %collective-permute-start.1 = (bf16[64,5120]{1,0:T(8,128)(2,1)}, bf16[64,5120]{1,0:T(8,128)(2,1)S(1)}, u32[]{:S(2)}, u32[]{:S(2)}) collective-permute-start(bf16[64,5120]{1,0:T(8,128)(2,1)} %get-tuple-element.52), channel_id=1, source_target_pairs={{0,16},{8,24},{16,0},{24,8},{1,17},{9,25},{17,1},{25,9},{2,18},{10... | collective-permute-start | bytes 1966088 | tf_op jit(solution)/shard_map/ppermute | solution.py:500
  6.4 4.0 %cast_rows.1 = (bf16[384,2048]{1,0:T(8,128)(2,1)}, bf16[256,2048]{1,0:T(8,128)(2,1)}) custom-call(f32[1,512,2048]{2,1,0:T(8,128)} %refs_0_.2, f32[1,256,2048]{2,1,0:T(8,128)} %refs_1_.3), custom_call_target="tpu_custom_call" | custom-call | tf_op jit(solution)/shard_map/cast_rows/pallas_call | solution.py:313
  10.6 11.6 %collective-permute-done.1.first.refs_20_.refs_21_ = bf16[64,5120]{1,0:T(8,128)(2,1)S(1)} collective-permute-done((bf16[64,5120]{1,0:T(8,128)(2,1)}, bf16[64,5120]{1,0:T(8,128)(2,1)S(1)}, u32[]{:S(2)}, u32[]{:S(2)}) %collective-permute-start.1) | collective-permute-done | bytes 655392 | tf_op jit(solution)/shard_map/ppermute | solution.py:500
  26.8 1.3 %norm.1 = (bf16[64,2048]{1,0:T(8,128)(2,1)S(1)}, bf16[32,2176]{1,0:T(8,128)(2,1)S(1)}, bf16[32,2176]{1,0:T(8,128)(2,1)S(1)}) custom-call(bf16[64,2048]{1,0:T(8,128)(2,1)S(1)} %bitcast.6, bf16[64,512]{1,0:T(8,128)(2,1)S(1)} %copy-done.6, bf16[64,512]{1,0:T(8,128)(2,1)} %collective-permute-done.a1, ...), custom_call_target="tpu_custom_call" | custom-call | flops 1 | bytes 1 | tf_op jit(solution)/shard_map/norm/pallas_call | solution.py:259
  28.0 2.2 %collective-permute-start.10 = (bf16[32,2176]{1,0:T(8,128)(2,1)S(1)}, bf16[32,2176]{1,0:T(8,128)(2,1)S(1)}, u32[]{:S(2)}, u32[]{:S(2)}) collective-permute-start(bf16[32,2176]{1,0:T(8,128)(2,1)S(1)} %get-tuple-element.55.refs_1_), channel_id=1, source_target_pairs={{0,2},{2,4},{4,6},{6,7},{7,5},{5,3},{3,1},{1,0},{8,10},{10,12},{12... | collective-permute-start | bytes 417800 | tf_op jit(solution)/shard_map/ppermute | solution.py:510
  30.2 2.0 %collective-permute-start.14 = (bf16[32,2176]{1,0:T(8,128)(2,1)S(1)}, bf16[32,2176]{1,0:T(8,128)(2,1)S(1)}, u32[]{:S(2)}, u32[]{:S(2)}) collective-permute-start(bf16[32,2176]{1,0:T(8,128)(2,1)S(1)} %get-tuple-element.54.refs_0_), channel_id=1, source_target_pairs={{0,2},{2,4},{4,6},{6,7},{7,5},{5,3},{3,1},{1,0},{8,10},{10,12},{12... | collective-permute-start | bytes 417800 | tf_op jit(solution)/shard_map/ppermute | solution.py:510
  32.3 2.3 %collective-permute-done.10.refs_15_ = bf16[32,2176]{1,0:T(8,128)(2,1)S(1)} collective-permute-done((bf16[32,2176]{1,0:T(8,128)(2,1)S(1)}, bf16[32,2176]{1,0:T(8,128)(2,1)S(1)}, u32[]{:S(2)}, u32[]{:S(2)}) %collective-permute-start.10) | collective-permute-done | bytes 139296 | tf_op jit(solution)/shard_map/ppermute | solution.py:510
  34.6 2.1 %collective-permute-start.11 = (bf16[32,2176]{1,0:T(8,128)(2,1)S(1)}, bf16[32,2176]{1,0:T(8,128)(2,1)S(1)}, u32[]{:S(2)}, u32[]{:S(2)}) collective-permute-start(bf16[32,2176]{1,0:T(8,128)(2,1)S(1)} %collective-permute-done.10.refs_15_), channel_id=1, source_target_pairs={{0,2},{2,4},{4,6},{6,7},{7,5},{5,3},{3,1},{1,0},{8,10},{10,12},{12... | collective-permute-start | bytes 417800 | tf_op jit(solution)/shard_map/ppermute | solution.py:510
  37.6 2.1 %collective-permute-start.15 = (bf16[32,2176]{1,0:T(8,128)(2,1)S(1)}, bf16[32,2176]{1,0:T(8,128)(2,1)S(1)}, u32[]{:S(2)}, u32[]{:S(2)}) collective-permute-start(bf16[32,2176]{1,0:T(8,128)(2,1)S(1)} %collective-permute-done.14.refs_14_), channel_id=1, source_target_pairs={{0,2},{2,4},{4,6},{6,7},{7,5},{5,3},{3,1},{1,0},{8,10},{10,12},{12... | collective-permute-start | bytes 417800 | tf_op jit(solution)/shard_map/ppermute | solution.py:510
  40.8 2.2 %collective-permute-start.12 = (bf16[32,2176]{1,0:T(8,128)(2,1)S(1)}, bf16[32,2176]{1,0:T(8,128)(2,1)S(1)}, u32[]{:S(2)}, u32[]{:S(2)}) collective-permute-start(bf16[32,2176]{1,0:T(8,128)(2,1)S(1)} %collective-permute-done.11.refs_13_), channel_id=1, source_target_pairs={{0,2},{2,4},{4,6},{6,7},{7,5},{5,3},{3,1},{1,0},{8,10},{10,12},{12... | collective-permute-start | bytes 417800 | tf_op jit(solution)/shard_map/ppermute | solution.py:510
  43.0 1.2 %collective-permute-done.15.refs_12_ = bf16[32,2176]{1,0:T(8,128)(2,1)S(1)} collective-permute-done((bf16[32,2176]{1,0:T(8,128)(2,1)S(1)}, bf16[32,2176]{1,0:T(8,128)(2,1)S(1)}, u32[]{:S(2)}, u32[]{:S(2)}) %collective-permute-start.15) | collective-permute-done | bytes 139296 | tf_op jit(solution)/shard_map/ppermute | solution.py:510
  44.2 2.1 %collective-permute-start.16 = (bf16[32,2176]{1,0:T(8,128)(2,1)S(1)}, bf16[32,2176]{1,0:T(8,128)(2,1)S(1)}, u32[]{:S(2)}, u32[]{:S(2)}) collective-permute-start(bf16[32,2176]{1,0:T(8,128)(2,1)S(1)} %collective-permute-done.15.refs_12_), channel_id=1, source_target_pairs={{0,2},{2,4},{4,6},{6,7},{7,5},{5,3},{3,1},{1,0},{8,10},{10,12},{12... | collective-permute-start | bytes 417800 | tf_op jit(solution)/shard_map/ppermute | solution.py:510
  46.3 1.2 %collective-permute-done.12.refs_11_ = bf16[32,2176]{1,0:T(8,128)(2,1)S(1)} collective-permute-done((bf16[32,2176]{1,0:T(8,128)(2,1)S(1)}, bf16[32,2176]{1,0:T(8,128)(2,1)S(1)}, u32[]{:S(2)}, u32[]{:S(2)}) %collective-permute-start.12) | collective-permute-done | bytes 139296 | tf_op jit(solution)/shard_map/ppermute | solution.py:510
  47.5 2.0 %collective-permute-start.8 = (bf16[32,2176]{1,0:T(8,128)(2,1)S(1)}, bf16[32,2176]{1,0:T(8,128)(2,1)S(1)}, u32[]{:S(2)}, u32[]{:S(2)}) collective-permute-start(bf16[32,2176]{1,0:T(8,128)(2,1)S(1)} %collective-permute-done.6.refs_5_), channel_id=1, source_target_pairs={{0,1},{2,0},{4,2},{6,4},{7,6},{5,7},{3,5},{1,3},{8,9},{10,8},{12,1... | collective-permute-start | bytes 417800 | tf_op jit(solution)/shard_map/ppermute | solution.py:510
  49.6 1.9 %collective-permute-start.9 = (bf16[32,2176]{1,0:T(8,128)(2,1)S(1)}, bf16[32,2176]{1,0:T(8,128)(2,1)S(1)}, u32[]{:S(2)}, u32[]{:S(2)}) collective-permute-start(bf16[32,2176]{1,0:T(8,128)(2,1)S(1)} %collective-permute-done.7.refs_6_), channel_id=1, source_target_pairs={{0,1},{2,0},{4,2},{6,4},{7,6},{5,7},{3,5},{1,3},{8,9},{10,8},{12,1... | collective-permute-start | bytes 417800 | tf_op jit(solution)/shard_map/ppermute | solution.py:510
  51.6 2.3 %collective-permute-done.8.refs_7_ = bf16[32,2176]{1,0:T(8,128)(2,1)S(1)} collective-permute-done((bf16[32,2176]{1,0:T(8,128)(2,1)S(1)}, bf16[32,2176]{1,0:T(8,128)(2,1)S(1)}, u32[]{:S(2)}, u32[]{:S(2)}) %collective-permute-start.8) | collective-permute-done | bytes 139296 | tf_op jit(solution)/shard_map/ppermute | solution.py:510
  55.4 1.5 %collective-permute-start.25 = (bf16[256,2048]{1,0:T(8,128)(2,1)S(1)}, bf16[256,2048]{1,0:T(8,128)(2,1)S(1)}, u32[]{:S(2)}, u32[]{:S(2)}) collective-permute-start(bf16[256,2048]{1,0:T(8,128)(2,1)S(1)} %copy-done.1), channel_id=1, source_target_pairs={{0,16},{8,24},{16,0},{24,8},{1,17},{9,25},{17,1},{25,9},{2,18},{10... | collective-permute-start | bytes 3145736 | tf_op jit(solution)/shard_map/ppermute | solution.py:500
  57.7 3.6 %collective-permute-done.17.refs_18_ = bf16[128,2048]{1,0:T(8,128)(2,1)S(1)} collective-permute-done((bf16[128,2048]{1,0:T(8,128)(2,1)S(1)}, bf16[128,2048]{1,0:T(8,128)(2,1)S(1)}, u32[]{:S(2)}, u32[]{:S(2)}) %collective-permute-start.17) | collective-permute-done | bytes 524320 | tf_op jit(solution)/shard_map/ppermute | solution.py:500
  61.4 8.1 %expert_up.1 = (bf16[512,1024]{1,0:T(8,128)(2,1)S(1)}, f32[512,1]{1,0:T(8,128)S(1)}) custom-call(bf16[32,2176]{1,0:T(8,128)(2,1)S(1)} %get-tuple-element.54.refs_0_, bf16[32,2176]{1,0:T(8,128)(2,1)S(1)} %get-tuple-element.55.refs_1_, bf16[32,2176]{1,0:T(8,128)(2,1)S(1)} %collective-permute-done.3.refs_2_, ...), custom_call_target="tpu_custom_call" | custom-call | flops 1 | bytes 1 | tf_op jit(solution)/shard_map/expert_up/pallas_call | solution.py:392
  69.5 10.7 %collective-permute-done.25.refs_2_ = bf16[256,2048]{1,0:T(8,128)(2,1)S(1)} collective-permute-done((bf16[256,2048]{1,0:T(8,128)(2,1)S(1)}, bf16[256,2048]{1,0:T(8,128)(2,1)S(1)}, u32[]{:S(2)}, u32[]{:S(2)}) %collective-permute-start.25) | collective-permute-done | bytes 1048608 | tf_op jit(solution)/shard_map/ppermute | solution.py:500
  80.8 2.0 %down_part.1.refs_1_ = f32[512,2048]{1,0:T(8,128)S(1)} custom-call(bf16[512,1024]{1,0:T(8,128)(2,1)S(1)} %get-tuple-element.61.hidden_ref.refs_0_, bf16[256,2048]{1,0:T(8,128)(2,1)S(1)} %copy-done.1, bf16[256,2048]{1,0:T(8,128)(2,1)S(1)} %collective-permute-done.24.refs_1_, bf16[256,2048]{1,0:T(8,128)(2,1)S(1)} %collective-permute-done.25.refs_2_), custom_call_target="tpu_custom_call" | custom-call | flops 1 | bytes 1 | tf_op jit(solution)/shard_map/down_part/pallas_call | solution.py:437
  86.0 1.1 collective-permute-start.27
  88.1 1.1 collective-permute-start.37
  90.8 1.2 %collective-permute-start.28 = (bf16[64,1024]{1,0:T(8,128)(2,1)S(1)}, bf16[64,1024]{1,0:T(8,128)(2,1)S(1)}, u32[]{:S(2)}, u32[]{:S(2)}) collective-permute-start(bf16[64,1024]{1,0:T(8,128)(2,1)S(1)} %pad_maximum_fusion), channel_id=1, source_target_pairs={{0,2},{2,4},{4,6},{6,7},{7,5},{5,3},{3,1},{1,0},{8,10},{10,12},{12... | collective-permute-start | bytes 393224 | tf_op jit(solution)/shard_map/ppermute | solution.py:510
  93.1 1.4 %collective-permute-done.37 = bf16[64,1024]{1,0:T(8,128)(2,1)S(1)} collective-permute-done((bf16[64,1024]{1,0:T(8,128)(2,1)S(1)}, bf16[64,1024]{1,0:T(8,128)(2,1)S(1)}, u32[]{:S(2)}, u32[]{:S(2)}) %collective-permute-start.37) | collective-permute-done | bytes 131104 | tf_op jit(solution)/shard_map/ppermute | solution.py:510
  94.5 1.1 collective-permute-start.38
  97.3 1.2 %collective-permute-start.29 = (bf16[64,1024]{1,0:T(8,128)(2,1)S(1)}, bf16[64,1024]{1,0:T(8,128)(2,1)S(1)}, u32[]{:S(2)}, u32[]{:S(2)}) collective-permute-start(bf16[64,1024]{1,0:T(8,128)(2,1)S(1)} %add_convert_fusion.9), channel_id=1, source_target_pairs={{0,2},{2,4},{4,6},{6,7},{7,5},{5,3},{3,1},{1,0},{8,10},{10,12},{12... | collective-permute-start | bytes 393224 | tf_op jit(solution)/shard_map/ppermute | solution.py:510
  102.3 1.3 %collective-permute-done.29 = bf16[64,1024]{1,0:T(8,128)(2,1)S(1)} collective-permute-done((bf16[64,1024]{1,0:T(8,128)(2,1)S(1)}, bf16[64,1024]{1,0:T(8,128)(2,1)S(1)}, u32[]{:S(2)}, u32[]{:S(2)}) %collective-permute-start.29) | collective-permute-done | bytes 131104 | tf_op jit(solution)/shard_map/ppermute | solution.py:510
  103.7 1.2 %collective-permute-start.30 = (bf16[64,1024]{1,0:T(8,128)(2,1)S(1)}, bf16[64,1024]{1,0:T(8,128)(2,1)S(1)}, u32[]{:S(2)}, u32[]{:S(2)}) collective-permute-start(bf16[64,1024]{1,0:T(8,128)(2,1)S(1)} %add_convert_fusion.8), channel_id=1, source_target_pairs={{0,2},{2,4},{4,6},{6,7},{7,5},{5,3},{3,1},{1,0},{8,10},{10,12},{12... | collective-permute-start | bytes 393224 | tf_op jit(solution)/shard_map/ppermute | solution.py:510
  106.7 2.0 %collective-permute-done.30 = bf16[64,1024]{1,0:T(8,128)(2,1)S(1)} collective-permute-done((bf16[64,1024]{1,0:T(8,128)(2,1)S(1)}, bf16[64,1024]{1,0:T(8,128)(2,1)S(1)}, u32[]{:S(2)}, u32[]{:S(2)}) %collective-permute-start.30) | collective-permute-done | bytes 131104 | tf_op jit(solution)/shard_map/ppermute | solution.py:510
  108.7 1.3 %collective-permute-done.34 = bf16[64,1024]{1,0:T(8,128)(2,1)S(1)} collective-permute-done((bf16[64,1024]{1,0:T(8,128)(2,1)S(1)}, bf16[64,1024]{1,0:T(8,128)(2,1)S(1)}, u32[]{:S(2)}, u32[]{:S(2)}) %collective-permute-start.34) | collective-permute-done | bytes 131104 | tf_op jit(solution)/shard_map/ppermute | solution.py:510
  (107 shorter events, 25.0 us)
Async XLA Ops:
  3.4 18.8 %collective-permute-start.1 = (bf16[64,5120]{1,0:T(8,128)(2,1)}, bf16[64,5120]{1,0:T(8,128)(2,1)S(1)}, u32[]{:S(2)}, u32[]{:S(2)}) collective-permute-start(bf16[64,5120]{1,0:T(8,128)(2,1)} %get-tuple-element.52), channel_id=1, source_target_pairs={{0,16},{8,24},{16,0},{24,8},{1,17},{9,25},{17,1},{25,9},{2,18},{10... | collective-permute-start | bytes 1966088 | tf_op jit(solution)/shard_map/ppermute | solution.py:500
  10.4 46.5 %collective-permute-start.19 = (bf16[384,2048]{1,0:T(8,128)(2,1)}, bf16[384,2048]{1,0:T(8,128)(2,1)S(1)}, u32[]{:S(2)}, u32[]{:S(2)}) collective-permute-start(bf16[384,2048]{1,0:T(8,128)(2,1)} %get-tuple-element.58.refs_17_), channel_id=1, source_target_pairs={{0,16},{8,24},{16,0},{24,8},{1,17},{9,25},{17,1},{25,9},{2,18},{10... | collective-permute-start | bytes 4718600 | tf_op jit(solution)/shard_map/ppermute | solution.py:500
  10.5 13.7 %collective-permute-start = (bf16[64,512]{1,0:T(8,128)(2,1)}, bf16[64,512]{1,0:T(8,128)(2,1)}, u32[]{:S(2)}, u32[]{:S(2)}) collective-permute-start(bf16[64,512]{1,0:T(8,128)(2,1)} %get-tuple-element.51), channel_id=1, source_target_pairs={{0,8},{8,0},{16,24},{24,16},{1,9},{9,1},{17,25},{25,17},{2,10},{10... | collective-permute-start | bytes 196616 | tf_op jit(solution)/shard_map/ppermute | solution.py:500
  28.0 6.6 %collective-permute-start.10 = (bf16[32,2176]{1,0:T(8,128)(2,1)S(1)}, bf16[32,2176]{1,0:T(8,128)(2,1)S(1)}, u32[]{:S(2)}, u32[]{:S(2)}) collective-permute-start(bf16[32,2176]{1,0:T(8,128)(2,1)S(1)} %get-tuple-element.55.refs_1_), channel_id=1, source_target_pairs={{0,2},{2,4},{4,6},{6,7},{7,5},{5,3},{3,1},{1,0},{8,10},{10,12},{12... | collective-permute-start | bytes 417800 | tf_op jit(solution)/shard_map/ppermute | solution.py:510
  30.2 6.5 %collective-permute-start.3 = (bf16[32,2176]{1,0:T(8,128)(2,1)S(1)}, bf16[32,2176]{1,0:T(8,128)(2,1)S(1)}, u32[]{:S(2)}, u32[]{:S(2)}) collective-permute-start(bf16[32,2176]{1,0:T(8,128)(2,1)S(1)} %get-tuple-element.54.refs_0_), channel_id=1, source_target_pairs={{0,1},{2,0},{4,2},{6,4},{7,6},{5,7},{3,5},{1,3},{8,9},{10,8},{12,1... | collective-permute-start | bytes 417800 | tf_op jit(solution)/shard_map/ppermute | solution.py:510
  30.2 7.4 %collective-permute-start.14 = (bf16[32,2176]{1,0:T(8,128)(2,1)S(1)}, bf16[32,2176]{1,0:T(8,128)(2,1)S(1)}, u32[]{:S(2)}, u32[]{:S(2)}) collective-permute-start(bf16[32,2176]{1,0:T(8,128)(2,1)S(1)} %get-tuple-element.54.refs_0_), channel_id=1, source_target_pairs={{0,2},{2,4},{4,6},{6,7},{7,5},{5,3},{3,1},{1,0},{8,10},{10,12},{12... | collective-permute-start | bytes 417800 | tf_op jit(solution)/shard_map/ppermute | solution.py:510
  32.3 7.5 %collective-permute-start.4 = (bf16[32,2176]{1,0:T(8,128)(2,1)S(1)}, bf16[32,2176]{1,0:T(8,128)(2,1)S(1)}, u32[]{:S(2)}, u32[]{:S(2)}) collective-permute-start(bf16[32,2176]{1,0:T(8,128)(2,1)S(1)} %get-tuple-element.55.refs_1_), channel_id=1, source_target_pairs={{0,1},{2,0},{4,2},{6,4},{7,6},{5,7},{3,5},{1,3},{8,9},{10,8},{12,1... | collective-permute-start | bytes 417800 | tf_op jit(solution)/shard_map/ppermute | solution.py:510
  34.6 6.2 %collective-permute-start.11 = (bf16[32,2176]{1,0:T(8,128)(2,1)S(1)}, bf16[32,2176]{1,0:T(8,128)(2,1)S(1)}, u32[]{:S(2)}, u32[]{:S(2)}) collective-permute-start(bf16[32,2176]{1,0:T(8,128)(2,1)S(1)} %collective-permute-done.10.refs_15_), channel_id=1, source_target_pairs={{0,2},{2,4},{4,6},{6,7},{7,5},{5,3},{3,1},{1,0},{8,10},{10,12},{12... | collective-permute-start | bytes 417800 | tf_op jit(solution)/shard_map/ppermute | solution.py:510
  36.8 6.2 %collective-permute-start.5 = (bf16[32,2176]{1,0:T(8,128)(2,1)S(1)}, bf16[32,2176]{1,0:T(8,128)(2,1)S(1)}, u32[]{:S(2)}, u32[]{:S(2)}) collective-permute-start(bf16[32,2176]{1,0:T(8,128)(2,1)S(1)} %collective-permute-done.3.refs_2_), channel_id=1, source_target_pairs={{0,1},{2,0},{4,2},{6,4},{7,6},{5,7},{3,5},{1,3},{8,9},{10,8},{12,1... | collective-permute-start | bytes 417800 | tf_op jit(solution)/shard_map/ppermute | solution.py:510
  37.6 6.6 %collective-permute-start.15 = (bf16[32,2176]{1,0:T(8,128)(2,1)S(1)}, bf16[32,2176]{1,0:T(8,128)(2,1)S(1)}, u32[]{:S(2)}, u32[]{:S(2)}) collective-permute-start(bf16[32,2176]{1,0:T(8,128)(2,1)S(1)} %collective-permute-done.14.refs_14_), channel_id=1, source_target_pairs={{0,2},{2,4},{4,6},{6,7},{7,5},{5,3},{3,1},{1,0},{8,10},{10,12},{12... | collective-permute-start | bytes 417800 | tf_op jit(solution)/shard_map/ppermute | solution.py:510
  39.7 6.6 %collective-permute-start.6 = (bf16[32,2176]{1,0:T(8,128)(2,1)S(1)}, bf16[32,2176]{1,0:T(8,128)(2,1)S(1)}, u32[]{:S(2)}, u32[]{:S(2)}) collective-permute-start(bf16[32,2176]{1,0:T(8,128)(2,1)S(1)} %collective-permute-done.4.refs_3_), channel_id=1, source_target_pairs={{0,1},{2,0},{4,2},{6,4},{7,6},{5,7},{3,5},{1,3},{8,9},{10,8},{12,1... | collective-permute-start | bytes 417800 | tf_op jit(solution)/shard_map/ppermute | solution.py:510
  40.8 6.7 %collective-permute-start.12 = (bf16[32,2176]{1,0:T(8,128)(2,1)S(1)}, bf16[32,2176]{1,0:T(8,128)(2,1)S(1)}, u32[]{:S(2)}, u32[]{:S(2)}) collective-permute-start(bf16[32,2176]{1,0:T(8,128)(2,1)S(1)} %collective-permute-done.11.refs_13_), channel_id=1, source_target_pairs={{0,2},{2,4},{4,6},{6,7},{7,5},{5,3},{3,1},{1,0},{8,10},{10,12},{12... | collective-permute-start | bytes 417800 | tf_op jit(solution)/shard_map/ppermute | solution.py:510
  43.0 6.5 %collective-permute-start.7 = (bf16[32,2176]{1,0:T(8,128)(2,1)S(1)}, bf16[32,2176]{1,0:T(8,128)(2,1)S(1)}, u32[]{:S(2)}, u32[]{:S(2)}) collective-permute-start(bf16[32,2176]{1,0:T(8,128)(2,1)S(1)} %collective-permute-done.5.refs_4_), channel_id=1, source_target_pairs={{0,1},{2,0},{4,2},{6,4},{7,6},{5,7},{3,5},{1,3},{8,9},{10,8},{12,1... | collective-permute-start | bytes 417800 | tf_op jit(solution)/shard_map/ppermute | solution.py:510
  44.2 5.4 %collective-permute-start.16 = (bf16[32,2176]{1,0:T(8,128)(2,1)S(1)}, bf16[32,2176]{1,0:T(8,128)(2,1)S(1)}, u32[]{:S(2)}, u32[]{:S(2)}) collective-permute-start(bf16[32,2176]{1,0:T(8,128)(2,1)S(1)} %collective-permute-done.15.refs_12_), channel_id=1, source_target_pairs={{0,2},{2,4},{4,6},{6,7},{7,5},{5,3},{3,1},{1,0},{8,10},{10,12},{12... | collective-permute-start | bytes 417800 | tf_op jit(solution)/shard_map/ppermute | solution.py:510
  46.3 15.1 %collective-permute-start.18 = (bf16[384,2048]{1,0:T(8,128)(2,1)}, bf16[384,2048]{1,0:T(8,128)(2,1)S(1)}, u32[]{:S(2)}, u32[]{:S(2)}) collective-permute-start(bf16[384,2048]{1,0:T(8,128)(2,1)} %get-tuple-element.58.refs_17_), channel_id=1, source_target_pairs={{0,8},{8,0},{16,24},{24,16},{1,9},{9,1},{17,25},{25,17},{2,10},{10... | collective-permute-start | bytes 4718600 | tf_op jit(solution)/shard_map/ppermute | solution.py:500
  47.5 6.4 %collective-permute-start.8 = (bf16[32,2176]{1,0:T(8,128)(2,1)S(1)}, bf16[32,2176]{1,0:T(8,128)(2,1)S(1)}, u32[]{:S(2)}, u32[]{:S(2)}) collective-permute-start(bf16[32,2176]{1,0:T(8,128)(2,1)S(1)} %collective-permute-done.6.refs_5_), channel_id=1, source_target_pairs={{0,1},{2,0},{4,2},{6,4},{7,6},{5,7},{3,5},{1,3},{8,9},{10,8},{12,1... | collective-permute-start | bytes 417800 | tf_op jit(solution)/shard_map/ppermute | solution.py:510
  49.5 5.1 %collective-permute-start.13 = (bf16[32,2176]{1,0:T(8,128)(2,1)S(1)}, bf16[32,2176]{1,0:T(8,128)(2,1)S(1)}, u32[]{:S(2)}, u32[]{:S(2)}) collective-permute-start(bf16[32,2176]{1,0:T(8,128)(2,1)S(1)} %collective-permute-done.12.refs_11_), channel_id=1, source_target_pairs={{0,2},{2,4},{4,6},{6,7},{7,5},{5,3},{3,1},{1,0},{8,10},{10,12},{12... | collective-permute-start | bytes 417800 | tf_op jit(solution)/shard_map/ppermute | solution.py:510
  49.6 5.8 %collective-permute-start.9 = (bf16[32,2176]{1,0:T(8,128)(2,1)S(1)}, bf16[32,2176]{1,0:T(8,128)(2,1)S(1)}, u32[]{:S(2)}, u32[]{:S(2)}) collective-permute-start(bf16[32,2176]{1,0:T(8,128)(2,1)S(1)} %collective-permute-done.7.refs_6_), channel_id=1, source_target_pairs={{0,1},{2,0},{4,2},{6,4},{7,6},{5,7},{3,5},{1,3},{8,9},{10,8},{12,1... | collective-permute-start | bytes 417800 | tf_op jit(solution)/shard_map/ppermute | solution.py:510
  55.4 24.7 %collective-permute-start.25 = (bf16[256,2048]{1,0:T(8,128)(2,1)S(1)}, bf16[256,2048]{1,0:T(8,128)(2,1)S(1)}, u32[]{:S(2)}, u32[]{:S(2)}) collective-permute-start(bf16[256,2048]{1,0:T(8,128)(2,1)S(1)} %copy-done.1), channel_id=1, source_target_pairs={{0,16},{8,24},{16,0},{24,8},{1,17},{9,25},{17,1},{25,9},{2,18},{10... | collective-permute-start | bytes 3145736 | tf_op jit(solution)/shard_map/ppermute | solution.py:500
  61.2 19.6 %collective-permute-start.24 = (bf16[256,2048]{1,0:T(8,128)(2,1)S(1)}, bf16[256,2048]{1,0:T(8,128)(2,1)S(1)}, u32[]{:S(2)}, u32[]{:S(2)}) collective-permute-start(bf16[256,2048]{1,0:T(8,128)(2,1)S(1)} %copy-done.1), channel_id=1, source_target_pairs={{0,8},{8,0},{16,24},{24,16},{1,9},{9,1},{17,25},{25,17},{2,10},{10... | collective-permute-start | bytes 3145736 | tf_op jit(solution)/shard_map/ppermute | solution.py:500
  80.3 5.2 %collective-permute-start.26 = (bf16[256,1024]{1,0:T(8,128)(2,1)S(1)}, bf16[256,1024]{1,0:T(8,128)(2,1)S(1)}, u32[]{:S(2)}, u32[]{:S(2)}) collective-permute-start(bf16[256,1024]{1,0:T(8,128)(2,1)S(1)} %get-tuple-element.91), channel_id=1, source_target_pairs={{0,8},{8,0},{16,24},{24,16},{1,9},{9,1},{17,25},{25,17},{2,10},{10... | collective-permute-start | bytes 1572872 | tf_op jit(solution)/shard_map/ppermute | solution.py:500
  88.1 6.4 %collective-permute-start.37 = (bf16[64,1024]{1,0:T(8,128)(2,1)S(1)}, bf16[64,1024]{1,0:T(8,128)(2,1)S(1)}, u32[]{:S(2)}, u32[]{:S(2)}) collective-permute-start(bf16[64,1024]{1,0:T(8,128)(2,1)S(1)} %pad_maximum_fusion.2), channel_id=1, source_target_pairs={{0,2},{2,4},{4,6},{6,7},{7,5},{5,3},{3,1},{1,0},{8,10},{10,12},{12... | collective-permute-start | bytes 393224 | tf_op jit(solution)/shard_map/ppermute | solution.py:510
  89.2 6.4 %collective-permute-start.41 = (bf16[64,1024]{1,0:T(8,128)(2,1)S(1)}, bf16[64,1024]{1,0:T(8,128)(2,1)S(1)}, u32[]{:S(2)}, u32[]{:S(2)}) collective-permute-start(bf16[64,1024]{1,0:T(8,128)(2,1)S(1)} %pad_maximum_fusion.3), channel_id=1, source_target_pairs={{0,1},{2,0},{4,2},{6,4},{7,6},{5,7},{3,5},{1,3},{8,9},{10,8},{12,1... | collective-permute-start | bytes 393224 | tf_op jit(solution)/shard_map/ppermute | solution.py:510
  90.8 6.4 %collective-permute-start.28 = (bf16[64,1024]{1,0:T(8,128)(2,1)S(1)}, bf16[64,1024]{1,0:T(8,128)(2,1)S(1)}, u32[]{:S(2)}, u32[]{:S(2)}) collective-permute-start(bf16[64,1024]{1,0:T(8,128)(2,1)S(1)} %pad_maximum_fusion), channel_id=1, source_target_pairs={{0,2},{2,4},{4,6},{6,7},{7,5},{5,3},{3,1},{1,0},{8,10},{10,12},{12... | collective-permute-start | bytes 393224 | tf_op jit(solution)/shard_map/ppermute | solution.py:510
  92.0 6.4 %collective-permute-start.32 = (bf16[64,1024]{1,0:T(8,128)(2,1)S(1)}, bf16[64,1024]{1,0:T(8,128)(2,1)S(1)}, u32[]{:S(2)}, u32[]{:S(2)}) collective-permute-start(bf16[64,1024]{1,0:T(8,128)(2,1)S(1)} %pad_maximum_fusion.1), channel_id=1, source_target_pairs={{0,1},{2,0},{4,2},{6,4},{7,6},{5,7},{3,5},{1,3},{8,9},{10,8},{12,1... | collective-permute-start | bytes 393224 | tf_op jit(solution)/shard_map/ppermute | solution.py:510
  94.5 5.6 %collective-permute-start.38 = (bf16[64,1024]{1,0:T(8,128)(2,1)S(1)}, bf16[64,1024]{1,0:T(8,128)(2,1)S(1)}, u32[]{:S(2)}, u32[]{:S(2)}) collective-permute-start(bf16[64,1024]{1,0:T(8,128)(2,1)S(1)} %add_convert_fusion.4), channel_id=1, source_target_pairs={{0,2},{2,4},{4,6},{6,7},{7,5},{5,3},{3,1},{1,0},{8,10},{10,12},{12... | collective-permute-start | bytes 393224 | tf_op jit(solution)/shard_map/ppermute | solution.py:510
  95.7 5.6 %collective-permute-start.42 = (bf16[64,1024]{1,0:T(8,128)(2,1)S(1)}, bf16[64,1024]{1,0:T(8,128)(2,1)S(1)}, u32[]{:S(2)}, u32[]{:S(2)}) collective-permute-start(bf16[64,1024]{1,0:T(8,128)(2,1)S(1)} %add_convert_fusion.2), channel_id=1, source_target_pairs={{0,1},{2,0},{4,2},{6,4},{7,6},{5,7},{3,5},{1,3},{8,9},{10,8},{12,1... | collective-permute-start | bytes 393224 | tf_op jit(solution)/shard_map/ppermute | solution.py:510
  97.3 6.4 %collective-permute-start.29 = (bf16[64,1024]{1,0:T(8,128)(2,1)S(1)}, bf16[64,1024]{1,0:T(8,128)(2,1)S(1)}, u32[]{:S(2)}, u32[]{:S(2)}) collective-permute-start(bf16[64,1024]{1,0:T(8,128)(2,1)S(1)} %add_convert_fusion.9), channel_id=1, source_target_pairs={{0,2},{2,4},{4,6},{6,7},{7,5},{5,3},{3,1},{1,0},{8,10},{10,12},{12... | collective-permute-start | bytes 393224 | tf_op jit(solution)/shard_map/ppermute | solution.py:510
  98.5 6.5 %collective-permute-start.33 = (bf16[64,1024]{1,0:T(8,128)(2,1)S(1)}, bf16[64,1024]{1,0:T(8,128)(2,1)S(1)}, u32[]{:S(2)}, u32[]{:S(2)}) collective-permute-start(bf16[64,1024]{1,0:T(8,128)(2,1)S(1)} %add_convert_fusion.7), channel_id=1, source_target_pairs={{0,1},{2,0},{4,2},{6,4},{7,6},{5,7},{3,5},{1,3},{8,9},{10,8},{12,1... | collective-permute-start | bytes 393224 | tf_op jit(solution)/shard_map/ppermute | solution.py:510
  100.1 5.9 %collective-permute-start.39 = (bf16[64,1024]{1,0:T(8,128)(2,1)S(1)}, bf16[64,1024]{1,0:T(8,128)(2,1)S(1)}, u32[]{:S(2)}, u32[]{:S(2)}) collective-permute-start(bf16[64,1024]{1,0:T(8,128)(2,1)S(1)} %add_convert_fusion.3), channel_id=1, source_target_pairs={{0,2},{2,4},{4,6},{6,7},{7,5},{5,3},{3,1},{1,0},{8,10},{10,12},{12... | collective-permute-start | bytes 393224 | tf_op jit(solution)/shard_map/ppermute | solution.py:510
  101.3 5.4 %collective-permute-start.43 = (bf16[64,1024]{1,0:T(8,128)(2,1)S(1)}, bf16[64,1024]{1,0:T(8,128)(2,1)S(1)}, u32[]{:S(2)}, u32[]{:S(2)}) collective-permute-start(bf16[64,1024]{1,0:T(8,128)(2,1)S(1)} %add_convert_fusion.1), channel_id=1, source_target_pairs={{0,1},{2,0},{4,2},{6,4},{7,6},{5,7},{3,5},{1,3},{8,9},{10,8},{12,1... | collective-permute-start | bytes 393224 | tf_op jit(solution)/shard_map/ppermute | solution.py:510
  103.7 5.0 %collective-permute-start.30 = (bf16[64,1024]{1,0:T(8,128)(2,1)S(1)}, bf16[64,1024]{1,0:T(8,128)(2,1)S(1)}, u32[]{:S(2)}, u32[]{:S(2)}) collective-permute-start(bf16[64,1024]{1,0:T(8,128)(2,1)S(1)} %add_convert_fusion.8), channel_id=1, source_target_pairs={{0,2},{2,4},{4,6},{6,7},{7,5},{5,3},{3,1},{1,0},{8,10},{10,12},{12... | collective-permute-start | bytes 393224 | tf_op jit(solution)/shard_map/ppermute | solution.py:510
  (22 other events, 173.6 us)

commit v13 on v12

--- a/solution.py
+++ b/solution.py
@@ -218,12 +218,22 @@
     )(page_table, prompt_lengths, queries, key_pool, value_pool, gate_up)
 
 
-def norm_kernel(hidden_ref, a0, a1, first, a3, gain_ref, ids_ref, gates_ref, resid_ref, *row_refs):
+def norm_kernel(*refs):
+    sources, outs, scratch = refs[:8], refs[8:11], refs[11:]
+    a0, a1, a2, a3, hidden_ref, gain_ref, ids_ref, gates_ref, arrived = scratch
+    resid_ref, row_refs = outs[0], outs[1:]
+    across, block = sources[2], a2.shape[1]
+    across = across.at[:, pl.ds(across.shape[1] - 2 * block, block)]
+    copies = [
+        pltpu.make_async_copy(source, target, arrived.at[i])
+        for i, (source, target) in enumerate(zip((*sources[:2], across, *sources[3:]), scratch))
+    ]
+    for copy in copies:
+        copy.start()
+    for copy in copies:
+        copy.wait()
     own = lax.axis_index("dp")
     tokens, width = hidden_ref.shape
-    block = width // 4
-    end = first.shape[1]
-    a2 = first.at[:, end - 2 * block : end - block]
     total = jnp.zeros((tokens, 1), jnp.float32)
     for d, attn in enumerate((a0, a1, a2, a3)):
         columns = pl.ds(pl.multiple_of((own ^ d) * block, block), block)
@@ -234,40 +244,44 @@
         resid32 = resid.astype(jnp.float32)
         total += jnp.sum(resid32 * resid32, axis=-1, keepdims=True)
     inverse = lax.rsqrt(total / width + epsilon)
+    halves = [slice(i * tokens // 2, (i + 1) * tokens // 2) for i in range(2)]
     for d in range(4):
         columns = pl.ds(pl.multiple_of((own ^ d) * block, block), block)
         normed = resid_ref[:, columns].astype(jnp.float32) * inverse * gain_ref[:, columns]
-        for i, ref in enumerate(row_refs):
-            here = slice(i * tokens // 2, (i + 1) * tokens // 2)
+        for here, ref in zip(halves, row_refs):
             ref[:, d * block : (d + 1) * block] = normed[here].astype(jnp.bfloat16)
-    lane = lax.broadcasted_iota(jnp.int32, (tokens, LANES), 1)
-    gates = jnp.zeros((tokens, LANES), jnp.float32)
+    place = lax.broadcasted_iota(jnp.int32, (LANES, tokens), 0)
+    gates = jnp.zeros((LANES, tokens), jnp.float32)
     for k in range(TOPK):
-        gates += jnp.where(ids_ref[:, k : k + 1] == lane % TOPK, gates_ref[:, k : k + 1], 0.0)
+        gates += jnp.where(ids_ref[k : k + 1] == place % TOPK, gates_ref[k : k + 1], 0.0)
     high = gates.astype(jnp.bfloat16).astype(jnp.float32)
     middle = (gates - high).astype(jnp.bfloat16).astype(jnp.float32)
     low = gates - high - middle
-    part = lane // TOPK
+    part = place // TOPK
     terms = jnp.where(part == 0, high, jnp.where(part == 1, middle, jnp.where(part == 2, low, 0.0)))
-    for i, ref in enumerate(row_refs):
-        here = slice(i * tokens // 2, (i + 1) * tokens // 2)
+    terms = jnp.transpose(terms)
+    for here, ref in zip(halves, row_refs):
         ref[:, width:] = terms[here].astype(jnp.bfloat16)
 
 
 def norm(hidden_in, attn, norm_gain, expert_ids, gate_weights):
     tokens, width = hidden_in.shape
+    operands = hidden_in, norm_gain[None, :], expert_ids.T, gate_weights.T
     return pl.pallas_call(
         norm_kernel,
         out_shape=[
             jax.ShapeDtypeStruct((tokens, width), jnp.bfloat16),
         ]
         + [jax.ShapeDtypeStruct((tokens // 2, width + LANES), jnp.bfloat16)] * 2,
-        in_specs=vmem(8),
+        in_specs=[pl.BlockSpec(memory_space=pl.ANY)] * 8,
         out_specs=vmem(3),
+        scratch_shapes=[pltpu.VMEM(attn[0].shape, jnp.bfloat16)] * 4
+        + [pltpu.VMEM(x.shape, x.dtype) for x in operands]
+        + [pltpu.SemaphoreType.DMA((8,))],
         compiler_params=params(),
         cost_estimate=SMALL,
         name="norm",
-    )(hidden_in, *attn, norm_gain[None, :], expert_ids, gate_weights)
+    )(*attn, *operands)
 
 
 def cast_kernel(spans, *refs):

time: 111 us -> 109 us (0.982)
  local copies, waits for them, and re-layouts: 4.59 us -> 0.32 us
  waiting for transfers between devices: 45 us -> 48.3 us
    unnamed x22 -> x18, local copies, waits for them, and re-layouts: 3.76 us -> 0.04 us
    ppermute x14, waiting for transfers between devices: 26 us -> 28.3 us  [partner(): return lax.ppermute(x, 'dp', [(i, i ^ distance) for i in range(4)])]
  transfers between devices with their start and end apart: 44 -> 44, of which waited for: 21 -> 22; matrix products, arithmetic and copies ran while one was open for 2% -> 1% of each run, Pallas kernels for 15% -> 14%
where the time goes in v13:
time: 109 us
  waiting for transfers between devices  48.3 us (44%)
  starting transfers between devices  39.8 us (37%)
  Pallas kernels  19.1 us (18%)
  other arithmetic  1.28 us (1%)
    ppermute x30, starting transfers between devices, around(): lax.ppermute(x, 'expert', [(ring[i], ring[(i + step) % count]) for i in r...  33.7 us
    ppermute x14, waiting for transfers between devices, partner(): return lax.ppermute(x, 'dp', [(i, i ^ distance) for i in range(4)])  28.3 us
    ppermute x30, waiting for transfers between devices, around(): lax.ppermute(x, 'expert', [(ring[i], ring[(i + step) % count]) for i in r...  20 us
    pallas_call x1, Pallas kernels, expert_up(): pl.pallas_call(lambda *refs: up_kernel(len(rows), starts, *refs), out_sha...  8.07 us
    ppermute x14, starting transfers between devices, partner(): return lax.ppermute(x, 'dp', [(i, i ^ distance) for i in range(4)])  6.07 us
    pallas_call x1, Pallas kernels, cast_rows(): pl.pallas_call(lambda *refs: cast_kernel(spans, *refs), out_shape=[jax.Sh...  3.98 us
    pallas_call x1, Pallas kernels, attention(): pl.pallas_call(attention_kernel, out_shape=[jax.ShapeDtypeStruct(shape, j...  3.4 us
  transfers between devices with their start and end apart: 44, of which 22 were waited for; matrix products, arithmetic and copies ran while one was open for 1% of the time, Pallas kernels for 14%

profile of v13, /device:TPU:0, one launch (start us, length us, event | category | flops | bytes accessed | tf_op | source)
XLA Modules:
  0.0 109.1 jit_solution(18389413290171840746)
XLA Ops:
  0.0 3.4 %attention.1 = (bf16[64,512]{1,0:T(8,128)(2,1)}, bf16[64,512]{1,0:T(8,128)(2,1)}, bf16[64,5120]{1,0:T(8,128)(2,1)}, bf16[128,2048]{1,0:T(8,128)(2,1)}) custom-call(s32[1,2]{1,0:T(1,128)} %refs_0_.1, s32[1,4]{1,0:T(1,128)} %refs_1_.2, bf16[1,256,512]{2,1,0:T(8,128)(2,1)} %refs_2_.1, bf16[2,128,512]{2,1,0:T(8,128)(2,1)} %refs_3_.1, ...), custom_call_target="tpu_custom_call" | custom-call | tf_op jit(solution)/shard_map/attention/pallas_call | solution.py:201
  3.4 3.0 %collective-permute-start.1 = (bf16[64,5120]{1,0:T(8,128)(2,1)}, bf16[64,5120]{1,0:T(8,128)(2,1)S(1)}, u32[]{:S(2)}, u32[]{:S(2)}) collective-permute-start(bf16[64,5120]{1,0:T(8,128)(2,1)} %get-tuple-element.49), channel_id=1, source_target_pairs={{0,16},{8,24},{16,0},{24,8},{1,17},{9,25},{17,1},{25,9},{2,18},{10... | collective-permute-start | bytes 1966088 | tf_op jit(solution)/shard_map/ppermute | solution.py:514
  6.5 4.0 %cast_rows.1 = (bf16[384,2048]{1,0:T(8,128)(2,1)}, bf16[256,2048]{1,0:T(8,128)(2,1)}) custom-call(f32[1,512,2048]{2,1,0:T(8,128)} %refs_0_.2, f32[1,256,2048]{2,1,0:T(8,128)} %refs_1_.3), custom_call_target="tpu_custom_call" | custom-call | tf_op jit(solution)/shard_map/cast_rows/pallas_call | solution.py:327
  10.6 11.6 %collective-permute-done.1.refs_2_.refs_20_.refs_21_ = bf16[64,5120]{1,0:T(8,128)(2,1)S(1)} collective-permute-done((bf16[64,5120]{1,0:T(8,128)(2,1)}, bf16[64,5120]{1,0:T(8,128)(2,1)S(1)}, u32[]{:S(2)}, u32[]{:S(2)}) %collective-permute-start.1) | collective-permute-done | bytes 655392 | tf_op jit(solution)/shard_map/ppermute | solution.py:514
  22.2 1.2 %collective-permute-done.2.refs_3_ = bf16[64,512]{1,0:T(8,128)(2,1)S(1)} collective-permute-done((bf16[64,512]{1,0:T(8,128)(2,1)S(1)}, bf16[64,512]{1,0:T(8,128)(2,1)S(1)}, u32[]{:S(2)}, u32[]{:S(2)}) %collective-permute-start.2) | collective-permute-done | bytes 65568 | tf_op jit(solution)/shard_map/ppermute | solution.py:514
  24.1 2.2 %collective-permute-start.10 = (bf16[32,2176]{1,0:T(8,128)(2,1)S(1)}, bf16[32,2176]{1,0:T(8,128)(2,1)S(1)}, u32[]{:S(2)}, u32[]{:S(2)}) collective-permute-start(bf16[32,2176]{1,0:T(8,128)(2,1)S(1)} %get-tuple-element.55.refs_1_), channel_id=1, source_target_pairs={{0,2},{2,4},{4,6},{6,7},{7,5},{5,3},{3,1},{1,0},{8,10},{10,12},{12... | collective-permute-start | bytes 417800 | tf_op jit(solution)/shard_map/ppermute | solution.py:524
  26.3 2.0 %collective-permute-start.14 = (bf16[32,2176]{1,0:T(8,128)(2,1)S(1)}, bf16[32,2176]{1,0:T(8,128)(2,1)S(1)}, u32[]{:S(2)}, u32[]{:S(2)}) collective-permute-start(bf16[32,2176]{1,0:T(8,128)(2,1)S(1)} %get-tuple-element.54.refs_0_), channel_id=1, source_target_pairs={{0,2},{2,4},{4,6},{6,7},{7,5},{5,3},{3,1},{1,0},{8,10},{10,12},{12... | collective-permute-start | bytes 417800 | tf_op jit(solution)/shard_map/ppermute | solution.py:524
  28.4 2.4 %collective-permute-done.10.refs_15_ = bf16[32,2176]{1,0:T(8,128)(2,1)S(1)} collective-permute-done((bf16[32,2176]{1,0:T(8,128)(2,1)S(1)}, bf16[32,2176]{1,0:T(8,128)(2,1)S(1)}, u32[]{:S(2)}, u32[]{:S(2)}) %collective-permute-start.10) | collective-permute-done | bytes 139296 | tf_op jit(solution)/shard_map/ppermute | solution.py:524
  30.7 2.1 %collective-permute-start.11 = (bf16[32,2176]{1,0:T(8,128)(2,1)S(1)}, bf16[32,2176]{1,0:T(8,128)(2,1)S(1)}, u32[]{:S(2)}, u32[]{:S(2)}) collective-permute-start(bf16[32,2176]{1,0:T(8,128)(2,1)S(1)} %collective-permute-done.10.refs_15_), channel_id=1, source_target_pairs={{0,2},{2,4},{4,6},{6,7},{7,5},{5,3},{3,1},{1,0},{8,10},{10,12},{12... | collective-permute-start | bytes 417800 | tf_op jit(solution)/shard_map/ppermute | solution.py:524
  33.7 2.1 %collective-permute-start.15 = (bf16[32,2176]{1,0:T(8,128)(2,1)S(1)}, bf16[32,2176]{1,0:T(8,128)(2,1)S(1)}, u32[]{:S(2)}, u32[]{:S(2)}) collective-permute-start(bf16[32,2176]{1,0:T(8,128)(2,1)S(1)} %collective-permute-done.14.refs_14_), channel_id=1, source_target_pairs={{0,2},{2,4},{4,6},{6,7},{7,5},{5,3},{3,1},{1,0},{8,10},{10,12},{12... | collective-permute-start | bytes 417800 | tf_op jit(solution)/shard_map/ppermute | solution.py:524
  37.0 2.2 %collective-permute-start.12 = (bf16[32,2176]{1,0:T(8,128)(2,1)S(1)}, bf16[32,2176]{1,0:T(8,128)(2,1)S(1)}, u32[]{:S(2)}, u32[]{:S(2)}) collective-permute-start(bf16[32,2176]{1,0:T(8,128)(2,1)S(1)} %collective-permute-done.11.refs_13_), channel_id=1, source_target_pairs={{0,2},{2,4},{4,6},{6,7},{7,5},{5,3},{3,1},{1,0},{8,10},{10,12},{12... | collective-permute-start | bytes 417800 | tf_op jit(solution)/shard_map/ppermute | solution.py:524
  40.4 2.1 %collective-permute-start.16 = (bf16[32,2176]{1,0:T(8,128)(2,1)S(1)}, bf16[32,2176]{1,0:T(8,128)(2,1)S(1)}, u32[]{:S(2)}, u32[]{:S(2)}) collective-permute-start(bf16[32,2176]{1,0:T(8,128)(2,1)S(1)} %collective-permute-done.15.refs_12_), channel_id=1, source_target_pairs={{0,2},{2,4},{4,6},{6,7},{7,5},{5,3},{3,1},{1,0},{8,10},{10,12},{12... | collective-permute-start | bytes 417800 | tf_op jit(solution)/shard_map/ppermute | solution.py:524
  43.6 1.8 %collective-permute-start.8 = (bf16[32,2176]{1,0:T(8,128)(2,1)S(1)}, bf16[32,2176]{1,0:T(8,128)(2,1)S(1)}, u32[]{:S(2)}, u32[]{:S(2)}) collective-permute-start(bf16[32,2176]{1,0:T(8,128)(2,1)S(1)} %collective-permute-done.6.refs_5_), channel_id=1, source_target_pairs={{0,1},{2,0},{4,2},{6,4},{7,6},{5,7},{3,5},{1,3},{8,9},{10,8},{12,1... | collective-permute-start | bytes 417800 | tf_op jit(solution)/shard_map/ppermute | solution.py:524
  45.8 1.8 %collective-permute-start.9 = (bf16[32,2176]{1,0:T(8,128)(2,1)S(1)}, bf16[32,2176]{1,0:T(8,128)(2,1)S(1)}, u32[]{:S(2)}, u32[]{:S(2)}) collective-permute-start(bf16[32,2176]{1,0:T(8,128)(2,1)S(1)} %collective-permute-done.7.refs_6_), channel_id=1, source_target_pairs={{0,1},{2,0},{4,2},{6,4},{7,6},{5,7},{3,5},{1,3},{8,9},{10,8},{12,1... | collective-permute-start | bytes 417800 | tf_op jit(solution)/shard_map/ppermute | solution.py:524
  47.6 2.4 %collective-permute-done.8.refs_7_ = bf16[32,2176]{1,0:T(8,128)(2,1)S(1)} collective-permute-done((bf16[32,2176]{1,0:T(8,128)(2,1)S(1)}, bf16[32,2176]{1,0:T(8,128)(2,1)S(1)}, u32[]{:S(2)}, u32[]{:S(2)}) %collective-permute-start.8) | collective-permute-done | bytes 139296 | tf_op jit(solution)/shard_map/ppermute | solution.py:524
  51.5 1.5 %collective-permute-start.25 = (bf16[256,2048]{1,0:T(8,128)(2,1)S(1)}, bf16[256,2048]{1,0:T(8,128)(2,1)S(1)}, u32[]{:S(2)}, u32[]{:S(2)}) collective-permute-start(bf16[256,2048]{1,0:T(8,128)(2,1)S(1)} %copy-done.1), channel_id=1, source_target_pairs={{0,16},{8,24},{16,0},{24,8},{1,17},{9,25},{17,1},{25,9},{2,18},{10... | collective-permute-start | bytes 3145736 | tf_op jit(solution)/shard_map/ppermute | solution.py:514
  53.0 2.9 %collective-permute-done.19.refs_22_ = bf16[384,2048]{1,0:T(8,128)(2,1)S(1)} collective-permute-done((bf16[384,2048]{1,0:T(8,128)(2,1)}, bf16[384,2048]{1,0:T(8,128)(2,1)S(1)}, u32[]{:S(2)}, u32[]{:S(2)}) %collective-permute-start.19) | collective-permute-done | bytes 1572896 | tf_op jit(solution)/shard_map/ppermute | solution.py:514
  56.7 3.6 %collective-permute-done.17.refs_18_ = bf16[128,2048]{1,0:T(8,128)(2,1)S(1)} collective-permute-done((bf16[128,2048]{1,0:T(8,128)(2,1)S(1)}, bf16[128,2048]{1,0:T(8,128)(2,1)S(1)}, u32[]{:S(2)}, u32[]{:S(2)}) %collective-permute-start.17) | collective-permute-done | bytes 524320 | tf_op jit(solution)/shard_map/ppermute | solution.py:514
  60.5 8.1 %expert_up.1 = (bf16[512,1024]{1,0:T(8,128)(2,1)S(1)}, f32[512,1]{1,0:T(8,128)S(1)}) custom-call(bf16[32,2176]{1,0:T(8,128)(2,1)S(1)} %get-tuple-element.54.refs_0_, bf16[32,2176]{1,0:T(8,128)(2,1)S(1)} %get-tuple-element.55.refs_1_, bf16[32,2176]{1,0:T(8,128)(2,1)S(1)} %collective-permute-done.3.refs_2_, ...), custom_call_target="tpu_custom_call" | custom-call | flops 1 | bytes 1 | tf_op jit(solution)/shard_map/expert_up/pallas_call | solution.py:406
  68.5 9.0 %collective-permute-done.25.refs_2_ = bf16[256,2048]{1,0:T(8,128)(2,1)S(1)} collective-permute-done((bf16[256,2048]{1,0:T(8,128)(2,1)S(1)}, bf16[256,2048]{1,0:T(8,128)(2,1)S(1)}, u32[]{:S(2)}, u32[]{:S(2)}) %collective-permute-start.25) | collective-permute-done | bytes 1048608 | tf_op jit(solution)/shard_map/ppermute | solution.py:514
  78.2 2.0 %down_part.1.refs_1_ = f32[512,2048]{1,0:T(8,128)S(1)} custom-call(bf16[512,1024]{1,0:T(8,128)(2,1)S(1)} %get-tuple-element.61.hidden_ref.refs_0_, bf16[256,2048]{1,0:T(8,128)(2,1)S(1)} %copy-done.1, bf16[256,2048]{1,0:T(8,128)(2,1)S(1)} %collective-permute-done.24.refs_1_, bf16[256,2048]{1,0:T(8,128)(2,1)S(1)} %collective-permute-done.25.refs_2_), custom_call_target="tpu_custom_call" | custom-call | flops 1 | bytes 1 | tf_op jit(solution)/shard_map/down_part/pallas_call | solution.py:451
  80.8 1.9 %collective-permute-start.36 = (bf16[32,1024]{1,0:T(8,128)(2,1)S(1)}, bf16[32,1024]{1,0:T(8,128)(2,1)S(1)}, u32[]{:S(2)}, u32[]{:S(2)}) collective-permute-start(bf16[32,1024]{1,0:T(8,128)(2,1)S(1)} %get-tuple-element.82), channel_id=1, source_target_pairs={{0,2},{2,4},{4,6},{6,7},{7,5},{5,3},{3,1},{1,0},{8,10},{10,12},{12... | collective-permute-start | bytes 196616 | tf_op jit(solution)/shard_map/ppermute | solution.py:524
  83.4 1.9 %collective-permute-start.27 = (bf16[32,1024]{1,0:T(8,128)(2,1)S(1)}, bf16[32,1024]{1,0:T(8,128)(2,1)S(1)}, u32[]{:S(2)}, u32[]{:S(2)}) collective-permute-start(bf16[32,1024]{1,0:T(8,128)(2,1)S(1)} %get-tuple-element.71), channel_id=1, source_target_pairs={{0,2},{2,4},{4,6},{6,7},{7,5},{5,3},{3,1},{1,0},{8,10},{10,12},{12... | collective-permute-start | bytes 196616 | tf_op jit(solution)/shard_map/ppermute | solution.py:524
  85.5 1.9 %collective-permute-start.37 = (bf16[64,1024]{1,0:T(8,128)(2,1)S(1)}, bf16[64,1024]{1,0:T(8,128)(2,1)S(1)}, u32[]{:S(2)}, u32[]{:S(2)}) collective-permute-start(bf16[64,1024]{1,0:T(8,128)(2,1)S(1)} %pad_maximum_fusion.2), channel_id=1, source_target_pairs={{0,2},{2,4},{4,6},{6,7},{7,5},{5,3},{3,1},{1,0},{8,10},{10,12},{12... | collective-permute-start | bytes 393224 | tf_op jit(solution)/shard_map/ppermute | solution.py:524
  88.2 2.0 %collective-permute-start.28 = (bf16[64,1024]{1,0:T(8,128)(2,1)S(1)}, bf16[64,1024]{1,0:T(8,128)(2,1)S(1)}, u32[]{:S(2)}, u32[]{:S(2)}) collective-permute-start(bf16[64,1024]{1,0:T(8,128)(2,1)S(1)} %pad_maximum_fusion), channel_id=1, source_target_pairs={{0,2},{2,4},{4,6},{6,7},{7,5},{5,3},{3,1},{1,0},{8,10},{10,12},{12... | collective-permute-start | bytes 393224 | tf_op jit(solution)/shard_map/ppermute | solution.py:524
  90.3 1.4 %collective-permute-done.37 = bf16[64,1024]{1,0:T(8,128)(2,1)S(1)} collective-permute-done((bf16[64,1024]{1,0:T(8,128)(2,1)S(1)}, bf16[64,1024]{1,0:T(8,128)(2,1)S(1)}, u32[]{:S(2)}, u32[]{:S(2)}) %collective-permute-start.37) | collective-permute-done | bytes 131104 | tf_op jit(solution)/shard_map/ppermute | solution.py:524
  91.8 2.0 %collective-permute-start.38 = (bf16[64,1024]{1,0:T(8,128)(2,1)S(1)}, bf16[64,1024]{1,0:T(8,128)(2,1)S(1)}, u32[]{:S(2)}, u32[]{:S(2)}) collective-permute-start(bf16[64,1024]{1,0:T(8,128)(2,1)S(1)} %add_convert_fusion.4), channel_id=1, source_target_pairs={{0,2},{2,4},{4,6},{6,7},{7,5},{5,3},{3,1},{1,0},{8,10},{10,12},{12... | collective-permute-start | bytes 393224 | tf_op jit(solution)/shard_map/ppermute | solution.py:524
  94.7 1.9 %collective-permute-start.29 = (bf16[64,1024]{1,0:T(8,128)(2,1)S(1)}, bf16[64,1024]{1,0:T(8,128)(2,1)S(1)}, u32[]{:S(2)}, u32[]{:S(2)}) collective-permute-start(bf16[64,1024]{1,0:T(8,128)(2,1)S(1)} %add_convert_fusion.9), channel_id=1, source_target_pairs={{0,2},{2,4},{4,6},{6,7},{7,5},{5,3},{3,1},{1,0},{8,10},{10,12},{12... | collective-permute-start | bytes 393224 | tf_op jit(solution)/shard_map/ppermute | solution.py:524
  97.6 1.8 %collective-permute-start.39 = (bf16[64,1024]{1,0:T(8,128)(2,1)S(1)}, bf16[64,1024]{1,0:T(8,128)(2,1)S(1)}, u32[]{:S(2)}, u32[]{:S(2)}) collective-permute-start(bf16[64,1024]{1,0:T(8,128)(2,1)S(1)} %add_convert_fusion.3), channel_id=1, source_target_pairs={{0,2},{2,4},{4,6},{6,7},{7,5},{5,3},{3,1},{1,0},{8,10},{10,12},{12... | collective-permute-start | bytes 393224 | tf_op jit(solution)/shard_map/ppermute | solution.py:524
  100.9 2.1 %collective-permute-start.30 = (bf16[64,1024]{1,0:T(8,128)(2,1)S(1)}, bf16[64,1024]{1,0:T(8,128)(2,1)S(1)}, u32[]{:S(2)}, u32[]{:S(2)}) collective-permute-start(bf16[64,1024]{1,0:T(8,128)(2,1)S(1)} %add_convert_fusion.8), channel_id=1, source_target_pairs={{0,2},{2,4},{4,6},{6,7},{7,5},{5,3},{3,1},{1,0},{8,10},{10,12},{12... | collective-permute-start | bytes 393224 | tf_op jit(solution)/shard_map/ppermute | solution.py:524
  103.3 1.6 %collective-permute-done.43 = bf16[64,1024]{1,0:T(8,128)(2,1)S(1)} collective-permute-done((bf16[64,1024]{1,0:T(8,128)(2,1)S(1)}, bf16[64,1024]{1,0:T(8,128)(2,1)S(1)}, u32[]{:S(2)}, u32[]{:S(2)}) %collective-permute-start.43) | collective-permute-done | bytes 131104 | tf_op jit(solution)/shard_map/ppermute | solution.py:524
  106.0 2.2 %collective-permute-done.34 = bf16[64,1024]{1,0:T(8,128)(2,1)S(1)} collective-permute-done((bf16[64,1024]{1,0:T(8,128)(2,1)S(1)}, bf16[64,1024]{1,0:T(8,128)(2,1)S(1)}, u32[]{:S(2)}, u32[]{:S(2)}) %collective-permute-start.34) | collective-permute-done | bytes 131104 | tf_op jit(solution)/shard_map/ppermute | solution.py:524
  (103 shorter events, 16.8 us)
Async XLA Ops:
  3.4 18.8 %collective-permute-start.1 = (bf16[64,5120]{1,0:T(8,128)(2,1)}, bf16[64,5120]{1,0:T(8,128)(2,1)S(1)}, u32[]{:S(2)}, u32[]{:S(2)}) collective-permute-start(bf16[64,5120]{1,0:T(8,128)(2,1)} %get-tuple-element.49), channel_id=1, source_target_pairs={{0,16},{8,24},{16,0},{24,8},{1,17},{9,25},{17,1},{25,9},{2,18},{10... | collective-permute-start | bytes 1966088 | tf_op jit(solution)/shard_map/ppermute | solution.py:514
  10.4 45.4 %collective-permute-start.19 = (bf16[384,2048]{1,0:T(8,128)(2,1)}, bf16[384,2048]{1,0:T(8,128)(2,1)S(1)}, u32[]{:S(2)}, u32[]{:S(2)}) collective-permute-start(bf16[384,2048]{1,0:T(8,128)(2,1)} %get-tuple-element.58.refs_17_), channel_id=1, source_target_pairs={{0,16},{8,24},{16,0},{24,8},{1,17},{9,25},{17,1},{25,9},{2,18},{10... | collective-permute-start | bytes 4718600 | tf_op jit(solution)/shard_map/ppermute | solution.py:514
  10.6 11.6 %collective-permute-start = (bf16[64,512]{1,0:T(8,128)(2,1)S(1)}, bf16[64,512]{1,0:T(8,128)(2,1)S(1)}, u32[]{:S(2)}, u32[]{:S(2)}) collective-permute-start(bf16[64,512]{1,0:T(8,128)(2,1)S(1)} %copy-done.8), channel_id=1, source_target_pairs={{0,8},{8,0},{16,24},{24,16},{1,9},{9,1},{17,25},{25,17},{2,10},{10... | collective-permute-start | bytes 196616 | tf_op jit(solution)/shard_map/ppermute | solution.py:514
  24.1 6.6 %collective-permute-start.10 = (bf16[32,2176]{1,0:T(8,128)(2,1)S(1)}, bf16[32,2176]{1,0:T(8,128)(2,1)S(1)}, u32[]{:S(2)}, u32[]{:S(2)}) collective-permute-start(bf16[32,2176]{1,0:T(8,128)(2,1)S(1)} %get-tuple-element.55.refs_1_), channel_id=1, source_target_pairs={{0,2},{2,4},{4,6},{6,7},{7,5},{5,3},{3,1},{1,0},{8,10},{10,12},{12... | collective-permute-start | bytes 417800 | tf_op jit(solution)/shard_map/ppermute | solution.py:524
  26.3 6.6 %collective-permute-start.3 = (bf16[32,2176]{1,0:T(8,128)(2,1)S(1)}, bf16[32,2176]{1,0:T(8,128)(2,1)S(1)}, u32[]{:S(2)}, u32[]{:S(2)}) collective-permute-start(bf16[32,2176]{1,0:T(8,128)(2,1)S(1)} %get-tuple-element.54.refs_0_), channel_id=1, source_target_pairs={{0,1},{2,0},{4,2},{6,4},{7,6},{5,7},{3,5},{1,3},{8,9},{10,8},{12,1... | collective-permute-start | bytes 417800 | tf_op jit(solution)/shard_map/ppermute | solution.py:524
  26.3 7.4 %collective-permute-start.14 = (bf16[32,2176]{1,0:T(8,128)(2,1)S(1)}, bf16[32,2176]{1,0:T(8,128)(2,1)S(1)}, u32[]{:S(2)}, u32[]{:S(2)}) collective-permute-start(bf16[32,2176]{1,0:T(8,128)(2,1)S(1)} %get-tuple-element.54.refs_0_), channel_id=1, source_target_pairs={{0,2},{2,4},{4,6},{6,7},{7,5},{5,3},{3,1},{1,0},{8,10},{10,12},{12... | collective-permute-start | bytes 417800 | tf_op jit(solution)/shard_map/ppermute | solution.py:524
  28.3 7.5 %collective-permute-start.4 = (bf16[32,2176]{1,0:T(8,128)(2,1)S(1)}, bf16[32,2176]{1,0:T(8,128)(2,1)S(1)}, u32[]{:S(2)}, u32[]{:S(2)}) collective-permute-start(bf16[32,2176]{1,0:T(8,128)(2,1)S(1)} %get-tuple-element.55.refs_1_), channel_id=1, source_target_pairs={{0,1},{2,0},{4,2},{6,4},{7,6},{5,7},{3,5},{1,3},{8,9},{10,8},{12,1... | collective-permute-start | bytes 417800 | tf_op jit(solution)/shard_map/ppermute | solution.py:524
  30.7 6.2 %collective-permute-start.11 = (bf16[32,2176]{1,0:T(8,128)(2,1)S(1)}, bf16[32,2176]{1,0:T(8,128)(2,1)S(1)}, u32[]{:S(2)}, u32[]{:S(2)}) collective-permute-start(bf16[32,2176]{1,0:T(8,128)(2,1)S(1)} %collective-permute-done.10.refs_15_), channel_id=1, source_target_pairs={{0,2},{2,4},{4,6},{6,7},{7,5},{5,3},{3,1},{1,0},{8,10},{10,12},{12... | collective-permute-start | bytes 417800 | tf_op jit(solution)/shard_map/ppermute | solution.py:524
  32.9 6.3 %collective-permute-start.5 = (bf16[32,2176]{1,0:T(8,128)(2,1)S(1)}, bf16[32,2176]{1,0:T(8,128)(2,1)S(1)}, u32[]{:S(2)}, u32[]{:S(2)}) collective-permute-start(bf16[32,2176]{1,0:T(8,128)(2,1)S(1)} %collective-permute-done.3.refs_2_), channel_id=1, source_target_pairs={{0,1},{2,0},{4,2},{6,4},{7,6},{5,7},{3,5},{1,3},{8,9},{10,8},{12,1... | collective-permute-start | bytes 417800 | tf_op jit(solution)/shard_map/ppermute | solution.py:524
  33.7 6.6 %collective-permute-start.15 = (bf16[32,2176]{1,0:T(8,128)(2,1)S(1)}, bf16[32,2176]{1,0:T(8,128)(2,1)S(1)}, u32[]{:S(2)}, u32[]{:S(2)}) collective-permute-start(bf16[32,2176]{1,0:T(8,128)(2,1)S(1)} %collective-permute-done.14.refs_14_), channel_id=1, source_target_pairs={{0,2},{2,4},{4,6},{6,7},{7,5},{5,3},{3,1},{1,0},{8,10},{10,12},{12... | collective-permute-start | bytes 417800 | tf_op jit(solution)/shard_map/ppermute | solution.py:524
  35.8 6.6 %collective-permute-start.6 = (bf16[32,2176]{1,0:T(8,128)(2,1)S(1)}, bf16[32,2176]{1,0:T(8,128)(2,1)S(1)}, u32[]{:S(2)}, u32[]{:S(2)}) collective-permute-start(bf16[32,2176]{1,0:T(8,128)(2,1)S(1)} %collective-permute-done.4.refs_3_), channel_id=1, source_target_pairs={{0,1},{2,0},{4,2},{6,4},{7,6},{5,7},{3,5},{1,3},{8,9},{10,8},{12,1... | collective-permute-start | bytes 417800 | tf_op jit(solution)/shard_map/ppermute | solution.py:524
  37.0 6.7 %collective-permute-start.12 = (bf16[32,2176]{1,0:T(8,128)(2,1)S(1)}, bf16[32,2176]{1,0:T(8,128)(2,1)S(1)}, u32[]{:S(2)}, u32[]{:S(2)}) collective-permute-start(bf16[32,2176]{1,0:T(8,128)(2,1)S(1)} %collective-permute-done.11.refs_13_), channel_id=1, source_target_pairs={{0,2},{2,4},{4,6},{6,7},{7,5},{5,3},{3,1},{1,0},{8,10},{10,12},{12... | collective-permute-start | bytes 417800 | tf_op jit(solution)/shard_map/ppermute | solution.py:524
  39.2 6.2 %collective-permute-start.7 = (bf16[32,2176]{1,0:T(8,128)(2,1)S(1)}, bf16[32,2176]{1,0:T(8,128)(2,1)S(1)}, u32[]{:S(2)}, u32[]{:S(2)}) collective-permute-start(bf16[32,2176]{1,0:T(8,128)(2,1)S(1)} %collective-permute-done.5.refs_4_), channel_id=1, source_target_pairs={{0,1},{2,0},{4,2},{6,4},{7,6},{5,7},{3,5},{1,3},{8,9},{10,8},{12,1... | collective-permute-start | bytes 417800 | tf_op jit(solution)/shard_map/ppermute | solution.py:524
  40.4 5.5 %collective-permute-start.16 = (bf16[32,2176]{1,0:T(8,128)(2,1)S(1)}, bf16[32,2176]{1,0:T(8,128)(2,1)S(1)}, u32[]{:S(2)}, u32[]{:S(2)}) collective-permute-start(bf16[32,2176]{1,0:T(8,128)(2,1)S(1)} %collective-permute-done.15.refs_12_), channel_id=1, source_target_pairs={{0,2},{2,4},{4,6},{6,7},{7,5},{5,3},{3,1},{1,0},{8,10},{10,12},{12... | collective-permute-start | bytes 417800 | tf_op jit(solution)/shard_map/ppermute | solution.py:524
  42.4 18.0 %collective-permute-start.18 = (bf16[384,2048]{1,0:T(8,128)(2,1)}, bf16[384,2048]{1,0:T(8,128)(2,1)S(1)}, u32[]{:S(2)}, u32[]{:S(2)}) collective-permute-start(bf16[384,2048]{1,0:T(8,128)(2,1)} %get-tuple-element.58.refs_17_), channel_id=1, source_target_pairs={{0,8},{8,0},{16,24},{24,16},{1,9},{9,1},{17,25},{25,17},{2,10},{10... | collective-permute-start | bytes 4718600 | tf_op jit(solution)/shard_map/ppermute | solution.py:514
  43.6 6.4 %collective-permute-start.8 = (bf16[32,2176]{1,0:T(8,128)(2,1)S(1)}, bf16[32,2176]{1,0:T(8,128)(2,1)S(1)}, u32[]{:S(2)}, u32[]{:S(2)}) collective-permute-start(bf16[32,2176]{1,0:T(8,128)(2,1)S(1)} %collective-permute-done.6.refs_5_), channel_id=1, source_target_pairs={{0,1},{2,0},{4,2},{6,4},{7,6},{5,7},{3,5},{1,3},{8,9},{10,8},{12,1... | collective-permute-start | bytes 417800 | tf_op jit(solution)/shard_map/ppermute | solution.py:524
  45.8 5.7 %collective-permute-start.9 = (bf16[32,2176]{1,0:T(8,128)(2,1)S(1)}, bf16[32,2176]{1,0:T(8,128)(2,1)S(1)}, u32[]{:S(2)}, u32[]{:S(2)}) collective-permute-start(bf16[32,2176]{1,0:T(8,128)(2,1)S(1)} %collective-permute-done.7.refs_6_), channel_id=1, source_target_pairs={{0,1},{2,0},{4,2},{6,4},{7,6},{5,7},{3,5},{1,3},{8,9},{10,8},{12,1... | collective-permute-start | bytes 417800 | tf_op jit(solution)/shard_map/ppermute | solution.py:524
  50.0 6.1 %collective-permute-start.20 = (bf16[64,2048]{1,0:T(8,128)(2,1)S(1)}, bf16[64,2048]{1,0:T(8,128)(2,1)S(1)}, u32[]{:S(2)}, u32[]{:S(2)}) collective-permute-start(bf16[64,2048]{1,0:T(8,128)(2,1)S(1)} %get-tuple-element.94), channel_id=1, source_target_pairs={{0,8},{8,0},{16,24},{24,16},{1,9},{9,1},{17,25},{25,17},{2,10},{10... | collective-permute-start | bytes 786440 | tf_op jit(solution)/shard_map/ppermute | solution.py:514
  50.5 6.2 %collective-permute-start.21 = (bf16[64,2048]{1,0:T(8,128)(2,1)S(1)}, bf16[64,2048]{1,0:T(8,128)(2,1)S(1)}, u32[]{:S(2)}, u32[]{:S(2)}) collective-permute-start(bf16[64,2048]{1,0:T(8,128)(2,1)S(1)} %get-tuple-element.93), channel_id=1, source_target_pairs={{0,8},{8,0},{16,24},{24,16},{1,9},{9,1},{17,25},{25,17},{2,10},{10... | collective-permute-start | bytes 786440 | tf_op jit(solution)/shard_map/ppermute | solution.py:514
  51.5 26.0 %collective-permute-start.25 = (bf16[256,2048]{1,0:T(8,128)(2,1)S(1)}, bf16[256,2048]{1,0:T(8,128)(2,1)S(1)}, u32[]{:S(2)}, u32[]{:S(2)}) collective-permute-start(bf16[256,2048]{1,0:T(8,128)(2,1)S(1)} %copy-done.1), channel_id=1, source_target_pairs={{0,16},{8,24},{16,0},{24,8},{1,17},{9,25},{17,1},{25,9},{2,18},{10... | collective-permute-start | bytes 3145736 | tf_op jit(solution)/shard_map/ppermute | solution.py:514
  60.3 17.9 %collective-permute-start.24 = (bf16[256,2048]{1,0:T(8,128)(2,1)S(1)}, bf16[256,2048]{1,0:T(8,128)(2,1)S(1)}, u32[]{:S(2)}, u32[]{:S(2)}) collective-permute-start(bf16[256,2048]{1,0:T(8,128)(2,1)S(1)} %copy-done.1), channel_id=1, source_target_pairs={{0,8},{8,0},{16,24},{24,16},{1,9},{9,1},{17,25},{25,17},{2,10},{10... | collective-permute-start | bytes 3145736 | tf_op jit(solution)/shard_map/ppermute | solution.py:514
  77.7 5.2 %collective-permute-start.26 = (bf16[256,1024]{1,0:T(8,128)(2,1)S(1)}, bf16[256,1024]{1,0:T(8,128)(2,1)S(1)}, u32[]{:S(2)}, u32[]{:S(2)}) collective-permute-start(bf16[256,1024]{1,0:T(8,128)(2,1)S(1)} %get-tuple-element.91), channel_id=1, source_target_pairs={{0,8},{8,0},{16,24},{24,16},{1,9},{9,1},{17,25},{25,17},{2,10},{10... | collective-permute-start | bytes 1572872 | tf_op jit(solution)/shard_map/ppermute | solution.py:514
  85.5 6.2 %collective-permute-start.37 = (bf16[64,1024]{1,0:T(8,128)(2,1)S(1)}, bf16[64,1024]{1,0:T(8,128)(2,1)S(1)}, u32[]{:S(2)}, u32[]{:S(2)}) collective-permute-start(bf16[64,1024]{1,0:T(8,128)(2,1)S(1)} %pad_maximum_fusion.2), channel_id=1, source_target_pairs={{0,2},{2,4},{4,6},{6,7},{7,5},{5,3},{3,1},{1,0},{8,10},{10,12},{12... | collective-permute-start | bytes 393224 | tf_op jit(solution)/shard_map/ppermute | solution.py:524
  87.4 6.4 %collective-permute-start.41 = (bf16[64,1024]{1,0:T(8,128)(2,1)S(1)}, bf16[64,1024]{1,0:T(8,128)(2,1)S(1)}, u32[]{:S(2)}, u32[]{:S(2)}) collective-permute-start(bf16[64,1024]{1,0:T(8,128)(2,1)S(1)} %pad_maximum_fusion.3), channel_id=1, source_target_pairs={{0,1},{2,0},{4,2},{6,4},{7,6},{5,7},{3,5},{1,3},{8,9},{10,8},{12,1... | collective-permute-start | bytes 393224 | tf_op jit(solution)/shard_map/ppermute | solution.py:524
  88.2 6.5 %collective-permute-start.28 = (bf16[64,1024]{1,0:T(8,128)(2,1)S(1)}, bf16[64,1024]{1,0:T(8,128)(2,1)S(1)}, u32[]{:S(2)}, u32[]{:S(2)}) collective-permute-start(bf16[64,1024]{1,0:T(8,128)(2,1)S(1)} %pad_maximum_fusion), channel_id=1, source_target_pairs={{0,2},{2,4},{4,6},{6,7},{7,5},{5,3},{3,1},{1,0},{8,10},{10,12},{12... | collective-permute-start | bytes 393224 | tf_op jit(solution)/shard_map/ppermute | solution.py:524
  90.2 6.4 %collective-permute-start.32 = (bf16[64,1024]{1,0:T(8,128)(2,1)S(1)}, bf16[64,1024]{1,0:T(8,128)(2,1)S(1)}, u32[]{:S(2)}, u32[]{:S(2)}) collective-permute-start(bf16[64,1024]{1,0:T(8,128)(2,1)S(1)} %pad_maximum_fusion.1), channel_id=1, source_target_pairs={{0,1},{2,0},{4,2},{6,4},{7,6},{5,7},{3,5},{1,3},{8,9},{10,8},{12,1... | collective-permute-start | bytes 393224 | tf_op jit(solution)/shard_map/ppermute | solution.py:524
  91.8 5.8 %collective-permute-start.38 = (bf16[64,1024]{1,0:T(8,128)(2,1)S(1)}, bf16[64,1024]{1,0:T(8,128)(2,1)S(1)}, u32[]{:S(2)}, u32[]{:S(2)}) collective-permute-start(bf16[64,1024]{1,0:T(8,128)(2,1)S(1)} %add_convert_fusion.4), channel_id=1, source_target_pairs={{0,2},{2,4},{4,6},{6,7},{7,5},{5,3},{3,1},{1,0},{8,10},{10,12},{12... | collective-permute-start | bytes 393224 | tf_op jit(solution)/shard_map/ppermute | solution.py:524
  93.8 5.6 %collective-permute-start.42 = (bf16[64,1024]{1,0:T(8,128)(2,1)S(1)}, bf16[64,1024]{1,0:T(8,128)(2,1)S(1)}, u32[]{:S(2)}, u32[]{:S(2)}) collective-permute-start(bf16[64,1024]{1,0:T(8,128)(2,1)S(1)} %add_convert_fusion.2), channel_id=1, source_target_pairs={{0,1},{2,0},{4,2},{6,4},{7,6},{5,7},{3,5},{1,3},{8,9},{10,8},{12,1... | collective-permute-start | bytes 393224 | tf_op jit(solution)/shard_map/ppermute | solution.py:524
  94.7 6.2 %collective-permute-start.29 = (bf16[64,1024]{1,0:T(8,128)(2,1)S(1)}, bf16[64,1024]{1,0:T(8,128)(2,1)S(1)}, u32[]{:S(2)}, u32[]{:S(2)}) collective-permute-start(bf16[64,1024]{1,0:T(8,128)(2,1)S(1)} %add_convert_fusion.9), channel_id=1, source_target_pairs={{0,2},{2,4},{4,6},{6,7},{7,5},{5,3},{3,1},{1,0},{8,10},{10,12},{12... | collective-permute-start | bytes 393224 | tf_op jit(solution)/shard_map/ppermute | solution.py:524
  96.7 6.5 %collective-permute-start.33 = (bf16[64,1024]{1,0:T(8,128)(2,1)S(1)}, bf16[64,1024]{1,0:T(8,128)(2,1)S(1)}, u32[]{:S(2)}, u32[]{:S(2)}) collective-permute-start(bf16[64,1024]{1,0:T(8,128)(2,1)S(1)} %add_convert_fusion.7), channel_id=1, source_target_pairs={{0,1},{2,0},{4,2},{6,4},{7,6},{5,7},{3,5},{1,3},{8,9},{10,8},{12,1... | collective-permute-start | bytes 393224 | tf_op jit(solution)/shard_map/ppermute | solution.py:524
  97.6 5.6 %collective-permute-start.39 = (bf16[64,1024]{1,0:T(8,128)(2,1)S(1)}, bf16[64,1024]{1,0:T(8,128)(2,1)S(1)}, u32[]{:S(2)}, u32[]{:S(2)}) collective-permute-start(bf16[64,1024]{1,0:T(8,128)(2,1)S(1)} %add_convert_fusion.3), channel_id=1, source_target_pairs={{0,2},{2,4},{4,6},{6,7},{7,5},{5,3},{3,1},{1,0},{8,10},{10,12},{12... | collective-permute-start | bytes 393224 | tf_op jit(solution)/shard_map/ppermute | solution.py:524
  99.5 5.4 %collective-permute-start.43 = (bf16[64,1024]{1,0:T(8,128)(2,1)S(1)}, bf16[64,1024]{1,0:T(8,128)(2,1)S(1)}, u32[]{:S(2)}, u32[]{:S(2)}) collective-permute-start(bf16[64,1024]{1,0:T(8,128)(2,1)S(1)} %add_convert_fusion.1), channel_id=1, source_target_pairs={{0,1},{2,0},{4,2},{6,4},{7,6},{5,7},{3,5},{1,3},{8,9},{10,8},{12,1... | collective-permute-start | bytes 393224 | tf_op jit(solution)/shard_map/ppermute | solution.py:524
  (21 other events, 197.0 us)

commit v14 on v13

--- a/solution.py
+++ b/solution.py
@@ -149,10 +149,10 @@
         copy.wait()
     tokens, width = q_ref.shape
     pages = k_ref.shape[0]
-    row = lax.broadcasted_iota(jnp.int32, (tokens, tokens), 0)
-    column = lax.broadcasted_iota(jnp.int32, (tokens, tokens), 1)
-    row_request = jnp.zeros((tokens, tokens), jnp.int32)
-    column_request = jnp.zeros((tokens, tokens), jnp.int32)
+    row = lax.broadcasted_iota(jnp.int32, (tokens, 1), 0)
+    column = lax.broadcasted_iota(jnp.int32, (1, tokens), 1)
+    row_request = jnp.zeros((tokens, 1), jnp.int32)
+    column_request = jnp.zeros((1, tokens), jnp.int32)
     end = jnp.int32(0)
     for r in range(lengths.shape[1]):
         end = end + lengths[0, r]
@@ -168,8 +168,9 @@
         ) * (1.0 / math.sqrt(HDIM))
         scores = jnp.where(same, scores, -1e30)
         highest = jnp.max(scores, axis=-1, keepdims=True)
-        weight = jnp.where(same, jnp.exp(scores - highest), 0.0)
-        probs = (weight / jnp.sum(weight, axis=-1, keepdims=True)).astype(jnp.bfloat16)
+        weight = jnp.exp(scores - highest)
+        share = 1.0 / jnp.sum(weight, axis=-1, keepdims=True)
+        probs = (weight * share).astype(jnp.bfloat16)
         attn[:, lanes] = jnp.dot(probs, values, preferred_element_type=jnp.float32).astype(
             jnp.bfloat16
         )

time: 109 us -> 109 us (level)
  no operation moved by 1% of the time
where the time goes in v14:
time: 109 us
  waiting for transfers between devices  48.2 us (44%)
  starting transfers between devices  39.8 us (37%)
  Pallas kernels  19.1 us (18%)
  other arithmetic  1.28 us (1%)
    ppermute x30, starting transfers between devices, around(): lax.ppermute(x, 'expert', [(ring[i], ring[(i + step) % count]) for i in r...  33.8 us
    ppermute x14, waiting for transfers between devices, partner(): return lax.ppermute(x, 'dp', [(i, i ^ distance) for i in range(4)])  28.3 us
    ppermute x30, waiting for transfers between devices, around(): lax.ppermute(x, 'expert', [(ring[i], ring[(i + step) % count]) for i in r...  20 us
    pallas_call x1, Pallas kernels, expert_up(): pl.pallas_call(lambda *refs: up_kernel(len(rows), starts, *refs), out_sha...  8.07 us
    ppermute x14, starting transfers between devices, partner(): return lax.ppermute(x, 'dp', [(i, i ^ distance) for i in range(4)])  6.07 us
    pallas_call x1, Pallas kernels, cast_rows(): pl.pallas_call(lambda *refs: cast_kernel(spans, *refs), out_shape=[jax.Sh...  3.98 us
    pallas_call x1, Pallas kernels, attention(): pl.pallas_call(attention_kernel, out_shape=[jax.ShapeDtypeStruct(shape, j...  3.39 us
  transfers between devices with their start and end apart: 44, of which 22 were waited for; matrix products, arithmetic and copies ran while one was open for 1% of the time, Pallas kernels for 14%

profile of v14, /device:TPU:0, one launch (start us, length us, event | category | flops | bytes accessed | tf_op | source)
XLA Modules:
  0.0 109.1 jit_solution(3568426893813768597)
XLA Ops:
  0.0 3.4 %attention.1 = (bf16[64,512]{1,0:T(8,128)(2,1)}, bf16[64,512]{1,0:T(8,128)(2,1)}, bf16[64,5120]{1,0:T(8,128)(2,1)}, bf16[128,2048]{1,0:T(8,128)(2,1)}) custom-call(s32[1,2]{1,0:T(1,128)} %refs_0_.1, s32[1,4]{1,0:T(1,128)} %refs_1_.2, bf16[1,256,512]{2,1,0:T(8,128)(2,1)} %refs_2_.1, bf16[2,128,512]{2,1,0:T(8,128)(2,1)} %refs_3_.1, ...), custom_call_target="tpu_custom_call" | custom-call | tf_op jit(solution)/shard_map/attention/pallas_call | solution.py:202
  3.4 3.0 %collective-permute-start.1 = (bf16[64,5120]{1,0:T(8,128)(2,1)}, bf16[64,5120]{1,0:T(8,128)(2,1)S(1)}, u32[]{:S(2)}, u32[]{:S(2)}) collective-permute-start(bf16[64,5120]{1,0:T(8,128)(2,1)} %get-tuple-element.49), channel_id=1, source_target_pairs={{0,16},{8,24},{16,0},{24,8},{1,17},{9,25},{17,1},{25,9},{2,18},{10... | collective-permute-start | bytes 1966088 | tf_op jit(solution)/shard_map/ppermute | solution.py:515
  6.4 4.0 %cast_rows.1 = (bf16[384,2048]{1,0:T(8,128)(2,1)}, bf16[256,2048]{1,0:T(8,128)(2,1)}) custom-call(f32[1,512,2048]{2,1,0:T(8,128)} %refs_0_.2, f32[1,256,2048]{2,1,0:T(8,128)} %refs_1_.3), custom_call_target="tpu_custom_call" | custom-call | tf_op jit(solution)/shard_map/cast_rows/pallas_call | solution.py:328
  10.6 11.6 %collective-permute-done.1.refs_2_.refs_20_.refs_21_ = bf16[64,5120]{1,0:T(8,128)(2,1)S(1)} collective-permute-done((bf16[64,5120]{1,0:T(8,128)(2,1)}, bf16[64,5120]{1,0:T(8,128)(2,1)S(1)}, u32[]{:S(2)}, u32[]{:S(2)}) %collective-permute-start.1) | collective-permute-done | bytes 655392 | tf_op jit(solution)/shard_map/ppermute | solution.py:515
  22.2 1.2 %collective-permute-done.2.refs_3_ = bf16[64,512]{1,0:T(8,128)(2,1)S(1)} collective-permute-done((bf16[64,512]{1,0:T(8,128)(2,1)S(1)}, bf16[64,512]{1,0:T(8,128)(2,1)S(1)}, u32[]{:S(2)}, u32[]{:S(2)}) %collective-permute-start.2) | collective-permute-done | bytes 65568 | tf_op jit(solution)/shard_map/ppermute | solution.py:515
  24.1 2.2 %collective-permute-start.10 = (bf16[32,2176]{1,0:T(8,128)(2,1)S(1)}, bf16[32,2176]{1,0:T(8,128)(2,1)S(1)}, u32[]{:S(2)}, u32[]{:S(2)}) collective-permute-start(bf16[32,2176]{1,0:T(8,128)(2,1)S(1)} %get-tuple-element.55.refs_1_), channel_id=1, source_target_pairs={{0,2},{2,4},{4,6},{6,7},{7,5},{5,3},{3,1},{1,0},{8,10},{10,12},{12... | collective-permute-start | bytes 417800 | tf_op jit(solution)/shard_map/ppermute | solution.py:525
  26.3 2.0 %collective-permute-start.14 = (bf16[32,2176]{1,0:T(8,128)(2,1)S(1)}, bf16[32,2176]{1,0:T(8,128)(2,1)S(1)}, u32[]{:S(2)}, u32[]{:S(2)}) collective-permute-start(bf16[32,2176]{1,0:T(8,128)(2,1)S(1)} %get-tuple-element.54.refs_0_), channel_id=1, source_target_pairs={{0,2},{2,4},{4,6},{6,7},{7,5},{5,3},{3,1},{1,0},{8,10},{10,12},{12... | collective-permute-start | bytes 417800 | tf_op jit(solution)/shard_map/ppermute | solution.py:525
  28.3 2.4 %collective-permute-done.10.refs_15_ = bf16[32,2176]{1,0:T(8,128)(2,1)S(1)} collective-permute-done((bf16[32,2176]{1,0:T(8,128)(2,1)S(1)}, bf16[32,2176]{1,0:T(8,128)(2,1)S(1)}, u32[]{:S(2)}, u32[]{:S(2)}) %collective-permute-start.10) | collective-permute-done | bytes 139296 | tf_op jit(solution)/shard_map/ppermute | solution.py:525
  30.7 2.1 %collective-permute-start.11 = (bf16[32,2176]{1,0:T(8,128)(2,1)S(1)}, bf16[32,2176]{1,0:T(8,128)(2,1)S(1)}, u32[]{:S(2)}, u32[]{:S(2)}) collective-permute-start(bf16[32,2176]{1,0:T(8,128)(2,1)S(1)} %collective-permute-done.10.refs_15_), channel_id=1, source_target_pairs={{0,2},{2,4},{4,6},{6,7},{7,5},{5,3},{3,1},{1,0},{8,10},{10,12},{12... | collective-permute-start | bytes 417800 | tf_op jit(solution)/shard_map/ppermute | solution.py:525
  33.7 2.1 %collective-permute-start.15 = (bf16[32,2176]{1,0:T(8,128)(2,1)S(1)}, bf16[32,2176]{1,0:T(8,128)(2,1)S(1)}, u32[]{:S(2)}, u32[]{:S(2)}) collective-permute-start(bf16[32,2176]{1,0:T(8,128)(2,1)S(1)} %collective-permute-done.14.refs_14_), channel_id=1, source_target_pairs={{0,2},{2,4},{4,6},{6,7},{7,5},{5,3},{3,1},{1,0},{8,10},{10,12},{12... | collective-permute-start | bytes 417800 | tf_op jit(solution)/shard_map/ppermute | solution.py:525
  36.9 2.2 %collective-permute-start.12 = (bf16[32,2176]{1,0:T(8,128)(2,1)S(1)}, bf16[32,2176]{1,0:T(8,128)(2,1)S(1)}, u32[]{:S(2)}, u32[]{:S(2)}) collective-permute-start(bf16[32,2176]{1,0:T(8,128)(2,1)S(1)} %collective-permute-done.11.refs_13_), channel_id=1, source_target_pairs={{0,2},{2,4},{4,6},{6,7},{7,5},{5,3},{3,1},{1,0},{8,10},{10,12},{12... | collective-permute-start | bytes 417800 | tf_op jit(solution)/shard_map/ppermute | solution.py:525
  40.3 2.1 %collective-permute-start.16 = (bf16[32,2176]{1,0:T(8,128)(2,1)S(1)}, bf16[32,2176]{1,0:T(8,128)(2,1)S(1)}, u32[]{:S(2)}, u32[]{:S(2)}) collective-permute-start(bf16[32,2176]{1,0:T(8,128)(2,1)S(1)} %collective-permute-done.15.refs_12_), channel_id=1, source_target_pairs={{0,2},{2,4},{4,6},{6,7},{7,5},{5,3},{3,1},{1,0},{8,10},{10,12},{12... | collective-permute-start | bytes 417800 | tf_op jit(solution)/shard_map/ppermute | solution.py:525
  43.6 1.8 %collective-permute-start.8 = (bf16[32,2176]{1,0:T(8,128)(2,1)S(1)}, bf16[32,2176]{1,0:T(8,128)(2,1)S(1)}, u32[]{:S(2)}, u32[]{:S(2)}) collective-permute-start(bf16[32,2176]{1,0:T(8,128)(2,1)S(1)} %collective-permute-done.6.refs_5_), channel_id=1, source_target_pairs={{0,1},{2,0},{4,2},{6,4},{7,6},{5,7},{3,5},{1,3},{8,9},{10,8},{12,1... | collective-permute-start | bytes 417800 | tf_op jit(solution)/shard_map/ppermute | solution.py:525
  45.8 1.8 %collective-permute-start.9 = (bf16[32,2176]{1,0:T(8,128)(2,1)S(1)}, bf16[32,2176]{1,0:T(8,128)(2,1)S(1)}, u32[]{:S(2)}, u32[]{:S(2)}) collective-permute-start(bf16[32,2176]{1,0:T(8,128)(2,1)S(1)} %collective-permute-done.7.refs_6_), channel_id=1, source_target_pairs={{0,1},{2,0},{4,2},{6,4},{7,6},{5,7},{3,5},{1,3},{8,9},{10,8},{12,1... | collective-permute-start | bytes 417800 | tf_op jit(solution)/shard_map/ppermute | solution.py:525
  47.6 2.4 %collective-permute-done.8.refs_7_ = bf16[32,2176]{1,0:T(8,128)(2,1)S(1)} collective-permute-done((bf16[32,2176]{1,0:T(8,128)(2,1)S(1)}, bf16[32,2176]{1,0:T(8,128)(2,1)S(1)}, u32[]{:S(2)}, u32[]{:S(2)}) %collective-permute-start.8) | collective-permute-done | bytes 139296 | tf_op jit(solution)/shard_map/ppermute | solution.py:525
  51.5 1.5 %collective-permute-start.25 = (bf16[256,2048]{1,0:T(8,128)(2,1)S(1)}, bf16[256,2048]{1,0:T(8,128)(2,1)S(1)}, u32[]{:S(2)}, u32[]{:S(2)}) collective-permute-start(bf16[256,2048]{1,0:T(8,128)(2,1)S(1)} %copy-done.1), channel_id=1, source_target_pairs={{0,16},{8,24},{16,0},{24,8},{1,17},{9,25},{17,1},{25,9},{2,18},{10... | collective-permute-start | bytes 3145736 | tf_op jit(solution)/shard_map/ppermute | solution.py:515
  53.0 2.9 %collective-permute-done.19.refs_22_ = bf16[384,2048]{1,0:T(8,128)(2,1)S(1)} collective-permute-done((bf16[384,2048]{1,0:T(8,128)(2,1)}, bf16[384,2048]{1,0:T(8,128)(2,1)S(1)}, u32[]{:S(2)}, u32[]{:S(2)}) %collective-permute-start.19) | collective-permute-done | bytes 1572896 | tf_op jit(solution)/shard_map/ppermute | solution.py:515
  56.7 3.6 %collective-permute-done.17.refs_18_ = bf16[128,2048]{1,0:T(8,128)(2,1)S(1)} collective-permute-done((bf16[128,2048]{1,0:T(8,128)(2,1)S(1)}, bf16[128,2048]{1,0:T(8,128)(2,1)S(1)}, u32[]{:S(2)}, u32[]{:S(2)}) %collective-permute-start.17) | collective-permute-done | bytes 524320 | tf_op jit(solution)/shard_map/ppermute | solution.py:515
  60.4 8.1 %expert_up.1 = (bf16[512,1024]{1,0:T(8,128)(2,1)S(1)}, f32[512,1]{1,0:T(8,128)S(1)}) custom-call(bf16[32,2176]{1,0:T(8,128)(2,1)S(1)} %get-tuple-element.54.refs_0_, bf16[32,2176]{1,0:T(8,128)(2,1)S(1)} %get-tuple-element.55.refs_1_, bf16[32,2176]{1,0:T(8,128)(2,1)S(1)} %collective-permute-done.3.refs_2_, ...), custom_call_target="tpu_custom_call" | custom-call | flops 1 | bytes 1 | tf_op jit(solution)/shard_map/expert_up/pallas_call | solution.py:407
  68.5 9.0 %collective-permute-done.25.refs_2_ = bf16[256,2048]{1,0:T(8,128)(2,1)S(1)} collective-permute-done((bf16[256,2048]{1,0:T(8,128)(2,1)S(1)}, bf16[256,2048]{1,0:T(8,128)(2,1)S(1)}, u32[]{:S(2)}, u32[]{:S(2)}) %collective-permute-start.25) | collective-permute-done | bytes 1048608 | tf_op jit(solution)/shard_map/ppermute | solution.py:515
  78.2 2.0 %down_part.1.refs_1_ = f32[512,2048]{1,0:T(8,128)S(1)} custom-call(bf16[512,1024]{1,0:T(8,128)(2,1)S(1)} %get-tuple-element.61.hidden_ref.refs_0_, bf16[256,2048]{1,0:T(8,128)(2,1)S(1)} %copy-done.1, bf16[256,2048]{1,0:T(8,128)(2,1)S(1)} %collective-permute-done.24.refs_1_, bf16[256,2048]{1,0:T(8,128)(2,1)S(1)} %collective-permute-done.25.refs_2_), custom_call_target="tpu_custom_call" | custom-call | flops 1 | bytes 1 | tf_op jit(solution)/shard_map/down_part/pallas_call | solution.py:452
  80.8 1.9 %collective-permute-start.36 = (bf16[32,1024]{1,0:T(8,128)(2,1)S(1)}, bf16[32,1024]{1,0:T(8,128)(2,1)S(1)}, u32[]{:S(2)}, u32[]{:S(2)}) collective-permute-start(bf16[32,1024]{1,0:T(8,128)(2,1)S(1)} %get-tuple-element.82), channel_id=1, source_target_pairs={{0,2},{2,4},{4,6},{6,7},{7,5},{5,3},{3,1},{1,0},{8,10},{10,12},{12... | collective-permute-start | bytes 196616 | tf_op jit(solution)/shard_map/ppermute | solution.py:525
  83.4 1.9 %collective-permute-start.27 = (bf16[32,1024]{1,0:T(8,128)(2,1)S(1)}, bf16[32,1024]{1,0:T(8,128)(2,1)S(1)}, u32[]{:S(2)}, u32[]{:S(2)}) collective-permute-start(bf16[32,1024]{1,0:T(8,128)(2,1)S(1)} %get-tuple-element.71), channel_id=1, source_target_pairs={{0,2},{2,4},{4,6},{6,7},{7,5},{5,3},{3,1},{1,0},{8,10},{10,12},{12... | collective-permute-start | bytes 196616 | tf_op jit(solution)/shard_map/ppermute | solution.py:525
  85.5 1.9 %collective-permute-start.37 = (bf16[64,1024]{1,0:T(8,128)(2,1)S(1)}, bf16[64,1024]{1,0:T(8,128)(2,1)S(1)}, u32[]{:S(2)}, u32[]{:S(2)}) collective-permute-start(bf16[64,1024]{1,0:T(8,128)(2,1)S(1)} %pad_maximum_fusion.2), channel_id=1, source_target_pairs={{0,2},{2,4},{4,6},{6,7},{7,5},{5,3},{3,1},{1,0},{8,10},{10,12},{12... | collective-permute-start | bytes 393224 | tf_op jit(solution)/shard_map/ppermute | solution.py:525
  88.1 2.0 %collective-permute-start.28 = (bf16[64,1024]{1,0:T(8,128)(2,1)S(1)}, bf16[64,1024]{1,0:T(8,128)(2,1)S(1)}, u32[]{:S(2)}, u32[]{:S(2)}) collective-permute-start(bf16[64,1024]{1,0:T(8,128)(2,1)S(1)} %pad_maximum_fusion), channel_id=1, source_target_pairs={{0,2},{2,4},{4,6},{6,7},{7,5},{5,3},{3,1},{1,0},{8,10},{10,12},{12... | collective-permute-start | bytes 393224 | tf_op jit(solution)/shard_map/ppermute | solution.py:525
  90.3 1.4 %collective-permute-done.37 = bf16[64,1024]{1,0:T(8,128)(2,1)S(1)} collective-permute-done((bf16[64,1024]{1,0:T(8,128)(2,1)S(1)}, bf16[64,1024]{1,0:T(8,128)(2,1)S(1)}, u32[]{:S(2)}, u32[]{:S(2)}) %collective-permute-start.37) | collective-permute-done | bytes 131104 | tf_op jit(solution)/shard_map/ppermute | solution.py:525
  91.8 2.0 %collective-permute-start.38 = (bf16[64,1024]{1,0:T(8,128)(2,1)S(1)}, bf16[64,1024]{1,0:T(8,128)(2,1)S(1)}, u32[]{:S(2)}, u32[]{:S(2)}) collective-permute-start(bf16[64,1024]{1,0:T(8,128)(2,1)S(1)} %add_convert_fusion.4), channel_id=1, source_target_pairs={{0,2},{2,4},{4,6},{6,7},{7,5},{5,3},{3,1},{1,0},{8,10},{10,12},{12... | collective-permute-start | bytes 393224 | tf_op jit(solution)/shard_map/ppermute | solution.py:525
  94.7 2.0 %collective-permute-start.29 = (bf16[64,1024]{1,0:T(8,128)(2,1)S(1)}, bf16[64,1024]{1,0:T(8,128)(2,1)S(1)}, u32[]{:S(2)}, u32[]{:S(2)}) collective-permute-start(bf16[64,1024]{1,0:T(8,128)(2,1)S(1)} %add_convert_fusion.9), channel_id=1, source_target_pairs={{0,2},{2,4},{4,6},{6,7},{7,5},{5,3},{3,1},{1,0},{8,10},{10,12},{12... | collective-permute-start | bytes 393224 | tf_op jit(solution)/shard_map/ppermute | solution.py:525
  97.6 1.8 %collective-permute-start.39 = (bf16[64,1024]{1,0:T(8,128)(2,1)S(1)}, bf16[64,1024]{1,0:T(8,128)(2,1)S(1)}, u32[]{:S(2)}, u32[]{:S(2)}) collective-permute-start(bf16[64,1024]{1,0:T(8,128)(2,1)S(1)} %add_convert_fusion.3), channel_id=1, source_target_pairs={{0,2},{2,4},{4,6},{6,7},{7,5},{5,3},{3,1},{1,0},{8,10},{10,12},{12... | collective-permute-start | bytes 393224 | tf_op jit(solution)/shard_map/ppermute | solution.py:525
  100.9 2.1 %collective-permute-start.30 = (bf16[64,1024]{1,0:T(8,128)(2,1)S(1)}, bf16[64,1024]{1,0:T(8,128)(2,1)S(1)}, u32[]{:S(2)}, u32[]{:S(2)}) collective-permute-start(bf16[64,1024]{1,0:T(8,128)(2,1)S(1)} %add_convert_fusion.8), channel_id=1, source_target_pairs={{0,2},{2,4},{4,6},{6,7},{7,5},{5,3},{3,1},{1,0},{8,10},{10,12},{12... | collective-permute-start | bytes 393224 | tf_op jit(solution)/shard_map/ppermute | solution.py:525
  103.3 1.6 %collective-permute-done.43 = bf16[64,1024]{1,0:T(8,128)(2,1)S(1)} collective-permute-done((bf16[64,1024]{1,0:T(8,128)(2,1)S(1)}, bf16[64,1024]{1,0:T(8,128)(2,1)S(1)}, u32[]{:S(2)}, u32[]{:S(2)}) %collective-permute-start.43) | collective-permute-done | bytes 131104 | tf_op jit(solution)/shard_map/ppermute | solution.py:525
  106.0 2.2 %collective-permute-done.34 = bf16[64,1024]{1,0:T(8,128)(2,1)S(1)} collective-permute-done((bf16[64,1024]{1,0:T(8,128)(2,1)S(1)}, bf16[64,1024]{1,0:T(8,128)(2,1)S(1)}, u32[]{:S(2)}, u32[]{:S(2)}) %collective-permute-start.34) | collective-permute-done | bytes 131104 | tf_op jit(solution)/shard_map/ppermute | solution.py:525
  (103 shorter events, 16.8 us)
Async XLA Ops:
  3.4 18.8 %collective-permute-start.1 = (bf16[64,5120]{1,0:T(8,128)(2,1)}, bf16[64,5120]{1,0:T(8,128)(2,1)S(1)}, u32[]{:S(2)}, u32[]{:S(2)}) collective-permute-start(bf16[64,5120]{1,0:T(8,128)(2,1)} %get-tuple-element.49), channel_id=1, source_target_pairs={{0,16},{8,24},{16,0},{24,8},{1,17},{9,25},{17,1},{25,9},{2,18},{10... | collective-permute-start | bytes 1966088 | tf_op jit(solution)/shard_map/ppermute | solution.py:515
  10.4 45.4 %collective-permute-start.19 = (bf16[384,2048]{1,0:T(8,128)(2,1)}, bf16[384,2048]{1,0:T(8,128)(2,1)S(1)}, u32[]{:S(2)}, u32[]{:S(2)}) collective-permute-start(bf16[384,2048]{1,0:T(8,128)(2,1)} %get-tuple-element.58.refs_17_), channel_id=1, source_target_pairs={{0,16},{8,24},{16,0},{24,8},{1,17},{9,25},{17,1},{25,9},{2,18},{10... | collective-permute-start | bytes 4718600 | tf_op jit(solution)/shard_map/ppermute | solution.py:515
  10.6 11.6 %collective-permute-start = (bf16[64,512]{1,0:T(8,128)(2,1)S(1)}, bf16[64,512]{1,0:T(8,128)(2,1)S(1)}, u32[]{:S(2)}, u32[]{:S(2)}) collective-permute-start(bf16[64,512]{1,0:T(8,128)(2,1)S(1)} %copy-done.8), channel_id=1, source_target_pairs={{0,8},{8,0},{16,24},{24,16},{1,9},{9,1},{17,25},{25,17},{2,10},{10... | collective-permute-start | bytes 196616 | tf_op jit(solution)/shard_map/ppermute | solution.py:515
  24.1 6.6 %collective-permute-start.10 = (bf16[32,2176]{1,0:T(8,128)(2,1)S(1)}, bf16[32,2176]{1,0:T(8,128)(2,1)S(1)}, u32[]{:S(2)}, u32[]{:S(2)}) collective-permute-start(bf16[32,2176]{1,0:T(8,128)(2,1)S(1)} %get-tuple-element.55.refs_1_), channel_id=1, source_target_pairs={{0,2},{2,4},{4,6},{6,7},{7,5},{5,3},{3,1},{1,0},{8,10},{10,12},{12... | collective-permute-start | bytes 417800 | tf_op jit(solution)/shard_map/ppermute | solution.py:525
  26.3 6.6 %collective-permute-start.3 = (bf16[32,2176]{1,0:T(8,128)(2,1)S(1)}, bf16[32,2176]{1,0:T(8,128)(2,1)S(1)}, u32[]{:S(2)}, u32[]{:S(2)}) collective-permute-start(bf16[32,2176]{1,0:T(8,128)(2,1)S(1)} %get-tuple-element.54.refs_0_), channel_id=1, source_target_pairs={{0,1},{2,0},{4,2},{6,4},{7,6},{5,7},{3,5},{1,3},{8,9},{10,8},{12,1... | collective-permute-start | bytes 417800 | tf_op jit(solution)/shard_map/ppermute | solution.py:525
  26.3 7.4 %collective-permute-start.14 = (bf16[32,2176]{1,0:T(8,128)(2,1)S(1)}, bf16[32,2176]{1,0:T(8,128)(2,1)S(1)}, u32[]{:S(2)}, u32[]{:S(2)}) collective-permute-start(bf16[32,2176]{1,0:T(8,128)(2,1)S(1)} %get-tuple-element.54.refs_0_), channel_id=1, source_target_pairs={{0,2},{2,4},{4,6},{6,7},{7,5},{5,3},{3,1},{1,0},{8,10},{10,12},{12... | collective-permute-start | bytes 417800 | tf_op jit(solution)/shard_map/ppermute | solution.py:525
  28.3 7.5 %collective-permute-start.4 = (bf16[32,2176]{1,0:T(8,128)(2,1)S(1)}, bf16[32,2176]{1,0:T(8,128)(2,1)S(1)}, u32[]{:S(2)}, u32[]{:S(2)}) collective-permute-start(bf16[32,2176]{1,0:T(8,128)(2,1)S(1)} %get-tuple-element.55.refs_1_), channel_id=1, source_target_pairs={{0,1},{2,0},{4,2},{6,4},{7,6},{5,7},{3,5},{1,3},{8,9},{10,8},{12,1... | collective-permute-start | bytes 417800 | tf_op jit(solution)/shard_map/ppermute | solution.py:525
  30.7 6.2 %collective-permute-start.11 = (bf16[32,2176]{1,0:T(8,128)(2,1)S(1)}, bf16[32,2176]{1,0:T(8,128)(2,1)S(1)}, u32[]{:S(2)}, u32[]{:S(2)}) collective-permute-start(bf16[32,2176]{1,0:T(8,128)(2,1)S(1)} %collective-permute-done.10.refs_15_), channel_id=1, source_target_pairs={{0,2},{2,4},{4,6},{6,7},{7,5},{5,3},{3,1},{1,0},{8,10},{10,12},{12... | collective-permute-start | bytes 417800 | tf_op jit(solution)/shard_map/ppermute | solution.py:525
  32.9 6.3 %collective-permute-start.5 = (bf16[32,2176]{1,0:T(8,128)(2,1)S(1)}, bf16[32,2176]{1,0:T(8,128)(2,1)S(1)}, u32[]{:S(2)}, u32[]{:S(2)}) collective-permute-start(bf16[32,2176]{1,0:T(8,128)(2,1)S(1)} %collective-permute-done.3.refs_2_), channel_id=1, source_target_pairs={{0,1},{2,0},{4,2},{6,4},{7,6},{5,7},{3,5},{1,3},{8,9},{10,8},{12,1... | collective-permute-start | bytes 417800 | tf_op jit(solution)/shard_map/ppermute | solution.py:525
  33.7 6.6 %collective-permute-start.15 = (bf16[32,2176]{1,0:T(8,128)(2,1)S(1)}, bf16[32,2176]{1,0:T(8,128)(2,1)S(1)}, u32[]{:S(2)}, u32[]{:S(2)}) collective-permute-start(bf16[32,2176]{1,0:T(8,128)(2,1)S(1)} %collective-permute-done.14.refs_14_), channel_id=1, source_target_pairs={{0,2},{2,4},{4,6},{6,7},{7,5},{5,3},{3,1},{1,0},{8,10},{10,12},{12... | collective-permute-start | bytes 417800 | tf_op jit(solution)/shard_map/ppermute | solution.py:525
  35.8 6.6 %collective-permute-start.6 = (bf16[32,2176]{1,0:T(8,128)(2,1)S(1)}, bf16[32,2176]{1,0:T(8,128)(2,1)S(1)}, u32[]{:S(2)}, u32[]{:S(2)}) collective-permute-start(bf16[32,2176]{1,0:T(8,128)(2,1)S(1)} %collective-permute-done.4.refs_3_), channel_id=1, source_target_pairs={{0,1},{2,0},{4,2},{6,4},{7,6},{5,7},{3,5},{1,3},{8,9},{10,8},{12,1... | collective-permute-start | bytes 417800 | tf_op jit(solution)/shard_map/ppermute | solution.py:525
  36.9 6.7 %collective-permute-start.12 = (bf16[32,2176]{1,0:T(8,128)(2,1)S(1)}, bf16[32,2176]{1,0:T(8,128)(2,1)S(1)}, u32[]{:S(2)}, u32[]{:S(2)}) collective-permute-start(bf16[32,2176]{1,0:T(8,128)(2,1)S(1)} %collective-permute-done.11.refs_13_), channel_id=1, source_target_pairs={{0,2},{2,4},{4,6},{6,7},{7,5},{5,3},{3,1},{1,0},{8,10},{10,12},{12... | collective-permute-start | bytes 417800 | tf_op jit(solution)/shard_map/ppermute | solution.py:525
  39.2 6.2 %collective-permute-start.7 = (bf16[32,2176]{1,0:T(8,128)(2,1)S(1)}, bf16[32,2176]{1,0:T(8,128)(2,1)S(1)}, u32[]{:S(2)}, u32[]{:S(2)}) collective-permute-start(bf16[32,2176]{1,0:T(8,128)(2,1)S(1)} %collective-permute-done.5.refs_4_), channel_id=1, source_target_pairs={{0,1},{2,0},{4,2},{6,4},{7,6},{5,7},{3,5},{1,3},{8,9},{10,8},{12,1... | collective-permute-start | bytes 417800 | tf_op jit(solution)/shard_map/ppermute | solution.py:525
  40.3 5.5 %collective-permute-start.16 = (bf16[32,2176]{1,0:T(8,128)(2,1)S(1)}, bf16[32,2176]{1,0:T(8,128)(2,1)S(1)}, u32[]{:S(2)}, u32[]{:S(2)}) collective-permute-start(bf16[32,2176]{1,0:T(8,128)(2,1)S(1)} %collective-permute-done.15.refs_12_), channel_id=1, source_target_pairs={{0,2},{2,4},{4,6},{6,7},{7,5},{5,3},{3,1},{1,0},{8,10},{10,12},{12... | collective-permute-start | bytes 417800 | tf_op jit(solution)/shard_map/ppermute | solution.py:525
  42.4 18.0 %collective-permute-start.18 = (bf16[384,2048]{1,0:T(8,128)(2,1)}, bf16[384,2048]{1,0:T(8,128)(2,1)S(1)}, u32[]{:S(2)}, u32[]{:S(2)}) collective-permute-start(bf16[384,2048]{1,0:T(8,128)(2,1)} %get-tuple-element.58.refs_17_), channel_id=1, source_target_pairs={{0,8},{8,0},{16,24},{24,16},{1,9},{9,1},{17,25},{25,17},{2,10},{10... | collective-permute-start | bytes 4718600 | tf_op jit(solution)/shard_map/ppermute | solution.py:515
  43.6 6.4 %collective-permute-start.8 = (bf16[32,2176]{1,0:T(8,128)(2,1)S(1)}, bf16[32,2176]{1,0:T(8,128)(2,1)S(1)}, u32[]{:S(2)}, u32[]{:S(2)}) collective-permute-start(bf16[32,2176]{1,0:T(8,128)(2,1)S(1)} %collective-permute-done.6.refs_5_), channel_id=1, source_target_pairs={{0,1},{2,0},{4,2},{6,4},{7,6},{5,7},{3,5},{1,3},{8,9},{10,8},{12,1... | collective-permute-start | bytes 417800 | tf_op jit(solution)/shard_map/ppermute | solution.py:525
  45.8 5.7 %collective-permute-start.9 = (bf16[32,2176]{1,0:T(8,128)(2,1)S(1)}, bf16[32,2176]{1,0:T(8,128)(2,1)S(1)}, u32[]{:S(2)}, u32[]{:S(2)}) collective-permute-start(bf16[32,2176]{1,0:T(8,128)(2,1)S(1)} %collective-permute-done.7.refs_6_), channel_id=1, source_target_pairs={{0,1},{2,0},{4,2},{6,4},{7,6},{5,7},{3,5},{1,3},{8,9},{10,8},{12,1... | collective-permute-start | bytes 417800 | tf_op jit(solution)/shard_map/ppermute | solution.py:525
  50.0 6.1 %collective-permute-start.20 = (bf16[64,2048]{1,0:T(8,128)(2,1)S(1)}, bf16[64,2048]{1,0:T(8,128)(2,1)S(1)}, u32[]{:S(2)}, u32[]{:S(2)}) collective-permute-start(bf16[64,2048]{1,0:T(8,128)(2,1)S(1)} %get-tuple-element.94), channel_id=1, source_target_pairs={{0,8},{8,0},{16,24},{24,16},{1,9},{9,1},{17,25},{25,17},{2,10},{10... | collective-permute-start | bytes 786440 | tf_op jit(solution)/shard_map/ppermute | solution.py:515
  50.5 6.2 %collective-permute-start.21 = (bf16[64,2048]{1,0:T(8,128)(2,1)S(1)}, bf16[64,2048]{1,0:T(8,128)(2,1)S(1)}, u32[]{:S(2)}, u32[]{:S(2)}) collective-permute-start(bf16[64,2048]{1,0:T(8,128)(2,1)S(1)} %get-tuple-element.93), channel_id=1, source_target_pairs={{0,8},{8,0},{16,24},{24,16},{1,9},{9,1},{17,25},{25,17},{2,10},{10... | collective-permute-start | bytes 786440 | tf_op jit(solution)/shard_map/ppermute | solution.py:515
  51.5 26.0 %collective-permute-start.25 = (bf16[256,2048]{1,0:T(8,128)(2,1)S(1)}, bf16[256,2048]{1,0:T(8,128)(2,1)S(1)}, u32[]{:S(2)}, u32[]{:S(2)}) collective-permute-start(bf16[256,2048]{1,0:T(8,128)(2,1)S(1)} %copy-done.1), channel_id=1, source_target_pairs={{0,16},{8,24},{16,0},{24,8},{1,17},{9,25},{17,1},{25,9},{2,18},{10... | collective-permute-start | bytes 3145736 | tf_op jit(solution)/shard_map/ppermute | solution.py:515
  60.3 17.9 %collective-permute-start.24 = (bf16[256,2048]{1,0:T(8,128)(2,1)S(1)}, bf16[256,2048]{1,0:T(8,128)(2,1)S(1)}, u32[]{:S(2)}, u32[]{:S(2)}) collective-permute-start(bf16[256,2048]{1,0:T(8,128)(2,1)S(1)} %copy-done.1), channel_id=1, source_target_pairs={{0,8},{8,0},{16,24},{24,16},{1,9},{9,1},{17,25},{25,17},{2,10},{10... | collective-permute-start | bytes 3145736 | tf_op jit(solution)/shard_map/ppermute | solution.py:515
  77.7 5.2 %collective-permute-start.26 = (bf16[256,1024]{1,0:T(8,128)(2,1)S(1)}, bf16[256,1024]{1,0:T(8,128)(2,1)S(1)}, u32[]{:S(2)}, u32[]{:S(2)}) collective-permute-start(bf16[256,1024]{1,0:T(8,128)(2,1)S(1)} %get-tuple-element.91), channel_id=1, source_target_pairs={{0,8},{8,0},{16,24},{24,16},{1,9},{9,1},{17,25},{25,17},{2,10},{10... | collective-permute-start | bytes 1572872 | tf_op jit(solution)/shard_map/ppermute | solution.py:515
  85.5 6.2 %collective-permute-start.37 = (bf16[64,1024]{1,0:T(8,128)(2,1)S(1)}, bf16[64,1024]{1,0:T(8,128)(2,1)S(1)}, u32[]{:S(2)}, u32[]{:S(2)}) collective-permute-start(bf16[64,1024]{1,0:T(8,128)(2,1)S(1)} %pad_maximum_fusion.2), channel_id=1, source_target_pairs={{0,2},{2,4},{4,6},{6,7},{7,5},{5,3},{3,1},{1,0},{8,10},{10,12},{12... | collective-permute-start | bytes 393224 | tf_op jit(solution)/shard_map/ppermute | solution.py:525
  87.4 6.4 %collective-permute-start.41 = (bf16[64,1024]{1,0:T(8,128)(2,1)S(1)}, bf16[64,1024]{1,0:T(8,128)(2,1)S(1)}, u32[]{:S(2)}, u32[]{:S(2)}) collective-permute-start(bf16[64,1024]{1,0:T(8,128)(2,1)S(1)} %pad_maximum_fusion.3), channel_id=1, source_target_pairs={{0,1},{2,0},{4,2},{6,4},{7,6},{5,7},{3,5},{1,3},{8,9},{10,8},{12,1... | collective-permute-start | bytes 393224 | tf_op jit(solution)/shard_map/ppermute | solution.py:525
  88.1 6.5 %collective-permute-start.28 = (bf16[64,1024]{1,0:T(8,128)(2,1)S(1)}, bf16[64,1024]{1,0:T(8,128)(2,1)S(1)}, u32[]{:S(2)}, u32[]{:S(2)}) collective-permute-start(bf16[64,1024]{1,0:T(8,128)(2,1)S(1)} %pad_maximum_fusion), channel_id=1, source_target_pairs={{0,2},{2,4},{4,6},{6,7},{7,5},{5,3},{3,1},{1,0},{8,10},{10,12},{12... | collective-permute-start | bytes 393224 | tf_op jit(solution)/shard_map/ppermute | solution.py:525
  90.2 6.4 %collective-permute-start.32 = (bf16[64,1024]{1,0:T(8,128)(2,1)S(1)}, bf16[64,1024]{1,0:T(8,128)(2,1)S(1)}, u32[]{:S(2)}, u32[]{:S(2)}) collective-permute-start(bf16[64,1024]{1,0:T(8,128)(2,1)S(1)} %pad_maximum_fusion.1), channel_id=1, source_target_pairs={{0,1},{2,0},{4,2},{6,4},{7,6},{5,7},{3,5},{1,3},{8,9},{10,8},{12,1... | collective-permute-start | bytes 393224 | tf_op jit(solution)/shard_map/ppermute | solution.py:525
  91.8 5.8 %collective-permute-start.38 = (bf16[64,1024]{1,0:T(8,128)(2,1)S(1)}, bf16[64,1024]{1,0:T(8,128)(2,1)S(1)}, u32[]{:S(2)}, u32[]{:S(2)}) collective-permute-start(bf16[64,1024]{1,0:T(8,128)(2,1)S(1)} %add_convert_fusion.4), channel_id=1, source_target_pairs={{0,2},{2,4},{4,6},{6,7},{7,5},{5,3},{3,1},{1,0},{8,10},{10,12},{12... | collective-permute-start | bytes 393224 | tf_op jit(solution)/shard_map/ppermute | solution.py:525
  93.8 5.6 %collective-permute-start.42 = (bf16[64,1024]{1,0:T(8,128)(2,1)S(1)}, bf16[64,1024]{1,0:T(8,128)(2,1)S(1)}, u32[]{:S(2)}, u32[]{:S(2)}) collective-permute-start(bf16[64,1024]{1,0:T(8,128)(2,1)S(1)} %add_convert_fusion.2), channel_id=1, source_target_pairs={{0,1},{2,0},{4,2},{6,4},{7,6},{5,7},{3,5},{1,3},{8,9},{10,8},{12,1... | collective-permute-start | bytes 393224 | tf_op jit(solution)/shard_map/ppermute | solution.py:525
  94.7 6.2 %collective-permute-start.29 = (bf16[64,1024]{1,0:T(8,128)(2,1)S(1)}, bf16[64,1024]{1,0:T(8,128)(2,1)S(1)}, u32[]{:S(2)}, u32[]{:S(2)}) collective-permute-start(bf16[64,1024]{1,0:T(8,128)(2,1)S(1)} %add_convert_fusion.9), channel_id=1, source_target_pairs={{0,2},{2,4},{4,6},{6,7},{7,5},{5,3},{3,1},{1,0},{8,10},{10,12},{12... | collective-permute-start | bytes 393224 | tf_op jit(solution)/shard_map/ppermute | solution.py:525
  96.7 6.5 %collective-permute-start.33 = (bf16[64,1024]{1,0:T(8,128)(2,1)S(1)}, bf16[64,1024]{1,0:T(8,128)(2,1)S(1)}, u32[]{:S(2)}, u32[]{:S(2)}) collective-permute-start(bf16[64,1024]{1,0:T(8,128)(2,1)S(1)} %add_convert_fusion.7), channel_id=1, source_target_pairs={{0,1},{2,0},{4,2},{6,4},{7,6},{5,7},{3,5},{1,3},{8,9},{10,8},{12,1... | collective-permute-start | bytes 393224 | tf_op jit(solution)/shard_map/ppermute | solution.py:525
  97.6 5.6 %collective-permute-start.39 = (bf16[64,1024]{1,0:T(8,128)(2,1)S(1)}, bf16[64,1024]{1,0:T(8,128)(2,1)S(1)}, u32[]{:S(2)}, u32[]{:S(2)}) collective-permute-start(bf16[64,1024]{1,0:T(8,128)(2,1)S(1)} %add_convert_fusion.3), channel_id=1, source_target_pairs={{0,2},{2,4},{4,6},{6,7},{7,5},{5,3},{3,1},{1,0},{8,10},{10,12},{12... | collective-permute-start | bytes 393224 | tf_op jit(solution)/shard_map/ppermute | solution.py:525
  99.5 5.4 %collective-permute-start.43 = (bf16[64,1024]{1,0:T(8,128)(2,1)S(1)}, bf16[64,1024]{1,0:T(8,128)(2,1)S(1)}, u32[]{:S(2)}, u32[]{:S(2)}) collective-permute-start(bf16[64,1024]{1,0:T(8,128)(2,1)S(1)} %add_convert_fusion.1), channel_id=1, source_target_pairs={{0,1},{2,0},{4,2},{6,4},{7,6},{5,7},{3,5},{1,3},{8,9},{10,8},{12,1... | collective-permute-start | bytes 393224 | tf_op jit(solution)/shard_map/ppermute | solution.py:525
  (21 other events, 197.0 us)

commit v15 on v14

--- a/solution.py
+++ b/solution.py
@@ -129,20 +129,17 @@
 def attention_kernel(*refs):
     sources, outs, scratch = refs[:6], refs[6:10], refs[10:]
     own_ref, beside_ref, sent_ref, rows_ref = outs
-    table, lengths, q_ref, k_ref, v_ref, weights, attn, arrived = scratch
+    table, lengths, q_ref, k_ref, v_ref, weights, attn, rounded, arrived, left = scratch
+    rows = weights.shape[0]
     copies = [
         pltpu.make_async_copy(source, target, arrived.at[i])
         for i, (source, target) in enumerate(
             zip(
-                (*sources[:2], sources[2].at[0], *sources[3:5]),
-                (table, lengths, q_ref, k_ref, v_ref),
+                (*sources[:2], sources[2].at[0], *sources[3:5], sources[5].at[0, pl.ds(0, rows)]),
+                (table, lengths, q_ref, k_ref, v_ref, weights),
             )
         )
     ]
-    rows = weights.shape[0]
-    copies.append(
-        pltpu.make_async_copy(sources[5].at[0, pl.ds(0, rows)], weights, arrived.at[5])
-    )
     for copy in copies:
         copy.start()
     for copy in copies[:5]:
@@ -159,7 +156,19 @@
         row_request += (row >= end).astype(jnp.int32)
         column_request += (column >= end).astype(jnp.int32)
     same = row_request == column_request
+    block, end, split = tokens // 4, sent_ref.shape[1], weights.shape[1]
+    results = []
     for h in range(width // HDIM):
+        if h == 2:
+            copies[5].wait()
+            rounded[...] = weights[...].astype(jnp.bfloat16)
+            pairs = [(rounded, rows_ref)]
+            for i in range(rows // block):
+                here, there = pl.ds(i * block, block), pl.ds(i * split, split)
+                pairs.append((rounded.at[here], sent_ref.at[:, there]))
+            for source, target in pairs:
+                results.append(pltpu.make_async_copy(source, target, left.at[len(results)]))
+                results[-1].start()
         lanes = slice(h * HDIM, (h + 1) * HDIM)
         keys = jnp.concatenate([k_ref[table[0, p], :, lanes] for p in range(pages)], axis=0)
         values = jnp.concatenate([v_ref[table[0, p], :, lanes] for p in range(pages)], axis=0)
@@ -175,22 +184,18 @@
             jnp.bfloat16
         )
     own = lax.axis_index("dp")
-    block = tokens // 4
-    split = weights.shape[1]
-    end = sent_ref.shape[1]
     targets = (
         own_ref,
         beside_ref,
-        sent_ref.at[:, end - 2 * width : end - width],
-        sent_ref.at[:, end - width :],
+        sent_ref.at[:, pl.ds(end - 2 * width, width)],
+        sent_ref.at[:, pl.ds(end - width, width)],
     )
     for d, target in enumerate(targets):
-        target[...] = attn[pl.ds(pl.multiple_of((own ^ d) * block, block), block), :]
-    copies[5].wait()
-    rows_ref[...] = weights[...].astype(jnp.bfloat16)
-    for i in range(rows // block):
-        here = slice(i * block, (i + 1) * block)
-        sent_ref[:, i * split : (i + 1) * split] = rows_ref[here]
+        here = pl.ds(pl.multiple_of((own ^ d) * block, block), block)
+        results.append(pltpu.make_async_copy(attn.at[here], target, left.at[len(results)]))
+        results[-1].start()
+    for copy in results:
+        copy.wait()
 
 
 def attention(queries, key_pool, value_pool, page_table, prompt_lengths, gate_up, blocks):
@@ -203,7 +208,7 @@
         attention_kernel,
         out_shape=[jax.ShapeDtypeStruct(shape, jnp.bfloat16) for shape in shapes],
         in_specs=[pl.BlockSpec(memory_space=pltpu.HBM)] * 6,
-        out_specs=vmem(4),
+        out_specs=[pl.BlockSpec(memory_space=pltpu.HBM)] * 4,
         scratch_shapes=[
             pltpu.SMEM(page_table.shape, jnp.int32),
             pltpu.SMEM(prompt_lengths.shape, jnp.int32),
@@ -212,7 +217,9 @@
             pltpu.VMEM(value_pool.shape, jnp.bfloat16),
             pltpu.VMEM((blocks * block, split), jnp.float32),
             pltpu.VMEM((tokens, width), jnp.bfloat16),
+            pltpu.VMEM((blocks * block, split), jnp.bfloat16),
             pltpu.SemaphoreType.DMA((6,)),
+            pltpu.SemaphoreType.DMA((blocks + 5,)),
         ],
         compiler_params=params(VMEM_MOST),
         name="attention",
@@ -363,11 +370,31 @@
     return wait
 
 
+def row_copies(pieces, weights, arrived):
+    first = 0
+    for i, ref in enumerate(pieces):
+        depth = ref.shape[0]
+        yield pltpu.make_async_copy(ref, weights.at[pl.ds(first, depth)], arrived.at[i])
+        first += depth
+
+
+def start_rows(pieces, weights, arrived):
+    for copy in row_copies(pieces, weights, arrived):
+        copy.start()
+
+
+def wait_rows(pieces, weights, arrived):
+    for copy in row_copies(pieces, weights, arrived):
+        copy.wait()
+
+
 def up_kernel(sources, starts, *refs):
     pieces = len(starts)
     row_refs = refs[:sources]
     weight_refs = refs[sources : sources + pieces]
-    hidden_ref, own_gate_ref, rows, weights, units, arrived = refs[sources + pieces :]
+    down_refs, refs = refs[sources + pieces : -9], refs[-9:]
+    hidden_ref, own_gate_ref, total_ref, rows, weights, units, down, arrived, down_arrived = refs
+    start_rows(down_refs, down, down_arrived)
     width = rows.shape[1]
     tiles, _, block = units.shape
     wait = load_tiles(weight_refs, starts, weights, arrived, tiles, block)
@@ -397,9 +424,13 @@
     own = lax.axis_index("dp")
     for d in range(4):
         hidden_ref[:, d * block : (d + 1) * block] = units[own ^ d]
-
-
-def expert_up(rows, weights, width):
+    wait_rows(down_refs, down, down_arrived)
+    total_ref[...] = jnp.dot(
+        hidden_ref[:, : down.shape[0]], down[...], preferred_element_type=jnp.float32
+    )
+
+
+def expert_up(rows, weights, width, down):
     weights, starts = zip(*weights)
     tokens = sum(piece.shape[0] for piece in rows)
     features = sum(piece.shape[0] for piece in weights)
@@ -409,67 +440,59 @@
         out_shape=[
             jax.ShapeDtypeStruct((tokens, hidden_size), jnp.bfloat16),
             jax.ShapeDtypeStruct((tokens, 1), jnp.float32),
+            jax.ShapeDtypeStruct((tokens, down[0].shape[1]), jnp.float32),
         ],
-        in_specs=vmem(len(rows)) + [pl.BlockSpec(memory_space=pl.ANY)] * len(weights),
-        out_specs=vmem(2),
+        in_specs=vmem(len(rows)) + [pl.BlockSpec(memory_space=pl.ANY)] * (len(weights) + len(down)),
+        out_specs=vmem(3),
         scratch_shapes=[
             pltpu.VMEM((tokens, features), jnp.bfloat16),
             pltpu.VMEM((features, width), jnp.bfloat16),
             pltpu.VMEM((4, tokens, hidden_size // 4), jnp.bfloat16),
+            pltpu.VMEM((sum(x.shape[0] for x in down), down[0].shape[1]), jnp.bfloat16),
             pltpu.SemaphoreType.DMA((4, len(weights), 2)),
+            pltpu.SemaphoreType.DMA((len(down),)),
         ],
         compiler_params=params(),
         cost_estimate=SMALL,
         name="expert_up",
-    )(*rows, *weights)
-
-
-def load_rows(pieces, weights, arrived):
-    copies, first = [], 0
-    for i, ref in enumerate(pieces):
-        depth = ref.shape[0]
-        copies.append(
-            pltpu.make_async_copy(ref, weights.at[pl.ds(first, depth)], arrived.at[i])
-        )
-        first += depth
-    for copy in copies:
-        copy.start()
-    for copy in copies:
-        copy.wait()
-
-
-def part_kernel(hidden_ref, *refs):
+    )(*rows, *weights, *down)
+
+
+def part_kernel(first, column, hidden_ref, before_ref, *refs):
     pieces, (total_ref, weights, arrived) = refs[:-3], refs[-3:]
-    load_rows(pieces, weights, arrived)
-    total_ref[...] = jnp.dot(
-        hidden_ref[:, : weights.shape[0]], weights[...], preferred_element_type=jnp.float32
-    )
-
-
-def down_part(hidden_units, weights):
+    depth, width = weights.shape
+    pieces = [piece.at[:, pl.ds(column, width)] for piece in pieces]
+    start_rows(pieces, weights, arrived)
+    wait_rows(pieces, weights, arrived)
+    total_ref[...] = before_ref[:, column : column + width] + jnp.dot(
+        hidden_ref[:, first : first + depth], weights[...], preferred_element_type=jnp.float32
+    )
+
+
+def down_part(hidden_units, before, weights, first, column, width):
     depth = sum(piece.shape[0] for piece in weights)
-    shape = hidden_units.shape[0], weights[0].shape[1]
     return pl.pallas_call(
-        part_kernel,
-        out_shape=jax.ShapeDtypeStruct(shape, jnp.float32),
-        in_specs=vmem(1) + [pl.BlockSpec(memory_space=pl.ANY)] * len(weights),
+        lambda *refs: part_kernel(first, column, *refs),
+        out_shape=jax.ShapeDtypeStruct((hidden_units.shape[0], width), jnp.float32),
+        in_specs=vmem(2) + [pl.BlockSpec(memory_space=pl.ANY)] * len(weights),
         out_specs=pl.BlockSpec(memory_space=pltpu.VMEM),
         scratch_shapes=[
-            pltpu.VMEM((depth, shape[1]), jnp.bfloat16),
+            pltpu.VMEM((depth, width), jnp.bfloat16),
             pltpu.SemaphoreType.DMA((len(weights),)),
         ],
         compiler_params=params(),
         cost_estimate=SMALL,
         name="down_part",
-    )(hidden_units, *weights)
-
-
-def down_kernel(first, column, sources, hidden_ref, total_ref, gate_ref, piece, *refs):
+    )(hidden_units, before, *weights)
+
+
+def down_kernel(first, sources, hidden_ref, total_ref, gate_ref, piece, *refs):
     outs, (weights, arrived) = refs[:-2], refs[-2:]
-    load_rows([piece], weights, arrived)
+    start_rows([piece], weights, arrived)
+    wait_rows([piece], weights, arrived)
     depth, width = weights.shape
     units = hidden_ref[:, first : first + depth]
-    total = total_ref[:, column : column + width] + jnp.dot(
+    total = total_ref[...] + jnp.dot(
         units, weights[...], preferred_element_type=jnp.float32
     )
     weighted = (total * gate_ref[...]).astype(jnp.bfloat16)
@@ -489,12 +512,12 @@
     return blocks
 
 
-def expert_down(hidden_units, total, gates, weights, column, sources):
+def expert_down(hidden_units, total, gates, weights, sources):
     tokens, hidden_size = hidden_units.shape
     depth, width = weights.shape
     rows = tokens // sources
     return pl.pallas_call(
-        lambda *refs: down_kernel(hidden_size - depth, column, sources, *refs),
+        lambda *refs: down_kernel(hidden_size - depth, sources, *refs),
         out_shape=[
             jax.ShapeDtypeStruct((count, width), jnp.bfloat16)
             for _, count in down_blocks(rows, sources)
@@ -615,19 +638,22 @@
     down_beside = partner(after(down_own, *arrived[1]), 1)
     down_across = partner(after(down_own, *arrived[2]), 2)
     rest_opposite = relayed(after(rest_across, *arrived[3]), (depth - early) // 2)
-    hidden_units, gates = expert_up(
+    hidden_units, gates, total = expert_up(
         gathered,
         [(ref, 0) for ref in (first_own, rest_own, first_beside, rest_beside)]
         + [(first_across, start) for start in side]
         + [(ref, 0) for ref in (rest_across, *first_opposite, *rest_opposite)],
         columns,
+        [down_own],
     )
     down_ready = after(down_across, hidden_units)
-    total = down_part(hidden_units, [down_own, down_beside, down_ready])
     mixed = []
     for first in range(0, width, slab):
         opposite = partner(down_ready[:, first : first + slab], 1)
-        weighted = expert_down(hidden_units, total, gates, opposite, first, expert_count)
+        part = down_part(
+            hidden_units, total, [down_beside, down_ready], down_depth, first, slab
+        )
+        weighted = expert_down(hidden_units, part, gates, opposite, expert_count)
         sum_here = resid[:, first : first + slab].astype(jnp.float32)
         for term in scatter_sum(*weighted):
             sum_here = sum_here + term.astype(jnp.float32)

time: 109 us -> 110 us (level)
    pallas_call x3 -> x4, Pallas kernels: 3.04 us -> 2.66 us  [the longest x2 1.66 us: down_part(): pl.pallas_call(lambda *refs: part_kernel(first, column, *refs), out_shape...]
  transfers between devices with their start and end apart: 44 -> 44, of which waited for: 22 -> 25; matrix products, arithmetic and copies ran while one was open for 1% -> 1% of each run, Pallas kernels for 14% -> 15%
where the time goes in v15:
time: 110 us
  waiting for transfers between devices  48.2 us (44%)
  starting transfers between devices  39.8 us (36%)
  Pallas kernels  20 us (18%)
  other arithmetic  1.29 us (1%)
    ppermute x30, starting transfers between devices, around(): lax.ppermute(x, 'expert', [(ring[i], ring[(i + step) % count]) for i in r...  33.8 us
    ppermute x14, waiting for transfers between devices, partner(): return lax.ppermute(x, 'dp', [(i, i ^ distance) for i in range(4)])  28 us
    ppermute x30, waiting for transfers between devices, around(): lax.ppermute(x, 'expert', [(ring[i], ring[(i + step) % count]) for i in r...  20.2 us
    pallas_call x1, Pallas kernels, expert_up(): pl.pallas_call(lambda *refs: up_kernel(len(rows), starts, *refs), out_sha...  8.89 us
    ppermute x14, starting transfers between devices, partner(): return lax.ppermute(x, 'dp', [(i, i ^ distance) for i in range(4)])  6.07 us
    pallas_call x1, Pallas kernels, cast_rows(): pl.pallas_call(lambda *refs: cast_kernel(spans, *refs), out_shape=[jax.Sh...  3.98 us
    pallas_call x1, Pallas kernels, attention(): pl.pallas_call(attention_kernel, out_shape=[jax.ShapeDtypeStruct(shape, j...  3.82 us
  transfers between devices with their start and end apart: 44, of which 25 were waited for; matrix products, arithmetic and copies ran while one was open for 1% of the time, Pallas kernels for 15%

profile of v15, /device:TPU:0, one launch (start us, length us, event | category | flops | bytes accessed | tf_op | source)
XLA Modules:
  0.0 109.9 jit_solution(11522654134269793356)
XLA Ops:
  0.0 3.8 %attention.1 = (bf16[64,512]{1,0:T(8,128)(2,1)}, bf16[64,512]{1,0:T(8,128)(2,1)}, bf16[64,5120]{1,0:T(8,128)(2,1)}, bf16[128,2048]{1,0:T(8,128)(2,1)}) custom-call(s32[1,2]{1,0:T(1,128)} %refs_0_.1, s32[1,4]{1,0:T(1,128)} %refs_1_.2, bf16[1,256,512]{2,1,0:T(8,128)(2,1)} %refs_2_.1, bf16[2,128,512]{2,1,0:T(8,128)(2,1)} %refs_3_.1, ...), custom_call_target="tpu_custom_call" | custom-call | tf_op jit(solution)/shard_map/attention/pallas_call | solution.py:207
  3.8 3.0 %collective-permute-start.1 = (bf16[64,5120]{1,0:T(8,128)(2,1)}, bf16[64,5120]{1,0:T(8,128)(2,1)S(1)}, u32[]{:S(2)}, u32[]{:S(2)}) collective-permute-start(bf16[64,5120]{1,0:T(8,128)(2,1)} %get-tuple-element.50), channel_id=1, source_target_pairs={{0,16},{8,24},{16,0},{24,8},{1,17},{9,25},{17,1},{25,9},{2,18},{10... | collective-permute-start | bytes 1966088 | tf_op jit(solution)/shard_map/ppermute | solution.py:538
  6.9 4.0 %cast_rows.1 = (bf16[384,2048]{1,0:T(8,128)(2,1)}, bf16[256,2048]{1,0:T(8,128)(2,1)}) custom-call(f32[1,512,2048]{2,1,0:T(8,128)} %refs_0_.2, f32[1,256,2048]{2,1,0:T(8,128)} %refs_1_.3), custom_call_target="tpu_custom_call" | custom-call | tf_op jit(solution)/shard_map/cast_rows/pallas_call | solution.py:335
  11.0 11.6 %collective-permute-done.1.refs_2_.refs_20_.refs_21_ = bf16[64,5120]{1,0:T(8,128)(2,1)S(1)} collective-permute-done((bf16[64,5120]{1,0:T(8,128)(2,1)}, bf16[64,5120]{1,0:T(8,128)(2,1)S(1)}, u32[]{:S(2)}, u32[]{:S(2)}) %collective-permute-start.1) | collective-permute-done | bytes 655392 | tf_op jit(solution)/shard_map/ppermute | solution.py:538
  22.6 1.2 %collective-permute-done.2.refs_3_ = bf16[64,512]{1,0:T(8,128)(2,1)S(1)} collective-permute-done((bf16[64,512]{1,0:T(8,128)(2,1)S(1)}, bf16[64,512]{1,0:T(8,128)(2,1)S(1)}, u32[]{:S(2)}, u32[]{:S(2)}) %collective-permute-start.2) | collective-permute-done | bytes 65568 | tf_op jit(solution)/shard_map/ppermute | solution.py:538
  24.5 2.2 %collective-permute-start.10 = (bf16[32,2176]{1,0:T(8,128)(2,1)S(1)}, bf16[32,2176]{1,0:T(8,128)(2,1)S(1)}, u32[]{:S(2)}, u32[]{:S(2)}) collective-permute-start(bf16[32,2176]{1,0:T(8,128)(2,1)S(1)} %get-tuple-element.56.refs_1_), channel_id=1, source_target_pairs={{0,2},{2,4},{4,6},{6,7},{7,5},{5,3},{3,1},{1,0},{8,10},{10,12},{12... | collective-permute-start | bytes 417800 | tf_op jit(solution)/shard_map/ppermute | solution.py:548
  26.8 2.0 %collective-permute-start.14 = (bf16[32,2176]{1,0:T(8,128)(2,1)S(1)}, bf16[32,2176]{1,0:T(8,128)(2,1)S(1)}, u32[]{:S(2)}, u32[]{:S(2)}) collective-permute-start(bf16[32,2176]{1,0:T(8,128)(2,1)S(1)} %get-tuple-element.55.refs_0_), channel_id=1, source_target_pairs={{0,2},{2,4},{4,6},{6,7},{7,5},{5,3},{3,1},{1,0},{8,10},{10,12},{12... | collective-permute-start | bytes 417800 | tf_op jit(solution)/shard_map/ppermute | solution.py:548
  28.8 2.3 %collective-permute-done.10.refs_15_ = bf16[32,2176]{1,0:T(8,128)(2,1)S(1)} collective-permute-done((bf16[32,2176]{1,0:T(8,128)(2,1)S(1)}, bf16[32,2176]{1,0:T(8,128)(2,1)S(1)}, u32[]{:S(2)}, u32[]{:S(2)}) %collective-permute-start.10) | collective-permute-done | bytes 139296 | tf_op jit(solution)/shard_map/ppermute | solution.py:548
  31.1 2.1 %collective-permute-start.11 = (bf16[32,2176]{1,0:T(8,128)(2,1)S(1)}, bf16[32,2176]{1,0:T(8,128)(2,1)S(1)}, u32[]{:S(2)}, u32[]{:S(2)}) collective-permute-start(bf16[32,2176]{1,0:T(8,128)(2,1)S(1)} %collective-permute-done.10.refs_15_), channel_id=1, source_target_pairs={{0,2},{2,4},{4,6},{6,7},{7,5},{5,3},{3,1},{1,0},{8,10},{10,12},{12... | collective-permute-start | bytes 417800 | tf_op jit(solution)/shard_map/ppermute | solution.py:548
  34.1 2.1 %collective-permute-start.15 = (bf16[32,2176]{1,0:T(8,128)(2,1)S(1)}, bf16[32,2176]{1,0:T(8,128)(2,1)S(1)}, u32[]{:S(2)}, u32[]{:S(2)}) collective-permute-start(bf16[32,2176]{1,0:T(8,128)(2,1)S(1)} %collective-permute-done.14.refs_14_), channel_id=1, source_target_pairs={{0,2},{2,4},{4,6},{6,7},{7,5},{5,3},{3,1},{1,0},{8,10},{10,12},{12... | collective-permute-start | bytes 417800 | tf_op jit(solution)/shard_map/ppermute | solution.py:548
  37.4 2.2 %collective-permute-start.12 = (bf16[32,2176]{1,0:T(8,128)(2,1)S(1)}, bf16[32,2176]{1,0:T(8,128)(2,1)S(1)}, u32[]{:S(2)}, u32[]{:S(2)}) collective-permute-start(bf16[32,2176]{1,0:T(8,128)(2,1)S(1)} %collective-permute-done.11.refs_13_), channel_id=1, source_target_pairs={{0,2},{2,4},{4,6},{6,7},{7,5},{5,3},{3,1},{1,0},{8,10},{10,12},{12... | collective-permute-start | bytes 417800 | tf_op jit(solution)/shard_map/ppermute | solution.py:548
  40.8 2.1 %collective-permute-start.16 = (bf16[32,2176]{1,0:T(8,128)(2,1)S(1)}, bf16[32,2176]{1,0:T(8,128)(2,1)S(1)}, u32[]{:S(2)}, u32[]{:S(2)}) collective-permute-start(bf16[32,2176]{1,0:T(8,128)(2,1)S(1)} %collective-permute-done.15.refs_12_), channel_id=1, source_target_pairs={{0,2},{2,4},{4,6},{6,7},{7,5},{5,3},{3,1},{1,0},{8,10},{10,12},{12... | collective-permute-start | bytes 417800 | tf_op jit(solution)/shard_map/ppermute | solution.py:548
  42.9 1.2 %collective-permute-done.12.refs_11_ = bf16[32,2176]{1,0:T(8,128)(2,1)S(1)} collective-permute-done((bf16[32,2176]{1,0:T(8,128)(2,1)S(1)}, bf16[32,2176]{1,0:T(8,128)(2,1)S(1)}, u32[]{:S(2)}, u32[]{:S(2)}) %collective-permute-start.12) | collective-permute-done | bytes 139296 | tf_op jit(solution)/shard_map/ppermute | solution.py:548
  44.0 1.8 %collective-permute-start.8 = (bf16[32,2176]{1,0:T(8,128)(2,1)S(1)}, bf16[32,2176]{1,0:T(8,128)(2,1)S(1)}, u32[]{:S(2)}, u32[]{:S(2)}) collective-permute-start(bf16[32,2176]{1,0:T(8,128)(2,1)S(1)} %collective-permute-done.6.refs_5_), channel_id=1, source_target_pairs={{0,1},{2,0},{4,2},{6,4},{7,6},{5,7},{3,5},{1,3},{8,9},{10,8},{12,1... | collective-permute-start | bytes 417800 | tf_op jit(solution)/shard_map/ppermute | solution.py:548
  46.2 1.7 %collective-permute-start.9 = (bf16[32,2176]{1,0:T(8,128)(2,1)S(1)}, bf16[32,2176]{1,0:T(8,128)(2,1)S(1)}, u32[]{:S(2)}, u32[]{:S(2)}) collective-permute-start(bf16[32,2176]{1,0:T(8,128)(2,1)S(1)} %collective-permute-done.7.refs_6_), channel_id=1, source_target_pairs={{0,1},{2,0},{4,2},{6,4},{7,6},{5,7},{3,5},{1,3},{8,9},{10,8},{12,1... | collective-permute-start | bytes 417800 | tf_op jit(solution)/shard_map/ppermute | solution.py:548
  48.0 2.4 %collective-permute-done.8.refs_7_ = bf16[32,2176]{1,0:T(8,128)(2,1)S(1)} collective-permute-done((bf16[32,2176]{1,0:T(8,128)(2,1)S(1)}, bf16[32,2176]{1,0:T(8,128)(2,1)S(1)}, u32[]{:S(2)}, u32[]{:S(2)}) %collective-permute-start.8) | collective-permute-done | bytes 139296 | tf_op jit(solution)/shard_map/ppermute | solution.py:548
  51.9 1.5 %collective-permute-start.25 = (bf16[256,2048]{1,0:T(8,128)(2,1)S(1)}, bf16[256,2048]{1,0:T(8,128)(2,1)S(1)}, u32[]{:S(2)}, u32[]{:S(2)}) collective-permute-start(bf16[256,2048]{1,0:T(8,128)(2,1)S(1)} %copy-done.1), channel_id=1, source_target_pairs={{0,16},{8,24},{16,0},{24,8},{1,17},{9,25},{17,1},{25,9},{2,18},{10... | collective-permute-start | bytes 3145736 | tf_op jit(solution)/shard_map/ppermute | solution.py:538
  53.4 2.9 %collective-permute-done.19.refs_22_ = bf16[384,2048]{1,0:T(8,128)(2,1)S(1)} collective-permute-done((bf16[384,2048]{1,0:T(8,128)(2,1)}, bf16[384,2048]{1,0:T(8,128)(2,1)S(1)}, u32[]{:S(2)}, u32[]{:S(2)}) %collective-permute-start.19) | collective-permute-done | bytes 1572896 | tf_op jit(solution)/shard_map/ppermute | solution.py:538
  57.2 3.6 %collective-permute-done.17.refs_18_ = bf16[128,2048]{1,0:T(8,128)(2,1)S(1)} collective-permute-done((bf16[128,2048]{1,0:T(8,128)(2,1)S(1)}, bf16[128,2048]{1,0:T(8,128)(2,1)S(1)}, u32[]{:S(2)}, u32[]{:S(2)}) %collective-permute-start.17) | collective-permute-done | bytes 524320 | tf_op jit(solution)/shard_map/ppermute | solution.py:538
  60.9 8.9 %expert_up.1 = (bf16[512,1024]{1,0:T(8,128)(2,1)S(1)}, f32[512,1]{1,0:T(8,128)S(1)}, f32[512,2048]{1,0:T(8,128)S(1)}) custom-call(bf16[32,2176]{1,0:T(8,128)(2,1)S(1)} %get-tuple-element.55.refs_0_, bf16[32,2176]{1,0:T(8,128)(2,1)S(1)} %get-tuple-element.56.refs_1_, bf16[32,2176]{1,0:T(8,128)(2,1)S(1)} %collective-permute-done.3.refs_2_, ...), custom_call_target="tpu_custom_call" | custom-call | flops 1 | bytes 1 | tf_op jit(solution)/shard_map/expert_up/pallas_call | solution.py:438
  69.8 8.2 %collective-permute-done.25.refs_3_ = bf16[256,2048]{1,0:T(8,128)(2,1)S(1)} collective-permute-done((bf16[256,2048]{1,0:T(8,128)(2,1)S(1)}, bf16[256,2048]{1,0:T(8,128)(2,1)S(1)}, u32[]{:S(2)}, u32[]{:S(2)}) %collective-permute-start.25) | collective-permute-done | bytes 1048608 | tf_op jit(solution)/shard_map/ppermute | solution.py:538
  80.5 2.1 %collective-permute-start.36 = (bf16[32,1024]{1,0:T(8,128)(2,1)S(1)}, bf16[32,1024]{1,0:T(8,128)(2,1)S(1)}, u32[]{:S(2)}, u32[]{:S(2)}) collective-permute-start(bf16[32,1024]{1,0:T(8,128)(2,1)S(1)} %get-tuple-element.84), channel_id=1, source_target_pairs={{0,2},{2,4},{4,6},{6,7},{7,5},{5,3},{3,1},{1,0},{8,10},{10,12},{12... | collective-permute-start | bytes 196616 | tf_op jit(solution)/shard_map/ppermute | solution.py:548
  84.2 1.9 %collective-permute-start.27 = (bf16[32,1024]{1,0:T(8,128)(2,1)S(1)}, bf16[32,1024]{1,0:T(8,128)(2,1)S(1)}, u32[]{:S(2)}, u32[]{:S(2)}) collective-permute-start(bf16[32,1024]{1,0:T(8,128)(2,1)S(1)} %get-tuple-element.73), channel_id=1, source_target_pairs={{0,2},{2,4},{4,6},{6,7},{7,5},{5,3},{3,1},{1,0},{8,10},{10,12},{12... | collective-permute-start | bytes 196616 | tf_op jit(solution)/shard_map/ppermute | solution.py:548
  86.3 1.9 %collective-permute-start.37 = (bf16[64,1024]{1,0:T(8,128)(2,1)S(1)}, bf16[64,1024]{1,0:T(8,128)(2,1)S(1)}, u32[]{:S(2)}, u32[]{:S(2)}) collective-permute-start(bf16[64,1024]{1,0:T(8,128)(2,1)S(1)} %pad_maximum_fusion.2), channel_id=1, source_target_pairs={{0,2},{2,4},{4,6},{6,7},{7,5},{5,3},{3,1},{1,0},{8,10},{10,12},{12... | collective-permute-start | bytes 393224 | tf_op jit(solution)/shard_map/ppermute | solution.py:548
  89.0 2.0 %collective-permute-start.28 = (bf16[64,1024]{1,0:T(8,128)(2,1)S(1)}, bf16[64,1024]{1,0:T(8,128)(2,1)S(1)}, u32[]{:S(2)}, u32[]{:S(2)}) collective-permute-start(bf16[64,1024]{1,0:T(8,128)(2,1)S(1)} %pad_maximum_fusion), channel_id=1, source_target_pairs={{0,2},{2,4},{4,6},{6,7},{7,5},{5,3},{3,1},{1,0},{8,10},{10,12},{12... | collective-permute-start | bytes 393224 | tf_op jit(solution)/shard_map/ppermute | solution.py:548
  91.2 1.4 %collective-permute-done.37 = bf16[64,1024]{1,0:T(8,128)(2,1)S(1)} collective-permute-done((bf16[64,1024]{1,0:T(8,128)(2,1)S(1)}, bf16[64,1024]{1,0:T(8,128)(2,1)S(1)}, u32[]{:S(2)}, u32[]{:S(2)}) %collective-permute-start.37) | collective-permute-done | bytes 131104 | tf_op jit(solution)/shard_map/ppermute | solution.py:548
  92.7 2.0 %collective-permute-start.38 = (bf16[64,1024]{1,0:T(8,128)(2,1)S(1)}, bf16[64,1024]{1,0:T(8,128)(2,1)S(1)}, u32[]{:S(2)}, u32[]{:S(2)}) collective-permute-start(bf16[64,1024]{1,0:T(8,128)(2,1)S(1)} %add_convert_fusion.4), channel_id=1, source_target_pairs={{0,2},{2,4},{4,6},{6,7},{7,5},{5,3},{3,1},{1,0},{8,10},{10,12},{12... | collective-permute-start | bytes 393224 | tf_op jit(solution)/shard_map/ppermute | solution.py:548
  95.5 1.9 %collective-permute-start.29 = (bf16[64,1024]{1,0:T(8,128)(2,1)S(1)}, bf16[64,1024]{1,0:T(8,128)(2,1)S(1)}, u32[]{:S(2)}, u32[]{:S(2)}) collective-permute-start(bf16[64,1024]{1,0:T(8,128)(2,1)S(1)} %add_convert_fusion.9), channel_id=1, source_target_pairs={{0,2},{2,4},{4,6},{6,7},{7,5},{5,3},{3,1},{1,0},{8,10},{10,12},{12... | collective-permute-start | bytes 393224 | tf_op jit(solution)/shard_map/ppermute | solution.py:548
  98.5 1.8 %collective-permute-start.39 = (bf16[64,1024]{1,0:T(8,128)(2,1)S(1)}, bf16[64,1024]{1,0:T(8,128)(2,1)S(1)}, u32[]{:S(2)}, u32[]{:S(2)}) collective-permute-start(bf16[64,1024]{1,0:T(8,128)(2,1)S(1)} %add_convert_fusion.3), channel_id=1, source_target_pairs={{0,2},{2,4},{4,6},{6,7},{7,5},{5,3},{3,1},{1,0},{8,10},{10,12},{12... | collective-permute-start | bytes 393224 | tf_op jit(solution)/shard_map/ppermute | solution.py:548
  101.8 2.0 %collective-permute-start.30 = (bf16[64,1024]{1,0:T(8,128)(2,1)S(1)}, bf16[64,1024]{1,0:T(8,128)(2,1)S(1)}, u32[]{:S(2)}, u32[]{:S(2)}) collective-permute-start(bf16[64,1024]{1,0:T(8,128)(2,1)S(1)} %add_convert_fusion.8), channel_id=1, source_target_pairs={{0,2},{2,4},{4,6},{6,7},{7,5},{5,3},{3,1},{1,0},{8,10},{10,12},{12... | collective-permute-start | bytes 393224 | tf_op jit(solution)/shard_map/ppermute | solution.py:548
  104.1 1.7 %collective-permute-done.43 = bf16[64,1024]{1,0:T(8,128)(2,1)S(1)} collective-permute-done((bf16[64,1024]{1,0:T(8,128)(2,1)S(1)}, bf16[64,1024]{1,0:T(8,128)(2,1)S(1)}, u32[]{:S(2)}, u32[]{:S(2)}) %collective-permute-start.43) | collective-permute-done | bytes 131104 | tf_op jit(solution)/shard_map/ppermute | solution.py:548
  106.9 2.2 %collective-permute-done.34 = bf16[64,1024]{1,0:T(8,128)(2,1)S(1)} collective-permute-done((bf16[64,1024]{1,0:T(8,128)(2,1)S(1)}, bf16[64,1024]{1,0:T(8,128)(2,1)S(1)}, u32[]{:S(2)}, u32[]{:S(2)}) %collective-permute-start.34) | collective-permute-done | bytes 131104 | tf_op jit(solution)/shard_map/ppermute | solution.py:548
  (104 shorter events, 18.2 us)
Async XLA Ops:
  3.8 18.8 %collective-permute-start.1 = (bf16[64,5120]{1,0:T(8,128)(2,1)}, bf16[64,5120]{1,0:T(8,128)(2,1)S(1)}, u32[]{:S(2)}, u32[]{:S(2)}) collective-permute-start(bf16[64,5120]{1,0:T(8,128)(2,1)} %get-tuple-element.50), channel_id=1, source_target_pairs={{0,16},{8,24},{16,0},{24,8},{1,17},{9,25},{17,1},{25,9},{2,18},{10... | collective-permute-start | bytes 1966088 | tf_op jit(solution)/shard_map/ppermute | solution.py:538
  10.9 45.4 %collective-permute-start.19 = (bf16[384,2048]{1,0:T(8,128)(2,1)}, bf16[384,2048]{1,0:T(8,128)(2,1)S(1)}, u32[]{:S(2)}, u32[]{:S(2)}) collective-permute-start(bf16[384,2048]{1,0:T(8,128)(2,1)} %get-tuple-element.59.refs_17_), channel_id=1, source_target_pairs={{0,16},{8,24},{16,0},{24,8},{1,17},{9,25},{17,1},{25,9},{2,18},{10... | collective-permute-start | bytes 4718600 | tf_op jit(solution)/shard_map/ppermute | solution.py:538
  11.0 11.6 %collective-permute-start = (bf16[64,512]{1,0:T(8,128)(2,1)S(1)}, bf16[64,512]{1,0:T(8,128)(2,1)S(1)}, u32[]{:S(2)}, u32[]{:S(2)}) collective-permute-start(bf16[64,512]{1,0:T(8,128)(2,1)S(1)} %copy-done.8), channel_id=1, source_target_pairs={{0,8},{8,0},{16,24},{24,16},{1,9},{9,1},{17,25},{25,17},{2,10},{10... | collective-permute-start | bytes 196616 | tf_op jit(solution)/shard_map/ppermute | solution.py:538
  24.5 6.6 %collective-permute-start.10 = (bf16[32,2176]{1,0:T(8,128)(2,1)S(1)}, bf16[32,2176]{1,0:T(8,128)(2,1)S(1)}, u32[]{:S(2)}, u32[]{:S(2)}) collective-permute-start(bf16[32,2176]{1,0:T(8,128)(2,1)S(1)} %get-tuple-element.56.refs_1_), channel_id=1, source_target_pairs={{0,2},{2,4},{4,6},{6,7},{7,5},{5,3},{3,1},{1,0},{8,10},{10,12},{12... | collective-permute-start | bytes 417800 | tf_op jit(solution)/shard_map/ppermute | solution.py:548
  26.7 6.6 %collective-permute-start.3 = (bf16[32,2176]{1,0:T(8,128)(2,1)S(1)}, bf16[32,2176]{1,0:T(8,128)(2,1)S(1)}, u32[]{:S(2)}, u32[]{:S(2)}) collective-permute-start(bf16[32,2176]{1,0:T(8,128)(2,1)S(1)} %get-tuple-element.55.refs_0_), channel_id=1, source_target_pairs={{0,1},{2,0},{4,2},{6,4},{7,6},{5,7},{3,5},{1,3},{8,9},{10,8},{12,1... | collective-permute-start | bytes 417800 | tf_op jit(solution)/shard_map/ppermute | solution.py:548
  26.8 7.4 %collective-permute-start.14 = (bf16[32,2176]{1,0:T(8,128)(2,1)S(1)}, bf16[32,2176]{1,0:T(8,128)(2,1)S(1)}, u32[]{:S(2)}, u32[]{:S(2)}) collective-permute-start(bf16[32,2176]{1,0:T(8,128)(2,1)S(1)} %get-tuple-element.55.refs_0_), channel_id=1, source_target_pairs={{0,2},{2,4},{4,6},{6,7},{7,5},{5,3},{3,1},{1,0},{8,10},{10,12},{12... | collective-permute-start | bytes 417800 | tf_op jit(solution)/shard_map/ppermute | solution.py:548
  28.8 7.5 %collective-permute-start.4 = (bf16[32,2176]{1,0:T(8,128)(2,1)S(1)}, bf16[32,2176]{1,0:T(8,128)(2,1)S(1)}, u32[]{:S(2)}, u32[]{:S(2)}) collective-permute-start(bf16[32,2176]{1,0:T(8,128)(2,1)S(1)} %get-tuple-element.56.refs_1_), channel_id=1, source_target_pairs={{0,1},{2,0},{4,2},{6,4},{7,6},{5,7},{3,5},{1,3},{8,9},{10,8},{12,1... | collective-permute-start | bytes 417800 | tf_op jit(solution)/shard_map/ppermute | solution.py:548
  31.1 6.2 %collective-permute-start.11 = (bf16[32,2176]{1,0:T(8,128)(2,1)S(1)}, bf16[32,2176]{1,0:T(8,128)(2,1)S(1)}, u32[]{:S(2)}, u32[]{:S(2)}) collective-permute-start(bf16[32,2176]{1,0:T(8,128)(2,1)S(1)} %collective-permute-done.10.refs_15_), channel_id=1, source_target_pairs={{0,2},{2,4},{4,6},{6,7},{7,5},{5,3},{3,1},{1,0},{8,10},{10,12},{12... | collective-permute-start | bytes 417800 | tf_op jit(solution)/shard_map/ppermute | solution.py:548
  33.3 6.3 %collective-permute-start.5 = (bf16[32,2176]{1,0:T(8,128)(2,1)S(1)}, bf16[32,2176]{1,0:T(8,128)(2,1)S(1)}, u32[]{:S(2)}, u32[]{:S(2)}) collective-permute-start(bf16[32,2176]{1,0:T(8,128)(2,1)S(1)} %collective-permute-done.3.refs_2_), channel_id=1, source_target_pairs={{0,1},{2,0},{4,2},{6,4},{7,6},{5,7},{3,5},{1,3},{8,9},{10,8},{12,1... | collective-permute-start | bytes 417800 | tf_op jit(solution)/shard_map/ppermute | solution.py:548
  34.1 6.6 %collective-permute-start.15 = (bf16[32,2176]{1,0:T(8,128)(2,1)S(1)}, bf16[32,2176]{1,0:T(8,128)(2,1)S(1)}, u32[]{:S(2)}, u32[]{:S(2)}) collective-permute-start(bf16[32,2176]{1,0:T(8,128)(2,1)S(1)} %collective-permute-done.14.refs_14_), channel_id=1, source_target_pairs={{0,2},{2,4},{4,6},{6,7},{7,5},{5,3},{3,1},{1,0},{8,10},{10,12},{12... | collective-permute-start | bytes 417800 | tf_op jit(solution)/shard_map/ppermute | solution.py:548
  36.2 6.6 %collective-permute-start.6 = (bf16[32,2176]{1,0:T(8,128)(2,1)S(1)}, bf16[32,2176]{1,0:T(8,128)(2,1)S(1)}, u32[]{:S(2)}, u32[]{:S(2)}) collective-permute-start(bf16[32,2176]{1,0:T(8,128)(2,1)S(1)} %collective-permute-done.4.refs_3_), channel_id=1, source_target_pairs={{0,1},{2,0},{4,2},{6,4},{7,6},{5,7},{3,5},{1,3},{8,9},{10,8},{12,1... | collective-permute-start | bytes 417800 | tf_op jit(solution)/shard_map/ppermute | solution.py:548
  37.4 6.7 %collective-permute-start.12 = (bf16[32,2176]{1,0:T(8,128)(2,1)S(1)}, bf16[32,2176]{1,0:T(8,128)(2,1)S(1)}, u32[]{:S(2)}, u32[]{:S(2)}) collective-permute-start(bf16[32,2176]{1,0:T(8,128)(2,1)S(1)} %collective-permute-done.11.refs_13_), channel_id=1, source_target_pairs={{0,2},{2,4},{4,6},{6,7},{7,5},{5,3},{3,1},{1,0},{8,10},{10,12},{12... | collective-permute-start | bytes 417800 | tf_op jit(solution)/shard_map/ppermute | solution.py:548
  39.6 6.2 %collective-permute-start.7 = (bf16[32,2176]{1,0:T(8,128)(2,1)S(1)}, bf16[32,2176]{1,0:T(8,128)(2,1)S(1)}, u32[]{:S(2)}, u32[]{:S(2)}) collective-permute-start(bf16[32,2176]{1,0:T(8,128)(2,1)S(1)} %collective-permute-done.5.refs_4_), channel_id=1, source_target_pairs={{0,1},{2,0},{4,2},{6,4},{7,6},{5,7},{3,5},{1,3},{8,9},{10,8},{12,1... | collective-permute-start | bytes 417800 | tf_op jit(solution)/shard_map/ppermute | solution.py:548
  40.8 5.5 %collective-permute-start.16 = (bf16[32,2176]{1,0:T(8,128)(2,1)S(1)}, bf16[32,2176]{1,0:T(8,128)(2,1)S(1)}, u32[]{:S(2)}, u32[]{:S(2)}) collective-permute-start(bf16[32,2176]{1,0:T(8,128)(2,1)S(1)} %collective-permute-done.15.refs_12_), channel_id=1, source_target_pairs={{0,2},{2,4},{4,6},{6,7},{7,5},{5,3},{3,1},{1,0},{8,10},{10,12},{12... | collective-permute-start | bytes 417800 | tf_op jit(solution)/shard_map/ppermute | solution.py:548
  42.8 18.0 %collective-permute-start.18 = (bf16[384,2048]{1,0:T(8,128)(2,1)}, bf16[384,2048]{1,0:T(8,128)(2,1)S(1)}, u32[]{:S(2)}, u32[]{:S(2)}) collective-permute-start(bf16[384,2048]{1,0:T(8,128)(2,1)} %get-tuple-element.59.refs_17_), channel_id=1, source_target_pairs={{0,8},{8,0},{16,24},{24,16},{1,9},{9,1},{17,25},{25,17},{2,10},{10... | collective-permute-start | bytes 4718600 | tf_op jit(solution)/shard_map/ppermute | solution.py:538
  44.0 6.4 %collective-permute-start.8 = (bf16[32,2176]{1,0:T(8,128)(2,1)S(1)}, bf16[32,2176]{1,0:T(8,128)(2,1)S(1)}, u32[]{:S(2)}, u32[]{:S(2)}) collective-permute-start(bf16[32,2176]{1,0:T(8,128)(2,1)S(1)} %collective-permute-done.6.refs_5_), channel_id=1, source_target_pairs={{0,1},{2,0},{4,2},{6,4},{7,6},{5,7},{3,5},{1,3},{8,9},{10,8},{12,1... | collective-permute-start | bytes 417800 | tf_op jit(solution)/shard_map/ppermute | solution.py:548
  46.2 5.7 %collective-permute-start.9 = (bf16[32,2176]{1,0:T(8,128)(2,1)S(1)}, bf16[32,2176]{1,0:T(8,128)(2,1)S(1)}, u32[]{:S(2)}, u32[]{:S(2)}) collective-permute-start(bf16[32,2176]{1,0:T(8,128)(2,1)S(1)} %collective-permute-done.7.refs_6_), channel_id=1, source_target_pairs={{0,1},{2,0},{4,2},{6,4},{7,6},{5,7},{3,5},{1,3},{8,9},{10,8},{12,1... | collective-permute-start | bytes 417800 | tf_op jit(solution)/shard_map/ppermute | solution.py:548
  50.4 6.1 %collective-permute-start.20 = (bf16[64,2048]{1,0:T(8,128)(2,1)S(1)}, bf16[64,2048]{1,0:T(8,128)(2,1)S(1)}, u32[]{:S(2)}, u32[]{:S(2)}) collective-permute-start(bf16[64,2048]{1,0:T(8,128)(2,1)S(1)} %get-tuple-element.96), channel_id=1, source_target_pairs={{0,8},{8,0},{16,24},{24,16},{1,9},{9,1},{17,25},{25,17},{2,10},{10... | collective-permute-start | bytes 786440 | tf_op jit(solution)/shard_map/ppermute | solution.py:538
  50.9 6.2 %collective-permute-start.21 = (bf16[64,2048]{1,0:T(8,128)(2,1)S(1)}, bf16[64,2048]{1,0:T(8,128)(2,1)S(1)}, u32[]{:S(2)}, u32[]{:S(2)}) collective-permute-start(bf16[64,2048]{1,0:T(8,128)(2,1)S(1)} %get-tuple-element.95), channel_id=1, source_target_pairs={{0,8},{8,0},{16,24},{24,16},{1,9},{9,1},{17,25},{25,17},{2,10},{10... | collective-permute-start | bytes 786440 | tf_op jit(solution)/shard_map/ppermute | solution.py:538
  51.9 26.0 %collective-permute-start.25 = (bf16[256,2048]{1,0:T(8,128)(2,1)S(1)}, bf16[256,2048]{1,0:T(8,128)(2,1)S(1)}, u32[]{:S(2)}, u32[]{:S(2)}) collective-permute-start(bf16[256,2048]{1,0:T(8,128)(2,1)S(1)} %copy-done.1), channel_id=1, source_target_pairs={{0,16},{8,24},{16,0},{24,8},{1,17},{9,25},{17,1},{25,9},{2,18},{10... | collective-permute-start | bytes 3145736 | tf_op jit(solution)/shard_map/ppermute | solution.py:538
  60.7 17.9 %collective-permute-start.24 = (bf16[256,2048]{1,0:T(8,128)(2,1)S(1)}, bf16[256,2048]{1,0:T(8,128)(2,1)S(1)}, u32[]{:S(2)}, u32[]{:S(2)}) collective-permute-start(bf16[256,2048]{1,0:T(8,128)(2,1)S(1)} %copy-done.1), channel_id=1, source_target_pairs={{0,8},{8,0},{16,24},{24,16},{1,9},{9,1},{17,25},{25,17},{2,10},{10... | collective-permute-start | bytes 3145736 | tf_op jit(solution)/shard_map/ppermute | solution.py:538
  78.1 5.6 %collective-permute-start.26 = (bf16[256,1024]{1,0:T(8,128)(2,1)S(1)}, bf16[256,1024]{1,0:T(8,128)(2,1)S(1)}, u32[]{:S(2)}, u32[]{:S(2)}) collective-permute-start(bf16[256,1024]{1,0:T(8,128)(2,1)S(1)} %get-tuple-element.93), channel_id=1, source_target_pairs={{0,8},{8,0},{16,24},{24,16},{1,9},{9,1},{17,25},{25,17},{2,10},{10... | collective-permute-start | bytes 1572872 | tf_op jit(solution)/shard_map/ppermute | solution.py:538
  80.5 5.7 %collective-permute-start.36 = (bf16[32,1024]{1,0:T(8,128)(2,1)S(1)}, bf16[32,1024]{1,0:T(8,128)(2,1)S(1)}, u32[]{:S(2)}, u32[]{:S(2)}) collective-permute-start(bf16[32,1024]{1,0:T(8,128)(2,1)S(1)} %get-tuple-element.84), channel_id=1, source_target_pairs={{0,2},{2,4},{4,6},{6,7},{7,5},{5,3},{3,1},{1,0},{8,10},{10,12},{12... | collective-permute-start | bytes 196616 | tf_op jit(solution)/shard_map/ppermute | solution.py:548
  86.3 6.3 %collective-permute-start.37 = (bf16[64,1024]{1,0:T(8,128)(2,1)S(1)}, bf16[64,1024]{1,0:T(8,128)(2,1)S(1)}, u32[]{:S(2)}, u32[]{:S(2)}) collective-permute-start(bf16[64,1024]{1,0:T(8,128)(2,1)S(1)} %pad_maximum_fusion.2), channel_id=1, source_target_pairs={{0,2},{2,4},{4,6},{6,7},{7,5},{5,3},{3,1},{1,0},{8,10},{10,12},{12... | collective-permute-start | bytes 393224 | tf_op jit(solution)/shard_map/ppermute | solution.py:548
  88.2 6.4 %collective-permute-start.41 = (bf16[64,1024]{1,0:T(8,128)(2,1)S(1)}, bf16[64,1024]{1,0:T(8,128)(2,1)S(1)}, u32[]{:S(2)}, u32[]{:S(2)}) collective-permute-start(bf16[64,1024]{1,0:T(8,128)(2,1)S(1)} %pad_maximum_fusion.3), channel_id=1, source_target_pairs={{0,1},{2,0},{4,2},{6,4},{7,6},{5,7},{3,5},{1,3},{8,9},{10,8},{12,1... | collective-permute-start | bytes 393224 | tf_op jit(solution)/shard_map/ppermute | solution.py:548
  89.0 6.5 %collective-permute-start.28 = (bf16[64,1024]{1,0:T(8,128)(2,1)S(1)}, bf16[64,1024]{1,0:T(8,128)(2,1)S(1)}, u32[]{:S(2)}, u32[]{:S(2)}) collective-permute-start(bf16[64,1024]{1,0:T(8,128)(2,1)S(1)} %pad_maximum_fusion), channel_id=1, source_target_pairs={{0,2},{2,4},{4,6},{6,7},{7,5},{5,3},{3,1},{1,0},{8,10},{10,12},{12... | collective-permute-start | bytes 393224 | tf_op jit(solution)/shard_map/ppermute | solution.py:548
  91.1 6.4 %collective-permute-start.32 = (bf16[64,1024]{1,0:T(8,128)(2,1)S(1)}, bf16[64,1024]{1,0:T(8,128)(2,1)S(1)}, u32[]{:S(2)}, u32[]{:S(2)}) collective-permute-start(bf16[64,1024]{1,0:T(8,128)(2,1)S(1)} %pad_maximum_fusion.1), channel_id=1, source_target_pairs={{0,1},{2,0},{4,2},{6,4},{7,6},{5,7},{3,5},{1,3},{8,9},{10,8},{12,1... | collective-permute-start | bytes 393224 | tf_op jit(solution)/shard_map/ppermute | solution.py:548
  92.7 5.8 %collective-permute-start.38 = (bf16[64,1024]{1,0:T(8,128)(2,1)S(1)}, bf16[64,1024]{1,0:T(8,128)(2,1)S(1)}, u32[]{:S(2)}, u32[]{:S(2)}) collective-permute-start(bf16[64,1024]{1,0:T(8,128)(2,1)S(1)} %add_convert_fusion.4), channel_id=1, source_target_pairs={{0,2},{2,4},{4,6},{6,7},{7,5},{5,3},{3,1},{1,0},{8,10},{10,12},{12... | collective-permute-start | bytes 393224 | tf_op jit(solution)/shard_map/ppermute | solution.py:548
  94.7 5.6 %collective-permute-start.42 = (bf16[64,1024]{1,0:T(8,128)(2,1)S(1)}, bf16[64,1024]{1,0:T(8,128)(2,1)S(1)}, u32[]{:S(2)}, u32[]{:S(2)}) collective-permute-start(bf16[64,1024]{1,0:T(8,128)(2,1)S(1)} %add_convert_fusion.2), channel_id=1, source_target_pairs={{0,1},{2,0},{4,2},{6,4},{7,6},{5,7},{3,5},{1,3},{8,9},{10,8},{12,1... | collective-permute-start | bytes 393224 | tf_op jit(solution)/shard_map/ppermute | solution.py:548
  95.5 6.3 %collective-permute-start.29 = (bf16[64,1024]{1,0:T(8,128)(2,1)S(1)}, bf16[64,1024]{1,0:T(8,128)(2,1)S(1)}, u32[]{:S(2)}, u32[]{:S(2)}) collective-permute-start(bf16[64,1024]{1,0:T(8,128)(2,1)S(1)} %add_convert_fusion.9), channel_id=1, source_target_pairs={{0,2},{2,4},{4,6},{6,7},{7,5},{5,3},{3,1},{1,0},{8,10},{10,12},{12... | collective-permute-start | bytes 393224 | tf_op jit(solution)/shard_map/ppermute | solution.py:548
  97.5 6.4 %collective-permute-start.33 = (bf16[64,1024]{1,0:T(8,128)(2,1)S(1)}, bf16[64,1024]{1,0:T(8,128)(2,1)S(1)}, u32[]{:S(2)}, u32[]{:S(2)}) collective-permute-start(bf16[64,1024]{1,0:T(8,128)(2,1)S(1)} %add_convert_fusion.7), channel_id=1, source_target_pairs={{0,1},{2,0},{4,2},{6,4},{7,6},{5,7},{3,5},{1,3},{8,9},{10,8},{12,1... | collective-permute-start | bytes 393224 | tf_op jit(solution)/shard_map/ppermute | solution.py:548
  98.5 5.6 %collective-permute-start.39 = (bf16[64,1024]{1,0:T(8,128)(2,1)S(1)}, bf16[64,1024]{1,0:T(8,128)(2,1)S(1)}, u32[]{:S(2)}, u32[]{:S(2)}) collective-permute-start(bf16[64,1024]{1,0:T(8,128)(2,1)S(1)} %add_convert_fusion.3), channel_id=1, source_target_pairs={{0,2},{2,4},{4,6},{6,7},{7,5},{5,3},{3,1},{1,0},{8,10},{10,12},{12... | collective-permute-start | bytes 393224 | tf_op jit(solution)/shard_map/ppermute | solution.py:548
  (21 other events, 245.4 us)

commit v16 on v14

--- a/solution.py
+++ b/solution.py
@@ -127,8 +127,8 @@
 
 
 def attention_kernel(*refs):
-    sources, outs, scratch = refs[:6], refs[6:10], refs[10:]
-    own_ref, beside_ref, sent_ref, rows_ref = outs
+    sources, outs, scratch = refs[:6], refs[6:9], refs[9:]
+    own_ref, beside_ref, sent_ref = outs
     table, lengths, q_ref, k_ref, v_ref, weights, attn, arrived = scratch
     copies = [
         pltpu.make_async_copy(source, target, arrived.at[i])
@@ -187,10 +187,9 @@
     for d, target in enumerate(targets):
         target[...] = attn[pl.ds(pl.multiple_of((own ^ d) * block, block), block), :]
     copies[5].wait()
-    rows_ref[...] = weights[...].astype(jnp.bfloat16)
     for i in range(rows // block):
         here = slice(i * block, (i + 1) * block)
-        sent_ref[:, i * split : (i + 1) * split] = rows_ref[here]
+        sent_ref[:, i * split : (i + 1) * split] = weights[here].astype(jnp.bfloat16)
 
 
 def attention(queries, key_pool, value_pool, page_table, prompt_lengths, gate_up, blocks):
@@ -198,12 +197,12 @@
     split = gate_up.shape[2]
     block = tokens // 4
     shapes = [(block, width)] * 2
-    shapes += [(block, blocks * split + 2 * width), (blocks * block, split)]
+    shapes.append((block, blocks * split + 2 * width))
     return pl.pallas_call(
         attention_kernel,
         out_shape=[jax.ShapeDtypeStruct(shape, jnp.bfloat16) for shape in shapes],
         in_specs=[pl.BlockSpec(memory_space=pltpu.HBM)] * 6,
-        out_specs=vmem(4),
+        out_specs=vmem(3),
         scratch_shapes=[
             pltpu.SMEM(page_table.shape, jnp.int32),
             pltpu.SMEM(prompt_lengths.shape, jnp.int32),
@@ -583,7 +582,7 @@
     slab = width // SLABS
     early = queries.shape[1] // 4 * FIRST_BLOCKS
     side = [i * columns for i in range(FIRST_BLOCKS)]
-    attn_own, attn_beside, first_sent, first_own = attention(
+    attn_own, attn_beside, first_sent = attention(
         queries,
         key_pool,
         value_pool,
@@ -593,9 +592,14 @@
         FIRST_BLOCKS,
     )
     first_across = partner(first_sent, 2)
-    rest_own, down_own = cast_rows(
-        [after(trainer_gate_up, attn_own), trainer_down],
-        [(early, depth - early, 0, columns), (0, down_depth, 0, width)],
+    gate_up = after(trainer_gate_up, attn_own)
+    rest_own, first_own, down_own = cast_rows(
+        [gate_up, gate_up, trainer_down],
+        [
+            (early, depth - early, 0, columns),
+            (0, early, 0, columns),
+            (0, down_depth, 0, width),
+        ],
     )
     attn_beside = partner(attn_beside, 1)
     attn_opposite = partner(first_across[:, -attn_own.shape[1] :], 1)

time: 109 us -> 109 us (level)
  transfers between devices with their start and end apart: 44 -> 44, of which waited for: 22 -> 22; matrix products, arithmetic and copies ran while one was open for 1% -> 1% of each run, Pallas kernels for 14% -> 15%
where the time goes in v16:
time: 109 us
  waiting for transfers between devices  47.5 us (44%)
  starting transfers between devices  39.8 us (37%)
  Pallas kernels  19.7 us (18%)
  other arithmetic  1.29 us (1%)
    ppermute x30, starting transfers between devices, around(): lax.ppermute(x, 'expert', [(ring[i], ring[(i + step) % count]) for i in r...  33.8 us
    ppermute x14, waiting for transfers between devices, partner(): return lax.ppermute(x, 'dp', [(i, i ^ distance) for i in range(4)])  27.6 us
    ppermute x30, waiting for transfers between devices, around(): lax.ppermute(x, 'expert', [(ring[i], ring[(i + step) % count]) for i in r...  19.9 us
    pallas_call x1, Pallas kernels, expert_up(): pl.pallas_call(lambda *refs: up_kernel(len(rows), starts, *refs), out_sha...  8.08 us
    ppermute x14, starting transfers between devices, partner(): return lax.ppermute(x, 'dp', [(i, i ^ distance) for i in range(4)])  6.07 us
    pallas_call x1, Pallas kernels, cast_rows(): pl.pallas_call(lambda *refs: cast_kernel(spans, *refs), out_shape=[jax.Sh...  4.7 us
    pallas_call x1, Pallas kernels, attention(): pl.pallas_call(attention_kernel, out_shape=[jax.ShapeDtypeStruct(shape, j...  3.2 us
  transfers between devices with their start and end apart: 44, of which 22 were waited for; matrix products, arithmetic and copies ran while one was open for 1% of the time, Pallas kernels for 15%

profile of v16, /device:TPU:0, one launch (start us, length us, event | category | flops | bytes accessed | tf_op | source)
XLA Modules:
  0.0 108.9 jit_solution(8843774801651518524)
XLA Ops:
  0.0 3.2 %attention.1 = (bf16[64,512]{1,0:T(8,128)(2,1)}, bf16[64,512]{1,0:T(8,128)(2,1)}, bf16[64,5120]{1,0:T(8,128)(2,1)}) custom-call(s32[1,2]{1,0:T(1,128)} %refs_0_.1, s32[1,4]{1,0:T(1,128)} %refs_1_.1, bf16[1,256,512]{2,1,0:T(8,128)(2,1)} %refs_2_.2, bf16[2,128,512]{2,1,0:T(8,128)(2,1)} %refs_3_.1, bf16[2,128,512]{2,1,0:T(8,128)(2,1)} %refs_4_.1, ...), custom_call_target="tpu_custom_call" | custom-call | tf_op jit(solution)/shard_map/attention/pallas_call | solution.py:201
  3.2 3.0 %collective-permute-start.1 = (bf16[64,5120]{1,0:T(8,128)(2,1)}, bf16[64,5120]{1,0:T(8,128)(2,1)S(1)}, u32[]{:S(2)}, u32[]{:S(2)}) collective-permute-start(bf16[64,5120]{1,0:T(8,128)(2,1)} %get-tuple-element.49), channel_id=1, source_target_pairs={{0,16},{8,24},{16,0},{24,8},{1,17},{9,25},{17,1},{25,9},{2,18},{10... | collective-permute-start | bytes 1966088 | tf_op jit(solution)/shard_map/ppermute | solution.py:514
  6.3 4.7 %cast_rows.1 = (bf16[384,2048]{1,0:T(8,128)(2,1)}, bf16[128,2048]{1,0:T(8,128)(2,1)}, bf16[256,2048]{1,0:T(8,128)(2,1)}) custom-call(f32[1,512,2048]{2,1,0:T(8,128)} %refs_1_.2, f32[1,512,2048]{2,1,0:T(8,128)} %refs_1_.2, f32[1,256,2048]{2,1,0:T(8,128)} %refs_2_.3), custom_call_target="tpu_custom_call" | custom-call | tf_op jit(solution)/shard_map/cast_rows/pallas_call | solution.py:327
  11.1 10.9 %collective-permute-done.1.refs_2_.refs_20_.refs_21_ = bf16[64,5120]{1,0:T(8,128)(2,1)S(1)} collective-permute-done((bf16[64,5120]{1,0:T(8,128)(2,1)}, bf16[64,5120]{1,0:T(8,128)(2,1)S(1)}, u32[]{:S(2)}, u32[]{:S(2)}) %collective-permute-start.1) | collective-permute-done | bytes 655392 | tf_op jit(solution)/shard_map/ppermute | solution.py:514
  22.0 1.2 %collective-permute-done.2.refs_3_ = bf16[64,512]{1,0:T(8,128)(2,1)S(1)} collective-permute-done((bf16[64,512]{1,0:T(8,128)(2,1)S(1)}, bf16[64,512]{1,0:T(8,128)(2,1)S(1)}, u32[]{:S(2)}, u32[]{:S(2)}) %collective-permute-start.2) | collective-permute-done | bytes 65568 | tf_op jit(solution)/shard_map/ppermute | solution.py:514
  23.9 2.2 %collective-permute-start.10 = (bf16[32,2176]{1,0:T(8,128)(2,1)S(1)}, bf16[32,2176]{1,0:T(8,128)(2,1)S(1)}, u32[]{:S(2)}, u32[]{:S(2)}) collective-permute-start(bf16[32,2176]{1,0:T(8,128)(2,1)S(1)} %get-tuple-element.55.refs_1_), channel_id=1, source_target_pairs={{0,2},{2,4},{4,6},{6,7},{7,5},{5,3},{3,1},{1,0},{8,10},{10,12},{12... | collective-permute-start | bytes 417800 | tf_op jit(solution)/shard_map/ppermute | solution.py:524
  26.1 2.0 %collective-permute-start.14 = (bf16[32,2176]{1,0:T(8,128)(2,1)S(1)}, bf16[32,2176]{1,0:T(8,128)(2,1)S(1)}, u32[]{:S(2)}, u32[]{:S(2)}) collective-permute-start(bf16[32,2176]{1,0:T(8,128)(2,1)S(1)} %get-tuple-element.54.refs_0_), channel_id=1, source_target_pairs={{0,2},{2,4},{4,6},{6,7},{7,5},{5,3},{3,1},{1,0},{8,10},{10,12},{12... | collective-permute-start | bytes 417800 | tf_op jit(solution)/shard_map/ppermute | solution.py:524
  28.2 2.4 %collective-permute-done.10.refs_15_ = bf16[32,2176]{1,0:T(8,128)(2,1)S(1)} collective-permute-done((bf16[32,2176]{1,0:T(8,128)(2,1)S(1)}, bf16[32,2176]{1,0:T(8,128)(2,1)S(1)}, u32[]{:S(2)}, u32[]{:S(2)}) %collective-permute-start.10) | collective-permute-done | bytes 139296 | tf_op jit(solution)/shard_map/ppermute | solution.py:524
  30.5 2.1 %collective-permute-start.11 = (bf16[32,2176]{1,0:T(8,128)(2,1)S(1)}, bf16[32,2176]{1,0:T(8,128)(2,1)S(1)}, u32[]{:S(2)}, u32[]{:S(2)}) collective-permute-start(bf16[32,2176]{1,0:T(8,128)(2,1)S(1)} %collective-permute-done.10.refs_15_), channel_id=1, source_target_pairs={{0,2},{2,4},{4,6},{6,7},{7,5},{5,3},{3,1},{1,0},{8,10},{10,12},{12... | collective-permute-start | bytes 417800 | tf_op jit(solution)/shard_map/ppermute | solution.py:524
  33.5 2.1 %collective-permute-start.15 = (bf16[32,2176]{1,0:T(8,128)(2,1)S(1)}, bf16[32,2176]{1,0:T(8,128)(2,1)S(1)}, u32[]{:S(2)}, u32[]{:S(2)}) collective-permute-start(bf16[32,2176]{1,0:T(8,128)(2,1)S(1)} %collective-permute-done.14.refs_14_), channel_id=1, source_target_pairs={{0,2},{2,4},{4,6},{6,7},{7,5},{5,3},{3,1},{1,0},{8,10},{10,12},{12... | collective-permute-start | bytes 417800 | tf_op jit(solution)/shard_map/ppermute | solution.py:524
  36.8 2.2 %collective-permute-start.12 = (bf16[32,2176]{1,0:T(8,128)(2,1)S(1)}, bf16[32,2176]{1,0:T(8,128)(2,1)S(1)}, u32[]{:S(2)}, u32[]{:S(2)}) collective-permute-start(bf16[32,2176]{1,0:T(8,128)(2,1)S(1)} %collective-permute-done.11.refs_13_), channel_id=1, source_target_pairs={{0,2},{2,4},{4,6},{6,7},{7,5},{5,3},{3,1},{1,0},{8,10},{10,12},{12... | collective-permute-start | bytes 417800 | tf_op jit(solution)/shard_map/ppermute | solution.py:524
  40.2 2.1 %collective-permute-start.16 = (bf16[32,2176]{1,0:T(8,128)(2,1)S(1)}, bf16[32,2176]{1,0:T(8,128)(2,1)S(1)}, u32[]{:S(2)}, u32[]{:S(2)}) collective-permute-start(bf16[32,2176]{1,0:T(8,128)(2,1)S(1)} %collective-permute-done.15.refs_12_), channel_id=1, source_target_pairs={{0,2},{2,4},{4,6},{6,7},{7,5},{5,3},{3,1},{1,0},{8,10},{10,12},{12... | collective-permute-start | bytes 417800 | tf_op jit(solution)/shard_map/ppermute | solution.py:524
  43.4 1.8 %collective-permute-start.8 = (bf16[32,2176]{1,0:T(8,128)(2,1)S(1)}, bf16[32,2176]{1,0:T(8,128)(2,1)S(1)}, u32[]{:S(2)}, u32[]{:S(2)}) collective-permute-start(bf16[32,2176]{1,0:T(8,128)(2,1)S(1)} %collective-permute-done.6.refs_5_), channel_id=1, source_target_pairs={{0,1},{2,0},{4,2},{6,4},{7,6},{5,7},{3,5},{1,3},{8,9},{10,8},{12,1... | collective-permute-start | bytes 417800 | tf_op jit(solution)/shard_map/ppermute | solution.py:524
  45.6 1.8 %collective-permute-start.9 = (bf16[32,2176]{1,0:T(8,128)(2,1)S(1)}, bf16[32,2176]{1,0:T(8,128)(2,1)S(1)}, u32[]{:S(2)}, u32[]{:S(2)}) collective-permute-start(bf16[32,2176]{1,0:T(8,128)(2,1)S(1)} %collective-permute-done.7.refs_6_), channel_id=1, source_target_pairs={{0,1},{2,0},{4,2},{6,4},{7,6},{5,7},{3,5},{1,3},{8,9},{10,8},{12,1... | collective-permute-start | bytes 417800 | tf_op jit(solution)/shard_map/ppermute | solution.py:524
  47.4 2.4 %collective-permute-done.8.refs_7_ = bf16[32,2176]{1,0:T(8,128)(2,1)S(1)} collective-permute-done((bf16[32,2176]{1,0:T(8,128)(2,1)S(1)}, bf16[32,2176]{1,0:T(8,128)(2,1)S(1)}, u32[]{:S(2)}, u32[]{:S(2)}) %collective-permute-start.8) | collective-permute-done | bytes 139296 | tf_op jit(solution)/shard_map/ppermute | solution.py:524
  51.3 1.5 %collective-permute-start.25 = (bf16[256,2048]{1,0:T(8,128)(2,1)S(1)}, bf16[256,2048]{1,0:T(8,128)(2,1)S(1)}, u32[]{:S(2)}, u32[]{:S(2)}) collective-permute-start(bf16[256,2048]{1,0:T(8,128)(2,1)S(1)} %copy-done.1), channel_id=1, source_target_pairs={{0,16},{8,24},{16,0},{24,8},{1,17},{9,25},{17,1},{25,9},{2,18},{10... | collective-permute-start | bytes 3145736 | tf_op jit(solution)/shard_map/ppermute | solution.py:514
  52.8 2.9 %collective-permute-done.19.refs_22_ = bf16[384,2048]{1,0:T(8,128)(2,1)S(1)} collective-permute-done((bf16[384,2048]{1,0:T(8,128)(2,1)}, bf16[384,2048]{1,0:T(8,128)(2,1)S(1)}, u32[]{:S(2)}, u32[]{:S(2)}) %collective-permute-start.19) | collective-permute-done | bytes 1572896 | tf_op jit(solution)/shard_map/ppermute | solution.py:514
  56.5 3.6 %collective-permute-done.17.refs_18_ = bf16[128,2048]{1,0:T(8,128)(2,1)S(1)} collective-permute-done((bf16[128,2048]{1,0:T(8,128)(2,1)S(1)}, bf16[128,2048]{1,0:T(8,128)(2,1)S(1)}, u32[]{:S(2)}, u32[]{:S(2)}) %collective-permute-start.17) | collective-permute-done | bytes 524320 | tf_op jit(solution)/shard_map/ppermute | solution.py:514
  60.3 8.1 %expert_up.1 = (bf16[512,1024]{1,0:T(8,128)(2,1)S(1)}, f32[512,1]{1,0:T(8,128)S(1)}) custom-call(bf16[32,2176]{1,0:T(8,128)(2,1)S(1)} %get-tuple-element.54.refs_0_, bf16[32,2176]{1,0:T(8,128)(2,1)S(1)} %get-tuple-element.55.refs_1_, bf16[32,2176]{1,0:T(8,128)(2,1)S(1)} %collective-permute-done.3.refs_2_, ...), custom_call_target="tpu_custom_call" | custom-call | flops 1 | bytes 1 | tf_op jit(solution)/shard_map/expert_up/pallas_call | solution.py:406
  68.3 9.0 %collective-permute-done.25.refs_2_ = bf16[256,2048]{1,0:T(8,128)(2,1)S(1)} collective-permute-done((bf16[256,2048]{1,0:T(8,128)(2,1)S(1)}, bf16[256,2048]{1,0:T(8,128)(2,1)S(1)}, u32[]{:S(2)}, u32[]{:S(2)}) %collective-permute-start.25) | collective-permute-done | bytes 1048608 | tf_op jit(solution)/shard_map/ppermute | solution.py:514
  78.0 2.0 %down_part.1.refs_1_ = f32[512,2048]{1,0:T(8,128)S(1)} custom-call(bf16[512,1024]{1,0:T(8,128)(2,1)S(1)} %get-tuple-element.61.hidden_ref.refs_0_, bf16[256,2048]{1,0:T(8,128)(2,1)S(1)} %copy-done.1, bf16[256,2048]{1,0:T(8,128)(2,1)S(1)} %collective-permute-done.24.refs_1_, bf16[256,2048]{1,0:T(8,128)(2,1)S(1)} %collective-permute-done.25.refs_2_), custom_call_target="tpu_custom_call" | custom-call | flops 1 | bytes 1 | tf_op jit(solution)/shard_map/down_part/pallas_call | solution.py:451
  80.6 1.9 %collective-permute-start.36 = (bf16[32,1024]{1,0:T(8,128)(2,1)S(1)}, bf16[32,1024]{1,0:T(8,128)(2,1)S(1)}, u32[]{:S(2)}, u32[]{:S(2)}) collective-permute-start(bf16[32,1024]{1,0:T(8,128)(2,1)S(1)} %get-tuple-element.82), channel_id=1, source_target_pairs={{0,2},{2,4},{4,6},{6,7},{7,5},{5,3},{3,1},{1,0},{8,10},{10,12},{12... | collective-permute-start | bytes 196616 | tf_op jit(solution)/shard_map/ppermute | solution.py:524
  83.2 1.9 %collective-permute-start.27 = (bf16[32,1024]{1,0:T(8,128)(2,1)S(1)}, bf16[32,1024]{1,0:T(8,128)(2,1)S(1)}, u32[]{:S(2)}, u32[]{:S(2)}) collective-permute-start(bf16[32,1024]{1,0:T(8,128)(2,1)S(1)} %get-tuple-element.71), channel_id=1, source_target_pairs={{0,2},{2,4},{4,6},{6,7},{7,5},{5,3},{3,1},{1,0},{8,10},{10,12},{12... | collective-permute-start | bytes 196616 | tf_op jit(solution)/shard_map/ppermute | solution.py:524
  85.3 1.9 %collective-permute-start.37 = (bf16[64,1024]{1,0:T(8,128)(2,1)S(1)}, bf16[64,1024]{1,0:T(8,128)(2,1)S(1)}, u32[]{:S(2)}, u32[]{:S(2)}) collective-permute-start(bf16[64,1024]{1,0:T(8,128)(2,1)S(1)} %pad_maximum_fusion.2), channel_id=1, source_target_pairs={{0,2},{2,4},{4,6},{6,7},{7,5},{5,3},{3,1},{1,0},{8,10},{10,12},{12... | collective-permute-start | bytes 393224 | tf_op jit(solution)/shard_map/ppermute | solution.py:524
  88.0 2.0 %collective-permute-start.28 = (bf16[64,1024]{1,0:T(8,128)(2,1)S(1)}, bf16[64,1024]{1,0:T(8,128)(2,1)S(1)}, u32[]{:S(2)}, u32[]{:S(2)}) collective-permute-start(bf16[64,1024]{1,0:T(8,128)(2,1)S(1)} %pad_maximum_fusion), channel_id=1, source_target_pairs={{0,2},{2,4},{4,6},{6,7},{7,5},{5,3},{3,1},{1,0},{8,10},{10,12},{12... | collective-permute-start | bytes 393224 | tf_op jit(solution)/shard_map/ppermute | solution.py:524
  90.1 1.4 %collective-permute-done.37 = bf16[64,1024]{1,0:T(8,128)(2,1)S(1)} collective-permute-done((bf16[64,1024]{1,0:T(8,128)(2,1)S(1)}, bf16[64,1024]{1,0:T(8,128)(2,1)S(1)}, u32[]{:S(2)}, u32[]{:S(2)}) %collective-permute-start.37) | collective-permute-done | bytes 131104 | tf_op jit(solution)/shard_map/ppermute | solution.py:524
  91.6 2.0 %collective-permute-start.38 = (bf16[64,1024]{1,0:T(8,128)(2,1)S(1)}, bf16[64,1024]{1,0:T(8,128)(2,1)S(1)}, u32[]{:S(2)}, u32[]{:S(2)}) collective-permute-start(bf16[64,1024]{1,0:T(8,128)(2,1)S(1)} %add_convert_fusion.4), channel_id=1, source_target_pairs={{0,2},{2,4},{4,6},{6,7},{7,5},{5,3},{3,1},{1,0},{8,10},{10,12},{12... | collective-permute-start | bytes 393224 | tf_op jit(solution)/shard_map/ppermute | solution.py:524
  94.5 2.0 %collective-permute-start.29 = (bf16[64,1024]{1,0:T(8,128)(2,1)S(1)}, bf16[64,1024]{1,0:T(8,128)(2,1)S(1)}, u32[]{:S(2)}, u32[]{:S(2)}) collective-permute-start(bf16[64,1024]{1,0:T(8,128)(2,1)S(1)} %add_convert_fusion.9), channel_id=1, source_target_pairs={{0,2},{2,4},{4,6},{6,7},{7,5},{5,3},{3,1},{1,0},{8,10},{10,12},{12... | collective-permute-start | bytes 393224 | tf_op jit(solution)/shard_map/ppermute | solution.py:524
  97.5 1.8 %collective-permute-start.39 = (bf16[64,1024]{1,0:T(8,128)(2,1)S(1)}, bf16[64,1024]{1,0:T(8,128)(2,1)S(1)}, u32[]{:S(2)}, u32[]{:S(2)}) collective-permute-start(bf16[64,1024]{1,0:T(8,128)(2,1)S(1)} %add_convert_fusion.3), channel_id=1, source_target_pairs={{0,2},{2,4},{4,6},{6,7},{7,5},{5,3},{3,1},{1,0},{8,10},{10,12},{12... | collective-permute-start | bytes 393224 | tf_op jit(solution)/shard_map/ppermute | solution.py:524
  100.8 2.1 %collective-permute-start.30 = (bf16[64,1024]{1,0:T(8,128)(2,1)S(1)}, bf16[64,1024]{1,0:T(8,128)(2,1)S(1)}, u32[]{:S(2)}, u32[]{:S(2)}) collective-permute-start(bf16[64,1024]{1,0:T(8,128)(2,1)S(1)} %add_convert_fusion.8), channel_id=1, source_target_pairs={{0,2},{2,4},{4,6},{6,7},{7,5},{5,3},{3,1},{1,0},{8,10},{10,12},{12... | collective-permute-start | bytes 393224 | tf_op jit(solution)/shard_map/ppermute | solution.py:524
  103.1 1.6 %collective-permute-done.43 = bf16[64,1024]{1,0:T(8,128)(2,1)S(1)} collective-permute-done((bf16[64,1024]{1,0:T(8,128)(2,1)S(1)}, bf16[64,1024]{1,0:T(8,128)(2,1)S(1)}, u32[]{:S(2)}, u32[]{:S(2)}) %collective-permute-start.43) | collective-permute-done | bytes 131104 | tf_op jit(solution)/shard_map/ppermute | solution.py:524
  105.9 2.2 %collective-permute-done.34 = bf16[64,1024]{1,0:T(8,128)(2,1)S(1)} collective-permute-done((bf16[64,1024]{1,0:T(8,128)(2,1)S(1)}, bf16[64,1024]{1,0:T(8,128)(2,1)S(1)}, u32[]{:S(2)}, u32[]{:S(2)}) %collective-permute-start.34) | collective-permute-done | bytes 131104 | tf_op jit(solution)/shard_map/ppermute | solution.py:524
  (103 shorter events, 16.8 us)
Async XLA Ops:
  3.2 18.8 %collective-permute-start.1 = (bf16[64,5120]{1,0:T(8,128)(2,1)}, bf16[64,5120]{1,0:T(8,128)(2,1)S(1)}, u32[]{:S(2)}, u32[]{:S(2)}) collective-permute-start(bf16[64,5120]{1,0:T(8,128)(2,1)} %get-tuple-element.49), channel_id=1, source_target_pairs={{0,16},{8,24},{16,0},{24,8},{1,17},{9,25},{17,1},{25,9},{2,18},{10... | collective-permute-start | bytes 1966088 | tf_op jit(solution)/shard_map/ppermute | solution.py:514
  11.0 44.7 %collective-permute-start.19 = (bf16[384,2048]{1,0:T(8,128)(2,1)}, bf16[384,2048]{1,0:T(8,128)(2,1)S(1)}, u32[]{:S(2)}, u32[]{:S(2)}) collective-permute-start(bf16[384,2048]{1,0:T(8,128)(2,1)} %get-tuple-element.58.refs_17_), channel_id=1, source_target_pairs={{0,16},{8,24},{16,0},{24,8},{1,17},{9,25},{17,1},{25,9},{2,18},{10... | collective-permute-start | bytes 4718600 | tf_op jit(solution)/shard_map/ppermute | solution.py:514
  11.1 10.9 %collective-permute-start = (bf16[64,512]{1,0:T(8,128)(2,1)S(1)}, bf16[64,512]{1,0:T(8,128)(2,1)S(1)}, u32[]{:S(2)}, u32[]{:S(2)}) collective-permute-start(bf16[64,512]{1,0:T(8,128)(2,1)S(1)} %copy-done.8), channel_id=1, source_target_pairs={{0,8},{8,0},{16,24},{24,16},{1,9},{9,1},{17,25},{25,17},{2,10},{10... | collective-permute-start | bytes 196616 | tf_op jit(solution)/shard_map/ppermute | solution.py:514
  23.9 6.6 %collective-permute-start.10 = (bf16[32,2176]{1,0:T(8,128)(2,1)S(1)}, bf16[32,2176]{1,0:T(8,128)(2,1)S(1)}, u32[]{:S(2)}, u32[]{:S(2)}) collective-permute-start(bf16[32,2176]{1,0:T(8,128)(2,1)S(1)} %get-tuple-element.55.refs_1_), channel_id=1, source_target_pairs={{0,2},{2,4},{4,6},{6,7},{7,5},{5,3},{3,1},{1,0},{8,10},{10,12},{12... | collective-permute-start | bytes 417800 | tf_op jit(solution)/shard_map/ppermute | solution.py:524
  26.1 6.6 %collective-permute-start.3 = (bf16[32,2176]{1,0:T(8,128)(2,1)S(1)}, bf16[32,2176]{1,0:T(8,128)(2,1)S(1)}, u32[]{:S(2)}, u32[]{:S(2)}) collective-permute-start(bf16[32,2176]{1,0:T(8,128)(2,1)S(1)} %get-tuple-element.54.refs_0_), channel_id=1, source_target_pairs={{0,1},{2,0},{4,2},{6,4},{7,6},{5,7},{3,5},{1,3},{8,9},{10,8},{12,1... | collective-permute-start | bytes 417800 | tf_op jit(solution)/shard_map/ppermute | solution.py:524
  26.1 7.4 %collective-permute-start.14 = (bf16[32,2176]{1,0:T(8,128)(2,1)S(1)}, bf16[32,2176]{1,0:T(8,128)(2,1)S(1)}, u32[]{:S(2)}, u32[]{:S(2)}) collective-permute-start(bf16[32,2176]{1,0:T(8,128)(2,1)S(1)} %get-tuple-element.54.refs_0_), channel_id=1, source_target_pairs={{0,2},{2,4},{4,6},{6,7},{7,5},{5,3},{3,1},{1,0},{8,10},{10,12},{12... | collective-permute-start | bytes 417800 | tf_op jit(solution)/shard_map/ppermute | solution.py:524
  28.1 7.5 %collective-permute-start.4 = (bf16[32,2176]{1,0:T(8,128)(2,1)S(1)}, bf16[32,2176]{1,0:T(8,128)(2,1)S(1)}, u32[]{:S(2)}, u32[]{:S(2)}) collective-permute-start(bf16[32,2176]{1,0:T(8,128)(2,1)S(1)} %get-tuple-element.55.refs_1_), channel_id=1, source_target_pairs={{0,1},{2,0},{4,2},{6,4},{7,6},{5,7},{3,5},{1,3},{8,9},{10,8},{12,1... | collective-permute-start | bytes 417800 | tf_op jit(solution)/shard_map/ppermute | solution.py:524
  30.5 6.2 %collective-permute-start.11 = (bf16[32,2176]{1,0:T(8,128)(2,1)S(1)}, bf16[32,2176]{1,0:T(8,128)(2,1)S(1)}, u32[]{:S(2)}, u32[]{:S(2)}) collective-permute-start(bf16[32,2176]{1,0:T(8,128)(2,1)S(1)} %collective-permute-done.10.refs_15_), channel_id=1, source_target_pairs={{0,2},{2,4},{4,6},{6,7},{7,5},{5,3},{3,1},{1,0},{8,10},{10,12},{12... | collective-permute-start | bytes 417800 | tf_op jit(solution)/shard_map/ppermute | solution.py:524
  32.7 6.3 %collective-permute-start.5 = (bf16[32,2176]{1,0:T(8,128)(2,1)S(1)}, bf16[32,2176]{1,0:T(8,128)(2,1)S(1)}, u32[]{:S(2)}, u32[]{:S(2)}) collective-permute-start(bf16[32,2176]{1,0:T(8,128)(2,1)S(1)} %collective-permute-done.3.refs_2_), channel_id=1, source_target_pairs={{0,1},{2,0},{4,2},{6,4},{7,6},{5,7},{3,5},{1,3},{8,9},{10,8},{12,1... | collective-permute-start | bytes 417800 | tf_op jit(solution)/shard_map/ppermute | solution.py:524
  33.5 6.6 %collective-permute-start.15 = (bf16[32,2176]{1,0:T(8,128)(2,1)S(1)}, bf16[32,2176]{1,0:T(8,128)(2,1)S(1)}, u32[]{:S(2)}, u32[]{:S(2)}) collective-permute-start(bf16[32,2176]{1,0:T(8,128)(2,1)S(1)} %collective-permute-done.14.refs_14_), channel_id=1, source_target_pairs={{0,2},{2,4},{4,6},{6,7},{7,5},{5,3},{3,1},{1,0},{8,10},{10,12},{12... | collective-permute-start | bytes 417800 | tf_op jit(solution)/shard_map/ppermute | solution.py:524
  35.6 6.6 %collective-permute-start.6 = (bf16[32,2176]{1,0:T(8,128)(2,1)S(1)}, bf16[32,2176]{1,0:T(8,128)(2,1)S(1)}, u32[]{:S(2)}, u32[]{:S(2)}) collective-permute-start(bf16[32,2176]{1,0:T(8,128)(2,1)S(1)} %collective-permute-done.4.refs_3_), channel_id=1, source_target_pairs={{0,1},{2,0},{4,2},{6,4},{7,6},{5,7},{3,5},{1,3},{8,9},{10,8},{12,1... | collective-permute-start | bytes 417800 | tf_op jit(solution)/shard_map/ppermute | solution.py:524
  36.8 6.7 %collective-permute-start.12 = (bf16[32,2176]{1,0:T(8,128)(2,1)S(1)}, bf16[32,2176]{1,0:T(8,128)(2,1)S(1)}, u32[]{:S(2)}, u32[]{:S(2)}) collective-permute-start(bf16[32,2176]{1,0:T(8,128)(2,1)S(1)} %collective-permute-done.11.refs_13_), channel_id=1, source_target_pairs={{0,2},{2,4},{4,6},{6,7},{7,5},{5,3},{3,1},{1,0},{8,10},{10,12},{12... | collective-permute-start | bytes 417800 | tf_op jit(solution)/shard_map/ppermute | solution.py:524
  39.0 6.2 %collective-permute-start.7 = (bf16[32,2176]{1,0:T(8,128)(2,1)S(1)}, bf16[32,2176]{1,0:T(8,128)(2,1)S(1)}, u32[]{:S(2)}, u32[]{:S(2)}) collective-permute-start(bf16[32,2176]{1,0:T(8,128)(2,1)S(1)} %collective-permute-done.5.refs_4_), channel_id=1, source_target_pairs={{0,1},{2,0},{4,2},{6,4},{7,6},{5,7},{3,5},{1,3},{8,9},{10,8},{12,1... | collective-permute-start | bytes 417800 | tf_op jit(solution)/shard_map/ppermute | solution.py:524
  40.2 5.5 %collective-permute-start.16 = (bf16[32,2176]{1,0:T(8,128)(2,1)S(1)}, bf16[32,2176]{1,0:T(8,128)(2,1)S(1)}, u32[]{:S(2)}, u32[]{:S(2)}) collective-permute-start(bf16[32,2176]{1,0:T(8,128)(2,1)S(1)} %collective-permute-done.15.refs_12_), channel_id=1, source_target_pairs={{0,2},{2,4},{4,6},{6,7},{7,5},{5,3},{3,1},{1,0},{8,10},{10,12},{12... | collective-permute-start | bytes 417800 | tf_op jit(solution)/shard_map/ppermute | solution.py:524
  42.2 18.0 %collective-permute-start.18 = (bf16[384,2048]{1,0:T(8,128)(2,1)}, bf16[384,2048]{1,0:T(8,128)(2,1)S(1)}, u32[]{:S(2)}, u32[]{:S(2)}) collective-permute-start(bf16[384,2048]{1,0:T(8,128)(2,1)} %get-tuple-element.58.refs_17_), channel_id=1, source_target_pairs={{0,8},{8,0},{16,24},{24,16},{1,9},{9,1},{17,25},{25,17},{2,10},{10... | collective-permute-start | bytes 4718600 | tf_op jit(solution)/shard_map/ppermute | solution.py:514
  43.4 6.4 %collective-permute-start.8 = (bf16[32,2176]{1,0:T(8,128)(2,1)S(1)}, bf16[32,2176]{1,0:T(8,128)(2,1)S(1)}, u32[]{:S(2)}, u32[]{:S(2)}) collective-permute-start(bf16[32,2176]{1,0:T(8,128)(2,1)S(1)} %collective-permute-done.6.refs_5_), channel_id=1, source_target_pairs={{0,1},{2,0},{4,2},{6,4},{7,6},{5,7},{3,5},{1,3},{8,9},{10,8},{12,1... | collective-permute-start | bytes 417800 | tf_op jit(solution)/shard_map/ppermute | solution.py:524
  45.6 5.7 %collective-permute-start.9 = (bf16[32,2176]{1,0:T(8,128)(2,1)S(1)}, bf16[32,2176]{1,0:T(8,128)(2,1)S(1)}, u32[]{:S(2)}, u32[]{:S(2)}) collective-permute-start(bf16[32,2176]{1,0:T(8,128)(2,1)S(1)} %collective-permute-done.7.refs_6_), channel_id=1, source_target_pairs={{0,1},{2,0},{4,2},{6,4},{7,6},{5,7},{3,5},{1,3},{8,9},{10,8},{12,1... | collective-permute-start | bytes 417800 | tf_op jit(solution)/shard_map/ppermute | solution.py:524
  49.8 6.1 %collective-permute-start.20 = (bf16[64,2048]{1,0:T(8,128)(2,1)S(1)}, bf16[64,2048]{1,0:T(8,128)(2,1)S(1)}, u32[]{:S(2)}, u32[]{:S(2)}) collective-permute-start(bf16[64,2048]{1,0:T(8,128)(2,1)S(1)} %get-tuple-element.94), channel_id=1, source_target_pairs={{0,8},{8,0},{16,24},{24,16},{1,9},{9,1},{17,25},{25,17},{2,10},{10... | collective-permute-start | bytes 786440 | tf_op jit(solution)/shard_map/ppermute | solution.py:514
  50.3 6.2 %collective-permute-start.21 = (bf16[64,2048]{1,0:T(8,128)(2,1)S(1)}, bf16[64,2048]{1,0:T(8,128)(2,1)S(1)}, u32[]{:S(2)}, u32[]{:S(2)}) collective-permute-start(bf16[64,2048]{1,0:T(8,128)(2,1)S(1)} %get-tuple-element.93), channel_id=1, source_target_pairs={{0,8},{8,0},{16,24},{24,16},{1,9},{9,1},{17,25},{25,17},{2,10},{10... | collective-permute-start | bytes 786440 | tf_op jit(solution)/shard_map/ppermute | solution.py:514
  51.3 26.0 %collective-permute-start.25 = (bf16[256,2048]{1,0:T(8,128)(2,1)S(1)}, bf16[256,2048]{1,0:T(8,128)(2,1)S(1)}, u32[]{:S(2)}, u32[]{:S(2)}) collective-permute-start(bf16[256,2048]{1,0:T(8,128)(2,1)S(1)} %copy-done.1), channel_id=1, source_target_pairs={{0,16},{8,24},{16,0},{24,8},{1,17},{9,25},{17,1},{25,9},{2,18},{10... | collective-permute-start | bytes 3145736 | tf_op jit(solution)/shard_map/ppermute | solution.py:514
  60.1 17.9 %collective-permute-start.24 = (bf16[256,2048]{1,0:T(8,128)(2,1)S(1)}, bf16[256,2048]{1,0:T(8,128)(2,1)S(1)}, u32[]{:S(2)}, u32[]{:S(2)}) collective-permute-start(bf16[256,2048]{1,0:T(8,128)(2,1)S(1)} %copy-done.1), channel_id=1, source_target_pairs={{0,8},{8,0},{16,24},{24,16},{1,9},{9,1},{17,25},{25,17},{2,10},{10... | collective-permute-start | bytes 3145736 | tf_op jit(solution)/shard_map/ppermute | solution.py:514
  77.5 5.2 %collective-permute-start.26 = (bf16[256,1024]{1,0:T(8,128)(2,1)S(1)}, bf16[256,1024]{1,0:T(8,128)(2,1)S(1)}, u32[]{:S(2)}, u32[]{:S(2)}) collective-permute-start(bf16[256,1024]{1,0:T(8,128)(2,1)S(1)} %get-tuple-element.91), channel_id=1, source_target_pairs={{0,8},{8,0},{16,24},{24,16},{1,9},{9,1},{17,25},{25,17},{2,10},{10... | collective-permute-start | bytes 1572872 | tf_op jit(solution)/shard_map/ppermute | solution.py:514
  85.3 6.2 %collective-permute-start.37 = (bf16[64,1024]{1,0:T(8,128)(2,1)S(1)}, bf16[64,1024]{1,0:T(8,128)(2,1)S(1)}, u32[]{:S(2)}, u32[]{:S(2)}) collective-permute-start(bf16[64,1024]{1,0:T(8,128)(2,1)S(1)} %pad_maximum_fusion.2), channel_id=1, source_target_pairs={{0,2},{2,4},{4,6},{6,7},{7,5},{5,3},{3,1},{1,0},{8,10},{10,12},{12... | collective-permute-start | bytes 393224 | tf_op jit(solution)/shard_map/ppermute | solution.py:524
  87.2 6.4 %collective-permute-start.41 = (bf16[64,1024]{1,0:T(8,128)(2,1)S(1)}, bf16[64,1024]{1,0:T(8,128)(2,1)S(1)}, u32[]{:S(2)}, u32[]{:S(2)}) collective-permute-start(bf16[64,1024]{1,0:T(8,128)(2,1)S(1)} %pad_maximum_fusion.3), channel_id=1, source_target_pairs={{0,1},{2,0},{4,2},{6,4},{7,6},{5,7},{3,5},{1,3},{8,9},{10,8},{12,1... | collective-permute-start | bytes 393224 | tf_op jit(solution)/shard_map/ppermute | solution.py:524
  88.0 6.5 %collective-permute-start.28 = (bf16[64,1024]{1,0:T(8,128)(2,1)S(1)}, bf16[64,1024]{1,0:T(8,128)(2,1)S(1)}, u32[]{:S(2)}, u32[]{:S(2)}) collective-permute-start(bf16[64,1024]{1,0:T(8,128)(2,1)S(1)} %pad_maximum_fusion), channel_id=1, source_target_pairs={{0,2},{2,4},{4,6},{6,7},{7,5},{5,3},{3,1},{1,0},{8,10},{10,12},{12... | collective-permute-start | bytes 393224 | tf_op jit(solution)/shard_map/ppermute | solution.py:524
  90.0 6.4 %collective-permute-start.32 = (bf16[64,1024]{1,0:T(8,128)(2,1)S(1)}, bf16[64,1024]{1,0:T(8,128)(2,1)S(1)}, u32[]{:S(2)}, u32[]{:S(2)}) collective-permute-start(bf16[64,1024]{1,0:T(8,128)(2,1)S(1)} %pad_maximum_fusion.1), channel_id=1, source_target_pairs={{0,1},{2,0},{4,2},{6,4},{7,6},{5,7},{3,5},{1,3},{8,9},{10,8},{12,1... | collective-permute-start | bytes 393224 | tf_op jit(solution)/shard_map/ppermute | solution.py:524
  91.6 5.9 %collective-permute-start.38 = (bf16[64,1024]{1,0:T(8,128)(2,1)S(1)}, bf16[64,1024]{1,0:T(8,128)(2,1)S(1)}, u32[]{:S(2)}, u32[]{:S(2)}) collective-permute-start(bf16[64,1024]{1,0:T(8,128)(2,1)S(1)} %add_convert_fusion.4), channel_id=1, source_target_pairs={{0,2},{2,4},{4,6},{6,7},{7,5},{5,3},{3,1},{1,0},{8,10},{10,12},{12... | collective-permute-start | bytes 393224 | tf_op jit(solution)/shard_map/ppermute | solution.py:524
  93.6 5.6 %collective-permute-start.42 = (bf16[64,1024]{1,0:T(8,128)(2,1)S(1)}, bf16[64,1024]{1,0:T(8,128)(2,1)S(1)}, u32[]{:S(2)}, u32[]{:S(2)}) collective-permute-start(bf16[64,1024]{1,0:T(8,128)(2,1)S(1)} %add_convert_fusion.2), channel_id=1, source_target_pairs={{0,1},{2,0},{4,2},{6,4},{7,6},{5,7},{3,5},{1,3},{8,9},{10,8},{12,1... | collective-permute-start | bytes 393224 | tf_op jit(solution)/shard_map/ppermute | solution.py:524
  94.5 6.2 %collective-permute-start.29 = (bf16[64,1024]{1,0:T(8,128)(2,1)S(1)}, bf16[64,1024]{1,0:T(8,128)(2,1)S(1)}, u32[]{:S(2)}, u32[]{:S(2)}) collective-permute-start(bf16[64,1024]{1,0:T(8,128)(2,1)S(1)} %add_convert_fusion.9), channel_id=1, source_target_pairs={{0,2},{2,4},{4,6},{6,7},{7,5},{5,3},{3,1},{1,0},{8,10},{10,12},{12... | collective-permute-start | bytes 393224 | tf_op jit(solution)/shard_map/ppermute | solution.py:524
  96.5 6.5 %collective-permute-start.33 = (bf16[64,1024]{1,0:T(8,128)(2,1)S(1)}, bf16[64,1024]{1,0:T(8,128)(2,1)S(1)}, u32[]{:S(2)}, u32[]{:S(2)}) collective-permute-start(bf16[64,1024]{1,0:T(8,128)(2,1)S(1)} %add_convert_fusion.7), channel_id=1, source_target_pairs={{0,1},{2,0},{4,2},{6,4},{7,6},{5,7},{3,5},{1,3},{8,9},{10,8},{12,1... | collective-permute-start | bytes 393224 | tf_op jit(solution)/shard_map/ppermute | solution.py:524
  97.5 5.6 %collective-permute-start.39 = (bf16[64,1024]{1,0:T(8,128)(2,1)S(1)}, bf16[64,1024]{1,0:T(8,128)(2,1)S(1)}, u32[]{:S(2)}, u32[]{:S(2)}) collective-permute-start(bf16[64,1024]{1,0:T(8,128)(2,1)S(1)} %add_convert_fusion.3), channel_id=1, source_target_pairs={{0,2},{2,4},{4,6},{6,7},{7,5},{5,3},{3,1},{1,0},{8,10},{10,12},{12... | collective-permute-start | bytes 393224 | tf_op jit(solution)/shard_map/ppermute | solution.py:524
  99.3 5.4 %collective-permute-start.43 = (bf16[64,1024]{1,0:T(8,128)(2,1)S(1)}, bf16[64,1024]{1,0:T(8,128)(2,1)S(1)}, u32[]{:S(2)}, u32[]{:S(2)}) collective-permute-start(bf16[64,1024]{1,0:T(8,128)(2,1)S(1)} %add_convert_fusion.1), channel_id=1, source_target_pairs={{0,1},{2,0},{4,2},{6,4},{7,6},{5,7},{3,5},{1,3},{8,9},{10,8},{12,1... | collective-permute-start | bytes 393224 | tf_op jit(solution)/shard_map/ppermute | solution.py:524
  (21 other events, 197.0 us)

commit v17 on v16

--- a/solution.py
+++ b/solution.py
@@ -562,6 +562,31 @@
     return [partner(x[i : i + rows], 1) for i in range(0, x.shape[0], rows)]
 
 
+def mix_kernel(resid_ref, *refs):
+    terms, out_ref = refs[:-1], refs[-1]
+    first = 0
+    for i in range(0, len(terms), 3):
+        columns = slice(first, first + terms[i].shape[1])
+        total = resid_ref[:, columns].astype(jnp.float32)
+        for ref in terms[i : i + 3]:
+            total += ref[...].astype(jnp.float32)
+        out_ref[0, :, columns] = total.astype(jnp.bfloat16)
+        first = columns.stop
+
+
+def mix(resid, halves):
+    terms = [term for half in halves for term in half]
+    return pl.pallas_call(
+        mix_kernel,
+        out_shape=jax.ShapeDtypeStruct((1, *resid.shape), jnp.bfloat16),
+        in_specs=vmem(1 + len(terms)),
+        out_specs=pl.BlockSpec(memory_space=pltpu.VMEM),
+        compiler_params=params(),
+        cost_estimate=SMALL,
+        name="mix",
+    )(resid, *terms)
+
+
 def every_expert(
     hidden_in,
     queries,
@@ -632,11 +657,8 @@
     for first in range(0, width, slab):
         opposite = partner(down_ready[:, first : first + slab], 1)
         weighted = expert_down(hidden_units, total, gates, opposite, first, expert_count)
-        sum_here = resid[:, first : first + slab].astype(jnp.float32)
-        for term in scatter_sum(*weighted):
-            sum_here = sum_here + term.astype(jnp.float32)
-        mixed.append(sum_here.astype(jnp.bfloat16))
-    return jnp.concatenate(mixed, axis=1)[None]
+        mixed.append(scatter_sum(*weighted))
+    return mix(resid, mixed)
 
 
 def solution(mesh):

time: 109 us -> 109 us (level)
    ppermute x14, waiting for transfers between devices: 27.6 us -> 25.5 us  [partner(): return lax.ppermute(x, 'dp', [(i, i ^ distance) for i in range(4)])]
    ppermute x30, waiting for transfers between devices: 19.9 us -> 21.1 us  [around(): lax.ppermute(x, 'expert', [(ring[i], ring[(i + step) % count]) for i in r...]
  transfers between devices with their start and end apart: 44 -> 44, of which waited for: 22 -> 23; matrix products, arithmetic and copies ran while one was open for 1% -> 1% of each run, Pallas kernels for 15% -> 15%
where the time goes in v17:
time: 109 us
  waiting for transfers between devices  46.6 us (43%)
  starting transfers between devices  40.8 us (37%)
  Pallas kernels  20.5 us (19%)
    ppermute x30, starting transfers between devices, around(): lax.ppermute(x, 'expert', [(ring[i], ring[(i + step) % count]) for i in r...  34.2 us
    ppermute x14, waiting for transfers between devices, partner(): return lax.ppermute(x, 'dp', [(i, i ^ distance) for i in range(4)])  25.5 us
    ppermute x30, waiting for transfers between devices, around(): lax.ppermute(x, 'expert', [(ring[i], ring[(i + step) % count]) for i in r...  21.1 us
    pallas_call x1, Pallas kernels, expert_up(): pl.pallas_call(lambda *refs: up_kernel(len(rows), starts, *refs), out_sha...  8.08 us
    ppermute x14, starting transfers between devices, partner(): return lax.ppermute(x, 'dp', [(i, i ^ distance) for i in range(4)])  6.51 us
    pallas_call x1, Pallas kernels, cast_rows(): pl.pallas_call(lambda *refs: cast_kernel(spans, *refs), out_shape=[jax.Sh...  4.68 us
    pallas_call x1, Pallas kernels, attention(): pl.pallas_call(attention_kernel, out_shape=[jax.ShapeDtypeStruct(shape, j...  3.2 us
  transfers between devices with their start and end apart: 44, of which 23 were waited for; matrix products, arithmetic and copies ran while one was open for 1% of the time, Pallas kernels for 15%

profile of v17, /device:TPU:0, one launch (start us, length us, event | category | flops | bytes accessed | tf_op | source)
XLA Modules:
  0.0 108.8 jit_solution(10653890903337704484)
XLA Ops:
  0.0 3.2 %attention.1 = (bf16[64,512]{1,0:T(8,128)(2,1)}, bf16[64,512]{1,0:T(8,128)(2,1)}, bf16[64,5120]{1,0:T(8,128)(2,1)}) custom-call(s32[1,2]{1,0:T(1,128)} %refs_0_.1, s32[1,4]{1,0:T(1,128)} %refs_1_.1, bf16[1,256,512]{2,1,0:T(8,128)(2,1)} %refs_2_.2, bf16[2,128,512]{2,1,0:T(8,128)(2,1)} %refs_3_.1, bf16[2,128,512]{2,1,0:T(8,128)(2,1)} %refs_4_.1, ...), custom_call_target="tpu_custom_call" | custom-call | tf_op jit(solution)/shard_map/attention/pallas_call | solution.py:201
  3.2 3.0 %collective-permute-start.1 = (bf16[64,5120]{1,0:T(8,128)(2,1)}, bf16[64,5120]{1,0:T(8,128)(2,1)S(1)}, u32[]{:S(2)}, u32[]{:S(2)}) collective-permute-start(bf16[64,5120]{1,0:T(8,128)(2,1)} %get-tuple-element.49), channel_id=1, source_target_pairs={{0,16},{8,24},{16,0},{24,8},{1,17},{9,25},{17,1},{25,9},{2,18},{10... | collective-permute-start | bytes 1966088 | tf_op jit(solution)/shard_map/ppermute | solution.py:514
  6.2 4.7 %cast_rows.1 = (bf16[384,2048]{1,0:T(8,128)(2,1)}, bf16[128,2048]{1,0:T(8,128)(2,1)}, bf16[256,2048]{1,0:T(8,128)(2,1)}) custom-call(f32[1,512,2048]{2,1,0:T(8,128)} %refs_1_.2, f32[1,512,2048]{2,1,0:T(8,128)} %refs_1_.2, f32[1,256,2048]{2,1,0:T(8,128)} %refs_2_.3), custom_call_target="tpu_custom_call" | custom-call | tf_op jit(solution)/shard_map/cast_rows/pallas_call | solution.py:327
  11.1 10.9 %collective-permute-done.1.refs_2_.refs_20_.refs_21_ = bf16[64,5120]{1,0:T(8,128)(2,1)S(1)} collective-permute-done((bf16[64,5120]{1,0:T(8,128)(2,1)}, bf16[64,5120]{1,0:T(8,128)(2,1)S(1)}, u32[]{:S(2)}, u32[]{:S(2)}) %collective-permute-start.1) | collective-permute-done | bytes 655392 | tf_op jit(solution)/shard_map/ppermute | solution.py:514
  23.9 2.1 %collective-permute-start.3 = (bf16[32,2176]{1,0:T(8,128)(2,1)S(1)}, bf16[32,2176]{1,0:T(8,128)(2,1)S(1)}, u32[]{:S(2)}, u32[]{:S(2)}) collective-permute-start(bf16[32,2176]{1,0:T(8,128)(2,1)S(1)} %get-tuple-element.54.refs_0_), channel_id=1, source_target_pairs={{0,1},{2,0},{4,2},{6,4},{7,6},{5,7},{3,5},{1,3},{8,9},{10,8},{12,1... | collective-permute-start | bytes 417800 | tf_op jit(solution)/shard_map/ppermute | solution.py:524
  26.1 1.6 %collective-permute-start.4 = (bf16[32,2176]{1,0:T(8,128)(2,1)S(1)}, bf16[32,2176]{1,0:T(8,128)(2,1)S(1)}, u32[]{:S(2)}, u32[]{:S(2)}) collective-permute-start(bf16[32,2176]{1,0:T(8,128)(2,1)S(1)} %get-tuple-element.55.refs_1_), channel_id=1, source_target_pairs={{0,1},{2,0},{4,2},{6,4},{7,6},{5,7},{3,5},{1,3},{8,9},{10,8},{12,1... | collective-permute-start | bytes 417800 | tf_op jit(solution)/shard_map/ppermute | solution.py:524
  28.2 2.4 %collective-permute-done.3.refs_2_ = bf16[32,2176]{1,0:T(8,128)(2,1)S(1)} collective-permute-done((bf16[32,2176]{1,0:T(8,128)(2,1)S(1)}, bf16[32,2176]{1,0:T(8,128)(2,1)S(1)}, u32[]{:S(2)}, u32[]{:S(2)}) %collective-permute-start.3) | collective-permute-done | bytes 139296 | tf_op jit(solution)/shard_map/ppermute | solution.py:524
  30.6 2.0 %collective-permute-start.5 = (bf16[32,2176]{1,0:T(8,128)(2,1)S(1)}, bf16[32,2176]{1,0:T(8,128)(2,1)S(1)}, u32[]{:S(2)}, u32[]{:S(2)}) collective-permute-start(bf16[32,2176]{1,0:T(8,128)(2,1)S(1)} %collective-permute-done.3.refs_2_), channel_id=1, source_target_pairs={{0,1},{2,0},{4,2},{6,4},{7,6},{5,7},{3,5},{1,3},{8,9},{10,8},{12,1... | collective-permute-start | bytes 417800 | tf_op jit(solution)/shard_map/ppermute | solution.py:524
  33.6 2.0 %collective-permute-start.6 = (bf16[32,2176]{1,0:T(8,128)(2,1)S(1)}, bf16[32,2176]{1,0:T(8,128)(2,1)S(1)}, u32[]{:S(2)}, u32[]{:S(2)}) collective-permute-start(bf16[32,2176]{1,0:T(8,128)(2,1)S(1)} %collective-permute-done.4.refs_3_), channel_id=1, source_target_pairs={{0,1},{2,0},{4,2},{6,4},{7,6},{5,7},{3,5},{1,3},{8,9},{10,8},{12,1... | collective-permute-start | bytes 417800 | tf_op jit(solution)/shard_map/ppermute | solution.py:524
  35.8 1.9 %collective-permute-start.15 = (bf16[32,2176]{1,0:T(8,128)(2,1)S(1)}, bf16[32,2176]{1,0:T(8,128)(2,1)S(1)}, u32[]{:S(2)}, u32[]{:S(2)}) collective-permute-start(bf16[32,2176]{1,0:T(8,128)(2,1)S(1)} %collective-permute-done.14.refs_14_), channel_id=1, source_target_pairs={{0,2},{2,4},{4,6},{6,7},{7,5},{5,3},{3,1},{1,0},{8,10},{10,12},{12... | collective-permute-start | bytes 417800 | tf_op jit(solution)/shard_map/ppermute | solution.py:524
  38.9 1.3 %collective-permute-done.6.refs_5_ = bf16[32,2176]{1,0:T(8,128)(2,1)S(1)} collective-permute-done((bf16[32,2176]{1,0:T(8,128)(2,1)S(1)}, bf16[32,2176]{1,0:T(8,128)(2,1)S(1)}, u32[]{:S(2)}, u32[]{:S(2)}) %collective-permute-start.6) | collective-permute-done | bytes 139296 | tf_op jit(solution)/shard_map/ppermute | solution.py:524
  40.2 2.0 %collective-permute-start.8 = (bf16[32,2176]{1,0:T(8,128)(2,1)S(1)}, bf16[32,2176]{1,0:T(8,128)(2,1)S(1)}, u32[]{:S(2)}, u32[]{:S(2)}) collective-permute-start(bf16[32,2176]{1,0:T(8,128)(2,1)S(1)} %collective-permute-done.6.refs_5_), channel_id=1, source_target_pairs={{0,1},{2,0},{4,2},{6,4},{7,6},{5,7},{3,5},{1,3},{8,9},{10,8},{12,1... | collective-permute-start | bytes 417800 | tf_op jit(solution)/shard_map/ppermute | solution.py:524
  43.6 1.7 %collective-permute-start.16 = (bf16[32,2176]{1,0:T(8,128)(2,1)S(1)}, bf16[32,2176]{1,0:T(8,128)(2,1)S(1)}, u32[]{:S(2)}, u32[]{:S(2)}) collective-permute-start(bf16[32,2176]{1,0:T(8,128)(2,1)S(1)} %collective-permute-done.15.refs_12_), channel_id=1, source_target_pairs={{0,2},{2,4},{4,6},{6,7},{7,5},{5,3},{3,1},{1,0},{8,10},{10,12},{12... | collective-permute-start | bytes 417800 | tf_op jit(solution)/shard_map/ppermute | solution.py:524
  45.3 2.0 %collective-permute-start.9 = (bf16[32,2176]{1,0:T(8,128)(2,1)S(1)}, bf16[32,2176]{1,0:T(8,128)(2,1)S(1)}, u32[]{:S(2)}, u32[]{:S(2)}) collective-permute-start(bf16[32,2176]{1,0:T(8,128)(2,1)S(1)} %collective-permute-done.7.refs_6_), channel_id=1, source_target_pairs={{0,1},{2,0},{4,2},{6,4},{7,6},{5,7},{3,5},{1,3},{8,9},{10,8},{12,1... | collective-permute-start | bytes 417800 | tf_op jit(solution)/shard_map/ppermute | solution.py:524
  48.4 2.9 %collective-permute-done.16.refs_10_ = bf16[32,2176]{1,0:T(8,128)(2,1)S(1)} collective-permute-done((bf16[32,2176]{1,0:T(8,128)(2,1)S(1)}, bf16[32,2176]{1,0:T(8,128)(2,1)S(1)}, u32[]{:S(2)}, u32[]{:S(2)}) %collective-permute-start.16) | collective-permute-done | bytes 139296 | tf_op jit(solution)/shard_map/ppermute | solution.py:524
  51.9 1.6 %collective-permute-done.13.refs_9_ = bf16[32,2176]{1,0:T(8,128)(2,1)S(1)} collective-permute-done((bf16[32,2176]{1,0:T(8,128)(2,1)S(1)}, bf16[32,2176]{1,0:T(8,128)(2,1)S(1)}, u32[]{:S(2)}, u32[]{:S(2)}) %collective-permute-start.13) | collective-permute-done | bytes 139296 | tf_op jit(solution)/shard_map/ppermute | solution.py:524
  53.5 1.5 %collective-permute-start.25 = (bf16[256,2048]{1,0:T(8,128)(2,1)S(1)}, bf16[256,2048]{1,0:T(8,128)(2,1)S(1)}, u32[]{:S(2)}, u32[]{:S(2)}) collective-permute-start(bf16[256,2048]{1,0:T(8,128)(2,1)S(1)} %copy-done.1), channel_id=1, source_target_pairs={{0,16},{8,24},{16,0},{24,8},{1,17},{9,25},{17,1},{25,9},{2,18},{10... | collective-permute-start | bytes 3145736 | tf_op jit(solution)/shard_map/ppermute | solution.py:514
  55.9 3.6 %collective-permute-done.17.refs_18_ = bf16[128,2048]{1,0:T(8,128)(2,1)S(1)} collective-permute-done((bf16[128,2048]{1,0:T(8,128)(2,1)S(1)}, bf16[128,2048]{1,0:T(8,128)(2,1)S(1)}, u32[]{:S(2)}, u32[]{:S(2)}) %collective-permute-start.17) | collective-permute-done | bytes 524320 | tf_op jit(solution)/shard_map/ppermute | solution.py:514
  59.6 8.1 %expert_up.1 = (bf16[512,1024]{1,0:T(8,128)(2,1)S(1)}, f32[512,1]{1,0:T(8,128)S(1)}) custom-call(bf16[32,2176]{1,0:T(8,128)(2,1)S(1)} %get-tuple-element.54.refs_0_, bf16[32,2176]{1,0:T(8,128)(2,1)S(1)} %get-tuple-element.55.refs_1_, bf16[32,2176]{1,0:T(8,128)(2,1)S(1)} %collective-permute-done.3.refs_2_, ...), custom_call_target="tpu_custom_call" | custom-call | flops 1 | bytes 1 | tf_op jit(solution)/shard_map/expert_up/pallas_call | solution.py:406
  67.7 9.6 %collective-permute-done.25.refs_2_ = bf16[256,2048]{1,0:T(8,128)(2,1)S(1)} collective-permute-done((bf16[256,2048]{1,0:T(8,128)(2,1)S(1)}, bf16[256,2048]{1,0:T(8,128)(2,1)S(1)}, u32[]{:S(2)}, u32[]{:S(2)}) %collective-permute-start.25) | collective-permute-done | bytes 1048608 | tf_op jit(solution)/shard_map/ppermute | solution.py:514
  78.0 2.0 %down_part.1.refs_1_ = f32[512,2048]{1,0:T(8,128)S(1)} custom-call(bf16[512,1024]{1,0:T(8,128)(2,1)S(1)} %get-tuple-element.61.hidden_ref.refs_0_, bf16[256,2048]{1,0:T(8,128)(2,1)S(1)} %copy-done.1, bf16[256,2048]{1,0:T(8,128)(2,1)S(1)} %collective-permute-done.24.refs_1_, bf16[256,2048]{1,0:T(8,128)(2,1)S(1)} %collective-permute-done.25.refs_2_), custom_call_target="tpu_custom_call" | custom-call | flops 1 | bytes 1 | tf_op jit(solution)/shard_map/down_part/pallas_call | solution.py:451
  80.6 1.9 %collective-permute-start.27 = (bf16[32,1024]{1,0:T(8,128)(2,1)S(1)}, bf16[32,1024]{1,0:T(8,128)(2,1)S(1)}, u32[]{:S(2)}, u32[]{:S(2)}) collective-permute-start(bf16[32,1024]{1,0:T(8,128)(2,1)S(1)} %get-tuple-element.71), channel_id=1, source_target_pairs={{0,2},{2,4},{4,6},{6,7},{7,5},{5,3},{3,1},{1,0},{8,10},{10,12},{12... | collective-permute-start | bytes 196616 | tf_op jit(solution)/shard_map/ppermute | solution.py:524
  83.2 1.9 %collective-permute-start.36 = (bf16[32,1024]{1,0:T(8,128)(2,1)S(1)}, bf16[32,1024]{1,0:T(8,128)(2,1)S(1)}, u32[]{:S(2)}, u32[]{:S(2)}) collective-permute-start(bf16[32,1024]{1,0:T(8,128)(2,1)S(1)} %get-tuple-element.82), channel_id=1, source_target_pairs={{0,2},{2,4},{4,6},{6,7},{7,5},{5,3},{3,1},{1,0},{8,10},{10,12},{12... | collective-permute-start | bytes 196616 | tf_op jit(solution)/shard_map/ppermute | solution.py:524
  85.3 1.9 %collective-permute-start.28 = (bf16[64,1024]{1,0:T(8,128)(2,1)S(1)}, bf16[64,1024]{1,0:T(8,128)(2,1)S(1)}, u32[]{:S(2)}, u32[]{:S(2)}) collective-permute-start(bf16[64,1024]{1,0:T(8,128)(2,1)S(1)} %pad_maximum_fusion), channel_id=1, source_target_pairs={{0,2},{2,4},{4,6},{6,7},{7,5},{5,3},{3,1},{1,0},{8,10},{10,12},{12... | collective-permute-start | bytes 393224 | tf_op jit(solution)/shard_map/ppermute | solution.py:524
  87.9 2.0 %collective-permute-start.37 = (bf16[64,1024]{1,0:T(8,128)(2,1)S(1)}, bf16[64,1024]{1,0:T(8,128)(2,1)S(1)}, u32[]{:S(2)}, u32[]{:S(2)}) collective-permute-start(bf16[64,1024]{1,0:T(8,128)(2,1)S(1)} %pad_maximum_fusion.2), channel_id=1, source_target_pairs={{0,2},{2,4},{4,6},{6,7},{7,5},{5,3},{3,1},{1,0},{8,10},{10,12},{12... | collective-permute-start | bytes 393224 | tf_op jit(solution)/shard_map/ppermute | solution.py:524
  90.1 1.4 %collective-permute-done.28 = bf16[64,1024]{1,0:T(8,128)(2,1)S(1)} collective-permute-done((bf16[64,1024]{1,0:T(8,128)(2,1)S(1)}, bf16[64,1024]{1,0:T(8,128)(2,1)S(1)}, u32[]{:S(2)}, u32[]{:S(2)}) %collective-permute-start.28) | collective-permute-done | bytes 131104 | tf_op jit(solution)/shard_map/ppermute | solution.py:524
  91.6 2.0 %collective-permute-start.29 = (bf16[64,1024]{1,0:T(8,128)(2,1)S(1)}, bf16[64,1024]{1,0:T(8,128)(2,1)S(1)}, u32[]{:S(2)}, u32[]{:S(2)}) collective-permute-start(bf16[64,1024]{1,0:T(8,128)(2,1)S(1)} %add_convert_fusion.7), channel_id=1, source_target_pairs={{0,2},{2,4},{4,6},{6,7},{7,5},{5,3},{3,1},{1,0},{8,10},{10,12},{12... | collective-permute-start | bytes 393224 | tf_op jit(solution)/shard_map/ppermute | solution.py:524
  94.5 2.0 %collective-permute-start.38 = (bf16[64,1024]{1,0:T(8,128)(2,1)S(1)}, bf16[64,1024]{1,0:T(8,128)(2,1)S(1)}, u32[]{:S(2)}, u32[]{:S(2)}) collective-permute-start(bf16[64,1024]{1,0:T(8,128)(2,1)S(1)} %add_convert_fusion.3), channel_id=1, source_target_pairs={{0,2},{2,4},{4,6},{6,7},{7,5},{5,3},{3,1},{1,0},{8,10},{10,12},{12... | collective-permute-start | bytes 393224 | tf_op jit(solution)/shard_map/ppermute | solution.py:524
  97.5 1.7 %collective-permute-start.30 = (bf16[64,1024]{1,0:T(8,128)(2,1)S(1)}, bf16[64,1024]{1,0:T(8,128)(2,1)S(1)}, u32[]{:S(2)}, u32[]{:S(2)}) collective-permute-start(bf16[64,1024]{1,0:T(8,128)(2,1)S(1)} %add_convert_fusion.6), channel_id=1, source_target_pairs={{0,2},{2,4},{4,6},{6,7},{7,5},{5,3},{3,1},{1,0},{8,10},{10,12},{12... | collective-permute-start | bytes 393224 | tf_op jit(solution)/shard_map/ppermute | solution.py:524
  100.7 2.2 %collective-permute-start.39 = (bf16[64,1024]{1,0:T(8,128)(2,1)S(1)}, bf16[64,1024]{1,0:T(8,128)(2,1)S(1)}, u32[]{:S(2)}, u32[]{:S(2)}) collective-permute-start(bf16[64,1024]{1,0:T(8,128)(2,1)S(1)} %add_convert_fusion.2), channel_id=1, source_target_pairs={{0,2},{2,4},{4,6},{6,7},{7,5},{5,3},{3,1},{1,0},{8,10},{10,12},{12... | collective-permute-start | bytes 393224 | tf_op jit(solution)/shard_map/ppermute | solution.py:524
  103.1 1.6 %collective-permute-done.34.refs_2_ = bf16[64,1024]{1,0:T(8,128)(2,1)S(1)} collective-permute-done((bf16[64,1024]{1,0:T(8,128)(2,1)S(1)}, bf16[64,1024]{1,0:T(8,128)(2,1)S(1)}, u32[]{:S(2)}, u32[]{:S(2)}) %collective-permute-start.34) | collective-permute-done | bytes 131104 | tf_op jit(solution)/shard_map/ppermute | solution.py:524
  105.8 2.2 %collective-permute-done.43.refs_5_ = bf16[64,1024]{1,0:T(8,128)(2,1)S(1)} collective-permute-done((bf16[64,1024]{1,0:T(8,128)(2,1)S(1)}, bf16[64,1024]{1,0:T(8,128)(2,1)S(1)}, u32[]{:S(2)}, u32[]{:S(2)}) %collective-permute-start.43) | collective-permute-done | bytes 131104 | tf_op jit(solution)/shard_map/ppermute | solution.py:524
  (102 shorter events, 17.9 us)
Async XLA Ops:
  3.2 18.8 %collective-permute-start.1 = (bf16[64,5120]{1,0:T(8,128)(2,1)}, bf16[64,5120]{1,0:T(8,128)(2,1)S(1)}, u32[]{:S(2)}, u32[]{:S(2)}) collective-permute-start(bf16[64,5120]{1,0:T(8,128)(2,1)} %get-tuple-element.49), channel_id=1, source_target_pairs={{0,16},{8,24},{16,0},{24,8},{1,17},{9,25},{17,1},{25,9},{2,18},{10... | collective-permute-start | bytes 1966088 | tf_op jit(solution)/shard_map/ppermute | solution.py:514
  10.9 44.1 %collective-permute-start.19 = (bf16[384,2048]{1,0:T(8,128)(2,1)}, bf16[384,2048]{1,0:T(8,128)(2,1)S(1)}, u32[]{:S(2)}, u32[]{:S(2)}) collective-permute-start(bf16[384,2048]{1,0:T(8,128)(2,1)} %get-tuple-element.58.refs_17_), channel_id=1, source_target_pairs={{0,16},{8,24},{16,0},{24,8},{1,17},{9,25},{17,1},{25,9},{2,18},{10... | collective-permute-start | bytes 4718600 | tf_op jit(solution)/shard_map/ppermute | solution.py:514
  11.1 10.9 %collective-permute-start = (bf16[64,512]{1,0:T(8,128)(2,1)S(1)}, bf16[64,512]{1,0:T(8,128)(2,1)S(1)}, u32[]{:S(2)}, u32[]{:S(2)}) collective-permute-start(bf16[64,512]{1,0:T(8,128)(2,1)S(1)} %copy-done.8), channel_id=1, source_target_pairs={{0,8},{8,0},{16,24},{24,16},{1,9},{9,1},{17,25},{25,17},{2,10},{10... | collective-permute-start | bytes 196616 | tf_op jit(solution)/shard_map/ppermute | solution.py:514
  23.9 6.7 %collective-permute-start.3 = (bf16[32,2176]{1,0:T(8,128)(2,1)S(1)}, bf16[32,2176]{1,0:T(8,128)(2,1)S(1)}, u32[]{:S(2)}, u32[]{:S(2)}) collective-permute-start(bf16[32,2176]{1,0:T(8,128)(2,1)S(1)} %get-tuple-element.54.refs_0_), channel_id=1, source_target_pairs={{0,1},{2,0},{4,2},{6,4},{7,6},{5,7},{3,5},{1,3},{8,9},{10,8},{12,1... | collective-permute-start | bytes 417800 | tf_op jit(solution)/shard_map/ppermute | solution.py:524
  26.1 7.5 %collective-permute-start.4 = (bf16[32,2176]{1,0:T(8,128)(2,1)S(1)}, bf16[32,2176]{1,0:T(8,128)(2,1)S(1)}, u32[]{:S(2)}, u32[]{:S(2)}) collective-permute-start(bf16[32,2176]{1,0:T(8,128)(2,1)S(1)} %get-tuple-element.55.refs_1_), channel_id=1, source_target_pairs={{0,1},{2,0},{4,2},{6,4},{7,6},{5,7},{3,5},{1,3},{8,9},{10,8},{12,1... | collective-permute-start | bytes 417800 | tf_op jit(solution)/shard_map/ppermute | solution.py:524
  27.6 7.9 %collective-permute-start.10 = (bf16[32,2176]{1,0:T(8,128)(2,1)S(1)}, bf16[32,2176]{1,0:T(8,128)(2,1)S(1)}, u32[]{:S(2)}, u32[]{:S(2)}) collective-permute-start(bf16[32,2176]{1,0:T(8,128)(2,1)S(1)} %get-tuple-element.55.refs_1_), channel_id=1, source_target_pairs={{0,2},{2,4},{4,6},{6,7},{7,5},{5,3},{3,1},{1,0},{8,10},{10,12},{12... | collective-permute-start | bytes 417800 | tf_op jit(solution)/shard_map/ppermute | solution.py:524
  28.1 7.7 %collective-permute-start.14 = (bf16[32,2176]{1,0:T(8,128)(2,1)S(1)}, bf16[32,2176]{1,0:T(8,128)(2,1)S(1)}, u32[]{:S(2)}, u32[]{:S(2)}) collective-permute-start(bf16[32,2176]{1,0:T(8,128)(2,1)S(1)} %get-tuple-element.54.refs_0_), channel_id=1, source_target_pairs={{0,2},{2,4},{4,6},{6,7},{7,5},{5,3},{3,1},{1,0},{8,10},{10,12},{12... | collective-permute-start | bytes 417800 | tf_op jit(solution)/shard_map/ppermute | solution.py:524
  30.6 7.1 %collective-permute-start.5 = (bf16[32,2176]{1,0:T(8,128)(2,1)S(1)}, bf16[32,2176]{1,0:T(8,128)(2,1)S(1)}, u32[]{:S(2)}, u32[]{:S(2)}) collective-permute-start(bf16[32,2176]{1,0:T(8,128)(2,1)S(1)} %collective-permute-done.3.refs_2_), channel_id=1, source_target_pairs={{0,1},{2,0},{4,2},{6,4},{7,6},{5,7},{3,5},{1,3},{8,9},{10,8},{12,1... | collective-permute-start | bytes 417800 | tf_op jit(solution)/shard_map/ppermute | solution.py:524
  33.6 6.6 %collective-permute-start.6 = (bf16[32,2176]{1,0:T(8,128)(2,1)S(1)}, bf16[32,2176]{1,0:T(8,128)(2,1)S(1)}, u32[]{:S(2)}, u32[]{:S(2)}) collective-permute-start(bf16[32,2176]{1,0:T(8,128)(2,1)S(1)} %collective-permute-done.4.refs_3_), channel_id=1, source_target_pairs={{0,1},{2,0},{4,2},{6,4},{7,6},{5,7},{3,5},{1,3},{8,9},{10,8},{12,1... | collective-permute-start | bytes 417800 | tf_op jit(solution)/shard_map/ppermute | solution.py:524
  35.6 6.6 %collective-permute-start.11 = (bf16[32,2176]{1,0:T(8,128)(2,1)S(1)}, bf16[32,2176]{1,0:T(8,128)(2,1)S(1)}, u32[]{:S(2)}, u32[]{:S(2)}) collective-permute-start(bf16[32,2176]{1,0:T(8,128)(2,1)S(1)} %collective-permute-done.10.refs_15_), channel_id=1, source_target_pairs={{0,2},{2,4},{4,6},{6,7},{7,5},{5,3},{3,1},{1,0},{8,10},{10,12},{12... | collective-permute-start | bytes 417800 | tf_op jit(solution)/shard_map/ppermute | solution.py:524
  35.8 7.2 %collective-permute-start.15 = (bf16[32,2176]{1,0:T(8,128)(2,1)S(1)}, bf16[32,2176]{1,0:T(8,128)(2,1)S(1)}, u32[]{:S(2)}, u32[]{:S(2)}) collective-permute-start(bf16[32,2176]{1,0:T(8,128)(2,1)S(1)} %collective-permute-done.14.refs_14_), channel_id=1, source_target_pairs={{0,2},{2,4},{4,6},{6,7},{7,5},{5,3},{3,1},{1,0},{8,10},{10,12},{12... | collective-permute-start | bytes 417800 | tf_op jit(solution)/shard_map/ppermute | solution.py:524
  37.7 5.9 %collective-permute-start.7 = (bf16[32,2176]{1,0:T(8,128)(2,1)S(1)}, bf16[32,2176]{1,0:T(8,128)(2,1)S(1)}, u32[]{:S(2)}, u32[]{:S(2)}) collective-permute-start(bf16[32,2176]{1,0:T(8,128)(2,1)S(1)} %collective-permute-done.5.refs_4_), channel_id=1, source_target_pairs={{0,1},{2,0},{4,2},{6,4},{7,6},{5,7},{3,5},{1,3},{8,9},{10,8},{12,1... | collective-permute-start | bytes 417800 | tf_op jit(solution)/shard_map/ppermute | solution.py:524
  40.2 5.1 %collective-permute-start.8 = (bf16[32,2176]{1,0:T(8,128)(2,1)S(1)}, bf16[32,2176]{1,0:T(8,128)(2,1)S(1)}, u32[]{:S(2)}, u32[]{:S(2)}) collective-permute-start(bf16[32,2176]{1,0:T(8,128)(2,1)S(1)} %collective-permute-done.6.refs_5_), channel_id=1, source_target_pairs={{0,1},{2,0},{4,2},{6,4},{7,6},{5,7},{3,5},{1,3},{8,9},{10,8},{12,1... | collective-permute-start | bytes 417800 | tf_op jit(solution)/shard_map/ppermute | solution.py:524
  42.2 6.2 %collective-permute-start.12 = (bf16[32,2176]{1,0:T(8,128)(2,1)S(1)}, bf16[32,2176]{1,0:T(8,128)(2,1)S(1)}, u32[]{:S(2)}, u32[]{:S(2)}) collective-permute-start(bf16[32,2176]{1,0:T(8,128)(2,1)S(1)} %collective-permute-done.11.refs_13_), channel_id=1, source_target_pairs={{0,2},{2,4},{4,6},{6,7},{7,5},{5,3},{3,1},{1,0},{8,10},{10,12},{12... | collective-permute-start | bytes 417800 | tf_op jit(solution)/shard_map/ppermute | solution.py:524
  43.0 16.7 %collective-permute-start.18 = (bf16[384,2048]{1,0:T(8,128)(2,1)}, bf16[384,2048]{1,0:T(8,128)(2,1)S(1)}, u32[]{:S(2)}, u32[]{:S(2)}) collective-permute-start(bf16[384,2048]{1,0:T(8,128)(2,1)} %get-tuple-element.58.refs_17_), channel_id=1, source_target_pairs={{0,8},{8,0},{16,24},{24,16},{1,9},{9,1},{17,25},{25,17},{2,10},{10... | collective-permute-start | bytes 4718600 | tf_op jit(solution)/shard_map/ppermute | solution.py:514
  43.6 7.8 %collective-permute-start.16 = (bf16[32,2176]{1,0:T(8,128)(2,1)S(1)}, bf16[32,2176]{1,0:T(8,128)(2,1)S(1)}, u32[]{:S(2)}, u32[]{:S(2)}) collective-permute-start(bf16[32,2176]{1,0:T(8,128)(2,1)S(1)} %collective-permute-done.15.refs_12_), channel_id=1, source_target_pairs={{0,2},{2,4},{4,6},{6,7},{7,5},{5,3},{3,1},{1,0},{8,10},{10,12},{12... | collective-permute-start | bytes 417800 | tf_op jit(solution)/shard_map/ppermute | solution.py:524
  45.3 6.1 %collective-permute-start.9 = (bf16[32,2176]{1,0:T(8,128)(2,1)S(1)}, bf16[32,2176]{1,0:T(8,128)(2,1)S(1)}, u32[]{:S(2)}, u32[]{:S(2)}) collective-permute-start(bf16[32,2176]{1,0:T(8,128)(2,1)S(1)} %collective-permute-done.7.refs_6_), channel_id=1, source_target_pairs={{0,1},{2,0},{4,2},{6,4},{7,6},{5,7},{3,5},{1,3},{8,9},{10,8},{12,1... | collective-permute-start | bytes 417800 | tf_op jit(solution)/shard_map/ppermute | solution.py:524
  48.4 5.1 %collective-permute-start.13 = (bf16[32,2176]{1,0:T(8,128)(2,1)S(1)}, bf16[32,2176]{1,0:T(8,128)(2,1)S(1)}, u32[]{:S(2)}, u32[]{:S(2)}) collective-permute-start(bf16[32,2176]{1,0:T(8,128)(2,1)S(1)} %collective-permute-done.12.refs_11_), channel_id=1, source_target_pairs={{0,2},{2,4},{4,6},{6,7},{7,5},{5,3},{3,1},{1,0},{8,10},{10,12},{12... | collective-permute-start | bytes 417800 | tf_op jit(solution)/shard_map/ppermute | solution.py:524
  53.5 23.9 %collective-permute-start.25 = (bf16[256,2048]{1,0:T(8,128)(2,1)S(1)}, bf16[256,2048]{1,0:T(8,128)(2,1)S(1)}, u32[]{:S(2)}, u32[]{:S(2)}) collective-permute-start(bf16[256,2048]{1,0:T(8,128)(2,1)S(1)} %copy-done.1), channel_id=1, source_target_pairs={{0,16},{8,24},{16,0},{24,8},{1,17},{9,25},{17,1},{25,9},{2,18},{10... | collective-permute-start | bytes 3145736 | tf_op jit(solution)/shard_map/ppermute | solution.py:514
  59.5 18.5 %collective-permute-start.24 = (bf16[256,2048]{1,0:T(8,128)(2,1)S(1)}, bf16[256,2048]{1,0:T(8,128)(2,1)S(1)}, u32[]{:S(2)}, u32[]{:S(2)}) collective-permute-start(bf16[256,2048]{1,0:T(8,128)(2,1)S(1)} %copy-done.1), channel_id=1, source_target_pairs={{0,8},{8,0},{16,24},{24,16},{1,9},{9,1},{17,25},{25,17},{2,10},{10... | collective-permute-start | bytes 3145736 | tf_op jit(solution)/shard_map/ppermute | solution.py:514
  77.5 5.2 %collective-permute-start.35 = (bf16[256,1024]{1,0:T(8,128)(2,1)S(1)}, bf16[256,1024]{1,0:T(8,128)(2,1)S(1)}, u32[]{:S(2)}, u32[]{:S(2)}) collective-permute-start(bf16[256,1024]{1,0:T(8,128)(2,1)S(1)} %get-tuple-element.91), channel_id=1, source_target_pairs={{0,8},{8,0},{16,24},{24,16},{1,9},{9,1},{17,25},{25,17},{2,10},{10... | collective-permute-start | bytes 1572872 | tf_op jit(solution)/shard_map/ppermute | solution.py:514
  85.3 6.2 %collective-permute-start.28 = (bf16[64,1024]{1,0:T(8,128)(2,1)S(1)}, bf16[64,1024]{1,0:T(8,128)(2,1)S(1)}, u32[]{:S(2)}, u32[]{:S(2)}) collective-permute-start(bf16[64,1024]{1,0:T(8,128)(2,1)S(1)} %pad_maximum_fusion), channel_id=1, source_target_pairs={{0,2},{2,4},{4,6},{6,7},{7,5},{5,3},{3,1},{1,0},{8,10},{10,12},{12... | collective-permute-start | bytes 393224 | tf_op jit(solution)/shard_map/ppermute | solution.py:524
  87.2 6.4 %collective-permute-start.32 = (bf16[64,1024]{1,0:T(8,128)(2,1)S(1)}, bf16[64,1024]{1,0:T(8,128)(2,1)S(1)}, u32[]{:S(2)}, u32[]{:S(2)}) collective-permute-start(bf16[64,1024]{1,0:T(8,128)(2,1)S(1)} %pad_maximum_fusion.1), channel_id=1, source_target_pairs={{0,1},{2,0},{4,2},{6,4},{7,6},{5,7},{3,5},{1,3},{8,9},{10,8},{12,1... | collective-permute-start | bytes 393224 | tf_op jit(solution)/shard_map/ppermute | solution.py:524
  87.9 6.5 %collective-permute-start.37 = (bf16[64,1024]{1,0:T(8,128)(2,1)S(1)}, bf16[64,1024]{1,0:T(8,128)(2,1)S(1)}, u32[]{:S(2)}, u32[]{:S(2)}) collective-permute-start(bf16[64,1024]{1,0:T(8,128)(2,1)S(1)} %pad_maximum_fusion.2), channel_id=1, source_target_pairs={{0,2},{2,4},{4,6},{6,7},{7,5},{5,3},{3,1},{1,0},{8,10},{10,12},{12... | collective-permute-start | bytes 393224 | tf_op jit(solution)/shard_map/ppermute | solution.py:524
  90.0 6.4 %collective-permute-start.41 = (bf16[64,1024]{1,0:T(8,128)(2,1)S(1)}, bf16[64,1024]{1,0:T(8,128)(2,1)S(1)}, u32[]{:S(2)}, u32[]{:S(2)}) collective-permute-start(bf16[64,1024]{1,0:T(8,128)(2,1)S(1)} %pad_maximum_fusion.3), channel_id=1, source_target_pairs={{0,1},{2,0},{4,2},{6,4},{7,6},{5,7},{3,5},{1,3},{8,9},{10,8},{12,1... | collective-permute-start | bytes 393224 | tf_op jit(solution)/shard_map/ppermute | solution.py:524
  91.6 5.9 %collective-permute-start.29 = (bf16[64,1024]{1,0:T(8,128)(2,1)S(1)}, bf16[64,1024]{1,0:T(8,128)(2,1)S(1)}, u32[]{:S(2)}, u32[]{:S(2)}) collective-permute-start(bf16[64,1024]{1,0:T(8,128)(2,1)S(1)} %add_convert_fusion.7), channel_id=1, source_target_pairs={{0,2},{2,4},{4,6},{6,7},{7,5},{5,3},{3,1},{1,0},{8,10},{10,12},{12... | collective-permute-start | bytes 393224 | tf_op jit(solution)/shard_map/ppermute | solution.py:524
  93.6 5.6 %collective-permute-start.33 = (bf16[64,1024]{1,0:T(8,128)(2,1)S(1)}, bf16[64,1024]{1,0:T(8,128)(2,1)S(1)}, u32[]{:S(2)}, u32[]{:S(2)}) collective-permute-start(bf16[64,1024]{1,0:T(8,128)(2,1)S(1)} %add_convert_fusion.5), channel_id=1, source_target_pairs={{0,1},{2,0},{4,2},{6,4},{7,6},{5,7},{3,5},{1,3},{8,9},{10,8},{12,1... | collective-permute-start | bytes 393224 | tf_op jit(solution)/shard_map/ppermute | solution.py:524
  94.5 6.2 %collective-permute-start.38 = (bf16[64,1024]{1,0:T(8,128)(2,1)S(1)}, bf16[64,1024]{1,0:T(8,128)(2,1)S(1)}, u32[]{:S(2)}, u32[]{:S(2)}) collective-permute-start(bf16[64,1024]{1,0:T(8,128)(2,1)S(1)} %add_convert_fusion.3), channel_id=1, source_target_pairs={{0,2},{2,4},{4,6},{6,7},{7,5},{5,3},{3,1},{1,0},{8,10},{10,12},{12... | collective-permute-start | bytes 393224 | tf_op jit(solution)/shard_map/ppermute | solution.py:524
  96.5 6.5 %collective-permute-start.42 = (bf16[64,1024]{1,0:T(8,128)(2,1)S(1)}, bf16[64,1024]{1,0:T(8,128)(2,1)S(1)}, u32[]{:S(2)}, u32[]{:S(2)}) collective-permute-start(bf16[64,1024]{1,0:T(8,128)(2,1)S(1)} %add_convert_fusion.1), channel_id=1, source_target_pairs={{0,1},{2,0},{4,2},{6,4},{7,6},{5,7},{3,5},{1,3},{8,9},{10,8},{12,1... | collective-permute-start | bytes 393224 | tf_op jit(solution)/shard_map/ppermute | solution.py:524
  97.5 5.5 %collective-permute-start.30 = (bf16[64,1024]{1,0:T(8,128)(2,1)S(1)}, bf16[64,1024]{1,0:T(8,128)(2,1)S(1)}, u32[]{:S(2)}, u32[]{:S(2)}) collective-permute-start(bf16[64,1024]{1,0:T(8,128)(2,1)S(1)} %add_convert_fusion.6), channel_id=1, source_target_pairs={{0,2},{2,4},{4,6},{6,7},{7,5},{5,3},{3,1},{1,0},{8,10},{10,12},{12... | collective-permute-start | bytes 393224 | tf_op jit(solution)/shard_map/ppermute | solution.py:524
  99.3 5.4 %collective-permute-start.34 = (bf16[64,1024]{1,0:T(8,128)(2,1)S(1)}, bf16[64,1024]{1,0:T(8,128)(2,1)S(1)}, u32[]{:S(2)}, u32[]{:S(2)}) collective-permute-start(bf16[64,1024]{1,0:T(8,128)(2,1)S(1)} %add_convert_fusion.4), channel_id=1, source_target_pairs={{0,1},{2,0},{4,2},{6,4},{7,6},{5,7},{3,5},{1,3},{8,9},{10,8},{12,1... | collective-permute-start | bytes 393224 | tf_op jit(solution)/shard_map/ppermute | solution.py:524
  100.7 5.1 %collective-permute-start.39 = (bf16[64,1024]{1,0:T(8,128)(2,1)S(1)}, bf16[64,1024]{1,0:T(8,128)(2,1)S(1)}, u32[]{:S(2)}, u32[]{:S(2)}) collective-permute-start(bf16[64,1024]{1,0:T(8,128)(2,1)S(1)} %add_convert_fusion.2), channel_id=1, source_target_pairs={{0,2},{2,4},{4,6},{6,7},{7,5},{5,3},{3,1},{1,0},{8,10},{10,12},{12... | collective-permute-start | bytes 393224 | tf_op jit(solution)/shard_map/ppermute | solution.py:524
  (21 other events, 193.8 us)

commit v18 on v17

--- a/solution.py
+++ b/solution.py
@@ -362,11 +362,31 @@
     return wait
 
 
+def row_copies(pieces, weights, arrived):
+    first = 0
+    for i, ref in enumerate(pieces):
+        depth = ref.shape[0]
+        yield pltpu.make_async_copy(ref, weights.at[pl.ds(first, depth)], arrived.at[i])
+        first += depth
+
+
+def start_rows(pieces, weights, arrived):
+    for copy in row_copies(pieces, weights, arrived):
+        copy.start()
+
+
+def wait_rows(pieces, weights, arrived):
+    for copy in row_copies(pieces, weights, arrived):
+        copy.wait()
+
+
 def up_kernel(sources, starts, *refs):
     pieces = len(starts)
     row_refs = refs[:sources]
     weight_refs = refs[sources : sources + pieces]
-    hidden_ref, own_gate_ref, rows, weights, units, arrived = refs[sources + pieces :]
+    down_refs, refs = refs[sources + pieces : -9], refs[-9:]
+    hidden_ref, own_gate_ref, total_ref, rows, weights, units, down, arrived, down_arrived = refs
+    start_rows(down_refs, down, down_arrived)
     width = rows.shape[1]
     tiles, _, block = units.shape
     wait = load_tiles(weight_refs, starts, weights, arrived, tiles, block)
@@ -396,9 +416,13 @@
     own = lax.axis_index("dp")
     for d in range(4):
         hidden_ref[:, d * block : (d + 1) * block] = units[own ^ d]
-
-
-def expert_up(rows, weights, width):
+    wait_rows(down_refs, down, down_arrived)
+    total_ref[...] = jnp.dot(
+        hidden_ref[:, : down.shape[0]], down[...], preferred_element_type=jnp.float32
+    )
+
+
+def expert_up(rows, weights, width, down):
     weights, starts = zip(*weights)
     tokens = sum(piece.shape[0] for piece in rows)
     features = sum(piece.shape[0] for piece in weights)
@@ -408,64 +432,55 @@
         out_shape=[
             jax.ShapeDtypeStruct((tokens, hidden_size), jnp.bfloat16),
             jax.ShapeDtypeStruct((tokens, 1), jnp.float32),
+            jax.ShapeDtypeStruct((tokens, down[0].shape[1]), jnp.float32),
         ],
-        in_specs=vmem(len(rows)) + [pl.BlockSpec(memory_space=pl.ANY)] * len(weights),
-        out_specs=vmem(2),
+        in_specs=vmem(len(rows)) + [pl.BlockSpec(memory_space=pl.ANY)] * (len(weights) + len(down)),
+        out_specs=vmem(3),
         scratch_shapes=[
             pltpu.VMEM((tokens, features), jnp.bfloat16),
             pltpu.VMEM((features, width), jnp.bfloat16),
             pltpu.VMEM((4, tokens, hidden_size // 4), jnp.bfloat16),
+            pltpu.VMEM((sum(x.shape[0] for x in down), down[0].shape[1]), jnp.bfloat16),
             pltpu.SemaphoreType.DMA((4, len(weights), 2)),
+            pltpu.SemaphoreType.DMA((len(down),)),
         ],
         compiler_params=params(),
         cost_estimate=SMALL,
         name="expert_up",
-    )(*rows, *weights)
-
-
-def load_rows(pieces, weights, arrived):
-    copies, first = [], 0
-    for i, ref in enumerate(pieces):
-        depth = ref.shape[0]
-        copies.append(
-            pltpu.make_async_copy(ref, weights.at[pl.ds(first, depth)], arrived.at[i])
-        )
-        first += depth
-    for copy in copies:
-        copy.start()
-    for copy in copies:
-        copy.wait()
-
-
-def part_kernel(hidden_ref, *refs):
+    )(*rows, *weights, *down)
+
+
+def part_kernel(first, hidden_ref, before_ref, *refs):
     pieces, (total_ref, weights, arrived) = refs[:-3], refs[-3:]
-    load_rows(pieces, weights, arrived)
-    total_ref[...] = jnp.dot(
-        hidden_ref[:, : weights.shape[0]], weights[...], preferred_element_type=jnp.float32
-    )
-
-
-def down_part(hidden_units, weights):
+    start_rows(pieces, weights, arrived)
+    wait_rows(pieces, weights, arrived)
+    units = hidden_ref[:, first : first + weights.shape[0]]
+    total_ref[...] = before_ref[...] + jnp.dot(
+        units, weights[...], preferred_element_type=jnp.float32
+    )
+
+
+def down_part(hidden_units, before, weights, first):
     depth = sum(piece.shape[0] for piece in weights)
-    shape = hidden_units.shape[0], weights[0].shape[1]
     return pl.pallas_call(
-        part_kernel,
-        out_shape=jax.ShapeDtypeStruct(shape, jnp.float32),
-        in_specs=vmem(1) + [pl.BlockSpec(memory_space=pl.ANY)] * len(weights),
+        lambda *refs: part_kernel(first, *refs),
+        out_shape=jax.ShapeDtypeStruct(before.shape, jnp.float32),
+        in_specs=vmem(2) + [pl.BlockSpec(memory_space=pl.ANY)] * len(weights),
         out_specs=pl.BlockSpec(memory_space=pltpu.VMEM),
         scratch_shapes=[
-            pltpu.VMEM((depth, shape[1]), jnp.bfloat16),
+            pltpu.VMEM((depth, before.shape[1]), jnp.bfloat16),
             pltpu.SemaphoreType.DMA((len(weights),)),
         ],
         compiler_params=params(),
         cost_estimate=SMALL,
         name="down_part",
-    )(hidden_units, *weights)
+    )(hidden_units, before, *weights)
 
 
 def down_kernel(first, column, sources, hidden_ref, total_ref, gate_ref, piece, *refs):
     outs, (weights, arrived) = refs[:-2], refs[-2:]
-    load_rows([piece], weights, arrived)
+    start_rows([piece], weights, arrived)
+    wait_rows([piece], weights, arrived)
     depth, width = weights.shape
     units = hidden_ref[:, first : first + depth]
     total = total_ref[:, column : column + width] + jnp.dot(
@@ -644,15 +659,16 @@
     down_beside = partner(after(down_own, *arrived[1]), 1)
     down_across = partner(after(down_own, *arrived[2]), 2)
     rest_opposite = relayed(after(rest_across, *arrived[3]), (depth - early) // 2)
-    hidden_units, gates = expert_up(
+    hidden_units, gates, total = expert_up(
         gathered,
         [(ref, 0) for ref in (first_own, rest_own, first_beside, rest_beside)]
         + [(first_across, start) for start in side]
         + [(ref, 0) for ref in (rest_across, *first_opposite, *rest_opposite)],
         columns,
+        [down_own],
     )
     down_ready = after(down_across, hidden_units)
-    total = down_part(hidden_units, [down_own, down_beside, down_ready])
+    total = down_part(hidden_units, total, [down_beside, down_ready], down_depth)
     mixed = []
     for first in range(0, width, slab):
         opposite = partner(down_ready[:, first : first + slab], 1)

time: 109 us -> 108 us (level)
  no operation moved by 1% of the time
where the time goes in v18:
time: 108 us
  waiting for transfers between devices  45.9 us (42%)
  starting transfers between devices  40.7 us (38%)
  Pallas kernels  20.7 us (19%)
    ppermute x30, starting transfers between devices, around(): lax.ppermute(x, 'expert', [(ring[i], ring[(i + step) % count]) for i in r...  34.1 us
    ppermute x14, waiting for transfers between devices, partner(): return lax.ppermute(x, 'dp', [(i, i ^ distance) for i in range(4)])  24.6 us
    ppermute x30, waiting for transfers between devices, around(): lax.ppermute(x, 'expert', [(ring[i], ring[(i + step) % count]) for i in r...  21.3 us
    pallas_call x1, Pallas kernels, expert_up(): pl.pallas_call(lambda *refs: up_kernel(len(rows), starts, *refs), out_sha...  8.91 us
    ppermute x14, starting transfers between devices, partner(): return lax.ppermute(x, 'dp', [(i, i ^ distance) for i in range(4)])  6.52 us
    pallas_call x1, Pallas kernels, cast_rows(): pl.pallas_call(lambda *refs: cast_kernel(spans, *refs), out_shape=[jax.Sh...  4.68 us
    pallas_call x1, Pallas kernels, attention(): pl.pallas_call(attention_kernel, out_shape=[jax.ShapeDtypeStruct(shape, j...  3.2 us
  transfers between devices with their start and end apart: 44, of which 23 were waited for; matrix products, arithmetic and copies ran while one was open for 1% of the time, Pallas kernels for 15%

profile of v18, /device:TPU:0, one launch (start us, length us, event | category | flops | bytes accessed | tf_op | source)
XLA Modules:
  0.0 108.2 jit_solution(3122695893225402553)
XLA Ops:
  0.0 3.2 %attention.1 = (bf16[64,512]{1,0:T(8,128)(2,1)}, bf16[64,512]{1,0:T(8,128)(2,1)}, bf16[64,5120]{1,0:T(8,128)(2,1)}) custom-call(s32[1,2]{1,0:T(1,128)} %refs_0_.1, s32[1,4]{1,0:T(1,128)} %refs_1_.1, bf16[1,256,512]{2,1,0:T(8,128)(2,1)} %refs_2_.2, bf16[2,128,512]{2,1,0:T(8,128)(2,1)} %refs_3_.1, bf16[2,128,512]{2,1,0:T(8,128)(2,1)} %refs_4_.1, ...), custom_call_target="tpu_custom_call" | custom-call | tf_op jit(solution)/shard_map/attention/pallas_call | solution.py:201
  3.2 3.0 %collective-permute-start.1 = (bf16[64,5120]{1,0:T(8,128)(2,1)}, bf16[64,5120]{1,0:T(8,128)(2,1)S(1)}, u32[]{:S(2)}, u32[]{:S(2)}) collective-permute-start(bf16[64,5120]{1,0:T(8,128)(2,1)} %get-tuple-element.50), channel_id=1, source_target_pairs={{0,16},{8,24},{16,0},{24,8},{1,17},{9,25},{17,1},{25,9},{2,18},{10... | collective-permute-start | bytes 1966088 | tf_op jit(solution)/shard_map/ppermute | solution.py:529
  6.2 4.7 %cast_rows.1 = (bf16[384,2048]{1,0:T(8,128)(2,1)}, bf16[128,2048]{1,0:T(8,128)(2,1)}, bf16[256,2048]{1,0:T(8,128)(2,1)}) custom-call(f32[1,512,2048]{2,1,0:T(8,128)} %refs_1_.2, f32[1,512,2048]{2,1,0:T(8,128)} %refs_1_.2, f32[1,256,2048]{2,1,0:T(8,128)} %refs_2_.3), custom_call_target="tpu_custom_call" | custom-call | tf_op jit(solution)/shard_map/cast_rows/pallas_call | solution.py:327
  11.1 10.9 %collective-permute-done.1.refs_2_.refs_20_.refs_21_ = bf16[64,5120]{1,0:T(8,128)(2,1)S(1)} collective-permute-done((bf16[64,5120]{1,0:T(8,128)(2,1)}, bf16[64,5120]{1,0:T(8,128)(2,1)S(1)}, u32[]{:S(2)}, u32[]{:S(2)}) %collective-permute-start.1) | collective-permute-done | bytes 655392 | tf_op jit(solution)/shard_map/ppermute | solution.py:529
  23.9 2.1 %collective-permute-start.3 = (bf16[32,2176]{1,0:T(8,128)(2,1)S(1)}, bf16[32,2176]{1,0:T(8,128)(2,1)S(1)}, u32[]{:S(2)}, u32[]{:S(2)}) collective-permute-start(bf16[32,2176]{1,0:T(8,128)(2,1)S(1)} %get-tuple-element.55.refs_0_), channel_id=1, source_target_pairs={{0,1},{2,0},{4,2},{6,4},{7,6},{5,7},{3,5},{1,3},{8,9},{10,8},{12,1... | collective-permute-start | bytes 417800 | tf_op jit(solution)/shard_map/ppermute | solution.py:539
  26.1 1.6 %collective-permute-start.4 = (bf16[32,2176]{1,0:T(8,128)(2,1)S(1)}, bf16[32,2176]{1,0:T(8,128)(2,1)S(1)}, u32[]{:S(2)}, u32[]{:S(2)}) collective-permute-start(bf16[32,2176]{1,0:T(8,128)(2,1)S(1)} %get-tuple-element.56.refs_1_), channel_id=1, source_target_pairs={{0,1},{2,0},{4,2},{6,4},{7,6},{5,7},{3,5},{1,3},{8,9},{10,8},{12,1... | collective-permute-start | bytes 417800 | tf_op jit(solution)/shard_map/ppermute | solution.py:539
  28.2 2.3 %collective-permute-done.3.refs_2_ = bf16[32,2176]{1,0:T(8,128)(2,1)S(1)} collective-permute-done((bf16[32,2176]{1,0:T(8,128)(2,1)S(1)}, bf16[32,2176]{1,0:T(8,128)(2,1)S(1)}, u32[]{:S(2)}, u32[]{:S(2)}) %collective-permute-start.3) | collective-permute-done | bytes 139296 | tf_op jit(solution)/shard_map/ppermute | solution.py:539
  30.6 2.0 %collective-permute-start.5 = (bf16[32,2176]{1,0:T(8,128)(2,1)S(1)}, bf16[32,2176]{1,0:T(8,128)(2,1)S(1)}, u32[]{:S(2)}, u32[]{:S(2)}) collective-permute-start(bf16[32,2176]{1,0:T(8,128)(2,1)S(1)} %collective-permute-done.3.refs_2_), channel_id=1, source_target_pairs={{0,1},{2,0},{4,2},{6,4},{7,6},{5,7},{3,5},{1,3},{8,9},{10,8},{12,1... | collective-permute-start | bytes 417800 | tf_op jit(solution)/shard_map/ppermute | solution.py:539
  33.6 2.0 %collective-permute-start.6 = (bf16[32,2176]{1,0:T(8,128)(2,1)S(1)}, bf16[32,2176]{1,0:T(8,128)(2,1)S(1)}, u32[]{:S(2)}, u32[]{:S(2)}) collective-permute-start(bf16[32,2176]{1,0:T(8,128)(2,1)S(1)} %collective-permute-done.4.refs_3_), channel_id=1, source_target_pairs={{0,1},{2,0},{4,2},{6,4},{7,6},{5,7},{3,5},{1,3},{8,9},{10,8},{12,1... | collective-permute-start | bytes 417800 | tf_op jit(solution)/shard_map/ppermute | solution.py:539
  35.8 1.9 %collective-permute-start.15 = (bf16[32,2176]{1,0:T(8,128)(2,1)S(1)}, bf16[32,2176]{1,0:T(8,128)(2,1)S(1)}, u32[]{:S(2)}, u32[]{:S(2)}) collective-permute-start(bf16[32,2176]{1,0:T(8,128)(2,1)S(1)} %collective-permute-done.14.refs_14_), channel_id=1, source_target_pairs={{0,2},{2,4},{4,6},{6,7},{7,5},{5,3},{3,1},{1,0},{8,10},{10,12},{12... | collective-permute-start | bytes 417800 | tf_op jit(solution)/shard_map/ppermute | solution.py:539
  40.2 2.0 %collective-permute-start.8 = (bf16[32,2176]{1,0:T(8,128)(2,1)S(1)}, bf16[32,2176]{1,0:T(8,128)(2,1)S(1)}, u32[]{:S(2)}, u32[]{:S(2)}) collective-permute-start(bf16[32,2176]{1,0:T(8,128)(2,1)S(1)} %collective-permute-done.6.refs_5_), channel_id=1, source_target_pairs={{0,1},{2,0},{4,2},{6,4},{7,6},{5,7},{3,5},{1,3},{8,9},{10,8},{12,1... | collective-permute-start | bytes 417800 | tf_op jit(solution)/shard_map/ppermute | solution.py:539
  43.6 1.7 %collective-permute-start.16 = (bf16[32,2176]{1,0:T(8,128)(2,1)S(1)}, bf16[32,2176]{1,0:T(8,128)(2,1)S(1)}, u32[]{:S(2)}, u32[]{:S(2)}) collective-permute-start(bf16[32,2176]{1,0:T(8,128)(2,1)S(1)} %collective-permute-done.15.refs_12_), channel_id=1, source_target_pairs={{0,2},{2,4},{4,6},{6,7},{7,5},{5,3},{3,1},{1,0},{8,10},{10,12},{12... | collective-permute-start | bytes 417800 | tf_op jit(solution)/shard_map/ppermute | solution.py:539
  45.3 2.0 %collective-permute-start.9 = (bf16[32,2176]{1,0:T(8,128)(2,1)S(1)}, bf16[32,2176]{1,0:T(8,128)(2,1)S(1)}, u32[]{:S(2)}, u32[]{:S(2)}) collective-permute-start(bf16[32,2176]{1,0:T(8,128)(2,1)S(1)} %collective-permute-done.7.refs_6_), channel_id=1, source_target_pairs={{0,1},{2,0},{4,2},{6,4},{7,6},{5,7},{3,5},{1,3},{8,9},{10,8},{12,1... | collective-permute-start | bytes 417800 | tf_op jit(solution)/shard_map/ppermute | solution.py:539
  48.4 2.9 %collective-permute-done.16.refs_10_ = bf16[32,2176]{1,0:T(8,128)(2,1)S(1)} collective-permute-done((bf16[32,2176]{1,0:T(8,128)(2,1)S(1)}, bf16[32,2176]{1,0:T(8,128)(2,1)S(1)}, u32[]{:S(2)}, u32[]{:S(2)}) %collective-permute-start.16) | collective-permute-done | bytes 139296 | tf_op jit(solution)/shard_map/ppermute | solution.py:539
  51.9 1.6 %collective-permute-done.13.refs_9_ = bf16[32,2176]{1,0:T(8,128)(2,1)S(1)} collective-permute-done((bf16[32,2176]{1,0:T(8,128)(2,1)S(1)}, bf16[32,2176]{1,0:T(8,128)(2,1)S(1)}, u32[]{:S(2)}, u32[]{:S(2)}) %collective-permute-start.13) | collective-permute-done | bytes 139296 | tf_op jit(solution)/shard_map/ppermute | solution.py:539
  53.5 1.5 %collective-permute-start.25 = (bf16[256,2048]{1,0:T(8,128)(2,1)S(1)}, bf16[256,2048]{1,0:T(8,128)(2,1)S(1)}, u32[]{:S(2)}, u32[]{:S(2)}) collective-permute-start(bf16[256,2048]{1,0:T(8,128)(2,1)S(1)} %copy-done.1), channel_id=1, source_target_pairs={{0,16},{8,24},{16,0},{24,8},{1,17},{9,25},{17,1},{25,9},{2,18},{10... | collective-permute-start | bytes 3145736 | tf_op jit(solution)/shard_map/ppermute | solution.py:529
  55.9 3.6 %collective-permute-done.17.refs_18_ = bf16[128,2048]{1,0:T(8,128)(2,1)S(1)} collective-permute-done((bf16[128,2048]{1,0:T(8,128)(2,1)S(1)}, bf16[128,2048]{1,0:T(8,128)(2,1)S(1)}, u32[]{:S(2)}, u32[]{:S(2)}) %collective-permute-start.17) | collective-permute-done | bytes 524320 | tf_op jit(solution)/shard_map/ppermute | solution.py:529
  59.7 8.9 %expert_up.1 = (bf16[512,1024]{1,0:T(8,128)(2,1)S(1)}, f32[512,1]{1,0:T(8,128)S(1)}, f32[512,2048]{1,0:T(8,128)S(1)}) custom-call(bf16[32,2176]{1,0:T(8,128)(2,1)S(1)} %get-tuple-element.55.refs_0_, bf16[32,2176]{1,0:T(8,128)(2,1)S(1)} %get-tuple-element.56.refs_1_, bf16[32,2176]{1,0:T(8,128)(2,1)S(1)} %collective-permute-done.3.refs_2_, ...), custom_call_target="tpu_custom_call" | custom-call | flops 1 | bytes 1 | tf_op jit(solution)/shard_map/expert_up/pallas_call | solution.py:430
  68.6 8.8 %collective-permute-done.25.refs_3_ = bf16[256,2048]{1,0:T(8,128)(2,1)S(1)} collective-permute-done((bf16[256,2048]{1,0:T(8,128)(2,1)S(1)}, bf16[256,2048]{1,0:T(8,128)(2,1)S(1)}, u32[]{:S(2)}, u32[]{:S(2)}) %collective-permute-start.25) | collective-permute-done | bytes 1048608 | tf_op jit(solution)/shard_map/ppermute | solution.py:529
  78.0 1.4 %down_part.1.refs_1_ = f32[512,2048]{1,0:T(8,128)S(1)} custom-call(bf16[512,1024]{1,0:T(8,128)(2,1)S(1)} %get-tuple-element.63.refs_0_, f32[512,2048]{1,0:T(8,128)S(1)} %get-tuple-element.64.refs_1_, bf16[256,2048]{1,0:T(8,128)(2,1)S(1)} %collective-permute-done.24.refs_2_, bf16[256,2048]{1,0:T(8,128)(2,1)S(1)} %collective-permute-done.25.refs_3_), custom_call_target="tpu_custom_call" | custom-call | flops 1 | bytes 1 | tf_op jit(solution)/shard_map/down_part/pallas_call | solution.py:465
  80.0 1.9 %collective-permute-start.27 = (bf16[32,1024]{1,0:T(8,128)(2,1)S(1)}, bf16[32,1024]{1,0:T(8,128)(2,1)S(1)}, u32[]{:S(2)}, u32[]{:S(2)}) collective-permute-start(bf16[32,1024]{1,0:T(8,128)(2,1)S(1)} %get-tuple-element.73), channel_id=1, source_target_pairs={{0,2},{2,4},{4,6},{6,7},{7,5},{5,3},{3,1},{1,0},{8,10},{10,12},{12... | collective-permute-start | bytes 196616 | tf_op jit(solution)/shard_map/ppermute | solution.py:539
  82.5 1.9 %collective-permute-start.36 = (bf16[32,1024]{1,0:T(8,128)(2,1)S(1)}, bf16[32,1024]{1,0:T(8,128)(2,1)S(1)}, u32[]{:S(2)}, u32[]{:S(2)}) collective-permute-start(bf16[32,1024]{1,0:T(8,128)(2,1)S(1)} %get-tuple-element.84), channel_id=1, source_target_pairs={{0,2},{2,4},{4,6},{6,7},{7,5},{5,3},{3,1},{1,0},{8,10},{10,12},{12... | collective-permute-start | bytes 196616 | tf_op jit(solution)/shard_map/ppermute | solution.py:539
  84.7 1.9 %collective-permute-start.28 = (bf16[64,1024]{1,0:T(8,128)(2,1)S(1)}, bf16[64,1024]{1,0:T(8,128)(2,1)S(1)}, u32[]{:S(2)}, u32[]{:S(2)}) collective-permute-start(bf16[64,1024]{1,0:T(8,128)(2,1)S(1)} %pad_maximum_fusion), channel_id=1, source_target_pairs={{0,2},{2,4},{4,6},{6,7},{7,5},{5,3},{3,1},{1,0},{8,10},{10,12},{12... | collective-permute-start | bytes 393224 | tf_op jit(solution)/shard_map/ppermute | solution.py:539
  87.4 1.9 %collective-permute-start.37 = (bf16[64,1024]{1,0:T(8,128)(2,1)S(1)}, bf16[64,1024]{1,0:T(8,128)(2,1)S(1)}, u32[]{:S(2)}, u32[]{:S(2)}) collective-permute-start(bf16[64,1024]{1,0:T(8,128)(2,1)S(1)} %pad_maximum_fusion.2), channel_id=1, source_target_pairs={{0,2},{2,4},{4,6},{6,7},{7,5},{5,3},{3,1},{1,0},{8,10},{10,12},{12... | collective-permute-start | bytes 393224 | tf_op jit(solution)/shard_map/ppermute | solution.py:539
  89.7 1.4 %collective-permute-done.28 = bf16[64,1024]{1,0:T(8,128)(2,1)S(1)} collective-permute-done((bf16[64,1024]{1,0:T(8,128)(2,1)S(1)}, bf16[64,1024]{1,0:T(8,128)(2,1)S(1)}, u32[]{:S(2)}, u32[]{:S(2)}) %collective-permute-start.28) | collective-permute-done | bytes 131104 | tf_op jit(solution)/shard_map/ppermute | solution.py:539
  91.1 1.9 %collective-permute-start.29 = (bf16[64,1024]{1,0:T(8,128)(2,1)S(1)}, bf16[64,1024]{1,0:T(8,128)(2,1)S(1)}, u32[]{:S(2)}, u32[]{:S(2)}) collective-permute-start(bf16[64,1024]{1,0:T(8,128)(2,1)S(1)} %add_convert_fusion.7), channel_id=1, source_target_pairs={{0,2},{2,4},{4,6},{6,7},{7,5},{5,3},{3,1},{1,0},{8,10},{10,12},{12... | collective-permute-start | bytes 393224 | tf_op jit(solution)/shard_map/ppermute | solution.py:539
  93.9 1.9 %collective-permute-start.38 = (bf16[64,1024]{1,0:T(8,128)(2,1)S(1)}, bf16[64,1024]{1,0:T(8,128)(2,1)S(1)}, u32[]{:S(2)}, u32[]{:S(2)}) collective-permute-start(bf16[64,1024]{1,0:T(8,128)(2,1)S(1)} %add_convert_fusion.3), channel_id=1, source_target_pairs={{0,2},{2,4},{4,6},{6,7},{7,5},{5,3},{3,1},{1,0},{8,10},{10,12},{12... | collective-permute-start | bytes 393224 | tf_op jit(solution)/shard_map/ppermute | solution.py:539
  96.8 1.8 %collective-permute-start.30 = (bf16[64,1024]{1,0:T(8,128)(2,1)S(1)}, bf16[64,1024]{1,0:T(8,128)(2,1)S(1)}, u32[]{:S(2)}, u32[]{:S(2)}) collective-permute-start(bf16[64,1024]{1,0:T(8,128)(2,1)S(1)} %add_convert_fusion.6), channel_id=1, source_target_pairs={{0,2},{2,4},{4,6},{6,7},{7,5},{5,3},{3,1},{1,0},{8,10},{10,12},{12... | collective-permute-start | bytes 393224 | tf_op jit(solution)/shard_map/ppermute | solution.py:539
  98.9 1.4 %collective-permute-done.38 = bf16[64,1024]{1,0:T(8,128)(2,1)S(1)} collective-permute-done((bf16[64,1024]{1,0:T(8,128)(2,1)S(1)}, bf16[64,1024]{1,0:T(8,128)(2,1)S(1)}, u32[]{:S(2)}, u32[]{:S(2)}) %collective-permute-start.38) | collective-permute-done | bytes 131104 | tf_op jit(solution)/shard_map/ppermute | solution.py:539
  100.4 1.9 %collective-permute-start.39 = (bf16[64,1024]{1,0:T(8,128)(2,1)S(1)}, bf16[64,1024]{1,0:T(8,128)(2,1)S(1)}, u32[]{:S(2)}, u32[]{:S(2)}) collective-permute-start(bf16[64,1024]{1,0:T(8,128)(2,1)S(1)} %add_convert_fusion.2), channel_id=1, source_target_pairs={{0,2},{2,4},{4,6},{6,7},{7,5},{5,3},{3,1},{1,0},{8,10},{10,12},{12... | collective-permute-start | bytes 393224 | tf_op jit(solution)/shard_map/ppermute | solution.py:539
  102.6 1.4 %collective-permute-done.34.refs_2_ = bf16[64,1024]{1,0:T(8,128)(2,1)S(1)} collective-permute-done((bf16[64,1024]{1,0:T(8,128)(2,1)S(1)}, bf16[64,1024]{1,0:T(8,128)(2,1)S(1)}, u32[]{:S(2)}, u32[]{:S(2)}) %collective-permute-start.34) | collective-permute-done | bytes 131104 | tf_op jit(solution)/shard_map/ppermute | solution.py:539
  105.4 2.0 %collective-permute-done.43.refs_5_ = bf16[64,1024]{1,0:T(8,128)(2,1)S(1)} collective-permute-done((bf16[64,1024]{1,0:T(8,128)(2,1)S(1)}, bf16[64,1024]{1,0:T(8,128)(2,1)S(1)}, u32[]{:S(2)}, u32[]{:S(2)}) %collective-permute-start.43) | collective-permute-done | bytes 131104 | tf_op jit(solution)/shard_map/ppermute | solution.py:539
  (102 shorter events, 18.7 us)
Async XLA Ops:
  3.2 18.8 %collective-permute-start.1 = (bf16[64,5120]{1,0:T(8,128)(2,1)}, bf16[64,5120]{1,0:T(8,128)(2,1)S(1)}, u32[]{:S(2)}, u32[]{:S(2)}) collective-permute-start(bf16[64,5120]{1,0:T(8,128)(2,1)} %get-tuple-element.50), channel_id=1, source_target_pairs={{0,16},{8,24},{16,0},{24,8},{1,17},{9,25},{17,1},{25,9},{2,18},{10... | collective-permute-start | bytes 1966088 | tf_op jit(solution)/shard_map/ppermute | solution.py:529
  10.9 44.2 %collective-permute-start.19 = (bf16[384,2048]{1,0:T(8,128)(2,1)}, bf16[384,2048]{1,0:T(8,128)(2,1)S(1)}, u32[]{:S(2)}, u32[]{:S(2)}) collective-permute-start(bf16[384,2048]{1,0:T(8,128)(2,1)} %get-tuple-element.59.refs_17_), channel_id=1, source_target_pairs={{0,16},{8,24},{16,0},{24,8},{1,17},{9,25},{17,1},{25,9},{2,18},{10... | collective-permute-start | bytes 4718600 | tf_op jit(solution)/shard_map/ppermute | solution.py:529
  11.1 10.9 %collective-permute-start = (bf16[64,512]{1,0:T(8,128)(2,1)S(1)}, bf16[64,512]{1,0:T(8,128)(2,1)S(1)}, u32[]{:S(2)}, u32[]{:S(2)}) collective-permute-start(bf16[64,512]{1,0:T(8,128)(2,1)S(1)} %copy-done.8), channel_id=1, source_target_pairs={{0,8},{8,0},{16,24},{24,16},{1,9},{9,1},{17,25},{25,17},{2,10},{10... | collective-permute-start | bytes 196616 | tf_op jit(solution)/shard_map/ppermute | solution.py:529
  23.9 6.7 %collective-permute-start.3 = (bf16[32,2176]{1,0:T(8,128)(2,1)S(1)}, bf16[32,2176]{1,0:T(8,128)(2,1)S(1)}, u32[]{:S(2)}, u32[]{:S(2)}) collective-permute-start(bf16[32,2176]{1,0:T(8,128)(2,1)S(1)} %get-tuple-element.55.refs_0_), channel_id=1, source_target_pairs={{0,1},{2,0},{4,2},{6,4},{7,6},{5,7},{3,5},{1,3},{8,9},{10,8},{12,1... | collective-permute-start | bytes 417800 | tf_op jit(solution)/shard_map/ppermute | solution.py:539
  26.1 7.5 %collective-permute-start.4 = (bf16[32,2176]{1,0:T(8,128)(2,1)S(1)}, bf16[32,2176]{1,0:T(8,128)(2,1)S(1)}, u32[]{:S(2)}, u32[]{:S(2)}) collective-permute-start(bf16[32,2176]{1,0:T(8,128)(2,1)S(1)} %get-tuple-element.56.refs_1_), channel_id=1, source_target_pairs={{0,1},{2,0},{4,2},{6,4},{7,6},{5,7},{3,5},{1,3},{8,9},{10,8},{12,1... | collective-permute-start | bytes 417800 | tf_op jit(solution)/shard_map/ppermute | solution.py:539
  27.6 7.9 %collective-permute-start.10 = (bf16[32,2176]{1,0:T(8,128)(2,1)S(1)}, bf16[32,2176]{1,0:T(8,128)(2,1)S(1)}, u32[]{:S(2)}, u32[]{:S(2)}) collective-permute-start(bf16[32,2176]{1,0:T(8,128)(2,1)S(1)} %get-tuple-element.56.refs_1_), channel_id=1, source_target_pairs={{0,2},{2,4},{4,6},{6,7},{7,5},{5,3},{3,1},{1,0},{8,10},{10,12},{12... | collective-permute-start | bytes 417800 | tf_op jit(solution)/shard_map/ppermute | solution.py:539
  28.1 7.7 %collective-permute-start.14 = (bf16[32,2176]{1,0:T(8,128)(2,1)S(1)}, bf16[32,2176]{1,0:T(8,128)(2,1)S(1)}, u32[]{:S(2)}, u32[]{:S(2)}) collective-permute-start(bf16[32,2176]{1,0:T(8,128)(2,1)S(1)} %get-tuple-element.55.refs_0_), channel_id=1, source_target_pairs={{0,2},{2,4},{4,6},{6,7},{7,5},{5,3},{3,1},{1,0},{8,10},{10,12},{12... | collective-permute-start | bytes 417800 | tf_op jit(solution)/shard_map/ppermute | solution.py:539
  30.6 7.1 %collective-permute-start.5 = (bf16[32,2176]{1,0:T(8,128)(2,1)S(1)}, bf16[32,2176]{1,0:T(8,128)(2,1)S(1)}, u32[]{:S(2)}, u32[]{:S(2)}) collective-permute-start(bf16[32,2176]{1,0:T(8,128)(2,1)S(1)} %collective-permute-done.3.refs_2_), channel_id=1, source_target_pairs={{0,1},{2,0},{4,2},{6,4},{7,6},{5,7},{3,5},{1,3},{8,9},{10,8},{12,1... | collective-permute-start | bytes 417800 | tf_op jit(solution)/shard_map/ppermute | solution.py:539
  33.6 6.6 %collective-permute-start.6 = (bf16[32,2176]{1,0:T(8,128)(2,1)S(1)}, bf16[32,2176]{1,0:T(8,128)(2,1)S(1)}, u32[]{:S(2)}, u32[]{:S(2)}) collective-permute-start(bf16[32,2176]{1,0:T(8,128)(2,1)S(1)} %collective-permute-done.4.refs_3_), channel_id=1, source_target_pairs={{0,1},{2,0},{4,2},{6,4},{7,6},{5,7},{3,5},{1,3},{8,9},{10,8},{12,1... | collective-permute-start | bytes 417800 | tf_op jit(solution)/shard_map/ppermute | solution.py:539
  35.6 6.6 %collective-permute-start.11 = (bf16[32,2176]{1,0:T(8,128)(2,1)S(1)}, bf16[32,2176]{1,0:T(8,128)(2,1)S(1)}, u32[]{:S(2)}, u32[]{:S(2)}) collective-permute-start(bf16[32,2176]{1,0:T(8,128)(2,1)S(1)} %collective-permute-done.10.refs_15_), channel_id=1, source_target_pairs={{0,2},{2,4},{4,6},{6,7},{7,5},{5,3},{3,1},{1,0},{8,10},{10,12},{12... | collective-permute-start | bytes 417800 | tf_op jit(solution)/shard_map/ppermute | solution.py:539
  35.8 7.2 %collective-permute-start.15 = (bf16[32,2176]{1,0:T(8,128)(2,1)S(1)}, bf16[32,2176]{1,0:T(8,128)(2,1)S(1)}, u32[]{:S(2)}, u32[]{:S(2)}) collective-permute-start(bf16[32,2176]{1,0:T(8,128)(2,1)S(1)} %collective-permute-done.14.refs_14_), channel_id=1, source_target_pairs={{0,2},{2,4},{4,6},{6,7},{7,5},{5,3},{3,1},{1,0},{8,10},{10,12},{12... | collective-permute-start | bytes 417800 | tf_op jit(solution)/shard_map/ppermute | solution.py:539
  37.7 5.9 %collective-permute-start.7 = (bf16[32,2176]{1,0:T(8,128)(2,1)S(1)}, bf16[32,2176]{1,0:T(8,128)(2,1)S(1)}, u32[]{:S(2)}, u32[]{:S(2)}) collective-permute-start(bf16[32,2176]{1,0:T(8,128)(2,1)S(1)} %collective-permute-done.5.refs_4_), channel_id=1, source_target_pairs={{0,1},{2,0},{4,2},{6,4},{7,6},{5,7},{3,5},{1,3},{8,9},{10,8},{12,1... | collective-permute-start | bytes 417800 | tf_op jit(solution)/shard_map/ppermute | solution.py:539
  40.2 5.1 %collective-permute-start.8 = (bf16[32,2176]{1,0:T(8,128)(2,1)S(1)}, bf16[32,2176]{1,0:T(8,128)(2,1)S(1)}, u32[]{:S(2)}, u32[]{:S(2)}) collective-permute-start(bf16[32,2176]{1,0:T(8,128)(2,1)S(1)} %collective-permute-done.6.refs_5_), channel_id=1, source_target_pairs={{0,1},{2,0},{4,2},{6,4},{7,6},{5,7},{3,5},{1,3},{8,9},{10,8},{12,1... | collective-permute-start | bytes 417800 | tf_op jit(solution)/shard_map/ppermute | solution.py:539
  42.2 6.2 %collective-permute-start.12 = (bf16[32,2176]{1,0:T(8,128)(2,1)S(1)}, bf16[32,2176]{1,0:T(8,128)(2,1)S(1)}, u32[]{:S(2)}, u32[]{:S(2)}) collective-permute-start(bf16[32,2176]{1,0:T(8,128)(2,1)S(1)} %collective-permute-done.11.refs_13_), channel_id=1, source_target_pairs={{0,2},{2,4},{4,6},{6,7},{7,5},{5,3},{3,1},{1,0},{8,10},{10,12},{12... | collective-permute-start | bytes 417800 | tf_op jit(solution)/shard_map/ppermute | solution.py:539
  43.0 16.7 %collective-permute-start.18 = (bf16[384,2048]{1,0:T(8,128)(2,1)}, bf16[384,2048]{1,0:T(8,128)(2,1)S(1)}, u32[]{:S(2)}, u32[]{:S(2)}) collective-permute-start(bf16[384,2048]{1,0:T(8,128)(2,1)} %get-tuple-element.59.refs_17_), channel_id=1, source_target_pairs={{0,8},{8,0},{16,24},{24,16},{1,9},{9,1},{17,25},{25,17},{2,10},{10... | collective-permute-start | bytes 4718600 | tf_op jit(solution)/shard_map/ppermute | solution.py:529
  43.6 7.8 %collective-permute-start.16 = (bf16[32,2176]{1,0:T(8,128)(2,1)S(1)}, bf16[32,2176]{1,0:T(8,128)(2,1)S(1)}, u32[]{:S(2)}, u32[]{:S(2)}) collective-permute-start(bf16[32,2176]{1,0:T(8,128)(2,1)S(1)} %collective-permute-done.15.refs_12_), channel_id=1, source_target_pairs={{0,2},{2,4},{4,6},{6,7},{7,5},{5,3},{3,1},{1,0},{8,10},{10,12},{12... | collective-permute-start | bytes 417800 | tf_op jit(solution)/shard_map/ppermute | solution.py:539
  45.3 6.1 %collective-permute-start.9 = (bf16[32,2176]{1,0:T(8,128)(2,1)S(1)}, bf16[32,2176]{1,0:T(8,128)(2,1)S(1)}, u32[]{:S(2)}, u32[]{:S(2)}) collective-permute-start(bf16[32,2176]{1,0:T(8,128)(2,1)S(1)} %collective-permute-done.7.refs_6_), channel_id=1, source_target_pairs={{0,1},{2,0},{4,2},{6,4},{7,6},{5,7},{3,5},{1,3},{8,9},{10,8},{12,1... | collective-permute-start | bytes 417800 | tf_op jit(solution)/shard_map/ppermute | solution.py:539
  48.4 5.1 %collective-permute-start.13 = (bf16[32,2176]{1,0:T(8,128)(2,1)S(1)}, bf16[32,2176]{1,0:T(8,128)(2,1)S(1)}, u32[]{:S(2)}, u32[]{:S(2)}) collective-permute-start(bf16[32,2176]{1,0:T(8,128)(2,1)S(1)} %collective-permute-done.12.refs_11_), channel_id=1, source_target_pairs={{0,2},{2,4},{4,6},{6,7},{7,5},{5,3},{3,1},{1,0},{8,10},{10,12},{12... | collective-permute-start | bytes 417800 | tf_op jit(solution)/shard_map/ppermute | solution.py:539
  53.5 23.9 %collective-permute-start.25 = (bf16[256,2048]{1,0:T(8,128)(2,1)S(1)}, bf16[256,2048]{1,0:T(8,128)(2,1)S(1)}, u32[]{:S(2)}, u32[]{:S(2)}) collective-permute-start(bf16[256,2048]{1,0:T(8,128)(2,1)S(1)} %copy-done.1), channel_id=1, source_target_pairs={{0,16},{8,24},{16,0},{24,8},{1,17},{9,25},{17,1},{25,9},{2,18},{10... | collective-permute-start | bytes 3145736 | tf_op jit(solution)/shard_map/ppermute | solution.py:529
  59.5 18.5 %collective-permute-start.24 = (bf16[256,2048]{1,0:T(8,128)(2,1)S(1)}, bf16[256,2048]{1,0:T(8,128)(2,1)S(1)}, u32[]{:S(2)}, u32[]{:S(2)}) collective-permute-start(bf16[256,2048]{1,0:T(8,128)(2,1)S(1)} %copy-done.1), channel_id=1, source_target_pairs={{0,8},{8,0},{16,24},{24,16},{1,9},{9,1},{17,25},{25,17},{2,10},{10... | collective-permute-start | bytes 3145736 | tf_op jit(solution)/shard_map/ppermute | solution.py:529
  84.7 6.4 %collective-permute-start.28 = (bf16[64,1024]{1,0:T(8,128)(2,1)S(1)}, bf16[64,1024]{1,0:T(8,128)(2,1)S(1)}, u32[]{:S(2)}, u32[]{:S(2)}) collective-permute-start(bf16[64,1024]{1,0:T(8,128)(2,1)S(1)} %pad_maximum_fusion), channel_id=1, source_target_pairs={{0,2},{2,4},{4,6},{6,7},{7,5},{5,3},{3,1},{1,0},{8,10},{10,12},{12... | collective-permute-start | bytes 393224 | tf_op jit(solution)/shard_map/ppermute | solution.py:539
  86.6 6.4 %collective-permute-start.32 = (bf16[64,1024]{1,0:T(8,128)(2,1)S(1)}, bf16[64,1024]{1,0:T(8,128)(2,1)S(1)}, u32[]{:S(2)}, u32[]{:S(2)}) collective-permute-start(bf16[64,1024]{1,0:T(8,128)(2,1)S(1)} %pad_maximum_fusion.1), channel_id=1, source_target_pairs={{0,1},{2,0},{4,2},{6,4},{7,6},{5,7},{3,5},{1,3},{8,9},{10,8},{12,1... | collective-permute-start | bytes 393224 | tf_op jit(solution)/shard_map/ppermute | solution.py:539
  87.4 6.5 %collective-permute-start.37 = (bf16[64,1024]{1,0:T(8,128)(2,1)S(1)}, bf16[64,1024]{1,0:T(8,128)(2,1)S(1)}, u32[]{:S(2)}, u32[]{:S(2)}) collective-permute-start(bf16[64,1024]{1,0:T(8,128)(2,1)S(1)} %pad_maximum_fusion.2), channel_id=1, source_target_pairs={{0,2},{2,4},{4,6},{6,7},{7,5},{5,3},{3,1},{1,0},{8,10},{10,12},{12... | collective-permute-start | bytes 393224 | tf_op jit(solution)/shard_map/ppermute | solution.py:539
  89.4 6.4 %collective-permute-start.41 = (bf16[64,1024]{1,0:T(8,128)(2,1)S(1)}, bf16[64,1024]{1,0:T(8,128)(2,1)S(1)}, u32[]{:S(2)}, u32[]{:S(2)}) collective-permute-start(bf16[64,1024]{1,0:T(8,128)(2,1)S(1)} %pad_maximum_fusion.3), channel_id=1, source_target_pairs={{0,1},{2,0},{4,2},{6,4},{7,6},{5,7},{3,5},{1,3},{8,9},{10,8},{12,1... | collective-permute-start | bytes 393224 | tf_op jit(solution)/shard_map/ppermute | solution.py:539
  91.1 5.6 %collective-permute-start.29 = (bf16[64,1024]{1,0:T(8,128)(2,1)S(1)}, bf16[64,1024]{1,0:T(8,128)(2,1)S(1)}, u32[]{:S(2)}, u32[]{:S(2)}) collective-permute-start(bf16[64,1024]{1,0:T(8,128)(2,1)S(1)} %add_convert_fusion.7), channel_id=1, source_target_pairs={{0,2},{2,4},{4,6},{6,7},{7,5},{5,3},{3,1},{1,0},{8,10},{10,12},{12... | collective-permute-start | bytes 393224 | tf_op jit(solution)/shard_map/ppermute | solution.py:539
  93.0 5.6 %collective-permute-start.33 = (bf16[64,1024]{1,0:T(8,128)(2,1)S(1)}, bf16[64,1024]{1,0:T(8,128)(2,1)S(1)}, u32[]{:S(2)}, u32[]{:S(2)}) collective-permute-start(bf16[64,1024]{1,0:T(8,128)(2,1)S(1)} %add_convert_fusion.5), channel_id=1, source_target_pairs={{0,1},{2,0},{4,2},{6,4},{7,6},{5,7},{3,5},{1,3},{8,9},{10,8},{12,1... | collective-permute-start | bytes 393224 | tf_op jit(solution)/shard_map/ppermute | solution.py:539
  93.9 6.4 %collective-permute-start.38 = (bf16[64,1024]{1,0:T(8,128)(2,1)S(1)}, bf16[64,1024]{1,0:T(8,128)(2,1)S(1)}, u32[]{:S(2)}, u32[]{:S(2)}) collective-permute-start(bf16[64,1024]{1,0:T(8,128)(2,1)S(1)} %add_convert_fusion.3), channel_id=1, source_target_pairs={{0,2},{2,4},{4,6},{6,7},{7,5},{5,3},{3,1},{1,0},{8,10},{10,12},{12... | collective-permute-start | bytes 393224 | tf_op jit(solution)/shard_map/ppermute | solution.py:539
  95.9 6.5 %collective-permute-start.42 = (bf16[64,1024]{1,0:T(8,128)(2,1)S(1)}, bf16[64,1024]{1,0:T(8,128)(2,1)S(1)}, u32[]{:S(2)}, u32[]{:S(2)}) collective-permute-start(bf16[64,1024]{1,0:T(8,128)(2,1)S(1)} %add_convert_fusion.1), channel_id=1, source_target_pairs={{0,1},{2,0},{4,2},{6,4},{7,6},{5,7},{3,5},{1,3},{8,9},{10,8},{12,1... | collective-permute-start | bytes 393224 | tf_op jit(solution)/shard_map/ppermute | solution.py:539
  96.8 5.9 %collective-permute-start.30 = (bf16[64,1024]{1,0:T(8,128)(2,1)S(1)}, bf16[64,1024]{1,0:T(8,128)(2,1)S(1)}, u32[]{:S(2)}, u32[]{:S(2)}) collective-permute-start(bf16[64,1024]{1,0:T(8,128)(2,1)S(1)} %add_convert_fusion.6), channel_id=1, source_target_pairs={{0,2},{2,4},{4,6},{6,7},{7,5},{5,3},{3,1},{1,0},{8,10},{10,12},{12... | collective-permute-start | bytes 393224 | tf_op jit(solution)/shard_map/ppermute | solution.py:539
  98.6 5.4 %collective-permute-start.34 = (bf16[64,1024]{1,0:T(8,128)(2,1)S(1)}, bf16[64,1024]{1,0:T(8,128)(2,1)S(1)}, u32[]{:S(2)}, u32[]{:S(2)}) collective-permute-start(bf16[64,1024]{1,0:T(8,128)(2,1)S(1)} %add_convert_fusion.4), channel_id=1, source_target_pairs={{0,1},{2,0},{4,2},{6,4},{7,6},{5,7},{3,5},{1,3},{8,9},{10,8},{12,1... | collective-permute-start | bytes 393224 | tf_op jit(solution)/shard_map/ppermute | solution.py:539
  100.4 5.0 %collective-permute-start.39 = (bf16[64,1024]{1,0:T(8,128)(2,1)S(1)}, bf16[64,1024]{1,0:T(8,128)(2,1)S(1)}, u32[]{:S(2)}, u32[]{:S(2)}) collective-permute-start(bf16[64,1024]{1,0:T(8,128)(2,1)S(1)} %add_convert_fusion.2), channel_id=1, source_target_pairs={{0,2},{2,4},{4,6},{6,7},{7,5},{5,3},{3,1},{1,0},{8,10},{10,12},{12... | collective-permute-start | bytes 393224 | tf_op jit(solution)/shard_map/ppermute | solution.py:539
  102.4 5.0 %collective-permute-start.43 = (bf16[64,1024]{1,0:T(8,128)(2,1)S(1)}, bf16[64,1024]{1,0:T(8,128)(2,1)S(1)}, u32[]{:S(2)}, u32[]{:S(2)}) collective-permute-start(bf16[64,1024]{1,0:T(8,128)(2,1)S(1)} %add_convert_fusion), channel_id=1, source_target_pairs={{0,1},{2,0},{4,2},{6,4},{7,6},{5,7},{3,5},{1,3},{8,9},{10,8},{12,1... | collective-permute-start | bytes 393224 | tf_op jit(solution)/shard_map/ppermute | solution.py:539
  (21 other events, 243.7 us)

commit v19 on v18

--- a/solution.py
+++ b/solution.py
@@ -478,17 +478,14 @@
 
 
 def down_kernel(first, column, sources, hidden_ref, total_ref, gate_ref, piece, *refs):
-    outs, (weights, arrived) = refs[:-2], refs[-2:]
-    start_rows([piece], weights, arrived)
-    wait_rows([piece], weights, arrived)
-    depth, width = weights.shape
+    depth, width = piece.shape
     units = hidden_ref[:, first : first + depth]
     total = total_ref[:, column : column + width] + jnp.dot(
-        units, weights[...], preferred_element_type=jnp.float32
+        units, piece[...], preferred_element_type=jnp.float32
     )
     weighted = (total * gate_ref[...]).astype(jnp.bfloat16)
     rows = weighted.shape[0] // sources
-    for (first, count), ref in zip(down_blocks(rows, sources), outs):
+    for (first, count), ref in zip(down_blocks(rows, sources), refs):
         ref[...] = weighted[first : first + count]
 
 
@@ -513,12 +510,8 @@
             jax.ShapeDtypeStruct((count, width), jnp.bfloat16)
             for _, count in down_blocks(rows, sources)
         ],
-        in_specs=vmem(3) + [pl.BlockSpec(memory_space=pl.ANY)],
+        in_specs=vmem(4),
         out_specs=vmem(sources + 3),
-        scratch_shapes=[
-            pltpu.VMEM((depth, width), jnp.bfloat16),
-            pltpu.SemaphoreType.DMA((1,)),
-        ],
         compiler_params=params(),
         cost_estimate=SMALL,
         name="expert_down",

time: 108 us -> 108 us (level)
  no operation moved by 1% of the time
where the time goes in v19:
time: 108 us
  waiting for transfers between devices  45.9 us (42%)
  starting transfers between devices  40.6 us (38%)
  Pallas kernels  20.6 us (19%)
    ppermute x30, starting transfers between devices, around(): lax.ppermute(x, 'expert', [(ring[i], ring[(i + step) % count]) for i in r...  34.1 us
    ppermute x14, waiting for transfers between devices, partner(): return lax.ppermute(x, 'dp', [(i, i ^ distance) for i in range(4)])  24.6 us
    ppermute x30, waiting for transfers between devices, around(): lax.ppermute(x, 'expert', [(ring[i], ring[(i + step) % count]) for i in r...  21.3 us
    pallas_call x1, Pallas kernels, expert_up(): pl.pallas_call(lambda *refs: up_kernel(len(rows), starts, *refs), out_sha...  8.91 us
    ppermute x14, starting transfers between devices, partner(): return lax.ppermute(x, 'dp', [(i, i ^ distance) for i in range(4)])  6.52 us
    pallas_call x1, Pallas kernels, cast_rows(): pl.pallas_call(lambda *refs: cast_kernel(spans, *refs), out_shape=[jax.Sh...  4.68 us
    pallas_call x1, Pallas kernels, attention(): pl.pallas_call(attention_kernel, out_shape=[jax.ShapeDtypeStruct(shape, j...  3.2 us
  transfers between devices with their start and end apart: 44, of which 23 were waited for; matrix products, arithmetic and copies ran while one was open for 1% of the time, Pallas kernels for 15%

profile of v19, /device:TPU:0, one launch (start us, length us, event | category | flops | bytes accessed | tf_op | source)
XLA Modules:
  0.0 108.1 jit_solution(2417717158602902171)
XLA Ops:
  0.0 3.2 %attention.1 = (bf16[64,512]{1,0:T(8,128)(2,1)}, bf16[64,512]{1,0:T(8,128)(2,1)}, bf16[64,5120]{1,0:T(8,128)(2,1)}) custom-call(s32[1,2]{1,0:T(1,128)} %refs_0_.1, s32[1,4]{1,0:T(1,128)} %refs_1_.1, bf16[1,256,512]{2,1,0:T(8,128)(2,1)} %refs_2_.2, bf16[2,128,512]{2,1,0:T(8,128)(2,1)} %refs_3_.1, bf16[2,128,512]{2,1,0:T(8,128)(2,1)} %refs_4_.1, ...), custom_call_target="tpu_custom_call" | custom-call | tf_op jit(solution)/shard_map/attention/pallas_call | solution.py:201
  3.2 3.0 %collective-permute-start.1 = (bf16[64,5120]{1,0:T(8,128)(2,1)}, bf16[64,5120]{1,0:T(8,128)(2,1)S(1)}, u32[]{:S(2)}, u32[]{:S(2)}) collective-permute-start(bf16[64,5120]{1,0:T(8,128)(2,1)} %get-tuple-element.50), channel_id=1, source_target_pairs={{0,16},{8,24},{16,0},{24,8},{1,17},{9,25},{17,1},{25,9},{2,18},{10... | collective-permute-start | bytes 1966088 | tf_op jit(solution)/shard_map/ppermute | solution.py:522
  6.2 4.7 %cast_rows.1 = (bf16[384,2048]{1,0:T(8,128)(2,1)}, bf16[128,2048]{1,0:T(8,128)(2,1)}, bf16[256,2048]{1,0:T(8,128)(2,1)}) custom-call(f32[1,512,2048]{2,1,0:T(8,128)} %refs_1_.2, f32[1,512,2048]{2,1,0:T(8,128)} %refs_1_.2, f32[1,256,2048]{2,1,0:T(8,128)} %refs_2_.3), custom_call_target="tpu_custom_call" | custom-call | tf_op jit(solution)/shard_map/cast_rows/pallas_call | solution.py:327
  11.1 10.9 %collective-permute-done.1.refs_2_.refs_20_.refs_21_ = bf16[64,5120]{1,0:T(8,128)(2,1)S(1)} collective-permute-done((bf16[64,5120]{1,0:T(8,128)(2,1)}, bf16[64,5120]{1,0:T(8,128)(2,1)S(1)}, u32[]{:S(2)}, u32[]{:S(2)}) %collective-permute-start.1) | collective-permute-done | bytes 655392 | tf_op jit(solution)/shard_map/ppermute | solution.py:522
  23.9 2.1 %collective-permute-start.3 = (bf16[32,2176]{1,0:T(8,128)(2,1)S(1)}, bf16[32,2176]{1,0:T(8,128)(2,1)S(1)}, u32[]{:S(2)}, u32[]{:S(2)}) collective-permute-start(bf16[32,2176]{1,0:T(8,128)(2,1)S(1)} %get-tuple-element.55.refs_0_), channel_id=1, source_target_pairs={{0,1},{2,0},{4,2},{6,4},{7,6},{5,7},{3,5},{1,3},{8,9},{10,8},{12,1... | collective-permute-start | bytes 417800 | tf_op jit(solution)/shard_map/ppermute | solution.py:532
  26.1 1.6 %collective-permute-start.4 = (bf16[32,2176]{1,0:T(8,128)(2,1)S(1)}, bf16[32,2176]{1,0:T(8,128)(2,1)S(1)}, u32[]{:S(2)}, u32[]{:S(2)}) collective-permute-start(bf16[32,2176]{1,0:T(8,128)(2,1)S(1)} %get-tuple-element.56.refs_1_), channel_id=1, source_target_pairs={{0,1},{2,0},{4,2},{6,4},{7,6},{5,7},{3,5},{1,3},{8,9},{10,8},{12,1... | collective-permute-start | bytes 417800 | tf_op jit(solution)/shard_map/ppermute | solution.py:532
  28.2 2.3 %collective-permute-done.3.refs_2_ = bf16[32,2176]{1,0:T(8,128)(2,1)S(1)} collective-permute-done((bf16[32,2176]{1,0:T(8,128)(2,1)S(1)}, bf16[32,2176]{1,0:T(8,128)(2,1)S(1)}, u32[]{:S(2)}, u32[]{:S(2)}) %collective-permute-start.3) | collective-permute-done | bytes 139296 | tf_op jit(solution)/shard_map/ppermute | solution.py:532
  30.6 2.0 %collective-permute-start.5 = (bf16[32,2176]{1,0:T(8,128)(2,1)S(1)}, bf16[32,2176]{1,0:T(8,128)(2,1)S(1)}, u32[]{:S(2)}, u32[]{:S(2)}) collective-permute-start(bf16[32,2176]{1,0:T(8,128)(2,1)S(1)} %collective-permute-done.3.refs_2_), channel_id=1, source_target_pairs={{0,1},{2,0},{4,2},{6,4},{7,6},{5,7},{3,5},{1,3},{8,9},{10,8},{12,1... | collective-permute-start | bytes 417800 | tf_op jit(solution)/shard_map/ppermute | solution.py:532
  33.6 2.0 %collective-permute-start.6 = (bf16[32,2176]{1,0:T(8,128)(2,1)S(1)}, bf16[32,2176]{1,0:T(8,128)(2,1)S(1)}, u32[]{:S(2)}, u32[]{:S(2)}) collective-permute-start(bf16[32,2176]{1,0:T(8,128)(2,1)S(1)} %collective-permute-done.4.refs_3_), channel_id=1, source_target_pairs={{0,1},{2,0},{4,2},{6,4},{7,6},{5,7},{3,5},{1,3},{8,9},{10,8},{12,1... | collective-permute-start | bytes 417800 | tf_op jit(solution)/shard_map/ppermute | solution.py:532
  35.8 1.9 %collective-permute-start.15 = (bf16[32,2176]{1,0:T(8,128)(2,1)S(1)}, bf16[32,2176]{1,0:T(8,128)(2,1)S(1)}, u32[]{:S(2)}, u32[]{:S(2)}) collective-permute-start(bf16[32,2176]{1,0:T(8,128)(2,1)S(1)} %collective-permute-done.14.refs_14_), channel_id=1, source_target_pairs={{0,2},{2,4},{4,6},{6,7},{7,5},{5,3},{3,1},{1,0},{8,10},{10,12},{12... | collective-permute-start | bytes 417800 | tf_op jit(solution)/shard_map/ppermute | solution.py:532
  40.2 2.0 %collective-permute-start.8 = (bf16[32,2176]{1,0:T(8,128)(2,1)S(1)}, bf16[32,2176]{1,0:T(8,128)(2,1)S(1)}, u32[]{:S(2)}, u32[]{:S(2)}) collective-permute-start(bf16[32,2176]{1,0:T(8,128)(2,1)S(1)} %collective-permute-done.6.refs_5_), channel_id=1, source_target_pairs={{0,1},{2,0},{4,2},{6,4},{7,6},{5,7},{3,5},{1,3},{8,9},{10,8},{12,1... | collective-permute-start | bytes 417800 | tf_op jit(solution)/shard_map/ppermute | solution.py:532
  43.6 1.7 %collective-permute-start.16 = (bf16[32,2176]{1,0:T(8,128)(2,1)S(1)}, bf16[32,2176]{1,0:T(8,128)(2,1)S(1)}, u32[]{:S(2)}, u32[]{:S(2)}) collective-permute-start(bf16[32,2176]{1,0:T(8,128)(2,1)S(1)} %collective-permute-done.15.refs_12_), channel_id=1, source_target_pairs={{0,2},{2,4},{4,6},{6,7},{7,5},{5,3},{3,1},{1,0},{8,10},{10,12},{12... | collective-permute-start | bytes 417800 | tf_op jit(solution)/shard_map/ppermute | solution.py:532
  45.3 2.0 %collective-permute-start.9 = (bf16[32,2176]{1,0:T(8,128)(2,1)S(1)}, bf16[32,2176]{1,0:T(8,128)(2,1)S(1)}, u32[]{:S(2)}, u32[]{:S(2)}) collective-permute-start(bf16[32,2176]{1,0:T(8,128)(2,1)S(1)} %collective-permute-done.7.refs_6_), channel_id=1, source_target_pairs={{0,1},{2,0},{4,2},{6,4},{7,6},{5,7},{3,5},{1,3},{8,9},{10,8},{12,1... | collective-permute-start | bytes 417800 | tf_op jit(solution)/shard_map/ppermute | solution.py:532
  48.4 2.9 %collective-permute-done.16.refs_10_ = bf16[32,2176]{1,0:T(8,128)(2,1)S(1)} collective-permute-done((bf16[32,2176]{1,0:T(8,128)(2,1)S(1)}, bf16[32,2176]{1,0:T(8,128)(2,1)S(1)}, u32[]{:S(2)}, u32[]{:S(2)}) %collective-permute-start.16) | collective-permute-done | bytes 139296 | tf_op jit(solution)/shard_map/ppermute | solution.py:532
  51.9 1.6 %collective-permute-done.13.refs_9_ = bf16[32,2176]{1,0:T(8,128)(2,1)S(1)} collective-permute-done((bf16[32,2176]{1,0:T(8,128)(2,1)S(1)}, bf16[32,2176]{1,0:T(8,128)(2,1)S(1)}, u32[]{:S(2)}, u32[]{:S(2)}) %collective-permute-start.13) | collective-permute-done | bytes 139296 | tf_op jit(solution)/shard_map/ppermute | solution.py:532
  53.5 1.5 %collective-permute-start.25 = (bf16[256,2048]{1,0:T(8,128)(2,1)S(1)}, bf16[256,2048]{1,0:T(8,128)(2,1)S(1)}, u32[]{:S(2)}, u32[]{:S(2)}) collective-permute-start(bf16[256,2048]{1,0:T(8,128)(2,1)S(1)} %copy-done.1), channel_id=1, source_target_pairs={{0,16},{8,24},{16,0},{24,8},{1,17},{9,25},{17,1},{25,9},{2,18},{10... | collective-permute-start | bytes 3145736 | tf_op jit(solution)/shard_map/ppermute | solution.py:522
  55.9 3.6 %collective-permute-done.17.refs_18_ = bf16[128,2048]{1,0:T(8,128)(2,1)S(1)} collective-permute-done((bf16[128,2048]{1,0:T(8,128)(2,1)S(1)}, bf16[128,2048]{1,0:T(8,128)(2,1)S(1)}, u32[]{:S(2)}, u32[]{:S(2)}) %collective-permute-start.17) | collective-permute-done | bytes 524320 | tf_op jit(solution)/shard_map/ppermute | solution.py:522
  59.7 8.9 %expert_up.1 = (bf16[512,1024]{1,0:T(8,128)(2,1)S(1)}, f32[512,1]{1,0:T(8,128)S(1)}, f32[512,2048]{1,0:T(8,128)S(1)}) custom-call(bf16[32,2176]{1,0:T(8,128)(2,1)S(1)} %get-tuple-element.55.refs_0_, bf16[32,2176]{1,0:T(8,128)(2,1)S(1)} %get-tuple-element.56.refs_1_, bf16[32,2176]{1,0:T(8,128)(2,1)S(1)} %collective-permute-done.3.refs_2_, ...), custom_call_target="tpu_custom_call" | custom-call | flops 1 | bytes 1 | tf_op jit(solution)/shard_map/expert_up/pallas_call | solution.py:430
  68.6 8.8 %collective-permute-done.25.refs_3_ = bf16[256,2048]{1,0:T(8,128)(2,1)S(1)} collective-permute-done((bf16[256,2048]{1,0:T(8,128)(2,1)S(1)}, bf16[256,2048]{1,0:T(8,128)(2,1)S(1)}, u32[]{:S(2)}, u32[]{:S(2)}) %collective-permute-start.25) | collective-permute-done | bytes 1048608 | tf_op jit(solution)/shard_map/ppermute | solution.py:522
  78.0 1.4 %down_part.1.refs_1_ = f32[512,2048]{1,0:T(8,128)S(1)} custom-call(bf16[512,1024]{1,0:T(8,128)(2,1)S(1)} %get-tuple-element.63.refs_0_, f32[512,2048]{1,0:T(8,128)S(1)} %get-tuple-element.64.refs_1_, bf16[256,2048]{1,0:T(8,128)(2,1)S(1)} %collective-permute-done.24.refs_2_, bf16[256,2048]{1,0:T(8,128)(2,1)S(1)} %collective-permute-done.25.refs_3_), custom_call_target="tpu_custom_call" | custom-call | flops 1 | bytes 1 | tf_op jit(solution)/shard_map/down_part/pallas_call | solution.py:465
  79.9 1.9 %collective-permute-start.27 = (bf16[32,1024]{1,0:T(8,128)(2,1)S(1)}, bf16[32,1024]{1,0:T(8,128)(2,1)S(1)}, u32[]{:S(2)}, u32[]{:S(2)}) collective-permute-start(bf16[32,1024]{1,0:T(8,128)(2,1)S(1)} %get-tuple-element.73), channel_id=1, source_target_pairs={{0,2},{2,4},{4,6},{6,7},{7,5},{5,3},{3,1},{1,0},{8,10},{10,12},{12... | collective-permute-start | bytes 196616 | tf_op jit(solution)/shard_map/ppermute | solution.py:532
  82.4 1.9 %collective-permute-start.36 = (bf16[32,1024]{1,0:T(8,128)(2,1)S(1)}, bf16[32,1024]{1,0:T(8,128)(2,1)S(1)}, u32[]{:S(2)}, u32[]{:S(2)}) collective-permute-start(bf16[32,1024]{1,0:T(8,128)(2,1)S(1)} %get-tuple-element.84), channel_id=1, source_target_pairs={{0,2},{2,4},{4,6},{6,7},{7,5},{5,3},{3,1},{1,0},{8,10},{10,12},{12... | collective-permute-start | bytes 196616 | tf_op jit(solution)/shard_map/ppermute | solution.py:532
  84.6 1.9 %collective-permute-start.28 = (bf16[64,1024]{1,0:T(8,128)(2,1)S(1)}, bf16[64,1024]{1,0:T(8,128)(2,1)S(1)}, u32[]{:S(2)}, u32[]{:S(2)}) collective-permute-start(bf16[64,1024]{1,0:T(8,128)(2,1)S(1)} %pad_maximum_fusion), channel_id=1, source_target_pairs={{0,2},{2,4},{4,6},{6,7},{7,5},{5,3},{3,1},{1,0},{8,10},{10,12},{12... | collective-permute-start | bytes 393224 | tf_op jit(solution)/shard_map/ppermute | solution.py:532
  87.3 1.9 %collective-permute-start.37 = (bf16[64,1024]{1,0:T(8,128)(2,1)S(1)}, bf16[64,1024]{1,0:T(8,128)(2,1)S(1)}, u32[]{:S(2)}, u32[]{:S(2)}) collective-permute-start(bf16[64,1024]{1,0:T(8,128)(2,1)S(1)} %pad_maximum_fusion.2), channel_id=1, source_target_pairs={{0,2},{2,4},{4,6},{6,7},{7,5},{5,3},{3,1},{1,0},{8,10},{10,12},{12... | collective-permute-start | bytes 393224 | tf_op jit(solution)/shard_map/ppermute | solution.py:532
  89.6 1.4 %collective-permute-done.28 = bf16[64,1024]{1,0:T(8,128)(2,1)S(1)} collective-permute-done((bf16[64,1024]{1,0:T(8,128)(2,1)S(1)}, bf16[64,1024]{1,0:T(8,128)(2,1)S(1)}, u32[]{:S(2)}, u32[]{:S(2)}) %collective-permute-start.28) | collective-permute-done | bytes 131104 | tf_op jit(solution)/shard_map/ppermute | solution.py:532
  91.0 1.9 %collective-permute-start.29 = (bf16[64,1024]{1,0:T(8,128)(2,1)S(1)}, bf16[64,1024]{1,0:T(8,128)(2,1)S(1)}, u32[]{:S(2)}, u32[]{:S(2)}) collective-permute-start(bf16[64,1024]{1,0:T(8,128)(2,1)S(1)} %add_convert_fusion.7), channel_id=1, source_target_pairs={{0,2},{2,4},{4,6},{6,7},{7,5},{5,3},{3,1},{1,0},{8,10},{10,12},{12... | collective-permute-start | bytes 393224 | tf_op jit(solution)/shard_map/ppermute | solution.py:532
  93.8 1.9 %collective-permute-start.38 = (bf16[64,1024]{1,0:T(8,128)(2,1)S(1)}, bf16[64,1024]{1,0:T(8,128)(2,1)S(1)}, u32[]{:S(2)}, u32[]{:S(2)}) collective-permute-start(bf16[64,1024]{1,0:T(8,128)(2,1)S(1)} %add_convert_fusion.3), channel_id=1, source_target_pairs={{0,2},{2,4},{4,6},{6,7},{7,5},{5,3},{3,1},{1,0},{8,10},{10,12},{12... | collective-permute-start | bytes 393224 | tf_op jit(solution)/shard_map/ppermute | solution.py:532
  96.6 1.8 %collective-permute-start.30 = (bf16[64,1024]{1,0:T(8,128)(2,1)S(1)}, bf16[64,1024]{1,0:T(8,128)(2,1)S(1)}, u32[]{:S(2)}, u32[]{:S(2)}) collective-permute-start(bf16[64,1024]{1,0:T(8,128)(2,1)S(1)} %add_convert_fusion.6), channel_id=1, source_target_pairs={{0,2},{2,4},{4,6},{6,7},{7,5},{5,3},{3,1},{1,0},{8,10},{10,12},{12... | collective-permute-start | bytes 393224 | tf_op jit(solution)/shard_map/ppermute | solution.py:532
  98.8 1.4 %collective-permute-done.38 = bf16[64,1024]{1,0:T(8,128)(2,1)S(1)} collective-permute-done((bf16[64,1024]{1,0:T(8,128)(2,1)S(1)}, bf16[64,1024]{1,0:T(8,128)(2,1)S(1)}, u32[]{:S(2)}, u32[]{:S(2)}) %collective-permute-start.38) | collective-permute-done | bytes 131104 | tf_op jit(solution)/shard_map/ppermute | solution.py:532
  100.3 1.9 %collective-permute-start.39 = (bf16[64,1024]{1,0:T(8,128)(2,1)S(1)}, bf16[64,1024]{1,0:T(8,128)(2,1)S(1)}, u32[]{:S(2)}, u32[]{:S(2)}) collective-permute-start(bf16[64,1024]{1,0:T(8,128)(2,1)S(1)} %add_convert_fusion.2), channel_id=1, source_target_pairs={{0,2},{2,4},{4,6},{6,7},{7,5},{5,3},{3,1},{1,0},{8,10},{10,12},{12... | collective-permute-start | bytes 393224 | tf_op jit(solution)/shard_map/ppermute | solution.py:532
  102.5 1.4 %collective-permute-done.34.refs_2_ = bf16[64,1024]{1,0:T(8,128)(2,1)S(1)} collective-permute-done((bf16[64,1024]{1,0:T(8,128)(2,1)S(1)}, bf16[64,1024]{1,0:T(8,128)(2,1)S(1)}, u32[]{:S(2)}, u32[]{:S(2)}) %collective-permute-start.34) | collective-permute-done | bytes 131104 | tf_op jit(solution)/shard_map/ppermute | solution.py:532
  105.3 2.0 %collective-permute-done.43.refs_5_ = bf16[64,1024]{1,0:T(8,128)(2,1)S(1)} collective-permute-done((bf16[64,1024]{1,0:T(8,128)(2,1)S(1)}, bf16[64,1024]{1,0:T(8,128)(2,1)S(1)}, u32[]{:S(2)}, u32[]{:S(2)}) %collective-permute-start.43) | collective-permute-done | bytes 131104 | tf_op jit(solution)/shard_map/ppermute | solution.py:532
  (102 shorter events, 18.6 us)
Async XLA Ops:
  3.2 18.8 %collective-permute-start.1 = (bf16[64,5120]{1,0:T(8,128)(2,1)}, bf16[64,5120]{1,0:T(8,128)(2,1)S(1)}, u32[]{:S(2)}, u32[]{:S(2)}) collective-permute-start(bf16[64,5120]{1,0:T(8,128)(2,1)} %get-tuple-element.50), channel_id=1, source_target_pairs={{0,16},{8,24},{16,0},{24,8},{1,17},{9,25},{17,1},{25,9},{2,18},{10... | collective-permute-start | bytes 1966088 | tf_op jit(solution)/shard_map/ppermute | solution.py:522
  10.9 44.2 %collective-permute-start.19 = (bf16[384,2048]{1,0:T(8,128)(2,1)}, bf16[384,2048]{1,0:T(8,128)(2,1)S(1)}, u32[]{:S(2)}, u32[]{:S(2)}) collective-permute-start(bf16[384,2048]{1,0:T(8,128)(2,1)} %get-tuple-element.59.refs_17_), channel_id=1, source_target_pairs={{0,16},{8,24},{16,0},{24,8},{1,17},{9,25},{17,1},{25,9},{2,18},{10... | collective-permute-start | bytes 4718600 | tf_op jit(solution)/shard_map/ppermute | solution.py:522
  11.1 10.9 %collective-permute-start = (bf16[64,512]{1,0:T(8,128)(2,1)S(1)}, bf16[64,512]{1,0:T(8,128)(2,1)S(1)}, u32[]{:S(2)}, u32[]{:S(2)}) collective-permute-start(bf16[64,512]{1,0:T(8,128)(2,1)S(1)} %copy-done.8), channel_id=1, source_target_pairs={{0,8},{8,0},{16,24},{24,16},{1,9},{9,1},{17,25},{25,17},{2,10},{10... | collective-permute-start | bytes 196616 | tf_op jit(solution)/shard_map/ppermute | solution.py:522
  23.9 6.7 %collective-permute-start.3 = (bf16[32,2176]{1,0:T(8,128)(2,1)S(1)}, bf16[32,2176]{1,0:T(8,128)(2,1)S(1)}, u32[]{:S(2)}, u32[]{:S(2)}) collective-permute-start(bf16[32,2176]{1,0:T(8,128)(2,1)S(1)} %get-tuple-element.55.refs_0_), channel_id=1, source_target_pairs={{0,1},{2,0},{4,2},{6,4},{7,6},{5,7},{3,5},{1,3},{8,9},{10,8},{12,1... | collective-permute-start | bytes 417800 | tf_op jit(solution)/shard_map/ppermute | solution.py:532
  26.1 7.5 %collective-permute-start.4 = (bf16[32,2176]{1,0:T(8,128)(2,1)S(1)}, bf16[32,2176]{1,0:T(8,128)(2,1)S(1)}, u32[]{:S(2)}, u32[]{:S(2)}) collective-permute-start(bf16[32,2176]{1,0:T(8,128)(2,1)S(1)} %get-tuple-element.56.refs_1_), channel_id=1, source_target_pairs={{0,1},{2,0},{4,2},{6,4},{7,6},{5,7},{3,5},{1,3},{8,9},{10,8},{12,1... | collective-permute-start | bytes 417800 | tf_op jit(solution)/shard_map/ppermute | solution.py:532
  27.6 7.9 %collective-permute-start.10 = (bf16[32,2176]{1,0:T(8,128)(2,1)S(1)}, bf16[32,2176]{1,0:T(8,128)(2,1)S(1)}, u32[]{:S(2)}, u32[]{:S(2)}) collective-permute-start(bf16[32,2176]{1,0:T(8,128)(2,1)S(1)} %get-tuple-element.56.refs_1_), channel_id=1, source_target_pairs={{0,2},{2,4},{4,6},{6,7},{7,5},{5,3},{3,1},{1,0},{8,10},{10,12},{12... | collective-permute-start | bytes 417800 | tf_op jit(solution)/shard_map/ppermute | solution.py:532
  28.1 7.7 %collective-permute-start.14 = (bf16[32,2176]{1,0:T(8,128)(2,1)S(1)}, bf16[32,2176]{1,0:T(8,128)(2,1)S(1)}, u32[]{:S(2)}, u32[]{:S(2)}) collective-permute-start(bf16[32,2176]{1,0:T(8,128)(2,1)S(1)} %get-tuple-element.55.refs_0_), channel_id=1, source_target_pairs={{0,2},{2,4},{4,6},{6,7},{7,5},{5,3},{3,1},{1,0},{8,10},{10,12},{12... | collective-permute-start | bytes 417800 | tf_op jit(solution)/shard_map/ppermute | solution.py:532
  30.6 7.1 %collective-permute-start.5 = (bf16[32,2176]{1,0:T(8,128)(2,1)S(1)}, bf16[32,2176]{1,0:T(8,128)(2,1)S(1)}, u32[]{:S(2)}, u32[]{:S(2)}) collective-permute-start(bf16[32,2176]{1,0:T(8,128)(2,1)S(1)} %collective-permute-done.3.refs_2_), channel_id=1, source_target_pairs={{0,1},{2,0},{4,2},{6,4},{7,6},{5,7},{3,5},{1,3},{8,9},{10,8},{12,1... | collective-permute-start | bytes 417800 | tf_op jit(solution)/shard_map/ppermute | solution.py:532
  33.6 6.6 %collective-permute-start.6 = (bf16[32,2176]{1,0:T(8,128)(2,1)S(1)}, bf16[32,2176]{1,0:T(8,128)(2,1)S(1)}, u32[]{:S(2)}, u32[]{:S(2)}) collective-permute-start(bf16[32,2176]{1,0:T(8,128)(2,1)S(1)} %collective-permute-done.4.refs_3_), channel_id=1, source_target_pairs={{0,1},{2,0},{4,2},{6,4},{7,6},{5,7},{3,5},{1,3},{8,9},{10,8},{12,1... | collective-permute-start | bytes 417800 | tf_op jit(solution)/shard_map/ppermute | solution.py:532
  35.6 6.6 %collective-permute-start.11 = (bf16[32,2176]{1,0:T(8,128)(2,1)S(1)}, bf16[32,2176]{1,0:T(8,128)(2,1)S(1)}, u32[]{:S(2)}, u32[]{:S(2)}) collective-permute-start(bf16[32,2176]{1,0:T(8,128)(2,1)S(1)} %collective-permute-done.10.refs_15_), channel_id=1, source_target_pairs={{0,2},{2,4},{4,6},{6,7},{7,5},{5,3},{3,1},{1,0},{8,10},{10,12},{12... | collective-permute-start | bytes 417800 | tf_op jit(solution)/shard_map/ppermute | solution.py:532
  35.8 7.2 %collective-permute-start.15 = (bf16[32,2176]{1,0:T(8,128)(2,1)S(1)}, bf16[32,2176]{1,0:T(8,128)(2,1)S(1)}, u32[]{:S(2)}, u32[]{:S(2)}) collective-permute-start(bf16[32,2176]{1,0:T(8,128)(2,1)S(1)} %collective-permute-done.14.refs_14_), channel_id=1, source_target_pairs={{0,2},{2,4},{4,6},{6,7},{7,5},{5,3},{3,1},{1,0},{8,10},{10,12},{12... | collective-permute-start | bytes 417800 | tf_op jit(solution)/shard_map/ppermute | solution.py:532
  37.7 5.9 %collective-permute-start.7 = (bf16[32,2176]{1,0:T(8,128)(2,1)S(1)}, bf16[32,2176]{1,0:T(8,128)(2,1)S(1)}, u32[]{:S(2)}, u32[]{:S(2)}) collective-permute-start(bf16[32,2176]{1,0:T(8,128)(2,1)S(1)} %collective-permute-done.5.refs_4_), channel_id=1, source_target_pairs={{0,1},{2,0},{4,2},{6,4},{7,6},{5,7},{3,5},{1,3},{8,9},{10,8},{12,1... | collective-permute-start | bytes 417800 | tf_op jit(solution)/shard_map/ppermute | solution.py:532
  40.2 5.1 %collective-permute-start.8 = (bf16[32,2176]{1,0:T(8,128)(2,1)S(1)}, bf16[32,2176]{1,0:T(8,128)(2,1)S(1)}, u32[]{:S(2)}, u32[]{:S(2)}) collective-permute-start(bf16[32,2176]{1,0:T(8,128)(2,1)S(1)} %collective-permute-done.6.refs_5_), channel_id=1, source_target_pairs={{0,1},{2,0},{4,2},{6,4},{7,6},{5,7},{3,5},{1,3},{8,9},{10,8},{12,1... | collective-permute-start | bytes 417800 | tf_op jit(solution)/shard_map/ppermute | solution.py:532
  42.2 6.2 %collective-permute-start.12 = (bf16[32,2176]{1,0:T(8,128)(2,1)S(1)}, bf16[32,2176]{1,0:T(8,128)(2,1)S(1)}, u32[]{:S(2)}, u32[]{:S(2)}) collective-permute-start(bf16[32,2176]{1,0:T(8,128)(2,1)S(1)} %collective-permute-done.11.refs_13_), channel_id=1, source_target_pairs={{0,2},{2,4},{4,6},{6,7},{7,5},{5,3},{3,1},{1,0},{8,10},{10,12},{12... | collective-permute-start | bytes 417800 | tf_op jit(solution)/shard_map/ppermute | solution.py:532
  43.0 16.7 %collective-permute-start.18 = (bf16[384,2048]{1,0:T(8,128)(2,1)}, bf16[384,2048]{1,0:T(8,128)(2,1)S(1)}, u32[]{:S(2)}, u32[]{:S(2)}) collective-permute-start(bf16[384,2048]{1,0:T(8,128)(2,1)} %get-tuple-element.59.refs_17_), channel_id=1, source_target_pairs={{0,8},{8,0},{16,24},{24,16},{1,9},{9,1},{17,25},{25,17},{2,10},{10... | collective-permute-start | bytes 4718600 | tf_op jit(solution)/shard_map/ppermute | solution.py:522
  43.6 7.8 %collective-permute-start.16 = (bf16[32,2176]{1,0:T(8,128)(2,1)S(1)}, bf16[32,2176]{1,0:T(8,128)(2,1)S(1)}, u32[]{:S(2)}, u32[]{:S(2)}) collective-permute-start(bf16[32,2176]{1,0:T(8,128)(2,1)S(1)} %collective-permute-done.15.refs_12_), channel_id=1, source_target_pairs={{0,2},{2,4},{4,6},{6,7},{7,5},{5,3},{3,1},{1,0},{8,10},{10,12},{12... | collective-permute-start | bytes 417800 | tf_op jit(solution)/shard_map/ppermute | solution.py:532
  45.3 6.1 %collective-permute-start.9 = (bf16[32,2176]{1,0:T(8,128)(2,1)S(1)}, bf16[32,2176]{1,0:T(8,128)(2,1)S(1)}, u32[]{:S(2)}, u32[]{:S(2)}) collective-permute-start(bf16[32,2176]{1,0:T(8,128)(2,1)S(1)} %collective-permute-done.7.refs_6_), channel_id=1, source_target_pairs={{0,1},{2,0},{4,2},{6,4},{7,6},{5,7},{3,5},{1,3},{8,9},{10,8},{12,1... | collective-permute-start | bytes 417800 | tf_op jit(solution)/shard_map/ppermute | solution.py:532
  48.4 5.1 %collective-permute-start.13 = (bf16[32,2176]{1,0:T(8,128)(2,1)S(1)}, bf16[32,2176]{1,0:T(8,128)(2,1)S(1)}, u32[]{:S(2)}, u32[]{:S(2)}) collective-permute-start(bf16[32,2176]{1,0:T(8,128)(2,1)S(1)} %collective-permute-done.12.refs_11_), channel_id=1, source_target_pairs={{0,2},{2,4},{4,6},{6,7},{7,5},{5,3},{3,1},{1,0},{8,10},{10,12},{12... | collective-permute-start | bytes 417800 | tf_op jit(solution)/shard_map/ppermute | solution.py:532
  53.5 23.9 %collective-permute-start.25 = (bf16[256,2048]{1,0:T(8,128)(2,1)S(1)}, bf16[256,2048]{1,0:T(8,128)(2,1)S(1)}, u32[]{:S(2)}, u32[]{:S(2)}) collective-permute-start(bf16[256,2048]{1,0:T(8,128)(2,1)S(1)} %copy-done.1), channel_id=1, source_target_pairs={{0,16},{8,24},{16,0},{24,8},{1,17},{9,25},{17,1},{25,9},{2,18},{10... | collective-permute-start | bytes 3145736 | tf_op jit(solution)/shard_map/ppermute | solution.py:522
  59.5 18.5 %collective-permute-start.24 = (bf16[256,2048]{1,0:T(8,128)(2,1)S(1)}, bf16[256,2048]{1,0:T(8,128)(2,1)S(1)}, u32[]{:S(2)}, u32[]{:S(2)}) collective-permute-start(bf16[256,2048]{1,0:T(8,128)(2,1)S(1)} %copy-done.1), channel_id=1, source_target_pairs={{0,8},{8,0},{16,24},{24,16},{1,9},{9,1},{17,25},{25,17},{2,10},{10... | collective-permute-start | bytes 3145736 | tf_op jit(solution)/shard_map/ppermute | solution.py:522
  84.6 6.4 %collective-permute-start.28 = (bf16[64,1024]{1,0:T(8,128)(2,1)S(1)}, bf16[64,1024]{1,0:T(8,128)(2,1)S(1)}, u32[]{:S(2)}, u32[]{:S(2)}) collective-permute-start(bf16[64,1024]{1,0:T(8,128)(2,1)S(1)} %pad_maximum_fusion), channel_id=1, source_target_pairs={{0,2},{2,4},{4,6},{6,7},{7,5},{5,3},{3,1},{1,0},{8,10},{10,12},{12... | collective-permute-start | bytes 393224 | tf_op jit(solution)/shard_map/ppermute | solution.py:532
  86.5 6.4 %collective-permute-start.32 = (bf16[64,1024]{1,0:T(8,128)(2,1)S(1)}, bf16[64,1024]{1,0:T(8,128)(2,1)S(1)}, u32[]{:S(2)}, u32[]{:S(2)}) collective-permute-start(bf16[64,1024]{1,0:T(8,128)(2,1)S(1)} %pad_maximum_fusion.1), channel_id=1, source_target_pairs={{0,1},{2,0},{4,2},{6,4},{7,6},{5,7},{3,5},{1,3},{8,9},{10,8},{12,1... | collective-permute-start | bytes 393224 | tf_op jit(solution)/shard_map/ppermute | solution.py:532
  87.3 6.5 %collective-permute-start.37 = (bf16[64,1024]{1,0:T(8,128)(2,1)S(1)}, bf16[64,1024]{1,0:T(8,128)(2,1)S(1)}, u32[]{:S(2)}, u32[]{:S(2)}) collective-permute-start(bf16[64,1024]{1,0:T(8,128)(2,1)S(1)} %pad_maximum_fusion.2), channel_id=1, source_target_pairs={{0,2},{2,4},{4,6},{6,7},{7,5},{5,3},{3,1},{1,0},{8,10},{10,12},{12... | collective-permute-start | bytes 393224 | tf_op jit(solution)/shard_map/ppermute | solution.py:532
  89.3 6.4 %collective-permute-start.41 = (bf16[64,1024]{1,0:T(8,128)(2,1)S(1)}, bf16[64,1024]{1,0:T(8,128)(2,1)S(1)}, u32[]{:S(2)}, u32[]{:S(2)}) collective-permute-start(bf16[64,1024]{1,0:T(8,128)(2,1)S(1)} %pad_maximum_fusion.3), channel_id=1, source_target_pairs={{0,1},{2,0},{4,2},{6,4},{7,6},{5,7},{3,5},{1,3},{8,9},{10,8},{12,1... | collective-permute-start | bytes 393224 | tf_op jit(solution)/shard_map/ppermute | solution.py:532
  91.0 5.6 %collective-permute-start.29 = (bf16[64,1024]{1,0:T(8,128)(2,1)S(1)}, bf16[64,1024]{1,0:T(8,128)(2,1)S(1)}, u32[]{:S(2)}, u32[]{:S(2)}) collective-permute-start(bf16[64,1024]{1,0:T(8,128)(2,1)S(1)} %add_convert_fusion.7), channel_id=1, source_target_pairs={{0,2},{2,4},{4,6},{6,7},{7,5},{5,3},{3,1},{1,0},{8,10},{10,12},{12... | collective-permute-start | bytes 393224 | tf_op jit(solution)/shard_map/ppermute | solution.py:532
  92.9 5.6 %collective-permute-start.33 = (bf16[64,1024]{1,0:T(8,128)(2,1)S(1)}, bf16[64,1024]{1,0:T(8,128)(2,1)S(1)}, u32[]{:S(2)}, u32[]{:S(2)}) collective-permute-start(bf16[64,1024]{1,0:T(8,128)(2,1)S(1)} %add_convert_fusion.5), channel_id=1, source_target_pairs={{0,1},{2,0},{4,2},{6,4},{7,6},{5,7},{3,5},{1,3},{8,9},{10,8},{12,1... | collective-permute-start | bytes 393224 | tf_op jit(solution)/shard_map/ppermute | solution.py:532
  93.8 6.4 %collective-permute-start.38 = (bf16[64,1024]{1,0:T(8,128)(2,1)S(1)}, bf16[64,1024]{1,0:T(8,128)(2,1)S(1)}, u32[]{:S(2)}, u32[]{:S(2)}) collective-permute-start(bf16[64,1024]{1,0:T(8,128)(2,1)S(1)} %add_convert_fusion.3), channel_id=1, source_target_pairs={{0,2},{2,4},{4,6},{6,7},{7,5},{5,3},{3,1},{1,0},{8,10},{10,12},{12... | collective-permute-start | bytes 393224 | tf_op jit(solution)/shard_map/ppermute | solution.py:532
  95.8 6.5 %collective-permute-start.42 = (bf16[64,1024]{1,0:T(8,128)(2,1)S(1)}, bf16[64,1024]{1,0:T(8,128)(2,1)S(1)}, u32[]{:S(2)}, u32[]{:S(2)}) collective-permute-start(bf16[64,1024]{1,0:T(8,128)(2,1)S(1)} %add_convert_fusion.1), channel_id=1, source_target_pairs={{0,1},{2,0},{4,2},{6,4},{7,6},{5,7},{3,5},{1,3},{8,9},{10,8},{12,1... | collective-permute-start | bytes 393224 | tf_op jit(solution)/shard_map/ppermute | solution.py:532
  96.6 5.9 %collective-permute-start.30 = (bf16[64,1024]{1,0:T(8,128)(2,1)S(1)}, bf16[64,1024]{1,0:T(8,128)(2,1)S(1)}, u32[]{:S(2)}, u32[]{:S(2)}) collective-permute-start(bf16[64,1024]{1,0:T(8,128)(2,1)S(1)} %add_convert_fusion.6), channel_id=1, source_target_pairs={{0,2},{2,4},{4,6},{6,7},{7,5},{5,3},{3,1},{1,0},{8,10},{10,12},{12... | collective-permute-start | bytes 393224 | tf_op jit(solution)/shard_map/ppermute | solution.py:532
  98.5 5.4 %collective-permute-start.34 = (bf16[64,1024]{1,0:T(8,128)(2,1)S(1)}, bf16[64,1024]{1,0:T(8,128)(2,1)S(1)}, u32[]{:S(2)}, u32[]{:S(2)}) collective-permute-start(bf16[64,1024]{1,0:T(8,128)(2,1)S(1)} %add_convert_fusion.4), channel_id=1, source_target_pairs={{0,1},{2,0},{4,2},{6,4},{7,6},{5,7},{3,5},{1,3},{8,9},{10,8},{12,1... | collective-permute-start | bytes 393224 | tf_op jit(solution)/shard_map/ppermute | solution.py:532
  100.3 5.0 %collective-permute-start.39 = (bf16[64,1024]{1,0:T(8,128)(2,1)S(1)}, bf16[64,1024]{1,0:T(8,128)(2,1)S(1)}, u32[]{:S(2)}, u32[]{:S(2)}) collective-permute-start(bf16[64,1024]{1,0:T(8,128)(2,1)S(1)} %add_convert_fusion.2), channel_id=1, source_target_pairs={{0,2},{2,4},{4,6},{6,7},{7,5},{5,3},{3,1},{1,0},{8,10},{10,12},{12... | collective-permute-start | bytes 393224 | tf_op jit(solution)/shard_map/ppermute | solution.py:532
  102.3 5.0 %collective-permute-start.43 = (bf16[64,1024]{1,0:T(8,128)(2,1)S(1)}, bf16[64,1024]{1,0:T(8,128)(2,1)S(1)}, u32[]{:S(2)}, u32[]{:S(2)}) collective-permute-start(bf16[64,1024]{1,0:T(8,128)(2,1)S(1)} %add_convert_fusion), channel_id=1, source_target_pairs={{0,1},{2,0},{4,2},{6,4},{7,6},{5,7},{3,5},{1,3},{8,9},{10,8},{12,1... | collective-permute-start | bytes 393224 | tf_op jit(solution)/shard_map/ppermute | solution.py:532
  (21 other events, 243.5 us)
